TPU v7x, 32 devices: a whole 2x2x4 slice. The times are simulated.
32 devices in a mesh: section: 4 (over y, x), tm: 2 (over core), space: 4 (over z).
Axes of the slice: x: 2, y: 2, z: 4, core: 2. Of those that a mesh axis runs over, the one named last changes fastest.
Arguments:
- video: bfloat16 [4, 32, 128, 128], P('tm', ('section', 'space')), may hold values from -6 to 6
- cotangent: bfloat16 [4, 32, 128, 128], P('tm', ('section', 'space')), may hold values from -6 to 6
- spatial_weights: bfloat16 [4, 9, 128, 128], P('section'), may hold values from -0.1875 to 0.1875
- temporal_weights: bfloat16 [4, 3, 128, 128], P('section'), may hold values from -0.3125 to 0.3125
Outputs:
- grad_spatial: float32 [4, 9, 128, 128], P('section')
- grad_temporal: float32 [4, 3, 128, 128], P('section')
- grad_video: bfloat16 [4, 32, 128, 128], P('tm', ('section', 'space'))
All inputs are finite; a program needn't handle non-finite values.
Results may differ from a plain program's by a relative error of at most 0.019.
Values may be sent and summed in bfloat16 or wider, within the bound.
No kernel may reach another device: no remote copies, remote signals or barrier semaphores. Data moves between devices by JAX's collectives and lax.ppermute only.
A program may use at most 64 MiB of HBM per device.

v0:
```python
import jax
import jax.numpy as jnp
from jax import lax
from jax.sharding import PartitionSpec as P


def with_halo(cells, sides, width):
    for axis, dim in sides:
        count = lax.axis_size(axis)
        ends = count - 1
        head = lax.slice_in_dim(cells, 0, width, axis=dim)
        tail = lax.slice_in_dim(cells, cells.shape[dim] - width, cells.shape[dim], axis=dim)
        cells = jnp.concatenate(
            [
                lax.ppermute(tail, axis, [(i, (i + 1) % count) for i in range(ends)]),
                cells,
                lax.ppermute(head, axis, [((i + 1) % count, i) for i in range(ends)]),
            ],
            axis=dim,
        )
    return cells


def shifted(value, axis, steps):
    count = lax.axis_size(axis)
    leading, last = (max(0, -steps), min(count, count - steps))
    return lax.ppermute(value, axis, [(source, source + steps) for source in range(leading, last)])


def forward_layer(inputs, spatial_weight, temporal_weight):
    frames = inputs.shape[0]
    height = inputs.shape[1]
    columns = inputs.shape[2]
    padded = with_halo(inputs, ((("section", "space"), 1),), 1)
    padded = jnp.pad(padded, ((0, 0), (0, 0), (1, 1), (0, 0)))
    before = jnp.einsum(
        "frwc,cd->frwd",
        padded[:, 0:height, 0:columns],
        spatial_weight[0],
        preferred_element_type=jnp.float32,
    )
    for offset in range(1, 9):
        row_off = offset // 3
        col_off = offset % 3
        before = before + jnp.einsum(
            "frwc,cd->frwd",
            padded[:, row_off : row_off + height, col_off : col_off + columns],
            spatial_weight[offset],
            preferred_element_type=jnp.float32,
        )
    hidden = jax.nn.silu(before).astype(jnp.bfloat16)
    earlier = shifted(hidden, "tm", 1)
    timeline = jnp.concatenate([earlier, hidden], 0)
    mixed = jnp.einsum(
        "frwc,cd->frwd", timeline[0:frames], temporal_weight[0], preferred_element_type=jnp.float32
    )
    for offset in range(1, 3):
        mixed = mixed + jnp.einsum(
            "frwc,cd->frwd",
            timeline[offset : offset + frames],
            temporal_weight[offset],
            preferred_element_type=jnp.float32,
        )
    outputs = (inputs.astype(jnp.float32) + mixed).astype(jnp.bfloat16)
    return (padded, before, timeline, outputs)


def backward_layer(grad, padded, before, timeline, spatial_weight, temporal_weight):
    frames = grad.shape[0]
    height = grad.shape[1]
    columns = grad.shape[2]
    later = shifted(grad, "tm", -1)
    ahead = jnp.concatenate([grad, later], 0)
    temporal_list = []
    hidden_grad = jnp.zeros(grad.shape, jnp.float32)
    for offset in range(3):
        temporal_list.append(
            jnp.einsum(
                "frwc,frwd->cd",
                timeline[offset : offset + frames],
                grad,
                preferred_element_type=jnp.float32,
            )
        )
        hidden_grad = hidden_grad + jnp.einsum(
            "frwd,cd->frwc",
            ahead[2 - offset : 2 - offset + frames],
            temporal_weight[offset],
            preferred_element_type=jnp.float32,
        )
    sigma = jax.nn.sigmoid(before)
    pre_grad = (hidden_grad * sigma * (1.0 + before * (1.0 - sigma))).astype(jnp.bfloat16)
    rimmed = with_halo(pre_grad, ((("section", "space"), 1),), 1)
    rimmed = jnp.pad(rimmed, ((0, 0), (0, 0), (1, 1), (0, 0)))
    spatial_list = []
    back = jnp.zeros(grad.shape, jnp.float32)
    for offset in range(9):
        row_off = offset // 3
        col_off = offset % 3
        spatial_list.append(
            jnp.einsum(
                "frwc,frwd->cd",
                padded[:, row_off : row_off + height, col_off : col_off + columns],
                pre_grad,
                preferred_element_type=jnp.float32,
            )
        )
        back = back + jnp.einsum(
            "frwd,cd->frwc",
            rimmed[:, 2 - row_off : 2 - row_off + height, 2 - col_off : 2 - col_off + columns],
            spatial_weight[offset],
            preferred_element_type=jnp.float32,
        )
    new_grad = (grad.astype(jnp.float32) + back).astype(jnp.bfloat16)
    return (jnp.stack(spatial_list), jnp.stack(temporal_list), new_grad)


def on_device(video, cotangent, spatial_weights, temporal_weights):
    spatial_all, temporal_all = (
        lax.all_gather(spatial_weights, "section", axis=0, tiled=True),
        lax.all_gather(temporal_weights, "section", axis=0, tiled=True),
    )
    blocks = spatial_all.shape[0]
    records = []
    inputs = video
    for step in range(blocks):
        padded, before, timeline, outputs = forward_layer(
            inputs, spatial_all[step], temporal_all[step]
        )
        records.append((padded, before, timeline))
        inputs = outputs
    grad = cotangent
    spatial_out = [None] * blocks
    temporal_out = [None] * blocks
    for step in reversed(range(blocks)):
        padded, before, timeline = records[step]
        spatial_grad, temporal_grad, grad = backward_layer(
            grad, padded, before, timeline, spatial_all[step], temporal_all[step]
        )
        spatial_out[step] = spatial_grad
        temporal_out[step] = temporal_grad
    pixel_count = (
        video.shape[0]
        * lax.axis_size("tm")
        * video.shape[1]
        * lax.axis_size("section")
        * lax.axis_size("space")
        * video.shape[2]
    )
    factor = 1.0 / float(pixel_count) ** 0.5
    spatial_stack = jnp.stack(spatial_out) * factor
    temporal_stack = jnp.stack(temporal_out) * factor
    spatial_sum, temporal_sum = lax.psum(
        (spatial_stack, temporal_stack), ("section", "tm", "space")
    )
    own_block = lax.axis_index("section")
    spatial_own = lax.dynamic_slice_in_dim(spatial_sum, own_block, 1, 0)
    temporal_own = lax.dynamic_slice_in_dim(temporal_sum, own_block, 1, 0)
    return (spatial_own, temporal_own, grad)


def solution(mesh):
    return jax.shard_map(
        on_device,
        mesh=mesh,
        in_specs=(
            P("tm", ("section", "space"), None, None),
            P("tm", ("section", "space"), None, None),
            P("section", None, None, None),
            P("section", None, None, None),
        ),
        out_specs=(
            P("section", None, None, None),
            P("section", None, None, None),
            P("tm", ("section", "space"), None, None),
        ),
        check_vma=False,
    )
```

profile of v0, /device:TPU:0, one launch (start us, length us, event | category | flops | bytes accessed | tf_op | source)
XLA Modules:
  0.0 320.7 jit_solution(329914535302346290)
XLA Ops:
  8.8 4.9 %collective-permute-start = (bf16[2,1,128,128]{3,2,1,0:T(8,128)(2,1)S(1)}, bf16[2,1,128,128]{3,2,1,0:T(8,128)(2,1)S(1)}, u32[]{:S(2)}, u32[]{:S(2)}) collective-permute-start(bf16[2,1,128,128]{3,2,1,0:T(8,128)(2,1)S(1)} %get-tuple-element.21), channel_id=1, source_target_pairs={{0,1},{1,2},{2,3},{3,8},{8,9},{9,10},{10,11},{11,16},{16,17},{17,1... | collective-permute-start | bytes 196616 | tf_op jit(solution)/shard_map/ppermute | solution.py:15
  15.1 15.2 %all_gather.6 = bf16[4,3,128,128]{3,2,1,0:T(8,128)(2,1)S(1)} all-gather(bf16[1,3,128,128]{3,2,1,0:T(8,128)(2,1)} %param.7), channel_id=1, replica_groups=mesh['section'=4,'tm'=2,'space'=4] {'section'}, dimensions={0}, use_global_device_ids=true | all-gather | bytes 491520 | tf_op jit(solution)/shard_map/all_gather | solution.py:121
  30.5 12.1 %all-gather.2.cloned.1.call-done = bf16[4,9,128,128]{3,2,1,0:T(8,128)(2,1)} async-done(((bf16[1,9,128,128]{3,2,1,0:T(8,128)(2,1)}), bf16[4,9,128,128]{3,2,1,0:T(8,128)(2,1)}) %all-gather.2.cloned.1.call-update) | async-done | bytes 1179664 | tf_op jit(solution)/shard_map/all_gather | solution.py:120
  47.7 1.9 collective-permute-start.3
  50.9 3.4 %collective-permute-start.4 = (bf16[2,1,128,128]{3,2,1,0:T(8,128)(2,1)S(1)}, bf16[2,1,128,128]{3,2,1,0:T(8,128)(2,1)S(1)}, u32[]{:S(2)}, u32[]{:S(2)}) collective-permute-start(bf16[2,1,128,128]{3,2,1,0:T(8,128)(2,1)S(1)} %get-tuple-element.17), channel_id=1, source_target_pairs={{0,1},{1,2},{2,3},{3,8},{8,9},{9,10},{10,11},{11,16},{16,17},{17,1... | collective-permute-start | bytes 196616 | tf_op jit(solution)/shard_map/ppermute | solution.py:15
  57.1 4.7 %collective-permute-done.5 = bf16[2,1,128,128]{3,2,1,0:T(8,128)(2,1)S(1)} collective-permute-done((bf16[2,1,128,128]{3,2,1,0:T(8,128)(2,1)S(1)}, bf16[2,1,128,128]{3,2,1,0:T(8,128)(2,1)S(1)}, u32[]{:S(2)}, u32[]{:S(2)}) %collective-permute-start.5) | collective-permute-done | bytes 65568 | tf_op jit(solution)/shard_map/ppermute | solution.py:17
  64.0 2.5 collective-permute-start.6
  68.5 3.4 %collective-permute-start.7 = (bf16[2,1,128,128]{3,2,1,0:T(8,128)(2,1)}, bf16[2,1,128,128]{3,2,1,0:T(8,128)(2,1)S(1)}, u32[]{:S(2)}, u32[]{:S(2)}) collective-permute-start(bf16[2,1,128,128]{3,2,1,0:T(8,128)(2,1)} %get-tuple-element.15), channel_id=1, source_target_pairs={{0,1},{1,2},{2,3},{3,8},{8,9},{9,10},{10,11},{11,16},{16,17},{17,1... | collective-permute-start | bytes 196616 | tf_op jit(solution)/shard_map/ppermute | solution.py:15
  74.3 6.1 %collective-permute-done.8 = bf16[2,1,128,128]{3,2,1,0:T(8,128)(2,1)S(1)} collective-permute-done((bf16[2,1,128,128]{3,2,1,0:T(8,128)(2,1)}, bf16[2,1,128,128]{3,2,1,0:T(8,128)(2,1)S(1)}, u32[]{:S(2)}, u32[]{:S(2)}) %collective-permute-start.8) | collective-permute-done | bytes 65568 | tf_op jit(solution)/shard_map/ppermute | solution.py:17
  81.9 1.7 collective-permute-start.9
  85.0 4.1 %collective-permute-start.10 = (bf16[2,1,128,128]{3,2,1,0:T(8,128)(2,1)S(1)}, bf16[2,1,128,128]{3,2,1,0:T(8,128)(2,1)S(1)}, u32[]{:S(2)}, u32[]{:S(2)}) collective-permute-start(bf16[2,1,128,128]{3,2,1,0:T(8,128)(2,1)S(1)} %get-tuple-element.13), channel_id=1, source_target_pairs={{0,1},{1,2},{2,3},{3,8},{8,9},{9,10},{10,11},{11,16},{16,17},{17,1... | collective-permute-start | bytes 196616 | tf_op jit(solution)/shard_map/ppermute | solution.py:15
  91.6 5.1 %collective-permute-done.11 = bf16[2,1,128,128]{3,2,1,0:T(8,128)(2,1)S(1)} collective-permute-done((bf16[2,1,128,128]{3,2,1,0:T(8,128)(2,1)S(1)}, bf16[2,1,128,128]{3,2,1,0:T(8,128)(2,1)S(1)}, u32[]{:S(2)}, u32[]{:S(2)}) %collective-permute-start.11) | collective-permute-done | bytes 65568 | tf_op jit(solution)/shard_map/ppermute | solution.py:17
  100.2 1.3 collective-permute-start.13
  101.5 4.9 %collective-permute-start.12 = (bf16[2,1,128,128]{3,2,1,0:T(8,128)(2,1)S(1)}, bf16[2,1,128,128]{3,2,1,0:T(8,128)(2,1)S(1)}, u32[]{:S(2)}, u32[]{:S(2)}) collective-permute-start(bf16[2,1,128,128]{3,2,1,0:T(8,128)(2,1)S(1)} %get-tuple-element.11), channel_id=1, source_target_pairs={{0,1},{1,2},{2,3},{3,8},{8,9},{9,10},{10,11},{11,16},{16,17},{17,1... | collective-permute-start | bytes 196616 | tf_op jit(solution)/shard_map/ppermute | solution.py:15
  106.4 1.3 collective-permute-start.21
  116.9 4.6 %collective-permute-start.15 = (bf16[2,1,128,128]{3,2,1,0:T(8,128)(2,1)S(1)}, bf16[2,1,128,128]{3,2,1,0:T(8,128)(2,1)S(1)}, u32[]{:S(2)}, u32[]{:S(2)}) collective-permute-start(bf16[2,1,128,128]{3,2,1,0:T(8,128)(2,1)S(1)} %get-tuple-element.9), channel_id=1, source_target_pairs={{0,1},{1,2},{2,3},{3,8},{8,9},{9,10},{10,11},{11,16},{16,17},{17,1... | collective-permute-start | bytes 196616 | tf_op jit(solution)/shard_map/ppermute | solution.py:15
  125.2 1.3 collective-permute-start.17
  129.1 1.4 collective-permute-start.19
  130.5 5.4 %collective-permute-start.18 = (bf16[2,1,128,128]{3,2,1,0:T(8,128)(2,1)S(1)}, bf16[2,1,128,128]{3,2,1,0:T(8,128)(2,1)S(1)}, u32[]{:S(2)}, u32[]{:S(2)}) collective-permute-start(bf16[2,1,128,128]{3,2,1,0:T(8,128)(2,1)S(1)} %get-tuple-element.7), channel_id=1, source_target_pairs={{0,1},{1,2},{2,3},{3,8},{8,9},{9,10},{10,11},{11,16},{16,17},{17,1... | collective-permute-start | bytes 196616 | tf_op jit(solution)/shard_map/ppermute | solution.py:15
  145.0 7.2 %collective-permute-start.22 = (bf16[2,1,128,128]{3,2,1,0:T(8,128)(2,1)S(1)}, bf16[2,1,128,128]{3,2,1,0:T(8,128)(2,1)S(1)}, u32[]{:S(2)}, u32[]{:S(2)}) collective-permute-start(bf16[2,1,128,128]{3,2,1,0:T(8,128)(2,1)S(1)} %get-tuple-element.5), channel_id=1, source_target_pairs={{0,1},{1,2},{2,3},{3,8},{8,9},{9,10},{10,11},{11,16},{16,17},{17,1... | collective-permute-start | bytes 196616 | tf_op jit(solution)/shard_map/ppermute | solution.py:15
  154.1 1.6 maximum_multiply_fusion
  158.3 152.0 %all-reduce.11.cloned.1.call-done = (f32[4,9,128,128]{3,2,1,0:T(8,128)}, f32[4,3,128,128]{3,2,1,0:T(8,128)}) async-done(((f32[4,9,128,128]{3,2,1,0:T(8,128)}, f32[4,3,128,128]{3,2,1,0:T(8,128)}), (f32[4,9,128,128]{3,2,1,0:T(8,128)}, f32[4,3,128,128]{3,2,1,0:T(8,128)})) %all-reduce.11.cloned.1.call-update) | async-done | bytes 3145744 | tf_op jit(solution)/shard_map/psum | solution.py:153
  310.3 1.9 constant_dynamic-slice_fusion.1
  312.2 1.6 constant_dynamic-slice_fusion
  (221 shorter events, 55.4 us)
Async XLA Ops:
  7.2 35.4 %all-gather.2.cloned.1.call-start = ((), (), s32[]{:S(2)}) async-start(), calls=%async_computation | async-start | bytes 1474560 | tf_op jit(solution)/shard_map/all_gather | solution.py:120
  7.9 302.4 %all-reduce.11.cloned.1.call-start = ((), (), s32[]{:S(2)}) async-start(), calls=%async_computation.1 | async-start | bytes 6291456 | tf_op jit(solution)/shard_map/psum | solution.py:153
  8.8 21.4 %collective-permute-start = (bf16[2,1,128,128]{3,2,1,0:T(8,128)(2,1)S(1)}, bf16[2,1,128,128]{3,2,1,0:T(8,128)(2,1)S(1)}, u32[]{:S(2)}, u32[]{:S(2)}) collective-permute-start(bf16[2,1,128,128]{3,2,1,0:T(8,128)(2,1)S(1)} %get-tuple-element.21), channel_id=1, source_target_pairs={{0,1},{1,2},{2,3},{3,8},{8,9},{9,10},{10,11},{11,16},{16,17},{17,1... | collective-permute-start | bytes 196616 | tf_op jit(solution)/shard_map/ppermute | solution.py:15
  13.8 16.6 %collective-permute-start.1 = (bf16[2,1,128,128]{3,2,1,0:T(8,128)(2,1)S(1)}, bf16[2,1,128,128]{3,2,1,0:T(8,128)(2,1)S(1)}, u32[]{:S(2)}, u32[]{:S(2)}) collective-permute-start(bf16[2,1,128,128]{3,2,1,0:T(8,128)(2,1)S(1)} %get-tuple-element.22), channel_id=1, source_target_pairs={{1,0},{2,1},{3,2},{8,3},{9,8},{10,9},{11,10},{16,11},{17,16},{18,1... | collective-permute-start | bytes 196616 | tf_op jit(solution)/shard_map/ppermute | solution.py:17
  50.9 6.0 %collective-permute-start.4 = (bf16[2,1,128,128]{3,2,1,0:T(8,128)(2,1)S(1)}, bf16[2,1,128,128]{3,2,1,0:T(8,128)(2,1)S(1)}, u32[]{:S(2)}, u32[]{:S(2)}) collective-permute-start(bf16[2,1,128,128]{3,2,1,0:T(8,128)(2,1)S(1)} %get-tuple-element.17), channel_id=1, source_target_pairs={{0,1},{1,2},{2,3},{3,8},{8,9},{9,10},{10,11},{11,16},{16,17},{17,1... | collective-permute-start | bytes 196616 | tf_op jit(solution)/shard_map/ppermute | solution.py:15
  54.3 34.8 %collective-permute-start.2 = (bf16[2,2,128,128]{3,2,1,0:T(8,128)(2,1)S(1)}, bf16[2,2,128,128]{3,2,1,0:T(8,128)(2,1)}, u32[]{:S(2)}, u32[]{:S(2)}) collective-permute-start(bf16[2,2,128,128]{3,2,1,0:T(8,128)(2,1)S(1)} %copy-done.2), channel_id=1, source_target_pairs={{4,0},{5,1},{6,2},{7,3},{12,8},{13,9},{14,10},{15,11},{20,16},{21,... | collective-permute-start | bytes 393224 | tf_op jit(solution)/shard_map/ppermute | solution.py:27
  55.6 6.2 %collective-permute-start.5 = (bf16[2,1,128,128]{3,2,1,0:T(8,128)(2,1)S(1)}, bf16[2,1,128,128]{3,2,1,0:T(8,128)(2,1)S(1)}, u32[]{:S(2)}, u32[]{:S(2)}) collective-permute-start(bf16[2,1,128,128]{3,2,1,0:T(8,128)(2,1)S(1)} %get-tuple-element.18), channel_id=1, source_target_pairs={{1,0},{2,1},{3,2},{8,3},{9,8},{10,9},{11,10},{16,11},{17,16},{18,1... | collective-permute-start | bytes 196616 | tf_op jit(solution)/shard_map/ppermute | solution.py:17
  64.0 3.5 %collective-permute-start.6 = (bf16[2,2,128,128]{3,2,1,0:T(8,128)(2,1)S(1)}, bf16[2,2,128,128]{3,2,1,0:T(8,128)(2,1)S(1)}, u32[]{:S(2)}, u32[]{:S(2)}) collective-permute-start(bf16[2,2,128,128]{3,2,1,0:T(8,128)(2,1)S(1)} %get-tuple-element.25), channel_id=1, source_target_pairs={{0,4},{1,5},{2,6},{3,7},{8,12},{9,13},{10,14},{11,15},{16,20},{17,... | collective-permute-start | bytes 393224 | tf_op jit(solution)/shard_map/ppermute | solution.py:27
  68.5 5.6 %collective-permute-start.7 = (bf16[2,1,128,128]{3,2,1,0:T(8,128)(2,1)}, bf16[2,1,128,128]{3,2,1,0:T(8,128)(2,1)S(1)}, u32[]{:S(2)}, u32[]{:S(2)}) collective-permute-start(bf16[2,1,128,128]{3,2,1,0:T(8,128)(2,1)} %get-tuple-element.15), channel_id=1, source_target_pairs={{0,1},{1,2},{2,3},{3,8},{8,9},{9,10},{10,11},{11,16},{16,17},{17,1... | collective-permute-start | bytes 196616 | tf_op jit(solution)/shard_map/ppermute | solution.py:15
  72.8 7.6 %collective-permute-start.8 = (bf16[2,1,128,128]{3,2,1,0:T(8,128)(2,1)}, bf16[2,1,128,128]{3,2,1,0:T(8,128)(2,1)S(1)}, u32[]{:S(2)}, u32[]{:S(2)}) collective-permute-start(bf16[2,1,128,128]{3,2,1,0:T(8,128)(2,1)} %get-tuple-element.16), channel_id=1, source_target_pairs={{1,0},{2,1},{3,2},{8,3},{9,8},{10,9},{11,10},{16,11},{17,16},{18,1... | collective-permute-start | bytes 196616 | tf_op jit(solution)/shard_map/ppermute | solution.py:17
  85.0 6.4 %collective-permute-start.10 = (bf16[2,1,128,128]{3,2,1,0:T(8,128)(2,1)S(1)}, bf16[2,1,128,128]{3,2,1,0:T(8,128)(2,1)S(1)}, u32[]{:S(2)}, u32[]{:S(2)}) collective-permute-start(bf16[2,1,128,128]{3,2,1,0:T(8,128)(2,1)S(1)} %get-tuple-element.13), channel_id=1, source_target_pairs={{0,1},{1,2},{2,3},{3,8},{8,9},{9,10},{10,11},{11,16},{16,17},{17,1... | collective-permute-start | bytes 196616 | tf_op jit(solution)/shard_map/ppermute | solution.py:15
  90.1 6.6 %collective-permute-start.11 = (bf16[2,1,128,128]{3,2,1,0:T(8,128)(2,1)S(1)}, bf16[2,1,128,128]{3,2,1,0:T(8,128)(2,1)S(1)}, u32[]{:S(2)}, u32[]{:S(2)}) collective-permute-start(bf16[2,1,128,128]{3,2,1,0:T(8,128)(2,1)S(1)} %get-tuple-element.14), channel_id=1, source_target_pairs={{1,0},{2,1},{3,2},{8,3},{9,8},{10,9},{11,10},{16,11},{17,16},{18,1... | collective-permute-start | bytes 196616 | tf_op jit(solution)/shard_map/ppermute | solution.py:17
  100.2 9.7 %collective-permute-start.13 = (bf16[2,1,128,128]{3,2,1,0:T(8,128)(2,1)S(1)}, bf16[2,1,128,128]{3,2,1,0:T(8,128)(2,1)S(1)}, u32[]{:S(2)}, u32[]{:S(2)}) collective-permute-start(bf16[2,1,128,128]{3,2,1,0:T(8,128)(2,1)S(1)} %get-tuple-element.12), channel_id=1, source_target_pairs={{1,0},{2,1},{3,2},{8,3},{9,8},{10,9},{11,10},{16,11},{17,16},{18,1... | collective-permute-start | bytes 196616 | tf_op jit(solution)/shard_map/ppermute | solution.py:17
  101.5 8.6 %collective-permute-start.12 = (bf16[2,1,128,128]{3,2,1,0:T(8,128)(2,1)S(1)}, bf16[2,1,128,128]{3,2,1,0:T(8,128)(2,1)S(1)}, u32[]{:S(2)}, u32[]{:S(2)}) collective-permute-start(bf16[2,1,128,128]{3,2,1,0:T(8,128)(2,1)S(1)} %get-tuple-element.11), channel_id=1, source_target_pairs={{0,1},{1,2},{2,3},{3,8},{8,9},{9,10},{10,11},{11,16},{16,17},{17,1... | collective-permute-start | bytes 196616 | tf_op jit(solution)/shard_map/ppermute | solution.py:15
  106.4 7.5 %collective-permute-start.21 = (bf16[2,2,128,128]{3,2,1,0:T(8,128)(2,1)S(1)}, bf16[2,2,128,128]{3,2,1,0:T(8,128)(2,1)S(1)}, u32[]{:S(2)}, u32[]{:S(2)}) collective-permute-start(bf16[2,2,128,128]{3,2,1,0:T(8,128)(2,1)S(1)} %get-tuple-element.29), channel_id=1, source_target_pairs={{0,4},{1,5},{2,6},{3,7},{8,12},{9,13},{10,14},{11,15},{16,20},{17,... | collective-permute-start | bytes 393224 | tf_op jit(solution)/shard_map/ppermute | solution.py:27
  111.7 3.2 %collective-permute-start.14 = (bf16[2,2,128,128]{3,2,1,0:T(8,128)(2,1)S(1)}, bf16[2,2,128,128]{3,2,1,0:T(8,128)(2,1)S(1)}, u32[]{:S(2)}, u32[]{:S(2)}) collective-permute-start(bf16[2,2,128,128]{3,2,1,0:T(8,128)(2,1)S(1)} %fusion.33), channel_id=1, source_target_pairs={{4,0},{5,1},{6,2},{7,3},{12,8},{13,9},{14,10},{15,11},{20,16},{21,... | collective-permute-start | bytes 393224 | tf_op jit(solution)/shard_map/ppermute | solution.py:27
  115.6 7.8 %collective-permute-start.16 = (bf16[2,1,128,128]{3,2,1,0:T(8,128)(2,1)S(1)}, bf16[2,1,128,128]{3,2,1,0:T(8,128)(2,1)S(1)}, u32[]{:S(2)}, u32[]{:S(2)}) collective-permute-start(bf16[2,1,128,128]{3,2,1,0:T(8,128)(2,1)S(1)} %get-tuple-element.10), channel_id=1, source_target_pairs={{1,0},{2,1},{3,2},{8,3},{9,8},{10,9},{11,10},{16,11},{17,16},{18,1... | collective-permute-start | bytes 196616 | tf_op jit(solution)/shard_map/ppermute | solution.py:17
  116.9 6.6 %collective-permute-start.15 = (bf16[2,1,128,128]{3,2,1,0:T(8,128)(2,1)S(1)}, bf16[2,1,128,128]{3,2,1,0:T(8,128)(2,1)S(1)}, u32[]{:S(2)}, u32[]{:S(2)}) collective-permute-start(bf16[2,1,128,128]{3,2,1,0:T(8,128)(2,1)S(1)} %get-tuple-element.9), channel_id=1, source_target_pairs={{0,1},{1,2},{2,3},{3,8},{8,9},{9,10},{10,11},{11,16},{16,17},{17,1... | collective-permute-start | bytes 196616 | tf_op jit(solution)/shard_map/ppermute | solution.py:15
  125.2 3.2 %collective-permute-start.17 = (bf16[2,2,128,128]{3,2,1,0:T(8,128)(2,1)S(1)}, bf16[2,2,128,128]{3,2,1,0:T(8,128)(2,1)S(1)}, u32[]{:S(2)}, u32[]{:S(2)}) collective-permute-start(bf16[2,2,128,128]{3,2,1,0:T(8,128)(2,1)S(1)} %fusion.34), channel_id=1, source_target_pairs={{4,0},{5,1},{6,2},{7,3},{12,8},{13,9},{14,10},{15,11},{20,16},{21,... | collective-permute-start | bytes 393224 | tf_op jit(solution)/shard_map/ppermute | solution.py:27
  129.1 8.8 %collective-permute-start.19 = (bf16[2,1,128,128]{3,2,1,0:T(8,128)(2,1)S(1)}, bf16[2,1,128,128]{3,2,1,0:T(8,128)(2,1)S(1)}, u32[]{:S(2)}, u32[]{:S(2)}) collective-permute-start(bf16[2,1,128,128]{3,2,1,0:T(8,128)(2,1)S(1)} %get-tuple-element.8), channel_id=1, source_target_pairs={{1,0},{2,1},{3,2},{8,3},{9,8},{10,9},{11,10},{16,11},{17,16},{18,1... | collective-permute-start | bytes 196616 | tf_op jit(solution)/shard_map/ppermute | solution.py:17
  130.5 7.5 %collective-permute-start.18 = (bf16[2,1,128,128]{3,2,1,0:T(8,128)(2,1)S(1)}, bf16[2,1,128,128]{3,2,1,0:T(8,128)(2,1)S(1)}, u32[]{:S(2)}, u32[]{:S(2)}) collective-permute-start(bf16[2,1,128,128]{3,2,1,0:T(8,128)(2,1)S(1)} %get-tuple-element.7), channel_id=1, source_target_pairs={{0,1},{1,2},{2,3},{3,8},{8,9},{9,10},{10,11},{11,16},{16,17},{17,1... | collective-permute-start | bytes 196616 | tf_op jit(solution)/shard_map/ppermute | solution.py:15
  139.7 3.2 %collective-permute-start.20 = (bf16[2,2,128,128]{3,2,1,0:T(8,128)(2,1)S(1)}, bf16[2,2,128,128]{3,2,1,0:T(8,128)(2,1)S(1)}, u32[]{:S(2)}, u32[]{:S(2)}) collective-permute-start(bf16[2,2,128,128]{3,2,1,0:T(8,128)(2,1)S(1)} %fusion.35), channel_id=1, source_target_pairs={{4,0},{5,1},{6,2},{7,3},{12,8},{13,9},{14,10},{15,11},{20,16},{21,... | collective-permute-start | bytes 393224 | tf_op jit(solution)/shard_map/ppermute | solution.py:27
  143.7 12.1 %collective-permute-start.23 = (bf16[2,1,128,128]{3,2,1,0:T(8,128)(2,1)S(1)}, bf16[2,1,128,128]{3,2,1,0:T(8,128)(2,1)S(1)}, u32[]{:S(2)}, u32[]{:S(2)}) collective-permute-start(bf16[2,1,128,128]{3,2,1,0:T(8,128)(2,1)S(1)} %get-tuple-element.6), channel_id=1, source_target_pairs={{1,0},{2,1},{3,2},{8,3},{9,8},{10,9},{11,10},{16,11},{17,16},{18,1... | collective-permute-start | bytes 196616 | tf_op jit(solution)/shard_map/ppermute | solution.py:17
  145.0 11.0 %collective-permute-start.22 = (bf16[2,1,128,128]{3,2,1,0:T(8,128)(2,1)S(1)}, bf16[2,1,128,128]{3,2,1,0:T(8,128)(2,1)S(1)}, u32[]{:S(2)}, u32[]{:S(2)}) collective-permute-start(bf16[2,1,128,128]{3,2,1,0:T(8,128)(2,1)S(1)} %get-tuple-element.5), channel_id=1, source_target_pairs={{0,1},{1,2},{2,3},{3,8},{8,9},{9,10},{10,11},{11,16},{16,17},{17,1... | collective-permute-start | bytes 196616 | tf_op jit(solution)/shard_map/ppermute | solution.py:15
  (13 other events, 75.3 us)
Sparse Core Ops, SparseCore 0:
  9.8 32.6 all-gather.1
  155.9 154.3 all-reduce.10
where the time goes:
time: 322 us; the launch traced here: 321 us
  waiting for transfers between devices  185 us (57%)
  starting transfers between devices  61.1 us (19%)
  matrix products  34.6 us (11%)
  between operations  15.6 us (5%)
  blocking collectives  15.2 us (5%)
  local copies, waits for them, and re-layouts  6.17 us (2%)
  other arithmetic  3.33 us (1%)
    psum x1, waiting for transfers between devices, on_device(): lax.psum((spatial_stack, temporal_stack), ('section', 'tm', 'space'))  152 us
    ppermute x8, starting transfers between devices, with_halo(): lax.ppermute(tail, axis, [(i, (i + 1) % count) for i in range(ends)])  37.9 us
    ppermute x8, waiting for transfers between devices, with_halo(): lax.ppermute(head, axis, [((i + 1) % count, i) for i in range(ends)])  15.9 us
    all_gather x1, blocking collectives, on_device(): lax.all_gather(temporal_weights, 'section', axis=0, tiled=True)  15.2 us
    ppermute x8, starting transfers between devices, shifted(): lax.ppermute(value, axis, [(source, source + steps) for source in range(l...  12.6 us
    all_gather x1, waiting for transfers between devices, on_device(): lax.all_gather(spatial_weights, 'section', axis=0, tiled=True)  12.1 us
    ppermute x8, starting transfers between devices, with_halo(): lax.ppermute(head, axis, [((i + 1) % count, i) for i in range(ends)])  10.5 us
    dot_general x32, matrix products, forward_layer(): jnp.einsum('frwc,cd->frwd', padded[:, row_off:row_off + height, col_off:c...  8.6 us
  transfers between devices with their start and end apart: 26, of which 11 were waited for; matrix products, arithmetic and copies ran while one was open for 8% of the time, Pallas kernels for 0%

commit v1 on v0

--- a/solution.py
+++ b/solution.py
@@ -115,11 +115,42 @@
     return (jnp.stack(spatial_list), jnp.stack(temporal_list), new_grad)
 
 
+def gathered_kernels(spatial_weights, temporal_weights):
+    cores = lax.axis_size("tm")
+    blocks = lax.axis_size("section")
+    own = jnp.concatenate([spatial_weights[0], temporal_weights[0]], 0)
+    taps = own.shape[0] // cores
+    half = lax.dynamic_slice_in_dim(own, lax.axis_index("tm") * taps, taps, 0)
+    halves = lax.all_to_all(
+        jnp.broadcast_to(half[None], (blocks,) + half.shape), "section", 0, 0, tiled=True
+    )
+    both = lax.all_to_all(
+        jnp.broadcast_to(halves[None], (cores,) + halves.shape), "tm", 0, 0, tiled=True
+    )
+    whole = jnp.concatenate([both[core] for core in range(cores)], 1)
+    split = spatial_weights.shape[1]
+    return whole[:, :split], whole[:, split:]
+
+
+def summed_kernels(partial):
+    blocks, taps, chans, outs = partial.shape
+    cores, tiles = lax.axis_size("tm"), lax.axis_size("space")
+    part = partial.astype(jnp.bfloat16).reshape(blocks, cores, taps // cores, chans, outs)
+    part = lax.all_to_all(part.swapaxes(0, 1), "tm", 0, 0, tiled=True)
+    part = part.astype(jnp.float32).sum(0).astype(jnp.bfloat16)
+    part = lax.all_to_all(part, "section", 0, 0, tiled=True)
+    part = part.astype(jnp.float32).sum(0).astype(jnp.bfloat16)
+    part = lax.all_to_all(part.reshape(tiles, -1, outs), "space", 0, 0, tiled=True)
+    part = part.astype(jnp.float32).sum(0).astype(jnp.bfloat16)
+    whole = lax.all_to_all(
+        jnp.broadcast_to(part[None], (cores * tiles,) + part.shape),
+        ("tm", "space"), 0, 0, tiled=True,
+    )
+    return whole.reshape(taps, chans, outs).astype(jnp.float32)
+
+
 def on_device(video, cotangent, spatial_weights, temporal_weights):
-    spatial_all, temporal_all = (
-        lax.all_gather(spatial_weights, "section", axis=0, tiled=True),
-        lax.all_gather(temporal_weights, "section", axis=0, tiled=True),
-    )
+    spatial_all, temporal_all = gathered_kernels(spatial_weights, temporal_weights)
     blocks = spatial_all.shape[0]
     records = []
     inputs = video
@@ -148,15 +179,10 @@
         * video.shape[2]
     )
     factor = 1.0 / float(pixel_count) ** 0.5
-    spatial_stack = jnp.stack(spatial_out) * factor
-    temporal_stack = jnp.stack(temporal_out) * factor
-    spatial_sum, temporal_sum = lax.psum(
-        (spatial_stack, temporal_stack), ("section", "tm", "space")
-    )
-    own_block = lax.axis_index("section")
-    spatial_own = lax.dynamic_slice_in_dim(spatial_sum, own_block, 1, 0)
-    temporal_own = lax.dynamic_slice_in_dim(temporal_sum, own_block, 1, 0)
-    return (spatial_own, temporal_own, grad)
+    stacked = jnp.concatenate([jnp.stack(spatial_out), jnp.stack(temporal_out)], 1) * factor
+    own = summed_kernels(stacked)[None]
+    split = spatial_weights.shape[1]
+    return (own[:, :split], own[:, split:], grad)
 
 
 def solution(mesh):

time: 322 us -> 198 us (0.61)
  waiting for transfers between devices: 185 us -> 55.5 us
  starting transfers between devices: 61.1 us -> 89 us
  between operations: 15.6 us -> 2.19 us
  blocking collectives: 15.2 us -> 9.99 us
  matrix products: 34.6 us -> 30.2 us
    psum x1 -> x0, waiting for transfers between devices: 152 us -> none  [on_device(): lax.psum((spatial_stack, temporal_stack), ('section', 'tm', 'space'))]
    all_to_all x0 -> x4, starting transfers between devices: none -> 31.9 us  [the longest x1 19.2 us: summed_kernels(): part = lax.all_to_all(part, 'section', 0, 0, tiled=True)]
    all_to_all x0 -> x4, waiting for transfers between devices: none -> 27.9 us  [the longest x1 9.9 us: summed_kernels(): lax.all_to_all(jnp.broadcast_to(part[None], (cores * tiles,) + part.shape...]
    all_gather x1 -> x0, blocking collectives: 15.2 us -> none  [on_device(): lax.all_gather(temporal_weights, 'section', axis=0, tiled=True)]
    all_gather x1 -> x0, waiting for transfers between devices: 12.1 us -> none  [on_device(): lax.all_gather(spatial_weights, 'section', axis=0, tiled=True)]
    all_to_all x0 -> x2, blocking collectives: none -> 9.99 us  [the longest x1 5 us: summed_kernels(): part = lax.all_to_all(part.swapaxes(0, 1), 'tm', 0, 0, tiled=True)]
    ppermute x8, waiting for transfers between devices: 15.9 us -> 21 us  [with_halo(): lax.ppermute(head, axis, [((i + 1) % count, i) for i in range(ends)])]
    dynamic_slice x2 -> x0, local copies, waits for them, and re-layouts: 3.53 us -> none  [the longest x1 1.92 us: on_device(): spatial_own = lax.dynamic_slice_in_dim(spatial_sum, own_block, 1, 0)]
  transfers between devices with their start and end apart: 26 -> 28, of which waited for: 11 -> 18; matrix products, arithmetic and copies ran while one was open for 8% -> 12% of each run, Pallas kernels for 0% -> 0%
where the time goes in v1:
time: 198 us; the launch traced here: 197 us
  starting transfers between devices  89 us (45%)
  waiting for transfers between devices  55.5 us (28%)
  matrix products  30.2 us (15%)
  blocking collectives  9.99 us (5%)
  other arithmetic  5.36 us (3%)
  local copies, waits for them, and re-layouts  4.93 us (2%)
  between operations  2.19 us (1%)
    ppermute x8, starting transfers between devices, with_halo(): lax.ppermute(tail, axis, [(i, (i + 1) % count) for i in range(ends)])  35.7 us
    ppermute x8, waiting for transfers between devices, with_halo(): lax.ppermute(head, axis, [((i + 1) % count, i) for i in range(ends)])  21 us
    all_to_all x1, starting transfers between devices, summed_kernels(): part = lax.all_to_all(part, 'section', 0, 0, tiled=True)  19.2 us
    ppermute x8, starting transfers between devices, shifted(): lax.ppermute(value, axis, [(source, source + steps) for source in range(l...  11.1 us
    ppermute x8, starting transfers between devices, with_halo(): lax.ppermute(head, axis, [((i + 1) % count, i) for i in range(ends)])  10.3 us
    all_to_all x1, waiting for transfers between devices, summed_kernels(): lax.all_to_all(jnp.broadcast_to(part[None], (cores * tiles,) + part.shape...  9.9 us
    all_to_all x1, waiting for transfers between devices, summed_kernels(): part = lax.all_to_all(part, 'section', 0, 0, tiled=True)  9.25 us
    dot_general x36, matrix products, backward_layer(): jnp.einsum('frwd,cd->frwc', rimmed[:, 2 - row_off:2 - row_off + height, 2...  9.09 us
  transfers between devices with their start and end apart: 28, of which 18 were waited for; matrix products, arithmetic and copies ran while one was open for 12% of the time, Pallas kernels for 0%

profile of v1, /device:TPU:0, one launch (start us, length us, event | category | flops | bytes accessed | tf_op | source)
XLA Modules:
  0.0 197.1 jit_solution(5800896057886073124)
XLA Ops:
  2.8 5.2 %all-to-all-start = ((bf16[4,6,128,128]{3,2,1,0:T(8,128)(2,1)}), bf16[4,6,128,128]{3,2,1,0:T(8,128)(2,1)S(1)}, u32[]{:S(2)}, u32[]{:S(2)}) async-start(bf16[4,6,128,128]{3,2,1,0:T(8,128)(2,1)} %broadcast_in_dim.6), calls=%async_computation | async-start | bytes 1572864 | tf_op jit(solution)/shard_map/all_to_all | solution.py:124
  7.9 3.5 %collective-permute-start = (bf16[2,1,128,128]{3,2,1,0:T(8,128)(2,1)S(1)}, bf16[2,1,128,128]{3,2,1,0:T(8,128)(2,1)S(1)}, u32[]{:S(2)}, u32[]{:S(2)}) collective-permute-start(bf16[2,1,128,128]{3,2,1,0:T(8,128)(2,1)S(1)} %get-tuple-element.21), channel_id=1, source_target_pairs={{0,1},{1,2},{2,3},{3,8},{8,9},{9,10},{10,11},{11,16},{16,17},{17,1... | collective-permute-start | bytes 196616 | tf_op jit(solution)/shard_map/ppermute | solution.py:15
  13.4 4.8 %collective-permute-done.1 = bf16[2,1,128,128]{3,2,1,0:T(8,128)(2,1)S(1)} collective-permute-done((bf16[2,1,128,128]{3,2,1,0:T(8,128)(2,1)S(1)}, bf16[2,1,128,128]{3,2,1,0:T(8,128)(2,1)S(1)}, u32[]{:S(2)}, u32[]{:S(2)}) %collective-permute-start.1) | collective-permute-done | bytes 65568 | tf_op jit(solution)/shard_map/ppermute | solution.py:17
  18.3 1.9 all-to-all-done
  20.5 5.0 %all_to_all.30 = bf16[2,4,6,128,128]{4,3,2,1,0:T(8,128)(2,1)S(1)} all-to-all(bf16[2,4,6,128,128]{4,3,2,1,0:T(8,128)(2,1)S(1)} %broadcast_in_dim.7), channel_id=1, replica_groups=mesh['section'=4,'tm'=2,'space'=4] {'tm'}, dimensions={0} | all-to-all | bytes 3145728 | tf_op jit(solution)/shard_map/all_to_all | solution.py:127
  27.4 2.0 %collective-permute-start.3 = (bf16[2,2,128,128]{3,2,1,0:T(8,128)(2,1)S(1)}, bf16[2,2,128,128]{3,2,1,0:T(8,128)(2,1)S(1)}, u32[]{:S(2)}, u32[]{:S(2)}) collective-permute-start(bf16[2,2,128,128]{3,2,1,0:T(8,128)(2,1)S(1)} %get-tuple-element.23), channel_id=1, source_target_pairs={{0,4},{1,5},{2,6},{3,7},{8,12},{9,13},{10,14},{11,15},{16,20},{17,... | collective-permute-start | bytes 393224 | tf_op jit(solution)/shard_map/ppermute | solution.py:27
  30.8 2.1 %collective-permute-start.4 = (bf16[2,1,128,128]{3,2,1,0:T(8,128)(2,1)S(1)}, bf16[2,1,128,128]{3,2,1,0:T(8,128)(2,1)S(1)}, u32[]{:S(2)}, u32[]{:S(2)}) collective-permute-start(bf16[2,1,128,128]{3,2,1,0:T(8,128)(2,1)S(1)} %get-tuple-element.17), channel_id=1, source_target_pairs={{0,1},{1,2},{2,3},{3,8},{8,9},{9,10},{10,11},{11,16},{16,17},{17,1... | collective-permute-start | bytes 196616 | tf_op jit(solution)/shard_map/ppermute | solution.py:15
  35.5 4.9 %collective-permute-done.5 = bf16[2,1,128,128]{3,2,1,0:T(8,128)(2,1)S(1)} collective-permute-done((bf16[2,1,128,128]{3,2,1,0:T(8,128)(2,1)S(1)}, bf16[2,1,128,128]{3,2,1,0:T(8,128)(2,1)S(1)}, u32[]{:S(2)}, u32[]{:S(2)}) %collective-permute-start.5) | collective-permute-done | bytes 65568 | tf_op jit(solution)/shard_map/ppermute | solution.py:17
  44.8 3.7 %collective-permute-start.7 = (bf16[2,1,128,128]{3,2,1,0:T(8,128)(2,1)S(1)}, bf16[2,1,128,128]{3,2,1,0:T(8,128)(2,1)S(1)}, u32[]{:S(2)}, u32[]{:S(2)}) collective-permute-start(bf16[2,1,128,128]{3,2,1,0:T(8,128)(2,1)S(1)} %get-tuple-element.15), channel_id=1, source_target_pairs={{0,1},{1,2},{2,3},{3,8},{8,9},{9,10},{10,11},{11,16},{16,17},{17,1... | collective-permute-start | bytes 196616 | tf_op jit(solution)/shard_map/ppermute | solution.py:15
  50.4 5.7 %collective-permute-done.8 = bf16[2,1,128,128]{3,2,1,0:T(8,128)(2,1)S(1)} collective-permute-done((bf16[2,1,128,128]{3,2,1,0:T(8,128)(2,1)S(1)}, bf16[2,1,128,128]{3,2,1,0:T(8,128)(2,1)S(1)}, u32[]{:S(2)}, u32[]{:S(2)}) %collective-permute-start.8) | collective-permute-done | bytes 65568 | tf_op jit(solution)/shard_map/ppermute | solution.py:17
  60.4 3.9 %collective-permute-start.10 = (bf16[2,1,128,128]{3,2,1,0:T(8,128)(2,1)S(1)}, bf16[2,1,128,128]{3,2,1,0:T(8,128)(2,1)S(1)}, u32[]{:S(2)}, u32[]{:S(2)}) collective-permute-start(bf16[2,1,128,128]{3,2,1,0:T(8,128)(2,1)S(1)} %get-tuple-element.13), channel_id=1, source_target_pairs={{0,1},{1,2},{2,3},{3,8},{8,9},{9,10},{10,11},{11,16},{16,17},{17,1... | collective-permute-start | bytes 196616 | tf_op jit(solution)/shard_map/ppermute | solution.py:15
  66.3 5.6 %collective-permute-done.11 = bf16[2,1,128,128]{3,2,1,0:T(8,128)(2,1)S(1)} collective-permute-done((bf16[2,1,128,128]{3,2,1,0:T(8,128)(2,1)S(1)}, bf16[2,1,128,128]{3,2,1,0:T(8,128)(2,1)S(1)}, u32[]{:S(2)}, u32[]{:S(2)}) %collective-permute-start.11) | collective-permute-done | bytes 65568 | tf_op jit(solution)/shard_map/ppermute | solution.py:17
  75.4 4.6 %collective-permute-start.12 = (bf16[2,1,128,128]{3,2,1,0:T(8,128)(2,1)S(1)}, bf16[2,1,128,128]{3,2,1,0:T(8,128)(2,1)S(1)}, u32[]{:S(2)}, u32[]{:S(2)}) collective-permute-start(bf16[2,1,128,128]{3,2,1,0:T(8,128)(2,1)S(1)} %get-tuple-element.11), channel_id=1, source_target_pairs={{0,1},{1,2},{2,3},{3,8},{8,9},{9,10},{10,11},{11,16},{16,17},{17,1... | collective-permute-start | bytes 196616 | tf_op jit(solution)/shard_map/ppermute | solution.py:15
  90.5 4.6 %collective-permute-start.15 = (bf16[2,1,128,128]{3,2,1,0:T(8,128)(2,1)S(1)}, bf16[2,1,128,128]{3,2,1,0:T(8,128)(2,1)S(1)}, u32[]{:S(2)}, u32[]{:S(2)}) collective-permute-start(bf16[2,1,128,128]{3,2,1,0:T(8,128)(2,1)S(1)} %get-tuple-element.9), channel_id=1, source_target_pairs={{0,1},{1,2},{2,3},{3,8},{8,9},{9,10},{10,11},{11,16},{16,17},{17,1... | collective-permute-start | bytes 196616 | tf_op jit(solution)/shard_map/ppermute | solution.py:15
  104.2 5.4 %collective-permute-start.18 = (bf16[2,1,128,128]{3,2,1,0:T(8,128)(2,1)S(1)}, bf16[2,1,128,128]{3,2,1,0:T(8,128)(2,1)S(1)}, u32[]{:S(2)}, u32[]{:S(2)}) collective-permute-start(bf16[2,1,128,128]{3,2,1,0:T(8,128)(2,1)S(1)} %get-tuple-element.7), channel_id=1, source_target_pairs={{0,1},{1,2},{2,3},{3,8},{8,9},{9,10},{10,11},{11,16},{16,17},{17,1... | collective-permute-start | bytes 196616 | tf_op jit(solution)/shard_map/ppermute | solution.py:15
  119.3 7.9 %collective-permute-start.22 = (bf16[2,1,128,128]{3,2,1,0:T(8,128)(2,1)}, bf16[2,1,128,128]{3,2,1,0:T(8,128)(2,1)}, u32[]{:S(2)}, u32[]{:S(2)}) collective-permute-start(bf16[2,1,128,128]{3,2,1,0:T(8,128)(2,1)} %get-tuple-element.5), channel_id=1, source_target_pairs={{0,1},{1,2},{2,3},{3,8},{8,9},{9,10},{10,11},{11,16},{16,17},{17,1... | collective-permute-start | bytes 196616 | tf_op jit(solution)/shard_map/ppermute | solution.py:15
  129.6 5.0 %all_to_all.31 = bf16[2,4,6,128,128]{4,3,2,1,0:T(8,128)(2,1)S(1)} all-to-all(bf16[2,4,6,128,128]{4,3,2,1,0:T(8,128)(2,1)S(1)} %bitcast.876), channel_id=1, replica_groups=mesh['section'=4,'tm'=2,'space'=4] {'tm'}, dimensions={0} | all-to-all | bytes 3145728 | tf_op jit(solution)/shard_map/all_to_all | solution.py:139
  136.1 19.2 %all-to-all-start.3 = ((bf16[4,6,128,128]{3,2,1,0:T(8,128)(2,1)}), bf16[4,6,128,128]{3,2,1,0:T(8,128)(2,1)S(1)}, u32[]{:S(2)}, u32[]{:S(2)}) async-start(bf16[4,6,128,128]{3,2,1,0:T(8,128)(2,1)} %reduce_sum.36), calls=%async_computation.3 | async-start | bytes 1572864 | tf_op jit(solution)/shard_map/all_to_all | solution.py:141
  157.9 9.3 %all-to-all-done.3 = bf16[4,6,128,128]{3,2,1,0:T(8,128)(2,1)S(1)} async-done(((bf16[4,6,128,128]{3,2,1,0:T(8,128)(2,1)}), bf16[4,6,128,128]{3,2,1,0:T(8,128)(2,1)S(1)}, u32[]{:S(2)}, u32[]{:S(2)}) %all-to-all-start.3) | async-done | bytes 786464 | tf_op jit(solution)/shard_map/all_to_all | solution.py:141
  168.0 4.0 %all-to-all-start.4 = ((bf16[4,192,128]{2,1,0:T(8,128)(2,1)}), bf16[4,192,128]{2,1,0:T(8,128)(2,1)S(1)}, u32[]{:S(2)}, u32[]{:S(2)}) async-start(bf16[4,192,128]{2,1,0:T(8,128)(2,1)} %bitcast.373), calls=%async_computation.4 | async-start | bytes 393216 | tf_op jit(solution)/shard_map/all_to_all | solution.py:143
  172.4 6.9 %all-to-all-done.4 = bf16[4,192,128]{2,1,0:T(8,128)(2,1)S(1)} async-done(((bf16[4,192,128]{2,1,0:T(8,128)(2,1)}), bf16[4,192,128]{2,1,0:T(8,128)(2,1)S(1)}, u32[]{:S(2)}, u32[]{:S(2)}) %all-to-all-start.4) | async-done | bytes 196640 | tf_op jit(solution)/shard_map/all_to_all | solution.py:143
  180.1 3.5 %all-to-all-start.5 = ((bf16[8,192,128]{2,1,0:T(8,128)(2,1)}), bf16[8,192,128]{2,1,0:T(8,128)(2,1)S(1)}, u32[]{:S(2)}, u32[]{:S(2)}) async-start(bf16[8,192,128]{2,1,0:T(8,128)(2,1)} %broadcast_in_dim.8), calls=%async_computation.5 | async-start | bytes 786432 | tf_op jit(solution)/shard_map/all_to_all | solution.py:145
  184.0 1.7 fusion.39
  185.7 9.9 %all-to-all-done.5 = bf16[8,192,128]{2,1,0:T(8,128)(2,1)S(1)} async-done(((bf16[8,192,128]{2,1,0:T(8,128)(2,1)}), bf16[8,192,128]{2,1,0:T(8,128)(2,1)S(1)}, u32[]{:S(2)}, u32[]{:S(2)}) %all-to-all-start.5) | async-done | bytes 393248 | tf_op jit(solution)/shard_map/all_to_all | solution.py:145
  (222 shorter events, 64.7 us)
Async XLA Ops:
  2.8 17.4 %all-to-all-start = ((bf16[4,6,128,128]{3,2,1,0:T(8,128)(2,1)}), bf16[4,6,128,128]{3,2,1,0:T(8,128)(2,1)S(1)}, u32[]{:S(2)}, u32[]{:S(2)}) async-start(bf16[4,6,128,128]{3,2,1,0:T(8,128)(2,1)} %broadcast_in_dim.6), calls=%async_computation | async-start | bytes 1572864 | tf_op jit(solution)/shard_map/all_to_all | solution.py:124
  7.9 5.4 %collective-permute-start = (bf16[2,1,128,128]{3,2,1,0:T(8,128)(2,1)S(1)}, bf16[2,1,128,128]{3,2,1,0:T(8,128)(2,1)S(1)}, u32[]{:S(2)}, u32[]{:S(2)}) collective-permute-start(bf16[2,1,128,128]{3,2,1,0:T(8,128)(2,1)S(1)} %get-tuple-element.21), channel_id=1, source_target_pairs={{0,1},{1,2},{2,3},{3,8},{8,9},{9,10},{10,11},{11,16},{16,17},{17,1... | collective-permute-start | bytes 196616 | tf_op jit(solution)/shard_map/ppermute | solution.py:15
  11.4 6.7 %collective-permute-start.1 = (bf16[2,1,128,128]{3,2,1,0:T(8,128)(2,1)S(1)}, bf16[2,1,128,128]{3,2,1,0:T(8,128)(2,1)S(1)}, u32[]{:S(2)}, u32[]{:S(2)}) collective-permute-start(bf16[2,1,128,128]{3,2,1,0:T(8,128)(2,1)S(1)} %get-tuple-element.22), channel_id=1, source_target_pairs={{1,0},{2,1},{3,2},{8,3},{9,8},{10,9},{11,10},{16,11},{17,16},{18,1... | collective-permute-start | bytes 196616 | tf_op jit(solution)/shard_map/ppermute | solution.py:17
  30.8 4.7 %collective-permute-start.4 = (bf16[2,1,128,128]{3,2,1,0:T(8,128)(2,1)S(1)}, bf16[2,1,128,128]{3,2,1,0:T(8,128)(2,1)S(1)}, u32[]{:S(2)}, u32[]{:S(2)}) collective-permute-start(bf16[2,1,128,128]{3,2,1,0:T(8,128)(2,1)S(1)} %get-tuple-element.17), channel_id=1, source_target_pairs={{0,1},{1,2},{2,3},{3,8},{8,9},{9,10},{10,11},{11,16},{16,17},{17,1... | collective-permute-start | bytes 196616 | tf_op jit(solution)/shard_map/ppermute | solution.py:15
  32.9 7.5 %collective-permute-start.5 = (bf16[2,1,128,128]{3,2,1,0:T(8,128)(2,1)S(1)}, bf16[2,1,128,128]{3,2,1,0:T(8,128)(2,1)S(1)}, u32[]{:S(2)}, u32[]{:S(2)}) collective-permute-start(bf16[2,1,128,128]{3,2,1,0:T(8,128)(2,1)S(1)} %get-tuple-element.18), channel_id=1, source_target_pairs={{1,0},{2,1},{3,2},{8,3},{9,8},{10,9},{11,10},{16,11},{17,16},{18,1... | collective-permute-start | bytes 196616 | tf_op jit(solution)/shard_map/ppermute | solution.py:17
  34.2 31.5 %collective-permute-start.2 = (bf16[2,2,128,128]{3,2,1,0:T(8,128)(2,1)S(1)}, bf16[2,2,128,128]{3,2,1,0:T(8,128)(2,1)S(1)}, u32[]{:S(2)}, u32[]{:S(2)}) collective-permute-start(bf16[2,2,128,128]{3,2,1,0:T(8,128)(2,1)S(1)} %copy-done.3), channel_id=1, source_target_pairs={{4,0},{5,1},{6,2},{7,3},{12,8},{13,9},{14,10},{15,11},{20,16},{21,... | collective-permute-start | bytes 393224 | tf_op jit(solution)/shard_map/ppermute | solution.py:27
  44.8 5.6 %collective-permute-start.7 = (bf16[2,1,128,128]{3,2,1,0:T(8,128)(2,1)S(1)}, bf16[2,1,128,128]{3,2,1,0:T(8,128)(2,1)S(1)}, u32[]{:S(2)}, u32[]{:S(2)}) collective-permute-start(bf16[2,1,128,128]{3,2,1,0:T(8,128)(2,1)S(1)} %get-tuple-element.15), channel_id=1, source_target_pairs={{0,1},{1,2},{2,3},{3,8},{8,9},{9,10},{10,11},{11,16},{16,17},{17,1... | collective-permute-start | bytes 196616 | tf_op jit(solution)/shard_map/ppermute | solution.py:15
  48.5 7.6 %collective-permute-start.8 = (bf16[2,1,128,128]{3,2,1,0:T(8,128)(2,1)S(1)}, bf16[2,1,128,128]{3,2,1,0:T(8,128)(2,1)S(1)}, u32[]{:S(2)}, u32[]{:S(2)}) collective-permute-start(bf16[2,1,128,128]{3,2,1,0:T(8,128)(2,1)S(1)} %get-tuple-element.16), channel_id=1, source_target_pairs={{1,0},{2,1},{3,2},{8,3},{9,8},{10,9},{11,10},{16,11},{17,16},{18,1... | collective-permute-start | bytes 196616 | tf_op jit(solution)/shard_map/ppermute | solution.py:17
  60.4 5.8 %collective-permute-start.10 = (bf16[2,1,128,128]{3,2,1,0:T(8,128)(2,1)S(1)}, bf16[2,1,128,128]{3,2,1,0:T(8,128)(2,1)S(1)}, u32[]{:S(2)}, u32[]{:S(2)}) collective-permute-start(bf16[2,1,128,128]{3,2,1,0:T(8,128)(2,1)S(1)} %get-tuple-element.13), channel_id=1, source_target_pairs={{0,1},{1,2},{2,3},{3,8},{8,9},{9,10},{10,11},{11,16},{16,17},{17,1... | collective-permute-start | bytes 196616 | tf_op jit(solution)/shard_map/ppermute | solution.py:15
  64.4 7.5 %collective-permute-start.11 = (bf16[2,1,128,128]{3,2,1,0:T(8,128)(2,1)S(1)}, bf16[2,1,128,128]{3,2,1,0:T(8,128)(2,1)S(1)}, u32[]{:S(2)}, u32[]{:S(2)}) collective-permute-start(bf16[2,1,128,128]{3,2,1,0:T(8,128)(2,1)S(1)} %get-tuple-element.14), channel_id=1, source_target_pairs={{1,0},{2,1},{3,2},{8,3},{9,8},{10,9},{11,10},{16,11},{17,16},{18,1... | collective-permute-start | bytes 196616 | tf_op jit(solution)/shard_map/ppermute | solution.py:17
  74.1 9.3 %collective-permute-start.13 = (bf16[2,1,128,128]{3,2,1,0:T(8,128)(2,1)S(1)}, bf16[2,1,128,128]{3,2,1,0:T(8,128)(2,1)S(1)}, u32[]{:S(2)}, u32[]{:S(2)}) collective-permute-start(bf16[2,1,128,128]{3,2,1,0:T(8,128)(2,1)S(1)} %get-tuple-element.12), channel_id=1, source_target_pairs={{1,0},{2,1},{3,2},{8,3},{9,8},{10,9},{11,10},{16,11},{17,16},{18,1... | collective-permute-start | bytes 196616 | tf_op jit(solution)/shard_map/ppermute | solution.py:17
  75.4 8.0 %collective-permute-start.12 = (bf16[2,1,128,128]{3,2,1,0:T(8,128)(2,1)S(1)}, bf16[2,1,128,128]{3,2,1,0:T(8,128)(2,1)S(1)}, u32[]{:S(2)}, u32[]{:S(2)}) collective-permute-start(bf16[2,1,128,128]{3,2,1,0:T(8,128)(2,1)S(1)} %get-tuple-element.11), channel_id=1, source_target_pairs={{0,1},{1,2},{2,3},{3,8},{8,9},{9,10},{10,11},{11,16},{16,17},{17,1... | collective-permute-start | bytes 196616 | tf_op jit(solution)/shard_map/ppermute | solution.py:15
  81.9 5.6 %collective-permute-start.21 = (bf16[2,2,128,128]{3,2,1,0:T(8,128)(2,1)S(1)}, bf16[2,2,128,128]{3,2,1,0:T(8,128)(2,1)S(1)}, u32[]{:S(2)}, u32[]{:S(2)}) collective-permute-start(bf16[2,2,128,128]{3,2,1,0:T(8,128)(2,1)S(1)} %get-tuple-element.29), channel_id=1, source_target_pairs={{0,4},{1,5},{2,6},{3,7},{8,12},{9,13},{10,14},{11,15},{16,20},{17,... | collective-permute-start | bytes 393224 | tf_op jit(solution)/shard_map/ppermute | solution.py:27
  85.3 3.2 %collective-permute-start.14 = (bf16[2,2,128,128]{3,2,1,0:T(8,128)(2,1)S(1)}, bf16[2,2,128,128]{3,2,1,0:T(8,128)(2,1)S(1)}, u32[]{:S(2)}, u32[]{:S(2)}) collective-permute-start(bf16[2,2,128,128]{3,2,1,0:T(8,128)(2,1)S(1)} %fusion.36), channel_id=1, source_target_pairs={{4,0},{5,1},{6,2},{7,3},{12,8},{13,9},{14,10},{15,11},{20,16},{21,... | collective-permute-start | bytes 393224 | tf_op jit(solution)/shard_map/ppermute | solution.py:27
  89.2 7.7 %collective-permute-start.16 = (bf16[2,1,128,128]{3,2,1,0:T(8,128)(2,1)S(1)}, bf16[2,1,128,128]{3,2,1,0:T(8,128)(2,1)S(1)}, u32[]{:S(2)}, u32[]{:S(2)}) collective-permute-start(bf16[2,1,128,128]{3,2,1,0:T(8,128)(2,1)S(1)} %get-tuple-element.10), channel_id=1, source_target_pairs={{1,0},{2,1},{3,2},{8,3},{9,8},{10,9},{11,10},{16,11},{17,16},{18,1... | collective-permute-start | bytes 196616 | tf_op jit(solution)/shard_map/ppermute | solution.py:17
  90.5 6.7 %collective-permute-start.15 = (bf16[2,1,128,128]{3,2,1,0:T(8,128)(2,1)S(1)}, bf16[2,1,128,128]{3,2,1,0:T(8,128)(2,1)S(1)}, u32[]{:S(2)}, u32[]{:S(2)}) collective-permute-start(bf16[2,1,128,128]{3,2,1,0:T(8,128)(2,1)S(1)} %get-tuple-element.9), channel_id=1, source_target_pairs={{0,1},{1,2},{2,3},{3,8},{8,9},{9,10},{10,11},{11,16},{16,17},{17,1... | collective-permute-start | bytes 196616 | tf_op jit(solution)/shard_map/ppermute | solution.py:15
  99.0 3.2 %collective-permute-start.17 = (bf16[2,2,128,128]{3,2,1,0:T(8,128)(2,1)S(1)}, bf16[2,2,128,128]{3,2,1,0:T(8,128)(2,1)S(1)}, u32[]{:S(2)}, u32[]{:S(2)}) collective-permute-start(bf16[2,2,128,128]{3,2,1,0:T(8,128)(2,1)S(1)} %fusion.37), channel_id=1, source_target_pairs={{4,0},{5,1},{6,2},{7,3},{12,8},{13,9},{14,10},{15,11},{20,16},{21,... | collective-permute-start | bytes 393224 | tf_op jit(solution)/shard_map/ppermute | solution.py:27
  102.9 8.6 %collective-permute-start.19 = (bf16[2,1,128,128]{3,2,1,0:T(8,128)(2,1)S(1)}, bf16[2,1,128,128]{3,2,1,0:T(8,128)(2,1)S(1)}, u32[]{:S(2)}, u32[]{:S(2)}) collective-permute-start(bf16[2,1,128,128]{3,2,1,0:T(8,128)(2,1)S(1)} %get-tuple-element.8), channel_id=1, source_target_pairs={{1,0},{2,1},{3,2},{8,3},{9,8},{10,9},{11,10},{16,11},{17,16},{18,1... | collective-permute-start | bytes 196616 | tf_op jit(solution)/shard_map/ppermute | solution.py:17
  104.2 7.3 %collective-permute-start.18 = (bf16[2,1,128,128]{3,2,1,0:T(8,128)(2,1)S(1)}, bf16[2,1,128,128]{3,2,1,0:T(8,128)(2,1)S(1)}, u32[]{:S(2)}, u32[]{:S(2)}) collective-permute-start(bf16[2,1,128,128]{3,2,1,0:T(8,128)(2,1)S(1)} %get-tuple-element.7), channel_id=1, source_target_pairs={{0,1},{1,2},{2,3},{3,8},{8,9},{9,10},{10,11},{11,16},{16,17},{17,1... | collective-permute-start | bytes 196616 | tf_op jit(solution)/shard_map/ppermute | solution.py:15
  118.0 37.3 %collective-permute-start.23 = (bf16[2,1,128,128]{3,2,1,0:T(8,128)(2,1)}, bf16[2,1,128,128]{3,2,1,0:T(8,128)(2,1)}, u32[]{:S(2)}, u32[]{:S(2)}) collective-permute-start(bf16[2,1,128,128]{3,2,1,0:T(8,128)(2,1)} %get-tuple-element.6), channel_id=1, source_target_pairs={{1,0},{2,1},{3,2},{8,3},{9,8},{10,9},{11,10},{16,11},{17,16},{18,1... | collective-permute-start | bytes 196616 | tf_op jit(solution)/shard_map/ppermute | solution.py:17
  119.3 37.1 %collective-permute-start.22 = (bf16[2,1,128,128]{3,2,1,0:T(8,128)(2,1)}, bf16[2,1,128,128]{3,2,1,0:T(8,128)(2,1)}, u32[]{:S(2)}, u32[]{:S(2)}) collective-permute-start(bf16[2,1,128,128]{3,2,1,0:T(8,128)(2,1)} %get-tuple-element.5), channel_id=1, source_target_pairs={{0,1},{1,2},{2,3},{3,8},{8,9},{9,10},{10,11},{11,16},{16,17},{17,1... | collective-permute-start | bytes 196616 | tf_op jit(solution)/shard_map/ppermute | solution.py:15
  136.1 31.1 %all-to-all-start.3 = ((bf16[4,6,128,128]{3,2,1,0:T(8,128)(2,1)}), bf16[4,6,128,128]{3,2,1,0:T(8,128)(2,1)S(1)}, u32[]{:S(2)}, u32[]{:S(2)}) async-start(bf16[4,6,128,128]{3,2,1,0:T(8,128)(2,1)} %reduce_sum.36), calls=%async_computation.3 | async-start | bytes 1572864 | tf_op jit(solution)/shard_map/all_to_all | solution.py:141
  168.0 11.3 %all-to-all-start.4 = ((bf16[4,192,128]{2,1,0:T(8,128)(2,1)}), bf16[4,192,128]{2,1,0:T(8,128)(2,1)S(1)}, u32[]{:S(2)}, u32[]{:S(2)}) async-start(bf16[4,192,128]{2,1,0:T(8,128)(2,1)} %bitcast.373), calls=%async_computation.4 | async-start | bytes 393216 | tf_op jit(solution)/shard_map/all_to_all | solution.py:143
  180.1 15.5 %all-to-all-start.5 = ((bf16[8,192,128]{2,1,0:T(8,128)(2,1)}), bf16[8,192,128]{2,1,0:T(8,128)(2,1)S(1)}, u32[]{:S(2)}, u32[]{:S(2)}) async-start(bf16[8,192,128]{2,1,0:T(8,128)(2,1)} %broadcast_in_dim.8), calls=%async_computation.5 | async-start | bytes 786432 | tf_op jit(solution)/shard_map/all_to_all | solution.py:145
  (10 other events, 61.0 us)

commit v2 on v1

v2 whole, which is shorter than its diff:
```python
import functools

import jax
import jax.numpy as jnp
from jax import lax
from jax.experimental import pallas as pl
from jax.experimental.pallas import tpu as pltpu
from jax.sharding import PartitionSpec as P

F32 = jnp.float32
BF16 = jnp.bfloat16


def rolled(value, steps):
    return pltpu.roll(value, steps % value.shape[0], 0)


def dot_t(left, right):
    return lax.dot_general(left, right, (((1,), (1,)), ((), ())), preferred_element_type=F32)


def dot_first(left, right):
    return lax.dot_general(left, right, (((0,), (0,)), ((), ())), preferred_element_type=F32)


def kernel_of(w_ref, block, tap):
    taps = w_ref.shape[2]
    return w_ref[tap // taps, block, tap % taps]


def rows_of(w_ref, block, first, last):
    return jnp.concatenate([kernel_of(w_ref, block, tap) for tap in range(first, last)], 0)


def lanes_of(w_ref, block, order):
    return jnp.concatenate([kernel_of(w_ref, block, tap) for tap in order], 1)


def forward_kernel(
    geometry, place_ref, w_ref, own_ref, above_ref, below_ref, xo_ref, ho_ref, *rest
):
    blocks, cores, group, frames_in, rows_in, halo, tile, width = geometry
    d_refs = rest[:blocks]
    x_ref, h_ref, mask_ref = rest[blocks:]
    frames = cores * frames_in
    high = tile + 2 * halo
    chans = w_ref.shape[-1]
    own_rows, own_cols = (halo, halo + tile), (halo, width - halo)
    height, columns = place_ref[2], place_ref[3]
    row = place_ref[0] + lax.broadcasted_iota(jnp.int32, (high, width, chans), 0)
    col = place_ref[1] + lax.broadcasted_iota(jnp.int32, (high, width, chans), 1)
    inside = (row >= 0) & (row < height) & (col >= 0) & (col < columns)
    mask_ref[...] = jnp.where(inside, 1.0, 0.0).astype(F32)

    def keep(block, frame, value, first):
        triple = [rolled(value, 1), value, rolled(value, -1)]
        count = value.shape[0] // width
        both = jnp.concatenate([part.astype(BF16) for part in triple], 1)
        x_ref[frame, first : first + count] = both.reshape(count, width, 3 * chans)
        start = own_rows[0] - 1 - first
        cut = [
            part.reshape(count, width, chans)[
                start : start + tile + 2, own_cols[0] : own_cols[1]
            ].astype(BF16)
            for part in triple
        ]
        xo_ref[block, frame] = jnp.concatenate(cut, 2)

    for frame in range(frames):
        core, inner = divmod(frame, frames_in)
        pieces = [
            ref[core * group + unit, inner]
            for ref in (above_ref, own_ref, below_ref)
            for unit in range(group)
        ]
        whole = jnp.concatenate(pieces, 0).reshape(high * width, chans)
        keep(0, frame, whole.astype(F32), 0)

    for block in range(blocks):
        first, last = block + 1, high - block - 1
        count = last - first
        spatial = rows_of(w_ref, block, 0, 9)
        mask = mask_ref[first:last].reshape(count * width, chans)
        for frame in range(frames):
            taps = jnp.concatenate(
                [
                    x_ref[frame, first - 1 + ky : last - 1 + ky].reshape(count * width, 3 * chans)
                    for ky in range(3)
                ],
                1,
            )
            before = jnp.dot(taps, spatial, preferred_element_type=F32)
            sigma = 1.0 / (1.0 + jnp.exp(-before))
            hidden = before * sigma * mask
            slope = (sigma * (1.0 + before * (1.0 - sigma))) * mask
            h_ref[frame, first:last] = hidden.astype(BF16).reshape(count, width, chans)
            ho_ref[block, frame] = hidden.reshape(count, width, chans)[
                own_rows[0] - first : own_rows[1] - first, own_cols[0] : own_cols[1]
            ].astype(BF16)
            rim = block + 1
            d_refs[block][frame] = slope.reshape(count, width, chans)[
                own_rows[0] - rim - first : own_rows[1] + rim - first
            ]
        if block + 1 == blocks:
            break
        for frame in range(frames):
            offsets = [kt for kt in range(3) if frame + kt - 2 >= 0]
            timeline = jnp.concatenate(
                [
                    h_ref[frame + kt - 2, first:last].reshape(count * width, chans)
                    for kt in offsets
                ],
                1,
            )
            mixed = jnp.dot(
                timeline, rows_of(w_ref, block, 9 + offsets[0], 12), preferred_element_type=F32
            )
            old = x_ref[frame, first:last, :, chans : 2 * chans].astype(F32)
            new = old.reshape(count * width, chans) + mixed
            keep(block + 1, frame, new.astype(BF16).astype(F32), first)


def backward_kernel(geometry, factor, w_ref, own_ref, above_ref, below_ref, xo_ref, ho_ref, *rest):
    blocks, cores, group, frames_in, rows_in, halo, tile, width = geometry
    d_refs = rest[:blocks]
    grad_ref, out_ref, g_ref, da_ref, dao_ref, go_ref = rest[blocks:]
    frames = cores * frames_in
    chans = w_ref.shape[-1]
    rim = blocks
    own_cols = (halo, width - halo)
    per_core = w_ref.shape[2]
    pixels = tile * (own_cols[1] - own_cols[0])

    for frame in range(frames):
        core, inner = divmod(frame, frames_in)
        half = group // 2
        pieces = [above_ref[core * half + unit, inner] for unit in range(half)]
        pieces += [own_ref[core * group + unit, inner] for unit in range(group)]
        pieces += [below_ref[core * half + unit, inner] for unit in range(half)]
        g_ref[frame] = jnp.concatenate(pieces, 0)

    def put(block, tap, value):
        grad_ref[tap // per_core, block, tap % per_core] = (value * factor).astype(BF16)

    for block in reversed(range(blocks)):
        edge = block + 1
        first, last = rim - edge, rim + tile + edge
        count = last - first
        for frame in range(frames):
            go_ref[frame] = g_ref[frame, rim : rim + tile].astype(F32)[
                :, own_cols[0] : own_cols[1]
            ].astype(BF16)
            offsets = [kt for kt in (2, 1, 0) if frame + 2 - kt < frames]
            ahead = jnp.concatenate(
                [
                    g_ref[frame + 2 - kt, first:last].reshape(count * width, chans)
                    for kt in offsets
                ],
                1,
            )
            hidden = dot_t(ahead, lanes_of(w_ref, block, [9 + kt for kt in offsets]))
            slope = d_refs[block][frame].reshape(count * width, chans)
            value = (hidden * slope).astype(BF16).astype(F32)
            triple = [rolled(value, -1), value, rolled(value, 1)]
            both = jnp.concatenate([part.astype(BF16) for part in triple], 1)
            da_ref[frame, first:last] = both.reshape(count, width, 3 * chans)
            dao_ref[frame] = value.reshape(count, width, chans)[
                edge : edge + tile, own_cols[0] : own_cols[1]
            ].astype(BF16)
        for frame in range(frames):
            inner = count - 2
            taps = jnp.concatenate(
                [
                    da_ref[frame, first + 2 - ky : first + 2 - ky + inner].reshape(
                        inner * width, 3 * chans
                    )
                    for ky in range(3)
                ],
                1,
            )
            back = dot_t(taps, lanes_of(w_ref, block, range(9)))
            old = g_ref[frame, first + 1 : last - 1].astype(F32).reshape(inner * width, chans)
            new = (old + back).astype(BF16)
            if block:
                g_ref[frame, first + 1 : last - 1] = new.reshape(inner, width, chans)
            else:
                out_ref[frame] = new.astype(F32).reshape(inner, width, chans)[
                    :, own_cols[0] : own_cols[1]
                ].astype(BF16)
        slopes = dao_ref[...].reshape(frames * pixels, chans)
        for ky in range(3):
            taps = xo_ref[block, :, ky : ky + tile].reshape(frames * pixels, 3 * chans)
            sums = dot_first(slopes, taps)
            for kx in range(3):
                put(block, 3 * ky + kx, sums[:, kx * chans : (kx + 1) * chans])
        for kt in range(3):
            skip = 2 - kt
            later = go_ref[skip:].reshape((frames - skip) * pixels, chans)
            earlier = ho_ref[block, : frames - skip].reshape((frames - skip) * pixels, chans)
            put(block, 9 + kt, dot_first(later, earlier))


def gathered_kernels(spatial_weights, temporal_weights):
    cores = lax.axis_size("tm")
    blocks = lax.axis_size("section")
    own = jnp.concatenate([spatial_weights[0], temporal_weights[0]], 0)
    taps = own.shape[0] // cores
    half = lax.dynamic_slice_in_dim(own, lax.axis_index("tm") * taps, taps, 0)
    halves = lax.all_to_all(
        jnp.broadcast_to(half[None], (blocks,) + half.shape), "section", 0, 0, tiled=True
    )
    return lax.all_to_all(
        jnp.broadcast_to(halves[None], (cores,) + halves.shape), "tm", 0, 0, tiled=True
    )


def summed_kernels(part):
    cores, blocks, taps, outs, chans = part.shape
    tiles = lax.axis_size("space")
    part = lax.all_to_all(part, "tm", 0, 0, tiled=True)
    part = part.astype(F32).sum(0).astype(BF16)
    part = lax.all_to_all(part, "section", 0, 0, tiled=True)
    part = part.astype(F32).sum(0).astype(BF16)
    part = lax.all_to_all(part.reshape(tiles, -1, chans), "space", 0, 0, tiled=True)
    part = part.astype(F32).sum(0).astype(BF16)
    whole = lax.all_to_all(
        jnp.broadcast_to(part[None], (cores * tiles,) + part.shape),
        ("tm", "space"), 0, 0, tiled=True,
    )
    return whole.reshape(cores * taps, outs, chans)


def on_device(video, cotangent, spatial_weights, temporal_weights):
    blocks, cores, tiles = (lax.axis_size(name) for name in ("section", "tm", "space"))
    frames_in, rows_in, columns, chans = video.shape
    halo = 2 * blocks
    tile = halo
    group = tile // rows_in
    parties = cores * group
    own_width = columns // parties
    width = own_width + 2 * halo
    sets = None
    if tiles != group:
        sets = [
            [core * tiles + base + unit for core in range(cores) for unit in range(group)]
            for base in range(0, tiles, group)
        ]

    kernels = gathered_kernels(spatial_weights, temporal_weights)

    both = jnp.stack([video, cotangent])
    padded = jnp.pad(both, ((0, 0), (0, 0), (0, 0), (halo, halo), (0, 0)))
    windows = jnp.stack(
        [padded[:, :, :, unit * own_width : unit * own_width + width] for unit in range(parties)]
    )
    mine = lax.all_to_all(
        windows, ("tm", "space"), 0, 0, axis_index_groups=sets, tiled=True
    )
    own_video, own_cot = mine[:, 0], mine[:, 1]
    half = group // 2
    split = own_cot.reshape((cores, group) + own_cot.shape[1:])
    upper, lower = split[:, :half], split[:, half:]
    rows = blocks * tiles

    def sent(cot, step):
        flat = jnp.concatenate([own_video, cot.reshape((cores * half,) + own_cot.shape[1:])], 0)
        pairs = [(i, i + step) for i in range(rows) if 0 <= i + step < rows]
        got = lax.ppermute(flat, ("section", "space"), pairs)
        return got[:parties], got[parties:]

    video_above, cot_above = sent(lower, group)
    video_below, cot_below = sent(upper, -group)

    place = lax.axis_index("space")
    band = (lax.axis_index("section") * tiles + place) // group
    unit = lax.axis_index("tm") * group + place % group
    total_rows = blocks * tiles * rows_in
    corner = jnp.stack(
        [band * tile - halo, unit * own_width - halo, total_rows, columns]
    ).astype(jnp.int32)
    geometry = (blocks, cores, group, frames_in, rows_in, halo, tile, width)
    frames = cores * frames_in
    high = tile + 2 * halo
    vmem = pl.BlockSpec(memory_space=pltpu.VMEM)
    params = pltpu.CompilerParams(vmem_limit_bytes=56 * 2**20)
    saved = [
        jax.ShapeDtypeStruct((frames, tile + 2 * block + 2, width, chans), F32)
        for block in range(blocks)
    ]
    features, hidden, *slopes = pl.pallas_call(
        functools.partial(forward_kernel, geometry),
        name="forward",
        in_specs=[pl.BlockSpec(memory_space=pltpu.SMEM)] + [vmem] * 4,
        out_specs=[vmem] * (2 + blocks),
        out_shape=[
            jax.ShapeDtypeStruct((blocks, frames, tile + 2, own_width, 3 * chans), BF16),
            jax.ShapeDtypeStruct((blocks, frames, tile, own_width, chans), BF16),
        ]
        + saved,
        scratch_shapes=[
            pltpu.VMEM((frames, high, width, 3 * chans), BF16),
            pltpu.VMEM((frames, high, width, chans), BF16),
            pltpu.VMEM((high, width, chans), F32),
        ],
        compiler_params=params,
    )(corner, kernels, own_video, video_above, video_below)

    pixel_count = frames * total_rows * columns
    factor = 1.0 / float(pixel_count) ** 0.5
    partial, tile_grad = pl.pallas_call(
        functools.partial(backward_kernel, geometry, factor),
        name="backward",
        in_specs=[vmem] * (6 + blocks),
        out_specs=[vmem] * 2,
        out_shape=[
            jax.ShapeDtypeStruct(kernels.shape, BF16),
            jax.ShapeDtypeStruct((frames, tile, own_width, chans), BF16),
        ],
        scratch_shapes=[
            pltpu.VMEM((frames, tile + 2 * blocks, width, chans), BF16),
            pltpu.VMEM((frames, tile + 2 * blocks, width, 3 * chans), BF16),
            pltpu.VMEM((frames, tile, own_width, chans), BF16),
            pltpu.VMEM((frames, tile, own_width, chans), BF16),
        ],
        compiler_params=params,
    )(kernels, own_cot, cot_above, cot_below, features, hidden, *slopes)

    back = tile_grad.reshape(cores, frames_in, group, rows_in, own_width, chans)
    back = back.swapaxes(1, 2).reshape(parties, frames_in, rows_in, own_width, chans)
    back = lax.all_to_all(back, ("tm", "space"), 0, 0, axis_index_groups=sets, tiled=True)
    grad_video = back.transpose(1, 2, 0, 3, 4).reshape(video.shape)

    own = summed_kernels(partial).swapaxes(1, 2).astype(F32)[None]
    count = spatial_weights.shape[1]
    return own[:, :count], own[:, count:], grad_video


def solution(mesh):
    return jax.shard_map(
        on_device,
        mesh=mesh,
        in_specs=(
            P("tm", ("section", "space"), None, None),
            P("tm", ("section", "space"), None, None),
            P("section", None, None, None),
            P("section", None, None, None),
        ),
        out_specs=(
            P("section", None, None, None),
            P("section", None, None, None),
            P("tm", ("section", "space"), None, None),
        ),
        check_vma=False,
    )
```

time: 198 us -> 147 us (0.74)
  starting transfers between devices: 89 us -> 29.8 us
  matrix products: 30.2 us -> 0 us
  Pallas kernels: 0 us -> 20.8 us
  blocking collectives: 9.99 us -> 26.6 us
  waiting for transfers between devices: 55.5 us -> 46.4 us
  local copies, waits for them, and re-layouts: 4.93 us -> 12.8 us
  other arithmetic: 5.36 us -> 8.51 us
    ppermute x24 -> x2, starting transfers between devices: 57.1 us -> 5.87 us  [sent(): got = lax.ppermute(flat, ('section', 'space'), pairs)]
    dot_general x141 -> x0, matrix products: 30.2 us -> none  [the longest x36 9.09 us: backward_layer(): jnp.einsum('frwd,cd->frwc', rimmed[:, 2 - row_off:2 - row_off + height, 2...]
    ppermute x24 -> x2, waiting for transfers between devices: 27.5 us -> 3.2 us  [sent(): got = lax.ppermute(flat, ('section', 'space'), pairs)]
    pallas_call x0 -> x2, Pallas kernels: none -> 20.8 us  [the longest x1 10.5 us: on_device(): pl.pallas_call(functools.partial(forward_kernel, geometry), name='forward...]
    all_to_all x2, blocking collectives: 9.99 us -> 26.6 us  [the longest x1 20.4 us: summed_kernels(): part = lax.all_to_all(part, 'section', 0, 0, tiled=True)]
    all_to_all x2 -> x4, waiting for transfers between devices: 16.2 us -> 27.2 us  [the longest x1 14.8 us: on_device(): lax.all_to_all(windows, ('tm', 'space'), 0, 0, axis_index_groups=sets, ti...]
    all_to_all x2 -> x4, starting transfers between devices: 23.2 us -> 16.7 us  [the longest x1 6.33 us: on_device(): lax.all_to_all(windows, ('tm', 'space'), 0, 0, axis_index_groups=sets, ti...]
    unnamed x0 -> x6, other arithmetic: none -> 5.4 us
  transfers between devices with their start and end apart: 28 -> 8, of which waited for: 18 -> 6; matrix products, arithmetic and copies ran while one was open for 12% -> 5% of each run, Pallas kernels for 0% -> 0%
where the time goes in v2:
time: 147 us; the launch traced here: 146 us
  waiting for transfers between devices  46.4 us (32%)
  starting transfers between devices  29.8 us (20%)
  blocking collectives  26.6 us (18%)
  Pallas kernels  20.8 us (14%)
  local copies, waits for them, and re-layouts  12.8 us (9%)
  other arithmetic  8.51 us (6%)
    all_to_all x1, blocking collectives, summed_kernels(): part = lax.all_to_all(part, 'section', 0, 0, tiled=True)  20.4 us
    all_to_all x1, waiting for transfers between devices, on_device(): lax.all_to_all(windows, ('tm', 'space'), 0, 0, axis_index_groups=sets, ti...  14.8 us
    all_to_all x1, waiting for transfers between devices, summed_kernels(): lax.all_to_all(jnp.broadcast_to(part[None], (cores * tiles,) + part.shape...  11.3 us
    pallas_call x1, Pallas kernels, on_device(): pl.pallas_call(functools.partial(forward_kernel, geometry), name='forward...  10.5 us
    pallas_call x1, Pallas kernels, on_device(): pl.pallas_call(functools.partial(backward_kernel, geometry, factor), name...  10.4 us
    all_to_all x1, waiting for transfers between devices, on_device(): lax.all_to_all(back, ('tm', 'space'), 0, 0, axis_index_groups=sets, tiled...  6.83 us
    all_to_all x1, starting transfers between devices, on_device(): lax.all_to_all(windows, ('tm', 'space'), 0, 0, axis_index_groups=sets, ti...  6.33 us
    all_to_all x1, blocking collectives, summed_kernels(): part = lax.all_to_all(part, 'tm', 0, 0, tiled=True)  6.15 us
  transfers between devices with their start and end apart: 8, of which 6 were waited for; matrix products, arithmetic and copies ran while one was open for 5% of the time, Pallas kernels for 0%

profile of v2, /device:TPU:0, one launch (start us, length us, event | category | flops | bytes accessed | tf_op | source)
XLA Modules:
  0.0 145.7 jit_solution(1714053902372114966)
XLA Ops:
  2.3 1.4 fusion.7
  3.7 1.5 %fusion.10 = bf16[8,2,2,2,32,128]{5,4,3,2,1,0:T(8,128)(2,1)} fusion(bf16[8,2,2,2,32,128]{5,4,3,2,1,0:T(8,128)(2,1)} %fusion.7, bf16[1,2,2,128,128]{4,3,2,1,0:T(8,128)(2,1)} %bitcast.72, bf16[1,2,2,128,128]{4,3,2,1,0:T(8,128)(2,1)} %bitcast.65), kind=kLoop, calls=%fused_computation.31 | loop fusion | flops 131072 | bytes 327680
  8.4 6.3 %all-to-all-start.2 = ((bf16[8,2,2,2,32,128]{5,4,3,2,1,0:T(8,128)(2,1)}), bf16[8,2,2,2,32,128]{5,4,3,2,1,0:T(8,128)(2,1)S(1)}, u32[]{:S(2)}, u32[]{:S(2)}) async-start(bf16[8,2,2,2,32,128]{5,4,3,2,1,0:T(8,128)(2,1)} %fusion.4), calls=%async_computation.2 | async-start | bytes 1048576 | tf_op jit(solution)/shard_map/all_to_all | solution.py:256
  14.8 14.8 %all-to-all-done.2 = bf16[8,2,2,2,32,128]{5,4,3,2,1,0:T(8,128)(2,1)S(1)} async-done(((bf16[8,2,2,2,32,128]{5,4,3,2,1,0:T(8,128)(2,1)}), bf16[8,2,2,2,32,128]{5,4,3,2,1,0:T(8,128)(2,1)S(1)}, u32[]{:S(2)}, u32[]{:S(2)}) %all-to-all-start.2) | async-done | bytes 524320 | tf_op jit(solution)/shard_map/all_to_all | solution.py:256
  29.6 1.1 broadcast_in_dim.11
  30.7 3.7 %all-to-all-start = ((bf16[4,6,128,128]{3,2,1,0:T(8,128)(2,1)}), bf16[4,6,128,128]{3,2,1,0:T(8,128)(2,1)S(1)}, u32[]{:S(2)}, u32[]{:S(2)}) async-start(bf16[4,6,128,128]{3,2,1,0:T(8,128)(2,1)} %broadcast_in_dim.11), calls=%async_computation | async-start | bytes 1572864 | tf_op jit(solution)/shard_map/all_to_all | solution.py:209
  35.3 1.3 collective-permute-start.1
  36.6 4.6 %collective-permute-start = (bf16[12,2,2,32,128]{4,3,2,1,0:T(8,128)(2,1)S(1)}, bf16[12,2,2,32,128]{4,3,2,1,0:T(8,128)(2,1)S(1)}, u32[]{:S(2)}, u32[]{:S(2)}) collective-permute-start(bf16[12,2,2,32,128]{4,3,2,1,0:T(8,128)(2,1)S(1)} %get-tuple-element.35), channel_id=1, source_target_pairs={{0,8},{1,9},{2,10},{3,11},{8,16},{9,17},{10,18},{11,19},{16,24},{1... | collective-permute-start | bytes 1179656 | tf_op jit(solution)/shard_map/ppermute | solution.py:268
  41.9 4.8 %all-to-all-done = bf16[4,6,128,128]{3,2,1,0:T(8,128)(2,1)S(1)} async-done(((bf16[4,6,128,128]{3,2,1,0:T(8,128)(2,1)}), bf16[4,6,128,128]{3,2,1,0:T(8,128)(2,1)S(1)}, u32[]{:S(2)}, u32[]{:S(2)}) %all-to-all-start) | async-done | bytes 786464 | tf_op jit(solution)/shard_map/all_to_all | solution.py:209
  46.6 1.5 %broadcast_in_dim.12 = bf16[2,4,6,128,128]{4,3,2,1,0:T(8,128)(2,1)} broadcast(bf16[4,6,128,128]{3,2,1,0:T(8,128)(2,1)S(1)} %all-to-all-done), dimensions={1,2,3,4} | broadcast | bytes 2359296 | tf_op jit(solution)/shard_map/broadcast_in_dim | solution.py:213
  48.2 3.7 %all-to-all-start.1 = ((bf16[2,4,6,128,128]{4,3,2,1,0:T(8,128)(2,1)}), bf16[2,4,6,128,128]{4,3,2,1,0:T(8,128)(2,1)S(1)}, u32[]{:S(2)}, u32[]{:S(2)}) async-start(bf16[2,4,6,128,128]{4,3,2,1,0:T(8,128)(2,1)} %broadcast_in_dim.12), calls=%async_computation.1 | async-start | bytes 3145728 | tf_op jit(solution)/shard_map/all_to_all | solution.py:212
  51.8 3.2 %collective-permute-done.1 = bf16[12,2,2,32,128]{4,3,2,1,0:T(8,128)(2,1)S(1)} collective-permute-done((bf16[12,2,2,32,128]{4,3,2,1,0:T(8,128)(2,1)S(1)}, bf16[12,2,2,32,128]{4,3,2,1,0:T(8,128)(2,1)S(1)}, u32[]{:S(2)}, u32[]{:S(2)}) %collective-permute-start.1) | collective-permute-done | bytes 393248 | tf_op jit(solution)/shard_map/ppermute | solution.py:268
  57.8 1.2 copy-done
  59.0 10.5 %forward.1 = (bf16[4,4,10,16,384]{4,3,2,1,0:T(8,128)(2,1)}, bf16[4,4,8,16,128]{4,3,2,1,0:T(8,128)(2,1)}, f32[4,10,32,128]{3,2,1,0:T(8,128)}, f32[4,12,32,128]{3,...) custom-call(s32[4]{0:T(128)} %pad_add_fusion.place_ref, bf16[2,4,6,128,128]{4,3,2,1,0:T(8,128)(2,1)} %copy-done, ...), custom_call_target="tpu_custom_call" | custom-call | tf_op jit(solution)/shard_map/forward/pallas_call | solution.py:290
  69.4 10.4 %backward.1 = (bf16[2,4,6,128,128]{4,3,2,1,0:T(8,128)(2,1)}, bf16[4,8,16,128]{3,2,1,0:T(8,128)(2,1)}) custom-call(bf16[2,4,6,128,128]{4,3,2,1,0:T(8,128)(2,1)} %copy-done, bf16[8,2,2,32,128]{4,3,2,1,0:T(8,128)(2,1)} %get-tuple-element.32.own_ref, bf16[4,2,2,32,128]{4,3,2,1,0:T(8,128)(2,1)} %slice.93.above_ref, bf16[4,2,2,32,128]{4,3,2,1,0:T(8,128)(2,1)} %slice.95.below_ref, ...), custom_call_target="tpu_custom_call" | custom-call | tf_op jit(solution)/shard_map/backward/pallas_call | solution.py:310
  79.8 6.1 %all_to_all.40 = bf16[2,4,6,128,128]{4,3,2,1,0:T(8,128)(2,1)S(1)} all-to-all(bf16[2,4,6,128,128]{4,3,2,1,0:T(8,128)(2,1)} %get-tuple-element.17), channel_id=1, replica_groups=mesh['section'=4,'tm'=2,'space'=4] {'tm'}, dimensions={0} | all-to-all | bytes 3145728 | tf_op jit(solution)/shard_map/all_to_all | solution.py:220
  86.4 20.4 %all_to_all.41 = bf16[4,6,128,128]{3,2,1,0:T(8,128)(2,1)S(1)} all-to-all(bf16[4,6,128,128]{3,2,1,0:T(8,128)(2,1)S(1)} %reduce_sum.36), channel_id=1, replica_groups=mesh['section'=4,'tm'=2,'space'=4] {'section'}, dimensions={0} | all-to-all | bytes 1572864 | tf_op jit(solution)/shard_map/all_to_all | solution.py:222
  107.6 3.4 %all-to-all-start.5 = ((bf16[4,192,128]{2,1,0:T(8,128)(2,1)}), bf16[4,192,128]{2,1,0:T(8,128)(2,1)S(1)}, u32[]{:S(2)}, u32[]{:S(2)}) async-start(bf16[4,192,128]{2,1,0:T(8,128)(2,1)} %bitcast.19), calls=%async_computation.5 | async-start | bytes 393216 | tf_op jit(solution)/shard_map/all_to_all | solution.py:224
  111.7 5.5 %all-to-all-done.5 = bf16[4,192,128]{2,1,0:T(8,128)(2,1)S(1)} async-done(((bf16[4,192,128]{2,1,0:T(8,128)(2,1)}), bf16[4,192,128]{2,1,0:T(8,128)(2,1)S(1)}, u32[]{:S(2)}, u32[]{:S(2)}) %all-to-all-start.5) | async-done | bytes 196640 | tf_op jit(solution)/shard_map/all_to_all | solution.py:224
  117.2 3.4 %all-to-all-start.7 = ((bf16[8,2,2,16,128]{4,3,2,1,0:T(8,128)(2,1)}), bf16[8,2,2,16,128]{4,3,2,1,0:T(8,128)(2,1)S(1)}, u32[]{:S(2)}, u32[]{:S(2)}) async-start(bf16[8,2,2,16,128]{4,3,2,1,0:T(8,128)(2,1)} %bitcast.27), calls=%async_computation.7 | async-start | bytes 262144 | tf_op jit(solution)/shard_map/all_to_all | solution.py:330
  120.6 6.8 %all-to-all-done.7 = bf16[8,2,2,16,128]{4,3,2,1,0:T(8,128)(2,1)S(1)} async-done(((bf16[8,2,2,16,128]{4,3,2,1,0:T(8,128)(2,1)}), bf16[8,2,2,16,128]{4,3,2,1,0:T(8,128)(2,1)S(1)}, u32[]{:S(2)}, u32[]{:S(2)}) %all-to-all-start.7) | async-done | bytes 131104 | tf_op jit(solution)/shard_map/all_to_all | solution.py:330
  128.3 3.5 %all-to-all-start.6 = ((bf16[8,192,128]{2,1,0:T(8,128)(2,1)}), bf16[8,192,128]{2,1,0:T(8,128)(2,1)S(1)}, u32[]{:S(2)}, u32[]{:S(2)}) async-start(bf16[8,192,128]{2,1,0:T(8,128)(2,1)} %broadcast_in_dim.26), calls=%async_computation.6 | async-start | bytes 786432 | tf_op jit(solution)/shard_map/all_to_all | solution.py:226
  132.4 11.3 %all-to-all-done.6 = bf16[8,192,128]{2,1,0:T(8,128)(2,1)S(1)} async-done(((bf16[8,192,128]{2,1,0:T(8,128)(2,1)}), bf16[8,192,128]{2,1,0:T(8,128)(2,1)S(1)}, u32[]{:S(2)}, u32[]{:S(2)}) %all-to-all-start.6) | async-done | bytes 393248 | tf_op jit(solution)/shard_map/all_to_all | solution.py:226
  143.9 1.1 copy.45
  (41 shorter events, 13.6 us)
Async XLA Ops:
  0.6 4.6 %copy-start.1 = (bf16[2,2,128,128]{3,2,1,0:T(8,128)(2,1)S(1)}, bf16[2,2,128,128]{3,2,1,0:T(8,128)(2,1)}, u32[]{:S(2)}) copy-start(bf16[2,2,128,128]{3,2,1,0:T(8,128)(2,1)} %param.5) | copy-start | bytes 393220
  0.6 4.6 %copy-start.2 = (bf16[2,2,128,128]{3,2,1,0:T(8,128)(2,1)S(1)}, bf16[2,2,128,128]{3,2,1,0:T(8,128)(2,1)}, u32[]{:S(2)}) copy-start(bf16[2,2,128,128]{3,2,1,0:T(8,128)(2,1)} %param.4) | copy-start | bytes 393220
  3.7 11.0 %copy-start.4 = (bf16[1,9,128,128]{3,2,1,0:T(8,128)(2,1)S(1)}, bf16[1,9,128,128]{3,2,1,0:T(8,128)(2,1)}, u32[]{:S(2)}) copy-start(bf16[1,9,128,128]{3,2,1,0:T(8,128)(2,1)} %param.6) | copy-start | bytes 884740
  3.7 11.0 %copy-start.6 = (bf16[1,3,128,128]{3,2,1,0:T(8,128)(2,1)S(1)}, bf16[1,3,128,128]{3,2,1,0:T(8,128)(2,1)}, u32[]{:S(2)}) copy-start(bf16[1,3,128,128]{3,2,1,0:T(8,128)(2,1)} %param.7) | copy-start | bytes 294916
  8.4 21.2 %all-to-all-start.2 = ((bf16[8,2,2,2,32,128]{5,4,3,2,1,0:T(8,128)(2,1)}), bf16[8,2,2,2,32,128]{5,4,3,2,1,0:T(8,128)(2,1)S(1)}, u32[]{:S(2)}, u32[]{:S(2)}) async-start(bf16[8,2,2,2,32,128]{5,4,3,2,1,0:T(8,128)(2,1)} %fusion.4), calls=%async_computation.2 | async-start | bytes 1048576 | tf_op jit(solution)/shard_map/all_to_all | solution.py:256
  30.7 15.9 %all-to-all-start = ((bf16[4,6,128,128]{3,2,1,0:T(8,128)(2,1)}), bf16[4,6,128,128]{3,2,1,0:T(8,128)(2,1)S(1)}, u32[]{:S(2)}, u32[]{:S(2)}) async-start(bf16[4,6,128,128]{3,2,1,0:T(8,128)(2,1)} %broadcast_in_dim.11), calls=%async_computation | async-start | bytes 1572864 | tf_op jit(solution)/shard_map/all_to_all | solution.py:209
  35.2 12.9 %copy-start.3 = (bf16[8,2,2,32,128]{4,3,2,1,0:T(8,128)(2,1)}, bf16[8,2,2,32,128]{4,3,2,1,0:T(8,128)(2,1)S(1)}, u32[]{:S(2)}) copy-start(bf16[8,2,2,32,128]{4,3,2,1,0:T(8,128)(2,1)S(1)} %get-tuple-element.33.own_ref) | copy-start | bytes 786436
  35.3 19.7 %collective-permute-start.1 = (bf16[12,2,2,32,128]{4,3,2,1,0:T(8,128)(2,1)S(1)}, bf16[12,2,2,32,128]{4,3,2,1,0:T(8,128)(2,1)S(1)}, u32[]{:S(2)}, u32[]{:S(2)}) collective-permute-start(bf16[12,2,2,32,128]{4,3,2,1,0:T(8,128)(2,1)S(1)} %get-tuple-element.34), channel_id=1, source_target_pairs={{8,0},{9,1},{10,2},{11,3},{16,8},{17,9},{18,10},{19,11},{24,16},{2... | collective-permute-start | bytes 1179656 | tf_op jit(solution)/shard_map/ppermute | solution.py:268
  36.6 19.8 %collective-permute-start = (bf16[12,2,2,32,128]{4,3,2,1,0:T(8,128)(2,1)S(1)}, bf16[12,2,2,32,128]{4,3,2,1,0:T(8,128)(2,1)S(1)}, u32[]{:S(2)}, u32[]{:S(2)}) collective-permute-start(bf16[12,2,2,32,128]{4,3,2,1,0:T(8,128)(2,1)S(1)} %get-tuple-element.35), channel_id=1, source_target_pairs={{0,8},{1,9},{2,10},{3,11},{8,16},{9,17},{10,18},{11,19},{16,24},{1... | collective-permute-start | bytes 1179656 | tf_op jit(solution)/shard_map/ppermute | solution.py:268
  48.2 9.6 %all-to-all-start.1 = ((bf16[2,4,6,128,128]{4,3,2,1,0:T(8,128)(2,1)}), bf16[2,4,6,128,128]{4,3,2,1,0:T(8,128)(2,1)S(1)}, u32[]{:S(2)}, u32[]{:S(2)}) async-start(bf16[2,4,6,128,128]{4,3,2,1,0:T(8,128)(2,1)} %broadcast_in_dim.12), calls=%async_computation.1 | async-start | bytes 3145728 | tf_op jit(solution)/shard_map/all_to_all | solution.py:212
  57.8 1.2 copy-start
  86.4 24.6 %copy-start.5 = (bf16[4,8,16,128]{3,2,1,0:T(8,128)(2,1)S(1)}, bf16[4,8,16,128]{3,2,1,0:T(8,128)(2,1)}, u32[]{:S(2)}) copy-start(bf16[4,8,16,128]{3,2,1,0:T(8,128)(2,1)} %get-tuple-element.18) | copy-start | bytes 393220
  107.6 9.6 %all-to-all-start.5 = ((bf16[4,192,128]{2,1,0:T(8,128)(2,1)}), bf16[4,192,128]{2,1,0:T(8,128)(2,1)S(1)}, u32[]{:S(2)}, u32[]{:S(2)}) async-start(bf16[4,192,128]{2,1,0:T(8,128)(2,1)} %bitcast.19), calls=%async_computation.5 | async-start | bytes 393216 | tf_op jit(solution)/shard_map/all_to_all | solution.py:224
  117.2 10.3 %all-to-all-start.7 = ((bf16[8,2,2,16,128]{4,3,2,1,0:T(8,128)(2,1)}), bf16[8,2,2,16,128]{4,3,2,1,0:T(8,128)(2,1)S(1)}, u32[]{:S(2)}, u32[]{:S(2)}) async-start(bf16[8,2,2,16,128]{4,3,2,1,0:T(8,128)(2,1)} %bitcast.27), calls=%async_computation.7 | async-start | bytes 262144 | tf_op jit(solution)/shard_map/all_to_all | solution.py:330
  128.3 15.5 %all-to-all-start.6 = ((bf16[8,192,128]{2,1,0:T(8,128)(2,1)}), bf16[8,192,128]{2,1,0:T(8,128)(2,1)S(1)}, u32[]{:S(2)}, u32[]{:S(2)}) async-start(bf16[8,192,128]{2,1,0:T(8,128)(2,1)} %broadcast_in_dim.26), calls=%async_computation.6 | async-start | bytes 786432 | tf_op jit(solution)/shard_map/all_to_all | solution.py:226

commit v3 on v2

--- a/solution.py
+++ b/solution.py
@@ -36,12 +36,37 @@
     return jnp.concatenate([kernel_of(w_ref, block, tap) for tap in order], 1)
 
 
+def window_kernel(halo, width, video_ref, cot_ref, video_out, cot_out):
+    parties = video_out.shape[0]
+    frames, rows, columns, chans = video_ref.shape
+    own = width - 2 * halo
+    for source, target in ((video_ref, video_out), (cot_ref, cot_out)):
+        whole = source[...].astype(F32)
+        for unit in range(parties):
+            first, last = unit * own - halo, unit * own - halo + width
+            parts = []
+            if first < 0:
+                parts.append(jnp.zeros((frames, rows, -first, chans), F32))
+            parts.append(whole[:, :, max(first, 0) : min(last, columns)])
+            if last > columns:
+                parts.append(jnp.zeros((frames, rows, last - columns, chans), F32))
+            piece = jnp.concatenate(parts, 2) if len(parts) > 1 else parts[0]
+            target[unit] = piece.astype(BF16)
+
+
+def place_kernels(place_ref, w_ref, mine_ref, other_ref):
+    core = place_ref[4]
+    w_ref[core] = mine_ref[...]
+    w_ref[1 - core] = other_ref[...]
+
+
 def forward_kernel(
-    geometry, place_ref, w_ref, own_ref, above_ref, below_ref, xo_ref, ho_ref, *rest
+    geometry, place_ref, mine_ref, other_ref, own_ref, above_ref, below_ref, xo_ref, ho_ref, *rest
 ):
     blocks, cores, group, frames_in, rows_in, halo, tile, width = geometry
     d_refs = rest[:blocks]
-    x_ref, h_ref, mask_ref = rest[blocks:]
+    x_ref, h_ref, mask_ref, w_ref = rest[blocks:]
+    place_kernels(place_ref, w_ref, mine_ref, other_ref)
     frames = cores * frames_in
     high = tile + 2 * halo
     chans = w_ref.shape[-1]
@@ -120,10 +145,13 @@
             keep(block + 1, frame, new.astype(BF16).astype(F32), first)
 
 
-def backward_kernel(geometry, factor, w_ref, own_ref, above_ref, below_ref, xo_ref, ho_ref, *rest):
+def backward_kernel(
+    geometry, factor, place_ref, mine_ref, other_ref, own_ref, above_ref, below_ref, xo_ref, ho_ref, *rest
+):
     blocks, cores, group, frames_in, rows_in, halo, tile, width = geometry
     d_refs = rest[:blocks]
-    grad_ref, out_ref, g_ref, da_ref, dao_ref, go_ref = rest[blocks:]
+    keep_ref, give_ref, out_ref, g_ref, da_ref, dao_ref, go_ref, w_ref, grad_ref = rest[blocks:]
+    place_kernels(place_ref, w_ref, mine_ref, other_ref)
     frames = cores * frames_in
     chans = w_ref.shape[-1]
     rim = blocks
@@ -140,7 +168,8 @@
         g_ref[frame] = jnp.concatenate(pieces, 0)
 
     def put(block, tap, value):
-        grad_ref[tap // per_core, block, tap % per_core] = (value * factor).astype(BF16)
+        slot = jnp.where(place_ref[4] == tap // per_core, 0, 1)
+        grad_ref[slot, block, tap % per_core] = (value * factor).astype(BF16)
 
     for block in reversed(range(blocks)):
         edge = block + 1
@@ -184,9 +213,12 @@
             if block:
                 g_ref[frame, first + 1 : last - 1] = new.reshape(inner, width, chans)
             else:
-                out_ref[frame] = new.astype(F32).reshape(inner, width, chans)[
-                    :, own_cols[0] : own_cols[1]
-                ].astype(BF16)
+                core, within = divmod(frame, frames_in)
+                cut = new.astype(F32).reshape(inner, width, chans)[:, own_cols[0] : own_cols[1]]
+                for unit in range(group):
+                    out_ref[core * group + unit, within] = cut[
+                        unit * rows_in : (unit + 1) * rows_in
+                    ].astype(BF16)
         slopes = dao_ref[...].reshape(frames * pixels, chans)
         for ky in range(3):
             taps = xo_ref[block, :, ky : ky + tile].reshape(frames * pixels, 3 * chans)
@@ -198,36 +230,18 @@
             later = go_ref[skip:].reshape((frames - skip) * pixels, chans)
             earlier = ho_ref[block, : frames - skip].reshape((frames - skip) * pixels, chans)
             put(block, 9 + kt, dot_first(later, earlier))
-
-
-def gathered_kernels(spatial_weights, temporal_weights):
-    cores = lax.axis_size("tm")
-    blocks = lax.axis_size("section")
+    keep_ref[...] = grad_ref[0]
+    give_ref[...] = grad_ref[1]
+
+
+def swapped(value):
+    return lax.ppermute(value, "tm", [(0, 1), (1, 0)])
+
+
+def own_half(spatial_weights, temporal_weights):
     own = jnp.concatenate([spatial_weights[0], temporal_weights[0]], 0)
-    taps = own.shape[0] // cores
-    half = lax.dynamic_slice_in_dim(own, lax.axis_index("tm") * taps, taps, 0)
-    halves = lax.all_to_all(
-        jnp.broadcast_to(half[None], (blocks,) + half.shape), "section", 0, 0, tiled=True
-    )
-    return lax.all_to_all(
-        jnp.broadcast_to(halves[None], (cores,) + halves.shape), "tm", 0, 0, tiled=True
-    )
-
-
-def summed_kernels(part):
-    cores, blocks, taps, outs, chans = part.shape
-    tiles = lax.axis_size("space")
-    part = lax.all_to_all(part, "tm", 0, 0, tiled=True)
-    part = part.astype(F32).sum(0).astype(BF16)
-    part = lax.all_to_all(part, "section", 0, 0, tiled=True)
-    part = part.astype(F32).sum(0).astype(BF16)
-    part = lax.all_to_all(part.reshape(tiles, -1, chans), "space", 0, 0, tiled=True)
-    part = part.astype(F32).sum(0).astype(BF16)
-    whole = lax.all_to_all(
-        jnp.broadcast_to(part[None], (cores * tiles,) + part.shape),
-        ("tm", "space"), 0, 0, tiled=True,
-    )
-    return whole.reshape(cores * taps, outs, chans)
+    taps = own.shape[0] // lax.axis_size("tm")
+    return lax.dynamic_slice_in_dim(own, lax.axis_index("tm") * taps, taps, 0)
 
 
 def on_device(video, cotangent, spatial_weights, temporal_weights):
@@ -245,52 +259,64 @@
             [core * tiles + base + unit for core in range(cores) for unit in range(group)]
             for base in range(0, tiles, group)
         ]
-
-    kernels = gathered_kernels(spatial_weights, temporal_weights)
-
-    both = jnp.stack([video, cotangent])
-    padded = jnp.pad(both, ((0, 0), (0, 0), (0, 0), (halo, halo), (0, 0)))
-    windows = jnp.stack(
-        [padded[:, :, :, unit * own_width : unit * own_width + width] for unit in range(parties)]
+    vmem = pl.BlockSpec(memory_space=pltpu.VMEM)
+    smem = pl.BlockSpec(memory_space=pltpu.SMEM)
+    params = pltpu.CompilerParams(vmem_limit_bytes=56 * 2**20)
+
+    windows = jax.ShapeDtypeStruct((parties, frames_in, rows_in, width, chans), BF16)
+    video_windows, cot_windows = pl.pallas_call(
+        functools.partial(window_kernel, halo, width),
+        name="windows",
+        in_specs=[vmem] * 2,
+        out_specs=[vmem] * 2,
+        out_shape=[windows] * 2,
+        compiler_params=params,
+    )(video, cotangent)
+
+    def spread(value):
+        return lax.all_to_all(value, ("tm", "space"), 0, 0, axis_index_groups=sets, tiled=True)
+
+    def moved(value, step):
+        rows = blocks * tiles
+        pairs = [(i, i + step) for i in range(rows) if 0 <= i + step < rows]
+        return lax.ppermute(value, ("section", "space"), pairs)
+
+    own_video = spread(video_windows)
+    half_kernels = own_half(spatial_weights, temporal_weights)
+    mine = lax.all_to_all(
+        jnp.broadcast_to(half_kernels[None], (blocks,) + half_kernels.shape),
+        "section", 0, 0, tiled=True,
     )
-    mine = lax.all_to_all(
-        windows, ("tm", "space"), 0, 0, axis_index_groups=sets, tiled=True
-    )
-    own_video, own_cot = mine[:, 0], mine[:, 1]
+    video_above, video_below = moved(own_video, group), moved(own_video, -group)
+    other = swapped(mine)
+
+    own_cot = spread(cot_windows)
     half = group // 2
     split = own_cot.reshape((cores, group) + own_cot.shape[1:])
-    upper, lower = split[:, :half], split[:, half:]
-    rows = blocks * tiles
-
-    def sent(cot, step):
-        flat = jnp.concatenate([own_video, cot.reshape((cores * half,) + own_cot.shape[1:])], 0)
-        pairs = [(i, i + step) for i in range(rows) if 0 <= i + step < rows]
-        got = lax.ppermute(flat, ("section", "space"), pairs)
-        return got[:parties], got[parties:]
-
-    video_above, cot_above = sent(lower, group)
-    video_below, cot_below = sent(upper, -group)
+    edge = (cores * half,) + own_cot.shape[1:]
+    cot_above = moved(split[:, half:].reshape(edge), group)
+    cot_below = moved(split[:, :half].reshape(edge), -group)
 
     place = lax.axis_index("space")
     band = (lax.axis_index("section") * tiles + place) // group
     unit = lax.axis_index("tm") * group + place % group
     total_rows = blocks * tiles * rows_in
     corner = jnp.stack(
-        [band * tile - halo, unit * own_width - halo, total_rows, columns]
+        [band * tile - halo, unit * own_width - halo, total_rows, columns, lax.axis_index("tm")]
     ).astype(jnp.int32)
     geometry = (blocks, cores, group, frames_in, rows_in, halo, tile, width)
     frames = cores * frames_in
     high = tile + 2 * halo
-    vmem = pl.BlockSpec(memory_space=pltpu.VMEM)
-    params = pltpu.CompilerParams(vmem_limit_bytes=56 * 2**20)
+    all_kernels = (cores,) + mine.shape
     saved = [
         jax.ShapeDtypeStruct((frames, tile + 2 * block + 2, width, chans), F32)
         for block in range(blocks)
     ]
+    cost = pl.CostEstimate(flops=6 * 10**9, bytes_accessed=8 * 10**6, transcendentals=10**6)
     features, hidden, *slopes = pl.pallas_call(
         functools.partial(forward_kernel, geometry),
         name="forward",
-        in_specs=[pl.BlockSpec(memory_space=pltpu.SMEM)] + [vmem] * 4,
+        in_specs=[smem] + [vmem] * 5,
         out_specs=[vmem] * (2 + blocks),
         out_shape=[
             jax.ShapeDtypeStruct((blocks, frames, tile + 2, own_width, 3 * chans), BF16),
@@ -301,36 +327,54 @@
             pltpu.VMEM((frames, high, width, 3 * chans), BF16),
             pltpu.VMEM((frames, high, width, chans), BF16),
             pltpu.VMEM((high, width, chans), F32),
+            pltpu.VMEM(all_kernels, BF16),
         ],
         compiler_params=params,
-    )(corner, kernels, own_video, video_above, video_below)
+        cost_estimate=cost,
+    )(corner, mine, other, own_video, video_above, video_below)
 
     pixel_count = frames * total_rows * columns
     factor = 1.0 / float(pixel_count) ** 0.5
-    partial, tile_grad = pl.pallas_call(
+    keep, give, tile_grad = pl.pallas_call(
         functools.partial(backward_kernel, geometry, factor),
         name="backward",
-        in_specs=[vmem] * (6 + blocks),
-        out_specs=[vmem] * 2,
+        in_specs=[smem] + [vmem] * (7 + blocks),
+        out_specs=[vmem] * 3,
         out_shape=[
-            jax.ShapeDtypeStruct(kernels.shape, BF16),
-            jax.ShapeDtypeStruct((frames, tile, own_width, chans), BF16),
+            jax.ShapeDtypeStruct(mine.shape, BF16),
+            jax.ShapeDtypeStruct(mine.shape, BF16),
+            jax.ShapeDtypeStruct((parties, frames_in, rows_in, own_width, chans), BF16),
         ],
         scratch_shapes=[
             pltpu.VMEM((frames, tile + 2 * blocks, width, chans), BF16),
             pltpu.VMEM((frames, tile + 2 * blocks, width, 3 * chans), BF16),
             pltpu.VMEM((frames, tile, own_width, chans), BF16),
             pltpu.VMEM((frames, tile, own_width, chans), BF16),
+            pltpu.VMEM(all_kernels, BF16),
+            pltpu.VMEM(all_kernels, BF16),
         ],
         compiler_params=params,
-    )(kernels, own_cot, cot_above, cot_below, features, hidden, *slopes)
-
-    back = tile_grad.reshape(cores, frames_in, group, rows_in, own_width, chans)
-    back = back.swapaxes(1, 2).reshape(parties, frames_in, rows_in, own_width, chans)
-    back = lax.all_to_all(back, ("tm", "space"), 0, 0, axis_index_groups=sets, tiled=True)
+        cost_estimate=cost,
+    )(corner, mine, other, own_cot, cot_above, cot_below, features, hidden, *slopes)
+
+    part = (keep.astype(F32) + swapped(give).astype(F32)).astype(BF16)
+    part = lax.all_to_all(part, "section", 0, 0, tiled=True)
+    part = part.astype(F32).sum(0).astype(BF16)
+    part = lax.all_to_all(part.reshape(tiles, -1, chans), "space", 0, 0, tiled=True)
+    part = part.astype(F32).sum(0).astype(BF16)
+    shares = jnp.broadcast_to(part[None], (cores * tiles,) + part.shape)
+    back = tile_grad.reshape(parties, -1, chans)
+    everyone = ("tm", "space")
+    if sets is None:
+        got = lax.all_to_all(
+            jnp.concatenate([shares, back], 1), everyone, 0, 0, tiled=True
+        )
+        whole, back = got[:, : part.shape[0]], got[:, part.shape[0] :]
+    else:
+        whole, back = lax.all_to_all(shares, everyone, 0, 0, tiled=True), spread(back)
+    back = back.reshape(parties, frames_in, rows_in, own_width, chans)
     grad_video = back.transpose(1, 2, 0, 3, 4).reshape(video.shape)
-
-    own = summed_kernels(partial).swapaxes(1, 2).astype(F32)[None]
+    own = whole.reshape(-1, chans, chans).swapaxes(1, 2).astype(F32)[None]
     count = spatial_weights.shape[1]
     return own[:, :count], own[:, count:], grad_video
 

time: 147 us -> 129 us (0.88)
  waiting for transfers between devices: 46.4 us -> 23 us
  blocking collectives: 26.6 us -> 46.8 us
  local copies, waits for them, and re-layouts: 12.8 us -> 6.66 us
  other arithmetic: 8.51 us -> 2.63 us
  starting transfers between devices: 29.8 us -> 24.7 us
  Pallas kernels: 20.8 us -> 23.2 us
    all_to_all x6 -> x3, waiting for transfers between devices: 43.2 us -> 20.7 us  [the longest x2 11.7 us: spread(): lax.all_to_all(value, ('tm', 'space'), 0, 0, axis_index_groups=sets, tile...]
    all_to_all x2 -> x3, blocking collectives: 26.6 us -> 46.8 us  [the longest x1 17.7 us: on_device(): part = lax.all_to_all(part, 'section', 0, 0, tiled=True)]
    all_to_all x6 -> x3, starting transfers between devices: 23.9 us -> 13.5 us  [the longest x2 8.32 us: spread(): lax.all_to_all(value, ('tm', 'space'), 0, 0, axis_index_groups=sets, tile...]
    unnamed x6 -> x0, other arithmetic: 5.4 us -> none
    ppermute x2 -> x6, starting transfers between devices: 5.87 us -> 11.2 us  [the longest x4 10.5 us: moved(): return lax.ppermute(value, ('section', 'space'), pairs)]
    slice x6 -> x3, local copies, waits for them, and re-layouts: 3.65 us -> 0.05 us  [the longest x2 0.04 us: on_device(): whole, back = (got[:, :part.shape[0]], got[:, part.shape[0]:])]
    broadcast_in_dim x3 -> x2, local copies, waits for them, and re-layouts: 3.41 us -> 1.11 us  [the longest x1 1.06 us: on_device(): jnp.broadcast_to(half_kernels[None], (blocks,) + half_kernels.shape)]
    pallas_call x0 -> x1, Pallas kernels: none -> 1.82 us  [on_device(): pl.pallas_call(functools.partial(window_kernel, halo, width), name='windo...]
  transfers between devices with their start and end apart: 8 -> 9, of which waited for: 6 -> 4; matrix products, arithmetic and copies ran while one was open for 5% -> 0% of each run, Pallas kernels for 0% -> 10%
where the time goes in v3:
time: 129 us; the launch traced here: 128 us
  blocking collectives  46.8 us (36%)
  starting transfers between devices  24.7 us (19%)
  Pallas kernels  23.2 us (18%)
  waiting for transfers between devices  23 us (18%)
  local copies, waits for them, and re-layouts  6.66 us (5%)
  other arithmetic  2.63 us (2%)
    all_to_all x1, blocking collectives, on_device(): part = lax.all_to_all(part, 'section', 0, 0, tiled=True)  17.7 us
    all_to_all x1, blocking collectives, on_device(): lax.all_to_all(jnp.concatenate([shares, back], 1), everyone, 0, 0, tiled=...  17.4 us
    all_to_all x2, waiting for transfers between devices, spread(): lax.all_to_all(value, ('tm', 'space'), 0, 0, axis_index_groups=sets, tile...  11.7 us
    all_to_all x1, blocking collectives, on_device(): lax.all_to_all(part.reshape(tiles, -1, chans), 'space', 0, 0, tiled=True)  11.6 us
    pallas_call x1, Pallas kernels, on_device(): pl.pallas_call(functools.partial(backward_kernel, geometry, factor), name...  10.8 us
    pallas_call x1, Pallas kernels, on_device(): pl.pallas_call(functools.partial(forward_kernel, geometry), name='forward...  10.6 us
    ppermute x4, starting transfers between devices, moved(): return lax.ppermute(value, ('section', 'space'), pairs)  10.5 us
    all_to_all x1, waiting for transfers between devices, on_device(): lax.all_to_all(jnp.broadcast_to(half_kernels[None], (blocks,) + half_kern...  9.01 us
  transfers between devices with their start and end apart: 9, of which 4 were waited for; matrix products, arithmetic and copies ran while one was open for 0% of the time, Pallas kernels for 10%

profile of v3, /device:TPU:0, one launch (start us, length us, event | category | flops | bytes accessed | tf_op | source)
XLA Modules:
  0.0 127.8 jit_solution(17448665508352978345)
XLA Ops:
  0.6 1.0 fusion
  1.6 1.1 broadcast_in_dim.18
  2.7 5.2 %all-to-all-start = ((bf16[4,6,128,128]{3,2,1,0:T(8,128)(2,1)}), bf16[4,6,128,128]{3,2,1,0:T(8,128)(2,1)S(1)}, u32[]{:S(2)}, u32[]{:S(2)}) async-start(bf16[4,6,128,128]{3,2,1,0:T(8,128)(2,1)} %broadcast_in_dim.18), calls=%async_computation | async-start | bytes 1572864 | tf_op jit(solution)/shard_map/all_to_all | solution.py:286
  7.9 1.8 %windows.1 = (bf16[8,2,2,32,128]{4,3,2,1,0:T(8,128)(2,1)}, bf16[8,2,2,32,128]{4,3,2,1,0:T(8,128)(2,1)}) custom-call(bf16[2,2,128,128]{3,2,1,0:T(8,128)(2,1)} %video_ref.1, bf16[2,2,128,128]{3,2,1,0:T(8,128)(2,1)} %cot_ref.1), custom_call_target="tpu_custom_call" | custom-call | tf_op jit(solution)/shard_map/windows/pallas_call | solution.py:267
  9.7 9.0 %all-to-all-done.mine_ref = bf16[4,6,128,128]{3,2,1,0:T(8,128)(2,1)S(1)} async-done(((bf16[4,6,128,128]{3,2,1,0:T(8,128)(2,1)}), bf16[4,6,128,128]{3,2,1,0:T(8,128)(2,1)S(1)}, u32[]{:S(2)}, u32[]{:S(2)}) %all-to-all-start) | async-done | bytes 786464 | tf_op jit(solution)/shard_map/all_to_all | solution.py:286
  18.7 4.9 %all-to-all-start.2 = ((bf16[8,2,2,32,128]{4,3,2,1,0:T(8,128)(2,1)}), bf16[8,2,2,32,128]{4,3,2,1,0:T(8,128)(2,1)S(1)}, u32[]{:S(2)}, u32[]{:S(2)}) async-start(bf16[8,2,2,32,128]{4,3,2,1,0:T(8,128)(2,1)} %get-tuple-element.15), calls=%async_computation.2 | async-start | bytes 524288 | tf_op jit(solution)/shard_map/all_to_all | solution.py:277
  24.1 8.9 %all-to-all-done.2.own_ref = bf16[8,2,2,32,128]{4,3,2,1,0:T(8,128)(2,1)S(1)} async-done(((bf16[8,2,2,32,128]{4,3,2,1,0:T(8,128)(2,1)}), bf16[8,2,2,32,128]{4,3,2,1,0:T(8,128)(2,1)S(1)}, u32[]{:S(2)}, u32[]{:S(2)}) %all-to-all-start.2) | async-done | bytes 262176 | tf_op jit(solution)/shard_map/all_to_all | solution.py:277
  33.0 3.4 %all-to-all-start.1 = ((bf16[8,2,2,32,128]{4,3,2,1,0:T(8,128)(2,1)}), bf16[8,2,2,32,128]{4,3,2,1,0:T(8,128)(2,1)S(1)}, u32[]{:S(2)}, u32[]{:S(2)}) async-start(bf16[8,2,2,32,128]{4,3,2,1,0:T(8,128)(2,1)} %get-tuple-element.14), calls=%async_computation.1 | async-start | bytes 524288 | tf_op jit(solution)/shard_map/all_to_all | solution.py:277
  36.4 1.3 %collective-permute-start.4 = (bf16[8,2,2,32,128]{4,3,2,1,0:T(8,128)(2,1)S(1)}, bf16[8,2,2,32,128]{4,3,2,1,0:T(8,128)(2,1)S(1)}, u32[]{:S(2)}, u32[]{:S(2)}) collective-permute-start(bf16[8,2,2,32,128]{4,3,2,1,0:T(8,128)(2,1)S(1)} %all-to-all-done.2.own_ref), channel_id=1, source_target_pairs={{8,0},{9,1},{10,2},{11,3},{16,8},{17,9},{18,10},{19,11},{24,16},{2... | collective-permute-start | bytes 786440 | tf_op jit(solution)/shard_map/ppermute | solution.py:282
  37.7 4.6 %collective-permute-start.3 = (bf16[8,2,2,32,128]{4,3,2,1,0:T(8,128)(2,1)S(1)}, bf16[8,2,2,32,128]{4,3,2,1,0:T(8,128)(2,1)S(1)}, u32[]{:S(2)}, u32[]{:S(2)}) collective-permute-start(bf16[8,2,2,32,128]{4,3,2,1,0:T(8,128)(2,1)S(1)} %all-to-all-done.2.own_ref), channel_id=1, source_target_pairs={{0,8},{1,9},{2,10},{3,11},{8,16},{9,17},{10,18},{11,19},{16,24},{1... | collective-permute-start | bytes 786440 | tf_op jit(solution)/shard_map/ppermute | solution.py:282
  42.9 2.8 %all-to-all-done.1.own_ref = bf16[8,2,2,32,128]{4,3,2,1,0:T(8,128)(2,1)S(1)} async-done(((bf16[8,2,2,32,128]{4,3,2,1,0:T(8,128)(2,1)}), bf16[8,2,2,32,128]{4,3,2,1,0:T(8,128)(2,1)S(1)}, u32[]{:S(2)}, u32[]{:S(2)}) %all-to-all-start.1) | async-done | bytes 262176 | tf_op jit(solution)/shard_map/all_to_all | solution.py:277
  45.7 3.3 %collective-permute-start.1 = (bf16[4,2,2,32,128]{4,3,2,1,0:T(8,128)(2,1)S(1)}, bf16[4,2,2,32,128]{4,3,2,1,0:T(8,128)(2,1)S(1)}, u32[]{:S(2)}, u32[]{:S(2)}) collective-permute-start(bf16[4,2,2,32,128]{4,3,2,1,0:T(8,128)(2,1)S(1)} %bitcast.27), channel_id=1, source_target_pairs={{0,8},{1,9},{2,10},{3,11},{8,16},{9,17},{10,18},{11,19},{16,24},{1... | collective-permute-start | bytes 393224 | tf_op jit(solution)/shard_map/ppermute | solution.py:282
  49.1 1.3 %collective-permute-start.2 = (bf16[4,2,2,32,128]{4,3,2,1,0:T(8,128)(2,1)S(1)}, bf16[4,2,2,32,128]{4,3,2,1,0:T(8,128)(2,1)S(1)}, u32[]{:S(2)}, u32[]{:S(2)}) collective-permute-start(bf16[4,2,2,32,128]{4,3,2,1,0:T(8,128)(2,1)S(1)} %bitcast.26), channel_id=1, source_target_pairs={{8,0},{9,1},{10,2},{11,3},{16,8},{17,9},{18,10},{19,11},{24,16},{2... | collective-permute-start | bytes 393224 | tf_op jit(solution)/shard_map/ppermute | solution.py:282
  51.2 0.9 copy-done.4
  52.1 10.6 %forward.1 = (bf16[4,4,10,16,384]{4,3,2,1,0:T(8,128)(2,1)}, bf16[4,4,8,16,128]{4,3,2,1,0:T(8,128)(2,1)}, f32[4,10,32,128]{3,2,1,0:T(8,128)}, f32[4,12,32,128]{3,...) custom-call(s32[5]{0:T(128)} %stack.15.place_ref, bf16[4,6,128,128]{3,2,1,0:T(8,128)(2,1)} %copy-done.1, ...), custom_call_target="tpu_custom_call" | custom-call | flops 6000000000 | bytes 8000000 | tf_op jit(solution)/shard_map/forward/pallas_call | solution.py:316
  63.4 10.8 %backward.1 = (bf16[4,6,128,128]{3,2,1,0:T(8,128)(2,1)}, bf16[4,6,128,128]{3,2,1,0:T(8,128)(2,1)}, bf16[8,2,2,16,128]{4,3,2,1,0:T(8,128)(2,1)}) custom-call(s32[5]{0:T(128)} %stack.15.place_ref, bf16[4,6,128,128]{3,2,1,0:T(8,128)(2,1)} %copy-done.1, bf16[4,6,128,128]{3,2,1,0:T(8,128)(2,1)} %copy-done.4, bf16[8,2,2,32,128]{4,3,2,1,0:T(8,128)(2,1)} %copy-done, ...), custom_call_target="tpu_custom_call" | custom-call | flops 6000000000 | bytes 8000000 | tf_op jit(solution)/shard_map/backward/pallas_call | solution.py:338
  74.4 2.3 %collective-permute-done.5 = bf16[4,6,128,128]{3,2,1,0:T(8,128)(2,1)S(1)} collective-permute-done((bf16[4,6,128,128]{3,2,1,0:T(8,128)(2,1)}, bf16[4,6,128,128]{3,2,1,0:T(8,128)(2,1)S(1)}, u32[]{:S(2)}, u32[]{:S(2)}) %collective-permute-start.5) | collective-permute-done | bytes 786464 | tf_op jit(solution)/shard_map/ppermute | solution.py:238
  76.7 1.4 %add_convert_fusion = bf16[4,6,128,128]{3,2,1,0:T(8,128)(2,1)S(1)} fusion(bf16[4,6,128,128]{3,2,1,0:T(8,128)(2,1)S(1)} %collective-permute-done.5, bf16[4,6,128,128]{3,2,1,0:T(8,128)(2,1)} %get-tuple-element.22), kind=kLoop, calls=%fused_computation | loop fusion | flops 1572864 | bytes 2359296 | tf_op jit(solution)/shard_map/convert_element_type | solution.py:360
  78.1 17.7 %all_to_all.30 = bf16[4,6,128,128]{3,2,1,0:T(8,128)(2,1)S(1)} all-to-all(bf16[4,6,128,128]{3,2,1,0:T(8,128)(2,1)S(1)} %add_convert_fusion), channel_id=1, replica_groups=mesh['section'=4,'tm'=2,'space'=4] {'section'}, dimensions={0} | all-to-all | bytes 1572864 | tf_op jit(solution)/shard_map/all_to_all | solution.py:361
  95.9 11.6 %all_to_all.31 = bf16[4,192,128]{2,1,0:T(8,128)(2,1)S(1)} all-to-all(bf16[4,192,128]{2,1,0:T(8,128)(2,1)S(1)} %bitcast.22), channel_id=1, replica_groups=mesh['section'=4,'tm'=2,'space'=4] {'space'}, dimensions={0} | all-to-all | bytes 393216 | tf_op jit(solution)/shard_map/all_to_all | solution.py:363
  107.7 17.4 %all_to_all.32 = bf16[8,256,128]{2,1,0:T(8,128)(2,1)S(1)} all-to-all(bf16[8,256,128]{2,1,0:T(8,128)(2,1)S(1)} %pad_maximum_fusion), channel_id=1, replica_groups=mesh['section'=4,'tm'=2,'space'=4] {'tm','space'}, dimensions={0} | all-to-all | bytes 1048576 | tf_op jit(solution)/shard_map/all_to_all | solution.py:369
  125.3 0.7 copy.12
  126.0 1.0 copy.13
  127.0 0.8 copy.14
  (35 shorter events, 3.2 us)
Async XLA Ops:
  2.7 16.0 %all-to-all-start = ((bf16[4,6,128,128]{3,2,1,0:T(8,128)(2,1)}), bf16[4,6,128,128]{3,2,1,0:T(8,128)(2,1)S(1)}, u32[]{:S(2)}, u32[]{:S(2)}) async-start(bf16[4,6,128,128]{3,2,1,0:T(8,128)(2,1)} %broadcast_in_dim.18), calls=%async_computation | async-start | bytes 1572864 | tf_op jit(solution)/shard_map/all_to_all | solution.py:286
  18.7 31.7 %copy-start.1 = (bf16[4,6,128,128]{3,2,1,0:T(8,128)(2,1)}, bf16[4,6,128,128]{3,2,1,0:T(8,128)(2,1)S(1)}, u32[]{:S(2)}) copy-start(bf16[4,6,128,128]{3,2,1,0:T(8,128)(2,1)S(1)} %all-to-all-done.mine_ref) | copy-start | bytes 2359300
  18.7 14.3 %all-to-all-start.2 = ((bf16[8,2,2,32,128]{4,3,2,1,0:T(8,128)(2,1)}), bf16[8,2,2,32,128]{4,3,2,1,0:T(8,128)(2,1)S(1)}, u32[]{:S(2)}, u32[]{:S(2)}) async-start(bf16[8,2,2,32,128]{4,3,2,1,0:T(8,128)(2,1)} %get-tuple-element.15), calls=%async_computation.2 | async-start | bytes 524288 | tf_op jit(solution)/shard_map/all_to_all | solution.py:277
  23.6 26.8 %collective-permute-start = (bf16[4,6,128,128]{3,2,1,0:T(8,128)(2,1)S(1)}, bf16[4,6,128,128]{3,2,1,0:T(8,128)(2,1)S(1)}, u32[]{:S(2)}, u32[]{:S(2)}) collective-permute-start(bf16[4,6,128,128]{3,2,1,0:T(8,128)(2,1)S(1)} %all-to-all-done.mine_ref), channel_id=1, source_target_pairs={{0,4},{4,0},{1,5},{5,1},{2,6},{6,2},{3,7},{7,3},{8,12},{12,8},{9,1... | collective-permute-start | bytes 2359304 | tf_op jit(solution)/shard_map/ppermute | solution.py:238
  33.0 17.5 %copy-start.2 = (bf16[8,2,2,32,128]{4,3,2,1,0:T(8,128)(2,1)}, bf16[8,2,2,32,128]{4,3,2,1,0:T(8,128)(2,1)S(1)}, u32[]{:S(2)}) copy-start(bf16[8,2,2,32,128]{4,3,2,1,0:T(8,128)(2,1)S(1)} %all-to-all-done.2.own_ref) | copy-start | bytes 786436
  33.0 12.7 %all-to-all-start.1 = ((bf16[8,2,2,32,128]{4,3,2,1,0:T(8,128)(2,1)}), bf16[8,2,2,32,128]{4,3,2,1,0:T(8,128)(2,1)S(1)}, u32[]{:S(2)}, u32[]{:S(2)}) async-start(bf16[8,2,2,32,128]{4,3,2,1,0:T(8,128)(2,1)} %get-tuple-element.14), calls=%async_computation.1 | async-start | bytes 524288 | tf_op jit(solution)/shard_map/all_to_all | solution.py:277
  36.4 14.0 %collective-permute-start.4 = (bf16[8,2,2,32,128]{4,3,2,1,0:T(8,128)(2,1)S(1)}, bf16[8,2,2,32,128]{4,3,2,1,0:T(8,128)(2,1)S(1)}, u32[]{:S(2)}, u32[]{:S(2)}) collective-permute-start(bf16[8,2,2,32,128]{4,3,2,1,0:T(8,128)(2,1)S(1)} %all-to-all-done.2.own_ref), channel_id=1, source_target_pairs={{8,0},{9,1},{10,2},{11,3},{16,8},{17,9},{18,10},{19,11},{24,16},{2... | collective-permute-start | bytes 786440 | tf_op jit(solution)/shard_map/ppermute | solution.py:282
  37.7 12.7 %collective-permute-start.3 = (bf16[8,2,2,32,128]{4,3,2,1,0:T(8,128)(2,1)S(1)}, bf16[8,2,2,32,128]{4,3,2,1,0:T(8,128)(2,1)S(1)}, u32[]{:S(2)}, u32[]{:S(2)}) collective-permute-start(bf16[8,2,2,32,128]{4,3,2,1,0:T(8,128)(2,1)S(1)} %all-to-all-done.2.own_ref), channel_id=1, source_target_pairs={{0,8},{1,9},{2,10},{3,11},{8,16},{9,17},{10,18},{11,19},{16,24},{1... | collective-permute-start | bytes 786440 | tf_op jit(solution)/shard_map/ppermute | solution.py:282
  45.7 17.0 %copy-start = (bf16[8,2,2,32,128]{4,3,2,1,0:T(8,128)(2,1)}, bf16[8,2,2,32,128]{4,3,2,1,0:T(8,128)(2,1)S(1)}, u32[]{:S(2)}) copy-start(bf16[8,2,2,32,128]{4,3,2,1,0:T(8,128)(2,1)S(1)} %all-to-all-done.1.own_ref) | copy-start | bytes 786436
  45.7 16.9 %collective-permute-start.1 = (bf16[4,2,2,32,128]{4,3,2,1,0:T(8,128)(2,1)S(1)}, bf16[4,2,2,32,128]{4,3,2,1,0:T(8,128)(2,1)S(1)}, u32[]{:S(2)}, u32[]{:S(2)}) collective-permute-start(bf16[4,2,2,32,128]{4,3,2,1,0:T(8,128)(2,1)S(1)} %bitcast.27), channel_id=1, source_target_pairs={{0,8},{1,9},{2,10},{3,11},{8,16},{9,17},{10,18},{11,19},{16,24},{1... | collective-permute-start | bytes 393224 | tf_op jit(solution)/shard_map/ppermute | solution.py:282
  49.1 13.6 %collective-permute-start.2 = (bf16[4,2,2,32,128]{4,3,2,1,0:T(8,128)(2,1)S(1)}, bf16[4,2,2,32,128]{4,3,2,1,0:T(8,128)(2,1)S(1)}, u32[]{:S(2)}, u32[]{:S(2)}) collective-permute-start(bf16[4,2,2,32,128]{4,3,2,1,0:T(8,128)(2,1)S(1)} %bitcast.26), channel_id=1, source_target_pairs={{8,0},{9,1},{10,2},{11,3},{16,8},{17,9},{18,10},{19,11},{24,16},{2... | collective-permute-start | bytes 393224 | tf_op jit(solution)/shard_map/ppermute | solution.py:282
  50.4 0.7 copy-start.5
  50.4 0.8 copy-start.6
  51.2 0.9 copy-start.4
  62.7 0.7 copy-start.7
  62.7 0.7 copy-start.8
  74.2 2.5 %collective-permute-start.5 = (bf16[4,6,128,128]{3,2,1,0:T(8,128)(2,1)}, bf16[4,6,128,128]{3,2,1,0:T(8,128)(2,1)S(1)}, u32[]{:S(2)}, u32[]{:S(2)}) collective-permute-start(bf16[4,6,128,128]{3,2,1,0:T(8,128)(2,1)} %get-tuple-element.23), channel_id=1, source_target_pairs={{0,4},{4,0},{1,5},{5,1},{2,6},{6,2},{3,7},{7,3},{8,12},{12,8},{9,1... | collective-permute-start | bytes 2359304 | tf_op jit(solution)/shard_map/ppermute | solution.py:238
  78.1 29.6 %copy-start.3 = (bf16[8,2,2,16,128]{4,3,2,1,0:T(8,128)(2,1)S(1)}, bf16[8,2,2,16,128]{4,3,2,1,0:T(8,128)(2,1)}, u32[]{:S(2)}) copy-start(bf16[8,2,2,16,128]{4,3,2,1,0:T(8,128)(2,1)} %get-tuple-element.24) | copy-start | bytes 393220

commit v4 on v3

--- a/solution.py
+++ b/solution.py
@@ -54,19 +54,27 @@
             target[unit] = piece.astype(BF16)
 
 
-def place_kernels(place_ref, w_ref, mine_ref, other_ref):
-    core = place_ref[4]
-    w_ref[core] = mine_ref[...]
-    w_ref[1 - core] = other_ref[...]
-
-
-def forward_kernel(
-    geometry, place_ref, mine_ref, other_ref, own_ref, above_ref, below_ref, xo_ref, ho_ref, *rest
-):
+def place_kernels(place_ref, w_ref, spatial_ref, temporal_ref, mine_refs, other_refs):
+    core, section = place_ref[4], place_ref[5]
+    cores, _, taps = w_ref.shape[:3]
+    count = spatial_ref.shape[1]
+    for tap in range(cores * taps):
+        one = spatial_ref[0, tap] if tap < count else temporal_ref[0, tap - count]
+        w_ref[tap // taps, section, tap % taps] = one
+    for step, (mine_ref, other_ref) in enumerate(zip(mine_refs, other_refs)):
+        block = jnp.bitwise_xor(section, step + 1)
+        w_ref[core, block] = mine_ref[...]
+        w_ref[1 - core, block] = other_ref[...]
+
+
+def forward_kernel(geometry, place_ref, *rest):
     blocks, cores, group, frames_in, rows_in, halo, tile, width = geometry
-    d_refs = rest[:blocks]
-    x_ref, h_ref, mask_ref, w_ref = rest[blocks:]
-    place_kernels(place_ref, w_ref, mine_ref, other_ref)
+    shared, rest = rest[: 2 * blocks], rest[2 * blocks :]
+    own_ref, inner_ref, outer_ref, xo_ref, ho_ref = rest[:5]
+    d_refs = rest[5 : 5 + blocks]
+    x_ref, h_ref, mask_ref, w_ref = rest[5 + blocks :]
+    place_kernels(place_ref, w_ref, shared[0], shared[1], shared[2 : 1 + blocks], shared[1 + blocks :])
+    odd = place_ref[6] == 1
     frames = cores * frames_in
     high = tile + 2 * halo
     chans = w_ref.shape[-1]
@@ -93,11 +101,12 @@
 
     for frame in range(frames):
         core, inner = divmod(frame, frames_in)
-        pieces = [
-            ref[core * group + unit, inner]
-            for ref in (above_ref, own_ref, below_ref)
-            for unit in range(group)
-        ]
+        units = [core * group + unit for unit in range(group)]
+        near = [inner_ref[unit, inner] for unit in units]
+        far = [outer_ref[unit, inner] for unit in units]
+        pieces = [jnp.where(odd, a, b) for a, b in zip(near, far)]
+        pieces += [own_ref[unit, inner] for unit in units]
+        pieces += [jnp.where(odd, b, a) for a, b in zip(near, far)]
         whole = jnp.concatenate(pieces, 0).reshape(high * width, chans)
         keep(0, frame, whole.astype(F32), 0)
 
@@ -145,13 +154,14 @@
             keep(block + 1, frame, new.astype(BF16).astype(F32), first)
 
 
-def backward_kernel(
-    geometry, factor, place_ref, mine_ref, other_ref, own_ref, above_ref, below_ref, xo_ref, ho_ref, *rest
-):
+def backward_kernel(geometry, factor, place_ref, *rest):
     blocks, cores, group, frames_in, rows_in, halo, tile, width = geometry
-    d_refs = rest[:blocks]
-    keep_ref, give_ref, out_ref, g_ref, da_ref, dao_ref, go_ref, w_ref, grad_ref = rest[blocks:]
-    place_kernels(place_ref, w_ref, mine_ref, other_ref)
+    shared, rest = rest[: 2 * blocks], rest[2 * blocks :]
+    own_ref, inner_ref, outer_ref, xo_ref, ho_ref = rest[:5]
+    d_refs = rest[5 : 5 + blocks]
+    keep_ref, give_ref, out_ref, g_ref, da_ref, dao_ref, go_ref, w_ref, grad_ref = rest[5 + blocks :]
+    place_kernels(place_ref, w_ref, shared[0], shared[1], shared[2 : 1 + blocks], shared[1 + blocks :])
+    odd = place_ref[6] == 1
     frames = cores * frames_in
     chans = w_ref.shape[-1]
     rim = blocks
@@ -162,14 +172,17 @@
     for frame in range(frames):
         core, inner = divmod(frame, frames_in)
         half = group // 2
-        pieces = [above_ref[core * half + unit, inner] for unit in range(half)]
+        near = [inner_ref[core * half + unit, inner] for unit in range(half)]
+        far = [outer_ref[core * half + unit, inner] for unit in range(half)]
+        pieces = [jnp.where(odd, a, b) for a, b in zip(near, far)]
         pieces += [own_ref[core * group + unit, inner] for unit in range(group)]
-        pieces += [below_ref[core * half + unit, inner] for unit in range(half)]
+        pieces += [jnp.where(odd, b, a) for a, b in zip(near, far)]
         g_ref[frame] = jnp.concatenate(pieces, 0)
 
     def put(block, tap, value):
         slot = jnp.where(place_ref[4] == tap // per_core, 0, 1)
-        grad_ref[slot, block, tap % per_core] = (value * factor).astype(BF16)
+        where = jnp.bitwise_xor(place_ref[5], block)
+        grad_ref[slot, where, tap % per_core] = (value * factor).astype(BF16)
 
     for block in reversed(range(blocks)):
         edge = block + 1
@@ -234,8 +247,9 @@
     give_ref[...] = grad_ref[1]
 
 
-def swapped(value):
-    return lax.ppermute(value, "tm", [(0, 1), (1, 0)])
+def swapped(value, axis="tm", step=1):
+    count = lax.axis_size(axis)
+    return lax.ppermute(value, axis, [(i, i ^ step) for i in range(count)])
 
 
 def own_half(spatial_weights, temporal_weights):
@@ -276,38 +290,45 @@
     def spread(value):
         return lax.all_to_all(value, ("tm", "space"), 0, 0, axis_index_groups=sets, tiled=True)
 
-    def moved(value, step):
-        rows = blocks * tiles
-        pairs = [(i, i + step) for i in range(rows) if 0 <= i + step < rows]
+    bands = blocks * tiles // group
+    place = lax.axis_index("space")
+    band = (lax.axis_index("section") * tiles + place) // group
+    odd = band % 2
+
+    def traded(value, shift):
+        pairs = []
+        for one in range(bands):
+            other = ((one + shift) ^ 1) - shift
+            if 0 <= other < bands:
+                pairs += [(one * group + i, other * group + i) for i in range(group)]
         return lax.ppermute(value, ("section", "space"), pairs)
 
+    half_kernels = own_half(spatial_weights, temporal_weights)
+    mine = [swapped(half_kernels, "section", step) for step in range(1, blocks)]
     own_video = spread(video_windows)
-    half_kernels = own_half(spatial_weights, temporal_weights)
-    mine = lax.all_to_all(
-        jnp.broadcast_to(half_kernels[None], (blocks,) + half_kernels.shape),
-        "section", 0, 0, tiled=True,
-    )
-    video_above, video_below = moved(own_video, group), moved(own_video, -group)
-    other = swapped(mine)
+    video_near, video_far = traded(own_video, 0), traded(own_video, 1)
+    shared = [spatial_weights, temporal_weights] + mine + [swapped(each) for each in mine]
 
     own_cot = spread(cot_windows)
     half = group // 2
     split = own_cot.reshape((cores, group) + own_cot.shape[1:])
     edge = (cores * half,) + own_cot.shape[1:]
-    cot_above = moved(split[:, half:].reshape(edge), group)
-    cot_below = moved(split[:, :half].reshape(edge), -group)
-
-    place = lax.axis_index("space")
-    band = (lax.axis_index("section") * tiles + place) // group
+    cot_near = traded(lax.dynamic_slice_in_dim(split, (1 - odd) * half, half, 1).reshape(edge), 0)
+    cot_far = traded(lax.dynamic_slice_in_dim(split, odd * half, half, 1).reshape(edge), 1)
+
     unit = lax.axis_index("tm") * group + place % group
     total_rows = blocks * tiles * rows_in
     corner = jnp.stack(
-        [band * tile - halo, unit * own_width - halo, total_rows, columns, lax.axis_index("tm")]
+        [
+            band * tile - halo, unit * own_width - halo, total_rows, columns,
+            lax.axis_index("tm"), lax.axis_index("section"), odd,
+        ]
     ).astype(jnp.int32)
     geometry = (blocks, cores, group, frames_in, rows_in, halo, tile, width)
     frames = cores * frames_in
     high = tile + 2 * halo
-    all_kernels = (cores,) + mine.shape
+    per_section = (blocks,) + half_kernels.shape
+    all_kernels = (cores,) + per_section
     saved = [
         jax.ShapeDtypeStruct((frames, tile + 2 * block + 2, width, chans), F32)
         for block in range(blocks)
@@ -316,7 +337,7 @@
     features, hidden, *slopes = pl.pallas_call(
         functools.partial(forward_kernel, geometry),
         name="forward",
-        in_specs=[smem] + [vmem] * 5,
+        in_specs=[smem] + [vmem] * (2 * blocks + 3),
         out_specs=[vmem] * (2 + blocks),
         out_shape=[
             jax.ShapeDtypeStruct((blocks, frames, tile + 2, own_width, 3 * chans), BF16),
@@ -331,18 +352,18 @@
         ],
         compiler_params=params,
         cost_estimate=cost,
-    )(corner, mine, other, own_video, video_above, video_below)
+    )(corner, *shared, own_video, video_near, video_far)
 
     pixel_count = frames * total_rows * columns
     factor = 1.0 / float(pixel_count) ** 0.5
     keep, give, tile_grad = pl.pallas_call(
         functools.partial(backward_kernel, geometry, factor),
         name="backward",
-        in_specs=[smem] + [vmem] * (7 + blocks),
+        in_specs=[smem] + [vmem] * (3 * blocks + 5),
         out_specs=[vmem] * 3,
         out_shape=[
-            jax.ShapeDtypeStruct(mine.shape, BF16),
-            jax.ShapeDtypeStruct(mine.shape, BF16),
+            jax.ShapeDtypeStruct(per_section, BF16),
+            jax.ShapeDtypeStruct(per_section, BF16),
             jax.ShapeDtypeStruct((parties, frames_in, rows_in, own_width, chans), BF16),
         ],
         scratch_shapes=[
@@ -355,24 +376,35 @@
         ],
         compiler_params=params,
         cost_estimate=cost,
-    )(corner, mine, other, own_cot, cot_above, cot_below, features, hidden, *slopes)
-
-    part = (keep.astype(F32) + swapped(give).astype(F32)).astype(BF16)
-    part = lax.all_to_all(part, "section", 0, 0, tiled=True)
-    part = part.astype(F32).sum(0).astype(BF16)
-    part = lax.all_to_all(part.reshape(tiles, -1, chans), "space", 0, 0, tiled=True)
-    part = part.astype(F32).sum(0).astype(BF16)
-    shares = jnp.broadcast_to(part[None], (cores * tiles,) + part.shape)
-    back = tile_grad.reshape(parties, -1, chans)
-    everyone = ("tm", "space")
-    if sets is None:
-        got = lax.all_to_all(
-            jnp.concatenate([shares, back], 1), everyone, 0, 0, tiled=True
+    )(corner, *shared, own_cot, cot_near, cot_far, features, hidden, *slopes)
+
+    got = swapped(give)
+    parts = [(keep[i].astype(F32) + got[i].astype(F32)).astype(BF16) for i in range(blocks)]
+    back = spread(tile_grad)
+    parts = parts[:1] + [swapped(parts[i], "section", i) for i in range(1, blocks)]
+    part = sum(each.astype(F32) for each in parts).astype(BF16)
+    units = part.reshape(group, -1, chans)
+    unit = place % group
+
+    def chunk(step):
+        return lax.dynamic_index_in_dim(units, unit ^ step, 0, keepdims=False)
+
+    parts = [chunk(0)] + [swapped(chunk(i), "space", i) for i in range(1, group)]
+    part = sum(each.astype(F32) for each in parts)
+    if sets is not None:
+        part = lax.psum(
+            part, "space", axis_index_groups=[list(range(i, tiles, group)) for i in range(group)]
         )
-        whole, back = got[:, : part.shape[0]], got[:, part.shape[0] :]
-    else:
-        whole, back = lax.all_to_all(shares, everyone, 0, 0, tiled=True), spread(back)
-    back = back.reshape(parties, frames_in, rows_in, own_width, chans)
+    part = part.astype(BF16)
+    mine = [part] + [swapped(part, "space", i) for i in range(1, group)]
+    other = [swapped(each) for each in mine]
+    core = lax.axis_index("tm")
+    whole = jnp.zeros((cores, group) + part.shape, BF16)
+    for which, chunks in ((core, mine), (1 - core, other)):
+        for step, each in enumerate(chunks):
+            whole = lax.dynamic_update_slice(
+                whole, each[None, None], (which, unit ^ step, 0, 0)
+            )
     grad_video = back.transpose(1, 2, 0, 3, 4).reshape(video.shape)
     own = whole.reshape(-1, chans, chans).swapaxes(1, 2).astype(F32)[None]
     count = spatial_weights.shape[1]

time: 129 us -> 115 us (0.89)
  blocking collectives: 46.8 us -> 15.7 us
  starting transfers between devices: 24.7 us -> 34.4 us
  waiting for transfers between devices: 23 us -> 31.3 us
    all_to_all x3 -> x1, blocking collectives: 46.8 us -> 15.7 us  [spread(): lax.all_to_all(value, ('tm', 'space'), 0, 0, axis_index_groups=sets, tile...]
    ppermute x6 -> x24, waiting for transfers between devices: 2.3 us -> 26.3 us  [the longest x20 24.5 us: swapped(): return lax.ppermute(value, axis, [(i, i ^ step) for i in range(count)])]
    ppermute x6 -> x24, starting transfers between devices: 11.2 us -> 25.9 us  [the longest x20 21.6 us: swapped(): return lax.ppermute(value, axis, [(i, i ^ step) for i in range(count)])]
    all_to_all x1 -> x0, waiting for transfers between devices: 9.01 us -> none  [on_device(): lax.all_to_all(jnp.broadcast_to(half_kernels[None], (blocks,) + half_kern...]
    all_to_all x2, waiting for transfers between devices: 11.7 us -> 5.04 us  [spread(): lax.all_to_all(value, ('tm', 'space'), 0, 0, axis_index_groups=sets, tile...]
    all_to_all x1 -> x0, starting transfers between devices: 5.16 us -> none  [on_device(): lax.all_to_all(jnp.broadcast_to(half_kernels[None], (blocks,) + half_kern...]
    unnamed x20 -> x26, local copies, waits for them, and re-layouts: 4.19 us -> 3.92 us
  transfers between devices with their start and end apart: 9 -> 26, of which waited for: 4 -> 12; matrix products, arithmetic and copies ran while one was open for 0% -> 2% of each run, Pallas kernels for 10% -> 9%
where the time goes in v4:
time: 115 us
  starting transfers between devices  34.4 us (30%)
  waiting for transfers between devices  31.3 us (27%)
  Pallas kernels  23.5 us (20%)
  blocking collectives  15.7 us (14%)
  local copies, waits for them, and re-layouts  5.41 us (5%)
  other arithmetic  3.46 us (3%)
    ppermute x20, waiting for transfers between devices, swapped(): return lax.ppermute(value, axis, [(i, i ^ step) for i in range(count)])  24.5 us
    ppermute x20, starting transfers between devices, swapped(): return lax.ppermute(value, axis, [(i, i ^ step) for i in range(count)])  21.6 us
    all_to_all x1, blocking collectives, spread(): lax.all_to_all(value, ('tm', 'space'), 0, 0, axis_index_groups=sets, tile...  15.7 us
    pallas_call x1, Pallas kernels, on_device(): pl.pallas_call(functools.partial(backward_kernel, geometry, factor), name...  11 us
    pallas_call x1, Pallas kernels, on_device(): pl.pallas_call(functools.partial(forward_kernel, geometry), name='forward...  10.7 us
    all_to_all x2, starting transfers between devices, spread(): lax.all_to_all(value, ('tm', 'space'), 0, 0, axis_index_groups=sets, tile...  8.44 us
    all_to_all x2, waiting for transfers between devices, spread(): lax.all_to_all(value, ('tm', 'space'), 0, 0, axis_index_groups=sets, tile...  5.04 us
    ppermute x4, starting transfers between devices, traded(): return lax.ppermute(value, ('section', 'space'), pairs)  4.33 us
  transfers between devices with their start and end apart: 26, of which 12 were waited for; matrix products, arithmetic and copies ran while one was open for 2% of the time, Pallas kernels for 9%

profile of v4, /device:TPU:0, one launch (start us, length us, event | category | flops | bytes accessed | tf_op | source)
XLA Modules:
  0.0 114.7 jit_solution(17686536050551290731)
XLA Ops:
  0.6 1.8 %windows.1 = (bf16[8,2,2,32,128]{4,3,2,1,0:T(8,128)(2,1)}, bf16[8,2,2,32,128]{4,3,2,1,0:T(8,128)(2,1)}) custom-call(bf16[2,2,128,128]{3,2,1,0:T(8,128)(2,1)} %video_ref.1, bf16[2,2,128,128]{3,2,1,0:T(8,128)(2,1)} %cot_ref.1), custom_call_target="tpu_custom_call" | custom-call | tf_op jit(solution)/shard_map/windows/pallas_call | solution.py:281
  2.5 15.7 %all_to_all.15.rest_8_ = bf16[8,2,2,32,128]{4,3,2,1,0:T(8,128)(2,1)S(1)} all-to-all(bf16[8,2,2,32,128]{4,3,2,1,0:T(8,128)(2,1)} %get-tuple-element.15), channel_id=1, replica_groups=mesh['section'=4,'tm'=2,'space'=4] {'tm','space'}, dimensions={0} | all-to-all | bytes 524288 | tf_op jit(solution)/shard_map/all_to_all | solution.py:291
  18.2 3.4 %all-to-all-start = ((bf16[8,2,2,32,128]{4,3,2,1,0:T(8,128)(2,1)}), bf16[8,2,2,32,128]{4,3,2,1,0:T(8,128)(2,1)S(1)}, u32[]{:S(2)}, u32[]{:S(2)}) async-start(bf16[8,2,2,32,128]{4,3,2,1,0:T(8,128)(2,1)} %get-tuple-element.14), calls=%async_computation | async-start | bytes 524288 | tf_op jit(solution)/shard_map/all_to_all | solution.py:291
  22.6 1.6 %collective-permute-start = (bf16[6,128,128]{2,1,0:T(8,128)(2,1)S(1)}, bf16[6,128,128]{2,1,0:T(8,128)(2,1)S(1)}, u32[]{:S(2)}, u32[]{:S(2)}) collective-permute-start(bf16[6,128,128]{2,1,0:T(8,128)(2,1)S(1)} %fusion.7), channel_id=1, source_target_pairs={{0,8},{8,0},{16,24},{24,16},{1,9},{9,1},{17,25},{25,17},{2,10},{10... | collective-permute-start | bytes 589832 | tf_op jit(solution)/shard_map/ppermute | solution.py:252
  24.2 1.5 %collective-permute-start.1 = (bf16[6,128,128]{2,1,0:T(8,128)(2,1)S(1)}, bf16[6,128,128]{2,1,0:T(8,128)(2,1)S(1)}, u32[]{:S(2)}, u32[]{:S(2)}) collective-permute-start(bf16[6,128,128]{2,1,0:T(8,128)(2,1)S(1)} %fusion.7), channel_id=1, source_target_pairs={{0,16},{8,24},{16,0},{24,8},{1,17},{9,25},{17,1},{25,9},{2,18},{10... | collective-permute-start | bytes 589832 | tf_op jit(solution)/shard_map/ppermute | solution.py:252
  26.2 1.5 %collective-permute-start.8 = (bf16[8,2,2,32,128]{4,3,2,1,0:T(8,128)(2,1)S(1)}, bf16[8,2,2,32,128]{4,3,2,1,0:T(8,128)(2,1)S(1)}, u32[]{:S(2)}, u32[]{:S(2)}) collective-permute-start(bf16[8,2,2,32,128]{4,3,2,1,0:T(8,128)(2,1)S(1)} %all_to_all.15.rest_8_), channel_id=1, source_target_pairs={{0,8},{1,9},{2,10},{3,11},{8,0},{9,1},{10,2},{11,3},{16,24},{17,25... | collective-permute-start | bytes 786440 | tf_op jit(solution)/shard_map/ppermute | solution.py:304
  28.3 2.1 %collective-permute-done.rest_2_ = bf16[6,128,128]{2,1,0:T(8,128)(2,1)S(1)} collective-permute-done((bf16[6,128,128]{2,1,0:T(8,128)(2,1)S(1)}, bf16[6,128,128]{2,1,0:T(8,128)(2,1)S(1)}, u32[]{:S(2)}, u32[]{:S(2)}) %collective-permute-start) | collective-permute-done | bytes 196640 | tf_op jit(solution)/shard_map/ppermute | solution.py:252
  30.4 4.7 %collective-permute-done.1.rest_3_ = bf16[6,128,128]{2,1,0:T(8,128)(2,1)S(1)} collective-permute-done((bf16[6,128,128]{2,1,0:T(8,128)(2,1)S(1)}, bf16[6,128,128]{2,1,0:T(8,128)(2,1)S(1)}, u32[]{:S(2)}, u32[]{:S(2)}) %collective-permute-start.1) | collective-permute-done | bytes 196640 | tf_op jit(solution)/shard_map/ppermute | solution.py:252
  36.2 1.5 %collective-permute-start.6 = (bf16[4,2,2,32,128]{4,3,2,1,0:T(8,128)(2,1)S(1)}, bf16[4,2,2,32,128]{4,3,2,1,0:T(8,128)(2,1)S(1)}, u32[]{:S(2)}, u32[]{:S(2)}) collective-permute-start(bf16[4,2,2,32,128]{4,3,2,1,0:T(8,128)(2,1)S(1)} %bitcast.64), channel_id=1, source_target_pairs={{0,8},{1,9},{2,10},{3,11},{8,0},{9,1},{10,2},{11,3},{16,24},{17,25... | collective-permute-start | bytes 393224 | tf_op jit(solution)/shard_map/ppermute | solution.py:304
  38.4 1.8 %collective-permute-done.8.rest_9_ = bf16[8,2,2,32,128]{4,3,2,1,0:T(8,128)(2,1)S(1)} collective-permute-done((bf16[8,2,2,32,128]{4,3,2,1,0:T(8,128)(2,1)S(1)}, bf16[8,2,2,32,128]{4,3,2,1,0:T(8,128)(2,1)S(1)}, u32[]{:S(2)}, u32[]{:S(2)}) %collective-permute-start.8) | collective-permute-done | bytes 262176 | tf_op jit(solution)/shard_map/ppermute | solution.py:304
  41.7 10.7 %forward.1 = (bf16[4,4,10,16,384]{4,3,2,1,0:T(8,128)(2,1)}, bf16[4,4,8,16,128]{4,3,2,1,0:T(8,128)(2,1)}, f32[4,10,32,128]{3,2,1,0:T(8,128)}, f32[4,12,32,128]{3,...) custom-call(s32[7]{0:T(128)} %stack.23.place_ref, bf16[1,9,128,128]{3,2,1,0:T(8,128)(2,1)} %rest_0_.3, ...), custom_call_target="tpu_custom_call" | custom-call | flops 6000000000 | bytes 8000000 | tf_op jit(solution)/shard_map/forward/pallas_call | solution.py:337
  53.1 11.0 %backward.1 = (bf16[4,6,128,128]{3,2,1,0:T(8,128)(2,1)}, bf16[4,6,128,128]{3,2,1,0:T(8,128)(2,1)}, bf16[8,2,2,16,128]{4,3,2,1,0:T(8,128)(2,1)}) custom-call(s32[7]{0:T(128)} %stack.23.place_ref, bf16[1,9,128,128]{3,2,1,0:T(8,128)(2,1)} %rest_0_.3, bf16[1,3,128,128]{3,2,1,0:T(8,128)(2,1)} %rest_1_.3, bf16[6,128,128]{2,1,0:T(8,128)(2,1)} %copy-done.4, ...), custom_call_target="tpu_custom_call" | custom-call | flops 6000000000 | bytes 8000000 | tf_op jit(solution)/shard_map/backward/pallas_call | solution.py:359
  64.1 2.5 %collective-permute-done.10 = bf16[4,6,128,128]{3,2,1,0:T(8,128)(2,1)S(1)} collective-permute-done((bf16[4,6,128,128]{3,2,1,0:T(8,128)(2,1)}, bf16[4,6,128,128]{3,2,1,0:T(8,128)(2,1)S(1)}, u32[]{:S(2)}, u32[]{:S(2)}) %collective-permute-start.10) | collective-permute-done | bytes 786464 | tf_op jit(solution)/shard_map/ppermute | solution.py:252
  67.8 7.4 %collective-permute-start.11 = (bf16[6,128,128]{2,1,0:T(8,128)(2,1)S(1)}, bf16[6,128,128]{2,1,0:T(8,128)(2,1)S(1)}, u32[]{:S(2)}, u32[]{:S(2)}) collective-permute-start(bf16[6,128,128]{2,1,0:T(8,128)(2,1)S(1)} %get-tuple-element.30), channel_id=1, source_target_pairs={{0,8},{8,0},{16,24},{24,16},{1,9},{9,1},{17,25},{25,17},{2,10},{10... | collective-permute-start | bytes 589832 | tf_op jit(solution)/shard_map/ppermute | solution.py:252
  75.3 1.5 %collective-permute-start.13 = (bf16[6,128,128]{2,1,0:T(8,128)(2,1)S(1)}, bf16[6,128,128]{2,1,0:T(8,128)(2,1)S(1)}, u32[]{:S(2)}, u32[]{:S(2)}) collective-permute-start(bf16[6,128,128]{2,1,0:T(8,128)(2,1)S(1)} %get-tuple-element.31), channel_id=1, source_target_pairs={{0,24},{8,16},{16,8},{24,0},{1,25},{9,17},{17,9},{25,1},{2,26},{10... | collective-permute-start | bytes 589832 | tf_op jit(solution)/shard_map/ppermute | solution.py:252
  76.8 4.1 %collective-permute-done.11 = bf16[6,128,128]{2,1,0:T(8,128)(2,1)S(1)} collective-permute-done((bf16[6,128,128]{2,1,0:T(8,128)(2,1)S(1)}, bf16[6,128,128]{2,1,0:T(8,128)(2,1)S(1)}, u32[]{:S(2)}, u32[]{:S(2)}) %collective-permute-start.11) | collective-permute-done | bytes 196640 | tf_op jit(solution)/shard_map/ppermute | solution.py:252
  81.0 5.2 %collective-permute-done.12 = bf16[6,128,128]{2,1,0:T(8,128)(2,1)S(1)} collective-permute-done((bf16[6,128,128]{2,1,0:T(8,128)(2,1)S(1)}, bf16[6,128,128]{2,1,0:T(8,128)(2,1)S(1)}, u32[]{:S(2)}, u32[]{:S(2)}) %collective-permute-start.12) | collective-permute-done | bytes 196640 | tf_op jit(solution)/shard_map/ppermute | solution.py:252
  87.2 2.0 %collective-permute-start.14 = (bf16[192,128]{1,0:T(8,128)(2,1)S(1)}, bf16[192,128]{1,0:T(8,128)(2,1)S(1)}, u32[]{:S(2)}, u32[]{:S(2)}) collective-permute-start(bf16[192,128]{1,0:T(8,128)(2,1)S(1)} %get-tuple-element.35), channel_id=1, source_target_pairs={{0,1},{1,0},{2,3},{3,2},{4,5},{5,4},{6,7},{7,6},{8,9},{9,8},{10,11... | collective-permute-start | bytes 147464 | tf_op jit(solution)/shard_map/ppermute | solution.py:252
  89.3 2.4 %collective-permute-start.15 = (bf16[192,128]{1,0:T(8,128)(2,1)S(1)}, bf16[192,128]{1,0:T(8,128)(2,1)S(1)}, u32[]{:S(2)}, u32[]{:S(2)}) collective-permute-start(bf16[192,128]{1,0:T(8,128)(2,1)S(1)} %get-tuple-element.37), channel_id=1, source_target_pairs={{0,2},{1,3},{2,0},{3,1},{4,6},{5,7},{6,4},{7,5},{8,10},{9,11},{10,... | collective-permute-start | bytes 147464 | tf_op jit(solution)/shard_map/ppermute | solution.py:252
  91.7 5.0 %all-to-all-start.2 = ((bf16[8,2,2,16,128]{4,3,2,1,0:T(8,128)(2,1)}), bf16[8,2,2,16,128]{4,3,2,1,0:T(8,128)(2,1)S(1)}, u32[]{:S(2)}, u32[]{:S(2)}) async-start(bf16[8,2,2,16,128]{4,3,2,1,0:T(8,128)(2,1)} %get-tuple-element.24), calls=%async_computation.2 | async-start | bytes 262144 | tf_op jit(solution)/shard_map/all_to_all | solution.py:291
  97.6 1.3 %collective-permute-start.17 = (bf16[192,128]{1,0:T(8,128)(2,1)S(1)}, bf16[192,128]{1,0:T(8,128)(2,1)S(1)}, u32[]{:S(2)}, u32[]{:S(2)}) collective-permute-start(bf16[192,128]{1,0:T(8,128)(2,1)S(1)} %get-tuple-element.29), channel_id=1, source_target_pairs={{0,1},{1,0},{2,3},{3,2},{4,5},{5,4},{6,7},{7,6},{8,9},{9,8},{10,11... | collective-permute-start | bytes 147464 | tf_op jit(solution)/shard_map/ppermute | solution.py:252
  98.9 5.0 %all-to-all-done.2 = bf16[8,2,2,16,128]{4,3,2,1,0:T(8,128)(2,1)S(1)} async-done(((bf16[8,2,2,16,128]{4,3,2,1,0:T(8,128)(2,1)}), bf16[8,2,2,16,128]{4,3,2,1,0:T(8,128)(2,1)S(1)}, u32[]{:S(2)}, u32[]{:S(2)}) %all-to-all-start.2) | async-done | bytes 131104 | tf_op jit(solution)/shard_map/all_to_all | solution.py:291
  104.7 2.2 %collective-permute-start.19 = (bf16[192,128]{1,0:T(8,128)(2,1)S(1)}, bf16[192,128]{1,0:T(8,128)(2,1)S(1)}, u32[]{:S(2)}, u32[]{:S(2)}) collective-permute-start(bf16[192,128]{1,0:T(8,128)(2,1)S(1)} %get-tuple-element.29), channel_id=1, source_target_pairs={{0,3},{1,2},{2,1},{3,0},{4,7},{5,6},{6,5},{7,4},{8,11},{9,10},{10,... | collective-permute-start | bytes 147464 | tf_op jit(solution)/shard_map/ppermute | solution.py:252
  107.4 3.8 %collective-permute-done.18 = bf16[192,128]{1,0:T(8,128)(2,1)S(1)} collective-permute-done((bf16[192,128]{1,0:T(8,128)(2,1)S(1)}, bf16[192,128]{1,0:T(8,128)(2,1)S(1)}, u32[]{:S(2)}, u32[]{:S(2)}) %collective-permute-start.18) | collective-permute-done | bytes 49184 | tf_op jit(solution)/shard_map/ppermute | solution.py:252
  (77 shorter events, 14.0 us)
Async XLA Ops:
  18.2 18.0 %all-to-all-start = ((bf16[8,2,2,32,128]{4,3,2,1,0:T(8,128)(2,1)}), bf16[8,2,2,32,128]{4,3,2,1,0:T(8,128)(2,1)S(1)}, u32[]{:S(2)}, u32[]{:S(2)}) async-start(bf16[8,2,2,32,128]{4,3,2,1,0:T(8,128)(2,1)} %get-tuple-element.14), calls=%async_computation | async-start | bytes 524288 | tf_op jit(solution)/shard_map/all_to_all | solution.py:291
  22.6 7.8 %collective-permute-start = (bf16[6,128,128]{2,1,0:T(8,128)(2,1)S(1)}, bf16[6,128,128]{2,1,0:T(8,128)(2,1)S(1)}, u32[]{:S(2)}, u32[]{:S(2)}) collective-permute-start(bf16[6,128,128]{2,1,0:T(8,128)(2,1)S(1)} %fusion.7), channel_id=1, source_target_pairs={{0,8},{8,0},{16,24},{24,16},{1,9},{9,1},{17,25},{25,17},{2,10},{10... | collective-permute-start | bytes 589832 | tf_op jit(solution)/shard_map/ppermute | solution.py:252
  24.2 10.9 %collective-permute-start.1 = (bf16[6,128,128]{2,1,0:T(8,128)(2,1)S(1)}, bf16[6,128,128]{2,1,0:T(8,128)(2,1)S(1)}, u32[]{:S(2)}, u32[]{:S(2)}) collective-permute-start(bf16[6,128,128]{2,1,0:T(8,128)(2,1)S(1)} %fusion.7), channel_id=1, source_target_pairs={{0,16},{8,24},{16,0},{24,8},{1,17},{9,25},{17,1},{25,9},{2,18},{10... | collective-permute-start | bytes 589832 | tf_op jit(solution)/shard_map/ppermute | solution.py:252
  25.7 9.9 %collective-permute-start.2 = (bf16[6,128,128]{2,1,0:T(8,128)(2,1)S(1)}, bf16[6,128,128]{2,1,0:T(8,128)(2,1)S(1)}, u32[]{:S(2)}, u32[]{:S(2)}) collective-permute-start(bf16[6,128,128]{2,1,0:T(8,128)(2,1)S(1)} %fusion.7), channel_id=1, source_target_pairs={{0,24},{8,16},{16,8},{24,0},{1,25},{9,17},{17,9},{25,1},{2,26},{10... | collective-permute-start | bytes 589832 | tf_op jit(solution)/shard_map/ppermute | solution.py:252
  26.2 14.1 %collective-permute-start.8 = (bf16[8,2,2,32,128]{4,3,2,1,0:T(8,128)(2,1)S(1)}, bf16[8,2,2,32,128]{4,3,2,1,0:T(8,128)(2,1)S(1)}, u32[]{:S(2)}, u32[]{:S(2)}) collective-permute-start(bf16[8,2,2,32,128]{4,3,2,1,0:T(8,128)(2,1)S(1)} %all_to_all.15.rest_8_), channel_id=1, source_target_pairs={{0,8},{1,9},{2,10},{3,11},{8,0},{9,1},{10,2},{11,3},{16,24},{17,25... | collective-permute-start | bytes 786440 | tf_op jit(solution)/shard_map/ppermute | solution.py:304
  27.6 12.6 %collective-permute-start.9 = (bf16[8,2,2,32,128]{4,3,2,1,0:T(8,128)(2,1)S(1)}, bf16[8,2,2,32,128]{4,3,2,1,0:T(8,128)(2,1)S(1)}, u32[]{:S(2)}, u32[]{:S(2)}) collective-permute-start(bf16[8,2,2,32,128]{4,3,2,1,0:T(8,128)(2,1)S(1)} %all_to_all.15.rest_8_), channel_id=1, source_target_pairs={{8,16},{9,17},{10,18},{11,19},{16,8},{17,9},{18,10},{19,11},{12,20... | collective-permute-start | bytes 786440 | tf_op jit(solution)/shard_map/ppermute | solution.py:304
  30.4 5.8 %collective-permute-start.3 = (bf16[6,128,128]{2,1,0:T(8,128)(2,1)S(1)}, bf16[6,128,128]{2,1,0:T(8,128)(2,1)S(1)}, u32[]{:S(2)}, u32[]{:S(2)}) collective-permute-start(bf16[6,128,128]{2,1,0:T(8,128)(2,1)S(1)} %collective-permute-done.rest_2_), channel_id=1, source_target_pairs={{0,4},{4,0},{1,5},{5,1},{2,6},{6,2},{3,7},{7,3},{8,12},{12,8},{9,1... | collective-permute-start | bytes 589832 | tf_op jit(solution)/shard_map/ppermute | solution.py:252
  35.1 2.7 %collective-permute-start.4 = (bf16[6,128,128]{2,1,0:T(8,128)(2,1)S(1)}, bf16[6,128,128]{2,1,0:T(8,128)(2,1)S(1)}, u32[]{:S(2)}, u32[]{:S(2)}) collective-permute-start(bf16[6,128,128]{2,1,0:T(8,128)(2,1)S(1)} %collective-permute-done.1.rest_3_), channel_id=1, source_target_pairs={{0,4},{4,0},{1,5},{5,1},{2,6},{6,2},{3,7},{7,3},{8,12},{12,8},{9,1... | collective-permute-start | bytes 589832 | tf_op jit(solution)/shard_map/ppermute | solution.py:252
  35.6 2.8 %collective-permute-start.5 = (bf16[6,128,128]{2,1,0:T(8,128)(2,1)S(1)}, bf16[6,128,128]{2,1,0:T(8,128)(2,1)S(1)}, u32[]{:S(2)}, u32[]{:S(2)}) collective-permute-start(bf16[6,128,128]{2,1,0:T(8,128)(2,1)S(1)} %collective-permute-done.2.rest_4_), channel_id=1, source_target_pairs={{0,4},{4,0},{1,5},{5,1},{2,6},{6,2},{3,7},{7,3},{8,12},{12,8},{9,1... | collective-permute-start | bytes 589832 | tf_op jit(solution)/shard_map/ppermute | solution.py:252
  36.2 16.2 %collective-permute-start.6 = (bf16[4,2,2,32,128]{4,3,2,1,0:T(8,128)(2,1)S(1)}, bf16[4,2,2,32,128]{4,3,2,1,0:T(8,128)(2,1)S(1)}, u32[]{:S(2)}, u32[]{:S(2)}) collective-permute-start(bf16[4,2,2,32,128]{4,3,2,1,0:T(8,128)(2,1)S(1)} %bitcast.64), channel_id=1, source_target_pairs={{0,8},{1,9},{2,10},{3,11},{8,0},{9,1},{10,2},{11,3},{16,24},{17,25... | collective-permute-start | bytes 393224 | tf_op jit(solution)/shard_map/ppermute | solution.py:304
  37.8 14.7 %collective-permute-start.7 = (bf16[4,2,2,32,128]{4,3,2,1,0:T(8,128)(2,1)S(1)}, bf16[4,2,2,32,128]{4,3,2,1,0:T(8,128)(2,1)S(1)}, u32[]{:S(2)}, u32[]{:S(2)}) collective-permute-start(bf16[4,2,2,32,128]{4,3,2,1,0:T(8,128)(2,1)S(1)} %bitcast.63), channel_id=1, source_target_pairs={{8,16},{9,17},{10,18},{11,19},{16,8},{17,9},{18,10},{19,11},{12,20... | collective-permute-start | bytes 393224 | tf_op jit(solution)/shard_map/ppermute | solution.py:304
  64.1 2.5 %collective-permute-start.10 = (bf16[4,6,128,128]{3,2,1,0:T(8,128)(2,1)}, bf16[4,6,128,128]{3,2,1,0:T(8,128)(2,1)S(1)}, u32[]{:S(2)}, u32[]{:S(2)}) collective-permute-start(bf16[4,6,128,128]{3,2,1,0:T(8,128)(2,1)} %get-tuple-element.23), channel_id=1, source_target_pairs={{0,4},{4,0},{1,5},{5,1},{2,6},{6,2},{3,7},{7,3},{8,12},{12,8},{9,1... | collective-permute-start | bytes 2359304 | tf_op jit(solution)/shard_map/ppermute | solution.py:252
  67.8 13.1 %collective-permute-start.11 = (bf16[6,128,128]{2,1,0:T(8,128)(2,1)S(1)}, bf16[6,128,128]{2,1,0:T(8,128)(2,1)S(1)}, u32[]{:S(2)}, u32[]{:S(2)}) collective-permute-start(bf16[6,128,128]{2,1,0:T(8,128)(2,1)S(1)} %get-tuple-element.30), channel_id=1, source_target_pairs={{0,8},{8,0},{16,24},{24,16},{1,9},{9,1},{17,25},{25,17},{2,10},{10... | collective-permute-start | bytes 589832 | tf_op jit(solution)/shard_map/ppermute | solution.py:252
  75.3 10.9 %collective-permute-start.12 = (bf16[6,128,128]{2,1,0:T(8,128)(2,1)S(1)}, bf16[6,128,128]{2,1,0:T(8,128)(2,1)S(1)}, u32[]{:S(2)}, u32[]{:S(2)}) collective-permute-start(bf16[6,128,128]{2,1,0:T(8,128)(2,1)S(1)} %get-tuple-element.32), channel_id=1, source_target_pairs={{0,16},{8,24},{16,0},{24,8},{1,17},{9,25},{17,1},{25,9},{2,18},{10... | collective-permute-start | bytes 589832 | tf_op jit(solution)/shard_map/ppermute | solution.py:252
  75.3 10.9 %collective-permute-start.13 = (bf16[6,128,128]{2,1,0:T(8,128)(2,1)S(1)}, bf16[6,128,128]{2,1,0:T(8,128)(2,1)S(1)}, u32[]{:S(2)}, u32[]{:S(2)}) collective-permute-start(bf16[6,128,128]{2,1,0:T(8,128)(2,1)S(1)} %get-tuple-element.31), channel_id=1, source_target_pairs={{0,24},{8,16},{16,8},{24,0},{1,25},{9,17},{17,9},{25,1},{2,26},{10... | collective-permute-start | bytes 589832 | tf_op jit(solution)/shard_map/ppermute | solution.py:252
  87.2 9.5 %collective-permute-start.14 = (bf16[192,128]{1,0:T(8,128)(2,1)S(1)}, bf16[192,128]{1,0:T(8,128)(2,1)S(1)}, u32[]{:S(2)}, u32[]{:S(2)}) collective-permute-start(bf16[192,128]{1,0:T(8,128)(2,1)S(1)} %get-tuple-element.35), channel_id=1, source_target_pairs={{0,1},{1,0},{2,3},{3,2},{4,5},{5,4},{6,7},{7,6},{8,9},{9,8},{10,11... | collective-permute-start | bytes 147464 | tf_op jit(solution)/shard_map/ppermute | solution.py:252
  89.3 7.5 %collective-permute-start.15 = (bf16[192,128]{1,0:T(8,128)(2,1)S(1)}, bf16[192,128]{1,0:T(8,128)(2,1)S(1)}, u32[]{:S(2)}, u32[]{:S(2)}) collective-permute-start(bf16[192,128]{1,0:T(8,128)(2,1)S(1)} %get-tuple-element.37), channel_id=1, source_target_pairs={{0,2},{1,3},{2,0},{3,1},{4,6},{5,7},{6,4},{7,5},{8,10},{9,11},{10,... | collective-permute-start | bytes 147464 | tf_op jit(solution)/shard_map/ppermute | solution.py:252
  91.6 5.9 %collective-permute-start.16 = (bf16[192,128]{1,0:T(8,128)(2,1)S(1)}, bf16[192,128]{1,0:T(8,128)(2,1)S(1)}, u32[]{:S(2)}, u32[]{:S(2)}) collective-permute-start(bf16[192,128]{1,0:T(8,128)(2,1)S(1)} %get-tuple-element.36), channel_id=1, source_target_pairs={{0,3},{1,2},{2,1},{3,0},{4,7},{5,6},{6,5},{7,4},{8,11},{9,10},{10,... | collective-permute-start | bytes 147464 | tf_op jit(solution)/shard_map/ppermute | solution.py:252
  91.7 12.3 %all-to-all-start.2 = ((bf16[8,2,2,16,128]{4,3,2,1,0:T(8,128)(2,1)}), bf16[8,2,2,16,128]{4,3,2,1,0:T(8,128)(2,1)S(1)}, u32[]{:S(2)}, u32[]{:S(2)}) async-start(bf16[8,2,2,16,128]{4,3,2,1,0:T(8,128)(2,1)} %get-tuple-element.24), calls=%async_computation.2 | async-start | bytes 262144 | tf_op jit(solution)/shard_map/all_to_all | solution.py:291
  97.6 9.3 %collective-permute-start.17 = (bf16[192,128]{1,0:T(8,128)(2,1)S(1)}, bf16[192,128]{1,0:T(8,128)(2,1)S(1)}, u32[]{:S(2)}, u32[]{:S(2)}) collective-permute-start(bf16[192,128]{1,0:T(8,128)(2,1)S(1)} %get-tuple-element.29), channel_id=1, source_target_pairs={{0,1},{1,0},{2,3},{3,2},{4,5},{5,4},{6,7},{7,6},{8,9},{9,8},{10,11... | collective-permute-start | bytes 147464 | tf_op jit(solution)/shard_map/ppermute | solution.py:252
  104.6 6.6 %collective-permute-start.18 = (bf16[192,128]{1,0:T(8,128)(2,1)S(1)}, bf16[192,128]{1,0:T(8,128)(2,1)S(1)}, u32[]{:S(2)}, u32[]{:S(2)}) collective-permute-start(bf16[192,128]{1,0:T(8,128)(2,1)S(1)} %get-tuple-element.29), channel_id=1, source_target_pairs={{0,2},{1,3},{2,0},{3,1},{4,6},{5,7},{6,4},{7,5},{8,10},{9,11},{10,... | collective-permute-start | bytes 147464 | tf_op jit(solution)/shard_map/ppermute | solution.py:252
  104.7 6.5 %collective-permute-start.19 = (bf16[192,128]{1,0:T(8,128)(2,1)S(1)}, bf16[192,128]{1,0:T(8,128)(2,1)S(1)}, u32[]{:S(2)}, u32[]{:S(2)}) collective-permute-start(bf16[192,128]{1,0:T(8,128)(2,1)S(1)} %get-tuple-element.29), channel_id=1, source_target_pairs={{0,3},{1,2},{2,1},{3,0},{4,7},{5,6},{6,5},{7,4},{8,11},{9,10},{10,... | collective-permute-start | bytes 147464 | tf_op jit(solution)/shard_map/ppermute | solution.py:252
  106.9 5.0 %collective-permute-start.20 = (bf16[192,128]{1,0:T(8,128)(2,1)S(1)}, bf16[192,128]{1,0:T(8,128)(2,1)S(1)}, u32[]{:S(2)}, u32[]{:S(2)}) collective-permute-start(bf16[192,128]{1,0:T(8,128)(2,1)S(1)} %get-tuple-element.29), channel_id=1, source_target_pairs={{0,4},{4,0},{1,5},{5,1},{2,6},{6,2},{3,7},{7,3},{8,12},{12,8},{9,1... | collective-permute-start | bytes 147464 | tf_op jit(solution)/shard_map/ppermute | solution.py:252
  106.9 5.0 %collective-permute-start.21 = (bf16[192,128]{1,0:T(8,128)(2,1)S(1)}, bf16[192,128]{1,0:T(8,128)(2,1)S(1)}, u32[]{:S(2)}, u32[]{:S(2)}) collective-permute-start(bf16[192,128]{1,0:T(8,128)(2,1)S(1)} %collective-permute-done.17), channel_id=1, source_target_pairs={{0,4},{4,0},{1,5},{5,1},{2,6},{6,2},{3,7},{7,3},{8,12},{12,8},{9,1... | collective-permute-start | bytes 147464 | tf_op jit(solution)/shard_map/ppermute | solution.py:252
  (14 other events, 72.0 us)

commit v5 on v4

--- a/solution.py
+++ b/solution.py
@@ -36,14 +36,14 @@
     return jnp.concatenate([kernel_of(w_ref, block, tap) for tap in order], 1)
 
 
-def window_kernel(halo, width, video_ref, cot_ref, video_out, cot_out):
-    parties = video_out.shape[0]
+def window_kernel(halo, span, place_ref, video_ref, cot_ref, *rest):
+    video_outs, cot_outs, cut_ref = rest[: len(rest) // 2], rest[len(rest) // 2 : -1], rest[-1]
     frames, rows, columns, chans = video_ref.shape
-    own = width - 2 * halo
-    for source, target in ((video_ref, video_out), (cot_ref, cot_out)):
+    own = span - 2 * halo
+    for source, targets in ((video_ref, video_outs), (cot_ref, cot_outs)):
         whole = source[...].astype(F32)
-        for unit in range(parties):
-            first, last = unit * own - halo, unit * own - halo + width
+        for unit in range(len(targets)):
+            first, last = unit * own - halo, unit * own - halo + span
             parts = []
             if first < 0:
                 parts.append(jnp.zeros((frames, rows, -first, chans), F32))
@@ -51,7 +51,9 @@
             if last > columns:
                 parts.append(jnp.zeros((frames, rows, last - columns, chans), F32))
             piece = jnp.concatenate(parts, 2) if len(parts) > 1 else parts[0]
-            target[unit] = piece.astype(BF16)
+            cut_ref[unit] = piece.astype(BF16)
+        for step, target in enumerate(targets):
+            target[...] = cut_ref[jnp.bitwise_xor(place_ref[7], step)]
 
 
 def place_kernels(place_ref, w_ref, spatial_ref, temporal_ref, mine_refs, other_refs):
@@ -70,11 +72,11 @@
 def forward_kernel(geometry, place_ref, *rest):
     blocks, cores, group, frames_in, rows_in, halo, tile, width = geometry
     shared, rest = rest[: 2 * blocks], rest[2 * blocks :]
-    own_ref, inner_ref, outer_ref, xo_ref, ho_ref = rest[:5]
-    d_refs = rest[5 : 5 + blocks]
-    x_ref, h_ref, mask_ref, w_ref = rest[5 + blocks :]
+    arrived, rest = rest[:6], rest[6:]
+    xo_ref, ho_ref = rest[:2]
+    d_refs = rest[2 : 2 + blocks]
+    x_ref, h_ref, mask_ref, w_ref, start_ref = rest[2 + blocks :]
     place_kernels(place_ref, w_ref, shared[0], shared[1], shared[2 : 1 + blocks], shared[1 + blocks :])
-    odd = place_ref[6] == 1
     frames = cores * frames_in
     high = tile + 2 * halo
     chans = w_ref.shape[-1]
@@ -99,16 +101,19 @@
         ]
         xo_ref[block, frame] = jnp.concatenate(cut, 2)
 
+    core, odd, unit = place_ref[4], place_ref[6], place_ref[7]
+    near = tile + halo - odd * (tile + halo)
+    columns_at = pl.ds(pl.multiple_of(core * (width - 2 * halo), 16), width)
+    for index, ref in enumerate(arrived):
+        base = (halo, near, tile + halo - near)[index % 3]
+        whose = core if index < 3 else 1 - core
+        for step in range(group):
+            row = base + jnp.bitwise_xor(unit, step) * rows_in
+            start_ref[pl.ds(whose * frames_in, frames_in), pl.ds(row, rows_in)] = ref[
+                step, :, :, columns_at, :
+            ]
     for frame in range(frames):
-        core, inner = divmod(frame, frames_in)
-        units = [core * group + unit for unit in range(group)]
-        near = [inner_ref[unit, inner] for unit in units]
-        far = [outer_ref[unit, inner] for unit in units]
-        pieces = [jnp.where(odd, a, b) for a, b in zip(near, far)]
-        pieces += [own_ref[unit, inner] for unit in units]
-        pieces += [jnp.where(odd, b, a) for a, b in zip(near, far)]
-        whole = jnp.concatenate(pieces, 0).reshape(high * width, chans)
-        keep(0, frame, whole.astype(F32), 0)
+        keep(0, frame, start_ref[frame].reshape(high * width, chans).astype(F32), 0)
 
     for block in range(blocks):
         first, last = block + 1, high - block - 1
@@ -157,11 +162,12 @@
 def backward_kernel(geometry, factor, place_ref, *rest):
     blocks, cores, group, frames_in, rows_in, halo, tile, width = geometry
     shared, rest = rest[: 2 * blocks], rest[2 * blocks :]
-    own_ref, inner_ref, outer_ref, xo_ref, ho_ref = rest[:5]
-    d_refs = rest[5 : 5 + blocks]
-    keep_ref, give_ref, out_ref, g_ref, da_ref, dao_ref, go_ref, w_ref, grad_ref = rest[5 + blocks :]
+    arrived, rest = rest[:6], rest[6:]
+    xo_ref, ho_ref = rest[:2]
+    d_refs = rest[2 : 2 + blocks]
+    keep_ref, give_ref, mine_out, other_out = rest[2 + blocks : 6 + blocks]
+    g_ref, da_ref, dao_ref, go_ref, w_ref, grad_ref, out_ref = rest[6 + blocks :]
     place_kernels(place_ref, w_ref, shared[0], shared[1], shared[2 : 1 + blocks], shared[1 + blocks :])
-    odd = place_ref[6] == 1
     frames = cores * frames_in
     chans = w_ref.shape[-1]
     rim = blocks
@@ -169,15 +175,19 @@
     per_core = w_ref.shape[2]
     pixels = tile * (own_cols[1] - own_cols[0])
 
-    for frame in range(frames):
-        core, inner = divmod(frame, frames_in)
-        half = group // 2
-        near = [inner_ref[core * half + unit, inner] for unit in range(half)]
-        far = [outer_ref[core * half + unit, inner] for unit in range(half)]
-        pieces = [jnp.where(odd, a, b) for a, b in zip(near, far)]
-        pieces += [own_ref[core * group + unit, inner] for unit in range(group)]
-        pieces += [jnp.where(odd, b, a) for a, b in zip(near, far)]
-        g_ref[frame] = jnp.concatenate(pieces, 0)
+    core, odd, unit = place_ref[4], place_ref[6], place_ref[7]
+    half = group // 2
+    near = tile + rim - odd * (tile + rim)
+    columns_at = pl.ds(pl.multiple_of(core * (width - 2 * halo), 16), width)
+    for index, ref in enumerate(arrived):
+        base = (rim, near, tile + rim - near)[index % 3]
+        whose = core if index < 3 else 1 - core
+        mask = group - 1 if index % 3 == 0 else half - 1
+        for step in range(ref.shape[0]):
+            row = base + jnp.bitwise_and(jnp.bitwise_xor(unit, step), mask) * rows_in
+            g_ref[pl.ds(whose * frames_in, frames_in), pl.ds(row, rows_in)] = ref[
+                step, :, :, columns_at, :
+            ]
 
     def put(block, tap, value):
         slot = jnp.where(place_ref[4] == tap // per_core, 0, 1)
@@ -226,12 +236,8 @@
             if block:
                 g_ref[frame, first + 1 : last - 1] = new.reshape(inner, width, chans)
             else:
-                core, within = divmod(frame, frames_in)
                 cut = new.astype(F32).reshape(inner, width, chans)[:, own_cols[0] : own_cols[1]]
-                for unit in range(group):
-                    out_ref[core * group + unit, within] = cut[
-                        unit * rows_in : (unit + 1) * rows_in
-                    ].astype(BF16)
+                out_ref[frame] = cut.astype(BF16)
         slopes = dao_ref[...].reshape(frames * pixels, chans)
         for ky in range(3):
             taps = xo_ref[block, :, ky : ky + tile].reshape(frames * pixels, 3 * chans)
@@ -245,6 +251,10 @@
             put(block, 9 + kt, dot_first(later, earlier))
     keep_ref[...] = grad_ref[0]
     give_ref[...] = grad_ref[1]
+    for whose, target in ((core, mine_out), (1 - core, other_out)):
+        for step in range(group):
+            row = jnp.bitwise_xor(unit, step) * rows_in
+            target[step] = out_ref[pl.ds(whose * frames_in, frames_in), pl.ds(row, rows_in)]
 
 
 def swapped(value, axis="tm", step=1):
@@ -267,28 +277,10 @@
     parties = cores * group
     own_width = columns // parties
     width = own_width + 2 * halo
-    sets = None
-    if tiles != group:
-        sets = [
-            [core * tiles + base + unit for core in range(cores) for unit in range(group)]
-            for base in range(0, tiles, group)
-        ]
+    span = cores * own_width + 2 * halo
     vmem = pl.BlockSpec(memory_space=pltpu.VMEM)
     smem = pl.BlockSpec(memory_space=pltpu.SMEM)
-    params = pltpu.CompilerParams(vmem_limit_bytes=56 * 2**20)
-
-    windows = jax.ShapeDtypeStruct((parties, frames_in, rows_in, width, chans), BF16)
-    video_windows, cot_windows = pl.pallas_call(
-        functools.partial(window_kernel, halo, width),
-        name="windows",
-        in_specs=[vmem] * 2,
-        out_specs=[vmem] * 2,
-        out_shape=[windows] * 2,
-        compiler_params=params,
-    )(video, cotangent)
-
-    def spread(value):
-        return lax.all_to_all(value, ("tm", "space"), 0, 0, axis_index_groups=sets, tiled=True)
+    params = pltpu.CompilerParams(vmem_limit_bytes=32 * 2**20)
 
     bands = blocks * tiles // group
     place = lax.axis_index("space")
@@ -303,27 +295,47 @@
                 pairs += [(one * group + i, other * group + i) for i in range(group)]
         return lax.ppermute(value, ("section", "space"), pairs)
 
-    half_kernels = own_half(spatial_weights, temporal_weights)
-    mine = [swapped(half_kernels, "section", step) for step in range(1, blocks)]
-    own_video = spread(video_windows)
-    video_near, video_far = traded(own_video, 0), traded(own_video, 1)
-    shared = [spatial_weights, temporal_weights] + mine + [swapped(each) for each in mine]
-
-    own_cot = spread(cot_windows)
-    half = group // 2
-    split = own_cot.reshape((cores, group) + own_cot.shape[1:])
-    edge = (cores * half,) + own_cot.shape[1:]
-    cot_near = traded(lax.dynamic_slice_in_dim(split, (1 - odd) * half, half, 1).reshape(edge), 0)
-    cot_far = traded(lax.dynamic_slice_in_dim(split, odd * half, half, 1).reshape(edge), 1)
-
-    unit = lax.axis_index("tm") * group + place % group
+    core, section = lax.axis_index("tm"), lax.axis_index("section")
+    unit = place % group
     total_rows = blocks * tiles * rows_in
     corner = jnp.stack(
         [
-            band * tile - halo, unit * own_width - halo, total_rows, columns,
-            lax.axis_index("tm"), lax.axis_index("section"), odd,
+            band * tile - halo, (unit * cores + core) * own_width - halo, total_rows, columns,
+            core, section, odd, unit,
         ]
     ).astype(jnp.int32)
+
+    half_kernels = own_half(spatial_weights, temporal_weights)
+    mine = [swapped(half_kernels, "section", step) for step in range(1, blocks)]
+
+    windows = jax.ShapeDtypeStruct((frames_in, rows_in, span, chans), BF16)
+    cuts = pl.pallas_call(
+        functools.partial(window_kernel, halo, span),
+        name="windows",
+        in_specs=[smem] + [vmem] * 2,
+        out_specs=[vmem] * (2 * group),
+        out_shape=[windows] * (2 * group),
+        scratch_shapes=[pltpu.VMEM((group,) + windows.shape, BF16)],
+        compiler_params=params,
+    )(corner, video, cotangent)
+
+    def gathered(pieces):
+        return jnp.stack([pieces[0]] + [swapped(pieces[i], "space", i) for i in range(1, group)])
+
+    own_video = gathered(cuts[:group])
+    videos = [own_video, traded(own_video, 0), traded(own_video, 1)]
+    videos += [swapped(each) for each in videos]
+    shared = [spatial_weights, temporal_weights] + mine + [swapped(each) for each in mine]
+
+    own_cot = gathered(cuts[group:])
+    half = group // 2
+    upper = unit // half
+    cots = [own_cot] + [
+        traded(lax.dynamic_slice_in_dim(own_cot, (upper ^ side) * half, half, 0), shift)
+        for shift, side in ((0, 1 - odd), (1, odd))
+    ]
+    cots += [swapped(each) for each in cots]
+
     geometry = (blocks, cores, group, frames_in, rows_in, halo, tile, width)
     frames = cores * frames_in
     high = tile + 2 * halo
@@ -337,7 +349,7 @@
     features, hidden, *slopes = pl.pallas_call(
         functools.partial(forward_kernel, geometry),
         name="forward",
-        in_specs=[smem] + [vmem] * (2 * blocks + 3),
+        in_specs=[smem] + [vmem] * (2 * blocks + 6),
         out_specs=[vmem] * (2 + blocks),
         out_shape=[
             jax.ShapeDtypeStruct((blocks, frames, tile + 2, own_width, 3 * chans), BF16),
@@ -349,22 +361,25 @@
             pltpu.VMEM((frames, high, width, chans), BF16),
             pltpu.VMEM((high, width, chans), F32),
             pltpu.VMEM(all_kernels, BF16),
+            pltpu.VMEM((frames, high, width, chans), BF16),
         ],
         compiler_params=params,
         cost_estimate=cost,
-    )(corner, *shared, own_video, video_near, video_far)
-
+    )(corner, *shared, *videos)
+
+    back = jax.ShapeDtypeStruct((group, frames_in, rows_in, own_width, chans), BF16)
     pixel_count = frames * total_rows * columns
     factor = 1.0 / float(pixel_count) ** 0.5
-    keep, give, tile_grad = pl.pallas_call(
+    keep, give, mine_grad, other_grad = pl.pallas_call(
         functools.partial(backward_kernel, geometry, factor),
         name="backward",
-        in_specs=[smem] + [vmem] * (3 * blocks + 5),
-        out_specs=[vmem] * 3,
+        in_specs=[smem] + [vmem] * (3 * blocks + 8),
+        out_specs=[vmem] * 4,
         out_shape=[
             jax.ShapeDtypeStruct(per_section, BF16),
             jax.ShapeDtypeStruct(per_section, BF16),
-            jax.ShapeDtypeStruct((parties, frames_in, rows_in, own_width, chans), BF16),
+            back,
+            back,
         ],
         scratch_shapes=[
             pltpu.VMEM((frames, tile + 2 * blocks, width, chans), BF16),
@@ -373,39 +388,46 @@
             pltpu.VMEM((frames, tile, own_width, chans), BF16),
             pltpu.VMEM(all_kernels, BF16),
             pltpu.VMEM(all_kernels, BF16),
+            pltpu.VMEM((frames, tile, own_width, chans), BF16),
         ],
         compiler_params=params,
         cost_estimate=cost,
-    )(corner, *shared, own_cot, cot_near, cot_far, features, hidden, *slopes)
+    )(corner, *shared, *cots, features, hidden, *slopes)
 
     got = swapped(give)
     parts = [(keep[i].astype(F32) + got[i].astype(F32)).astype(BF16) for i in range(blocks)]
-    back = spread(tile_grad)
+    other_grad = swapped(other_grad)
+    first = core == 0
+    wide = jnp.concatenate(
+        [jnp.where(first, mine_grad, other_grad), jnp.where(first, other_grad, mine_grad)], 3
+    )
+    strips = [wide[0]] + [swapped(wide[i], "space", i) for i in range(1, group)]
     parts = parts[:1] + [swapped(parts[i], "section", i) for i in range(1, blocks)]
     part = sum(each.astype(F32) for each in parts).astype(BF16)
     units = part.reshape(group, -1, chans)
-    unit = place % group
 
     def chunk(step):
         return lax.dynamic_index_in_dim(units, unit ^ step, 0, keepdims=False)
 
     parts = [chunk(0)] + [swapped(chunk(i), "space", i) for i in range(1, group)]
     part = sum(each.astype(F32) for each in parts)
-    if sets is not None:
+    if tiles != group:
         part = lax.psum(
             part, "space", axis_index_groups=[list(range(i, tiles, group)) for i in range(group)]
         )
     part = part.astype(BF16)
-    mine = [part] + [swapped(part, "space", i) for i in range(1, group)]
-    other = [swapped(each) for each in mine]
-    core = lax.axis_index("tm")
-    whole = jnp.zeros((cores, group) + part.shape, BF16)
-    for which, chunks in ((core, mine), (1 - core, other)):
-        for step, each in enumerate(chunks):
+    chunks = jnp.stack([part] + [swapped(part, "space", i) for i in range(1, group)])
+    whole = jnp.zeros((cores,) + chunks.shape, BF16)
+    for which, each in ((core, chunks), (1 - core, swapped(chunks))):
+        for step in range(group):
             whole = lax.dynamic_update_slice(
-                whole, each[None, None], (which, unit ^ step, 0, 0)
-            )
-    grad_video = back.transpose(1, 2, 0, 3, 4).reshape(video.shape)
+                whole, each[step][None, None], (which, unit ^ step, 0, 0)
+            )
+    grad_video = jnp.zeros(video.shape, BF16)
+    for step, strip in enumerate(strips):
+        grad_video = lax.dynamic_update_slice(
+            grad_video, strip, (0, 0, (unit ^ step) * cores * own_width, 0)
+        )
     own = whole.reshape(-1, chans, chans).swapaxes(1, 2).astype(F32)[None]
     count = spatial_weights.shape[1]
     return own[:, :count], own[:, count:], grad_video

time: 115 us -> 93.8 us (0.82)
  blocking collectives: 15.7 us -> 0 us
  starting transfers between devices: 34.4 us -> 42.4 us
  Pallas kernels: 23.5 us -> 15.9 us
  waiting for transfers between devices: 31.3 us -> 28.8 us
  other arithmetic: 3.46 us -> 1.53 us
  local copies, waits for them, and re-layouts: 5.41 us -> 4.08 us
    ppermute x20 -> x33, starting transfers between devices: 21.6 us -> 39.3 us  [swapped(): return lax.ppermute(value, axis, [(i, i ^ step) for i in range(count)])]
    all_to_all x1 -> x0, blocking collectives: 15.7 us -> none  [spread(): lax.all_to_all(value, ('tm', 'space'), 0, 0, axis_index_groups=sets, tile...]
    all_to_all x2 -> x0, starting transfers between devices: 8.44 us -> none  [spread(): lax.all_to_all(value, ('tm', 'space'), 0, 0, axis_index_groups=sets, tile...]
    all_to_all x2 -> x0, waiting for transfers between devices: 5.04 us -> none  [spread(): lax.all_to_all(value, ('tm', 'space'), 0, 0, axis_index_groups=sets, tile...]
    ppermute x4, waiting for transfers between devices: 1.82 us -> 6.11 us  [traded(): return lax.ppermute(value, ('section', 'space'), pairs)]
    pallas_call x1, Pallas kernels: 11 us -> 6.97 us  [on_device(): pl.pallas_call(functools.partial(backward_kernel, geometry, factor), name...]
    pallas_call x1, Pallas kernels: 10.7 us -> 8.24 us  [on_device(): pl.pallas_call(functools.partial(forward_kernel, geometry), name='forward...]
    ppermute x20 -> x33, waiting for transfers between devices: 24.5 us -> 22.7 us  [swapped(): return lax.ppermute(value, axis, [(i, i ^ step) for i in range(count)])]
  transfers between devices with their start and end apart: 26 -> 37, of which waited for: 12 -> 15; matrix products, arithmetic and copies ran while one was open for 2% -> 2% of each run, Pallas kernels for 9% -> 9%
where the time goes in v5:
time: 93.8 us; the launch traced here: 93.6 us
  starting transfers between devices  42.4 us (45%)
  waiting for transfers between devices  28.8 us (31%)
  Pallas kernels  15.9 us (17%)
  local copies, waits for them, and re-layouts  4.08 us (4%)
  other arithmetic  1.53 us (2%)
  between operations  0.99 us (1%)
    ppermute x33, starting transfers between devices, swapped(): return lax.ppermute(value, axis, [(i, i ^ step) for i in range(count)])  39.3 us
    ppermute x33, waiting for transfers between devices, swapped(): return lax.ppermute(value, axis, [(i, i ^ step) for i in range(count)])  22.7 us
    pallas_call x1, Pallas kernels, on_device(): pl.pallas_call(functools.partial(forward_kernel, geometry), name='forward...  8.24 us
    pallas_call x1, Pallas kernels, on_device(): pl.pallas_call(functools.partial(backward_kernel, geometry, factor), name...  6.97 us
    ppermute x4, waiting for transfers between devices, traded(): return lax.ppermute(value, ('section', 'space'), pairs)  6.11 us
    unnamed x12, local copies, waits for them, and re-layouts  3.69 us
    ppermute x4, starting transfers between devices, traded(): return lax.ppermute(value, ('section', 'space'), pairs)  3.1 us
  transfers between devices with their start and end apart: 37, of which 15 were waited for; matrix products, arithmetic and copies ran while one was open for 2% of the time, Pallas kernels for 9%

profile of v5, /device:TPU:0, one launch (start us, length us, event | category | flops | bytes accessed | tf_op | source)
XLA Modules:
  0.0 93.6 jit_solution(11481725600282893503)
XLA Ops:
  3.2 4.1 %collective-permute-start.7 = (bf16[2,2,48,128]{3,2,1,0:T(8,128)(2,1)S(1)}, bf16[2,2,48,128]{3,2,1,0:T(8,128)(2,1)S(1)}, u32[]{:S(2)}, u32[]{:S(2)}) collective-permute-start(bf16[2,2,48,128]{3,2,1,0:T(8,128)(2,1)S(1)} %get-tuple-element.23), channel_id=1, source_target_pairs={{0,2},{1,3},{2,0},{3,1},{4,6},{5,7},{6,4},{7,5},{8,10},{9,11},{10,... | collective-permute-start | bytes 147464 | tf_op jit(solution)/shard_map/ppermute | solution.py:262
  7.3 1.3 %collective-permute-start.8 = (bf16[2,2,48,128]{3,2,1,0:T(8,128)(2,1)S(1)}, bf16[2,2,48,128]{3,2,1,0:T(8,128)(2,1)S(1)}, u32[]{:S(2)}, u32[]{:S(2)}) collective-permute-start(bf16[2,2,48,128]{3,2,1,0:T(8,128)(2,1)S(1)} %get-tuple-element.24), channel_id=1, source_target_pairs={{0,3},{1,2},{2,1},{3,0},{4,7},{5,6},{6,5},{7,4},{8,11},{9,10},{10,... | collective-permute-start | bytes 147464 | tf_op jit(solution)/shard_map/ppermute | solution.py:262
  9.9 1.6 %collective-permute-start = (bf16[6,128,128]{2,1,0:T(8,128)(2,1)S(1)}, bf16[6,128,128]{2,1,0:T(8,128)(2,1)S(1)}, u32[]{:S(2)}, u32[]{:S(2)}) collective-permute-start(bf16[6,128,128]{2,1,0:T(8,128)(2,1)S(1)} %fusion.7), channel_id=1, source_target_pairs={{0,8},{8,0},{16,24},{24,16},{1,9},{9,1},{17,25},{25,17},{2,10},{10... | collective-permute-start | bytes 589832 | tf_op jit(solution)/shard_map/ppermute | solution.py:262
  11.5 1.5 %collective-permute-start.1 = (bf16[6,128,128]{2,1,0:T(8,128)(2,1)S(1)}, bf16[6,128,128]{2,1,0:T(8,128)(2,1)S(1)}, u32[]{:S(2)}, u32[]{:S(2)}) collective-permute-start(bf16[6,128,128]{2,1,0:T(8,128)(2,1)S(1)} %fusion.7), channel_id=1, source_target_pairs={{0,16},{8,24},{16,0},{24,8},{1,17},{9,25},{17,1},{25,9},{2,18},{10... | collective-permute-start | bytes 589832 | tf_op jit(solution)/shard_map/ppermute | solution.py:262
  13.0 1.8 %collective-permute-start.14 = (bf16[2,2,48,128]{3,2,1,0:T(8,128)(2,1)S(1)}, bf16[2,2,48,128]{3,2,1,0:T(8,128)(2,1)S(1)}, u32[]{:S(2)}, u32[]{:S(2)}) collective-permute-start(bf16[2,2,48,128]{3,2,1,0:T(8,128)(2,1)S(1)} %get-tuple-element.26), channel_id=1, source_target_pairs={{0,1},{1,0},{2,3},{3,2},{4,5},{5,4},{6,7},{7,6},{8,9},{9,8},{10,11... | collective-permute-start | bytes 147464 | tf_op jit(solution)/shard_map/ppermute | solution.py:262
  14.8 1.7 %collective-permute-start.15 = (bf16[2,2,48,128]{3,2,1,0:T(8,128)(2,1)S(1)}, bf16[2,2,48,128]{3,2,1,0:T(8,128)(2,1)S(1)}, u32[]{:S(2)}, u32[]{:S(2)}) collective-permute-start(bf16[2,2,48,128]{3,2,1,0:T(8,128)(2,1)S(1)} %get-tuple-element.27), channel_id=1, source_target_pairs={{0,2},{1,3},{2,0},{3,1},{4,6},{5,7},{6,4},{7,5},{8,10},{9,11},{10,... | collective-permute-start | bytes 147464 | tf_op jit(solution)/shard_map/ppermute | solution.py:262
  18.6 1.9 %collective-permute-done.15 = bf16[2,2,48,128]{3,2,1,0:T(8,128)(2,1)S(1)} collective-permute-done((bf16[2,2,48,128]{3,2,1,0:T(8,128)(2,1)S(1)}, bf16[2,2,48,128]{3,2,1,0:T(8,128)(2,1)S(1)}, u32[]{:S(2)}, u32[]{:S(2)}) %collective-permute-start.15) | collective-permute-done | bytes 49184 | tf_op jit(solution)/shard_map/ppermute | solution.py:262
  23.1 2.7 %collective-permute-done.9.rest_9_ = bf16[2,2,2,48,128]{4,3,2,1,0:T(8,128)(2,1)S(1)} collective-permute-done((bf16[2,2,2,48,128]{4,3,2,1,0:T(8,128)(2,1)S(1)}, bf16[2,2,2,48,128]{4,3,2,1,0:T(8,128)(2,1)S(1)}, u32[]{:S(2)}, u32[]{:S(2)}) %collective-permute-start.9) | collective-permute-done | bytes 98336 | tf_op jit(solution)/shard_map/ppermute | solution.py:296
  28.1 3.4 %collective-permute-done.17.rest_9_ = bf16[4,2,2,48,128]{4,3,2,1,0:T(8,128)(2,1)S(1)} collective-permute-done((bf16[4,2,2,48,128]{4,3,2,1,0:T(8,128)(2,1)S(1)}, bf16[4,2,2,48,128]{4,3,2,1,0:T(8,128)(2,1)S(1)}, u32[]{:S(2)}, u32[]{:S(2)}) %collective-permute-start.17) | collective-permute-done | bytes 196640 | tf_op jit(solution)/shard_map/ppermute | solution.py:296
  33.5 8.2 %forward.1 = (bf16[4,4,10,16,384]{4,3,2,1,0:T(8,128)(2,1)S(1)}, bf16[4,4,8,16,128]{4,3,2,1,0:T(8,128)(2,1)S(1)}, f32[4,10,32,128]{3,2,1,0:T(8,128)S(1)}, f32[4,1...) custom-call(s32[8]{0:T(128)S(1)} %stack.72.place_ref, ...), custom_call_target="tpu_custom_call" | custom-call | flops 6000000000 | bytes 8000000 | tf_op jit(solution)/shard_map/forward/pallas_call | solution.py:349
  41.8 7.0 %backward.1 = (bf16[4,6,128,128]{3,2,1,0:T(8,128)(2,1)S(1)}, bf16[4,6,128,128]{3,2,1,0:T(8,128)(2,1)S(1)}, bf16[4,2,2,16,128]{4,3,2,1,0:T(8,128)(2,1)S(1)}, bf16[4,2,2,16,128]{4,3,2,1,0:T(8,128)(2,1)S(1)}) custom-call(s32[8]{0:T(128)S(1)} %stack.72.place_ref, bf16[1,9,128,128]{3,2,1,0:T(8,128)(2,1)S(1)} %copy-done, bf16[1,3,128,128]{3,2,1,0:T(8,128)(2,1)S(1)} %copy-done.3, ...), custom_call_target="tpu_custom_call" | custom-call | flops 6000000000 | bytes 8000000 | tf_op jit(solution)/shard_map/backward/pallas_call | solution.py:373
  49.4 1.9 %collective-permute-done.33 = bf16[4,2,2,16,128]{4,3,2,1,0:T(8,128)(2,1)S(1)} collective-permute-done((bf16[4,2,2,16,128]{4,3,2,1,0:T(8,128)(2,1)S(1)}, bf16[4,2,2,16,128]{4,3,2,1,0:T(8,128)(2,1)S(1)}, u32[]{:S(2)}, u32[]{:S(2)}) %collective-permute-start.33) | collective-permute-done | bytes 65568 | tf_op jit(solution)/shard_map/ppermute | solution.py:262
  51.3 3.6 %collective-permute-start.34 = (bf16[2,2,32,128]{3,2,1,0:T(8,128)(2,1)S(1)}, bf16[2,2,32,128]{3,2,1,0:T(8,128)(2,1)S(1)}, u32[]{:S(2)}, u32[]{:S(2)}) collective-permute-start(bf16[2,2,32,128]{3,2,1,0:T(8,128)(2,1)S(1)} %get-tuple-element.53), channel_id=1, source_target_pairs={{0,1},{1,0},{2,3},{3,2},{4,5},{5,4},{6,7},{7,6},{8,9},{9,8},{10,11... | collective-permute-start | bytes 98312 | tf_op jit(solution)/shard_map/ppermute | solution.py:262
  54.9 2.7 %collective-permute-start.35 = (bf16[2,2,32,128]{3,2,1,0:T(8,128)(2,1)S(1)}, bf16[2,2,32,128]{3,2,1,0:T(8,128)(2,1)S(1)}, u32[]{:S(2)}, u32[]{:S(2)}) collective-permute-start(bf16[2,2,32,128]{3,2,1,0:T(8,128)(2,1)S(1)} %get-tuple-element.54), channel_id=1, source_target_pairs={{0,2},{1,3},{2,0},{3,1},{4,6},{5,7},{6,4},{7,5},{8,10},{9,11},{10,... | collective-permute-start | bytes 98312 | tf_op jit(solution)/shard_map/ppermute | solution.py:262
  57.8 4.3 %collective-permute-start.23 = (bf16[6,128,128]{2,1,0:T(8,128)(2,1)S(1)}, bf16[6,128,128]{2,1,0:T(8,128)(2,1)S(1)}, u32[]{:S(2)}, u32[]{:S(2)}) collective-permute-start(bf16[6,128,128]{2,1,0:T(8,128)(2,1)S(1)} %get-tuple-element.44), channel_id=1, source_target_pairs={{0,8},{8,0},{16,24},{24,16},{1,9},{9,1},{17,25},{25,17},{2,10},{10... | collective-permute-start | bytes 589832 | tf_op jit(solution)/shard_map/ppermute | solution.py:262
  62.0 1.5 %collective-permute-start.25 = (bf16[6,128,128]{2,1,0:T(8,128)(2,1)S(1)}, bf16[6,128,128]{2,1,0:T(8,128)(2,1)S(1)}, u32[]{:S(2)}, u32[]{:S(2)}) collective-permute-start(bf16[6,128,128]{2,1,0:T(8,128)(2,1)S(1)} %get-tuple-element.45), channel_id=1, source_target_pairs={{0,24},{8,16},{16,8},{24,0},{1,25},{9,17},{17,9},{25,1},{2,26},{10... | collective-permute-start | bytes 589832 | tf_op jit(solution)/shard_map/ppermute | solution.py:262
  63.6 1.5 %collective-permute-start.36 = (bf16[2,2,32,128]{3,2,1,0:T(8,128)(2,1)S(1)}, bf16[2,2,32,128]{3,2,1,0:T(8,128)(2,1)S(1)}, u32[]{:S(2)}, u32[]{:S(2)}) collective-permute-start(bf16[2,2,32,128]{3,2,1,0:T(8,128)(2,1)S(1)} %get-tuple-element.52), channel_id=1, source_target_pairs={{0,3},{1,2},{2,1},{3,0},{4,7},{5,6},{6,5},{7,4},{8,11},{9,10},{10,... | collective-permute-start | bytes 98312 | tf_op jit(solution)/shard_map/ppermute | solution.py:262
  65.1 2.7 %collective-permute-done.23 = bf16[6,128,128]{2,1,0:T(8,128)(2,1)S(1)} collective-permute-done((bf16[6,128,128]{2,1,0:T(8,128)(2,1)S(1)}, bf16[6,128,128]{2,1,0:T(8,128)(2,1)S(1)}, u32[]{:S(2)}, u32[]{:S(2)}) %collective-permute-start.23) | collective-permute-done | bytes 196640 | tf_op jit(solution)/shard_map/ppermute | solution.py:262
  67.8 4.7 %collective-permute-done.24 = bf16[6,128,128]{2,1,0:T(8,128)(2,1)S(1)} collective-permute-done((bf16[6,128,128]{2,1,0:T(8,128)(2,1)S(1)}, bf16[6,128,128]{2,1,0:T(8,128)(2,1)S(1)}, u32[]{:S(2)}, u32[]{:S(2)}) %collective-permute-start.24) | collective-permute-done | bytes 196640 | tf_op jit(solution)/shard_map/ppermute | solution.py:262
  74.4 2.6 %collective-permute-start.28 = (bf16[192,128]{1,0:T(8,128)(2,1)S(1)}, bf16[192,128]{1,0:T(8,128)(2,1)S(1)}, u32[]{:S(2)}, u32[]{:S(2)}) collective-permute-start(bf16[192,128]{1,0:T(8,128)(2,1)S(1)} %get-tuple-element.48), channel_id=1, source_target_pairs={{0,3},{1,2},{2,1},{3,0},{4,7},{5,6},{6,5},{7,4},{8,11},{9,10},{10,... | collective-permute-start | bytes 147464 | tf_op jit(solution)/shard_map/ppermute | solution.py:262
  78.2 2.2 %collective-permute-done.28 = bf16[192,128]{1,0:T(8,128)(2,1)S(1)} collective-permute-done((bf16[192,128]{1,0:T(8,128)(2,1)S(1)}, bf16[192,128]{1,0:T(8,128)(2,1)S(1)}, u32[]{:S(2)}, u32[]{:S(2)}) %collective-permute-start.28) | collective-permute-done | bytes 49184 | tf_op jit(solution)/shard_map/ppermute | solution.py:262
  80.5 3.6 %collective-permute-start.30 = (bf16[192,128]{1,0:T(8,128)(2,1)S(1)}, bf16[192,128]{1,0:T(8,128)(2,1)S(1)}, u32[]{:S(2)}, u32[]{:S(2)}) collective-permute-start(bf16[192,128]{1,0:T(8,128)(2,1)S(1)} %get-tuple-element.43), channel_id=1, source_target_pairs={{0,2},{1,3},{2,0},{3,1},{4,6},{5,7},{6,4},{7,5},{8,10},{9,11},{10,... | collective-permute-start | bytes 147464 | tf_op jit(solution)/shard_map/ppermute | solution.py:262
  86.2 3.8 %collective-permute-done.31 = bf16[192,128]{1,0:T(8,128)(2,1)S(1)} collective-permute-done((bf16[192,128]{1,0:T(8,128)(2,1)S(1)}, bf16[192,128]{1,0:T(8,128)(2,1)S(1)}, u32[]{:S(2)}, u32[]{:S(2)}) %collective-permute-start.31) | collective-permute-done | bytes 49184 | tf_op jit(solution)/shard_map/ppermute | solution.py:262
  90.2 1.4 %collective-permute-done.32 = bf16[4,192,128]{2,1,0:T(8,128)(2,1)S(1)} collective-permute-done((bf16[4,192,128]{2,1,0:T(8,128)(2,1)S(1)}, bf16[4,192,128]{2,1,0:T(8,128)(2,1)S(1)}, u32[]{:S(2)}, u32[]{:S(2)}) %collective-permute-start.32) | collective-permute-done | bytes 196640 | tf_op jit(solution)/shard_map/ppermute | solution.py:262
  (93 shorter events, 21.0 us)
Async XLA Ops:
  3.2 9.8 %collective-permute-start.7 = (bf16[2,2,48,128]{3,2,1,0:T(8,128)(2,1)S(1)}, bf16[2,2,48,128]{3,2,1,0:T(8,128)(2,1)S(1)}, u32[]{:S(2)}, u32[]{:S(2)}) collective-permute-start(bf16[2,2,48,128]{3,2,1,0:T(8,128)(2,1)S(1)} %get-tuple-element.23), channel_id=1, source_target_pairs={{0,2},{1,3},{2,0},{3,1},{4,6},{5,7},{6,4},{7,5},{8,10},{9,11},{10,... | collective-permute-start | bytes 147464 | tf_op jit(solution)/shard_map/ppermute | solution.py:262
  7.3 7.5 %collective-permute-start.8 = (bf16[2,2,48,128]{3,2,1,0:T(8,128)(2,1)S(1)}, bf16[2,2,48,128]{3,2,1,0:T(8,128)(2,1)S(1)}, u32[]{:S(2)}, u32[]{:S(2)}) collective-permute-start(bf16[2,2,48,128]{3,2,1,0:T(8,128)(2,1)S(1)} %get-tuple-element.24), channel_id=1, source_target_pairs={{0,3},{1,2},{2,1},{3,0},{4,7},{5,6},{6,5},{7,4},{8,11},{9,10},{10,... | collective-permute-start | bytes 147464 | tf_op jit(solution)/shard_map/ppermute | solution.py:262
  8.7 7.8 %collective-permute-start.6 = (bf16[2,2,48,128]{3,2,1,0:T(8,128)(2,1)S(1)}, bf16[2,2,48,128]{3,2,1,0:T(8,128)(2,1)S(1)}, u32[]{:S(2)}, u32[]{:S(2)}) collective-permute-start(bf16[2,2,48,128]{3,2,1,0:T(8,128)(2,1)S(1)} %get-tuple-element.22), channel_id=1, source_target_pairs={{0,1},{1,0},{2,3},{3,2},{4,5},{5,4},{6,7},{7,6},{8,9},{9,8},{10,11... | collective-permute-start | bytes 147464 | tf_op jit(solution)/shard_map/ppermute | solution.py:262
  9.9 17.5 %collective-permute-start = (bf16[6,128,128]{2,1,0:T(8,128)(2,1)S(1)}, bf16[6,128,128]{2,1,0:T(8,128)(2,1)S(1)}, u32[]{:S(2)}, u32[]{:S(2)}) collective-permute-start(bf16[6,128,128]{2,1,0:T(8,128)(2,1)S(1)} %fusion.7), channel_id=1, source_target_pairs={{0,8},{8,0},{16,24},{24,16},{1,9},{9,1},{17,25},{25,17},{2,10},{10... | collective-permute-start | bytes 589832 | tf_op jit(solution)/shard_map/ppermute | solution.py:262
  11.5 16.0 %collective-permute-start.1 = (bf16[6,128,128]{2,1,0:T(8,128)(2,1)S(1)}, bf16[6,128,128]{2,1,0:T(8,128)(2,1)S(1)}, u32[]{:S(2)}, u32[]{:S(2)}) collective-permute-start(bf16[6,128,128]{2,1,0:T(8,128)(2,1)S(1)} %fusion.7), channel_id=1, source_target_pairs={{0,16},{8,24},{16,0},{24,8},{1,17},{9,25},{17,1},{25,9},{2,18},{10... | collective-permute-start | bytes 589832 | tf_op jit(solution)/shard_map/ppermute | solution.py:262
  14.8 5.8 %collective-permute-start.15 = (bf16[2,2,48,128]{3,2,1,0:T(8,128)(2,1)S(1)}, bf16[2,2,48,128]{3,2,1,0:T(8,128)(2,1)S(1)}, u32[]{:S(2)}, u32[]{:S(2)}) collective-permute-start(bf16[2,2,48,128]{3,2,1,0:T(8,128)(2,1)S(1)} %get-tuple-element.27), channel_id=1, source_target_pairs={{0,2},{1,3},{2,0},{3,1},{4,6},{5,7},{6,4},{7,5},{8,10},{9,11},{10,... | collective-permute-start | bytes 147464 | tf_op jit(solution)/shard_map/ppermute | solution.py:262
  16.5 5.9 %collective-permute-start.16 = (bf16[2,2,48,128]{3,2,1,0:T(8,128)(2,1)S(1)}, bf16[2,2,48,128]{3,2,1,0:T(8,128)(2,1)S(1)}, u32[]{:S(2)}, u32[]{:S(2)}) collective-permute-start(bf16[2,2,48,128]{3,2,1,0:T(8,128)(2,1)S(1)} %get-tuple-element.28), channel_id=1, source_target_pairs={{0,3},{1,2},{2,1},{3,0},{4,7},{5,6},{6,5},{7,4},{8,11},{9,10},{10,... | collective-permute-start | bytes 147464 | tf_op jit(solution)/shard_map/ppermute | solution.py:262
  17.5 10.5 %collective-permute-start.2 = (bf16[6,128,128]{2,1,0:T(8,128)(2,1)S(1)}, bf16[6,128,128]{2,1,0:T(8,128)(2,1)S(1)}, u32[]{:S(2)}, u32[]{:S(2)}) collective-permute-start(bf16[6,128,128]{2,1,0:T(8,128)(2,1)S(1)} %fusion.7), channel_id=1, source_target_pairs={{0,24},{8,16},{16,8},{24,0},{1,25},{9,17},{17,9},{25,1},{2,26},{10... | collective-permute-start | bytes 589832 | tf_op jit(solution)/shard_map/ppermute | solution.py:262
  20.6 5.2 %collective-permute-start.9 = (bf16[2,2,2,48,128]{4,3,2,1,0:T(8,128)(2,1)S(1)}, bf16[2,2,2,48,128]{4,3,2,1,0:T(8,128)(2,1)S(1)}, u32[]{:S(2)}, u32[]{:S(2)}) collective-permute-start(bf16[2,2,2,48,128]{4,3,2,1,0:T(8,128)(2,1)S(1)} %get-tuple-element.51), channel_id=1, source_target_pairs={{0,8},{1,9},{2,10},{3,11},{8,0},{9,1},{10,2},{11,3},{16,24},{17,25... | collective-permute-start | bytes 294920 | tf_op jit(solution)/shard_map/ppermute | solution.py:296
  25.7 5.8 %collective-permute-start.17 = (bf16[4,2,2,48,128]{4,3,2,1,0:T(8,128)(2,1)S(1)}, bf16[4,2,2,48,128]{4,3,2,1,0:T(8,128)(2,1)S(1)}, u32[]{:S(2)}, u32[]{:S(2)}) collective-permute-start(bf16[4,2,2,48,128]{4,3,2,1,0:T(8,128)(2,1)S(1)} %pad_maximum_fusion.1.rest_8_), channel_id=1, source_target_pairs={{0,8},{1,9},{2,10},{3,11},{8,0},{9,1},{10,2},{11,3},{16,24},{17,25... | collective-permute-start | bytes 589832 | tf_op jit(solution)/shard_map/ppermute | solution.py:296
  32.1 9.7 %collective-permute-start.11 = (bf16[4,2,2,48,128]{4,3,2,1,0:T(8,128)(2,1)S(1)}, bf16[4,2,2,48,128]{4,3,2,1,0:T(8,128)(2,1)S(1)}, u32[]{:S(2)}, u32[]{:S(2)}) collective-permute-start(bf16[4,2,2,48,128]{4,3,2,1,0:T(8,128)(2,1)S(1)} %pad_maximum_fusion.rest_8_), channel_id=1, source_target_pairs={{0,4},{4,0},{1,5},{5,1},{2,6},{6,2},{3,7},{7,3},{8,12},{12,8},{9,1... | collective-permute-start | bytes 589832 | tf_op jit(solution)/shard_map/ppermute | solution.py:262
  32.6 9.2 %collective-permute-start.12 = (bf16[2,2,2,48,128]{4,3,2,1,0:T(8,128)(2,1)S(1)}, bf16[2,2,2,48,128]{4,3,2,1,0:T(8,128)(2,1)S(1)}, u32[]{:S(2)}, u32[]{:S(2)}) collective-permute-start(bf16[2,2,2,48,128]{4,3,2,1,0:T(8,128)(2,1)S(1)} %collective-permute-done.9.rest_9_), channel_id=1, source_target_pairs={{0,4},{4,0},{1,5},{5,1},{2,6},{6,2},{3,7},{7,3},{8,12},{12,8},{9,1... | collective-permute-start | bytes 294920 | tf_op jit(solution)/shard_map/ppermute | solution.py:262
  33.0 8.8 %collective-permute-start.13 = (bf16[2,2,2,48,128]{4,3,2,1,0:T(8,128)(2,1)S(1)}, bf16[2,2,2,48,128]{4,3,2,1,0:T(8,128)(2,1)S(1)}, u32[]{:S(2)}, u32[]{:S(2)}) collective-permute-start(bf16[2,2,2,48,128]{4,3,2,1,0:T(8,128)(2,1)S(1)} %collective-permute-done.10.rest_10_), channel_id=1, source_target_pairs={{0,4},{4,0},{1,5},{5,1},{2,6},{6,2},{3,7},{7,3},{8,12},{12,8},{9,1... | collective-permute-start | bytes 294920 | tf_op jit(solution)/shard_map/ppermute | solution.py:262
  48.8 8.8 %collective-permute-start.22 = (bf16[4,6,128,128]{3,2,1,0:T(8,128)(2,1)S(1)}, bf16[4,6,128,128]{3,2,1,0:T(8,128)(2,1)S(1)}, u32[]{:S(2)}, u32[]{:S(2)}) collective-permute-start(bf16[4,6,128,128]{3,2,1,0:T(8,128)(2,1)S(1)} %get-tuple-element.36), channel_id=1, source_target_pairs={{0,4},{4,0},{1,5},{5,1},{2,6},{6,2},{3,7},{7,3},{8,12},{12,8},{9,1... | collective-permute-start | bytes 2359304 | tf_op jit(solution)/shard_map/ppermute | solution.py:262
  51.3 12.3 %collective-permute-start.34 = (bf16[2,2,32,128]{3,2,1,0:T(8,128)(2,1)S(1)}, bf16[2,2,32,128]{3,2,1,0:T(8,128)(2,1)S(1)}, u32[]{:S(2)}, u32[]{:S(2)}) collective-permute-start(bf16[2,2,32,128]{3,2,1,0:T(8,128)(2,1)S(1)} %get-tuple-element.53), channel_id=1, source_target_pairs={{0,1},{1,0},{2,3},{3,2},{4,5},{5,4},{6,7},{7,6},{8,9},{9,8},{10,11... | collective-permute-start | bytes 98312 | tf_op jit(solution)/shard_map/ppermute | solution.py:262
  54.9 22.2 %collective-permute-start.35 = (bf16[2,2,32,128]{3,2,1,0:T(8,128)(2,1)S(1)}, bf16[2,2,32,128]{3,2,1,0:T(8,128)(2,1)S(1)}, u32[]{:S(2)}, u32[]{:S(2)}) collective-permute-start(bf16[2,2,32,128]{3,2,1,0:T(8,128)(2,1)S(1)} %get-tuple-element.54), channel_id=1, source_target_pairs={{0,2},{1,3},{2,0},{3,1},{4,6},{5,7},{6,4},{7,5},{8,10},{9,11},{10,... | collective-permute-start | bytes 98312 | tf_op jit(solution)/shard_map/ppermute | solution.py:262
  57.8 10.0 %collective-permute-start.23 = (bf16[6,128,128]{2,1,0:T(8,128)(2,1)S(1)}, bf16[6,128,128]{2,1,0:T(8,128)(2,1)S(1)}, u32[]{:S(2)}, u32[]{:S(2)}) collective-permute-start(bf16[6,128,128]{2,1,0:T(8,128)(2,1)S(1)} %get-tuple-element.44), channel_id=1, source_target_pairs={{0,8},{8,0},{16,24},{24,16},{1,9},{9,1},{17,25},{25,17},{2,10},{10... | collective-permute-start | bytes 589832 | tf_op jit(solution)/shard_map/ppermute | solution.py:262
  62.0 10.4 %collective-permute-start.24 = (bf16[6,128,128]{2,1,0:T(8,128)(2,1)S(1)}, bf16[6,128,128]{2,1,0:T(8,128)(2,1)S(1)}, u32[]{:S(2)}, u32[]{:S(2)}) collective-permute-start(bf16[6,128,128]{2,1,0:T(8,128)(2,1)S(1)} %get-tuple-element.46), channel_id=1, source_target_pairs={{0,16},{8,24},{16,0},{24,8},{1,17},{9,25},{17,1},{25,9},{2,18},{10... | collective-permute-start | bytes 589832 | tf_op jit(solution)/shard_map/ppermute | solution.py:262
  62.0 10.4 %collective-permute-start.25 = (bf16[6,128,128]{2,1,0:T(8,128)(2,1)S(1)}, bf16[6,128,128]{2,1,0:T(8,128)(2,1)S(1)}, u32[]{:S(2)}, u32[]{:S(2)}) collective-permute-start(bf16[6,128,128]{2,1,0:T(8,128)(2,1)S(1)} %get-tuple-element.45), channel_id=1, source_target_pairs={{0,24},{8,16},{16,8},{24,0},{1,25},{9,17},{17,9},{25,1},{2,26},{10... | collective-permute-start | bytes 589832 | tf_op jit(solution)/shard_map/ppermute | solution.py:262
  63.6 21.3 %collective-permute-start.36 = (bf16[2,2,32,128]{3,2,1,0:T(8,128)(2,1)S(1)}, bf16[2,2,32,128]{3,2,1,0:T(8,128)(2,1)S(1)}, u32[]{:S(2)}, u32[]{:S(2)}) collective-permute-start(bf16[2,2,32,128]{3,2,1,0:T(8,128)(2,1)S(1)} %get-tuple-element.52), channel_id=1, source_target_pairs={{0,3},{1,2},{2,1},{3,0},{4,7},{5,6},{6,5},{7,4},{8,11},{9,10},{10,... | collective-permute-start | bytes 98312 | tf_op jit(solution)/shard_map/ppermute | solution.py:262
  73.2 5.0 %collective-permute-start.27 = (bf16[192,128]{1,0:T(8,128)(2,1)S(1)}, bf16[192,128]{1,0:T(8,128)(2,1)S(1)}, u32[]{:S(2)}, u32[]{:S(2)}) collective-permute-start(bf16[192,128]{1,0:T(8,128)(2,1)S(1)} %get-tuple-element.49), channel_id=1, source_target_pairs={{0,2},{1,3},{2,0},{3,1},{4,6},{5,7},{6,4},{7,5},{8,10},{9,11},{10,... | collective-permute-start | bytes 147464 | tf_op jit(solution)/shard_map/ppermute | solution.py:262
  74.4 5.9 %collective-permute-start.28 = (bf16[192,128]{1,0:T(8,128)(2,1)S(1)}, bf16[192,128]{1,0:T(8,128)(2,1)S(1)}, u32[]{:S(2)}, u32[]{:S(2)}) collective-permute-start(bf16[192,128]{1,0:T(8,128)(2,1)S(1)} %get-tuple-element.48), channel_id=1, source_target_pairs={{0,3},{1,2},{2,1},{3,0},{4,7},{5,6},{6,5},{7,4},{8,11},{9,10},{10,... | collective-permute-start | bytes 147464 | tf_op jit(solution)/shard_map/ppermute | solution.py:262
  80.5 5.6 %collective-permute-start.30 = (bf16[192,128]{1,0:T(8,128)(2,1)S(1)}, bf16[192,128]{1,0:T(8,128)(2,1)S(1)}, u32[]{:S(2)}, u32[]{:S(2)}) collective-permute-start(bf16[192,128]{1,0:T(8,128)(2,1)S(1)} %get-tuple-element.43), channel_id=1, source_target_pairs={{0,2},{1,3},{2,0},{3,1},{4,6},{5,7},{6,4},{7,5},{8,10},{9,11},{10,... | collective-permute-start | bytes 147464 | tf_op jit(solution)/shard_map/ppermute | solution.py:262
  84.1 5.9 %collective-permute-start.31 = (bf16[192,128]{1,0:T(8,128)(2,1)S(1)}, bf16[192,128]{1,0:T(8,128)(2,1)S(1)}, u32[]{:S(2)}, u32[]{:S(2)}) collective-permute-start(bf16[192,128]{1,0:T(8,128)(2,1)S(1)} %get-tuple-element.43), channel_id=1, source_target_pairs={{0,3},{1,2},{2,1},{3,0},{4,7},{5,6},{6,5},{7,4},{8,11},{9,10},{10,... | collective-permute-start | bytes 147464 | tf_op jit(solution)/shard_map/ppermute | solution.py:262
  (18 other events, 118.2 us)

commit v6 on v5

--- a/solution.py
+++ b/solution.py
@@ -36,33 +36,84 @@
     return jnp.concatenate([kernel_of(w_ref, block, tap) for tap in order], 1)
 
 
-def window_kernel(halo, span, place_ref, video_ref, cot_ref, *rest):
-    video_outs, cot_outs, cut_ref = rest[: len(rest) // 2], rest[len(rest) // 2 : -1], rest[-1]
+def opening_kernel(
+    halo, span, place_ref, video_hbm, spatial_hbm, temporal_hbm, mine_ref, other_ref, *rest
+):
+    targets, (video_ref, wide_ref, sems) = rest[:-3], rest[-3:]
+    taps, count = mine_ref.shape[0], spatial_hbm.shape[1]
+    copy_video = pltpu.make_async_copy(video_hbm, video_ref, sems.at[0])
+    copy_video.start()
+
+    def kernel_copies(core):
+        copies = []
+        for half, ref in ((core, mine_ref), (1 - core, other_ref)):
+            first, last = half * taps, (half + 1) * taps
+            split = min(max(count, first), last)
+            if split > first:
+                source, target = spatial_hbm.at[0, first:split], ref.at[: split - first]
+                copies.append(pltpu.make_async_copy(source, target, sems.at[1 + len(copies)]))
+            if last > split:
+                source, target = temporal_hbm.at[0, split - count : last - count], ref.at[split - first :]
+                copies.append(pltpu.make_async_copy(source, target, sems.at[1 + len(copies)]))
+        return copies
+
+    for core in range(2):
+        @pl.when(place_ref[4] == core)
+        def _(core=core):
+            for copy in kernel_copies(core):
+                copy.start()
+
     frames, rows, columns, chans = video_ref.shape
-    own = span - 2 * halo
-    for source, targets in ((video_ref, video_outs), (cot_ref, cot_outs)):
-        whole = source[...].astype(F32)
-        for unit in range(len(targets)):
-            first, last = unit * own - halo, unit * own - halo + span
-            parts = []
-            if first < 0:
-                parts.append(jnp.zeros((frames, rows, -first, chans), F32))
-            parts.append(whole[:, :, max(first, 0) : min(last, columns)])
-            if last > columns:
-                parts.append(jnp.zeros((frames, rows, last - columns, chans), F32))
-            piece = jnp.concatenate(parts, 2) if len(parts) > 1 else parts[0]
-            cut_ref[unit] = piece.astype(BF16)
-        for step, target in enumerate(targets):
-            target[...] = cut_ref[jnp.bitwise_xor(place_ref[7], step)]
-
-
-def place_kernels(place_ref, w_ref, spatial_ref, temporal_ref, mine_refs, other_refs):
+    edge = jnp.zeros((frames, rows, halo, chans), F32)
+    wide_ref[:, :, :halo] = edge
+    wide_ref[:, :, halo + columns :] = edge
+    copy_video.wait()
+    wide_ref[:, :, halo : halo + columns] = video_ref[...].astype(F32)
+    for step, target in enumerate(targets):
+        at = jnp.bitwise_xor(place_ref[7], step) * (span - 2 * halo)
+        target[...] = wide_ref[:, :, pl.ds(pl.multiple_of(at, 16), span)].astype(BF16)
+    for core in range(2):
+        @pl.when(place_ref[4] == core)
+        def _(core=core):
+            for copy in kernel_copies(core):
+                copy.wait()
+
+
+def cotangent_kernel(halo, width, place_ref, mine_ref, other_ref, *rest):
+    targets, wide_ref = rest[:-1], rest[-1]
+    frames_in, rows, columns, chans = mine_ref.shape
+    core = place_ref[4]
+    edge = jnp.zeros((2 * frames_in, rows, halo, chans), F32)
+    wide_ref[:, :, :halo] = edge
+    wide_ref[:, :, halo + columns :] = edge
+    for whose, ref in ((core, mine_ref), (1 - core, other_ref)):
+        wide_ref[pl.ds(whose * frames_in, frames_in), :, halo : halo + columns] = ref[...].astype(F32)
+    own = width - 2 * halo
+    for step, target in enumerate(targets):
+        at = (jnp.bitwise_xor(place_ref[7], step) * 2 + core) * own
+        target[...] = wide_ref[:, :, pl.ds(pl.multiple_of(at, 16), width)].astype(BF16)
+
+
+def closing_kernel(place_ref, mine_ref, other_ref, spatial_ref, temporal_ref, flat_ref):
+    pieces, rows, chans = mine_ref.shape
+    core, unit = place_ref[4], place_ref[7]
+    for whose, ref in ((core, mine_ref), (1 - core, other_ref)):
+        for step in range(pieces):
+            index = whose * pieces + jnp.bitwise_xor(jnp.bitwise_and(unit, pieces - 1), step)
+            flat_ref[pl.ds(pl.multiple_of(index * rows, 16), rows)] = ref[step]
+    count = spatial_ref.shape[1]
+    for tap in range(count + temporal_ref.shape[1]):
+        turned = flat_ref[tap * chans : (tap + 1) * chans].astype(F32).T
+        if tap < count:
+            spatial_ref[0, tap] = turned
+        else:
+            temporal_ref[0, tap - count] = turned
+
+
+def place_kernels(place_ref, w_ref, own_ref, mine_refs, other_refs):
     core, section = place_ref[4], place_ref[5]
-    cores, _, taps = w_ref.shape[:3]
-    count = spatial_ref.shape[1]
-    for tap in range(cores * taps):
-        one = spatial_ref[0, tap] if tap < count else temporal_ref[0, tap - count]
-        w_ref[tap // taps, section, tap % taps] = one
+    w_ref[core, section] = own_ref[0]
+    w_ref[1 - core, section] = own_ref[1]
     for step, (mine_ref, other_ref) in enumerate(zip(mine_refs, other_refs)):
         block = jnp.bitwise_xor(section, step + 1)
         w_ref[core, block] = mine_ref[...]
@@ -71,12 +122,12 @@
 
 def forward_kernel(geometry, place_ref, *rest):
     blocks, cores, group, frames_in, rows_in, halo, tile, width = geometry
-    shared, rest = rest[: 2 * blocks], rest[2 * blocks :]
+    shared, rest = rest[: 2 * blocks - 1], rest[2 * blocks - 1 :]
     arrived, rest = rest[:6], rest[6:]
     xo_ref, ho_ref = rest[:2]
     d_refs = rest[2 : 2 + blocks]
     x_ref, h_ref, mask_ref, w_ref, start_ref = rest[2 + blocks :]
-    place_kernels(place_ref, w_ref, shared[0], shared[1], shared[2 : 1 + blocks], shared[1 + blocks :])
+    place_kernels(place_ref, w_ref, shared[0], shared[1:blocks], shared[blocks:])
     frames = cores * frames_in
     high = tile + 2 * halo
     chans = w_ref.shape[-1]
@@ -161,13 +212,13 @@
 
 def backward_kernel(geometry, factor, place_ref, *rest):
     blocks, cores, group, frames_in, rows_in, halo, tile, width = geometry
-    shared, rest = rest[: 2 * blocks], rest[2 * blocks :]
-    arrived, rest = rest[:6], rest[6:]
+    shared, rest = rest[: 2 * blocks - 1], rest[2 * blocks - 1 :]
+    arrived, rest = rest[:3], rest[3:]
     xo_ref, ho_ref = rest[:2]
     d_refs = rest[2 : 2 + blocks]
     keep_ref, give_ref, mine_out, other_out = rest[2 + blocks : 6 + blocks]
     g_ref, da_ref, dao_ref, go_ref, w_ref, grad_ref, out_ref = rest[6 + blocks :]
-    place_kernels(place_ref, w_ref, shared[0], shared[1], shared[2 : 1 + blocks], shared[1 + blocks :])
+    place_kernels(place_ref, w_ref, shared[0], shared[1:blocks], shared[blocks:])
     frames = cores * frames_in
     chans = w_ref.shape[-1]
     rim = blocks
@@ -176,18 +227,12 @@
     pixels = tile * (own_cols[1] - own_cols[0])
 
     core, odd, unit = place_ref[4], place_ref[6], place_ref[7]
-    half = group // 2
     near = tile + rim - odd * (tile + rim)
-    columns_at = pl.ds(pl.multiple_of(core * (width - 2 * halo), 16), width)
-    for index, ref in enumerate(arrived):
-        base = (rim, near, tile + rim - near)[index % 3]
-        whose = core if index < 3 else 1 - core
-        mask = group - 1 if index % 3 == 0 else half - 1
-        for step in range(ref.shape[0]):
-            row = base + jnp.bitwise_and(jnp.bitwise_xor(unit, step), mask) * rows_in
-            g_ref[pl.ds(whose * frames_in, frames_in), pl.ds(row, rows_in)] = ref[
-                step, :, :, columns_at, :
-            ]
+    for base, ref in zip((rim, near, tile + rim - near), arrived):
+        count = ref.shape[0]
+        for step in range(count):
+            row = base + jnp.bitwise_and(jnp.bitwise_xor(unit, step), count - 1) * rows_in
+            g_ref[:, pl.ds(row, rows_in)] = ref[step]
 
     def put(block, tap, value):
         slot = jnp.where(place_ref[4] == tap // per_core, 0, 1)
@@ -262,12 +307,6 @@
     return lax.ppermute(value, axis, [(i, i ^ step) for i in range(count)])
 
 
-def own_half(spatial_weights, temporal_weights):
-    own = jnp.concatenate([spatial_weights[0], temporal_weights[0]], 0)
-    taps = own.shape[0] // lax.axis_size("tm")
-    return lax.dynamic_slice_in_dim(own, lax.axis_index("tm") * taps, taps, 0)
-
-
 def on_device(video, cotangent, spatial_weights, temporal_weights):
     blocks, cores, tiles = (lax.axis_size(name) for name in ("section", "tm", "space"))
     frames_in, rows_in, columns, chans = video.shape
@@ -305,41 +344,62 @@
         ]
     ).astype(jnp.int32)
 
-    half_kernels = own_half(spatial_weights, temporal_weights)
-    mine = [swapped(half_kernels, "section", step) for step in range(1, blocks)]
-
-    windows = jax.ShapeDtypeStruct((frames_in, rows_in, span, chans), BF16)
-    cuts = pl.pallas_call(
-        functools.partial(window_kernel, halo, span),
-        name="windows",
-        in_specs=[smem] + [vmem] * 2,
-        out_specs=[vmem] * (2 * group),
-        out_shape=[windows] * (2 * group),
-        scratch_shapes=[pltpu.VMEM((group,) + windows.shape, BF16)],
-        compiler_params=params,
-    )(corner, video, cotangent)
+    hbm = pl.BlockSpec(memory_space=pltpu.HBM)
+    taps = (spatial_weights.shape[1] + temporal_weights.shape[1]) // cores
+    one_half = jax.ShapeDtypeStruct((taps, chans, chans), BF16)
+    padded = columns + 2 * halo
+    cot_other = swapped(cotangent)
+    half_kernels, rest_kernels, *cuts = pl.pallas_call(
+        functools.partial(opening_kernel, halo, span),
+        name="opening",
+        in_specs=[smem] + [hbm] * 3,
+        out_specs=[vmem] * (2 + group),
+        out_shape=[one_half] * 2
+        + [jax.ShapeDtypeStruct((frames_in, rows_in, span, chans), BF16)] * group,
+        scratch_shapes=[
+            pltpu.VMEM(video.shape, BF16),
+            pltpu.VMEM((frames_in, rows_in, padded, chans), F32),
+            pltpu.SemaphoreType.DMA((4,)),
+        ],
+        compiler_params=pltpu.CompilerParams(vmem_limit_bytes=60 * 2**20),
+    )(corner, video, spatial_weights, temporal_weights)
 
     def gathered(pieces):
         return jnp.stack([pieces[0]] + [swapped(pieces[i], "space", i) for i in range(1, group)])
 
-    own_video = gathered(cuts[:group])
-    videos = [own_video, traded(own_video, 0), traded(own_video, 1)]
+    along_x = swapped(half_kernels, "section", 1)
+    along_y = swapped(half_kernels, "section", 2)
+    own_video, along_x, along_y = lax.optimization_barrier([gathered(cuts), along_x, along_y])
+    near, far = traded(own_video, 0), traded(own_video, 1)
+    mine = [along_x, along_y, swapped(along_x, "section", 2)]
+    shared = mine + [swapped(each) for each in mine]
+    own_kernels = jnp.stack([half_kernels, rest_kernels])
+
+    cuts = pl.pallas_call(
+        functools.partial(cotangent_kernel, halo, width),
+        name="cotangent",
+        in_specs=[smem] + [vmem] * 2,
+        out_specs=[vmem] * group,
+        out_shape=[jax.ShapeDtypeStruct((cores * frames_in, rows_in, width, chans), BF16)] * group,
+        scratch_shapes=[pltpu.VMEM((cores * frames_in, rows_in, padded, chans), F32)],
+        compiler_params=params,
+    )(corner, cotangent, cot_other)
+    near, own_kernels, *cuts = lax.optimization_barrier([near, own_kernels] + list(cuts))
+    shared = [own_kernels] + shared
+    videos = [own_video, near, far]
     videos += [swapped(each) for each in videos]
-    shared = [spatial_weights, temporal_weights] + mine + [swapped(each) for each in mine]
-
-    own_cot = gathered(cuts[group:])
+    own_cot = gathered(cuts)
     half = group // 2
     upper = unit // half
     cots = [own_cot] + [
         traded(lax.dynamic_slice_in_dim(own_cot, (upper ^ side) * half, half, 0), shift)
         for shift, side in ((0, 1 - odd), (1, odd))
     ]
-    cots += [swapped(each) for each in cots]
 
     geometry = (blocks, cores, group, frames_in, rows_in, halo, tile, width)
     frames = cores * frames_in
     high = tile + 2 * halo
-    per_section = (blocks,) + half_kernels.shape
+    per_section = (blocks,) + one_half.shape
     all_kernels = (cores,) + per_section
     saved = [
         jax.ShapeDtypeStruct((frames, tile + 2 * block + 2, width, chans), F32)
@@ -349,7 +409,7 @@
     features, hidden, *slopes = pl.pallas_call(
         functools.partial(forward_kernel, geometry),
         name="forward",
-        in_specs=[smem] + [vmem] * (2 * blocks + 6),
+        in_specs=[smem] + [vmem] * (2 * blocks + 5),
         out_specs=[vmem] * (2 + blocks),
         out_shape=[
             jax.ShapeDtypeStruct((blocks, frames, tile + 2, own_width, 3 * chans), BF16),
@@ -373,7 +433,7 @@
     keep, give, mine_grad, other_grad = pl.pallas_call(
         functools.partial(backward_kernel, geometry, factor),
         name="backward",
-        in_specs=[smem] + [vmem] * (3 * blocks + 8),
+        in_specs=[smem] + [vmem] * (3 * blocks + 4),
         out_specs=[vmem] * 4,
         out_shape=[
             jax.ShapeDtypeStruct(per_section, BF16),
@@ -396,41 +456,49 @@
 
     got = swapped(give)
     parts = [(keep[i].astype(F32) + got[i].astype(F32)).astype(BF16) for i in range(blocks)]
+    other_grad, *parts = lax.optimization_barrier([other_grad] + parts)
+    parts = parts[:1] + [swapped(parts[i], "section", i) for i in range(1, blocks)]
+    part = sum(each.astype(F32) for each in parts).astype(BF16)
+
+    halves = part.reshape(2, -1, chans)
+    low = unit % 2
+
+    def picked(which):
+        return lax.dynamic_index_in_dim(halves, which, 0, keepdims=False)
+
+    part = (picked(low).astype(F32) + swapped(picked(1 - low), "space", 1).astype(F32)).astype(BF16)
+    part = part.astype(F32) + swapped(part, "space", 2).astype(F32)
+    if tiles != group:
+        part = lax.psum(
+            part, "space", axis_index_groups=[list(range(i, tiles, group)) for i in range(group)]
+        )
+    part = part.astype(BF16)
+    pair = jnp.stack([part, swapped(part, "space", 1)])
+    spatial_out, temporal_out = pl.pallas_call(
+        closing_kernel,
+        name="closing",
+        in_specs=[smem] + [vmem] * 2,
+        out_specs=[vmem] * 2,
+        out_shape=[
+            jax.ShapeDtypeStruct(spatial_weights.shape, F32),
+            jax.ShapeDtypeStruct(temporal_weights.shape, F32),
+        ],
+        scratch_shapes=[pltpu.VMEM((cores * taps * chans, chans), BF16)],
+        compiler_params=params,
+    )(corner, pair, swapped(pair))
+
     other_grad = swapped(other_grad)
     first = core == 0
     wide = jnp.concatenate(
         [jnp.where(first, mine_grad, other_grad), jnp.where(first, other_grad, mine_grad)], 3
     )
     strips = [wide[0]] + [swapped(wide[i], "space", i) for i in range(1, group)]
-    parts = parts[:1] + [swapped(parts[i], "section", i) for i in range(1, blocks)]
-    part = sum(each.astype(F32) for each in parts).astype(BF16)
-    units = part.reshape(group, -1, chans)
-
-    def chunk(step):
-        return lax.dynamic_index_in_dim(units, unit ^ step, 0, keepdims=False)
-
-    parts = [chunk(0)] + [swapped(chunk(i), "space", i) for i in range(1, group)]
-    part = sum(each.astype(F32) for each in parts)
-    if tiles != group:
-        part = lax.psum(
-            part, "space", axis_index_groups=[list(range(i, tiles, group)) for i in range(group)]
-        )
-    part = part.astype(BF16)
-    chunks = jnp.stack([part] + [swapped(part, "space", i) for i in range(1, group)])
-    whole = jnp.zeros((cores,) + chunks.shape, BF16)
-    for which, each in ((core, chunks), (1 - core, swapped(chunks))):
-        for step in range(group):
-            whole = lax.dynamic_update_slice(
-                whole, each[step][None, None], (which, unit ^ step, 0, 0)
-            )
     grad_video = jnp.zeros(video.shape, BF16)
     for step, strip in enumerate(strips):
         grad_video = lax.dynamic_update_slice(
             grad_video, strip, (0, 0, (unit ^ step) * cores * own_width, 0)
         )
-    own = whole.reshape(-1, chans, chans).swapaxes(1, 2).astype(F32)[None]
-    count = spatial_weights.shape[1]
-    return own[:, :count], own[:, count:], grad_video
+    return spatial_out, temporal_out, grad_video
 
 
 def solution(mesh):

time: 93.8 us -> 91.5 us (0.975)
  starting transfers between devices: 42.4 us -> 31.9 us
  waiting for transfers between devices: 28.8 us -> 33.7 us
  Pallas kernels: 15.9 us -> 19.9 us
  local copies, waits for them, and re-layouts: 4.08 us -> 2.35 us
    ppermute x33 -> x28, starting transfers between devices: 39.3 us -> 25.8 us  [swapped(): return lax.ppermute(value, axis, [(i, i ^ step) for i in range(count)])]
    ppermute x33 -> x28, waiting for transfers between devices: 22.7 us -> 33.6 us  [swapped(): return lax.ppermute(value, axis, [(i, i ^ step) for i in range(count)])]
    ppermute x4, waiting for transfers between devices: 6.11 us -> 0.13 us  [traded(): return lax.ppermute(value, ('section', 'space'), pairs)]
    pallas_call x1 -> x3, Pallas kernels: 0.64 us -> 4.88 us  [the longest x1 2.66 us: on_device(): pl.pallas_call(functools.partial(opening_kernel, halo, span), name='openi...]
    ppermute x4, starting transfers between devices: 3.1 us -> 6.13 us  [traded(): return lax.ppermute(value, ('section', 'space'), pairs)]
    unnamed x12 -> x8, local copies, waits for them, and re-layouts: 3.69 us -> 1.57 us
    another operation x1 -> x2, other arithmetic: 0.03 us -> 1.08 us  [the longest x1 1.06 us: on_device(): own_kernels = jnp.stack([half_kernels, rest_kernels])]
    concatenate x1 -> x0, other arithmetic: 0.99 us -> none  [own_half(): own = jnp.concatenate([spatial_weights[0], temporal_weights[0]], 0)]
  transfers between devices with their start and end apart: 37 -> 32, of which waited for: 15 -> 11; matrix products, arithmetic and copies ran while one was open for 2% -> 2% of each run, Pallas kernels for 9% -> 10%
where the time goes in v6:
time: 91.5 us; the launch traced here: 91.2 us
  waiting for transfers between devices  33.7 us (37%)
  starting transfers between devices  31.9 us (35%)
  Pallas kernels  19.9 us (22%)
  other arithmetic  2.36 us (3%)
  local copies, waits for them, and re-layouts  2.35 us (3%)
  between operations  0.97 us (1%)
    ppermute x28, waiting for transfers between devices, swapped(): return lax.ppermute(value, axis, [(i, i ^ step) for i in range(count)])  33.6 us
    ppermute x28, starting transfers between devices, swapped(): return lax.ppermute(value, axis, [(i, i ^ step) for i in range(count)])  25.8 us
    pallas_call x1, Pallas kernels, on_device(): pl.pallas_call(functools.partial(forward_kernel, geometry), name='forward...  8.26 us
    pallas_call x1, Pallas kernels, on_device(): pl.pallas_call(functools.partial(backward_kernel, geometry, factor), name...  6.71 us
    ppermute x4, starting transfers between devices, traded(): return lax.ppermute(value, ('section', 'space'), pairs)  6.13 us
    pallas_call x1, Pallas kernels, on_device(): pl.pallas_call(functools.partial(opening_kernel, halo, span), name='openi...  2.66 us
  transfers between devices with their start and end apart: 32, of which 11 were waited for; matrix products, arithmetic and copies ran while one was open for 2% of the time, Pallas kernels for 10%

profile of v6, /device:TPU:0, one launch (start us, length us, event | category | flops | bytes accessed | tf_op | source)
XLA Modules:
  0.0 91.2 jit_solution(771261851392283553)
XLA Ops:
  1.3 2.7 %opening.1 = (bf16[6,128,128]{2,1,0:T(8,128)(2,1)}, bf16[6,128,128]{2,1,0:T(8,128)(2,1)}, bf16[2,2,48,128]{3,2,1,0:T(8,128)(2,1)}, bf16[2,2,48,128]{3,2,1,0:T(8,...) custom-call(s32[8]{0:T(128)} %stack.75.place_ref, bf16[2,2,128,128]{3,2,1,0:T(8,128)(2,1)} %video_hbm.1, ...), custom_call_target="tpu_custom_call" | custom-call | tf_op jit(solution)/shard_map/opening/pallas_call | solution.py:352
  4.0 3.0 %collective-permute-start.3 = (bf16[6,128,128]{2,1,0:T(8,128)(2,1)}, bf16[6,128,128]{2,1,0:T(8,128)(2,1)S(1)}, u32[]{:S(2)}, u32[]{:S(2)}) collective-permute-start(bf16[6,128,128]{2,1,0:T(8,128)(2,1)} %get-tuple-element.43), channel_id=1, source_target_pairs={{0,8},{8,0},{16,24},{24,16},{1,9},{9,1},{17,25},{25,17},{2,10},{10... | collective-permute-start | bytes 589832 | tf_op jit(solution)/shard_map/ppermute | solution.py:307
  7.0 1.5 %collective-permute-start.4 = (bf16[6,128,128]{2,1,0:T(8,128)(2,1)}, bf16[6,128,128]{2,1,0:T(8,128)(2,1)S(1)}, u32[]{:S(2)}, u32[]{:S(2)}) collective-permute-start(bf16[6,128,128]{2,1,0:T(8,128)(2,1)} %get-tuple-element.43), channel_id=1, source_target_pairs={{0,16},{8,24},{16,0},{24,8},{1,17},{9,25},{17,1},{25,9},{2,18},{10... | collective-permute-start | bytes 589832 | tf_op jit(solution)/shard_map/ppermute | solution.py:307
  8.5 1.6 %collective-permute-start = (bf16[2,2,48,128]{3,2,1,0:T(8,128)(2,1)}, bf16[2,2,48,128]{3,2,1,0:T(8,128)(2,1)S(1)}, u32[]{:S(2)}, u32[]{:S(2)}) collective-permute-start(bf16[2,2,48,128]{3,2,1,0:T(8,128)(2,1)} %get-tuple-element.40), channel_id=1, source_target_pairs={{0,1},{1,0},{2,3},{3,2},{4,5},{5,4},{6,7},{7,6},{8,9},{9,8},{10,11... | collective-permute-start | bytes 147464 | tf_op jit(solution)/shard_map/ppermute | solution.py:307
  10.1 2.6 %collective-permute-start.1 = (bf16[2,2,48,128]{3,2,1,0:T(8,128)(2,1)}, bf16[2,2,48,128]{3,2,1,0:T(8,128)(2,1)S(1)}, u32[]{:S(2)}, u32[]{:S(2)}) collective-permute-start(bf16[2,2,48,128]{3,2,1,0:T(8,128)(2,1)} %get-tuple-element.41), channel_id=1, source_target_pairs={{0,2},{1,3},{2,0},{3,1},{4,6},{5,7},{6,4},{7,5},{8,10},{9,11},{10,... | collective-permute-start | bytes 147464 | tf_op jit(solution)/shard_map/ppermute | solution.py:307
  12.9 2.9 %collective-permute-done.1 = bf16[2,2,48,128]{3,2,1,0:T(8,128)(2,1)S(1)} collective-permute-done((bf16[2,2,48,128]{3,2,1,0:T(8,128)(2,1)}, bf16[2,2,48,128]{3,2,1,0:T(8,128)(2,1)S(1)}, u32[]{:S(2)}, u32[]{:S(2)}) %collective-permute-start.1) | collective-permute-done | bytes 49184 | tf_op jit(solution)/shard_map/ppermute | solution.py:307
  15.8 3.0 %collective-permute-done.2 = bf16[2,2,48,128]{3,2,1,0:T(8,128)(2,1)S(1)} collective-permute-done((bf16[2,2,48,128]{3,2,1,0:T(8,128)(2,1)}, bf16[2,2,48,128]{3,2,1,0:T(8,128)(2,1)S(1)}, u32[]{:S(2)}, u32[]{:S(2)}) %collective-permute-start.2) | collective-permute-done | bytes 49184 | tf_op jit(solution)/shard_map/ppermute | solution.py:307
  25.4 1.2 %collective-permute-start.12 = (bf16[4,2,32,128]{3,2,1,0:T(8,128)(2,1)S(1)}, bf16[4,2,32,128]{3,2,1,0:T(8,128)(2,1)S(1)}, u32[]{:S(2)}, u32[]{:S(2)}) collective-permute-start(bf16[4,2,32,128]{3,2,1,0:T(8,128)(2,1)S(1)} %get-tuple-element.55), channel_id=1, source_target_pairs={{0,2},{1,3},{2,0},{3,1},{4,6},{5,7},{6,4},{7,5},{8,10},{9,11},{10,... | collective-permute-start | bytes 196616 | tf_op jit(solution)/shard_map/ppermute | solution.py:307
  26.6 3.2 %collective-permute-start.13 = (bf16[4,2,32,128]{3,2,1,0:T(8,128)(2,1)S(1)}, bf16[4,2,32,128]{3,2,1,0:T(8,128)(2,1)S(1)}, u32[]{:S(2)}, u32[]{:S(2)}) collective-permute-start(bf16[4,2,32,128]{3,2,1,0:T(8,128)(2,1)S(1)} %get-tuple-element.56), channel_id=1, source_target_pairs={{0,3},{1,2},{2,1},{3,0},{4,7},{5,6},{6,5},{7,4},{8,11},{9,10},{10,... | collective-permute-start | bytes 196616 | tf_op jit(solution)/shard_map/ppermute | solution.py:307
  30.5 3.4 %collective-permute-done.12 = bf16[4,2,32,128]{3,2,1,0:T(8,128)(2,1)S(1)} collective-permute-done((bf16[4,2,32,128]{3,2,1,0:T(8,128)(2,1)S(1)}, bf16[4,2,32,128]{3,2,1,0:T(8,128)(2,1)S(1)}, u32[]{:S(2)}, u32[]{:S(2)}) %collective-permute-start.12) | collective-permute-done | bytes 65568 | tf_op jit(solution)/shard_map/ppermute | solution.py:307
  34.4 4.2 %collective-permute-start.14 = (bf16[2,4,2,32,128]{4,3,2,1,0:T(8,128)(2,1)S(1)}, bf16[2,4,2,32,128]{4,3,2,1,0:T(8,128)(2,1)S(1)}, u32[]{:S(2)}, u32[]{:S(2)}) collective-permute-start(bf16[2,4,2,32,128]{4,3,2,1,0:T(8,128)(2,1)S(1)} %get-tuple-element.80), channel_id=1, source_target_pairs={{0,8},{1,9},{2,10},{3,11},{8,0},{9,1},{10,2},{11,3},{16,24},{17,25... | collective-permute-start | bytes 393224 | tf_op jit(solution)/shard_map/ppermute | solution.py:335
  39.4 8.3 %forward.1 = (bf16[4,4,10,16,384]{4,3,2,1,0:T(8,128)(2,1)S(1)}, bf16[4,4,8,16,128]{4,3,2,1,0:T(8,128)(2,1)S(1)}, f32[4,10,32,128]{3,2,1,0:T(8,128)S(1)}, f32[4,1...) custom-call(s32[8]{0:T(128)S(1)} %copy-done.2, ...), custom_call_target="tpu_custom_call" | custom-call | flops 6000000000 | bytes 8000000 | tf_op jit(solution)/shard_map/forward/pallas_call | solution.py:409
  47.6 6.7 %backward.1 = (bf16[4,6,128,128]{3,2,1,0:T(8,128)(2,1)S(1)}, bf16[4,6,128,128]{3,2,1,0:T(8,128)(2,1)S(1)}, bf16[4,2,2,16,128]{4,3,2,1,0:T(8,128)(2,1)S(1)}, bf16[4,2,2,16,128]{4,3,2,1,0:T(8,128)(2,1)S(1)}) custom-call(s32[8]{0:T(128)S(1)} %copy-done.2, bf16[2,6,128,128]{3,2,1,0:T(8,128)(2,1)S(1)} %pad_maximum_fusion.rest_0_, ...), custom_call_target="tpu_custom_call" | custom-call | flops 6000000000 | bytes 8000000 | tf_op jit(solution)/shard_map/backward/pallas_call | solution.py:433
  54.4 2.3 %collective-permute-done.20 = bf16[4,6,128,128]{3,2,1,0:T(8,128)(2,1)S(1)} collective-permute-done((bf16[4,6,128,128]{3,2,1,0:T(8,128)(2,1)S(1)}, bf16[4,6,128,128]{3,2,1,0:T(8,128)(2,1)S(1)}, u32[]{:S(2)}, u32[]{:S(2)}) %collective-permute-start.20) | collective-permute-done | bytes 786464 | tf_op jit(solution)/shard_map/ppermute | solution.py:307
  57.1 2.7 %collective-permute-start.21 = (bf16[6,128,128]{2,1,0:T(8,128)(2,1)S(1)}, bf16[6,128,128]{2,1,0:T(8,128)(2,1)S(1)}, u32[]{:S(2)}, u32[]{:S(2)}) collective-permute-start(bf16[6,128,128]{2,1,0:T(8,128)(2,1)S(1)} %get-tuple-element.68), channel_id=1, source_target_pairs={{0,8},{8,0},{16,24},{24,16},{1,9},{9,1},{17,25},{25,17},{2,10},{10... | collective-permute-start | bytes 589832 | tf_op jit(solution)/shard_map/ppermute | solution.py:307
  59.9 1.4 %collective-permute-start.23 = (bf16[6,128,128]{2,1,0:T(8,128)(2,1)S(1)}, bf16[6,128,128]{2,1,0:T(8,128)(2,1)S(1)}, u32[]{:S(2)}, u32[]{:S(2)}) collective-permute-start(bf16[6,128,128]{2,1,0:T(8,128)(2,1)S(1)} %get-tuple-element.70), channel_id=1, source_target_pairs={{0,24},{8,16},{16,8},{24,0},{1,25},{9,17},{17,9},{25,1},{2,26},{10... | collective-permute-start | bytes 589832 | tf_op jit(solution)/shard_map/ppermute | solution.py:307
  61.4 4.2 %collective-permute-done.21 = bf16[6,128,128]{2,1,0:T(8,128)(2,1)S(1)} collective-permute-done((bf16[6,128,128]{2,1,0:T(8,128)(2,1)S(1)}, bf16[6,128,128]{2,1,0:T(8,128)(2,1)S(1)}, u32[]{:S(2)}, u32[]{:S(2)}) %collective-permute-start.21) | collective-permute-done | bytes 196640 | tf_op jit(solution)/shard_map/ppermute | solution.py:307
  65.6 5.4 %collective-permute-done.22 = bf16[6,128,128]{2,1,0:T(8,128)(2,1)S(1)} collective-permute-done((bf16[6,128,128]{2,1,0:T(8,128)(2,1)S(1)}, bf16[6,128,128]{2,1,0:T(8,128)(2,1)S(1)}, u32[]{:S(2)}, u32[]{:S(2)}) %collective-permute-start.22) | collective-permute-done | bytes 196640 | tf_op jit(solution)/shard_map/ppermute | solution.py:307
  72.0 1.3 %collective-permute-start.29 = (bf16[2,2,32,128]{3,2,1,0:T(8,128)(2,1)S(1)}, bf16[2,2,32,128]{3,2,1,0:T(8,128)(2,1)S(1)}, u32[]{:S(2)}, u32[]{:S(2)}) collective-permute-start(bf16[2,2,32,128]{3,2,1,0:T(8,128)(2,1)S(1)} %get-tuple-element.82), channel_id=1, source_target_pairs={{0,1},{1,0},{2,3},{3,2},{4,5},{5,4},{6,7},{7,6},{8,9},{9,8},{10,11... | collective-permute-start | bytes 98312 | tf_op jit(solution)/shard_map/ppermute | solution.py:307
  74.0 2.4 %collective-permute-start.31 = (bf16[2,2,32,128]{3,2,1,0:T(8,128)(2,1)S(1)}, bf16[2,2,32,128]{3,2,1,0:T(8,128)(2,1)S(1)}, u32[]{:S(2)}, u32[]{:S(2)}) collective-permute-start(bf16[2,2,32,128]{3,2,1,0:T(8,128)(2,1)S(1)} %get-tuple-element.81), channel_id=1, source_target_pairs={{0,3},{1,2},{2,1},{3,0},{4,7},{5,6},{6,5},{7,4},{8,11},{9,10},{10,... | collective-permute-start | bytes 98312 | tf_op jit(solution)/shard_map/ppermute | solution.py:307
  76.9 6.4 %collective-permute-done.25 = bf16[384,128]{1,0:T(8,128)(2,1)S(1)} collective-permute-done((bf16[384,128]{1,0:T(8,128)(2,1)S(1)}, bf16[384,128]{1,0:T(8,128)(2,1)S(1)}, u32[]{:S(2)}, u32[]{:S(2)}) %collective-permute-start.25) | collective-permute-done | bytes 98336 | tf_op jit(solution)/shard_map/ppermute | solution.py:307
  83.5 4.6 %collective-permute-done.26 = bf16[384,128]{1,0:T(8,128)(2,1)S(1)} collective-permute-done((bf16[384,128]{1,0:T(8,128)(2,1)S(1)}, bf16[384,128]{1,0:T(8,128)(2,1)S(1)}, u32[]{:S(2)}, u32[]{:S(2)}) %collective-permute-start.26) | collective-permute-done | bytes 98336 | tf_op jit(solution)/shard_map/ppermute | solution.py:307
  88.2 1.4 %collective-permute-done.27.other_ref = bf16[2,384,128]{2,1,0:T(8,128)(2,1)S(1)} collective-permute-done((bf16[2,384,128]{2,1,0:T(8,128)(2,1)S(1)}, bf16[2,384,128]{2,1,0:T(8,128)(2,1)S(1)}, u32[]{:S(2)}, u32[]{:S(2)}) %collective-permute-start.27) | collective-permute-done | bytes 196640 | tf_op jit(solution)/shard_map/ppermute | solution.py:307
  89.6 1.6 %closing.1 = (f32[1,9,128,128]{3,2,1,0:T(8,128)}, f32[1,3,128,128]{3,2,1,0:T(8,128)}) custom-call(s32[8]{0:T(128)S(1)} %copy-done.2, bf16[2,384,128]{2,1,0:T(8,128)(2,1)S(1)} %pad_maximum_fusion.3.mine_ref, bf16[2,384,128]{2,1,0:T(8,128)(2,1)S(1)} %collective-permute-done.27.other_ref), custom_call_target="tpu_custom_call" | custom-call | tf_op jit(solution)/shard_map/closing/pallas_call | solution.py:477
  (71 shorter events, 12.5 us)
Async XLA Ops:
  4.0 15.6 %collective-permute-start.3 = (bf16[6,128,128]{2,1,0:T(8,128)(2,1)}, bf16[6,128,128]{2,1,0:T(8,128)(2,1)S(1)}, u32[]{:S(2)}, u32[]{:S(2)}) collective-permute-start(bf16[6,128,128]{2,1,0:T(8,128)(2,1)} %get-tuple-element.43), channel_id=1, source_target_pairs={{0,8},{8,0},{16,24},{24,16},{1,9},{9,1},{17,25},{25,17},{2,10},{10... | collective-permute-start | bytes 589832 | tf_op jit(solution)/shard_map/ppermute | solution.py:307
  7.0 12.6 %collective-permute-start.4 = (bf16[6,128,128]{2,1,0:T(8,128)(2,1)}, bf16[6,128,128]{2,1,0:T(8,128)(2,1)S(1)}, u32[]{:S(2)}, u32[]{:S(2)}) collective-permute-start(bf16[6,128,128]{2,1,0:T(8,128)(2,1)} %get-tuple-element.43), channel_id=1, source_target_pairs={{0,16},{8,24},{16,0},{24,8},{1,17},{9,25},{17,1},{25,9},{2,18},{10... | collective-permute-start | bytes 589832 | tf_op jit(solution)/shard_map/ppermute | solution.py:307
  10.1 5.7 %collective-permute-start.1 = (bf16[2,2,48,128]{3,2,1,0:T(8,128)(2,1)}, bf16[2,2,48,128]{3,2,1,0:T(8,128)(2,1)S(1)}, u32[]{:S(2)}, u32[]{:S(2)}) collective-permute-start(bf16[2,2,48,128]{3,2,1,0:T(8,128)(2,1)} %get-tuple-element.41), channel_id=1, source_target_pairs={{0,2},{1,3},{2,0},{3,1},{4,6},{5,7},{6,4},{7,5},{8,10},{9,11},{10,... | collective-permute-start | bytes 147464 | tf_op jit(solution)/shard_map/ppermute | solution.py:307
  12.7 6.1 %collective-permute-start.2 = (bf16[2,2,48,128]{3,2,1,0:T(8,128)(2,1)}, bf16[2,2,48,128]{3,2,1,0:T(8,128)(2,1)S(1)}, u32[]{:S(2)}, u32[]{:S(2)}) collective-permute-start(bf16[2,2,48,128]{3,2,1,0:T(8,128)(2,1)} %get-tuple-element.42), channel_id=1, source_target_pairs={{0,3},{1,2},{2,1},{3,0},{4,7},{5,6},{6,5},{7,4},{8,11},{9,10},{10,... | collective-permute-start | bytes 147464 | tf_op jit(solution)/shard_map/ppermute | solution.py:307
  19.6 5.7 %collective-permute-start.5 = (bf16[4,2,2,48,128]{4,3,2,1,0:T(8,128)(2,1)S(1)}, bf16[4,2,2,48,128]{4,3,2,1,0:T(8,128)(2,1)S(1)}, u32[]{:S(2)}, u32[]{:S(2)}) collective-permute-start(bf16[4,2,2,48,128]{4,3,2,1,0:T(8,128)(2,1)S(1)} %pad_maximum_fusion.2.rest_7_), channel_id=1, source_target_pairs={{0,8},{1,9},{2,10},{3,11},{8,0},{9,1},{10,2},{11,3},{16,24},{17,25... | collective-permute-start | bytes 589832 | tf_op jit(solution)/shard_map/ppermute | solution.py:335
  20.2 6.3 %collective-permute-start.7 = (bf16[6,128,128]{2,1,0:T(8,128)(2,1)S(1)}, bf16[6,128,128]{2,1,0:T(8,128)(2,1)S(1)}, u32[]{:S(2)}, u32[]{:S(2)}) collective-permute-start(bf16[6,128,128]{2,1,0:T(8,128)(2,1)S(1)} %collective-permute-done.3.rest_1_), channel_id=1, source_target_pairs={{0,16},{8,24},{16,0},{24,8},{1,17},{9,25},{17,1},{25,9},{2,18},{10... | collective-permute-start | bytes 589832 | tf_op jit(solution)/shard_map/ppermute | solution.py:307
  20.8 9.0 %collective-permute-start.16 = (bf16[4,2,2,48,128]{4,3,2,1,0:T(8,128)(2,1)S(1)}, bf16[4,2,2,48,128]{4,3,2,1,0:T(8,128)(2,1)S(1)}, u32[]{:S(2)}, u32[]{:S(2)}) collective-permute-start(bf16[4,2,2,48,128]{4,3,2,1,0:T(8,128)(2,1)S(1)} %pad_maximum_fusion.2.rest_7_), channel_id=1, source_target_pairs={{8,16},{9,17},{10,18},{11,19},{16,8},{17,9},{18,10},{19,11},{12,20... | collective-permute-start | bytes 589832 | tf_op jit(solution)/shard_map/ppermute | solution.py:335
  21.4 8.4 %collective-permute-start.17 = (bf16[4,2,2,48,128]{4,3,2,1,0:T(8,128)(2,1)S(1)}, bf16[4,2,2,48,128]{4,3,2,1,0:T(8,128)(2,1)S(1)}, u32[]{:S(2)}, u32[]{:S(2)}) collective-permute-start(bf16[4,2,2,48,128]{4,3,2,1,0:T(8,128)(2,1)S(1)} %pad_maximum_fusion.2.rest_7_), channel_id=1, source_target_pairs={{0,4},{4,0},{1,5},{5,1},{2,6},{6,2},{3,7},{7,3},{8,12},{12,8},{9,1... | collective-permute-start | bytes 589832 | tf_op jit(solution)/shard_map/ppermute | solution.py:307
  25.4 8.4 %collective-permute-start.12 = (bf16[4,2,32,128]{3,2,1,0:T(8,128)(2,1)S(1)}, bf16[4,2,32,128]{3,2,1,0:T(8,128)(2,1)S(1)}, u32[]{:S(2)}, u32[]{:S(2)}) collective-permute-start(bf16[4,2,32,128]{3,2,1,0:T(8,128)(2,1)S(1)} %get-tuple-element.55), channel_id=1, source_target_pairs={{0,2},{1,3},{2,0},{3,1},{4,6},{5,7},{6,4},{7,5},{8,10},{9,11},{10,... | collective-permute-start | bytes 196616 | tf_op jit(solution)/shard_map/ppermute | solution.py:307
  26.6 7.3 %collective-permute-start.13 = (bf16[4,2,32,128]{3,2,1,0:T(8,128)(2,1)S(1)}, bf16[4,2,32,128]{3,2,1,0:T(8,128)(2,1)S(1)}, u32[]{:S(2)}, u32[]{:S(2)}) collective-permute-start(bf16[4,2,32,128]{3,2,1,0:T(8,128)(2,1)S(1)} %get-tuple-element.56), channel_id=1, source_target_pairs={{0,3},{1,2},{2,1},{3,0},{4,7},{5,6},{6,5},{7,4},{8,11},{9,10},{10,... | collective-permute-start | bytes 196616 | tf_op jit(solution)/shard_map/ppermute | solution.py:307
  29.8 8.9 %collective-permute-start.9 = (bf16[6,128,128]{2,1,0:T(8,128)(2,1)S(1)}, bf16[6,128,128]{2,1,0:T(8,128)(2,1)S(1)}, u32[]{:S(2)}, u32[]{:S(2)}) collective-permute-start(bf16[6,128,128]{2,1,0:T(8,128)(2,1)S(1)} %collective-permute-done.4.rest_2_), channel_id=1, source_target_pairs={{0,4},{4,0},{1,5},{5,1},{2,6},{6,2},{3,7},{7,3},{8,12},{12,8},{9,1... | collective-permute-start | bytes 589832 | tf_op jit(solution)/shard_map/ppermute | solution.py:307
  30.5 8.9 %collective-permute-start.18 = (bf16[4,2,2,48,128]{4,3,2,1,0:T(8,128)(2,1)S(1)}, bf16[4,2,2,48,128]{4,3,2,1,0:T(8,128)(2,1)S(1)}, u32[]{:S(2)}, u32[]{:S(2)}) collective-permute-start(bf16[4,2,2,48,128]{4,3,2,1,0:T(8,128)(2,1)S(1)} %collective-permute-done.5.rest_8_), channel_id=1, source_target_pairs={{0,4},{4,0},{1,5},{5,1},{2,6},{6,2},{3,7},{7,3},{8,12},{12,8},{9,1... | collective-permute-start | bytes 589832 | tf_op jit(solution)/shard_map/ppermute | solution.py:307
  33.8 5.5 %collective-permute-start.10 = (bf16[6,128,128]{2,1,0:T(8,128)(2,1)S(1)}, bf16[6,128,128]{2,1,0:T(8,128)(2,1)S(1)}, u32[]{:S(2)}, u32[]{:S(2)}) collective-permute-start(bf16[6,128,128]{2,1,0:T(8,128)(2,1)S(1)} %collective-permute-done.7.rest_3_), channel_id=1, source_target_pairs={{0,4},{4,0},{1,5},{5,1},{2,6},{6,2},{3,7},{7,3},{8,12},{12,8},{9,1... | collective-permute-start | bytes 589832 | tf_op jit(solution)/shard_map/ppermute | solution.py:307
  33.8 5.5 %collective-permute-start.19 = (bf16[4,2,2,48,128]{4,3,2,1,0:T(8,128)(2,1)S(1)}, bf16[4,2,2,48,128]{4,3,2,1,0:T(8,128)(2,1)S(1)}, u32[]{:S(2)}, u32[]{:S(2)}) collective-permute-start(bf16[4,2,2,48,128]{4,3,2,1,0:T(8,128)(2,1)S(1)} %collective-permute-done.16.rest_9_), channel_id=1, source_target_pairs={{0,4},{4,0},{1,5},{5,1},{2,6},{6,2},{3,7},{7,3},{8,12},{12,8},{9,1... | collective-permute-start | bytes 589832 | tf_op jit(solution)/shard_map/ppermute | solution.py:307
  34.4 13.2 %collective-permute-start.14 = (bf16[2,4,2,32,128]{4,3,2,1,0:T(8,128)(2,1)S(1)}, bf16[2,4,2,32,128]{4,3,2,1,0:T(8,128)(2,1)S(1)}, u32[]{:S(2)}, u32[]{:S(2)}) collective-permute-start(bf16[2,4,2,32,128]{4,3,2,1,0:T(8,128)(2,1)S(1)} %get-tuple-element.80), channel_id=1, source_target_pairs={{0,8},{1,9},{2,10},{3,11},{8,0},{9,1},{10,2},{11,3},{16,24},{17,25... | collective-permute-start | bytes 393224 | tf_op jit(solution)/shard_map/ppermute | solution.py:335
  38.6 9.0 %collective-permute-start.15 = (bf16[2,4,2,32,128]{4,3,2,1,0:T(8,128)(2,1)S(1)}, bf16[2,4,2,32,128]{4,3,2,1,0:T(8,128)(2,1)S(1)}, u32[]{:S(2)}, u32[]{:S(2)}) collective-permute-start(bf16[2,4,2,32,128]{4,3,2,1,0:T(8,128)(2,1)S(1)} %get-tuple-element.79), channel_id=1, source_target_pairs={{8,16},{9,17},{10,18},{11,19},{16,8},{17,9},{18,10},{19,11},{12,20... | collective-permute-start | bytes 393224 | tf_op jit(solution)/shard_map/ppermute | solution.py:335
  57.1 8.5 %collective-permute-start.21 = (bf16[6,128,128]{2,1,0:T(8,128)(2,1)S(1)}, bf16[6,128,128]{2,1,0:T(8,128)(2,1)S(1)}, u32[]{:S(2)}, u32[]{:S(2)}) collective-permute-start(bf16[6,128,128]{2,1,0:T(8,128)(2,1)S(1)} %get-tuple-element.68), channel_id=1, source_target_pairs={{0,8},{8,0},{16,24},{24,16},{1,9},{9,1},{17,25},{25,17},{2,10},{10... | collective-permute-start | bytes 589832 | tf_op jit(solution)/shard_map/ppermute | solution.py:307
  59.8 11.1 %collective-permute-start.22 = (bf16[6,128,128]{2,1,0:T(8,128)(2,1)S(1)}, bf16[6,128,128]{2,1,0:T(8,128)(2,1)S(1)}, u32[]{:S(2)}, u32[]{:S(2)}) collective-permute-start(bf16[6,128,128]{2,1,0:T(8,128)(2,1)S(1)} %get-tuple-element.69), channel_id=1, source_target_pairs={{0,16},{8,24},{16,0},{24,8},{1,17},{9,25},{17,1},{25,9},{2,18},{10... | collective-permute-start | bytes 589832 | tf_op jit(solution)/shard_map/ppermute | solution.py:307
  59.9 11.0 %collective-permute-start.23 = (bf16[6,128,128]{2,1,0:T(8,128)(2,1)S(1)}, bf16[6,128,128]{2,1,0:T(8,128)(2,1)S(1)}, u32[]{:S(2)}, u32[]{:S(2)}) collective-permute-start(bf16[6,128,128]{2,1,0:T(8,128)(2,1)S(1)} %get-tuple-element.70), channel_id=1, source_target_pairs={{0,24},{8,16},{16,8},{24,0},{1,25},{9,17},{17,9},{25,1},{2,26},{10... | collective-permute-start | bytes 589832 | tf_op jit(solution)/shard_map/ppermute | solution.py:307
  71.1 5.3 %collective-permute-start.24 = (bf16[384,128]{1,0:T(8,128)(2,1)S(1)}, bf16[384,128]{1,0:T(8,128)(2,1)S(1)}, u32[]{:S(2)}, u32[]{:S(2)}) collective-permute-start(bf16[384,128]{1,0:T(8,128)(2,1)S(1)} %dynamic-slice_bitcast_fusion), channel_id=1, source_target_pairs={{0,1},{1,0},{2,3},{3,2},{4,5},{5,4},{6,7},{7,6},{8,9},{9,8},{10,11... | collective-permute-start | bytes 294920 | tf_op jit(solution)/shard_map/ppermute | solution.py:307
  72.0 11.5 %collective-permute-start.29 = (bf16[2,2,32,128]{3,2,1,0:T(8,128)(2,1)S(1)}, bf16[2,2,32,128]{3,2,1,0:T(8,128)(2,1)S(1)}, u32[]{:S(2)}, u32[]{:S(2)}) collective-permute-start(bf16[2,2,32,128]{3,2,1,0:T(8,128)(2,1)S(1)} %get-tuple-element.82), channel_id=1, source_target_pairs={{0,1},{1,0},{2,3},{3,2},{4,5},{5,4},{6,7},{7,6},{8,9},{9,8},{10,11... | collective-permute-start | bytes 98312 | tf_op jit(solution)/shard_map/ppermute | solution.py:307
  73.3 14.9 %collective-permute-start.30 = (bf16[2,2,32,128]{3,2,1,0:T(8,128)(2,1)S(1)}, bf16[2,2,32,128]{3,2,1,0:T(8,128)(2,1)S(1)}, u32[]{:S(2)}, u32[]{:S(2)}) collective-permute-start(bf16[2,2,32,128]{3,2,1,0:T(8,128)(2,1)S(1)} %get-tuple-element.83), channel_id=1, source_target_pairs={{0,2},{1,3},{2,0},{3,1},{4,6},{5,7},{6,4},{7,5},{8,10},{9,11},{10,... | collective-permute-start | bytes 98312 | tf_op jit(solution)/shard_map/ppermute | solution.py:307
  74.0 14.2 %collective-permute-start.31 = (bf16[2,2,32,128]{3,2,1,0:T(8,128)(2,1)S(1)}, bf16[2,2,32,128]{3,2,1,0:T(8,128)(2,1)S(1)}, u32[]{:S(2)}, u32[]{:S(2)}) collective-permute-start(bf16[2,2,32,128]{3,2,1,0:T(8,128)(2,1)S(1)} %get-tuple-element.81), channel_id=1, source_target_pairs={{0,3},{1,2},{2,1},{3,0},{4,7},{5,6},{6,5},{7,4},{8,11},{9,10},{10,... | collective-permute-start | bytes 98312 | tf_op jit(solution)/shard_map/ppermute | solution.py:307
  76.5 6.9 %collective-permute-start.25 = (bf16[384,128]{1,0:T(8,128)(2,1)S(1)}, bf16[384,128]{1,0:T(8,128)(2,1)S(1)}, u32[]{:S(2)}, u32[]{:S(2)}) collective-permute-start(bf16[384,128]{1,0:T(8,128)(2,1)S(1)} %fusion.4), channel_id=1, source_target_pairs={{0,2},{1,3},{2,0},{3,1},{4,6},{5,7},{6,4},{7,5},{8,10},{9,11},{10,... | collective-permute-start | bytes 294920 | tf_op jit(solution)/shard_map/ppermute | solution.py:307
  (12 other events, 72.0 us)

commit v7 on v6

--- a/solution.py
+++ b/solution.py
@@ -36,67 +36,57 @@
     return jnp.concatenate([kernel_of(w_ref, block, tap) for tap in order], 1)
 
 
-def opening_kernel(
-    halo, span, place_ref, video_hbm, spatial_hbm, temporal_hbm, mine_ref, other_ref, *rest
-):
-    targets, (video_ref, wide_ref, sems) = rest[:-3], rest[-3:]
-    taps, count = mine_ref.shape[0], spatial_hbm.shape[1]
-    copy_video = pltpu.make_async_copy(video_hbm, video_ref, sems.at[0])
-    copy_video.start()
-
-    def kernel_copies(core):
-        copies = []
-        for half, ref in ((core, mine_ref), (1 - core, other_ref)):
-            first, last = half * taps, (half + 1) * taps
-            split = min(max(count, first), last)
-            if split > first:
-                source, target = spatial_hbm.at[0, first:split], ref.at[: split - first]
-                copies.append(pltpu.make_async_copy(source, target, sems.at[1 + len(copies)]))
-            if last > split:
-                source, target = temporal_hbm.at[0, split - count : last - count], ref.at[split - first :]
-                copies.append(pltpu.make_async_copy(source, target, sems.at[1 + len(copies)]))
-        return copies
-
-    for core in range(2):
-        @pl.when(place_ref[4] == core)
-        def _(core=core):
-            for copy in kernel_copies(core):
-                copy.start()
-
+def placed(group):
+    place, section = lax.axis_index("space"), lax.axis_index("section")
+    band = (section * lax.axis_size("space") + place) // group
+    return lax.axis_index("tm"), section, band, place % group
+
+
+def window_kernel(halo, span, video_ref, *rest):
+    targets, wide_ref = rest[:-1], rest[-1]
+    unit = placed(len(targets))[3]
     frames, rows, columns, chans = video_ref.shape
     edge = jnp.zeros((frames, rows, halo, chans), F32)
     wide_ref[:, :, :halo] = edge
     wide_ref[:, :, halo + columns :] = edge
-    copy_video.wait()
     wide_ref[:, :, halo : halo + columns] = video_ref[...].astype(F32)
     for step, target in enumerate(targets):
-        at = jnp.bitwise_xor(place_ref[7], step) * (span - 2 * halo)
+        at = jnp.bitwise_xor(unit, step) * (span - 2 * halo)
         target[...] = wide_ref[:, :, pl.ds(pl.multiple_of(at, 16), span)].astype(BF16)
-    for core in range(2):
-        @pl.when(place_ref[4] == core)
-        def _(core=core):
-            for copy in kernel_copies(core):
-                copy.wait()
-
-
-def cotangent_kernel(halo, width, place_ref, mine_ref, other_ref, *rest):
-    targets, wide_ref = rest[:-1], rest[-1]
-    frames_in, rows, columns, chans = mine_ref.shape
-    core = place_ref[4]
-    edge = jnp.zeros((2 * frames_in, rows, halo, chans), F32)
-    wide_ref[:, :, :halo] = edge
-    wide_ref[:, :, halo + columns :] = edge
-    for whose, ref in ((core, mine_ref), (1 - core, other_ref)):
-        wide_ref[pl.ds(whose * frames_in, frames_in), :, halo : halo + columns] = ref[...].astype(F32)
+
+
+def halves_kernel(spatial_ref, temporal_ref, half_ref, both_ref, all_ref):
+    core = lax.axis_index("tm")
+    count = spatial_ref.shape[1]
+    taps = half_ref.shape[0]
+    all_ref[:count] = spatial_ref[0]
+    all_ref[count:] = temporal_ref[0]
+    half_ref[...] = all_ref[pl.ds(core * taps, taps)]
+    both_ref[0] = all_ref[pl.ds(core * taps, taps)]
+    both_ref[1] = all_ref[pl.ds((1 - core) * taps, taps)]
+
+
+def cotangent_kernel(halo, width, *rest):
+    sources, targets, wide_ref = rest[:4], rest[4:-1], rest[-1]
+    core, _, _, unit = placed(len(targets))
+    frames_in, rows, columns, chans = sources[0].shape
+    edge = jnp.zeros((2, 2 * frames_in, rows, halo, chans), F32)
+    wide_ref[:, :, :, :halo] = edge
+    wide_ref[:, :, :, halo + columns :] = edge
+    for index, ref in enumerate(sources):
+        whose = core if index % 2 == 0 else 1 - core
+        wide_ref[index // 2, pl.ds(whose * frames_in, frames_in), :, halo : halo + columns] = ref[
+            ...
+        ].astype(F32)
     own = width - 2 * halo
     for step, target in enumerate(targets):
-        at = (jnp.bitwise_xor(place_ref[7], step) * 2 + core) * own
-        target[...] = wide_ref[:, :, pl.ds(pl.multiple_of(at, 16), width)].astype(BF16)
-
-
-def closing_kernel(place_ref, mine_ref, other_ref, spatial_ref, temporal_ref, flat_ref):
+        at = (jnp.bitwise_xor(unit, step) * 2 + core) * own
+        target[...] = wide_ref[:, :, :, pl.ds(pl.multiple_of(at, 16), width)].astype(BF16)
+
+
+def closing_kernel(group, mine_ref, other_ref, spatial_ref, temporal_ref, flat_ref):
     pieces, rows, chans = mine_ref.shape
-    core, unit = place_ref[4], place_ref[7]
+    core, _, _, unit = placed(group)
     for whose, ref in ((core, mine_ref), (1 - core, other_ref)):
         for step in range(pieces):
             index = whose * pieces + jnp.bitwise_xor(jnp.bitwise_and(unit, pieces - 1), step)
@@ -110,8 +100,7 @@
             temporal_ref[0, tap - count] = turned
 
 
-def place_kernels(place_ref, w_ref, own_ref, mine_refs, other_refs):
-    core, section = place_ref[4], place_ref[5]
+def place_kernels(core, section, w_ref, own_ref, mine_refs, other_refs):
     w_ref[core, section] = own_ref[0]
     w_ref[1 - core, section] = own_ref[1]
     for step, (mine_ref, other_ref) in enumerate(zip(mine_refs, other_refs)):
@@ -120,21 +109,23 @@
         w_ref[1 - core, block] = other_ref[...]
 
 
-def forward_kernel(geometry, place_ref, *rest):
-    blocks, cores, group, frames_in, rows_in, halo, tile, width = geometry
+def forward_kernel(geometry, *rest):
+    blocks, cores, group, frames_in, rows_in, halo, tile, width, height, columns = geometry
+    core, section, band, unit = placed(group)
+    odd = band % 2
     shared, rest = rest[: 2 * blocks - 1], rest[2 * blocks - 1 :]
     arrived, rest = rest[:6], rest[6:]
     xo_ref, ho_ref = rest[:2]
     d_refs = rest[2 : 2 + blocks]
     x_ref, h_ref, mask_ref, w_ref, start_ref = rest[2 + blocks :]
-    place_kernels(place_ref, w_ref, shared[0], shared[1:blocks], shared[blocks:])
+    place_kernels(core, section, w_ref, shared[0], shared[1:blocks], shared[blocks:])
     frames = cores * frames_in
     high = tile + 2 * halo
     chans = w_ref.shape[-1]
     own_rows, own_cols = (halo, halo + tile), (halo, width - halo)
-    height, columns = place_ref[2], place_ref[3]
-    row = place_ref[0] + lax.broadcasted_iota(jnp.int32, (high, width, chans), 0)
-    col = place_ref[1] + lax.broadcasted_iota(jnp.int32, (high, width, chans), 1)
+    row = band * tile - halo + lax.broadcasted_iota(jnp.int32, (high, width, chans), 0)
+    left = (unit * cores + core) * (width - 2 * halo) - halo
+    col = left + lax.broadcasted_iota(jnp.int32, (high, width, chans), 1)
     inside = (row >= 0) & (row < height) & (col >= 0) & (col < columns)
     mask_ref[...] = jnp.where(inside, 1.0, 0.0).astype(F32)
 
@@ -152,7 +143,6 @@
         ]
         xo_ref[block, frame] = jnp.concatenate(cut, 2)
 
-    core, odd, unit = place_ref[4], place_ref[6], place_ref[7]
     near = tile + halo - odd * (tile + halo)
     columns_at = pl.ds(pl.multiple_of(core * (width - 2 * halo), 16), width)
     for index, ref in enumerate(arrived):
@@ -210,15 +200,16 @@
             keep(block + 1, frame, new.astype(BF16).astype(F32), first)
 
 
-def backward_kernel(geometry, factor, place_ref, *rest):
-    blocks, cores, group, frames_in, rows_in, halo, tile, width = geometry
+def backward_kernel(geometry, factor, *rest):
+    blocks, cores, group, frames_in, rows_in, halo, tile, width, height, columns = geometry
+    core, section, band, unit = placed(group)
     shared, rest = rest[: 2 * blocks - 1], rest[2 * blocks - 1 :]
-    arrived, rest = rest[:3], rest[3:]
+    arrived, rest = rest[:group], rest[group:]
     xo_ref, ho_ref = rest[:2]
     d_refs = rest[2 : 2 + blocks]
     keep_ref, give_ref, mine_out, other_out = rest[2 + blocks : 6 + blocks]
     g_ref, da_ref, dao_ref, go_ref, w_ref, grad_ref, out_ref = rest[6 + blocks :]
-    place_kernels(place_ref, w_ref, shared[0], shared[1:blocks], shared[blocks:])
+    place_kernels(core, section, w_ref, shared[0], shared[1:blocks], shared[blocks:])
     frames = cores * frames_in
     chans = w_ref.shape[-1]
     rim = blocks
@@ -226,17 +217,16 @@
     per_core = w_ref.shape[2]
     pixels = tile * (own_cols[1] - own_cols[0])
 
-    core, odd, unit = place_ref[4], place_ref[6], place_ref[7]
-    near = tile + rim - odd * (tile + rim)
-    for base, ref in zip((rim, near, tile + rim - near), arrived):
-        count = ref.shape[0]
-        for step in range(count):
-            row = base + jnp.bitwise_and(jnp.bitwise_xor(unit, step), count - 1) * rows_in
-            g_ref[:, pl.ds(row, rows_in)] = ref[step]
+    half = group // 2
+    for step, ref in enumerate(arrived):
+        at = jnp.bitwise_xor(unit, step)
+        g_ref[:, pl.ds(rim + at * rows_in, rows_in)] = ref[0]
+        beyond = jnp.where(at < half, rim + tile + at * rows_in, (at - half) * rows_in)
+        g_ref[:, pl.ds(beyond, rows_in)] = ref[1]
 
     def put(block, tap, value):
-        slot = jnp.where(place_ref[4] == tap // per_core, 0, 1)
-        where = jnp.bitwise_xor(place_ref[5], block)
+        slot = jnp.where(core == tap // per_core, 0, 1)
+        where = jnp.bitwise_xor(section, block)
         grad_ref[slot, where, tap % per_core] = (value * factor).astype(BF16)
 
     for block in reversed(range(blocks)):
@@ -318,13 +308,10 @@
     width = own_width + 2 * halo
     span = cores * own_width + 2 * halo
     vmem = pl.BlockSpec(memory_space=pltpu.VMEM)
-    smem = pl.BlockSpec(memory_space=pltpu.SMEM)
     params = pltpu.CompilerParams(vmem_limit_bytes=32 * 2**20)
 
     bands = blocks * tiles // group
-    place = lax.axis_index("space")
-    band = (lax.axis_index("section") * tiles + place) // group
-    odd = band % 2
+    core, section, band, unit = placed(group)
 
     def traded(value, shift):
         pairs = []
@@ -334,35 +321,40 @@
                 pairs += [(one * group + i, other * group + i) for i in range(group)]
         return lax.ppermute(value, ("section", "space"), pairs)
 
-    core, section = lax.axis_index("tm"), lax.axis_index("section")
-    unit = place % group
     total_rows = blocks * tiles * rows_in
-    corner = jnp.stack(
-        [
-            band * tile - halo, (unit * cores + core) * own_width - halo, total_rows, columns,
-            core, section, odd, unit,
-        ]
-    ).astype(jnp.int32)
-
-    hbm = pl.BlockSpec(memory_space=pltpu.HBM)
-    taps = (spatial_weights.shape[1] + temporal_weights.shape[1]) // cores
+    half = group // 2
+    passed = []
+    for one in range(bands - 1):
+        for i in range(group):
+            low, high = one * group + i, (one + 1) * group + i
+            passed.append((high, low) if i < half else (low, high))
+    cot_halo = lax.ppermute(cotangent, ("section", "space"), passed)
+
+    padded = columns + 2 * halo
+    cuts = pl.pallas_call(
+        functools.partial(window_kernel, halo, span),
+        name="windows",
+        in_specs=[vmem],
+        out_specs=[vmem] * group,
+        out_shape=[jax.ShapeDtypeStruct((frames_in, rows_in, span, chans), BF16)] * group,
+        scratch_shapes=[pltpu.VMEM((frames_in, rows_in, padded, chans), F32)],
+        compiler_params=params,
+    )(video)
+    *cuts, spatial, temporal = lax.optimization_barrier(
+        list(cuts) + [spatial_weights, temporal_weights]
+    )
+    count = spatial_weights.shape[1]
+    taps = (count + temporal_weights.shape[1]) // cores
     one_half = jax.ShapeDtypeStruct((taps, chans, chans), BF16)
-    padded = columns + 2 * halo
-    cot_other = swapped(cotangent)
-    half_kernels, rest_kernels, *cuts = pl.pallas_call(
-        functools.partial(opening_kernel, halo, span),
-        name="opening",
-        in_specs=[smem] + [hbm] * 3,
-        out_specs=[vmem] * (2 + group),
-        out_shape=[one_half] * 2
-        + [jax.ShapeDtypeStruct((frames_in, rows_in, span, chans), BF16)] * group,
-        scratch_shapes=[
-            pltpu.VMEM(video.shape, BF16),
-            pltpu.VMEM((frames_in, rows_in, padded, chans), F32),
-            pltpu.SemaphoreType.DMA((4,)),
-        ],
-        compiler_params=pltpu.CompilerParams(vmem_limit_bytes=60 * 2**20),
-    )(corner, video, spatial_weights, temporal_weights)
+    half_kernels, own_kernels = pl.pallas_call(
+        halves_kernel,
+        name="halves",
+        in_specs=[vmem] * 2,
+        out_specs=[vmem] * 2,
+        out_shape=[one_half, jax.ShapeDtypeStruct((cores,) + one_half.shape, BF16)],
+        scratch_shapes=[pltpu.VMEM((cores * taps, chans, chans), BF16)],
+        compiler_params=params,
+    )(spatial, temporal)
 
     def gathered(pieces):
         return jnp.stack([pieces[0]] + [swapped(pieces[i], "space", i) for i in range(1, group)])
@@ -373,30 +365,23 @@
     near, far = traded(own_video, 0), traded(own_video, 1)
     mine = [along_x, along_y, swapped(along_x, "section", 2)]
     shared = mine + [swapped(each) for each in mine]
-    own_kernels = jnp.stack([half_kernels, rest_kernels])
+    shared = [own_kernels] + shared
 
     cuts = pl.pallas_call(
         functools.partial(cotangent_kernel, halo, width),
         name="cotangent",
-        in_specs=[smem] + [vmem] * 2,
+        in_specs=[vmem] * 4,
         out_specs=[vmem] * group,
-        out_shape=[jax.ShapeDtypeStruct((cores * frames_in, rows_in, width, chans), BF16)] * group,
-        scratch_shapes=[pltpu.VMEM((cores * frames_in, rows_in, padded, chans), F32)],
+        out_shape=[jax.ShapeDtypeStruct((2, cores * frames_in, rows_in, width, chans), BF16)] * group,
+        scratch_shapes=[pltpu.VMEM((2, cores * frames_in, rows_in, padded, chans), F32)],
         compiler_params=params,
-    )(corner, cotangent, cot_other)
-    near, own_kernels, *cuts = lax.optimization_barrier([near, own_kernels] + list(cuts))
-    shared = [own_kernels] + shared
+    )(cotangent, swapped(cotangent), cot_halo, swapped(cot_halo))
+    near, *cuts = lax.optimization_barrier([near] + list(cuts))
     videos = [own_video, near, far]
     videos += [swapped(each) for each in videos]
-    own_cot = gathered(cuts)
-    half = group // 2
-    upper = unit // half
-    cots = [own_cot] + [
-        traded(lax.dynamic_slice_in_dim(own_cot, (upper ^ side) * half, half, 0), shift)
-        for shift, side in ((0, 1 - odd), (1, odd))
-    ]
-
-    geometry = (blocks, cores, group, frames_in, rows_in, halo, tile, width)
+    cots = [cuts[0]] + [swapped(cuts[i], "space", i) for i in range(1, group)]
+
+    geometry = (blocks, cores, group, frames_in, rows_in, halo, tile, width, total_rows, columns)
     frames = cores * frames_in
     high = tile + 2 * halo
     per_section = (blocks,) + one_half.shape
@@ -409,7 +394,7 @@
     features, hidden, *slopes = pl.pallas_call(
         functools.partial(forward_kernel, geometry),
         name="forward",
-        in_specs=[smem] + [vmem] * (2 * blocks + 5),
+        in_specs=[vmem] * (2 * blocks + 5),
         out_specs=[vmem] * (2 + blocks),
         out_shape=[
             jax.ShapeDtypeStruct((blocks, frames, tile + 2, own_width, 3 * chans), BF16),
@@ -425,7 +410,7 @@
         ],
         compiler_params=params,
         cost_estimate=cost,
-    )(corner, *shared, *videos)
+    )(*shared, *videos)
 
     back = jax.ShapeDtypeStruct((group, frames_in, rows_in, own_width, chans), BF16)
     pixel_count = frames * total_rows * columns
@@ -433,7 +418,7 @@
     keep, give, mine_grad, other_grad = pl.pallas_call(
         functools.partial(backward_kernel, geometry, factor),
         name="backward",
-        in_specs=[smem] + [vmem] * (3 * blocks + 4),
+        in_specs=[vmem] * (3 * blocks + group + 1),
         out_specs=[vmem] * 4,
         out_shape=[
             jax.ShapeDtypeStruct(per_section, BF16),
@@ -452,12 +437,20 @@
         ],
         compiler_params=params,
         cost_estimate=cost,
-    )(corner, *shared, *cots, features, hidden, *slopes)
+    )(*shared, *cots, features, hidden, *slopes)
 
     got = swapped(give)
     parts = [(keep[i].astype(F32) + got[i].astype(F32)).astype(BF16) for i in range(blocks)]
     other_grad, *parts = lax.optimization_barrier([other_grad] + parts)
     parts = parts[:1] + [swapped(parts[i], "section", i) for i in range(1, blocks)]
+    other_grad = swapped(other_grad)
+    first = core == 0
+    wide = jnp.concatenate(
+        [jnp.where(first, mine_grad, other_grad), jnp.where(first, other_grad, mine_grad)], 3
+    )
+    strips = [wide[0]] + [swapped(wide[i], "space", i) for i in range(1, group)]
+    received = lax.optimization_barrier(parts + strips)
+    parts, strips = received[:blocks], received[blocks:]
     part = sum(each.astype(F32) for each in parts).astype(BF16)
 
     halves = part.reshape(2, -1, chans)
@@ -475,9 +468,9 @@
     part = part.astype(BF16)
     pair = jnp.stack([part, swapped(part, "space", 1)])
     spatial_out, temporal_out = pl.pallas_call(
-        closing_kernel,
+        functools.partial(closing_kernel, group),
         name="closing",
-        in_specs=[smem] + [vmem] * 2,
+        in_specs=[vmem] * 2,
         out_specs=[vmem] * 2,
         out_shape=[
             jax.ShapeDtypeStruct(spatial_weights.shape, F32),
@@ -485,14 +478,8 @@
         ],
         scratch_shapes=[pltpu.VMEM((cores * taps * chans, chans), BF16)],
         compiler_params=params,
-    )(corner, pair, swapped(pair))
-
-    other_grad = swapped(other_grad)
-    first = core == 0
-    wide = jnp.concatenate(
-        [jnp.where(first, mine_grad, other_grad), jnp.where(first, other_grad, mine_grad)], 3
-    )
-    strips = [wide[0]] + [swapped(wide[i], "space", i) for i in range(1, group)]
+    )(pair, swapped(pair))
+
     grad_video = jnp.zeros(video.shape, BF16)
     for step, strip in enumerate(strips):
         grad_video = lax.dynamic_update_slice(

time: 91.5 us -> 83.1 us (0.908)
  waiting for transfers between devices: 33.7 us -> 26.4 us
  Pallas kernels: 19.9 us -> 15.4 us
  starting transfers between devices: 31.9 us -> 36 us
  other arithmetic: 2.36 us -> 0.48 us
  local copies, waits for them, and re-layouts: 2.35 us -> 3.75 us
    ppermute x28 -> x29, waiting for transfers between devices: 33.6 us -> 23.8 us  [swapped(): return lax.ppermute(value, axis, [(i, i ^ step) for i in range(count)])]
    ppermute x28 -> x29, starting transfers between devices: 25.8 us -> 33.5 us  [swapped(): return lax.ppermute(value, axis, [(i, i ^ step) for i in range(count)])]
    ppermute x4 -> x2, starting transfers between devices: 6.13 us -> 1.26 us  [traded(): return lax.ppermute(value, ('section', 'space'), pairs)]
    pallas_call x2 -> x3, Pallas kernels: 4.27 us -> 1.21 us  [the longest x1 1.08 us: on_device(): pl.pallas_call(functools.partial(closing_kernel, group), name='closing',...]
    unnamed x8 -> x10, local copies, waits for them, and re-layouts: 1.57 us -> 3.66 us
    ppermute x4 -> x2, waiting for transfers between devices: 0.13 us -> 1.87 us  [traded(): return lax.ppermute(value, ('section', 'space'), pairs)]
    ppermute x0 -> x1, starting transfers between devices: none -> 1.28 us  [on_device(): cot_halo = lax.ppermute(cotangent, ('section', 'space'), passed)]
    another operation x1 -> x0, other arithmetic: 1.06 us -> none  [on_device(): own_kernels = jnp.stack([half_kernels, rest_kernels])]
  transfers between devices with their start and end apart: 32 -> 32, of which waited for: 11 -> 14; matrix products, arithmetic and copies ran while one was open for 2% -> 0% of each run, Pallas kernels for 10% -> 9%
where the time goes in v7:
time: 83.1 us; the launch traced here: 82.8 us
  starting transfers between devices  36 us (43%)
  waiting for transfers between devices  26.4 us (32%)
  Pallas kernels  15.4 us (19%)
  local copies, waits for them, and re-layouts  3.75 us (5%)
  between operations  0.84 us (1%)
    ppermute x29, starting transfers between devices, swapped(): return lax.ppermute(value, axis, [(i, i ^ step) for i in range(count)])  33.5 us
    ppermute x29, waiting for transfers between devices, swapped(): return lax.ppermute(value, axis, [(i, i ^ step) for i in range(count)])  23.8 us
    pallas_call x1, Pallas kernels, on_device(): pl.pallas_call(functools.partial(forward_kernel, geometry), name='forward...  7.7 us
    pallas_call x1, Pallas kernels, on_device(): pl.pallas_call(functools.partial(backward_kernel, geometry, factor), name...  6.31 us
    unnamed x10, local copies, waits for them, and re-layouts  3.66 us
    ppermute x2, waiting for transfers between devices, traded(): return lax.ppermute(value, ('section', 'space'), pairs)  1.87 us
  transfers between devices with their start and end apart: 32, of which 14 were waited for; matrix products, arithmetic and copies ran while one was open for 0% of the time, Pallas kernels for 9%

profile of v7, /device:TPU:0, one launch (start us, length us, event | category | flops | bytes accessed | tf_op | source)
XLA Modules:
  0.0 82.8 jit_solution(12085760326062595270)
XLA Ops:
  3.5 3.0 %collective-permute-start.3 = (bf16[6,128,128]{2,1,0:T(8,128)(2,1)S(1)}, bf16[6,128,128]{2,1,0:T(8,128)(2,1)S(1)}, u32[]{:S(2)}, u32[]{:S(2)}) collective-permute-start(bf16[6,128,128]{2,1,0:T(8,128)(2,1)S(1)} %get-tuple-element.63), channel_id=1, source_target_pairs={{0,8},{8,0},{16,24},{24,16},{1,9},{9,1},{17,25},{25,17},{2,10},{10... | collective-permute-start | bytes 589832 | tf_op jit(solution)/shard_map/ppermute | solution.py:297
  6.5 1.5 %collective-permute-start.4 = (bf16[6,128,128]{2,1,0:T(8,128)(2,1)S(1)}, bf16[6,128,128]{2,1,0:T(8,128)(2,1)S(1)}, u32[]{:S(2)}, u32[]{:S(2)}) collective-permute-start(bf16[6,128,128]{2,1,0:T(8,128)(2,1)S(1)} %get-tuple-element.63), channel_id=1, source_target_pairs={{0,16},{8,24},{16,0},{24,8},{1,17},{9,25},{17,1},{25,9},{2,18},{10... | collective-permute-start | bytes 589832 | tf_op jit(solution)/shard_map/ppermute | solution.py:297
  8.1 1.6 %collective-permute-start = (bf16[2,2,48,128]{3,2,1,0:T(8,128)(2,1)S(1)}, bf16[2,2,48,128]{3,2,1,0:T(8,128)(2,1)S(1)}, u32[]{:S(2)}, u32[]{:S(2)}) collective-permute-start(bf16[2,2,48,128]{3,2,1,0:T(8,128)(2,1)S(1)} %get-tuple-element.60), channel_id=1, source_target_pairs={{0,1},{1,0},{2,3},{3,2},{4,5},{5,4},{6,7},{7,6},{8,9},{9,8},{10,11... | collective-permute-start | bytes 147464 | tf_op jit(solution)/shard_map/ppermute | solution.py:297
  9.6 2.6 %collective-permute-start.1 = (bf16[2,2,48,128]{3,2,1,0:T(8,128)(2,1)S(1)}, bf16[2,2,48,128]{3,2,1,0:T(8,128)(2,1)S(1)}, u32[]{:S(2)}, u32[]{:S(2)}) collective-permute-start(bf16[2,2,48,128]{3,2,1,0:T(8,128)(2,1)S(1)} %get-tuple-element.61), channel_id=1, source_target_pairs={{0,2},{1,3},{2,0},{3,1},{4,6},{5,7},{6,4},{7,5},{8,10},{9,11},{10,... | collective-permute-start | bytes 147464 | tf_op jit(solution)/shard_map/ppermute | solution.py:297
  13.7 1.4 %collective-permute-done.1 = bf16[2,2,48,128]{3,2,1,0:T(8,128)(2,1)S(1)} collective-permute-done((bf16[2,2,48,128]{3,2,1,0:T(8,128)(2,1)S(1)}, bf16[2,2,48,128]{3,2,1,0:T(8,128)(2,1)S(1)}, u32[]{:S(2)}, u32[]{:S(2)}) %collective-permute-start.1) | collective-permute-done | bytes 49184 | tf_op jit(solution)/shard_map/ppermute | solution.py:297
  15.2 3.0 %collective-permute-done.2 = bf16[2,2,48,128]{3,2,1,0:T(8,128)(2,1)S(1)} collective-permute-done((bf16[2,2,48,128]{3,2,1,0:T(8,128)(2,1)S(1)}, bf16[2,2,48,128]{3,2,1,0:T(8,128)(2,1)S(1)}, u32[]{:S(2)}, u32[]{:S(2)}) %collective-permute-start.2) | collective-permute-done | bytes 49184 | tf_op jit(solution)/shard_map/ppermute | solution.py:297
  23.5 1.9 %collective-permute-done.9.rest_8_ = bf16[4,2,2,48,128]{4,3,2,1,0:T(8,128)(2,1)S(1)} collective-permute-done((bf16[4,2,2,48,128]{4,3,2,1,0:T(8,128)(2,1)S(1)}, bf16[4,2,2,48,128]{4,3,2,1,0:T(8,128)(2,1)S(1)}, u32[]{:S(2)}, u32[]{:S(2)}) %collective-permute-start.9) | collective-permute-done | bytes 196640 | tf_op jit(solution)/shard_map/ppermute | solution.py:322
  26.9 3.2 %collective-permute-start.14 = (bf16[2,4,2,32,128]{4,3,2,1,0:T(8,128)(2,1)S(1)}, bf16[2,4,2,32,128]{4,3,2,1,0:T(8,128)(2,1)S(1)}, u32[]{:S(2)}, u32[]{:S(2)}) collective-permute-start(bf16[2,4,2,32,128]{4,3,2,1,0:T(8,128)(2,1)S(1)} %get-tuple-element.73), channel_id=1, source_target_pairs={{0,2},{1,3},{2,0},{3,1},{4,6},{5,7},{6,4},{7,5},{8,10},{9,11},{10,... | collective-permute-start | bytes 393224 | tf_op jit(solution)/shard_map/ppermute | solution.py:297
  30.8 7.7 %forward.1 = (bf16[4,4,10,16,384]{4,3,2,1,0:T(8,128)(2,1)S(1)}, bf16[4,4,8,16,128]{4,3,2,1,0:T(8,128)(2,1)S(1)}, f32[4,10,32,128]{3,2,1,0:T(8,128)S(1)}, f32[4,1...) custom-call(bf16[2,6,128,128]{3,2,1,0:T(8,128)(2,1)S(1)} %get-tuple-element.58.rest_0_, ...), custom_call_target="tpu_custom_call" | custom-call | flops 6000000000 | bytes 8000000 | tf_op jit(solution)/shard_map/forward/pallas_call | solution.py:394
  38.5 1.5 %collective-permute-done.14.rest_9_ = bf16[2,4,2,32,128]{4,3,2,1,0:T(8,128)(2,1)S(1)} collective-permute-done((bf16[2,4,2,32,128]{4,3,2,1,0:T(8,128)(2,1)S(1)}, bf16[2,4,2,32,128]{4,3,2,1,0:T(8,128)(2,1)S(1)}, u32[]{:S(2)}, u32[]{:S(2)}) %collective-permute-start.14) | collective-permute-done | bytes 131104 | tf_op jit(solution)/shard_map/ppermute | solution.py:297
  40.1 6.3 %backward.1 = (bf16[4,6,128,128]{3,2,1,0:T(8,128)(2,1)S(1)}, bf16[4,6,128,128]{3,2,1,0:T(8,128)(2,1)S(1)}, bf16[4,2,2,16,128]{4,3,2,1,0:T(8,128)(2,1)S(1)}, bf16[4,2,2,16,128]{4,3,2,1,0:T(8,128)(2,1)S(1)}) custom-call(bf16[2,6,128,128]{3,2,1,0:T(8,128)(2,1)S(1)} %get-tuple-element.58.rest_0_, bf16[6,128,128]{2,1,0:T(8,128)(2,1)S(1)} %collective-permute-done.3.rest_1_, ...), custom_call_target="tpu_custom_call" | custom-call | flops 6000000000 | bytes 8000000 | tf_op jit(solution)/shard_map/backward/pallas_call | solution.py:418
  46.5 2.3 %collective-permute-done.20 = bf16[4,6,128,128]{3,2,1,0:T(8,128)(2,1)S(1)} collective-permute-done((bf16[4,6,128,128]{3,2,1,0:T(8,128)(2,1)S(1)}, bf16[4,6,128,128]{3,2,1,0:T(8,128)(2,1)S(1)}, u32[]{:S(2)}, u32[]{:S(2)}) %collective-permute-start.20) | collective-permute-done | bytes 786464 | tf_op jit(solution)/shard_map/ppermute | solution.py:297
  49.2 4.1 %collective-permute-start.21 = (bf16[6,128,128]{2,1,0:T(8,128)(2,1)S(1)}, bf16[6,128,128]{2,1,0:T(8,128)(2,1)S(1)}, u32[]{:S(2)}, u32[]{:S(2)}) collective-permute-start(bf16[6,128,128]{2,1,0:T(8,128)(2,1)S(1)} %get-tuple-element.86), channel_id=1, source_target_pairs={{0,8},{8,0},{16,24},{24,16},{1,9},{9,1},{17,25},{25,17},{2,10},{10... | collective-permute-start | bytes 589832 | tf_op jit(solution)/shard_map/ppermute | solution.py:297
  53.3 1.5 %collective-permute-start.23 = (bf16[6,128,128]{2,1,0:T(8,128)(2,1)S(1)}, bf16[6,128,128]{2,1,0:T(8,128)(2,1)S(1)}, u32[]{:S(2)}, u32[]{:S(2)}) collective-permute-start(bf16[6,128,128]{2,1,0:T(8,128)(2,1)S(1)} %get-tuple-element.88), channel_id=1, source_target_pairs={{0,24},{8,16},{16,8},{24,0},{1,25},{9,17},{17,9},{25,1},{2,26},{10... | collective-permute-start | bytes 589832 | tf_op jit(solution)/shard_map/ppermute | solution.py:297
  54.8 2.5 %collective-permute-start.25 = (bf16[2,2,32,128]{3,2,1,0:T(8,128)(2,1)S(1)}, bf16[2,2,32,128]{3,2,1,0:T(8,128)(2,1)S(1)}, u32[]{:S(2)}, u32[]{:S(2)}) collective-permute-start(bf16[2,2,32,128]{3,2,1,0:T(8,128)(2,1)S(1)} %get-tuple-element.107), channel_id=1, source_target_pairs={{0,1},{1,0},{2,3},{3,2},{4,5},{5,4},{6,7},{7,6},{8,9},{9,8},{10,11... | collective-permute-start | bytes 98312 | tf_op jit(solution)/shard_map/ppermute | solution.py:297
  59.2 2.4 %collective-permute-start.27 = (bf16[2,2,32,128]{3,2,1,0:T(8,128)(2,1)S(1)}, bf16[2,2,32,128]{3,2,1,0:T(8,128)(2,1)S(1)}, u32[]{:S(2)}, u32[]{:S(2)}) collective-permute-start(bf16[2,2,32,128]{3,2,1,0:T(8,128)(2,1)S(1)} %get-tuple-element.105), channel_id=1, source_target_pairs={{0,3},{1,2},{2,1},{3,0},{4,7},{5,6},{6,5},{7,4},{8,11},{9,10},{10,... | collective-permute-start | bytes 98312 | tf_op jit(solution)/shard_map/ppermute | solution.py:297
  62.3 2.7 %collective-permute-done.27 = bf16[2,2,32,128]{3,2,1,0:T(8,128)(2,1)S(1)} collective-permute-done((bf16[2,2,32,128]{3,2,1,0:T(8,128)(2,1)S(1)}, bf16[2,2,32,128]{3,2,1,0:T(8,128)(2,1)S(1)}, u32[]{:S(2)}, u32[]{:S(2)}) %collective-permute-start.27) | collective-permute-done | bytes 32800 | tf_op jit(solution)/shard_map/ppermute | solution.py:297
  65.2 1.9 %collective-permute-start.28 = (bf16[384,128]{1,0:T(8,128)(2,1)S(1)}, bf16[384,128]{1,0:T(8,128)(2,1)S(1)}, u32[]{:S(2)}, u32[]{:S(2)}) collective-permute-start(bf16[384,128]{1,0:T(8,128)(2,1)S(1)} %dynamic-slice_bitcast_fusion), channel_id=1, source_target_pairs={{0,1},{1,0},{2,3},{3,2},{4,5},{5,4},{6,7},{7,6},{8,9},{9,8},{10,11... | collective-permute-start | bytes 294920 | tf_op jit(solution)/shard_map/ppermute | solution.py:297
  67.0 2.8 %collective-permute-done.28 = bf16[384,128]{1,0:T(8,128)(2,1)S(1)} collective-permute-done((bf16[384,128]{1,0:T(8,128)(2,1)S(1)}, bf16[384,128]{1,0:T(8,128)(2,1)S(1)}, u32[]{:S(2)}, u32[]{:S(2)}) %collective-permute-start.28) | collective-permute-done | bytes 98336 | tf_op jit(solution)/shard_map/ppermute | solution.py:297
  69.9 2.5 %collective-permute-start.29 = (bf16[384,128]{1,0:T(8,128)(2,1)S(1)}, bf16[384,128]{1,0:T(8,128)(2,1)S(1)}, u32[]{:S(2)}, u32[]{:S(2)}) collective-permute-start(bf16[384,128]{1,0:T(8,128)(2,1)S(1)} %fusion.4), channel_id=1, source_target_pairs={{0,2},{1,3},{2,0},{3,1},{4,6},{5,7},{6,4},{7,5},{8,10},{9,11},{10,... | collective-permute-start | bytes 294920 | tf_op jit(solution)/shard_map/ppermute | solution.py:297
  72.4 3.1 %collective-permute-done.29 = bf16[384,128]{1,0:T(8,128)(2,1)S(1)} collective-permute-done((bf16[384,128]{1,0:T(8,128)(2,1)S(1)}, bf16[384,128]{1,0:T(8,128)(2,1)S(1)}, u32[]{:S(2)}, u32[]{:S(2)}) %collective-permute-start.29) | collective-permute-done | bytes 98336 | tf_op jit(solution)/shard_map/ppermute | solution.py:297
  75.5 1.8 %collective-permute-start.30 = (bf16[384,128]{1,0:T(8,128)(2,1)S(1)}, bf16[384,128]{1,0:T(8,128)(2,1)S(1)}, u32[]{:S(2)}, u32[]{:S(2)}) collective-permute-start(bf16[384,128]{1,0:T(8,128)(2,1)S(1)} %add_convert_fusion.5), channel_id=1, source_target_pairs={{0,1},{1,0},{2,3},{3,2},{4,5},{5,4},{6,7},{7,6},{8,9},{9,8},{10,11... | collective-permute-start | bytes 294920 | tf_op jit(solution)/shard_map/ppermute | solution.py:297
  77.4 2.8 %collective-permute-done.30 = bf16[384,128]{1,0:T(8,128)(2,1)S(1)} collective-permute-done((bf16[384,128]{1,0:T(8,128)(2,1)S(1)}, bf16[384,128]{1,0:T(8,128)(2,1)S(1)}, u32[]{:S(2)}, u32[]{:S(2)}) %collective-permute-start.30) | collective-permute-done | bytes 98336 | tf_op jit(solution)/shard_map/ppermute | solution.py:297
  80.4 1.4 %collective-permute-done.31.other_ref = bf16[2,384,128]{2,1,0:T(8,128)(2,1)S(1)} collective-permute-done((bf16[2,384,128]{2,1,0:T(8,128)(2,1)S(1)}, bf16[2,384,128]{2,1,0:T(8,128)(2,1)S(1)}, u32[]{:S(2)}, u32[]{:S(2)}) %collective-permute-start.31) | collective-permute-done | bytes 196640 | tf_op jit(solution)/shard_map/ppermute | solution.py:297
  (70 shorter events, 16.7 us)
Async XLA Ops:
  3.5 14.6 %collective-permute-start.3 = (bf16[6,128,128]{2,1,0:T(8,128)(2,1)S(1)}, bf16[6,128,128]{2,1,0:T(8,128)(2,1)S(1)}, u32[]{:S(2)}, u32[]{:S(2)}) collective-permute-start(bf16[6,128,128]{2,1,0:T(8,128)(2,1)S(1)} %get-tuple-element.63), channel_id=1, source_target_pairs={{0,8},{8,0},{16,24},{24,16},{1,9},{9,1},{17,25},{25,17},{2,10},{10... | collective-permute-start | bytes 589832 | tf_op jit(solution)/shard_map/ppermute | solution.py:297
  6.5 11.6 %collective-permute-start.4 = (bf16[6,128,128]{2,1,0:T(8,128)(2,1)S(1)}, bf16[6,128,128]{2,1,0:T(8,128)(2,1)S(1)}, u32[]{:S(2)}, u32[]{:S(2)}) collective-permute-start(bf16[6,128,128]{2,1,0:T(8,128)(2,1)S(1)} %get-tuple-element.63), channel_id=1, source_target_pairs={{0,16},{8,24},{16,0},{24,8},{1,17},{9,25},{17,1},{25,9},{2,18},{10... | collective-permute-start | bytes 589832 | tf_op jit(solution)/shard_map/ppermute | solution.py:297
  9.6 5.5 %collective-permute-start.1 = (bf16[2,2,48,128]{3,2,1,0:T(8,128)(2,1)S(1)}, bf16[2,2,48,128]{3,2,1,0:T(8,128)(2,1)S(1)}, u32[]{:S(2)}, u32[]{:S(2)}) collective-permute-start(bf16[2,2,48,128]{3,2,1,0:T(8,128)(2,1)S(1)} %get-tuple-element.61), channel_id=1, source_target_pairs={{0,2},{1,3},{2,0},{3,1},{4,6},{5,7},{6,4},{7,5},{8,10},{9,11},{10,... | collective-permute-start | bytes 147464 | tf_op jit(solution)/shard_map/ppermute | solution.py:297
  12.2 5.9 %collective-permute-start.2 = (bf16[2,2,48,128]{3,2,1,0:T(8,128)(2,1)S(1)}, bf16[2,2,48,128]{3,2,1,0:T(8,128)(2,1)S(1)}, u32[]{:S(2)}, u32[]{:S(2)}) collective-permute-start(bf16[2,2,48,128]{3,2,1,0:T(8,128)(2,1)S(1)} %get-tuple-element.62), channel_id=1, source_target_pairs={{0,3},{1,2},{2,1},{3,0},{4,7},{5,6},{6,5},{7,4},{8,11},{9,10},{10,... | collective-permute-start | bytes 147464 | tf_op jit(solution)/shard_map/ppermute | solution.py:297
  12.4 8.2 %collective-permute-start.11 = (bf16[2,2,128,128]{3,2,1,0:T(8,128)(2,1)}, bf16[2,2,128,128]{3,2,1,0:T(8,128)(2,1)S(1)}, u32[]{:S(2)}, u32[]{:S(2)}) collective-permute-start(bf16[2,2,128,128]{3,2,1,0:T(8,128)(2,1)} %rest_0_.1), channel_id=1, source_target_pairs={{8,0},{9,1},{2,10},{3,11},{16,8},{17,9},{10,18},{11,19},{24,16},{2... | collective-permute-start | bytes 393224 | tf_op jit(solution)/shard_map/ppermute | solution.py:331
  15.1 5.5 %collective-permute-start.10 = (bf16[2,2,128,128]{3,2,1,0:T(8,128)(2,1)}, bf16[2,2,128,128]{3,2,1,0:T(8,128)(2,1)S(1)}, u32[]{:S(2)}, u32[]{:S(2)}) collective-permute-start(bf16[2,2,128,128]{3,2,1,0:T(8,128)(2,1)} %rest_0_.1), channel_id=1, source_target_pairs={{0,4},{4,0},{1,5},{5,1},{2,6},{6,2},{3,7},{7,3},{8,12},{12,8},{9,1... | collective-permute-start | bytes 393224 | tf_op jit(solution)/shard_map/ppermute | solution.py:297
  18.2 7.2 %collective-permute-start.9 = (bf16[4,2,2,48,128]{4,3,2,1,0:T(8,128)(2,1)S(1)}, bf16[4,2,2,48,128]{4,3,2,1,0:T(8,128)(2,1)S(1)}, u32[]{:S(2)}, u32[]{:S(2)}) collective-permute-start(bf16[4,2,2,48,128]{4,3,2,1,0:T(8,128)(2,1)S(1)} %pad_maximum_fusion.rest_7_), channel_id=1, source_target_pairs={{0,8},{1,9},{2,10},{3,11},{8,0},{9,1},{10,2},{11,3},{16,24},{17,25... | collective-permute-start | bytes 589832 | tf_op jit(solution)/shard_map/ppermute | solution.py:322
  18.8 6.6 %collective-permute-start.5 = (bf16[6,128,128]{2,1,0:T(8,128)(2,1)S(1)}, bf16[6,128,128]{2,1,0:T(8,128)(2,1)S(1)}, u32[]{:S(2)}, u32[]{:S(2)}) collective-permute-start(bf16[6,128,128]{2,1,0:T(8,128)(2,1)S(1)} %collective-permute-done.3.rest_1_), channel_id=1, source_target_pairs={{0,16},{8,24},{16,0},{24,8},{1,17},{9,25},{17,1},{25,9},{2,18},{10... | collective-permute-start | bytes 589832 | tf_op jit(solution)/shard_map/ppermute | solution.py:297
  19.3 6.6 %collective-permute-start.16 = (bf16[4,2,2,48,128]{4,3,2,1,0:T(8,128)(2,1)S(1)}, bf16[4,2,2,48,128]{4,3,2,1,0:T(8,128)(2,1)S(1)}, u32[]{:S(2)}, u32[]{:S(2)}) collective-permute-start(bf16[4,2,2,48,128]{4,3,2,1,0:T(8,128)(2,1)S(1)} %pad_maximum_fusion.rest_7_), channel_id=1, source_target_pairs={{8,16},{9,17},{10,18},{11,19},{16,8},{17,9},{18,10},{19,11},{12,20... | collective-permute-start | bytes 589832 | tf_op jit(solution)/shard_map/ppermute | solution.py:322
  20.6 5.4 %collective-permute-start.6 = (bf16[6,128,128]{2,1,0:T(8,128)(2,1)S(1)}, bf16[6,128,128]{2,1,0:T(8,128)(2,1)S(1)}, u32[]{:S(2)}, u32[]{:S(2)}) collective-permute-start(bf16[6,128,128]{2,1,0:T(8,128)(2,1)S(1)} %collective-permute-done.3.rest_1_), channel_id=1, source_target_pairs={{0,4},{4,0},{1,5},{5,1},{2,6},{6,2},{3,7},{7,3},{8,12},{12,8},{9,1... | collective-permute-start | bytes 589832 | tf_op jit(solution)/shard_map/ppermute | solution.py:297
  25.4 4.7 %collective-permute-start.18 = (bf16[4,2,2,48,128]{4,3,2,1,0:T(8,128)(2,1)S(1)}, bf16[4,2,2,48,128]{4,3,2,1,0:T(8,128)(2,1)S(1)}, u32[]{:S(2)}, u32[]{:S(2)}) collective-permute-start(bf16[4,2,2,48,128]{4,3,2,1,0:T(8,128)(2,1)S(1)} %collective-permute-done.9.rest_8_), channel_id=1, source_target_pairs={{0,4},{4,0},{1,5},{5,1},{2,6},{6,2},{3,7},{7,3},{8,12},{12,8},{9,1... | collective-permute-start | bytes 589832 | tf_op jit(solution)/shard_map/ppermute | solution.py:297
  25.9 4.9 %collective-permute-start.8 = (bf16[6,128,128]{2,1,0:T(8,128)(2,1)S(1)}, bf16[6,128,128]{2,1,0:T(8,128)(2,1)S(1)}, u32[]{:S(2)}, u32[]{:S(2)}) collective-permute-start(bf16[6,128,128]{2,1,0:T(8,128)(2,1)S(1)} %collective-permute-done.5.rest_3_), channel_id=1, source_target_pairs={{0,4},{4,0},{1,5},{5,1},{2,6},{6,2},{3,7},{7,3},{8,12},{12,8},{9,1... | collective-permute-start | bytes 589832 | tf_op jit(solution)/shard_map/ppermute | solution.py:297
  26.0 4.8 %collective-permute-start.19 = (bf16[4,2,2,48,128]{4,3,2,1,0:T(8,128)(2,1)S(1)}, bf16[4,2,2,48,128]{4,3,2,1,0:T(8,128)(2,1)S(1)}, u32[]{:S(2)}, u32[]{:S(2)}) collective-permute-start(bf16[4,2,2,48,128]{4,3,2,1,0:T(8,128)(2,1)S(1)} %collective-permute-done.16.rest_9_), channel_id=1, source_target_pairs={{0,4},{4,0},{1,5},{5,1},{2,6},{6,2},{3,7},{7,3},{8,12},{12,8},{9,1... | collective-permute-start | bytes 589832 | tf_op jit(solution)/shard_map/ppermute | solution.py:297
  26.4 12.1 %collective-permute-start.13 = (bf16[2,4,2,32,128]{4,3,2,1,0:T(8,128)(2,1)S(1)}, bf16[2,4,2,32,128]{4,3,2,1,0:T(8,128)(2,1)S(1)}, u32[]{:S(2)}, u32[]{:S(2)}) collective-permute-start(bf16[2,4,2,32,128]{4,3,2,1,0:T(8,128)(2,1)S(1)} %get-tuple-element.72), channel_id=1, source_target_pairs={{0,1},{1,0},{2,3},{3,2},{4,5},{5,4},{6,7},{7,6},{8,9},{9,8},{10,11... | collective-permute-start | bytes 393224 | tf_op jit(solution)/shard_map/ppermute | solution.py:297
  26.9 13.2 %collective-permute-start.14 = (bf16[2,4,2,32,128]{4,3,2,1,0:T(8,128)(2,1)S(1)}, bf16[2,4,2,32,128]{4,3,2,1,0:T(8,128)(2,1)S(1)}, u32[]{:S(2)}, u32[]{:S(2)}) collective-permute-start(bf16[2,4,2,32,128]{4,3,2,1,0:T(8,128)(2,1)S(1)} %get-tuple-element.73), channel_id=1, source_target_pairs={{0,2},{1,3},{2,0},{3,1},{4,6},{5,7},{6,4},{7,5},{8,10},{9,11},{10,... | collective-permute-start | bytes 393224 | tf_op jit(solution)/shard_map/ppermute | solution.py:297
  30.1 10.0 %collective-permute-start.15 = (bf16[2,4,2,32,128]{4,3,2,1,0:T(8,128)(2,1)S(1)}, bf16[2,4,2,32,128]{4,3,2,1,0:T(8,128)(2,1)S(1)}, u32[]{:S(2)}, u32[]{:S(2)}) collective-permute-start(bf16[2,4,2,32,128]{4,3,2,1,0:T(8,128)(2,1)S(1)} %get-tuple-element.74), channel_id=1, source_target_pairs={{0,3},{1,2},{2,1},{3,0},{4,7},{5,6},{6,5},{7,4},{8,11},{9,10},{10,... | collective-permute-start | bytes 393224 | tf_op jit(solution)/shard_map/ppermute | solution.py:297
  49.0 5.8 %collective-permute-start.24 = (bf16[4,2,2,16,128]{4,3,2,1,0:T(8,128)(2,1)S(1)}, bf16[4,2,2,16,128]{4,3,2,1,0:T(8,128)(2,1)S(1)}, u32[]{:S(2)}, u32[]{:S(2)}) collective-permute-start(bf16[4,2,2,16,128]{4,3,2,1,0:T(8,128)(2,1)S(1)} %get-tuple-element.90), channel_id=1, source_target_pairs={{0,4},{4,0},{1,5},{5,1},{2,6},{6,2},{3,7},{7,3},{8,12},{12,8},{9,1... | collective-permute-start | bytes 196616 | tf_op jit(solution)/shard_map/ppermute | solution.py:297
  49.2 15.8 %collective-permute-start.21 = (bf16[6,128,128]{2,1,0:T(8,128)(2,1)S(1)}, bf16[6,128,128]{2,1,0:T(8,128)(2,1)S(1)}, u32[]{:S(2)}, u32[]{:S(2)}) collective-permute-start(bf16[6,128,128]{2,1,0:T(8,128)(2,1)S(1)} %get-tuple-element.86), channel_id=1, source_target_pairs={{0,8},{8,0},{16,24},{24,16},{1,9},{9,1},{17,25},{25,17},{2,10},{10... | collective-permute-start | bytes 589832 | tf_op jit(solution)/shard_map/ppermute | solution.py:297
  53.3 11.7 %collective-permute-start.22 = (bf16[6,128,128]{2,1,0:T(8,128)(2,1)S(1)}, bf16[6,128,128]{2,1,0:T(8,128)(2,1)S(1)}, u32[]{:S(2)}, u32[]{:S(2)}) collective-permute-start(bf16[6,128,128]{2,1,0:T(8,128)(2,1)S(1)} %get-tuple-element.87), channel_id=1, source_target_pairs={{0,16},{8,24},{16,0},{24,8},{1,17},{9,25},{17,1},{25,9},{2,18},{10... | collective-permute-start | bytes 589832 | tf_op jit(solution)/shard_map/ppermute | solution.py:297
  53.3 11.7 %collective-permute-start.23 = (bf16[6,128,128]{2,1,0:T(8,128)(2,1)S(1)}, bf16[6,128,128]{2,1,0:T(8,128)(2,1)S(1)}, u32[]{:S(2)}, u32[]{:S(2)}) collective-permute-start(bf16[6,128,128]{2,1,0:T(8,128)(2,1)S(1)} %get-tuple-element.88), channel_id=1, source_target_pairs={{0,24},{8,16},{16,8},{24,0},{1,25},{9,17},{17,9},{25,1},{2,26},{10... | collective-permute-start | bytes 589832 | tf_op jit(solution)/shard_map/ppermute | solution.py:297
  57.3 5.0 %collective-permute-start.26 = (bf16[2,2,32,128]{3,2,1,0:T(8,128)(2,1)S(1)}, bf16[2,2,32,128]{3,2,1,0:T(8,128)(2,1)S(1)}, u32[]{:S(2)}, u32[]{:S(2)}) collective-permute-start(bf16[2,2,32,128]{3,2,1,0:T(8,128)(2,1)S(1)} %get-tuple-element.108), channel_id=1, source_target_pairs={{0,2},{1,3},{2,0},{3,1},{4,6},{5,7},{6,4},{7,5},{8,10},{9,11},{10,... | collective-permute-start | bytes 98312 | tf_op jit(solution)/shard_map/ppermute | solution.py:297
  59.2 5.8 %collective-permute-start.27 = (bf16[2,2,32,128]{3,2,1,0:T(8,128)(2,1)S(1)}, bf16[2,2,32,128]{3,2,1,0:T(8,128)(2,1)S(1)}, u32[]{:S(2)}, u32[]{:S(2)}) collective-permute-start(bf16[2,2,32,128]{3,2,1,0:T(8,128)(2,1)S(1)} %get-tuple-element.105), channel_id=1, source_target_pairs={{0,3},{1,2},{2,1},{3,0},{4,7},{5,6},{6,5},{7,4},{8,11},{9,10},{10,... | collective-permute-start | bytes 98312 | tf_op jit(solution)/shard_map/ppermute | solution.py:297
  65.2 4.7 %collective-permute-start.28 = (bf16[384,128]{1,0:T(8,128)(2,1)S(1)}, bf16[384,128]{1,0:T(8,128)(2,1)S(1)}, u32[]{:S(2)}, u32[]{:S(2)}) collective-permute-start(bf16[384,128]{1,0:T(8,128)(2,1)S(1)} %dynamic-slice_bitcast_fusion), channel_id=1, source_target_pairs={{0,1},{1,0},{2,3},{3,2},{4,5},{5,4},{6,7},{7,6},{8,9},{9,8},{10,11... | collective-permute-start | bytes 294920 | tf_op jit(solution)/shard_map/ppermute | solution.py:297
  69.9 5.6 %collective-permute-start.29 = (bf16[384,128]{1,0:T(8,128)(2,1)S(1)}, bf16[384,128]{1,0:T(8,128)(2,1)S(1)}, u32[]{:S(2)}, u32[]{:S(2)}) collective-permute-start(bf16[384,128]{1,0:T(8,128)(2,1)S(1)} %fusion.4), channel_id=1, source_target_pairs={{0,2},{1,3},{2,0},{3,1},{4,6},{5,7},{6,4},{7,5},{8,10},{9,11},{10,... | collective-permute-start | bytes 294920 | tf_op jit(solution)/shard_map/ppermute | solution.py:297
  (13 other events, 30.8 us)

commit v8 on v7

--- a/solution.py
+++ b/solution.py
@@ -42,17 +42,21 @@
     return lax.axis_index("tm"), section, band, place % group
 
 
-def window_kernel(halo, span, video_ref, *rest):
-    targets, wide_ref = rest[:-1], rest[-1]
-    unit = placed(len(targets))[3]
-    frames, rows, columns, chans = video_ref.shape
-    edge = jnp.zeros((frames, rows, halo, chans), F32)
-    wide_ref[:, :, :halo] = edge
-    wide_ref[:, :, halo + columns :] = edge
-    wide_ref[:, :, halo : halo + columns] = video_ref[...].astype(F32)
+def window_kernel(halo, width, *rest):
+    (mine_ref, other_ref), targets, wide_ref = rest[:2], rest[2:-1], rest[-1]
+    core, _, _, unit = placed(len(targets))
+    lead, frames_in, rows, columns, chans = mine_ref.shape
+    edge = jnp.zeros((lead, 2 * frames_in, rows, halo, chans), F32)
+    wide_ref[:, :, :, :halo] = edge
+    wide_ref[:, :, :, halo + columns :] = edge
+    for whose, ref in ((core, mine_ref), (1 - core, other_ref)):
+        wide_ref[:, pl.ds(whose * frames_in, frames_in), :, halo : halo + columns] = ref[
+            ...
+        ].astype(F32)
+    own = width - 2 * halo
     for step, target in enumerate(targets):
-        at = jnp.bitwise_xor(unit, step) * (span - 2 * halo)
-        target[...] = wide_ref[:, :, pl.ds(pl.multiple_of(at, 16), span)].astype(BF16)
+        at = (jnp.bitwise_xor(unit, step) * 2 + core) * own
+        target[...] = wide_ref[:, :, :, pl.ds(pl.multiple_of(at, 16), width)].astype(BF16)
 
 
 def halves_kernel(spatial_ref, temporal_ref, half_ref, both_ref, all_ref):
@@ -64,24 +68,6 @@
     half_ref[...] = all_ref[pl.ds(core * taps, taps)]
     both_ref[0] = all_ref[pl.ds(core * taps, taps)]
     both_ref[1] = all_ref[pl.ds((1 - core) * taps, taps)]
-
-
-def cotangent_kernel(halo, width, *rest):
-    sources, targets, wide_ref = rest[:4], rest[4:-1], rest[-1]
-    core, _, _, unit = placed(len(targets))
-    frames_in, rows, columns, chans = sources[0].shape
-    edge = jnp.zeros((2, 2 * frames_in, rows, halo, chans), F32)
-    wide_ref[:, :, :, :halo] = edge
-    wide_ref[:, :, :, halo + columns :] = edge
-    for index, ref in enumerate(sources):
-        whose = core if index % 2 == 0 else 1 - core
-        wide_ref[index // 2, pl.ds(whose * frames_in, frames_in), :, halo : halo + columns] = ref[
-            ...
-        ].astype(F32)
-    own = width - 2 * halo
-    for step, target in enumerate(targets):
-        at = (jnp.bitwise_xor(unit, step) * 2 + core) * own
-        target[...] = wide_ref[:, :, :, pl.ds(pl.multiple_of(at, 16), width)].astype(BF16)
 
 
 def closing_kernel(group, mine_ref, other_ref, spatial_ref, temporal_ref, flat_ref):
@@ -100,25 +86,25 @@
             temporal_ref[0, tap - count] = turned
 
 
-def place_kernels(core, section, w_ref, own_ref, mine_refs, other_refs):
+def place_kernels(core, section, w_ref, own_ref, x_mine, x_other, y_mine, y_other):
     w_ref[core, section] = own_ref[0]
     w_ref[1 - core, section] = own_ref[1]
-    for step, (mine_ref, other_ref) in enumerate(zip(mine_refs, other_refs)):
-        block = jnp.bitwise_xor(section, step + 1)
-        w_ref[core, block] = mine_ref[...]
-        w_ref[1 - core, block] = other_ref[...]
+    for half, x_ref, y_ref in ((core, x_mine, y_mine), (1 - core, x_other, y_other)):
+        w_ref[half, jnp.bitwise_xor(section, 1)] = x_ref[...]
+        for step in range(2):
+            w_ref[half, jnp.bitwise_xor(section, 2 + step)] = y_ref[step]
 
 
 def forward_kernel(geometry, *rest):
     blocks, cores, group, frames_in, rows_in, halo, tile, width, height, columns = geometry
     core, section, band, unit = placed(group)
     odd = band % 2
-    shared, rest = rest[: 2 * blocks - 1], rest[2 * blocks - 1 :]
-    arrived, rest = rest[:6], rest[6:]
+    shared, rest = rest[:5], rest[5:]
+    arrived, rest = rest[:3], rest[3:]
     xo_ref, ho_ref = rest[:2]
     d_refs = rest[2 : 2 + blocks]
     x_ref, h_ref, mask_ref, w_ref, start_ref = rest[2 + blocks :]
-    place_kernels(core, section, w_ref, shared[0], shared[1:blocks], shared[blocks:])
+    place_kernels(core, section, w_ref, *shared)
     frames = cores * frames_in
     high = tile + 2 * halo
     chans = w_ref.shape[-1]
@@ -144,15 +130,10 @@
         xo_ref[block, frame] = jnp.concatenate(cut, 2)
 
     near = tile + halo - odd * (tile + halo)
-    columns_at = pl.ds(pl.multiple_of(core * (width - 2 * halo), 16), width)
-    for index, ref in enumerate(arrived):
-        base = (halo, near, tile + halo - near)[index % 3]
-        whose = core if index < 3 else 1 - core
+    for base, ref in zip((halo, near, tile + halo - near), arrived):
         for step in range(group):
             row = base + jnp.bitwise_xor(unit, step) * rows_in
-            start_ref[pl.ds(whose * frames_in, frames_in), pl.ds(row, rows_in)] = ref[
-                step, :, :, columns_at, :
-            ]
+            start_ref[:, pl.ds(row, rows_in)] = ref[step]
     for frame in range(frames):
         keep(0, frame, start_ref[frame].reshape(high * width, chans).astype(F32), 0)
 
@@ -203,13 +184,13 @@
 def backward_kernel(geometry, factor, *rest):
     blocks, cores, group, frames_in, rows_in, halo, tile, width, height, columns = geometry
     core, section, band, unit = placed(group)
-    shared, rest = rest[: 2 * blocks - 1], rest[2 * blocks - 1 :]
+    shared, rest = rest[:5], rest[5:]
     arrived, rest = rest[:group], rest[group:]
     xo_ref, ho_ref = rest[:2]
     d_refs = rest[2 : 2 + blocks]
     keep_ref, give_ref, mine_out, other_out = rest[2 + blocks : 6 + blocks]
     g_ref, da_ref, dao_ref, go_ref, w_ref, grad_ref, out_ref = rest[6 + blocks :]
-    place_kernels(core, section, w_ref, shared[0], shared[1:blocks], shared[blocks:])
+    place_kernels(core, section, w_ref, *shared)
     frames = cores * frames_in
     chans = w_ref.shape[-1]
     rim = blocks
@@ -306,7 +287,6 @@
     parties = cores * group
     own_width = columns // parties
     width = own_width + 2 * halo
-    span = cores * own_width + 2 * halo
     vmem = pl.BlockSpec(memory_space=pltpu.VMEM)
     params = pltpu.CompilerParams(vmem_limit_bytes=32 * 2**20)
 
@@ -330,19 +310,24 @@
             passed.append((high, low) if i < half else (low, high))
     cot_halo = lax.ppermute(cotangent, ("section", "space"), passed)
 
-    padded = columns + 2 * halo
-    cuts = pl.pallas_call(
-        functools.partial(window_kernel, halo, span),
-        name="windows",
-        in_specs=[vmem],
-        out_specs=[vmem] * group,
-        out_shape=[jax.ShapeDtypeStruct((frames_in, rows_in, span, chans), BF16)] * group,
-        scratch_shapes=[pltpu.VMEM((frames_in, rows_in, padded, chans), F32)],
-        compiler_params=params,
-    )(video)
-    *cuts, spatial, temporal = lax.optimization_barrier(
-        list(cuts) + [spatial_weights, temporal_weights]
-    )
+    frames = cores * frames_in
+
+    def windows(name, mine, other):
+        lead = mine.shape[0]
+        one = (lead, frames, rows_in, width, chans)
+        return pl.pallas_call(
+            functools.partial(window_kernel, halo, width),
+            name=name,
+            in_specs=[vmem] * 2,
+            out_specs=[vmem] * group,
+            out_shape=[jax.ShapeDtypeStruct(one, BF16)] * group,
+            scratch_shapes=[
+                pltpu.VMEM((lead, frames, rows_in, columns + 2 * halo, chans), F32)
+            ],
+            compiler_params=params,
+        )(mine, other)
+
+    cuts = windows("video_windows", video[None], swapped(video)[None])
     count = spatial_weights.shape[1]
     taps = (count + temporal_weights.shape[1]) // cores
     one_half = jax.ShapeDtypeStruct((taps, chans, chans), BF16)
@@ -354,35 +339,26 @@
         out_shape=[one_half, jax.ShapeDtypeStruct((cores,) + one_half.shape, BF16)],
         scratch_shapes=[pltpu.VMEM((cores * taps, chans, chans), BF16)],
         compiler_params=params,
-    )(spatial, temporal)
+    )(spatial_weights, temporal_weights)
 
     def gathered(pieces):
         return jnp.stack([pieces[0]] + [swapped(pieces[i], "space", i) for i in range(1, group)])
 
     along_x = swapped(half_kernels, "section", 1)
-    along_y = swapped(half_kernels, "section", 2)
-    own_video, along_x, along_y = lax.optimization_barrier([gathered(cuts), along_x, along_y])
+    own_video, along_x, cot_halo = lax.optimization_barrier(
+        [gathered([cut[0] for cut in cuts]), along_x, cot_halo]
+    )
     near, far = traded(own_video, 0), traded(own_video, 1)
-    mine = [along_x, along_y, swapped(along_x, "section", 2)]
-    shared = mine + [swapped(each) for each in mine]
-    shared = [own_kernels] + shared
-
-    cuts = pl.pallas_call(
-        functools.partial(cotangent_kernel, halo, width),
-        name="cotangent",
-        in_specs=[vmem] * 4,
-        out_specs=[vmem] * group,
-        out_shape=[jax.ShapeDtypeStruct((2, cores * frames_in, rows_in, width, chans), BF16)] * group,
-        scratch_shapes=[pltpu.VMEM((2, cores * frames_in, rows_in, padded, chans), F32)],
-        compiler_params=params,
-    )(cotangent, swapped(cotangent), cot_halo, swapped(cot_halo))
-    near, *cuts = lax.optimization_barrier([near] + list(cuts))
+    along_y = swapped(jnp.stack([half_kernels, along_x]), "section", 2)
+
+    both = jnp.stack([cotangent, cot_halo])
+    cuts = windows("cotangent_windows", both, swapped(both))
+    near, along_y, *cuts = lax.optimization_barrier([near, along_y] + list(cuts))
+    shared = [own_kernels, along_x, swapped(along_x), along_y, swapped(along_y)]
     videos = [own_video, near, far]
-    videos += [swapped(each) for each in videos]
     cots = [cuts[0]] + [swapped(cuts[i], "space", i) for i in range(1, group)]
 
     geometry = (blocks, cores, group, frames_in, rows_in, halo, tile, width, total_rows, columns)
-    frames = cores * frames_in
     high = tile + 2 * halo
     per_section = (blocks,) + one_half.shape
     all_kernels = (cores,) + per_section
@@ -394,7 +370,7 @@
     features, hidden, *slopes = pl.pallas_call(
         functools.partial(forward_kernel, geometry),
         name="forward",
-        in_specs=[vmem] * (2 * blocks + 5),
+        in_specs=[vmem] * 8,
         out_specs=[vmem] * (2 + blocks),
         out_shape=[
             jax.ShapeDtypeStruct((blocks, frames, tile + 2, own_width, 3 * chans), BF16),
@@ -418,7 +394,7 @@
     keep, give, mine_grad, other_grad = pl.pallas_call(
         functools.partial(backward_kernel, geometry, factor),
         name="backward",
-        in_specs=[vmem] * (3 * blocks + group + 1),
+        in_specs=[vmem] * (blocks + group + 7),
         out_specs=[vmem] * 4,
         out_shape=[
             jax.ShapeDtypeStruct(per_section, BF16),

time: 83.1 us -> 88.7 us (1.067)
  waiting for transfers between devices: 26.4 us -> 34.4 us
  starting transfers between devices: 36 us -> 34.6 us
  local copies, waits for them, and re-layouts: 3.75 us -> 2.86 us
    ppermute x2, waiting for transfers between devices: 1.87 us -> 7.07 us  [traded(): return lax.ppermute(value, ('section', 'space'), pairs)]
    ppermute x29 -> x24, waiting for transfers between devices: 23.8 us -> 26.3 us  [swapped(): return lax.ppermute(value, axis, [(i, i ^ step) for i in range(count)])]
    ppermute x29 -> x24, starting transfers between devices: 33.5 us -> 32.5 us  [swapped(): return lax.ppermute(value, axis, [(i, i ^ step) for i in range(count)])]
    unnamed x10, local copies, waits for them, and re-layouts: 3.66 us -> 2.77 us
  transfers between devices with their start and end apart: 32 -> 27, of which waited for: 14 -> 12; matrix products, arithmetic and copies ran while one was open for 0% -> 0% of each run, Pallas kernels for 9% -> 9%
where the time goes in v8:
time: 88.7 us; the launch traced here: 88.4 us
  starting transfers between devices  34.6 us (39%)
  waiting for transfers between devices  34.4 us (39%)
  Pallas kernels  15.2 us (17%)
  local copies, waits for them, and re-layouts  2.86 us (3%)
    ppermute x24, starting transfers between devices, swapped(): return lax.ppermute(value, axis, [(i, i ^ step) for i in range(count)])  32.5 us
    ppermute x24, waiting for transfers between devices, swapped(): return lax.ppermute(value, axis, [(i, i ^ step) for i in range(count)])  26.3 us
    pallas_call x1, Pallas kernels, on_device(): pl.pallas_call(functools.partial(forward_kernel, geometry), name='forward...  7.7 us
    ppermute x2, waiting for transfers between devices, traded(): return lax.ppermute(value, ('section', 'space'), pairs)  7.07 us
    pallas_call x1, Pallas kernels, on_device(): pl.pallas_call(functools.partial(backward_kernel, geometry, factor), name...  6.12 us
    unnamed x10, local copies, waits for them, and re-layouts  2.77 us
  transfers between devices with their start and end apart: 27, of which 12 were waited for; matrix products, arithmetic and copies ran while one was open for 0% of the time, Pallas kernels for 9%

profile of v8, /device:TPU:0, one launch (start us, length us, event | category | flops | bytes accessed | tf_op | source)
XLA Modules:
  0.0 88.4 jit_solution(15885759193733668793)
XLA Ops:
  3.1 2.6 %collective-permute-start.4 = (bf16[6,128,128]{2,1,0:T(8,128)(2,1)S(1)}, bf16[6,128,128]{2,1,0:T(8,128)(2,1)S(1)}, u32[]{:S(2)}, u32[]{:S(2)}) collective-permute-start(bf16[6,128,128]{2,1,0:T(8,128)(2,1)S(1)} %get-tuple-element.52), channel_id=1, source_target_pairs={{0,8},{8,0},{16,24},{24,16},{1,9},{9,1},{17,25},{25,17},{2,10},{10... | collective-permute-start | bytes 589832 | tf_op jit(solution)/shard_map/ppermute | solution.py:278
  6.7 1.6 %collective-permute-start.1 = (bf16[4,2,32,128]{3,2,1,0:T(8,128)(2,1)S(1)}, bf16[4,2,32,128]{3,2,1,0:T(8,128)(2,1)S(1)}, u32[]{:S(2)}, u32[]{:S(2)}) collective-permute-start(bf16[4,2,32,128]{3,2,1,0:T(8,128)(2,1)S(1)} %bitcast.42), channel_id=1, source_target_pairs={{0,1},{1,0},{2,3},{3,2},{4,5},{5,4},{6,7},{7,6},{8,9},{9,8},{10,11... | collective-permute-start | bytes 196616 | tf_op jit(solution)/shard_map/ppermute | solution.py:278
  8.3 2.6 %collective-permute-start.2 = (bf16[4,2,32,128]{3,2,1,0:T(8,128)(2,1)S(1)}, bf16[4,2,32,128]{3,2,1,0:T(8,128)(2,1)S(1)}, u32[]{:S(2)}, u32[]{:S(2)}) collective-permute-start(bf16[4,2,32,128]{3,2,1,0:T(8,128)(2,1)S(1)} %bitcast.41), channel_id=1, source_target_pairs={{0,2},{1,3},{2,0},{3,1},{4,6},{5,7},{6,4},{7,5},{8,10},{9,11},{10,... | collective-permute-start | bytes 196616 | tf_op jit(solution)/shard_map/ppermute | solution.py:278
  11.1 1.3 %collective-permute-start.5 = (bf16[2,2,128,128]{3,2,1,0:T(8,128)(2,1)}, bf16[2,2,128,128]{3,2,1,0:T(8,128)(2,1)S(1)}, u32[]{:S(2)}, u32[]{:S(2)}) collective-permute-start(bf16[2,2,128,128]{3,2,1,0:T(8,128)(2,1)} %param.5), channel_id=1, source_target_pairs={{8,0},{9,1},{2,10},{3,11},{16,8},{17,9},{10,18},{11,19},{24,16},{2... | collective-permute-start | bytes 393224 | tf_op jit(solution)/shard_map/ppermute | solution.py:311
  12.4 3.5 %collective-permute-done.2 = bf16[4,2,32,128]{3,2,1,0:T(8,128)(2,1)S(1)} collective-permute-done((bf16[4,2,32,128]{3,2,1,0:T(8,128)(2,1)S(1)}, bf16[4,2,32,128]{3,2,1,0:T(8,128)(2,1)S(1)}, u32[]{:S(2)}, u32[]{:S(2)}) %collective-permute-start.2) | collective-permute-done | bytes 65568 | tf_op jit(solution)/shard_map/ppermute | solution.py:278
  18.2 1.6 %collective-permute-start.8 = (bf16[2,6,128,128]{3,2,1,0:T(8,128)(2,1)S(1)}, bf16[2,6,128,128]{3,2,1,0:T(8,128)(2,1)S(1)}, u32[]{:S(2)}, u32[]{:S(2)}) collective-permute-start(bf16[2,6,128,128]{3,2,1,0:T(8,128)(2,1)S(1)} %pad_maximum_fusion), channel_id=1, source_target_pairs={{0,16},{8,24},{16,0},{24,8},{1,17},{9,25},{17,1},{25,9},{2,18},{10... | collective-permute-start | bytes 1179656 | tf_op jit(solution)/shard_map/ppermute | solution.py:278
  20.0 1.4 %collective-permute-done.9.rest_1_ = bf16[2,2,2,128,128]{4,3,2,1,0:T(8,128)(2,1)S(1)} collective-permute-done((bf16[2,2,2,128,128]{4,3,2,1,0:T(8,128)(2,1)S(1)}, bf16[2,2,2,128,128]{4,3,2,1,0:T(8,128)(2,1)S(1)}, u32[]{:S(2)}, u32[]{:S(2)}) %collective-permute-start.9) | collective-permute-done | bytes 262176 | tf_op jit(solution)/shard_map/ppermute | solution.py:278
  21.6 7.1 %collective-permute-done.7.rest_6_ = bf16[4,4,2,32,128]{4,3,2,1,0:T(8,128)(2,1)S(1)} collective-permute-done((bf16[4,4,2,32,128]{4,3,2,1,0:T(8,128)(2,1)S(1)}, bf16[4,4,2,32,128]{4,3,2,1,0:T(8,128)(2,1)S(1)}, u32[]{:S(2)}, u32[]{:S(2)}) %collective-permute-start.7) | collective-permute-done | bytes 262176 | tf_op jit(solution)/shard_map/ppermute | solution.py:302
  30.6 4.4 %collective-permute-start.12 = (bf16[2,4,2,32,128]{4,3,2,1,0:T(8,128)(2,1)S(1)}, bf16[2,4,2,32,128]{4,3,2,1,0:T(8,128)(2,1)S(1)}, u32[]{:S(2)}, u32[]{:S(2)}) collective-permute-start(bf16[2,4,2,32,128]{4,3,2,1,0:T(8,128)(2,1)S(1)} %get-tuple-element.63), channel_id=1, source_target_pairs={{0,2},{1,3},{2,0},{3,1},{4,6},{5,7},{6,4},{7,5},{8,10},{9,11},{10,... | collective-permute-start | bytes 393224 | tf_op jit(solution)/shard_map/ppermute | solution.py:278
  35.5 7.7 %forward.1 = (bf16[4,4,10,16,384]{4,3,2,1,0:T(8,128)(2,1)S(1)}, bf16[4,4,8,16,128]{4,3,2,1,0:T(8,128)(2,1)S(1)}, f32[4,10,32,128]{3,2,1,0:T(8,128)S(1)}, f32[4,1...) custom-call(bf16[2,6,128,128]{3,2,1,0:T(8,128)(2,1)S(1)} %get-tuple-element.47.rest_0_, ...), custom_call_target="tpu_custom_call" | custom-call | flops 6000000000 | bytes 8000000 | tf_op jit(solution)/shard_map/forward/pallas_call | solution.py:370
  43.2 1.7 %collective-permute-done.12.rest_7_ = bf16[2,4,2,32,128]{4,3,2,1,0:T(8,128)(2,1)S(1)} collective-permute-done((bf16[2,4,2,32,128]{4,3,2,1,0:T(8,128)(2,1)S(1)}, bf16[2,4,2,32,128]{4,3,2,1,0:T(8,128)(2,1)S(1)}, u32[]{:S(2)}, u32[]{:S(2)}) %collective-permute-start.12) | collective-permute-done | bytes 131104 | tf_op jit(solution)/shard_map/ppermute | solution.py:278
  44.9 6.1 %backward.1 = (bf16[4,6,128,128]{3,2,1,0:T(8,128)(2,1)S(1)}, bf16[4,6,128,128]{3,2,1,0:T(8,128)(2,1)S(1)}, bf16[4,2,2,16,128]{4,3,2,1,0:T(8,128)(2,1)S(1)}, bf16[4,2,2,16,128]{4,3,2,1,0:T(8,128)(2,1)S(1)}) custom-call(bf16[2,6,128,128]{3,2,1,0:T(8,128)(2,1)S(1)} %get-tuple-element.47.rest_0_, bf16[6,128,128]{2,1,0:T(8,128)(2,1)S(1)} %collective-permute-done.4.rest_1_, ...), custom_call_target="tpu_custom_call" | custom-call | flops 6000000000 | bytes 8000000 | tf_op jit(solution)/shard_map/backward/pallas_call | solution.py:394
  51.1 2.3 %collective-permute-done.15 = bf16[4,6,128,128]{3,2,1,0:T(8,128)(2,1)S(1)} collective-permute-done((bf16[4,6,128,128]{3,2,1,0:T(8,128)(2,1)S(1)}, bf16[4,6,128,128]{3,2,1,0:T(8,128)(2,1)S(1)}, u32[]{:S(2)}, u32[]{:S(2)}) %collective-permute-start.15) | collective-permute-done | bytes 786464 | tf_op jit(solution)/shard_map/ppermute | solution.py:278
  53.8 3.7 %collective-permute-start.16 = (bf16[6,128,128]{2,1,0:T(8,128)(2,1)S(1)}, bf16[6,128,128]{2,1,0:T(8,128)(2,1)S(1)}, u32[]{:S(2)}, u32[]{:S(2)}) collective-permute-start(bf16[6,128,128]{2,1,0:T(8,128)(2,1)S(1)} %get-tuple-element.76), channel_id=1, source_target_pairs={{0,8},{8,0},{16,24},{24,16},{1,9},{9,1},{17,25},{25,17},{2,10},{10... | collective-permute-start | bytes 589832 | tf_op jit(solution)/shard_map/ppermute | solution.py:278
  57.6 1.5 %collective-permute-start.18 = (bf16[6,128,128]{2,1,0:T(8,128)(2,1)S(1)}, bf16[6,128,128]{2,1,0:T(8,128)(2,1)S(1)}, u32[]{:S(2)}, u32[]{:S(2)}) collective-permute-start(bf16[6,128,128]{2,1,0:T(8,128)(2,1)S(1)} %get-tuple-element.78), channel_id=1, source_target_pairs={{0,24},{8,16},{16,8},{24,0},{1,25},{9,17},{17,9},{25,1},{2,26},{10... | collective-permute-start | bytes 589832 | tf_op jit(solution)/shard_map/ppermute | solution.py:278
  59.1 1.9 %collective-permute-start.20 = (bf16[2,2,32,128]{3,2,1,0:T(8,128)(2,1)S(1)}, bf16[2,2,32,128]{3,2,1,0:T(8,128)(2,1)S(1)}, u32[]{:S(2)}, u32[]{:S(2)}) collective-permute-start(bf16[2,2,32,128]{3,2,1,0:T(8,128)(2,1)S(1)} %get-tuple-element.97), channel_id=1, source_target_pairs={{0,1},{1,0},{2,3},{3,2},{4,5},{5,4},{6,7},{7,6},{8,9},{9,8},{10,11... | collective-permute-start | bytes 98312 | tf_op jit(solution)/shard_map/ppermute | solution.py:278
  61.0 2.9 %collective-permute-start.21 = (bf16[2,2,32,128]{3,2,1,0:T(8,128)(2,1)S(1)}, bf16[2,2,32,128]{3,2,1,0:T(8,128)(2,1)S(1)}, u32[]{:S(2)}, u32[]{:S(2)}) collective-permute-start(bf16[2,2,32,128]{3,2,1,0:T(8,128)(2,1)S(1)} %get-tuple-element.98), channel_id=1, source_target_pairs={{0,2},{1,3},{2,0},{3,1},{4,6},{5,7},{6,4},{7,5},{8,10},{9,11},{10,... | collective-permute-start | bytes 98312 | tf_op jit(solution)/shard_map/ppermute | solution.py:278
  63.9 3.5 %collective-permute-start.22 = (bf16[2,2,32,128]{3,2,1,0:T(8,128)(2,1)S(1)}, bf16[2,2,32,128]{3,2,1,0:T(8,128)(2,1)S(1)}, u32[]{:S(2)}, u32[]{:S(2)}) collective-permute-start(bf16[2,2,32,128]{3,2,1,0:T(8,128)(2,1)S(1)} %get-tuple-element.95), channel_id=1, source_target_pairs={{0,3},{1,2},{2,1},{3,0},{4,7},{5,6},{6,5},{7,4},{8,11},{9,10},{10,... | collective-permute-start | bytes 98312 | tf_op jit(solution)/shard_map/ppermute | solution.py:278
  67.4 2.2 %collective-permute-done.22 = bf16[2,2,32,128]{3,2,1,0:T(8,128)(2,1)S(1)} collective-permute-done((bf16[2,2,32,128]{3,2,1,0:T(8,128)(2,1)S(1)}, bf16[2,2,32,128]{3,2,1,0:T(8,128)(2,1)S(1)}, u32[]{:S(2)}, u32[]{:S(2)}) %collective-permute-start.22) | collective-permute-done | bytes 32800 | tf_op jit(solution)/shard_map/ppermute | solution.py:278
  70.7 3.7 %collective-permute-done.23 = bf16[384,128]{1,0:T(8,128)(2,1)S(1)} collective-permute-done((bf16[384,128]{1,0:T(8,128)(2,1)S(1)}, bf16[384,128]{1,0:T(8,128)(2,1)S(1)}, u32[]{:S(2)}, u32[]{:S(2)}) %collective-permute-start.23) | collective-permute-done | bytes 98336 | tf_op jit(solution)/shard_map/ppermute | solution.py:278
  74.5 2.1 %collective-permute-start.24 = (bf16[384,128]{1,0:T(8,128)(2,1)S(1)}, bf16[384,128]{1,0:T(8,128)(2,1)S(1)}, u32[]{:S(2)}, u32[]{:S(2)}) collective-permute-start(bf16[384,128]{1,0:T(8,128)(2,1)S(1)} %fusion.4), channel_id=1, source_target_pairs={{0,2},{1,3},{2,0},{3,1},{4,6},{5,7},{6,4},{7,5},{8,10},{9,11},{10,... | collective-permute-start | bytes 294920 | tf_op jit(solution)/shard_map/ppermute | solution.py:278
  76.6 4.5 %collective-permute-done.24 = bf16[384,128]{1,0:T(8,128)(2,1)S(1)} collective-permute-done((bf16[384,128]{1,0:T(8,128)(2,1)S(1)}, bf16[384,128]{1,0:T(8,128)(2,1)S(1)}, u32[]{:S(2)}, u32[]{:S(2)}) %collective-permute-start.24) | collective-permute-done | bytes 98336 | tf_op jit(solution)/shard_map/ppermute | solution.py:278
  81.4 4.4 %collective-permute-done.25 = bf16[384,128]{1,0:T(8,128)(2,1)S(1)} collective-permute-done((bf16[384,128]{1,0:T(8,128)(2,1)S(1)}, bf16[384,128]{1,0:T(8,128)(2,1)S(1)}, u32[]{:S(2)}, u32[]{:S(2)}) %collective-permute-start.25) | collective-permute-done | bytes 98336 | tf_op jit(solution)/shard_map/ppermute | solution.py:278
  86.0 1.4 %collective-permute-done.26.other_ref = bf16[2,384,128]{2,1,0:T(8,128)(2,1)S(1)} collective-permute-done((bf16[2,384,128]{2,1,0:T(8,128)(2,1)S(1)}, bf16[2,384,128]{2,1,0:T(8,128)(2,1)S(1)}, u32[]{:S(2)}, u32[]{:S(2)}) %collective-permute-start.26) | collective-permute-done | bytes 196640 | tf_op jit(solution)/shard_map/ppermute | solution.py:278
  (62 shorter events, 12.0 us)
Async XLA Ops:
  0.6 5.0 %collective-permute-start = (bf16[2,2,128,128]{3,2,1,0:T(8,128)(2,1)}, bf16[2,2,128,128]{3,2,1,0:T(8,128)(2,1)S(1)}, u32[]{:S(2)}, u32[]{:S(2)}) collective-permute-start(bf16[2,2,128,128]{3,2,1,0:T(8,128)(2,1)} %param.4), channel_id=1, source_target_pairs={{0,4},{4,0},{1,5},{5,1},{2,6},{6,2},{3,7},{7,3},{8,12},{12,8},{9,1... | collective-permute-start | bytes 393224 | tf_op jit(solution)/shard_map/ppermute | solution.py:278
  3.1 15.1 %collective-permute-start.4 = (bf16[6,128,128]{2,1,0:T(8,128)(2,1)S(1)}, bf16[6,128,128]{2,1,0:T(8,128)(2,1)S(1)}, u32[]{:S(2)}, u32[]{:S(2)}) collective-permute-start(bf16[6,128,128]{2,1,0:T(8,128)(2,1)S(1)} %get-tuple-element.52), channel_id=1, source_target_pairs={{0,8},{8,0},{16,24},{24,16},{1,9},{9,1},{17,25},{25,17},{2,10},{10... | collective-permute-start | bytes 589832 | tf_op jit(solution)/shard_map/ppermute | solution.py:278
  6.7 5.7 %collective-permute-start.1 = (bf16[4,2,32,128]{3,2,1,0:T(8,128)(2,1)S(1)}, bf16[4,2,32,128]{3,2,1,0:T(8,128)(2,1)S(1)}, u32[]{:S(2)}, u32[]{:S(2)}) collective-permute-start(bf16[4,2,32,128]{3,2,1,0:T(8,128)(2,1)S(1)} %bitcast.42), channel_id=1, source_target_pairs={{0,1},{1,0},{2,3},{3,2},{4,5},{5,4},{6,7},{7,6},{8,9},{9,8},{10,11... | collective-permute-start | bytes 196616 | tf_op jit(solution)/shard_map/ppermute | solution.py:278
  8.3 7.6 %collective-permute-start.2 = (bf16[4,2,32,128]{3,2,1,0:T(8,128)(2,1)S(1)}, bf16[4,2,32,128]{3,2,1,0:T(8,128)(2,1)S(1)}, u32[]{:S(2)}, u32[]{:S(2)}) collective-permute-start(bf16[4,2,32,128]{3,2,1,0:T(8,128)(2,1)S(1)} %bitcast.41), channel_id=1, source_target_pairs={{0,2},{1,3},{2,0},{3,1},{4,6},{5,7},{6,4},{7,5},{8,10},{9,11},{10,... | collective-permute-start | bytes 196616 | tf_op jit(solution)/shard_map/ppermute | solution.py:278
  10.9 6.2 %collective-permute-start.3 = (bf16[4,2,32,128]{3,2,1,0:T(8,128)(2,1)S(1)}, bf16[4,2,32,128]{3,2,1,0:T(8,128)(2,1)S(1)}, u32[]{:S(2)}, u32[]{:S(2)}) collective-permute-start(bf16[4,2,32,128]{3,2,1,0:T(8,128)(2,1)S(1)} %bitcast.40), channel_id=1, source_target_pairs={{0,3},{1,2},{2,1},{3,0},{4,7},{5,6},{6,5},{7,4},{8,11},{9,10},{10,... | collective-permute-start | bytes 196616 | tf_op jit(solution)/shard_map/ppermute | solution.py:278
  11.1 7.1 %collective-permute-start.5 = (bf16[2,2,128,128]{3,2,1,0:T(8,128)(2,1)}, bf16[2,2,128,128]{3,2,1,0:T(8,128)(2,1)S(1)}, u32[]{:S(2)}, u32[]{:S(2)}) collective-permute-start(bf16[2,2,128,128]{3,2,1,0:T(8,128)(2,1)} %param.5), channel_id=1, source_target_pairs={{8,0},{9,1},{2,10},{3,11},{16,8},{17,9},{10,18},{11,19},{24,16},{2... | collective-permute-start | bytes 393224 | tf_op jit(solution)/shard_map/ppermute | solution.py:311
  18.2 10.4 %collective-permute-start.8 = (bf16[2,6,128,128]{3,2,1,0:T(8,128)(2,1)S(1)}, bf16[2,6,128,128]{3,2,1,0:T(8,128)(2,1)S(1)}, u32[]{:S(2)}, u32[]{:S(2)}) collective-permute-start(bf16[2,6,128,128]{3,2,1,0:T(8,128)(2,1)S(1)} %pad_maximum_fusion), channel_id=1, source_target_pairs={{0,16},{8,24},{16,0},{24,8},{1,17},{9,25},{17,1},{25,9},{2,18},{10... | collective-permute-start | bytes 1179656 | tf_op jit(solution)/shard_map/ppermute | solution.py:278
  19.9 8.7 %collective-permute-start.7 = (bf16[4,4,2,32,128]{4,3,2,1,0:T(8,128)(2,1)S(1)}, bf16[4,4,2,32,128]{4,3,2,1,0:T(8,128)(2,1)S(1)}, u32[]{:S(2)}, u32[]{:S(2)}) collective-permute-start(bf16[4,4,2,32,128]{4,3,2,1,0:T(8,128)(2,1)S(1)} %pad_maximum_fusion.1.rest_5_), channel_id=1, source_target_pairs={{0,8},{1,9},{2,10},{3,11},{8,0},{9,1},{10,2},{11,3},{16,24},{17,25... | collective-permute-start | bytes 786440 | tf_op jit(solution)/shard_map/ppermute | solution.py:302
  28.6 6.8 %collective-permute-start.10 = (bf16[2,6,128,128]{3,2,1,0:T(8,128)(2,1)S(1)}, bf16[2,6,128,128]{3,2,1,0:T(8,128)(2,1)S(1)}, u32[]{:S(2)}, u32[]{:S(2)}) collective-permute-start(bf16[2,6,128,128]{3,2,1,0:T(8,128)(2,1)S(1)} %collective-permute-done.8.rest_3_), channel_id=1, source_target_pairs={{0,4},{4,0},{1,5},{5,1},{2,6},{6,2},{3,7},{7,3},{8,12},{12,8},{9,1... | collective-permute-start | bytes 1179656 | tf_op jit(solution)/shard_map/ppermute | solution.py:278
  28.6 6.8 %collective-permute-start.14 = (bf16[4,4,2,32,128]{4,3,2,1,0:T(8,128)(2,1)S(1)}, bf16[4,4,2,32,128]{4,3,2,1,0:T(8,128)(2,1)S(1)}, u32[]{:S(2)}, u32[]{:S(2)}) collective-permute-start(bf16[4,4,2,32,128]{4,3,2,1,0:T(8,128)(2,1)S(1)} %pad_maximum_fusion.1.rest_5_), channel_id=1, source_target_pairs={{8,16},{9,17},{10,18},{11,19},{16,8},{17,9},{18,10},{19,11},{12,20... | collective-permute-start | bytes 786440 | tf_op jit(solution)/shard_map/ppermute | solution.py:302
  29.3 5.6 %collective-permute-start.6 = (bf16[6,128,128]{2,1,0:T(8,128)(2,1)S(1)}, bf16[6,128,128]{2,1,0:T(8,128)(2,1)S(1)}, u32[]{:S(2)}, u32[]{:S(2)}) collective-permute-start(bf16[6,128,128]{2,1,0:T(8,128)(2,1)S(1)} %collective-permute-done.4.rest_1_), channel_id=1, source_target_pairs={{0,4},{4,0},{1,5},{5,1},{2,6},{6,2},{3,7},{7,3},{8,12},{12,8},{9,1... | collective-permute-start | bytes 589832 | tf_op jit(solution)/shard_map/ppermute | solution.py:278
  29.9 13.3 %collective-permute-start.11 = (bf16[2,4,2,32,128]{4,3,2,1,0:T(8,128)(2,1)S(1)}, bf16[2,4,2,32,128]{4,3,2,1,0:T(8,128)(2,1)S(1)}, u32[]{:S(2)}, u32[]{:S(2)}) collective-permute-start(bf16[2,4,2,32,128]{4,3,2,1,0:T(8,128)(2,1)S(1)} %get-tuple-element.62), channel_id=1, source_target_pairs={{0,1},{1,0},{2,3},{3,2},{4,5},{5,4},{6,7},{7,6},{8,9},{9,8},{10,11... | collective-permute-start | bytes 393224 | tf_op jit(solution)/shard_map/ppermute | solution.py:278
  30.6 14.3 %collective-permute-start.12 = (bf16[2,4,2,32,128]{4,3,2,1,0:T(8,128)(2,1)S(1)}, bf16[2,4,2,32,128]{4,3,2,1,0:T(8,128)(2,1)S(1)}, u32[]{:S(2)}, u32[]{:S(2)}) collective-permute-start(bf16[2,4,2,32,128]{4,3,2,1,0:T(8,128)(2,1)S(1)} %get-tuple-element.63), channel_id=1, source_target_pairs={{0,2},{1,3},{2,0},{3,1},{4,6},{5,7},{6,4},{7,5},{8,10},{9,11},{10,... | collective-permute-start | bytes 393224 | tf_op jit(solution)/shard_map/ppermute | solution.py:278
  35.0 9.9 %collective-permute-start.13 = (bf16[2,4,2,32,128]{4,3,2,1,0:T(8,128)(2,1)S(1)}, bf16[2,4,2,32,128]{4,3,2,1,0:T(8,128)(2,1)S(1)}, u32[]{:S(2)}, u32[]{:S(2)}) collective-permute-start(bf16[2,4,2,32,128]{4,3,2,1,0:T(8,128)(2,1)S(1)} %get-tuple-element.64), channel_id=1, source_target_pairs={{0,3},{1,2},{2,1},{3,0},{4,7},{5,6},{6,5},{7,4},{8,11},{9,10},{10,... | collective-permute-start | bytes 393224 | tf_op jit(solution)/shard_map/ppermute | solution.py:278
  53.6 5.4 %collective-permute-start.19 = (bf16[4,2,2,16,128]{4,3,2,1,0:T(8,128)(2,1)S(1)}, bf16[4,2,2,16,128]{4,3,2,1,0:T(8,128)(2,1)S(1)}, u32[]{:S(2)}, u32[]{:S(2)}) collective-permute-start(bf16[4,2,2,16,128]{4,3,2,1,0:T(8,128)(2,1)S(1)} %get-tuple-element.80), channel_id=1, source_target_pairs={{0,4},{4,0},{1,5},{5,1},{2,6},{6,2},{3,7},{7,3},{8,12},{12,8},{9,1... | collective-permute-start | bytes 196616 | tf_op jit(solution)/shard_map/ppermute | solution.py:278
  53.8 15.8 %collective-permute-start.16 = (bf16[6,128,128]{2,1,0:T(8,128)(2,1)S(1)}, bf16[6,128,128]{2,1,0:T(8,128)(2,1)S(1)}, u32[]{:S(2)}, u32[]{:S(2)}) collective-permute-start(bf16[6,128,128]{2,1,0:T(8,128)(2,1)S(1)} %get-tuple-element.76), channel_id=1, source_target_pairs={{0,8},{8,0},{16,24},{24,16},{1,9},{9,1},{17,25},{25,17},{2,10},{10... | collective-permute-start | bytes 589832 | tf_op jit(solution)/shard_map/ppermute | solution.py:278
  57.6 12.0 %collective-permute-start.17 = (bf16[6,128,128]{2,1,0:T(8,128)(2,1)S(1)}, bf16[6,128,128]{2,1,0:T(8,128)(2,1)S(1)}, u32[]{:S(2)}, u32[]{:S(2)}) collective-permute-start(bf16[6,128,128]{2,1,0:T(8,128)(2,1)S(1)} %get-tuple-element.77), channel_id=1, source_target_pairs={{0,16},{8,24},{16,0},{24,8},{1,17},{9,25},{17,1},{25,9},{2,18},{10... | collective-permute-start | bytes 589832 | tf_op jit(solution)/shard_map/ppermute | solution.py:278
  57.6 12.0 %collective-permute-start.18 = (bf16[6,128,128]{2,1,0:T(8,128)(2,1)S(1)}, bf16[6,128,128]{2,1,0:T(8,128)(2,1)S(1)}, u32[]{:S(2)}, u32[]{:S(2)}) collective-permute-start(bf16[6,128,128]{2,1,0:T(8,128)(2,1)S(1)} %get-tuple-element.78), channel_id=1, source_target_pairs={{0,24},{8,16},{16,8},{24,0},{1,25},{9,17},{17,9},{25,1},{2,26},{10... | collective-permute-start | bytes 589832 | tf_op jit(solution)/shard_map/ppermute | solution.py:278
  59.1 4.8 %collective-permute-start.20 = (bf16[2,2,32,128]{3,2,1,0:T(8,128)(2,1)S(1)}, bf16[2,2,32,128]{3,2,1,0:T(8,128)(2,1)S(1)}, u32[]{:S(2)}, u32[]{:S(2)}) collective-permute-start(bf16[2,2,32,128]{3,2,1,0:T(8,128)(2,1)S(1)} %get-tuple-element.97), channel_id=1, source_target_pairs={{0,1},{1,0},{2,3},{3,2},{4,5},{5,4},{6,7},{7,6},{8,9},{9,8},{10,11... | collective-permute-start | bytes 98312 | tf_op jit(solution)/shard_map/ppermute | solution.py:278
  61.0 6.4 %collective-permute-start.21 = (bf16[2,2,32,128]{3,2,1,0:T(8,128)(2,1)S(1)}, bf16[2,2,32,128]{3,2,1,0:T(8,128)(2,1)S(1)}, u32[]{:S(2)}, u32[]{:S(2)}) collective-permute-start(bf16[2,2,32,128]{3,2,1,0:T(8,128)(2,1)S(1)} %get-tuple-element.98), channel_id=1, source_target_pairs={{0,2},{1,3},{2,0},{3,1},{4,6},{5,7},{6,4},{7,5},{8,10},{9,11},{10,... | collective-permute-start | bytes 98312 | tf_op jit(solution)/shard_map/ppermute | solution.py:278
  63.9 5.7 %collective-permute-start.22 = (bf16[2,2,32,128]{3,2,1,0:T(8,128)(2,1)S(1)}, bf16[2,2,32,128]{3,2,1,0:T(8,128)(2,1)S(1)}, u32[]{:S(2)}, u32[]{:S(2)}) collective-permute-start(bf16[2,2,32,128]{3,2,1,0:T(8,128)(2,1)S(1)} %get-tuple-element.95), channel_id=1, source_target_pairs={{0,3},{1,2},{2,1},{3,0},{4,7},{5,6},{6,5},{7,4},{8,11},{9,10},{10,... | collective-permute-start | bytes 98312 | tf_op jit(solution)/shard_map/ppermute | solution.py:278
  69.7 4.7 %collective-permute-start.23 = (bf16[384,128]{1,0:T(8,128)(2,1)S(1)}, bf16[384,128]{1,0:T(8,128)(2,1)S(1)}, u32[]{:S(2)}, u32[]{:S(2)}) collective-permute-start(bf16[384,128]{1,0:T(8,128)(2,1)S(1)} %dynamic-slice_bitcast_fusion), channel_id=1, source_target_pairs={{0,1},{1,0},{2,3},{3,2},{4,5},{5,4},{6,7},{7,6},{8,9},{9,8},{10,11... | collective-permute-start | bytes 294920 | tf_op jit(solution)/shard_map/ppermute | solution.py:278
  74.5 6.6 %collective-permute-start.24 = (bf16[384,128]{1,0:T(8,128)(2,1)S(1)}, bf16[384,128]{1,0:T(8,128)(2,1)S(1)}, u32[]{:S(2)}, u32[]{:S(2)}) collective-permute-start(bf16[384,128]{1,0:T(8,128)(2,1)S(1)} %fusion.4), channel_id=1, source_target_pairs={{0,2},{1,3},{2,0},{3,1},{4,6},{5,7},{6,4},{7,5},{8,10},{9,11},{10,... | collective-permute-start | bytes 294920 | tf_op jit(solution)/shard_map/ppermute | solution.py:278
  81.1 4.7 %collective-permute-start.25 = (bf16[384,128]{1,0:T(8,128)(2,1)S(1)}, bf16[384,128]{1,0:T(8,128)(2,1)S(1)}, u32[]{:S(2)}, u32[]{:S(2)}) collective-permute-start(bf16[384,128]{1,0:T(8,128)(2,1)S(1)} %add_convert_fusion.5), channel_id=1, source_target_pairs={{0,1},{1,0},{2,3},{3,2},{4,5},{5,4},{6,7},{7,6},{8,9},{9,8},{10,11... | collective-permute-start | bytes 294920 | tf_op jit(solution)/shard_map/ppermute | solution.py:278
  (8 other events, 27.5 us)

commit v9 on v7

--- a/solution.py
+++ b/solution.py
@@ -84,13 +84,17 @@
         target[...] = wide_ref[:, :, :, pl.ds(pl.multiple_of(at, 16), width)].astype(BF16)
 
 
-def closing_kernel(group, mine_ref, other_ref, spatial_ref, temporal_ref, flat_ref):
-    pieces, rows, chans = mine_ref.shape
+def closing_kernel(group, *rest):
+    pairs, (spatial_ref, temporal_ref, flat_ref) = rest[:-3], rest[-3:]
     core, _, _, unit = placed(group)
-    for whose, ref in ((core, mine_ref), (1 - core, other_ref)):
+    shares = len(pairs) // 2
+    pieces, rows, chans = pairs[0].shape
+    for index, ref in enumerate(pairs):
+        whose = core if index % 2 == 0 else 1 - core
         for step in range(pieces):
-            index = whose * pieces + jnp.bitwise_xor(jnp.bitwise_and(unit, pieces - 1), step)
-            flat_ref[pl.ds(pl.multiple_of(index * rows, 16), rows)] = ref[step]
+            piece = jnp.bitwise_xor(jnp.bitwise_and(unit, pieces - 1), step)
+            first = ((whose * shares + index // 2) * pieces + piece) * rows
+            flat_ref[pl.ds(pl.multiple_of(first, 16), rows)] = ref[step]
     count = spatial_ref.shape[1]
     for tap in range(count + temporal_ref.shape[1]):
         turned = flat_ref[tap * chans : (tap + 1) * chans].astype(F32).T
@@ -440,37 +444,57 @@
     )(*shared, *cots, features, hidden, *slopes)
 
     got = swapped(give)
-    parts = [(keep[i].astype(F32) + got[i].astype(F32)).astype(BF16) for i in range(blocks)]
+    shares = 2
+    many = taps // shares
+    parts = [
+        [
+            (keep[i, at : at + many].astype(F32) + got[i, at : at + many].astype(F32)).astype(BF16)
+            for i in range(blocks)
+        ]
+        for at in range(0, taps, many)
+    ]
     other_grad, *parts = lax.optimization_barrier([other_grad] + parts)
-    parts = parts[:1] + [swapped(parts[i], "section", i) for i in range(1, blocks)]
+    parts = [
+        part[:1] + [swapped(part[i], "section", i) for i in range(1, blocks)] for part in parts
+    ]
     other_grad = swapped(other_grad)
     first = core == 0
     wide = jnp.concatenate(
         [jnp.where(first, mine_grad, other_grad), jnp.where(first, other_grad, mine_grad)], 3
     )
+
+    def along_z(part):
+        part = sum(each.astype(F32) for each in part).astype(BF16)
+        halves = part.reshape(2, -1, chans)
+        low = unit % 2
+
+        def picked(which):
+            return lax.dynamic_index_in_dim(halves, which, 0, keepdims=False)
+
+        part = picked(low).astype(F32) + swapped(picked(1 - low), "space", 1).astype(F32)
+        return part.astype(BF16)
+
+    def whole_z(part):
+        part = part.astype(F32) + swapped(part, "space", 2).astype(F32)
+        if tiles != group:
+            sets = [list(range(i, tiles, group)) for i in range(group)]
+            part = lax.psum(part, "space", axis_index_groups=sets)
+        return part.astype(BF16)
+
+    def gathered_pair(part):
+        pair = jnp.stack([part, swapped(part, "space", 1)])
+        return [pair, swapped(pair)]
+
+    early = along_z(parts[0])
+    early, *parts[1] = lax.optimization_barrier([early] + parts[1])
+    early = whole_z(early)
+    early, wide = lax.optimization_barrier([early, wide])
     strips = [wide[0]] + [swapped(wide[i], "space", i) for i in range(1, group)]
-    received = lax.optimization_barrier(parts + strips)
-    parts, strips = received[:blocks], received[blocks:]
-    part = sum(each.astype(F32) for each in parts).astype(BF16)
-
-    halves = part.reshape(2, -1, chans)
-    low = unit % 2
-
-    def picked(which):
-        return lax.dynamic_index_in_dim(halves, which, 0, keepdims=False)
-
-    part = (picked(low).astype(F32) + swapped(picked(1 - low), "space", 1).astype(F32)).astype(BF16)
-    part = part.astype(F32) + swapped(part, "space", 2).astype(F32)
-    if tiles != group:
-        part = lax.psum(
-            part, "space", axis_index_groups=[list(range(i, tiles, group)) for i in range(group)]
-        )
-    part = part.astype(BF16)
-    pair = jnp.stack([part, swapped(part, "space", 1)])
+    pairs = gathered_pair(early) + gathered_pair(whole_z(along_z(parts[1])))
     spatial_out, temporal_out = pl.pallas_call(
         functools.partial(closing_kernel, group),
         name="closing",
-        in_specs=[vmem] * 2,
+        in_specs=[vmem] * len(pairs),
         out_specs=[vmem] * 2,
         out_shape=[
             jax.ShapeDtypeStruct(spatial_weights.shape, F32),
@@ -478,7 +502,7 @@
         ],
         scratch_shapes=[pltpu.VMEM((cores * taps * chans, chans), BF16)],
         compiler_params=params,
-    )(pair, swapped(pair))
+    )(*pairs)
 
     grad_video = jnp.zeros(video.shape, BF16)
     for step, strip in enumerate(strips):

time: 83.1 us -> 87.4 us (1.052)
  starting transfers between devices: 36 us -> 41.3 us
  waiting for transfers between devices: 26.4 us -> 25.2 us
    ppermute x29 -> x36, starting transfers between devices: 33.5 us -> 38.8 us  [swapped(): return lax.ppermute(value, axis, [(i, i ^ step) for i in range(count)])]
    ppermute x29 -> x36, waiting for transfers between devices: 23.8 us -> 22.7 us  [swapped(): return lax.ppermute(value, axis, [(i, i ^ step) for i in range(count)])]
  transfers between devices with their start and end apart: 32 -> 39, of which waited for: 14 -> 13; matrix products, arithmetic and copies ran while one was open for 0% -> 0% of each run, Pallas kernels for 9% -> 9%
where the time goes in v9:
time: 87.4 us; the launch traced here: 87.1 us
  starting transfers between devices  41.3 us (47%)
  waiting for transfers between devices  25.2 us (29%)
  Pallas kernels  15.3 us (18%)
  local copies, waits for them, and re-layouts  3.77 us (4%)
  between operations  0.94 us (1%)
    ppermute x36, starting transfers between devices, swapped(): return lax.ppermute(value, axis, [(i, i ^ step) for i in range(count)])  38.8 us
    ppermute x36, waiting for transfers between devices, swapped(): return lax.ppermute(value, axis, [(i, i ^ step) for i in range(count)])  22.7 us
    pallas_call x1, Pallas kernels, on_device(): pl.pallas_call(functools.partial(forward_kernel, geometry), name='forward...  7.7 us
    pallas_call x1, Pallas kernels, on_device(): pl.pallas_call(functools.partial(backward_kernel, geometry, factor), name...  6.31 us
    unnamed x10, local copies, waits for them, and re-layouts  3.66 us
    ppermute x2, waiting for transfers between devices, traded(): return lax.ppermute(value, ('section', 'space'), pairs)  1.87 us
  transfers between devices with their start and end apart: 39, of which 13 were waited for; matrix products, arithmetic and copies ran while one was open for 0% of the time, Pallas kernels for 9%

profile of v9, /device:TPU:0, one launch (start us, length us, event | category | flops | bytes accessed | tf_op | source)
XLA Modules:
  0.0 87.1 jit_solution(9146363715299921199)
XLA Ops:
  3.5 3.0 %collective-permute-start.3 = (bf16[6,128,128]{2,1,0:T(8,128)(2,1)S(1)}, bf16[6,128,128]{2,1,0:T(8,128)(2,1)S(1)}, u32[]{:S(2)}, u32[]{:S(2)}) collective-permute-start(bf16[6,128,128]{2,1,0:T(8,128)(2,1)S(1)} %get-tuple-element.66), channel_id=1, source_target_pairs={{0,8},{8,0},{16,24},{24,16},{1,9},{9,1},{17,25},{25,17},{2,10},{10... | collective-permute-start | bytes 589832 | tf_op jit(solution)/shard_map/ppermute | solution.py:301
  6.5 1.5 %collective-permute-start.4 = (bf16[6,128,128]{2,1,0:T(8,128)(2,1)S(1)}, bf16[6,128,128]{2,1,0:T(8,128)(2,1)S(1)}, u32[]{:S(2)}, u32[]{:S(2)}) collective-permute-start(bf16[6,128,128]{2,1,0:T(8,128)(2,1)S(1)} %get-tuple-element.66), channel_id=1, source_target_pairs={{0,16},{8,24},{16,0},{24,8},{1,17},{9,25},{17,1},{25,9},{2,18},{10... | collective-permute-start | bytes 589832 | tf_op jit(solution)/shard_map/ppermute | solution.py:301
  8.1 1.6 %collective-permute-start = (bf16[2,2,48,128]{3,2,1,0:T(8,128)(2,1)S(1)}, bf16[2,2,48,128]{3,2,1,0:T(8,128)(2,1)S(1)}, u32[]{:S(2)}, u32[]{:S(2)}) collective-permute-start(bf16[2,2,48,128]{3,2,1,0:T(8,128)(2,1)S(1)} %get-tuple-element.63), channel_id=1, source_target_pairs={{0,1},{1,0},{2,3},{3,2},{4,5},{5,4},{6,7},{7,6},{8,9},{9,8},{10,11... | collective-permute-start | bytes 147464 | tf_op jit(solution)/shard_map/ppermute | solution.py:301
  9.6 2.6 %collective-permute-start.1 = (bf16[2,2,48,128]{3,2,1,0:T(8,128)(2,1)S(1)}, bf16[2,2,48,128]{3,2,1,0:T(8,128)(2,1)S(1)}, u32[]{:S(2)}, u32[]{:S(2)}) collective-permute-start(bf16[2,2,48,128]{3,2,1,0:T(8,128)(2,1)S(1)} %get-tuple-element.64), channel_id=1, source_target_pairs={{0,2},{1,3},{2,0},{3,1},{4,6},{5,7},{6,4},{7,5},{8,10},{9,11},{10,... | collective-permute-start | bytes 147464 | tf_op jit(solution)/shard_map/ppermute | solution.py:301
  15.2 3.0 %collective-permute-done.2 = bf16[2,2,48,128]{3,2,1,0:T(8,128)(2,1)S(1)} collective-permute-done((bf16[2,2,48,128]{3,2,1,0:T(8,128)(2,1)S(1)}, bf16[2,2,48,128]{3,2,1,0:T(8,128)(2,1)S(1)}, u32[]{:S(2)}, u32[]{:S(2)}) %collective-permute-start.2) | collective-permute-done | bytes 49184 | tf_op jit(solution)/shard_map/ppermute | solution.py:301
  23.5 1.9 %collective-permute-done.9.rest_8_ = bf16[4,2,2,48,128]{4,3,2,1,0:T(8,128)(2,1)S(1)} collective-permute-done((bf16[4,2,2,48,128]{4,3,2,1,0:T(8,128)(2,1)S(1)}, bf16[4,2,2,48,128]{4,3,2,1,0:T(8,128)(2,1)S(1)}, u32[]{:S(2)}, u32[]{:S(2)}) %collective-permute-start.9) | collective-permute-done | bytes 196640 | tf_op jit(solution)/shard_map/ppermute | solution.py:326
  26.9 3.2 %collective-permute-start.14 = (bf16[2,4,2,32,128]{4,3,2,1,0:T(8,128)(2,1)S(1)}, bf16[2,4,2,32,128]{4,3,2,1,0:T(8,128)(2,1)S(1)}, u32[]{:S(2)}, u32[]{:S(2)}) collective-permute-start(bf16[2,4,2,32,128]{4,3,2,1,0:T(8,128)(2,1)S(1)} %get-tuple-element.76), channel_id=1, source_target_pairs={{0,2},{1,3},{2,0},{3,1},{4,6},{5,7},{6,4},{7,5},{8,10},{9,11},{10,... | collective-permute-start | bytes 393224 | tf_op jit(solution)/shard_map/ppermute | solution.py:301
  30.8 7.7 %forward.1 = (bf16[4,4,10,16,384]{4,3,2,1,0:T(8,128)(2,1)S(1)}, bf16[4,4,8,16,128]{4,3,2,1,0:T(8,128)(2,1)S(1)}, f32[4,10,32,128]{3,2,1,0:T(8,128)S(1)}, f32[4,1...) custom-call(bf16[2,6,128,128]{3,2,1,0:T(8,128)(2,1)S(1)} %get-tuple-element.61.rest_0_, ...), custom_call_target="tpu_custom_call" | custom-call | flops 6000000000 | bytes 8000000 | tf_op jit(solution)/shard_map/forward/pallas_call | solution.py:398
  38.5 1.5 %collective-permute-done.14.rest_9_ = bf16[2,4,2,32,128]{4,3,2,1,0:T(8,128)(2,1)S(1)} collective-permute-done((bf16[2,4,2,32,128]{4,3,2,1,0:T(8,128)(2,1)S(1)}, bf16[2,4,2,32,128]{4,3,2,1,0:T(8,128)(2,1)S(1)}, u32[]{:S(2)}, u32[]{:S(2)}) %collective-permute-start.14) | collective-permute-done | bytes 131104 | tf_op jit(solution)/shard_map/ppermute | solution.py:301
  40.1 6.3 %backward.1 = (bf16[4,6,128,128]{3,2,1,0:T(8,128)(2,1)S(1)}, bf16[4,6,128,128]{3,2,1,0:T(8,128)(2,1)S(1)}, bf16[4,2,2,16,128]{4,3,2,1,0:T(8,128)(2,1)S(1)}, bf16[4,2,2,16,128]{4,3,2,1,0:T(8,128)(2,1)S(1)}) custom-call(bf16[2,6,128,128]{3,2,1,0:T(8,128)(2,1)S(1)} %get-tuple-element.61.rest_0_, bf16[6,128,128]{2,1,0:T(8,128)(2,1)S(1)} %collective-permute-done.3.rest_1_, ...), custom_call_target="tpu_custom_call" | custom-call | flops 6000000000 | bytes 8000000 | tf_op jit(solution)/shard_map/backward/pallas_call | solution.py:422
  46.5 2.3 %collective-permute-done.20 = bf16[4,6,128,128]{3,2,1,0:T(8,128)(2,1)S(1)} collective-permute-done((bf16[4,6,128,128]{3,2,1,0:T(8,128)(2,1)S(1)}, bf16[4,6,128,128]{3,2,1,0:T(8,128)(2,1)S(1)}, u32[]{:S(2)}, u32[]{:S(2)}) %collective-permute-start.20) | collective-permute-done | bytes 786464 | tf_op jit(solution)/shard_map/ppermute | solution.py:301
  49.2 4.1 %collective-permute-start.21 = (bf16[3,128,128]{2,1,0:T(8,128)(2,1)S(1)}, bf16[3,128,128]{2,1,0:T(8,128)(2,1)S(1)}, u32[]{:S(2)}, u32[]{:S(2)}) collective-permute-start(bf16[3,128,128]{2,1,0:T(8,128)(2,1)S(1)} %get-tuple-element.89), channel_id=1, source_target_pairs={{0,8},{8,0},{16,24},{24,16},{1,9},{9,1},{17,25},{25,17},{2,10},{10... | collective-permute-start | bytes 294920 | tf_op jit(solution)/shard_map/ppermute | solution.py:301
  53.3 1.5 %collective-permute-start.23 = (bf16[3,128,128]{2,1,0:T(8,128)(2,1)S(1)}, bf16[3,128,128]{2,1,0:T(8,128)(2,1)S(1)}, u32[]{:S(2)}, u32[]{:S(2)}) collective-permute-start(bf16[3,128,128]{2,1,0:T(8,128)(2,1)S(1)} %get-tuple-element.91), channel_id=1, source_target_pairs={{0,24},{8,16},{16,8},{24,0},{1,25},{9,17},{17,9},{25,1},{2,26},{10... | collective-permute-start | bytes 294920 | tf_op jit(solution)/shard_map/ppermute | solution.py:301
  54.8 2.0 %collective-permute-start.25 = (bf16[3,128,128]{2,1,0:T(8,128)(2,1)S(1)}, bf16[3,128,128]{2,1,0:T(8,128)(2,1)S(1)}, u32[]{:S(2)}, u32[]{:S(2)}) collective-permute-start(bf16[3,128,128]{2,1,0:T(8,128)(2,1)S(1)} %get-tuple-element.93), channel_id=1, source_target_pairs={{0,8},{8,0},{16,24},{24,16},{1,9},{9,1},{17,25},{25,17},{2,10},{10... | collective-permute-start | bytes 294920 | tf_op jit(solution)/shard_map/ppermute | solution.py:301
  56.8 1.6 %collective-permute-start.27 = (bf16[3,128,128]{2,1,0:T(8,128)(2,1)S(1)}, bf16[3,128,128]{2,1,0:T(8,128)(2,1)S(1)}, u32[]{:S(2)}, u32[]{:S(2)}) collective-permute-start(bf16[3,128,128]{2,1,0:T(8,128)(2,1)S(1)} %get-tuple-element.95), channel_id=1, source_target_pairs={{0,24},{8,16},{16,8},{24,0},{1,25},{9,17},{17,9},{25,1},{2,26},{10... | collective-permute-start | bytes 294920 | tf_op jit(solution)/shard_map/ppermute | solution.py:301
  58.4 2.0 %collective-permute-done.22 = bf16[3,128,128]{2,1,0:T(8,128)(2,1)S(1)} collective-permute-done((bf16[3,128,128]{2,1,0:T(8,128)(2,1)S(1)}, bf16[3,128,128]{2,1,0:T(8,128)(2,1)S(1)}, u32[]{:S(2)}, u32[]{:S(2)}) %collective-permute-start.22) | collective-permute-done | bytes 98336 | tf_op jit(solution)/shard_map/ppermute | solution.py:301
  60.5 2.5 %collective-permute-start.24 = (bf16[192,128]{1,0:T(8,128)(2,1)S(1)}, bf16[192,128]{1,0:T(8,128)(2,1)S(1)}, u32[]{:S(2)}, u32[]{:S(2)}) collective-permute-start(bf16[192,128]{1,0:T(8,128)(2,1)S(1)} %dynamic-slice_bitcast_fusion.1), channel_id=1, source_target_pairs={{0,1},{1,0},{2,3},{3,2},{4,5},{5,4},{6,7},{7,6},{8,9},{9,8},{10,11... | collective-permute-start | bytes 147464 | tf_op jit(solution)/shard_map/ppermute | solution.py:301
  63.0 2.1 %collective-permute-done.24 = bf16[192,128]{1,0:T(8,128)(2,1)S(1)} collective-permute-done((bf16[192,128]{1,0:T(8,128)(2,1)S(1)}, bf16[192,128]{1,0:T(8,128)(2,1)S(1)}, u32[]{:S(2)}, u32[]{:S(2)}) %collective-permute-start.24) | collective-permute-done | bytes 49184 | tf_op jit(solution)/shard_map/ppermute | solution.py:301
  65.1 3.1 %collective-permute-start.28 = (bf16[192,128]{1,0:T(8,128)(2,1)S(1)}, bf16[192,128]{1,0:T(8,128)(2,1)S(1)}, u32[]{:S(2)}, u32[]{:S(2)}) collective-permute-start(bf16[192,128]{1,0:T(8,128)(2,1)S(1)} %fusion.9), channel_id=1, source_target_pairs={{0,2},{1,3},{2,0},{3,1},{4,6},{5,7},{6,4},{7,5},{8,10},{9,11},{10,... | collective-permute-start | bytes 147464 | tf_op jit(solution)/shard_map/ppermute | solution.py:301
  68.4 2.0 %collective-permute-done.28 = bf16[192,128]{1,0:T(8,128)(2,1)S(1)} collective-permute-done((bf16[192,128]{1,0:T(8,128)(2,1)S(1)}, bf16[192,128]{1,0:T(8,128)(2,1)S(1)}, u32[]{:S(2)}, u32[]{:S(2)}) %collective-permute-start.28) | collective-permute-done | bytes 49184 | tf_op jit(solution)/shard_map/ppermute | solution.py:301
  70.4 1.9 %collective-permute-start.36 = (bf16[2,2,32,128]{3,2,1,0:T(8,128)(2,1)S(1)}, bf16[2,2,32,128]{3,2,1,0:T(8,128)(2,1)S(1)}, u32[]{:S(2)}, u32[]{:S(2)}) collective-permute-start(bf16[2,2,32,128]{3,2,1,0:T(8,128)(2,1)S(1)} %get-tuple-element.117), channel_id=1, source_target_pairs={{0,1},{1,0},{2,3},{3,2},{4,5},{5,4},{6,7},{7,6},{8,9},{9,8},{10,11... | collective-permute-start | bytes 98312 | tf_op jit(solution)/shard_map/ppermute | solution.py:301
  74.9 2.0 %collective-permute-start.33 = (bf16[192,128]{1,0:T(8,128)(2,1)S(1)}, bf16[192,128]{1,0:T(8,128)(2,1)S(1)}, u32[]{:S(2)}, u32[]{:S(2)}) collective-permute-start(bf16[192,128]{1,0:T(8,128)(2,1)S(1)} %fusion.8), channel_id=1, source_target_pairs={{0,2},{1,3},{2,0},{3,1},{4,6},{5,7},{6,4},{7,5},{8,10},{9,11},{10,... | collective-permute-start | bytes 147464 | tf_op jit(solution)/shard_map/ppermute | solution.py:301
  78.0 2.5 %collective-permute-done.33 = bf16[192,128]{1,0:T(8,128)(2,1)S(1)} collective-permute-done((bf16[192,128]{1,0:T(8,128)(2,1)S(1)}, bf16[192,128]{1,0:T(8,128)(2,1)S(1)}, u32[]{:S(2)}, u32[]{:S(2)}) %collective-permute-start.33) | collective-permute-done | bytes 49184 | tf_op jit(solution)/shard_map/ppermute | solution.py:301
  81.2 3.5 %collective-permute-done.34 = bf16[192,128]{1,0:T(8,128)(2,1)S(1)} collective-permute-done((bf16[192,128]{1,0:T(8,128)(2,1)S(1)}, bf16[192,128]{1,0:T(8,128)(2,1)S(1)}, u32[]{:S(2)}, u32[]{:S(2)}) %collective-permute-start.34) | collective-permute-done | bytes 49184 | tf_op jit(solution)/shard_map/ppermute | solution.py:301
  (90 shorter events, 21.0 us)
Async XLA Ops:
  3.5 14.6 %collective-permute-start.3 = (bf16[6,128,128]{2,1,0:T(8,128)(2,1)S(1)}, bf16[6,128,128]{2,1,0:T(8,128)(2,1)S(1)}, u32[]{:S(2)}, u32[]{:S(2)}) collective-permute-start(bf16[6,128,128]{2,1,0:T(8,128)(2,1)S(1)} %get-tuple-element.66), channel_id=1, source_target_pairs={{0,8},{8,0},{16,24},{24,16},{1,9},{9,1},{17,25},{25,17},{2,10},{10... | collective-permute-start | bytes 589832 | tf_op jit(solution)/shard_map/ppermute | solution.py:301
  6.5 11.6 %collective-permute-start.4 = (bf16[6,128,128]{2,1,0:T(8,128)(2,1)S(1)}, bf16[6,128,128]{2,1,0:T(8,128)(2,1)S(1)}, u32[]{:S(2)}, u32[]{:S(2)}) collective-permute-start(bf16[6,128,128]{2,1,0:T(8,128)(2,1)S(1)} %get-tuple-element.66), channel_id=1, source_target_pairs={{0,16},{8,24},{16,0},{24,8},{1,17},{9,25},{17,1},{25,9},{2,18},{10... | collective-permute-start | bytes 589832 | tf_op jit(solution)/shard_map/ppermute | solution.py:301
  9.6 5.5 %collective-permute-start.1 = (bf16[2,2,48,128]{3,2,1,0:T(8,128)(2,1)S(1)}, bf16[2,2,48,128]{3,2,1,0:T(8,128)(2,1)S(1)}, u32[]{:S(2)}, u32[]{:S(2)}) collective-permute-start(bf16[2,2,48,128]{3,2,1,0:T(8,128)(2,1)S(1)} %get-tuple-element.64), channel_id=1, source_target_pairs={{0,2},{1,3},{2,0},{3,1},{4,6},{5,7},{6,4},{7,5},{8,10},{9,11},{10,... | collective-permute-start | bytes 147464 | tf_op jit(solution)/shard_map/ppermute | solution.py:301
  12.2 5.9 %collective-permute-start.2 = (bf16[2,2,48,128]{3,2,1,0:T(8,128)(2,1)S(1)}, bf16[2,2,48,128]{3,2,1,0:T(8,128)(2,1)S(1)}, u32[]{:S(2)}, u32[]{:S(2)}) collective-permute-start(bf16[2,2,48,128]{3,2,1,0:T(8,128)(2,1)S(1)} %get-tuple-element.65), channel_id=1, source_target_pairs={{0,3},{1,2},{2,1},{3,0},{4,7},{5,6},{6,5},{7,4},{8,11},{9,10},{10,... | collective-permute-start | bytes 147464 | tf_op jit(solution)/shard_map/ppermute | solution.py:301
  12.4 8.2 %collective-permute-start.11 = (bf16[2,2,128,128]{3,2,1,0:T(8,128)(2,1)}, bf16[2,2,128,128]{3,2,1,0:T(8,128)(2,1)S(1)}, u32[]{:S(2)}, u32[]{:S(2)}) collective-permute-start(bf16[2,2,128,128]{3,2,1,0:T(8,128)(2,1)} %rest_0_.1), channel_id=1, source_target_pairs={{8,0},{9,1},{2,10},{3,11},{16,8},{17,9},{10,18},{11,19},{24,16},{2... | collective-permute-start | bytes 393224 | tf_op jit(solution)/shard_map/ppermute | solution.py:335
  15.1 5.5 %collective-permute-start.10 = (bf16[2,2,128,128]{3,2,1,0:T(8,128)(2,1)}, bf16[2,2,128,128]{3,2,1,0:T(8,128)(2,1)S(1)}, u32[]{:S(2)}, u32[]{:S(2)}) collective-permute-start(bf16[2,2,128,128]{3,2,1,0:T(8,128)(2,1)} %rest_0_.1), channel_id=1, source_target_pairs={{0,4},{4,0},{1,5},{5,1},{2,6},{6,2},{3,7},{7,3},{8,12},{12,8},{9,1... | collective-permute-start | bytes 393224 | tf_op jit(solution)/shard_map/ppermute | solution.py:301
  18.2 7.2 %collective-permute-start.9 = (bf16[4,2,2,48,128]{4,3,2,1,0:T(8,128)(2,1)S(1)}, bf16[4,2,2,48,128]{4,3,2,1,0:T(8,128)(2,1)S(1)}, u32[]{:S(2)}, u32[]{:S(2)}) collective-permute-start(bf16[4,2,2,48,128]{4,3,2,1,0:T(8,128)(2,1)S(1)} %pad_maximum_fusion.rest_7_), channel_id=1, source_target_pairs={{0,8},{1,9},{2,10},{3,11},{8,0},{9,1},{10,2},{11,3},{16,24},{17,25... | collective-permute-start | bytes 589832 | tf_op jit(solution)/shard_map/ppermute | solution.py:326
  18.8 6.6 %collective-permute-start.5 = (bf16[6,128,128]{2,1,0:T(8,128)(2,1)S(1)}, bf16[6,128,128]{2,1,0:T(8,128)(2,1)S(1)}, u32[]{:S(2)}, u32[]{:S(2)}) collective-permute-start(bf16[6,128,128]{2,1,0:T(8,128)(2,1)S(1)} %collective-permute-done.3.rest_1_), channel_id=1, source_target_pairs={{0,16},{8,24},{16,0},{24,8},{1,17},{9,25},{17,1},{25,9},{2,18},{10... | collective-permute-start | bytes 589832 | tf_op jit(solution)/shard_map/ppermute | solution.py:301
  19.3 6.6 %collective-permute-start.16 = (bf16[4,2,2,48,128]{4,3,2,1,0:T(8,128)(2,1)S(1)}, bf16[4,2,2,48,128]{4,3,2,1,0:T(8,128)(2,1)S(1)}, u32[]{:S(2)}, u32[]{:S(2)}) collective-permute-start(bf16[4,2,2,48,128]{4,3,2,1,0:T(8,128)(2,1)S(1)} %pad_maximum_fusion.rest_7_), channel_id=1, source_target_pairs={{8,16},{9,17},{10,18},{11,19},{16,8},{17,9},{18,10},{19,11},{12,20... | collective-permute-start | bytes 589832 | tf_op jit(solution)/shard_map/ppermute | solution.py:326
  26.4 12.1 %collective-permute-start.13 = (bf16[2,4,2,32,128]{4,3,2,1,0:T(8,128)(2,1)S(1)}, bf16[2,4,2,32,128]{4,3,2,1,0:T(8,128)(2,1)S(1)}, u32[]{:S(2)}, u32[]{:S(2)}) collective-permute-start(bf16[2,4,2,32,128]{4,3,2,1,0:T(8,128)(2,1)S(1)} %get-tuple-element.75), channel_id=1, source_target_pairs={{0,1},{1,0},{2,3},{3,2},{4,5},{5,4},{6,7},{7,6},{8,9},{9,8},{10,11... | collective-permute-start | bytes 393224 | tf_op jit(solution)/shard_map/ppermute | solution.py:301
  26.9 13.2 %collective-permute-start.14 = (bf16[2,4,2,32,128]{4,3,2,1,0:T(8,128)(2,1)S(1)}, bf16[2,4,2,32,128]{4,3,2,1,0:T(8,128)(2,1)S(1)}, u32[]{:S(2)}, u32[]{:S(2)}) collective-permute-start(bf16[2,4,2,32,128]{4,3,2,1,0:T(8,128)(2,1)S(1)} %get-tuple-element.76), channel_id=1, source_target_pairs={{0,2},{1,3},{2,0},{3,1},{4,6},{5,7},{6,4},{7,5},{8,10},{9,11},{10,... | collective-permute-start | bytes 393224 | tf_op jit(solution)/shard_map/ppermute | solution.py:301
  30.1 10.0 %collective-permute-start.15 = (bf16[2,4,2,32,128]{4,3,2,1,0:T(8,128)(2,1)S(1)}, bf16[2,4,2,32,128]{4,3,2,1,0:T(8,128)(2,1)S(1)}, u32[]{:S(2)}, u32[]{:S(2)}) collective-permute-start(bf16[2,4,2,32,128]{4,3,2,1,0:T(8,128)(2,1)S(1)} %get-tuple-element.77), channel_id=1, source_target_pairs={{0,3},{1,2},{2,1},{3,0},{4,7},{5,6},{6,5},{7,4},{8,11},{9,10},{10,... | collective-permute-start | bytes 393224 | tf_op jit(solution)/shard_map/ppermute | solution.py:301
  49.0 7.8 %collective-permute-start.29 = (bf16[4,2,2,16,128]{4,3,2,1,0:T(8,128)(2,1)S(1)}, bf16[4,2,2,16,128]{4,3,2,1,0:T(8,128)(2,1)S(1)}, u32[]{:S(2)}, u32[]{:S(2)}) collective-permute-start(bf16[4,2,2,16,128]{4,3,2,1,0:T(8,128)(2,1)S(1)} %get-tuple-element.98), channel_id=1, source_target_pairs={{0,4},{4,0},{1,5},{5,1},{2,6},{6,2},{3,7},{7,3},{8,12},{12,8},{9,1... | collective-permute-start | bytes 196616 | tf_op jit(solution)/shard_map/ppermute | solution.py:301
  49.2 7.6 %collective-permute-start.21 = (bf16[3,128,128]{2,1,0:T(8,128)(2,1)S(1)}, bf16[3,128,128]{2,1,0:T(8,128)(2,1)S(1)}, u32[]{:S(2)}, u32[]{:S(2)}) collective-permute-start(bf16[3,128,128]{2,1,0:T(8,128)(2,1)S(1)} %get-tuple-element.89), channel_id=1, source_target_pairs={{0,8},{8,0},{16,24},{24,16},{1,9},{9,1},{17,25},{25,17},{2,10},{10... | collective-permute-start | bytes 294920 | tf_op jit(solution)/shard_map/ppermute | solution.py:301
  53.3 7.1 %collective-permute-start.22 = (bf16[3,128,128]{2,1,0:T(8,128)(2,1)S(1)}, bf16[3,128,128]{2,1,0:T(8,128)(2,1)S(1)}, u32[]{:S(2)}, u32[]{:S(2)}) collective-permute-start(bf16[3,128,128]{2,1,0:T(8,128)(2,1)S(1)} %get-tuple-element.90), channel_id=1, source_target_pairs={{0,16},{8,24},{16,0},{24,8},{1,17},{9,25},{17,1},{25,9},{2,18},{10... | collective-permute-start | bytes 294920 | tf_op jit(solution)/shard_map/ppermute | solution.py:301
  53.3 7.1 %collective-permute-start.23 = (bf16[3,128,128]{2,1,0:T(8,128)(2,1)S(1)}, bf16[3,128,128]{2,1,0:T(8,128)(2,1)S(1)}, u32[]{:S(2)}, u32[]{:S(2)}) collective-permute-start(bf16[3,128,128]{2,1,0:T(8,128)(2,1)S(1)} %get-tuple-element.91), channel_id=1, source_target_pairs={{0,24},{8,16},{16,8},{24,0},{1,25},{9,17},{17,9},{25,1},{2,26},{10... | collective-permute-start | bytes 294920 | tf_op jit(solution)/shard_map/ppermute | solution.py:301
  54.8 10.3 %collective-permute-start.25 = (bf16[3,128,128]{2,1,0:T(8,128)(2,1)S(1)}, bf16[3,128,128]{2,1,0:T(8,128)(2,1)S(1)}, u32[]{:S(2)}, u32[]{:S(2)}) collective-permute-start(bf16[3,128,128]{2,1,0:T(8,128)(2,1)S(1)} %get-tuple-element.93), channel_id=1, source_target_pairs={{0,8},{8,0},{16,24},{24,16},{1,9},{9,1},{17,25},{25,17},{2,10},{10... | collective-permute-start | bytes 294920 | tf_op jit(solution)/shard_map/ppermute | solution.py:301
  56.8 8.3 %collective-permute-start.26 = (bf16[3,128,128]{2,1,0:T(8,128)(2,1)S(1)}, bf16[3,128,128]{2,1,0:T(8,128)(2,1)S(1)}, u32[]{:S(2)}, u32[]{:S(2)}) collective-permute-start(bf16[3,128,128]{2,1,0:T(8,128)(2,1)S(1)} %get-tuple-element.94), channel_id=1, source_target_pairs={{0,16},{8,24},{16,0},{24,8},{1,17},{9,25},{17,1},{25,9},{2,18},{10... | collective-permute-start | bytes 294920 | tf_op jit(solution)/shard_map/ppermute | solution.py:301
  56.8 8.3 %collective-permute-start.27 = (bf16[3,128,128]{2,1,0:T(8,128)(2,1)S(1)}, bf16[3,128,128]{2,1,0:T(8,128)(2,1)S(1)}, u32[]{:S(2)}, u32[]{:S(2)}) collective-permute-start(bf16[3,128,128]{2,1,0:T(8,128)(2,1)S(1)} %get-tuple-element.95), channel_id=1, source_target_pairs={{0,24},{8,16},{16,8},{24,0},{1,25},{9,17},{17,9},{25,1},{2,26},{10... | collective-permute-start | bytes 294920 | tf_op jit(solution)/shard_map/ppermute | solution.py:301
  68.3 6.6 %collective-permute-start.32 = (bf16[192,128]{1,0:T(8,128)(2,1)S(1)}, bf16[192,128]{1,0:T(8,128)(2,1)S(1)}, u32[]{:S(2)}, u32[]{:S(2)}) collective-permute-start(bf16[192,128]{1,0:T(8,128)(2,1)S(1)} %dynamic-slice_bitcast_fusion), channel_id=1, source_target_pairs={{0,1},{1,0},{2,3},{3,2},{4,5},{5,4},{6,7},{7,6},{8,9},{9,8},{10,11... | collective-permute-start | bytes 147464 | tf_op jit(solution)/shard_map/ppermute | solution.py:301
  70.4 7.5 %collective-permute-start.36 = (bf16[2,2,32,128]{3,2,1,0:T(8,128)(2,1)S(1)}, bf16[2,2,32,128]{3,2,1,0:T(8,128)(2,1)S(1)}, u32[]{:S(2)}, u32[]{:S(2)}) collective-permute-start(bf16[2,2,32,128]{3,2,1,0:T(8,128)(2,1)S(1)} %get-tuple-element.117), channel_id=1, source_target_pairs={{0,1},{1,0},{2,3},{3,2},{4,5},{5,4},{6,7},{7,6},{8,9},{9,8},{10,11... | collective-permute-start | bytes 98312 | tf_op jit(solution)/shard_map/ppermute | solution.py:301
  72.3 5.6 %collective-permute-start.37 = (bf16[2,2,32,128]{3,2,1,0:T(8,128)(2,1)S(1)}, bf16[2,2,32,128]{3,2,1,0:T(8,128)(2,1)S(1)}, u32[]{:S(2)}, u32[]{:S(2)}) collective-permute-start(bf16[2,2,32,128]{3,2,1,0:T(8,128)(2,1)S(1)} %get-tuple-element.116), channel_id=1, source_target_pairs={{0,2},{1,3},{2,0},{3,1},{4,6},{5,7},{6,4},{7,5},{8,10},{9,11},{10,... | collective-permute-start | bytes 98312 | tf_op jit(solution)/shard_map/ppermute | solution.py:301
  73.4 11.4 %collective-permute-start.38 = (bf16[2,2,32,128]{3,2,1,0:T(8,128)(2,1)S(1)}, bf16[2,2,32,128]{3,2,1,0:T(8,128)(2,1)S(1)}, u32[]{:S(2)}, u32[]{:S(2)}) collective-permute-start(bf16[2,2,32,128]{3,2,1,0:T(8,128)(2,1)S(1)} %get-tuple-element.115), channel_id=1, source_target_pairs={{0,3},{1,2},{2,1},{3,0},{4,7},{5,6},{6,5},{7,4},{8,11},{9,10},{10,... | collective-permute-start | bytes 98312 | tf_op jit(solution)/shard_map/ppermute | solution.py:301
  74.9 5.6 %collective-permute-start.33 = (bf16[192,128]{1,0:T(8,128)(2,1)S(1)}, bf16[192,128]{1,0:T(8,128)(2,1)S(1)}, u32[]{:S(2)}, u32[]{:S(2)}) collective-permute-start(bf16[192,128]{1,0:T(8,128)(2,1)S(1)} %fusion.8), channel_id=1, source_target_pairs={{0,2},{1,3},{2,0},{3,1},{4,6},{5,7},{6,4},{7,5},{8,10},{9,11},{10,... | collective-permute-start | bytes 147464 | tf_op jit(solution)/shard_map/ppermute | solution.py:301
  (20 other events, 63.1 us)

commit v10 on v7

--- a/solution.py
+++ b/solution.py
@@ -55,33 +55,22 @@
         target[...] = wide_ref[:, :, pl.ds(pl.multiple_of(at, 16), span)].astype(BF16)
 
 
-def halves_kernel(spatial_ref, temporal_ref, half_ref, both_ref, all_ref):
-    core = lax.axis_index("tm")
-    count = spatial_ref.shape[1]
-    taps = half_ref.shape[0]
-    all_ref[:count] = spatial_ref[0]
-    all_ref[count:] = temporal_ref[0]
-    half_ref[...] = all_ref[pl.ds(core * taps, taps)]
-    both_ref[0] = all_ref[pl.ds(core * taps, taps)]
-    both_ref[1] = all_ref[pl.ds((1 - core) * taps, taps)]
-
-
-def cotangent_kernel(halo, width, *rest):
-    sources, targets, wide_ref = rest[:4], rest[4:-1], rest[-1]
-    core, _, _, unit = placed(len(targets))
-    frames_in, rows, columns, chans = sources[0].shape
-    edge = jnp.zeros((2, 2 * frames_in, rows, halo, chans), F32)
-    wide_ref[:, :, :, :halo] = edge
-    wide_ref[:, :, :, halo + columns :] = edge
-    for index, ref in enumerate(sources):
-        whose = core if index % 2 == 0 else 1 - core
-        wide_ref[index // 2, pl.ds(whose * frames_in, frames_in), :, halo : halo + columns] = ref[
-            ...
-        ].astype(F32)
+def cotangent_kernel(halo, width, mine_ref, other_ref, *rest):
+    targets, wide_ref = rest[:-1], rest[-1]
+    count = targets[0].shape[0]
+    core, _, _, unit = placed(count * len(targets))
+    frames_in, rows, columns, chans = mine_ref.shape
+    edge = jnp.zeros((2 * frames_in, rows, halo, chans), F32)
+    wide_ref[:, :, :halo] = edge
+    wide_ref[:, :, halo + columns :] = edge
+    for whose, ref in ((core, mine_ref), (1 - core, other_ref)):
+        wide_ref[pl.ds(whose * frames_in, frames_in), :, halo : halo + columns] = ref[...].astype(F32)
     own = width - 2 * halo
-    for step, target in enumerate(targets):
-        at = (jnp.bitwise_xor(unit, step) * 2 + core) * own
-        target[...] = wide_ref[:, :, :, pl.ds(pl.multiple_of(at, 16), width)].astype(BF16)
+    for index, target in enumerate(targets):
+        for step in range(count):
+            at = (jnp.bitwise_xor(unit, index * count + step) * 2 + core) * own
+            at = pl.ds(pl.multiple_of(at, 16), width)
+            target[step] = wide_ref[:, :, at].astype(BF16)
 
 
 def closing_kernel(group, mine_ref, other_ref, spatial_ref, temporal_ref, flat_ref):
@@ -100,9 +89,9 @@
             temporal_ref[0, tap - count] = turned
 
 
-def place_kernels(core, section, w_ref, own_ref, mine_refs, other_refs):
-    w_ref[core, section] = own_ref[0]
-    w_ref[1 - core, section] = own_ref[1]
+def place_kernels(core, section, w_ref, own_mine, own_other, mine_refs, other_refs):
+    w_ref[core, section] = own_mine[...]
+    w_ref[1 - core, section] = own_other[...]
     for step, (mine_ref, other_ref) in enumerate(zip(mine_refs, other_refs)):
         block = jnp.bitwise_xor(section, step + 1)
         w_ref[core, block] = mine_ref[...]
@@ -113,12 +102,12 @@
     blocks, cores, group, frames_in, rows_in, halo, tile, width, height, columns = geometry
     core, section, band, unit = placed(group)
     odd = band % 2
-    shared, rest = rest[: 2 * blocks - 1], rest[2 * blocks - 1 :]
+    shared, rest = rest[: 2 * blocks], rest[2 * blocks :]
     arrived, rest = rest[:6], rest[6:]
     xo_ref, ho_ref = rest[:2]
     d_refs = rest[2 : 2 + blocks]
     x_ref, h_ref, mask_ref, w_ref, start_ref = rest[2 + blocks :]
-    place_kernels(core, section, w_ref, shared[0], shared[1:blocks], shared[blocks:])
+    place_kernels(core, section, w_ref, *shared[:2], shared[2 : 1 + blocks], shared[1 + blocks :])
     frames = cores * frames_in
     high = tile + 2 * halo
     chans = w_ref.shape[-1]
@@ -203,13 +192,13 @@
 def backward_kernel(geometry, factor, *rest):
     blocks, cores, group, frames_in, rows_in, halo, tile, width, height, columns = geometry
     core, section, band, unit = placed(group)
-    shared, rest = rest[: 2 * blocks - 1], rest[2 * blocks - 1 :]
-    arrived, rest = rest[:group], rest[group:]
+    shared, rest = rest[: 2 * blocks], rest[2 * blocks :]
+    arrived, rest = rest[:4], rest[4:]
     xo_ref, ho_ref = rest[:2]
     d_refs = rest[2 : 2 + blocks]
     keep_ref, give_ref, mine_out, other_out = rest[2 + blocks : 6 + blocks]
     g_ref, da_ref, dao_ref, go_ref, w_ref, grad_ref, out_ref = rest[6 + blocks :]
-    place_kernels(core, section, w_ref, shared[0], shared[1:blocks], shared[blocks:])
+    place_kernels(core, section, w_ref, *shared[:2], shared[2 : 1 + blocks], shared[1 + blocks :])
     frames = cores * frames_in
     chans = w_ref.shape[-1]
     rim = blocks
@@ -217,12 +206,14 @@
     per_core = w_ref.shape[2]
     pixels = tile * (own_cols[1] - own_cols[0])
 
+    odd = band % 2
+    near = tile + rim - odd * (tile + rim)
     half = group // 2
-    for step, ref in enumerate(arrived):
-        at = jnp.bitwise_xor(unit, step)
-        g_ref[:, pl.ds(rim + at * rows_in, rows_in)] = ref[0]
-        beyond = jnp.where(at < half, rim + tile + at * rows_in, (at - half) * rows_in)
-        g_ref[:, pl.ds(beyond, rows_in)] = ref[1]
+    for index, (base, ref) in enumerate(zip((rim, rim, near, tile + rim - near), arrived)):
+        for step in range(half):
+            at = jnp.bitwise_xor(unit, (half if index == 1 else 0) + step)
+            at = at if index < 2 else jnp.bitwise_and(at, half - 1)
+            g_ref[:, pl.ds(base + at * rows_in, rows_in)] = ref[step]
 
     def put(block, tap, value):
         slot = jnp.where(core == tap // per_core, 0, 1)
@@ -312,6 +303,7 @@
 
     bands = blocks * tiles // group
     core, section, band, unit = placed(group)
+    odd = band % 2
 
     def traded(value, shift):
         pairs = []
@@ -323,13 +315,6 @@
 
     total_rows = blocks * tiles * rows_in
     half = group // 2
-    passed = []
-    for one in range(bands - 1):
-        for i in range(group):
-            low, high = one * group + i, (one + 1) * group + i
-            passed.append((high, low) if i < half else (low, high))
-    cot_halo = lax.ppermute(cotangent, ("section", "space"), passed)
-
     padded = columns + 2 * halo
     cuts = pl.pallas_call(
         functools.partial(window_kernel, halo, span),
@@ -340,51 +325,56 @@
         scratch_shapes=[pltpu.VMEM((frames_in, rows_in, padded, chans), F32)],
         compiler_params=params,
     )(video)
-    *cuts, spatial, temporal = lax.optimization_barrier(
-        list(cuts) + [spatial_weights, temporal_weights]
-    )
-    count = spatial_weights.shape[1]
-    taps = (count + temporal_weights.shape[1]) // cores
-    one_half = jax.ShapeDtypeStruct((taps, chans, chans), BF16)
-    half_kernels, own_kernels = pl.pallas_call(
-        halves_kernel,
-        name="halves",
+    pair = jax.ShapeDtypeStruct((half, cores * frames_in, rows_in, width, chans), BF16)
+    low, high_pair = pl.pallas_call(
+        functools.partial(cotangent_kernel, halo, width),
+        name="cotangent",
         in_specs=[vmem] * 2,
         out_specs=[vmem] * 2,
-        out_shape=[one_half, jax.ShapeDtypeStruct((cores,) + one_half.shape, BF16)],
-        scratch_shapes=[pltpu.VMEM((cores * taps, chans, chans), BF16)],
+        out_shape=[pair] * 2,
+        scratch_shapes=[pltpu.VMEM((cores * frames_in, rows_in, padded, chans), F32)],
         compiler_params=params,
-    )(spatial, temporal)
+    )(cotangent, swapped(cotangent))
+
+    def core_half(which, spatial, temporal):
+        whole = jnp.concatenate([spatial[0], temporal[0]], 0)
+        taps = whole.shape[0] // cores
+        return lax.dynamic_slice_in_dim(whole, which * taps, taps, 0)
+
+    half_kernels = core_half(core, spatial_weights, temporal_weights)
 
     def gathered(pieces):
         return jnp.stack([pieces[0]] + [swapped(pieces[i], "space", i) for i in range(1, group)])
 
     along_x = swapped(half_kernels, "section", 1)
     along_y = swapped(half_kernels, "section", 2)
-    own_video, along_x, along_y = lax.optimization_barrier([gathered(cuts), along_x, along_y])
+    own_video, along_x, along_y, spatial, temporal = lax.optimization_barrier(
+        [gathered(cuts), along_x, along_y, spatial_weights, temporal_weights]
+    )
     near, far = traded(own_video, 0), traded(own_video, 1)
     mine = [along_x, along_y, swapped(along_x, "section", 2)]
-    shared = mine + [swapped(each) for each in mine]
-    shared = [own_kernels] + shared
-
-    cuts = pl.pallas_call(
-        functools.partial(cotangent_kernel, halo, width),
-        name="cotangent",
-        in_specs=[vmem] * 4,
-        out_specs=[vmem] * group,
-        out_shape=[jax.ShapeDtypeStruct((2, cores * frames_in, rows_in, width, chans), BF16)] * group,
-        scratch_shapes=[pltpu.VMEM((2, cores * frames_in, rows_in, padded, chans), F32)],
-        compiler_params=params,
-    )(cotangent, swapped(cotangent), cot_halo, swapped(cot_halo))
-    near, *cuts = lax.optimization_barrier([near] + list(cuts))
+    rest_kernels = core_half(1 - core, spatial, temporal)
+    shared = [half_kernels, rest_kernels] + mine + [swapped(each) for each in mine]
     videos = [own_video, near, far]
     videos += [swapped(each) for each in videos]
-    cots = [cuts[0]] + [swapped(cuts[i], "space", i) for i in range(1, group)]
+
+    from_far = swapped(high_pair, "space", 2)
+    from_near = swapped(jnp.stack([low[1], from_far[1]]), "space", 1)
+    low = jnp.stack([low[0], from_near[0]])
+    high_pair = jnp.stack([from_far[0], from_near[1]])
+    upper = unit < half
+    cots = [
+        low,
+        high_pair,
+        traded(jnp.where(upper == (odd == 1), low, high_pair), 0),
+        traded(jnp.where(upper == (odd == 0), low, high_pair), 1),
+    ]
 
     geometry = (blocks, cores, group, frames_in, rows_in, halo, tile, width, total_rows, columns)
     frames = cores * frames_in
     high = tile + 2 * halo
-    per_section = (blocks,) + one_half.shape
+    per_section = (blocks,) + half_kernels.shape
+    taps = half_kernels.shape[0]
     all_kernels = (cores,) + per_section
     saved = [
         jax.ShapeDtypeStruct((frames, tile + 2 * block + 2, width, chans), F32)
@@ -394,7 +384,7 @@
     features, hidden, *slopes = pl.pallas_call(
         functools.partial(forward_kernel, geometry),
         name="forward",
-        in_specs=[vmem] * (2 * blocks + 5),
+        in_specs=[vmem] * (2 * blocks + 6),
         out_specs=[vmem] * (2 + blocks),
         out_shape=[
             jax.ShapeDtypeStruct((blocks, frames, tile + 2, own_width, 3 * chans), BF16),
@@ -418,7 +408,7 @@
     keep, give, mine_grad, other_grad = pl.pallas_call(
         functools.partial(backward_kernel, geometry, factor),
         name="backward",
-        in_specs=[vmem] * (3 * blocks + group + 1),
+        in_specs=[vmem] * (3 * blocks + 6),
         out_specs=[vmem] * 4,
         out_shape=[
             jax.ShapeDtypeStruct(per_section, BF16),

time: 83.1 us -> 84.4 us (1.016)
  waiting for transfers between devices: 26.4 us -> 29.6 us
  local copies, waits for them, and re-layouts: 3.75 us -> 1.93 us
  other arithmetic: 0.48 us -> 1.59 us
  starting transfers between devices: 36 us -> 35.1 us
    ppermute x29 -> x27, waiting for transfers between devices: 23.8 us -> 29.6 us  [swapped(): return lax.ppermute(value, axis, [(i, i ^ step) for i in range(count)])]
    ppermute x2 -> x4, starting transfers between devices: 1.26 us -> 4.23 us  [traded(): return lax.ppermute(value, ('section', 'space'), pairs)]
    ppermute x29 -> x27, starting transfers between devices: 33.5 us -> 30.8 us  [swapped(): return lax.ppermute(value, axis, [(i, i ^ step) for i in range(count)])]
    ppermute x2 -> x4, waiting for transfers between devices: 1.87 us -> 0.01 us  [traded(): return lax.ppermute(value, ('section', 'space'), pairs)]
    unnamed x10, local copies, waits for them, and re-layouts: 3.66 us -> 1.81 us
    ppermute x1 -> x0, starting transfers between devices: 1.28 us -> none  [on_device(): cot_halo = lax.ppermute(cotangent, ('section', 'space'), passed)]
    concatenate x0 -> x2, other arithmetic: none -> 1.05 us  [core_half(): whole = jnp.concatenate([spatial[0], temporal[0]], 0)]
  transfers between devices with their start and end apart: 32 -> 31, of which waited for: 14 -> 11; matrix products, arithmetic and copies ran while one was open for 0% -> 2% of each run, Pallas kernels for 9% -> 9%
where the time goes in v10:
time: 84.4 us; the launch traced here: 84.2 us
  starting transfers between devices  35.1 us (42%)
  waiting for transfers between devices  29.6 us (35%)
  Pallas kernels  15 us (18%)
  local copies, waits for them, and re-layouts  1.93 us (2%)
  other arithmetic  1.59 us (2%)
  between operations  0.9 us (1%)
    ppermute x27, starting transfers between devices, swapped(): return lax.ppermute(value, axis, [(i, i ^ step) for i in range(count)])  30.8 us
    ppermute x27, waiting for transfers between devices, swapped(): return lax.ppermute(value, axis, [(i, i ^ step) for i in range(count)])  29.6 us
    pallas_call x1, Pallas kernels, on_device(): pl.pallas_call(functools.partial(forward_kernel, geometry), name='forward...  7.72 us
    pallas_call x1, Pallas kernels, on_device(): pl.pallas_call(functools.partial(backward_kernel, geometry, factor), name...  6.13 us
    ppermute x4, starting transfers between devices, traded(): return lax.ppermute(value, ('section', 'space'), pairs)  4.23 us
    unnamed x10, local copies, waits for them, and re-layouts  1.81 us
  transfers between devices with their start and end apart: 31, of which 11 were waited for; matrix products, arithmetic and copies ran while one was open for 2% of the time, Pallas kernels for 9%

profile of v10, /device:TPU:0, one launch (start us, length us, event | category | flops | bytes accessed | tf_op | source)
XLA Modules:
  0.0 84.2 jit_solution(14979464467929927226)
XLA Ops:
  1.6 3.1 %collective-permute-start = (bf16[2,2,48,128]{3,2,1,0:T(8,128)(2,1)S(1)}, bf16[2,2,48,128]{3,2,1,0:T(8,128)(2,1)S(1)}, u32[]{:S(2)}, u32[]{:S(2)}) collective-permute-start(bf16[2,2,48,128]{3,2,1,0:T(8,128)(2,1)S(1)} %get-tuple-element.40), channel_id=1, source_target_pairs={{0,1},{1,0},{2,3},{3,2},{4,5},{5,4},{6,7},{7,6},{8,9},{9,8},{10,11... | collective-permute-start | bytes 147464 | tf_op jit(solution)/shard_map/ppermute | solution.py:288
  4.7 2.6 %collective-permute-start.1 = (bf16[2,2,48,128]{3,2,1,0:T(8,128)(2,1)S(1)}, bf16[2,2,48,128]{3,2,1,0:T(8,128)(2,1)S(1)}, u32[]{:S(2)}, u32[]{:S(2)}) collective-permute-start(bf16[2,2,48,128]{3,2,1,0:T(8,128)(2,1)S(1)} %get-tuple-element.41), channel_id=1, source_target_pairs={{0,2},{1,3},{2,0},{3,1},{4,6},{5,7},{6,4},{7,5},{8,10},{9,11},{10,... | collective-permute-start | bytes 147464 | tf_op jit(solution)/shard_map/ppermute | solution.py:288
  8.3 1.8 %collective-permute-start.3 = (bf16[6,128,128]{2,1,0:T(8,128)(2,1)S(1)}, bf16[6,128,128]{2,1,0:T(8,128)(2,1)S(1)}, u32[]{:S(2)}, u32[]{:S(2)}) collective-permute-start(bf16[6,128,128]{2,1,0:T(8,128)(2,1)S(1)} %fusion.5.rest_0_), channel_id=1, source_target_pairs={{0,8},{8,0},{16,24},{24,16},{1,9},{9,1},{17,25},{25,17},{2,10},{10... | collective-permute-start | bytes 589832 | tf_op jit(solution)/shard_map/ppermute | solution.py:288
  10.0 1.5 %collective-permute-start.4 = (bf16[6,128,128]{2,1,0:T(8,128)(2,1)S(1)}, bf16[6,128,128]{2,1,0:T(8,128)(2,1)S(1)}, u32[]{:S(2)}, u32[]{:S(2)}) collective-permute-start(bf16[6,128,128]{2,1,0:T(8,128)(2,1)S(1)} %fusion.5.rest_0_), channel_id=1, source_target_pairs={{0,16},{8,24},{16,0},{24,8},{1,17},{9,25},{17,1},{25,9},{2,18},{10... | collective-permute-start | bytes 589832 | tf_op jit(solution)/shard_map/ppermute | solution.py:288
  11.6 1.6 %collective-permute-done.2 = bf16[2,2,48,128]{3,2,1,0:T(8,128)(2,1)S(1)} collective-permute-done((bf16[2,2,48,128]{3,2,1,0:T(8,128)(2,1)S(1)}, bf16[2,2,48,128]{3,2,1,0:T(8,128)(2,1)S(1)}, u32[]{:S(2)}, u32[]{:S(2)}) %collective-permute-start.2) | collective-permute-done | bytes 49184 | tf_op jit(solution)/shard_map/ppermute | solution.py:288
  15.7 1.4 %collective-permute-done.4.rest_3_ = bf16[6,128,128]{2,1,0:T(8,128)(2,1)S(1)} collective-permute-done((bf16[6,128,128]{2,1,0:T(8,128)(2,1)S(1)}, bf16[6,128,128]{2,1,0:T(8,128)(2,1)S(1)}, u32[]{:S(2)}, u32[]{:S(2)}) %collective-permute-start.4) | collective-permute-done | bytes 196640 | tf_op jit(solution)/shard_map/ppermute | solution.py:288
  18.1 4.4 %collective-permute-start.5 = (bf16[6,128,128]{2,1,0:T(8,128)(2,1)S(1)}, bf16[6,128,128]{2,1,0:T(8,128)(2,1)S(1)}, u32[]{:S(2)}, u32[]{:S(2)}) collective-permute-start(bf16[6,128,128]{2,1,0:T(8,128)(2,1)S(1)} %collective-permute-done.3.rest_2_), channel_id=1, source_target_pairs={{0,16},{8,24},{16,0},{24,8},{1,17},{9,25},{17,1},{25,9},{2,18},{10... | collective-permute-start | bytes 589832 | tf_op jit(solution)/shard_map/ppermute | solution.py:288
  23.4 5.2 %collective-permute-done.11 = bf16[2,4,2,32,128]{4,3,2,1,0:T(8,128)(2,1)S(1)} collective-permute-done((bf16[2,4,2,32,128]{4,3,2,1,0:T(8,128)(2,1)S(1)}, bf16[2,4,2,32,128]{4,3,2,1,0:T(8,128)(2,1)S(1)}, u32[]{:S(2)}, u32[]{:S(2)}) %collective-permute-start.11) | collective-permute-done | bytes 131104 | tf_op jit(solution)/shard_map/ppermute | solution.py:288
  28.6 1.3 %collective-permute-done.5.rest_4_ = bf16[6,128,128]{2,1,0:T(8,128)(2,1)S(1)} collective-permute-done((bf16[6,128,128]{2,1,0:T(8,128)(2,1)S(1)}, bf16[6,128,128]{2,1,0:T(8,128)(2,1)S(1)}, u32[]{:S(2)}, u32[]{:S(2)}) %collective-permute-start.5) | collective-permute-done | bytes 196640 | tf_op jit(solution)/shard_map/ppermute | solution.py:288
  30.9 2.5 %collective-permute-start.12 = (bf16[2,4,2,32,128]{4,3,2,1,0:T(8,128)(2,1)S(1)}, bf16[2,4,2,32,128]{4,3,2,1,0:T(8,128)(2,1)S(1)}, u32[]{:S(2)}, u32[]{:S(2)}) collective-permute-start(bf16[2,4,2,32,128]{4,3,2,1,0:T(8,128)(2,1)S(1)} %get-tuple-element.80), channel_id=1, source_target_pairs={{0,8},{1,9},{2,10},{3,11},{8,0},{9,1},{10,2},{11,3},{16,24},{17,25... | collective-permute-start | bytes 393224 | tf_op jit(solution)/shard_map/ppermute | solution.py:314
  34.2 7.7 %forward.1 = (bf16[4,4,10,16,384]{4,3,2,1,0:T(8,128)(2,1)S(1)}, bf16[4,4,8,16,128]{4,3,2,1,0:T(8,128)(2,1)S(1)}, f32[4,10,32,128]{3,2,1,0:T(8,128)S(1)}, f32[4,1...) custom-call(bf16[6,128,128]{2,1,0:T(8,128)(2,1)S(1)} %fusion.5.rest_0_, ...), custom_call_target="tpu_custom_call" | custom-call | flops 6000000000 | bytes 8000000 | tf_op jit(solution)/shard_map/forward/pallas_call | solution.py:384
  41.9 6.1 %backward.1 = (bf16[4,6,128,128]{3,2,1,0:T(8,128)(2,1)S(1)}, bf16[4,6,128,128]{3,2,1,0:T(8,128)(2,1)S(1)}, bf16[4,2,2,16,128]{4,3,2,1,0:T(8,128)(2,1)S(1)}, bf16[4,2,2,16,128]{4,3,2,1,0:T(8,128)(2,1)S(1)}) custom-call(bf16[6,128,128]{2,1,0:T(8,128)(2,1)S(1)} %fusion.5.rest_0_, bf16[6,128,128]{2,1,0:T(8,128)(2,1)S(1)} %fusion.4.rest_1_, ...), custom_call_target="tpu_custom_call" | custom-call | flops 6000000000 | bytes 8000000 | tf_op jit(solution)/shard_map/backward/pallas_call | solution.py:408
  48.2 2.3 %collective-permute-done.19 = bf16[4,6,128,128]{3,2,1,0:T(8,128)(2,1)S(1)} collective-permute-done((bf16[4,6,128,128]{3,2,1,0:T(8,128)(2,1)S(1)}, bf16[4,6,128,128]{3,2,1,0:T(8,128)(2,1)S(1)}, u32[]{:S(2)}, u32[]{:S(2)}) %collective-permute-start.19) | collective-permute-done | bytes 786464 | tf_op jit(solution)/shard_map/ppermute | solution.py:288
  50.9 3.0 %collective-permute-start.20 = (bf16[6,128,128]{2,1,0:T(8,128)(2,1)S(1)}, bf16[6,128,128]{2,1,0:T(8,128)(2,1)S(1)}, u32[]{:S(2)}, u32[]{:S(2)}) collective-permute-start(bf16[6,128,128]{2,1,0:T(8,128)(2,1)S(1)} %get-tuple-element.60), channel_id=1, source_target_pairs={{0,8},{8,0},{16,24},{24,16},{1,9},{9,1},{17,25},{25,17},{2,10},{10... | collective-permute-start | bytes 589832 | tf_op jit(solution)/shard_map/ppermute | solution.py:288
  53.9 1.5 %collective-permute-start.22 = (bf16[6,128,128]{2,1,0:T(8,128)(2,1)S(1)}, bf16[6,128,128]{2,1,0:T(8,128)(2,1)S(1)}, u32[]{:S(2)}, u32[]{:S(2)}) collective-permute-start(bf16[6,128,128]{2,1,0:T(8,128)(2,1)S(1)} %get-tuple-element.62), channel_id=1, source_target_pairs={{0,24},{8,16},{16,8},{24,0},{1,25},{9,17},{17,9},{25,1},{2,26},{10... | collective-permute-start | bytes 589832 | tf_op jit(solution)/shard_map/ppermute | solution.py:288
  56.1 3.5 %collective-permute-start.25 = (bf16[2,2,32,128]{3,2,1,0:T(8,128)(2,1)S(1)}, bf16[2,2,32,128]{3,2,1,0:T(8,128)(2,1)S(1)}, u32[]{:S(2)}, u32[]{:S(2)}) collective-permute-start(bf16[2,2,32,128]{3,2,1,0:T(8,128)(2,1)S(1)} %get-tuple-element.84), channel_id=1, source_target_pairs={{0,2},{1,3},{2,0},{3,1},{4,6},{5,7},{6,4},{7,5},{8,10},{9,11},{10,... | collective-permute-start | bytes 98312 | tf_op jit(solution)/shard_map/ppermute | solution.py:288
  59.6 3.5 %collective-permute-start.26 = (bf16[2,2,32,128]{3,2,1,0:T(8,128)(2,1)S(1)}, bf16[2,2,32,128]{3,2,1,0:T(8,128)(2,1)S(1)}, u32[]{:S(2)}, u32[]{:S(2)}) collective-permute-start(bf16[2,2,32,128]{3,2,1,0:T(8,128)(2,1)S(1)} %get-tuple-element.81), channel_id=1, source_target_pairs={{0,3},{1,2},{2,1},{3,0},{4,7},{5,6},{6,5},{7,4},{8,11},{9,10},{10,... | collective-permute-start | bytes 98312 | tf_op jit(solution)/shard_map/ppermute | solution.py:288
  63.1 2.2 %collective-permute-done.26 = bf16[2,2,32,128]{3,2,1,0:T(8,128)(2,1)S(1)} collective-permute-done((bf16[2,2,32,128]{3,2,1,0:T(8,128)(2,1)S(1)}, bf16[2,2,32,128]{3,2,1,0:T(8,128)(2,1)S(1)}, u32[]{:S(2)}, u32[]{:S(2)}) %collective-permute-start.26) | collective-permute-done | bytes 32800 | tf_op jit(solution)/shard_map/ppermute | solution.py:288
  65.8 4.3 %collective-permute-done.27 = bf16[384,128]{1,0:T(8,128)(2,1)S(1)} collective-permute-done((bf16[384,128]{1,0:T(8,128)(2,1)S(1)}, bf16[384,128]{1,0:T(8,128)(2,1)S(1)}, u32[]{:S(2)}, u32[]{:S(2)}) %collective-permute-start.27) | collective-permute-done | bytes 98336 | tf_op jit(solution)/shard_map/ppermute | solution.py:288
  70.2 2.1 %collective-permute-start.28 = (bf16[384,128]{1,0:T(8,128)(2,1)S(1)}, bf16[384,128]{1,0:T(8,128)(2,1)S(1)}, u32[]{:S(2)}, u32[]{:S(2)}) collective-permute-start(bf16[384,128]{1,0:T(8,128)(2,1)S(1)} %fusion.6), channel_id=1, source_target_pairs={{0,2},{1,3},{2,0},{3,1},{4,6},{5,7},{6,4},{7,5},{8,10},{9,11},{10,... | collective-permute-start | bytes 294920 | tf_op jit(solution)/shard_map/ppermute | solution.py:288
  72.3 4.5 %collective-permute-done.28 = bf16[384,128]{1,0:T(8,128)(2,1)S(1)} collective-permute-done((bf16[384,128]{1,0:T(8,128)(2,1)S(1)}, bf16[384,128]{1,0:T(8,128)(2,1)S(1)}, u32[]{:S(2)}, u32[]{:S(2)}) %collective-permute-start.28) | collective-permute-done | bytes 98336 | tf_op jit(solution)/shard_map/ppermute | solution.py:288
  77.1 4.4 %collective-permute-done.29 = bf16[384,128]{1,0:T(8,128)(2,1)S(1)} collective-permute-done((bf16[384,128]{1,0:T(8,128)(2,1)S(1)}, bf16[384,128]{1,0:T(8,128)(2,1)S(1)}, u32[]{:S(2)}, u32[]{:S(2)}) %collective-permute-start.29) | collective-permute-done | bytes 98336 | tf_op jit(solution)/shard_map/ppermute | solution.py:288
  81.7 1.4 %collective-permute-done.30.other_ref = bf16[2,384,128]{2,1,0:T(8,128)(2,1)S(1)} collective-permute-done((bf16[2,384,128]{2,1,0:T(8,128)(2,1)S(1)}, bf16[2,384,128]{2,1,0:T(8,128)(2,1)S(1)}, u32[]{:S(2)}, u32[]{:S(2)}) %collective-permute-start.30) | collective-permute-done | bytes 196640 | tf_op jit(solution)/shard_map/ppermute | solution.py:288
  83.1 1.1 %closing.1 = (f32[1,9,128,128]{3,2,1,0:T(8,128)}, f32[1,3,128,128]{3,2,1,0:T(8,128)}) custom-call(bf16[2,384,128]{2,1,0:T(8,128)(2,1)S(1)} %pad_maximum_fusion.1.mine_ref, bf16[2,384,128]{2,1,0:T(8,128)(2,1)S(1)} %collective-permute-done.30.other_ref), custom_call_target="tpu_custom_call" | custom-call | tf_op jit(solution)/shard_map/closing/pallas_call | solution.py:460
  (74 shorter events, 10.3 us)
Async XLA Ops:
  1.6 8.5 %collective-permute-start = (bf16[2,2,48,128]{3,2,1,0:T(8,128)(2,1)S(1)}, bf16[2,2,48,128]{3,2,1,0:T(8,128)(2,1)S(1)}, u32[]{:S(2)}, u32[]{:S(2)}) collective-permute-start(bf16[2,2,48,128]{3,2,1,0:T(8,128)(2,1)S(1)} %get-tuple-element.40), channel_id=1, source_target_pairs={{0,1},{1,0},{2,3},{3,2},{4,5},{5,4},{6,7},{7,6},{8,9},{9,8},{10,11... | collective-permute-start | bytes 147464 | tf_op jit(solution)/shard_map/ppermute | solution.py:288
  4.7 6.9 %collective-permute-start.1 = (bf16[2,2,48,128]{3,2,1,0:T(8,128)(2,1)S(1)}, bf16[2,2,48,128]{3,2,1,0:T(8,128)(2,1)S(1)}, u32[]{:S(2)}, u32[]{:S(2)}) collective-permute-start(bf16[2,2,48,128]{3,2,1,0:T(8,128)(2,1)S(1)} %get-tuple-element.41), channel_id=1, source_target_pairs={{0,2},{1,3},{2,0},{3,1},{4,6},{5,7},{6,4},{7,5},{8,10},{9,11},{10,... | collective-permute-start | bytes 147464 | tf_op jit(solution)/shard_map/ppermute | solution.py:288
  7.3 5.9 %collective-permute-start.2 = (bf16[2,2,48,128]{3,2,1,0:T(8,128)(2,1)S(1)}, bf16[2,2,48,128]{3,2,1,0:T(8,128)(2,1)S(1)}, u32[]{:S(2)}, u32[]{:S(2)}) collective-permute-start(bf16[2,2,48,128]{3,2,1,0:T(8,128)(2,1)S(1)} %get-tuple-element.42), channel_id=1, source_target_pairs={{0,3},{1,2},{2,1},{3,0},{4,7},{5,6},{6,5},{7,4},{8,11},{9,10},{10,... | collective-permute-start | bytes 147464 | tf_op jit(solution)/shard_map/ppermute | solution.py:288
  7.3 5.9 %collective-permute-start.9 = (bf16[2,2,128,128]{3,2,1,0:T(8,128)(2,1)}, bf16[2,2,128,128]{3,2,1,0:T(8,128)(2,1)S(1)}, u32[]{:S(2)}, u32[]{:S(2)}) collective-permute-start(bf16[2,2,128,128]{3,2,1,0:T(8,128)(2,1)} %mine_ref.1), channel_id=1, source_target_pairs={{0,4},{4,0},{1,5},{5,1},{2,6},{6,2},{3,7},{7,3},{8,12},{12,8},{9,1... | collective-permute-start | bytes 393224 | tf_op jit(solution)/shard_map/ppermute | solution.py:288
  8.3 7.4 %collective-permute-start.3 = (bf16[6,128,128]{2,1,0:T(8,128)(2,1)S(1)}, bf16[6,128,128]{2,1,0:T(8,128)(2,1)S(1)}, u32[]{:S(2)}, u32[]{:S(2)}) collective-permute-start(bf16[6,128,128]{2,1,0:T(8,128)(2,1)S(1)} %fusion.5.rest_0_), channel_id=1, source_target_pairs={{0,8},{8,0},{16,24},{24,16},{1,9},{9,1},{17,25},{25,17},{2,10},{10... | collective-permute-start | bytes 589832 | tf_op jit(solution)/shard_map/ppermute | solution.py:288
  10.0 7.0 %collective-permute-start.4 = (bf16[6,128,128]{2,1,0:T(8,128)(2,1)S(1)}, bf16[6,128,128]{2,1,0:T(8,128)(2,1)S(1)}, u32[]{:S(2)}, u32[]{:S(2)}) collective-permute-start(bf16[6,128,128]{2,1,0:T(8,128)(2,1)S(1)} %fusion.5.rest_0_), channel_id=1, source_target_pairs={{0,16},{8,24},{16,0},{24,8},{1,17},{9,25},{17,1},{25,9},{2,18},{10... | collective-permute-start | bytes 589832 | tf_op jit(solution)/shard_map/ppermute | solution.py:288
  14.2 8.4 %collective-permute-start.10 = (bf16[2,4,2,32,128]{4,3,2,1,0:T(8,128)(2,1)S(1)}, bf16[2,4,2,32,128]{4,3,2,1,0:T(8,128)(2,1)S(1)}, u32[]{:S(2)}, u32[]{:S(2)}) collective-permute-start(bf16[2,4,2,32,128]{4,3,2,1,0:T(8,128)(2,1)S(1)} %get-tuple-element.48), channel_id=1, source_target_pairs={{0,2},{1,3},{2,0},{3,1},{4,6},{5,7},{6,4},{7,5},{8,10},{9,11},{10,... | collective-permute-start | bytes 393224 | tf_op jit(solution)/shard_map/ppermute | solution.py:288
  17.1 12.8 %collective-permute-start.14 = (bf16[4,2,2,48,128]{4,3,2,1,0:T(8,128)(2,1)S(1)}, bf16[4,2,2,48,128]{4,3,2,1,0:T(8,128)(2,1)S(1)}, u32[]{:S(2)}, u32[]{:S(2)}) collective-permute-start(bf16[4,2,2,48,128]{4,3,2,1,0:T(8,128)(2,1)S(1)} %pad_maximum_fusion.rest_8_), channel_id=1, source_target_pairs={{0,8},{1,9},{2,10},{3,11},{8,0},{9,1},{10,2},{11,3},{16,24},{17,25... | collective-permute-start | bytes 589832 | tf_op jit(solution)/shard_map/ppermute | solution.py:314
  17.5 12.9 %collective-permute-start.15 = (bf16[4,2,2,48,128]{4,3,2,1,0:T(8,128)(2,1)S(1)}, bf16[4,2,2,48,128]{4,3,2,1,0:T(8,128)(2,1)S(1)}, u32[]{:S(2)}, u32[]{:S(2)}) collective-permute-start(bf16[4,2,2,48,128]{4,3,2,1,0:T(8,128)(2,1)S(1)} %pad_maximum_fusion.rest_8_), channel_id=1, source_target_pairs={{8,16},{9,17},{10,18},{11,19},{16,8},{17,9},{18,10},{19,11},{12,20... | collective-permute-start | bytes 589832 | tf_op jit(solution)/shard_map/ppermute | solution.py:314
  18.1 11.7 %collective-permute-start.5 = (bf16[6,128,128]{2,1,0:T(8,128)(2,1)S(1)}, bf16[6,128,128]{2,1,0:T(8,128)(2,1)S(1)}, u32[]{:S(2)}, u32[]{:S(2)}) collective-permute-start(bf16[6,128,128]{2,1,0:T(8,128)(2,1)S(1)} %collective-permute-done.3.rest_2_), channel_id=1, source_target_pairs={{0,16},{8,24},{16,0},{24,8},{1,17},{9,25},{17,1},{25,9},{2,18},{10... | collective-permute-start | bytes 589832 | tf_op jit(solution)/shard_map/ppermute | solution.py:288
  22.5 7.9 %collective-permute-start.6 = (bf16[6,128,128]{2,1,0:T(8,128)(2,1)S(1)}, bf16[6,128,128]{2,1,0:T(8,128)(2,1)S(1)}, u32[]{:S(2)}, u32[]{:S(2)}) collective-permute-start(bf16[6,128,128]{2,1,0:T(8,128)(2,1)S(1)} %collective-permute-done.3.rest_2_), channel_id=1, source_target_pairs={{0,4},{4,0},{1,5},{5,1},{2,6},{6,2},{3,7},{7,3},{8,12},{12,8},{9,1... | collective-permute-start | bytes 589832 | tf_op jit(solution)/shard_map/ppermute | solution.py:288
  22.6 6.0 %collective-permute-start.11 = (bf16[2,4,2,32,128]{4,3,2,1,0:T(8,128)(2,1)S(1)}, bf16[2,4,2,32,128]{4,3,2,1,0:T(8,128)(2,1)S(1)}, u32[]{:S(2)}, u32[]{:S(2)}) collective-permute-start(bf16[2,4,2,32,128]{4,3,2,1,0:T(8,128)(2,1)S(1)} %pad_maximum_fusion.2), channel_id=1, source_target_pairs={{0,1},{1,0},{2,3},{3,2},{4,5},{5,4},{6,7},{7,6},{8,9},{9,8},{10,11... | collective-permute-start | bytes 393224 | tf_op jit(solution)/shard_map/ppermute | solution.py:288
  29.8 4.3 %collective-permute-start.8 = (bf16[6,128,128]{2,1,0:T(8,128)(2,1)S(1)}, bf16[6,128,128]{2,1,0:T(8,128)(2,1)S(1)}, u32[]{:S(2)}, u32[]{:S(2)}) collective-permute-start(bf16[6,128,128]{2,1,0:T(8,128)(2,1)S(1)} %collective-permute-done.5.rest_4_), channel_id=1, source_target_pairs={{0,4},{4,0},{1,5},{5,1},{2,6},{6,2},{3,7},{7,3},{8,12},{12,8},{9,1... | collective-permute-start | bytes 589832 | tf_op jit(solution)/shard_map/ppermute | solution.py:288
  30.9 11.0 %collective-permute-start.12 = (bf16[2,4,2,32,128]{4,3,2,1,0:T(8,128)(2,1)S(1)}, bf16[2,4,2,32,128]{4,3,2,1,0:T(8,128)(2,1)S(1)}, u32[]{:S(2)}, u32[]{:S(2)}) collective-permute-start(bf16[2,4,2,32,128]{4,3,2,1,0:T(8,128)(2,1)S(1)} %get-tuple-element.80), channel_id=1, source_target_pairs={{0,8},{1,9},{2,10},{3,11},{8,0},{9,1},{10,2},{11,3},{16,24},{17,25... | collective-permute-start | bytes 393224 | tf_op jit(solution)/shard_map/ppermute | solution.py:314
  33.5 8.4 %collective-permute-start.13 = (bf16[2,4,2,32,128]{4,3,2,1,0:T(8,128)(2,1)S(1)}, bf16[2,4,2,32,128]{4,3,2,1,0:T(8,128)(2,1)S(1)}, u32[]{:S(2)}, u32[]{:S(2)}) collective-permute-start(bf16[2,4,2,32,128]{4,3,2,1,0:T(8,128)(2,1)S(1)} %get-tuple-element.79), channel_id=1, source_target_pairs={{8,16},{9,17},{10,18},{11,19},{16,8},{17,9},{18,10},{19,11},{12,20... | collective-permute-start | bytes 393224 | tf_op jit(solution)/shard_map/ppermute | solution.py:314
  50.7 4.7 %collective-permute-start.23 = (bf16[4,2,2,16,128]{4,3,2,1,0:T(8,128)(2,1)S(1)}, bf16[4,2,2,16,128]{4,3,2,1,0:T(8,128)(2,1)S(1)}, u32[]{:S(2)}, u32[]{:S(2)}) collective-permute-start(bf16[4,2,2,16,128]{4,3,2,1,0:T(8,128)(2,1)S(1)} %get-tuple-element.64), channel_id=1, source_target_pairs={{0,4},{4,0},{1,5},{5,1},{2,6},{6,2},{3,7},{7,3},{8,12},{12,8},{9,1... | collective-permute-start | bytes 196616 | tf_op jit(solution)/shard_map/ppermute | solution.py:288
  50.9 14.5 %collective-permute-start.20 = (bf16[6,128,128]{2,1,0:T(8,128)(2,1)S(1)}, bf16[6,128,128]{2,1,0:T(8,128)(2,1)S(1)}, u32[]{:S(2)}, u32[]{:S(2)}) collective-permute-start(bf16[6,128,128]{2,1,0:T(8,128)(2,1)S(1)} %get-tuple-element.60), channel_id=1, source_target_pairs={{0,8},{8,0},{16,24},{24,16},{1,9},{9,1},{17,25},{25,17},{2,10},{10... | collective-permute-start | bytes 589832 | tf_op jit(solution)/shard_map/ppermute | solution.py:288
  53.9 11.5 %collective-permute-start.21 = (bf16[6,128,128]{2,1,0:T(8,128)(2,1)S(1)}, bf16[6,128,128]{2,1,0:T(8,128)(2,1)S(1)}, u32[]{:S(2)}, u32[]{:S(2)}) collective-permute-start(bf16[6,128,128]{2,1,0:T(8,128)(2,1)S(1)} %get-tuple-element.61), channel_id=1, source_target_pairs={{0,16},{8,24},{16,0},{24,8},{1,17},{9,25},{17,1},{25,9},{2,18},{10... | collective-permute-start | bytes 589832 | tf_op jit(solution)/shard_map/ppermute | solution.py:288
  53.9 11.5 %collective-permute-start.22 = (bf16[6,128,128]{2,1,0:T(8,128)(2,1)S(1)}, bf16[6,128,128]{2,1,0:T(8,128)(2,1)S(1)}, u32[]{:S(2)}, u32[]{:S(2)}) collective-permute-start(bf16[6,128,128]{2,1,0:T(8,128)(2,1)S(1)} %get-tuple-element.62), channel_id=1, source_target_pairs={{0,24},{8,16},{16,8},{24,0},{1,25},{9,17},{17,9},{25,1},{2,26},{10... | collective-permute-start | bytes 589832 | tf_op jit(solution)/shard_map/ppermute | solution.py:288
  56.1 7.0 %collective-permute-start.25 = (bf16[2,2,32,128]{3,2,1,0:T(8,128)(2,1)S(1)}, bf16[2,2,32,128]{3,2,1,0:T(8,128)(2,1)S(1)}, u32[]{:S(2)}, u32[]{:S(2)}) collective-permute-start(bf16[2,2,32,128]{3,2,1,0:T(8,128)(2,1)S(1)} %get-tuple-element.84), channel_id=1, source_target_pairs={{0,2},{1,3},{2,0},{3,1},{4,6},{5,7},{6,4},{7,5},{8,10},{9,11},{10,... | collective-permute-start | bytes 98312 | tf_op jit(solution)/shard_map/ppermute | solution.py:288
  59.6 5.7 %collective-permute-start.26 = (bf16[2,2,32,128]{3,2,1,0:T(8,128)(2,1)S(1)}, bf16[2,2,32,128]{3,2,1,0:T(8,128)(2,1)S(1)}, u32[]{:S(2)}, u32[]{:S(2)}) collective-permute-start(bf16[2,2,32,128]{3,2,1,0:T(8,128)(2,1)S(1)} %get-tuple-element.81), channel_id=1, source_target_pairs={{0,3},{1,2},{2,1},{3,0},{4,7},{5,6},{6,5},{7,4},{8,11},{9,10},{10,... | collective-permute-start | bytes 98312 | tf_op jit(solution)/shard_map/ppermute | solution.py:288
  65.5 4.7 %collective-permute-start.27 = (bf16[384,128]{1,0:T(8,128)(2,1)S(1)}, bf16[384,128]{1,0:T(8,128)(2,1)S(1)}, u32[]{:S(2)}, u32[]{:S(2)}) collective-permute-start(bf16[384,128]{1,0:T(8,128)(2,1)S(1)} %dynamic-slice_bitcast_fusion), channel_id=1, source_target_pairs={{0,1},{1,0},{2,3},{3,2},{4,5},{5,4},{6,7},{7,6},{8,9},{9,8},{10,11... | collective-permute-start | bytes 294920 | tf_op jit(solution)/shard_map/ppermute | solution.py:288
  70.2 6.6 %collective-permute-start.28 = (bf16[384,128]{1,0:T(8,128)(2,1)S(1)}, bf16[384,128]{1,0:T(8,128)(2,1)S(1)}, u32[]{:S(2)}, u32[]{:S(2)}) collective-permute-start(bf16[384,128]{1,0:T(8,128)(2,1)S(1)} %fusion.6), channel_id=1, source_target_pairs={{0,2},{1,3},{2,0},{3,1},{4,6},{5,7},{6,4},{7,5},{8,10},{9,11},{10,... | collective-permute-start | bytes 294920 | tf_op jit(solution)/shard_map/ppermute | solution.py:288
  76.9 4.7 %collective-permute-start.29 = (bf16[384,128]{1,0:T(8,128)(2,1)S(1)}, bf16[384,128]{1,0:T(8,128)(2,1)S(1)}, u32[]{:S(2)}, u32[]{:S(2)}) collective-permute-start(bf16[384,128]{1,0:T(8,128)(2,1)S(1)} %add_convert_fusion.5), channel_id=1, source_target_pairs={{0,1},{1,0},{2,3},{3,2},{4,5},{5,4},{6,7},{7,6},{8,9},{9,8},{10,11... | collective-permute-start | bytes 294920 | tf_op jit(solution)/shard_map/ppermute | solution.py:288
  (12 other events, 69.6 us)

commit v11 on v10

--- a/solution.py
+++ b/solution.py
@@ -28,12 +28,65 @@
     return w_ref[tap // taps, block, tap % taps]
 
 
-def rows_of(w_ref, block, first, last):
-    return jnp.concatenate([kernel_of(w_ref, block, tap) for tap in range(first, last)], 0)
-
-
-def lanes_of(w_ref, block, order):
-    return jnp.concatenate([kernel_of(w_ref, block, tap) for tap in order], 1)
+def pair_rows(w_ref, block, pair_ref):
+    chans = w_ref.shape[-1]
+    for source in range(4):
+        for target in range(2):
+            ky = source - target
+            for kx in range(3):
+                at = (3 * source + kx) * chans
+                tile = kernel_of(w_ref, block, 3 * ky + kx) if 0 <= ky < 3 else jnp.zeros((chans, chans), BF16)
+                pair_ref[at : at + chans, target * chans : (target + 1) * chans] = tile
+
+
+def pair_rows_back(w_ref, block, pair_ref):
+    chans = w_ref.shape[-1]
+    for source in range(4):
+        for target in range(2):
+            ky = 2 + target - source
+            for kx in range(3):
+                at = (3 * source + kx) * chans
+                tile = kernel_of(w_ref, block, 3 * ky + kx) if 0 <= ky < 3 else jnp.zeros((chans, chans), BF16)
+                pair_ref[target * chans : (target + 1) * chans, at : at + chans] = tile
+
+
+def pair_frames(w_ref, block, first, count):
+    chans = w_ref.shape[-1]
+    columns = []
+    for target in (count - 2, count - 1):
+        tiles = []
+        for source in range(count):
+            kt = source - target + 2
+            tiles.append(kernel_of(w_ref, block, 9 + kt) if 0 <= kt < 3 else jnp.zeros((chans, chans), BF16))
+        columns.append(jnp.concatenate(tiles, 0))
+    return jnp.concatenate(columns, 1)
+
+
+def pair_frames_back(w_ref, block, count):
+    chans = w_ref.shape[-1]
+    rows = []
+    for target in range(2):
+        tiles = []
+        for source in range(count):
+            kt = 2 - (source - target)
+            tiles.append(kernel_of(w_ref, block, 9 + kt) if 0 <= kt < 3 else jnp.zeros((chans, chans), BF16))
+        rows.append(jnp.concatenate(tiles, 1))
+    return jnp.concatenate(rows, 0)
+
+
+def row_pairs(ref, frame, first, pairs):
+    width, lanes = ref.shape[2:]
+    rows = []
+    for start in (first, first + 2):
+        value = ref[frame, start : start + 2 * pairs].reshape(pairs, 2, width, lanes)
+        rows += [value[:, 0], value[:, 1]]
+    return jnp.concatenate(rows, 2).reshape(pairs * width, 4 * lanes)
+
+
+def woven(value, width):
+    chans = value.shape[1] // 2
+    split = [value[:, i * chans : (i + 1) * chans].reshape(-1, 1, width, chans) for i in range(2)]
+    return jnp.concatenate(split, 1).reshape(-1, chans)
 
 
 def placed(group):
@@ -106,7 +159,7 @@
     arrived, rest = rest[:6], rest[6:]
     xo_ref, ho_ref = rest[:2]
     d_refs = rest[2 : 2 + blocks]
-    x_ref, h_ref, mask_ref, w_ref, start_ref = rest[2 + blocks :]
+    x_ref, h_ref, mask_ref, w_ref, start_ref, pair_ref = rest[2 + blocks :]
     place_kernels(core, section, w_ref, *shared[:2], shared[2 : 1 + blocks], shared[1 + blocks :])
     frames = cores * frames_in
     high = tile + 2 * halo
@@ -148,17 +201,12 @@
     for block in range(blocks):
         first, last = block + 1, high - block - 1
         count = last - first
-        spatial = rows_of(w_ref, block, 0, 9)
+        pair_rows(w_ref, block, pair_ref)
         mask = mask_ref[first:last].reshape(count * width, chans)
         for frame in range(frames):
-            taps = jnp.concatenate(
-                [
-                    x_ref[frame, first - 1 + ky : last - 1 + ky].reshape(count * width, 3 * chans)
-                    for ky in range(3)
-                ],
-                1,
-            )
-            before = jnp.dot(taps, spatial, preferred_element_type=F32)
+            taps = row_pairs(x_ref, frame, first - 1, count // 2)
+            before = jnp.dot(taps, pair_ref[...], preferred_element_type=F32)
+            before = woven(before, width)
             sigma = 1.0 / (1.0 + jnp.exp(-before))
             hidden = before * sigma * mask
             slope = (sigma * (1.0 + before * (1.0 - sigma))) * mask
@@ -172,21 +220,22 @@
             ]
         if block + 1 == blocks:
             break
-        for frame in range(frames):
-            offsets = [kt for kt in range(3) if frame + kt - 2 >= 0]
+        for frame in range(0, frames, 2):
+            start = max(frame - 2, 0)
             timeline = jnp.concatenate(
                 [
-                    h_ref[frame + kt - 2, first:last].reshape(count * width, chans)
-                    for kt in offsets
+                    h_ref[each, first:last].reshape(count * width, chans)
+                    for each in range(start, frame + 2)
                 ],
                 1,
             )
-            mixed = jnp.dot(
-                timeline, rows_of(w_ref, block, 9 + offsets[0], 12), preferred_element_type=F32
-            )
-            old = x_ref[frame, first:last, :, chans : 2 * chans].astype(F32)
-            new = old.reshape(count * width, chans) + mixed
-            keep(block + 1, frame, new.astype(BF16).astype(F32), first)
+            weights = pair_frames(w_ref, block, start, frame + 2 - start)
+            both = jnp.dot(timeline, weights, preferred_element_type=F32)
+            for inner in range(2):
+                mixed = both[:, inner * chans : (inner + 1) * chans]
+                old = x_ref[frame + inner, first:last, :, chans : 2 * chans].astype(F32)
+                new = old.reshape(count * width, chans) + mixed
+                keep(block + 1, frame + inner, new.astype(BF16).astype(F32), first)
 
 
 def backward_kernel(geometry, factor, *rest):
@@ -197,7 +246,7 @@
     xo_ref, ho_ref = rest[:2]
     d_refs = rest[2 : 2 + blocks]
     keep_ref, give_ref, mine_out, other_out = rest[2 + blocks : 6 + blocks]
-    g_ref, da_ref, dao_ref, go_ref, w_ref, grad_ref, out_ref = rest[6 + blocks :]
+    g_ref, da_ref, dao_ref, go_ref, w_ref, grad_ref, out_ref, pair_ref = rest[6 + blocks :]
     place_kernels(core, section, w_ref, *shared[:2], shared[2 : 1 + blocks], shared[1 + blocks :])
     frames = cores * frames_in
     chans = w_ref.shape[-1]
@@ -228,15 +277,21 @@
             go_ref[frame] = g_ref[frame, rim : rim + tile].astype(F32)[
                 :, own_cols[0] : own_cols[1]
             ].astype(BF16)
-            offsets = [kt for kt in (2, 1, 0) if frame + 2 - kt < frames]
+        pair_rows_back(w_ref, block, pair_ref)
+        hiddens = []
+        for frame in range(0, frames, 2):
+            stop = min(frame + 4, frames)
             ahead = jnp.concatenate(
                 [
-                    g_ref[frame + 2 - kt, first:last].reshape(count * width, chans)
-                    for kt in offsets
+                    g_ref[each, first:last].reshape(count * width, chans)
+                    for each in range(frame, stop)
                 ],
                 1,
             )
-            hidden = dot_t(ahead, lanes_of(w_ref, block, [9 + kt for kt in offsets]))
+            both = dot_t(ahead, pair_frames_back(w_ref, block, stop - frame))
+            hiddens += [both[:, :chans], both[:, chans:]]
+        for frame in range(frames):
+            hidden = hiddens[frame]
             slope = d_refs[block][frame].reshape(count * width, chans)
             value = (hidden * slope).astype(BF16).astype(F32)
             triple = [rolled(value, -1), value, rolled(value, 1)]
@@ -247,16 +302,8 @@
             ].astype(BF16)
         for frame in range(frames):
             inner = count - 2
-            taps = jnp.concatenate(
-                [
-                    da_ref[frame, first + 2 - ky : first + 2 - ky + inner].reshape(
-                        inner * width, 3 * chans
-                    )
-                    for ky in range(3)
-                ],
-                1,
-            )
-            back = dot_t(taps, lanes_of(w_ref, block, range(9)))
+            taps = row_pairs(da_ref, frame, first, inner // 2)
+            back = woven(dot_t(taps, pair_ref[...]), width)
             old = g_ref[frame, first + 1 : last - 1].astype(F32).reshape(inner * width, chans)
             new = (old + back).astype(BF16)
             if block:
@@ -341,17 +388,19 @@
         taps = whole.shape[0] // cores
         return lax.dynamic_slice_in_dim(whole, which * taps, taps, 0)
 
-    half_kernels = core_half(core, spatial_weights, temporal_weights)
+    _, spatial, temporal = lax.optimization_barrier([cuts[0], spatial_weights, temporal_weights])
+    half_kernels = core_half(core, spatial, temporal)
 
     def gathered(pieces):
         return jnp.stack([pieces[0]] + [swapped(pieces[i], "space", i) for i in range(1, group)])
 
     along_x = swapped(half_kernels, "section", 1)
     along_y = swapped(half_kernels, "section", 2)
-    own_video, along_x, along_y, spatial, temporal = lax.optimization_barrier(
-        [gathered(cuts), along_x, along_y, spatial_weights, temporal_weights]
+    own_video = gathered(cuts)
+    near, far = traded(own_video, 0), traded(own_video, 1)
+    _, along_x, along_y, high_pair, spatial, temporal = lax.optimization_barrier(
+        [own_video, along_x, along_y, high_pair, spatial_weights, temporal_weights]
     )
-    near, far = traded(own_video, 0), traded(own_video, 1)
     mine = [along_x, along_y, swapped(along_x, "section", 2)]
     rest_kernels = core_half(1 - core, spatial, temporal)
     shared = [half_kernels, rest_kernels] + mine + [swapped(each) for each in mine]
@@ -397,6 +446,7 @@
             pltpu.VMEM((high, width, chans), F32),
             pltpu.VMEM(all_kernels, BF16),
             pltpu.VMEM((frames, high, width, chans), BF16),
+            pltpu.VMEM((12 * chans, 2 * chans), BF16),
         ],
         compiler_params=params,
         cost_estimate=cost,
@@ -424,6 +474,7 @@
             pltpu.VMEM(all_kernels, BF16),
             pltpu.VMEM(all_kernels, BF16),
             pltpu.VMEM((frames, tile, own_width, chans), BF16),
+            pltpu.VMEM((2 * chans, 12 * chans), BF16),
         ],
         compiler_params=params,
         cost_estimate=cost,

time: 84.4 us -> 87.1 us (1.032)
  waiting for transfers between devices: 29.6 us -> 37.2 us
  starting transfers between devices: 35.1 us -> 30.4 us
    ppermute x27, waiting for transfers between devices: 29.6 us -> 37.1 us  [swapped(): return lax.ppermute(value, axis, [(i, i ^ step) for i in range(count)])]
    ppermute x27, starting transfers between devices: 30.8 us -> 25.2 us  [swapped(): return lax.ppermute(value, axis, [(i, i ^ step) for i in range(count)])]
    pallas_call x1, Pallas kernels: 7.72 us -> 6.48 us  [on_device(): pl.pallas_call(functools.partial(forward_kernel, geometry), name='forward...]
    ppermute x4, starting transfers between devices: 4.23 us -> 5.19 us  [traded(): return lax.ppermute(value, ('section', 'space'), pairs)]
    pallas_call x1, Pallas kernels: 6.13 us -> 7.03 us  [on_device(): pl.pallas_call(functools.partial(backward_kernel, geometry, factor), name...]
  transfers between devices with their start and end apart: 31 -> 31, of which waited for: 11 -> 12; matrix products, arithmetic and copies ran while one was open for 2% -> 0% of each run, Pallas kernels for 9% -> 8%
where the time goes in v11:
time: 87.1 us; the launch traced here: 86.9 us
  waiting for transfers between devices  37.2 us (43%)
  starting transfers between devices  30.4 us (35%)
  Pallas kernels  14.7 us (17%)
  local copies, waits for them, and re-layouts  1.94 us (2%)
  other arithmetic  1.65 us (2%)
  between operations  1.07 us (1%)
    ppermute x27, waiting for transfers between devices, swapped(): return lax.ppermute(value, axis, [(i, i ^ step) for i in range(count)])  37.1 us
    ppermute x27, starting transfers between devices, swapped(): return lax.ppermute(value, axis, [(i, i ^ step) for i in range(count)])  25.2 us
    pallas_call x1, Pallas kernels, on_device(): pl.pallas_call(functools.partial(backward_kernel, geometry, factor), name...  7.03 us
    pallas_call x1, Pallas kernels, on_device(): pl.pallas_call(functools.partial(forward_kernel, geometry), name='forward...  6.48 us
    ppermute x4, starting transfers between devices, traded(): return lax.ppermute(value, ('section', 'space'), pairs)  5.19 us
    unnamed x10, local copies, waits for them, and re-layouts  1.81 us
  transfers between devices with their start and end apart: 31, of which 12 were waited for; matrix products, arithmetic and copies ran while one was open for 0% of the time, Pallas kernels for 8%

profile of v11, /device:TPU:0, one launch (start us, length us, event | category | flops | bytes accessed | tf_op | source)
XLA Modules:
  0.0 86.9 jit_solution(17151687420174909277)
XLA Ops:
  2.6 3.0 %collective-permute-start.3 = (bf16[6,128,128]{2,1,0:T(8,128)(2,1)S(1)}, bf16[6,128,128]{2,1,0:T(8,128)(2,1)S(1)}, u32[]{:S(2)}, u32[]{:S(2)}) collective-permute-start(bf16[6,128,128]{2,1,0:T(8,128)(2,1)S(1)} %fusion.5.rest_0_), channel_id=1, source_target_pairs={{0,8},{8,0},{16,24},{24,16},{1,9},{9,1},{17,25},{25,17},{2,10},{10... | collective-permute-start | bytes 589832 | tf_op jit(solution)/shard_map/ppermute | solution.py:335
  5.6 1.5 %collective-permute-start.4 = (bf16[6,128,128]{2,1,0:T(8,128)(2,1)S(1)}, bf16[6,128,128]{2,1,0:T(8,128)(2,1)S(1)}, u32[]{:S(2)}, u32[]{:S(2)}) collective-permute-start(bf16[6,128,128]{2,1,0:T(8,128)(2,1)S(1)} %fusion.5.rest_0_), channel_id=1, source_target_pairs={{0,16},{8,24},{16,0},{24,8},{1,17},{9,25},{17,1},{25,9},{2,18},{10... | collective-permute-start | bytes 589832 | tf_op jit(solution)/shard_map/ppermute | solution.py:335
  7.2 1.6 %collective-permute-start = (bf16[2,2,48,128]{3,2,1,0:T(8,128)(2,1)S(1)}, bf16[2,2,48,128]{3,2,1,0:T(8,128)(2,1)S(1)}, u32[]{:S(2)}, u32[]{:S(2)}) collective-permute-start(bf16[2,2,48,128]{3,2,1,0:T(8,128)(2,1)S(1)} %get-tuple-element.44), channel_id=1, source_target_pairs={{0,1},{1,0},{2,3},{3,2},{4,5},{5,4},{6,7},{7,6},{8,9},{9,8},{10,11... | collective-permute-start | bytes 147464 | tf_op jit(solution)/shard_map/ppermute | solution.py:335
  8.7 2.6 %collective-permute-start.1 = (bf16[2,2,48,128]{3,2,1,0:T(8,128)(2,1)S(1)}, bf16[2,2,48,128]{3,2,1,0:T(8,128)(2,1)S(1)}, u32[]{:S(2)}, u32[]{:S(2)}) collective-permute-start(bf16[2,2,48,128]{3,2,1,0:T(8,128)(2,1)S(1)} %get-tuple-element.45), channel_id=1, source_target_pairs={{0,2},{1,3},{2,0},{3,1},{4,6},{5,7},{6,4},{7,5},{8,10},{9,11},{10,... | collective-permute-start | bytes 147464 | tf_op jit(solution)/shard_map/ppermute | solution.py:335
  11.6 2.7 %collective-permute-done.1 = bf16[2,2,48,128]{3,2,1,0:T(8,128)(2,1)S(1)} collective-permute-done((bf16[2,2,48,128]{3,2,1,0:T(8,128)(2,1)S(1)}, bf16[2,2,48,128]{3,2,1,0:T(8,128)(2,1)S(1)}, u32[]{:S(2)}, u32[]{:S(2)}) %collective-permute-start.1) | collective-permute-done | bytes 49184 | tf_op jit(solution)/shard_map/ppermute | solution.py:335
  14.2 3.0 %collective-permute-done.2 = bf16[2,2,48,128]{3,2,1,0:T(8,128)(2,1)S(1)} collective-permute-done((bf16[2,2,48,128]{3,2,1,0:T(8,128)(2,1)S(1)}, bf16[2,2,48,128]{3,2,1,0:T(8,128)(2,1)S(1)}, u32[]{:S(2)}, u32[]{:S(2)}) %collective-permute-start.2) | collective-permute-done | bytes 49184 | tf_op jit(solution)/shard_map/ppermute | solution.py:335
  19.7 4.3 %collective-permute-start.6 = (bf16[6,128,128]{2,1,0:T(8,128)(2,1)S(1)}, bf16[6,128,128]{2,1,0:T(8,128)(2,1)S(1)}, u32[]{:S(2)}, u32[]{:S(2)}) collective-permute-start(bf16[6,128,128]{2,1,0:T(8,128)(2,1)S(1)} %collective-permute-done.3.rest_2_), channel_id=1, source_target_pairs={{0,16},{8,24},{16,0},{24,8},{1,17},{9,25},{17,1},{25,9},{2,18},{10... | collective-permute-start | bytes 589832 | tf_op jit(solution)/shard_map/ppermute | solution.py:335
  24.0 3.6 %collective-permute-done.10 = bf16[2,4,2,32,128]{4,3,2,1,0:T(8,128)(2,1)S(1)} collective-permute-done((bf16[2,4,2,32,128]{4,3,2,1,0:T(8,128)(2,1)S(1)}, bf16[2,4,2,32,128]{4,3,2,1,0:T(8,128)(2,1)S(1)}, u32[]{:S(2)}, u32[]{:S(2)}) %collective-permute-start.10) | collective-permute-done | bytes 131104 | tf_op jit(solution)/shard_map/ppermute | solution.py:335
  29.5 3.6 %collective-permute-done.11 = bf16[2,4,2,32,128]{4,3,2,1,0:T(8,128)(2,1)S(1)} collective-permute-done((bf16[2,4,2,32,128]{4,3,2,1,0:T(8,128)(2,1)S(1)}, bf16[2,4,2,32,128]{4,3,2,1,0:T(8,128)(2,1)S(1)}, u32[]{:S(2)}, u32[]{:S(2)}) %collective-permute-start.11) | collective-permute-done | bytes 131104 | tf_op jit(solution)/shard_map/ppermute | solution.py:335
  33.2 3.3 %collective-permute-start.12 = (bf16[2,4,2,32,128]{4,3,2,1,0:T(8,128)(2,1)S(1)}, bf16[2,4,2,32,128]{4,3,2,1,0:T(8,128)(2,1)S(1)}, u32[]{:S(2)}, u32[]{:S(2)}) collective-permute-start(bf16[2,4,2,32,128]{4,3,2,1,0:T(8,128)(2,1)S(1)} %get-tuple-element.84), channel_id=1, source_target_pairs={{0,8},{1,9},{2,10},{3,11},{8,0},{9,1},{10,2},{11,3},{16,24},{17,25... | collective-permute-start | bytes 393224 | tf_op jit(solution)/shard_map/ppermute | solution.py:361
  37.2 6.5 %forward.1 = (bf16[4,4,10,16,384]{4,3,2,1,0:T(8,128)(2,1)S(1)}, bf16[4,4,8,16,128]{4,3,2,1,0:T(8,128)(2,1)S(1)}, f32[4,10,32,128]{3,2,1,0:T(8,128)S(1)}, f32[4,1...) custom-call(bf16[6,128,128]{2,1,0:T(8,128)(2,1)S(1)} %fusion.5.rest_0_, ...), custom_call_target="tpu_custom_call" | custom-call | flops 6000000000 | bytes 8000000 | tf_op jit(solution)/shard_map/forward/pallas_call | solution.py:433
  43.7 7.0 %backward.1 = (bf16[4,6,128,128]{3,2,1,0:T(8,128)(2,1)S(1)}, bf16[4,6,128,128]{3,2,1,0:T(8,128)(2,1)S(1)}, bf16[4,2,2,16,128]{4,3,2,1,0:T(8,128)(2,1)S(1)}, bf16[4,2,2,16,128]{4,3,2,1,0:T(8,128)(2,1)S(1)}) custom-call(bf16[6,128,128]{2,1,0:T(8,128)(2,1)S(1)} %fusion.5.rest_0_, bf16[6,128,128]{2,1,0:T(8,128)(2,1)S(1)} %fusion.4.rest_1_, ...), custom_call_target="tpu_custom_call" | custom-call | flops 6000000000 | bytes 8000000 | tf_op jit(solution)/shard_map/backward/pallas_call | solution.py:458
  51.0 2.1 %collective-permute-done.19 = bf16[4,6,128,128]{3,2,1,0:T(8,128)(2,1)S(1)} collective-permute-done((bf16[4,6,128,128]{3,2,1,0:T(8,128)(2,1)S(1)}, bf16[4,6,128,128]{3,2,1,0:T(8,128)(2,1)S(1)}, u32[]{:S(2)}, u32[]{:S(2)}) %collective-permute-start.19) | collective-permute-done | bytes 786464 | tf_op jit(solution)/shard_map/ppermute | solution.py:335
  53.6 3.7 %collective-permute-start.20 = (bf16[6,128,128]{2,1,0:T(8,128)(2,1)S(1)}, bf16[6,128,128]{2,1,0:T(8,128)(2,1)S(1)}, u32[]{:S(2)}, u32[]{:S(2)}) collective-permute-start(bf16[6,128,128]{2,1,0:T(8,128)(2,1)S(1)} %get-tuple-element.64), channel_id=1, source_target_pairs={{0,8},{8,0},{16,24},{24,16},{1,9},{9,1},{17,25},{25,17},{2,10},{10... | collective-permute-start | bytes 589832 | tf_op jit(solution)/shard_map/ppermute | solution.py:335
  57.3 1.5 %collective-permute-start.22 = (bf16[6,128,128]{2,1,0:T(8,128)(2,1)S(1)}, bf16[6,128,128]{2,1,0:T(8,128)(2,1)S(1)}, u32[]{:S(2)}, u32[]{:S(2)}) collective-permute-start(bf16[6,128,128]{2,1,0:T(8,128)(2,1)S(1)} %get-tuple-element.66), channel_id=1, source_target_pairs={{0,24},{8,16},{16,8},{24,0},{1,25},{9,17},{17,9},{25,1},{2,26},{10... | collective-permute-start | bytes 589832 | tf_op jit(solution)/shard_map/ppermute | solution.py:335
  59.2 2.3 %collective-permute-start.25 = (bf16[2,2,32,128]{3,2,1,0:T(8,128)(2,1)S(1)}, bf16[2,2,32,128]{3,2,1,0:T(8,128)(2,1)S(1)}, u32[]{:S(2)}, u32[]{:S(2)}) collective-permute-start(bf16[2,2,32,128]{3,2,1,0:T(8,128)(2,1)S(1)} %get-tuple-element.88), channel_id=1, source_target_pairs={{0,2},{1,3},{2,0},{3,1},{4,6},{5,7},{6,4},{7,5},{8,10},{9,11},{10,... | collective-permute-start | bytes 98312 | tf_op jit(solution)/shard_map/ppermute | solution.py:335
  61.5 1.4 %collective-permute-done.24 = bf16[2,2,32,128]{3,2,1,0:T(8,128)(2,1)S(1)} collective-permute-done((bf16[2,2,32,128]{3,2,1,0:T(8,128)(2,1)S(1)}, bf16[2,2,32,128]{3,2,1,0:T(8,128)(2,1)S(1)}, u32[]{:S(2)}, u32[]{:S(2)}) %collective-permute-start.24) | collective-permute-done | bytes 32800 | tf_op jit(solution)/shard_map/ppermute | solution.py:335
  62.9 2.0 %collective-permute-start.26 = (bf16[2,2,32,128]{3,2,1,0:T(8,128)(2,1)S(1)}, bf16[2,2,32,128]{3,2,1,0:T(8,128)(2,1)S(1)}, u32[]{:S(2)}, u32[]{:S(2)}) collective-permute-start(bf16[2,2,32,128]{3,2,1,0:T(8,128)(2,1)S(1)} %get-tuple-element.85), channel_id=1, source_target_pairs={{0,3},{1,2},{2,1},{3,0},{4,7},{5,6},{6,5},{7,4},{8,11},{9,10},{10,... | collective-permute-start | bytes 98312 | tf_op jit(solution)/shard_map/ppermute | solution.py:335
  64.9 3.7 %collective-permute-done.26 = bf16[2,2,32,128]{3,2,1,0:T(8,128)(2,1)S(1)} collective-permute-done((bf16[2,2,32,128]{3,2,1,0:T(8,128)(2,1)S(1)}, bf16[2,2,32,128]{3,2,1,0:T(8,128)(2,1)S(1)}, u32[]{:S(2)}, u32[]{:S(2)}) %collective-permute-start.26) | collective-permute-done | bytes 32800 | tf_op jit(solution)/shard_map/ppermute | solution.py:335
  68.9 4.6 %collective-permute-done.27 = bf16[384,128]{1,0:T(8,128)(2,1)S(1)} collective-permute-done((bf16[384,128]{1,0:T(8,128)(2,1)S(1)}, bf16[384,128]{1,0:T(8,128)(2,1)S(1)}, u32[]{:S(2)}, u32[]{:S(2)}) %collective-permute-start.27) | collective-permute-done | bytes 98336 | tf_op jit(solution)/shard_map/ppermute | solution.py:335
  74.1 5.5 %collective-permute-done.28 = bf16[384,128]{1,0:T(8,128)(2,1)S(1)} collective-permute-done((bf16[384,128]{1,0:T(8,128)(2,1)S(1)}, bf16[384,128]{1,0:T(8,128)(2,1)S(1)}, u32[]{:S(2)}, u32[]{:S(2)}) %collective-permute-start.28) | collective-permute-done | bytes 98336 | tf_op jit(solution)/shard_map/ppermute | solution.py:335
  79.7 4.6 %collective-permute-done.29 = bf16[384,128]{1,0:T(8,128)(2,1)S(1)} collective-permute-done((bf16[384,128]{1,0:T(8,128)(2,1)S(1)}, bf16[384,128]{1,0:T(8,128)(2,1)S(1)}, u32[]{:S(2)}, u32[]{:S(2)}) %collective-permute-start.29) | collective-permute-done | bytes 98336 | tf_op jit(solution)/shard_map/ppermute | solution.py:335
  84.5 1.4 %collective-permute-done.30.other_ref = bf16[2,384,128]{2,1,0:T(8,128)(2,1)S(1)} collective-permute-done((bf16[2,384,128]{2,1,0:T(8,128)(2,1)S(1)}, bf16[2,384,128]{2,1,0:T(8,128)(2,1)S(1)}, u32[]{:S(2)}, u32[]{:S(2)}) %collective-permute-start.30) | collective-permute-done | bytes 196640 | tf_op jit(solution)/shard_map/ppermute | solution.py:335
  85.9 1.1 %closing.1 = (f32[1,9,128,128]{3,2,1,0:T(8,128)}, f32[1,3,128,128]{3,2,1,0:T(8,128)}) custom-call(bf16[2,384,128]{2,1,0:T(8,128)(2,1)S(1)} %pad_maximum_fusion.1.mine_ref, bf16[2,384,128]{2,1,0:T(8,128)(2,1)S(1)} %collective-permute-done.30.other_ref), custom_call_target="tpu_custom_call" | custom-call | tf_op jit(solution)/shard_map/closing/pallas_call | solution.py:511
  (74 shorter events, 9.6 us)
Async XLA Ops:
  2.6 17.0 %collective-permute-start.3 = (bf16[6,128,128]{2,1,0:T(8,128)(2,1)S(1)}, bf16[6,128,128]{2,1,0:T(8,128)(2,1)S(1)}, u32[]{:S(2)}, u32[]{:S(2)}) collective-permute-start(bf16[6,128,128]{2,1,0:T(8,128)(2,1)S(1)} %fusion.5.rest_0_), channel_id=1, source_target_pairs={{0,8},{8,0},{16,24},{24,16},{1,9},{9,1},{17,25},{25,17},{2,10},{10... | collective-permute-start | bytes 589832 | tf_op jit(solution)/shard_map/ppermute | solution.py:335
  5.6 14.0 %collective-permute-start.4 = (bf16[6,128,128]{2,1,0:T(8,128)(2,1)S(1)}, bf16[6,128,128]{2,1,0:T(8,128)(2,1)S(1)}, u32[]{:S(2)}, u32[]{:S(2)}) collective-permute-start(bf16[6,128,128]{2,1,0:T(8,128)(2,1)S(1)} %fusion.5.rest_0_), channel_id=1, source_target_pairs={{0,16},{8,24},{16,0},{24,8},{1,17},{9,25},{17,1},{25,9},{2,18},{10... | collective-permute-start | bytes 589832 | tf_op jit(solution)/shard_map/ppermute | solution.py:335
  8.7 5.5 %collective-permute-start.1 = (bf16[2,2,48,128]{3,2,1,0:T(8,128)(2,1)S(1)}, bf16[2,2,48,128]{3,2,1,0:T(8,128)(2,1)S(1)}, u32[]{:S(2)}, u32[]{:S(2)}) collective-permute-start(bf16[2,2,48,128]{3,2,1,0:T(8,128)(2,1)S(1)} %get-tuple-element.45), channel_id=1, source_target_pairs={{0,2},{1,3},{2,0},{3,1},{4,6},{5,7},{6,4},{7,5},{8,10},{9,11},{10,... | collective-permute-start | bytes 147464 | tf_op jit(solution)/shard_map/ppermute | solution.py:335
  11.3 5.9 %collective-permute-start.2 = (bf16[2,2,48,128]{3,2,1,0:T(8,128)(2,1)S(1)}, bf16[2,2,48,128]{3,2,1,0:T(8,128)(2,1)S(1)}, u32[]{:S(2)}, u32[]{:S(2)}) collective-permute-start(bf16[2,2,48,128]{3,2,1,0:T(8,128)(2,1)S(1)} %get-tuple-element.46), channel_id=1, source_target_pairs={{0,3},{1,2},{2,1},{3,0},{4,7},{5,6},{6,5},{7,4},{8,11},{9,10},{10,... | collective-permute-start | bytes 147464 | tf_op jit(solution)/shard_map/ppermute | solution.py:335
  11.5 7.0 %collective-permute-start.5 = (bf16[2,2,128,128]{3,2,1,0:T(8,128)(2,1)}, bf16[2,2,128,128]{3,2,1,0:T(8,128)(2,1)S(1)}, u32[]{:S(2)}, u32[]{:S(2)}) collective-permute-start(bf16[2,2,128,128]{3,2,1,0:T(8,128)(2,1)} %mine_ref.1), channel_id=1, source_target_pairs={{0,4},{4,0},{1,5},{5,1},{2,6},{6,2},{3,7},{7,3},{8,12},{12,8},{9,1... | collective-permute-start | bytes 393224 | tf_op jit(solution)/shard_map/ppermute | solution.py:335
  17.2 10.6 %collective-permute-start.14 = (bf16[4,2,2,48,128]{4,3,2,1,0:T(8,128)(2,1)S(1)}, bf16[4,2,2,48,128]{4,3,2,1,0:T(8,128)(2,1)S(1)}, u32[]{:S(2)}, u32[]{:S(2)}) collective-permute-start(bf16[4,2,2,48,128]{4,3,2,1,0:T(8,128)(2,1)S(1)} %pad_maximum_fusion.rest_8_), channel_id=1, source_target_pairs={{0,8},{1,9},{2,10},{3,11},{8,0},{9,1},{10,2},{11,3},{16,24},{17,25... | collective-permute-start | bytes 589832 | tf_op jit(solution)/shard_map/ppermute | solution.py:361
  17.8 10.1 %collective-permute-start.15 = (bf16[4,2,2,48,128]{4,3,2,1,0:T(8,128)(2,1)S(1)}, bf16[4,2,2,48,128]{4,3,2,1,0:T(8,128)(2,1)S(1)}, u32[]{:S(2)}, u32[]{:S(2)}) collective-permute-start(bf16[4,2,2,48,128]{4,3,2,1,0:T(8,128)(2,1)S(1)} %pad_maximum_fusion.rest_8_), channel_id=1, source_target_pairs={{8,16},{9,17},{10,18},{11,19},{16,8},{17,9},{18,10},{19,11},{12,20... | collective-permute-start | bytes 589832 | tf_op jit(solution)/shard_map/ppermute | solution.py:361
  18.5 9.9 %collective-permute-start.16 = (bf16[4,2,2,48,128]{4,3,2,1,0:T(8,128)(2,1)S(1)}, bf16[4,2,2,48,128]{4,3,2,1,0:T(8,128)(2,1)S(1)}, u32[]{:S(2)}, u32[]{:S(2)}) collective-permute-start(bf16[4,2,2,48,128]{4,3,2,1,0:T(8,128)(2,1)S(1)} %pad_maximum_fusion.rest_8_), channel_id=1, source_target_pairs={{0,4},{4,0},{1,5},{5,1},{2,6},{6,2},{3,7},{7,3},{8,12},{12,8},{9,1... | collective-permute-start | bytes 589832 | tf_op jit(solution)/shard_map/ppermute | solution.py:335
  19.6 8.0 %collective-permute-start.10 = (bf16[2,4,2,32,128]{4,3,2,1,0:T(8,128)(2,1)S(1)}, bf16[2,4,2,32,128]{4,3,2,1,0:T(8,128)(2,1)S(1)}, u32[]{:S(2)}, u32[]{:S(2)}) collective-permute-start(bf16[2,4,2,32,128]{4,3,2,1,0:T(8,128)(2,1)S(1)} %get-tuple-element.53), channel_id=1, source_target_pairs={{0,2},{1,3},{2,0},{3,1},{4,6},{5,7},{6,4},{7,5},{8,10},{9,11},{10,... | collective-permute-start | bytes 393224 | tf_op jit(solution)/shard_map/ppermute | solution.py:335
  19.7 9.8 %collective-permute-start.6 = (bf16[6,128,128]{2,1,0:T(8,128)(2,1)S(1)}, bf16[6,128,128]{2,1,0:T(8,128)(2,1)S(1)}, u32[]{:S(2)}, u32[]{:S(2)}) collective-permute-start(bf16[6,128,128]{2,1,0:T(8,128)(2,1)S(1)} %collective-permute-done.3.rest_2_), channel_id=1, source_target_pairs={{0,16},{8,24},{16,0},{24,8},{1,17},{9,25},{17,1},{25,9},{2,18},{10... | collective-permute-start | bytes 589832 | tf_op jit(solution)/shard_map/ppermute | solution.py:335
  27.6 5.5 %collective-permute-start.11 = (bf16[2,4,2,32,128]{4,3,2,1,0:T(8,128)(2,1)S(1)}, bf16[2,4,2,32,128]{4,3,2,1,0:T(8,128)(2,1)S(1)}, u32[]{:S(2)}, u32[]{:S(2)}) collective-permute-start(bf16[2,4,2,32,128]{4,3,2,1,0:T(8,128)(2,1)S(1)} %pad_maximum_fusion.2), channel_id=1, source_target_pairs={{0,1},{1,0},{2,3},{3,2},{4,5},{5,4},{6,7},{7,6},{8,9},{9,8},{10,11... | collective-permute-start | bytes 393224 | tf_op jit(solution)/shard_map/ppermute | solution.py:335
  27.8 5.4 %collective-permute-start.7 = (bf16[6,128,128]{2,1,0:T(8,128)(2,1)S(1)}, bf16[6,128,128]{2,1,0:T(8,128)(2,1)S(1)}, u32[]{:S(2)}, u32[]{:S(2)}) collective-permute-start(bf16[6,128,128]{2,1,0:T(8,128)(2,1)S(1)} %collective-permute-done.3.rest_2_), channel_id=1, source_target_pairs={{0,4},{4,0},{1,5},{5,1},{2,6},{6,2},{3,7},{7,3},{8,12},{12,8},{9,1... | collective-permute-start | bytes 589832 | tf_op jit(solution)/shard_map/ppermute | solution.py:335
  28.0 8.5 %collective-permute-start.8 = (bf16[6,128,128]{2,1,0:T(8,128)(2,1)S(1)}, bf16[6,128,128]{2,1,0:T(8,128)(2,1)S(1)}, u32[]{:S(2)}, u32[]{:S(2)}) collective-permute-start(bf16[6,128,128]{2,1,0:T(8,128)(2,1)S(1)} %collective-permute-done.4.rest_3_), channel_id=1, source_target_pairs={{0,4},{4,0},{1,5},{5,1},{2,6},{6,2},{3,7},{7,3},{8,12},{12,8},{9,1... | collective-permute-start | bytes 589832 | tf_op jit(solution)/shard_map/ppermute | solution.py:335
  28.4 8.7 %collective-permute-start.17 = (bf16[4,2,2,48,128]{4,3,2,1,0:T(8,128)(2,1)S(1)}, bf16[4,2,2,48,128]{4,3,2,1,0:T(8,128)(2,1)S(1)}, u32[]{:S(2)}, u32[]{:S(2)}) collective-permute-start(bf16[4,2,2,48,128]{4,3,2,1,0:T(8,128)(2,1)S(1)} %collective-permute-done.14.rest_9_), channel_id=1, source_target_pairs={{0,4},{4,0},{1,5},{5,1},{2,6},{6,2},{3,7},{7,3},{8,12},{12,8},{9,1... | collective-permute-start | bytes 589832 | tf_op jit(solution)/shard_map/ppermute | solution.py:335
  29.5 7.6 %collective-permute-start.18 = (bf16[4,2,2,48,128]{4,3,2,1,0:T(8,128)(2,1)S(1)}, bf16[4,2,2,48,128]{4,3,2,1,0:T(8,128)(2,1)S(1)}, u32[]{:S(2)}, u32[]{:S(2)}) collective-permute-start(bf16[4,2,2,48,128]{4,3,2,1,0:T(8,128)(2,1)S(1)} %collective-permute-done.15.rest_10_), channel_id=1, source_target_pairs={{0,4},{4,0},{1,5},{5,1},{2,6},{6,2},{3,7},{7,3},{8,12},{12,8},{9,1... | collective-permute-start | bytes 589832 | tf_op jit(solution)/shard_map/ppermute | solution.py:335
  33.2 10.5 %collective-permute-start.12 = (bf16[2,4,2,32,128]{4,3,2,1,0:T(8,128)(2,1)S(1)}, bf16[2,4,2,32,128]{4,3,2,1,0:T(8,128)(2,1)S(1)}, u32[]{:S(2)}, u32[]{:S(2)}) collective-permute-start(bf16[2,4,2,32,128]{4,3,2,1,0:T(8,128)(2,1)S(1)} %get-tuple-element.84), channel_id=1, source_target_pairs={{0,8},{1,9},{2,10},{3,11},{8,0},{9,1},{10,2},{11,3},{16,24},{17,25... | collective-permute-start | bytes 393224 | tf_op jit(solution)/shard_map/ppermute | solution.py:361
  36.5 7.2 %collective-permute-start.13 = (bf16[2,4,2,32,128]{4,3,2,1,0:T(8,128)(2,1)S(1)}, bf16[2,4,2,32,128]{4,3,2,1,0:T(8,128)(2,1)S(1)}, u32[]{:S(2)}, u32[]{:S(2)}) collective-permute-start(bf16[2,4,2,32,128]{4,3,2,1,0:T(8,128)(2,1)S(1)} %get-tuple-element.83), channel_id=1, source_target_pairs={{8,16},{9,17},{10,18},{11,19},{16,8},{17,9},{18,10},{19,11},{12,20... | collective-permute-start | bytes 393224 | tf_op jit(solution)/shard_map/ppermute | solution.py:361
  53.3 5.5 %collective-permute-start.23 = (bf16[4,2,2,16,128]{4,3,2,1,0:T(8,128)(2,1)S(1)}, bf16[4,2,2,16,128]{4,3,2,1,0:T(8,128)(2,1)S(1)}, u32[]{:S(2)}, u32[]{:S(2)}) collective-permute-start(bf16[4,2,2,16,128]{4,3,2,1,0:T(8,128)(2,1)S(1)} %get-tuple-element.68), channel_id=1, source_target_pairs={{0,4},{4,0},{1,5},{5,1},{2,6},{6,2},{3,7},{7,3},{8,12},{12,8},{9,1... | collective-permute-start | bytes 196616 | tf_op jit(solution)/shard_map/ppermute | solution.py:335
  53.6 15.0 %collective-permute-start.20 = (bf16[6,128,128]{2,1,0:T(8,128)(2,1)S(1)}, bf16[6,128,128]{2,1,0:T(8,128)(2,1)S(1)}, u32[]{:S(2)}, u32[]{:S(2)}) collective-permute-start(bf16[6,128,128]{2,1,0:T(8,128)(2,1)S(1)} %get-tuple-element.64), channel_id=1, source_target_pairs={{0,8},{8,0},{16,24},{24,16},{1,9},{9,1},{17,25},{25,17},{2,10},{10... | collective-permute-start | bytes 589832 | tf_op jit(solution)/shard_map/ppermute | solution.py:335
  57.3 11.3 %collective-permute-start.21 = (bf16[6,128,128]{2,1,0:T(8,128)(2,1)S(1)}, bf16[6,128,128]{2,1,0:T(8,128)(2,1)S(1)}, u32[]{:S(2)}, u32[]{:S(2)}) collective-permute-start(bf16[6,128,128]{2,1,0:T(8,128)(2,1)S(1)} %get-tuple-element.65), channel_id=1, source_target_pairs={{0,16},{8,24},{16,0},{24,8},{1,17},{9,25},{17,1},{25,9},{2,18},{10... | collective-permute-start | bytes 589832 | tf_op jit(solution)/shard_map/ppermute | solution.py:335
  57.3 11.3 %collective-permute-start.22 = (bf16[6,128,128]{2,1,0:T(8,128)(2,1)S(1)}, bf16[6,128,128]{2,1,0:T(8,128)(2,1)S(1)}, u32[]{:S(2)}, u32[]{:S(2)}) collective-permute-start(bf16[6,128,128]{2,1,0:T(8,128)(2,1)S(1)} %get-tuple-element.66), channel_id=1, source_target_pairs={{0,24},{8,16},{16,8},{24,0},{1,25},{9,17},{17,9},{25,1},{2,26},{10... | collective-permute-start | bytes 589832 | tf_op jit(solution)/shard_map/ppermute | solution.py:335
  59.2 5.7 %collective-permute-start.25 = (bf16[2,2,32,128]{3,2,1,0:T(8,128)(2,1)S(1)}, bf16[2,2,32,128]{3,2,1,0:T(8,128)(2,1)S(1)}, u32[]{:S(2)}, u32[]{:S(2)}) collective-permute-start(bf16[2,2,32,128]{3,2,1,0:T(8,128)(2,1)S(1)} %get-tuple-element.88), channel_id=1, source_target_pairs={{0,2},{1,3},{2,0},{3,1},{4,6},{5,7},{6,4},{7,5},{8,10},{9,11},{10,... | collective-permute-start | bytes 98312 | tf_op jit(solution)/shard_map/ppermute | solution.py:335
  62.9 5.7 %collective-permute-start.26 = (bf16[2,2,32,128]{3,2,1,0:T(8,128)(2,1)S(1)}, bf16[2,2,32,128]{3,2,1,0:T(8,128)(2,1)S(1)}, u32[]{:S(2)}, u32[]{:S(2)}) collective-permute-start(bf16[2,2,32,128]{3,2,1,0:T(8,128)(2,1)S(1)} %get-tuple-element.85), channel_id=1, source_target_pairs={{0,3},{1,2},{2,1},{3,0},{4,7},{5,6},{6,5},{7,4},{8,11},{9,10},{10,... | collective-permute-start | bytes 98312 | tf_op jit(solution)/shard_map/ppermute | solution.py:335
  73.5 6.1 %collective-permute-start.28 = (bf16[384,128]{1,0:T(8,128)(2,1)S(1)}, bf16[384,128]{1,0:T(8,128)(2,1)S(1)}, u32[]{:S(2)}, u32[]{:S(2)}) collective-permute-start(bf16[384,128]{1,0:T(8,128)(2,1)S(1)} %fusion.6), channel_id=1, source_target_pairs={{0,2},{1,3},{2,0},{3,1},{4,6},{5,7},{6,4},{7,5},{8,10},{9,11},{10,... | collective-permute-start | bytes 294920 | tf_op jit(solution)/shard_map/ppermute | solution.py:335
  (12 other events, 82.4 us)

commit v12 on v11

--- a/solution.py
+++ b/solution.py
@@ -13,10 +13,6 @@
 
 def rolled(value, steps):
     return pltpu.roll(value, steps % value.shape[0], 0)
-
-
-def dot_t(left, right):
-    return lax.dot_general(left, right, (((1,), (1,)), ((), ())), preferred_element_type=F32)
 
 
 def dot_first(left, right):
@@ -39,15 +35,22 @@
                 pair_ref[at : at + chans, target * chans : (target + 1) * chans] = tile
 
 
+def turned(w_ref, block, tap):
+    return kernel_of(w_ref, block, tap).astype(F32).T.astype(BF16)
+
+
 def pair_rows_back(w_ref, block, pair_ref):
     chans = w_ref.shape[-1]
-    for source in range(4):
-        for target in range(2):
-            ky = 2 + target - source
-            for kx in range(3):
-                at = (3 * source + kx) * chans
-                tile = kernel_of(w_ref, block, 3 * ky + kx) if 0 <= ky < 3 else jnp.zeros((chans, chans), BF16)
-                pair_ref[target * chans : (target + 1) * chans, at : at + chans] = tile
+    nothing = jnp.zeros((chans, chans), BF16)
+    for kx in range(3):
+        for ky in range(3):
+            tile = turned(w_ref, block, 3 * ky + kx)
+            for target in range(2):
+                at = (3 * (2 + target - ky) + kx) * chans
+                pair_ref[at : at + chans, target * chans : (target + 1) * chans] = tile
+        for source, target in ((3, 0), (0, 1)):
+            at = (3 * source + kx) * chans
+            pair_ref[at : at + chans, target * chans : (target + 1) * chans] = nothing
 
 
 def pair_frames(w_ref, block, first, count):
@@ -64,14 +67,15 @@
 
 def pair_frames_back(w_ref, block, count):
     chans = w_ref.shape[-1]
-    rows = []
+    tiles = [turned(w_ref, block, 9 + kt) for kt in range(3)]
+    columns = []
     for target in range(2):
-        tiles = []
+        column = []
         for source in range(count):
             kt = 2 - (source - target)
-            tiles.append(kernel_of(w_ref, block, 9 + kt) if 0 <= kt < 3 else jnp.zeros((chans, chans), BF16))
-        rows.append(jnp.concatenate(tiles, 1))
-    return jnp.concatenate(rows, 0)
+            column.append(tiles[kt] if 0 <= kt < 3 else jnp.zeros((chans, chans), BF16))
+        columns.append(jnp.concatenate(column, 0))
+    return jnp.concatenate(columns, 1)
 
 
 def row_pairs(ref, frame, first, pairs):
@@ -142,25 +146,17 @@
             temporal_ref[0, tap - count] = turned
 
 
-def place_kernels(core, section, w_ref, own_mine, own_other, mine_refs, other_refs):
-    w_ref[core, section] = own_mine[...]
-    w_ref[1 - core, section] = own_other[...]
-    for step, (mine_ref, other_ref) in enumerate(zip(mine_refs, other_refs)):
-        block = jnp.bitwise_xor(section, step + 1)
-        w_ref[core, block] = mine_ref[...]
-        w_ref[1 - core, block] = other_ref[...]
-
-
 def forward_kernel(geometry, *rest):
     blocks, cores, group, frames_in, rows_in, halo, tile, width, height, columns = geometry
     core, section, band, unit = placed(group)
     odd = band % 2
-    shared, rest = rest[: 2 * blocks], rest[2 * blocks :]
+    shared, rest = rest[:2], rest[2:]
     arrived, rest = rest[:6], rest[6:]
     xo_ref, ho_ref = rest[:2]
     d_refs = rest[2 : 2 + blocks]
     x_ref, h_ref, mask_ref, w_ref, start_ref, pair_ref = rest[2 + blocks :]
-    place_kernels(core, section, w_ref, *shared[:2], shared[2 : 1 + blocks], shared[1 + blocks :])
+    w_ref[core] = shared[0][...]
+    w_ref[1 - core] = shared[1][...]
     frames = cores * frames_in
     high = tile + 2 * halo
     chans = w_ref.shape[-1]
@@ -241,13 +237,14 @@
 def backward_kernel(geometry, factor, *rest):
     blocks, cores, group, frames_in, rows_in, halo, tile, width, height, columns = geometry
     core, section, band, unit = placed(group)
-    shared, rest = rest[: 2 * blocks], rest[2 * blocks :]
+    shared, rest = rest[:2], rest[2:]
     arrived, rest = rest[:4], rest[4:]
     xo_ref, ho_ref = rest[:2]
     d_refs = rest[2 : 2 + blocks]
     keep_ref, give_ref, mine_out, other_out = rest[2 + blocks : 6 + blocks]
     g_ref, da_ref, dao_ref, go_ref, w_ref, grad_ref, out_ref, pair_ref = rest[6 + blocks :]
-    place_kernels(core, section, w_ref, *shared[:2], shared[2 : 1 + blocks], shared[1 + blocks :])
+    w_ref[core] = shared[0][...]
+    w_ref[1 - core] = shared[1][...]
     frames = cores * frames_in
     chans = w_ref.shape[-1]
     rim = blocks
@@ -288,7 +285,8 @@
                 ],
                 1,
             )
-            both = dot_t(ahead, pair_frames_back(w_ref, block, stop - frame))
+            weights = pair_frames_back(w_ref, block, stop - frame)
+            both = jnp.dot(ahead, weights, preferred_element_type=F32)
             hiddens += [both[:, :chans], both[:, chans:]]
         for frame in range(frames):
             hidden = hiddens[frame]
@@ -303,7 +301,7 @@
         for frame in range(frames):
             inner = count - 2
             taps = row_pairs(da_ref, frame, first, inner // 2)
-            back = woven(dot_t(taps, pair_ref[...]), width)
+            back = woven(jnp.dot(taps, pair_ref[...], preferred_element_type=F32), width)
             old = g_ref[frame, first + 1 : last - 1].astype(F32).reshape(inner * width, chans)
             new = (old + back).astype(BF16)
             if block:
@@ -394,16 +392,11 @@
     def gathered(pieces):
         return jnp.stack([pieces[0]] + [swapped(pieces[i], "space", i) for i in range(1, group)])
 
-    along_x = swapped(half_kernels, "section", 1)
-    along_y = swapped(half_kernels, "section", 2)
+    mine = lax.all_gather(half_kernels, "section")
     own_video = gathered(cuts)
     near, far = traded(own_video, 0), traded(own_video, 1)
-    _, along_x, along_y, high_pair, spatial, temporal = lax.optimization_barrier(
-        [own_video, along_x, along_y, high_pair, spatial_weights, temporal_weights]
-    )
-    mine = [along_x, along_y, swapped(along_x, "section", 2)]
-    rest_kernels = core_half(1 - core, spatial, temporal)
-    shared = [half_kernels, rest_kernels] + mine + [swapped(each) for each in mine]
+    near, mine = lax.optimization_barrier([near, mine])
+    shared = [mine, swapped(mine)]
     videos = [own_video, near, far]
     videos += [swapped(each) for each in videos]
 
@@ -433,7 +426,7 @@
     features, hidden, *slopes = pl.pallas_call(
         functools.partial(forward_kernel, geometry),
         name="forward",
-        in_specs=[vmem] * (2 * blocks + 6),
+        in_specs=[vmem] * 8,
         out_specs=[vmem] * (2 + blocks),
         out_shape=[
             jax.ShapeDtypeStruct((blocks, frames, tile + 2, own_width, 3 * chans), BF16),
@@ -458,7 +451,7 @@
     keep, give, mine_grad, other_grad = pl.pallas_call(
         functools.partial(backward_kernel, geometry, factor),
         name="backward",
-        in_specs=[vmem] * (3 * blocks + 6),
+        in_specs=[vmem] * (blocks + 8),
         out_specs=[vmem] * 4,
         out_shape=[
             jax.ShapeDtypeStruct(per_section, BF16),
@@ -474,7 +467,7 @@
             pltpu.VMEM(all_kernels, BF16),
             pltpu.VMEM(all_kernels, BF16),
             pltpu.VMEM((frames, tile, own_width, chans), BF16),
-            pltpu.VMEM((2 * chans, 12 * chans), BF16),
+            pltpu.VMEM((12 * chans, 2 * chans), BF16),
         ],
         compiler_params=params,
         cost_estimate=cost,

time: 87.1 us -> 86.7 us (level)
  blocking collectives: 0 us -> 11.6 us
  starting transfers between devices: 30.4 us -> 25.4 us
  waiting for transfers between devices: 37.2 us -> 32.3 us
  Pallas kernels: 14.7 us -> 13.6 us
  local copies, waits for them, and re-layouts: 1.94 us -> 1.04 us
    all_gather x0 -> x1, blocking collectives: none -> 11.6 us  [on_device(): mine = lax.all_gather(half_kernels, 'section')]
    ppermute x27 -> x22, waiting for transfers between devices: 37.1 us -> 28.7 us  [swapped(): return lax.ppermute(value, axis, [(i, i ^ step) for i in range(count)])]
    ppermute x27 -> x22, starting transfers between devices: 25.2 us -> 19.2 us  [swapped(): return lax.ppermute(value, axis, [(i, i ^ step) for i in range(count)])]
    ppermute x4, waiting for transfers between devices: 0.01 us -> 3.61 us  [traded(): return lax.ppermute(value, ('section', 'space'), pairs)]
    pallas_call x1, Pallas kernels: 7.03 us -> 5.6 us  [on_device(): pl.pallas_call(functools.partial(backward_kernel, geometry, factor), name...]
    ppermute x4, starting transfers between devices: 5.19 us -> 6.22 us  [traded(): return lax.ppermute(value, ('section', 'space'), pairs)]
    unnamed x10 -> x6, local copies, waits for them, and re-layouts: 1.81 us -> 0.91 us
  transfers between devices with their start and end apart: 31 -> 26, of which waited for: 12 -> 10; matrix products, arithmetic and copies ran while one was open for 0% -> 1% of each run, Pallas kernels for 8% -> 8%
where the time goes in v12:
time: 86.7 us; the launch traced here: 86.5 us
  waiting for transfers between devices  32.3 us (37%)
  starting transfers between devices  25.4 us (29%)
  Pallas kernels  13.6 us (16%)
  blocking collectives  11.6 us (13%)
  other arithmetic  1.53 us (2%)
  local copies, waits for them, and re-layouts  1.04 us (1%)
  between operations  1.02 us (1%)
    ppermute x22, waiting for transfers between devices, swapped(): return lax.ppermute(value, axis, [(i, i ^ step) for i in range(count)])  28.7 us
    ppermute x22, starting transfers between devices, swapped(): return lax.ppermute(value, axis, [(i, i ^ step) for i in range(count)])  19.2 us
    all_gather x1, blocking collectives, on_device(): mine = lax.all_gather(half_kernels, 'section')  11.6 us
    pallas_call x1, Pallas kernels, on_device(): pl.pallas_call(functools.partial(forward_kernel, geometry), name='forward...  6.77 us
    ppermute x4, starting transfers between devices, traded(): return lax.ppermute(value, ('section', 'space'), pairs)  6.22 us
    pallas_call x1, Pallas kernels, on_device(): pl.pallas_call(functools.partial(backward_kernel, geometry, factor), name...  5.6 us
    ppermute x4, waiting for transfers between devices, traded(): return lax.ppermute(value, ('section', 'space'), pairs)  3.61 us
  transfers between devices with their start and end apart: 26, of which 10 were waited for; matrix products, arithmetic and copies ran while one was open for 1% of the time, Pallas kernels for 8%

profile of v12, /device:TPU:0, one launch (start us, length us, event | category | flops | bytes accessed | tf_op | source)
XLA Modules:
  0.0 86.5 jit_solution(2685067776413147547)
XLA Ops:
  2.1 2.6 %collective-permute-start = (bf16[2,2,48,128]{3,2,1,0:T(8,128)(2,1)S(1)}, bf16[2,2,48,128]{3,2,1,0:T(8,128)(2,1)S(1)}, u32[]{:S(2)}, u32[]{:S(2)}) collective-permute-start(bf16[2,2,48,128]{3,2,1,0:T(8,128)(2,1)S(1)} %get-tuple-element.39), channel_id=1, source_target_pairs={{0,1},{1,0},{2,3},{3,2},{4,5},{5,4},{6,7},{7,6},{8,9},{9,8},{10,11... | collective-permute-start | bytes 147464 | tf_op jit(solution)/shard_map/ppermute | solution.py:333
  4.7 2.6 %collective-permute-start.1 = (bf16[2,2,48,128]{3,2,1,0:T(8,128)(2,1)S(1)}, bf16[2,2,48,128]{3,2,1,0:T(8,128)(2,1)S(1)}, u32[]{:S(2)}, u32[]{:S(2)}) collective-permute-start(bf16[2,2,48,128]{3,2,1,0:T(8,128)(2,1)S(1)} %get-tuple-element.40), channel_id=1, source_target_pairs={{0,2},{1,3},{2,0},{3,1},{4,6},{5,7},{6,4},{7,5},{8,10},{9,11},{10,... | collective-permute-start | bytes 147464 | tf_op jit(solution)/shard_map/ppermute | solution.py:333
  8.3 11.6 %all-gather = bf16[24,128,128]{2,1,0:T(8,128)(2,1)S(1)} all-gather(bf16[6,128,128]{2,1,0:T(8,128)(2,1)S(1)} %fusion.4), channel_id=2, replica_groups=mesh['section'=4,'tm'=2,'space'=4] {'section'}, dimensions={0}, use_global_device_ids=true | all-gather | bytes 983040 | tf_op jit(solution)/shard_map/all_gather | solution.py:395
  20.0 1.6 %collective-permute-start.3 = (bf16[4,2,2,48,128]{4,3,2,1,0:T(8,128)(2,1)S(1)}, bf16[4,2,2,48,128]{4,3,2,1,0:T(8,128)(2,1)S(1)}, u32[]{:S(2)}, u32[]{:S(2)}) collective-permute-start(bf16[4,2,2,48,128]{4,3,2,1,0:T(8,128)(2,1)S(1)} %pad_maximum_fusion.rest_2_), channel_id=1, source_target_pairs={{0,8},{1,9},{2,10},{3,11},{8,0},{9,1},{10,2},{11,3},{16,24},{17,25... | collective-permute-start | bytes 589832 | tf_op jit(solution)/shard_map/ppermute | solution.py:359
  22.3 1.6 %collective-permute-start.6 = (bf16[2,4,2,32,128]{4,3,2,1,0:T(8,128)(2,1)S(1)}, bf16[2,4,2,32,128]{4,3,2,1,0:T(8,128)(2,1)S(1)}, u32[]{:S(2)}, u32[]{:S(2)}) collective-permute-start(bf16[2,4,2,32,128]{4,3,2,1,0:T(8,128)(2,1)S(1)} %get-tuple-element.46), channel_id=1, source_target_pairs={{0,2},{1,3},{2,0},{3,1},{4,6},{5,7},{6,4},{7,5},{8,10},{9,11},{10,... | collective-permute-start | bytes 393224 | tf_op jit(solution)/shard_map/ppermute | solution.py:333
  23.9 3.6 %collective-permute-done.3.rest_3_ = bf16[4,2,2,48,128]{4,3,2,1,0:T(8,128)(2,1)S(1)} collective-permute-done((bf16[4,2,2,48,128]{4,3,2,1,0:T(8,128)(2,1)S(1)}, bf16[4,2,2,48,128]{4,3,2,1,0:T(8,128)(2,1)S(1)}, u32[]{:S(2)}, u32[]{:S(2)}) %collective-permute-start.3) | collective-permute-done | bytes 196640 | tf_op jit(solution)/shard_map/ppermute | solution.py:359
  27.5 2.1 %collective-permute-done.6 = bf16[2,4,2,32,128]{4,3,2,1,0:T(8,128)(2,1)S(1)} collective-permute-done((bf16[2,4,2,32,128]{4,3,2,1,0:T(8,128)(2,1)S(1)}, bf16[2,4,2,32,128]{4,3,2,1,0:T(8,128)(2,1)S(1)}, u32[]{:S(2)}, u32[]{:S(2)}) %collective-permute-start.6) | collective-permute-done | bytes 131104 | tf_op jit(solution)/shard_map/ppermute | solution.py:333
  30.5 4.2 %collective-permute-done.7 = bf16[2,4,2,32,128]{4,3,2,1,0:T(8,128)(2,1)S(1)} collective-permute-done((bf16[2,4,2,32,128]{4,3,2,1,0:T(8,128)(2,1)S(1)}, bf16[2,4,2,32,128]{4,3,2,1,0:T(8,128)(2,1)S(1)}, u32[]{:S(2)}, u32[]{:S(2)}) %collective-permute-start.7) | collective-permute-done | bytes 131104 | tf_op jit(solution)/shard_map/ppermute | solution.py:333
  34.8 3.3 %collective-permute-start.8 = (bf16[2,4,2,32,128]{4,3,2,1,0:T(8,128)(2,1)S(1)}, bf16[2,4,2,32,128]{4,3,2,1,0:T(8,128)(2,1)S(1)}, u32[]{:S(2)}, u32[]{:S(2)}) collective-permute-start(bf16[2,4,2,32,128]{4,3,2,1,0:T(8,128)(2,1)S(1)} %get-tuple-element.78), channel_id=1, source_target_pairs={{0,8},{1,9},{2,10},{3,11},{8,0},{9,1},{10,2},{11,3},{16,24},{17,25... | collective-permute-start | bytes 393224 | tf_op jit(solution)/shard_map/ppermute | solution.py:359
  38.8 6.8 %forward.1 = (bf16[4,4,10,16,384]{4,3,2,1,0:T(8,128)(2,1)S(1)}, bf16[4,4,8,16,128]{4,3,2,1,0:T(8,128)(2,1)S(1)}, f32[4,10,32,128]{3,2,1,0:T(8,128)S(1)}, f32[4,1...) custom-call(bf16[4,6,128,128]{3,2,1,0:T(8,128)(2,1)S(1)} %bitcast.32, ...), custom_call_target="tpu_custom_call" | custom-call | flops 6000000000 | bytes 8000000 | tf_op jit(solution)/shard_map/forward/pallas_call | solution.py:426
  45.6 5.6 %backward.1 = (bf16[4,6,128,128]{3,2,1,0:T(8,128)(2,1)S(1)}, bf16[4,6,128,128]{3,2,1,0:T(8,128)(2,1)S(1)}, bf16[4,2,2,16,128]{4,3,2,1,0:T(8,128)(2,1)S(1)}, bf16[4,2,2,16,128]{4,3,2,1,0:T(8,128)(2,1)S(1)}) custom-call(bf16[4,6,128,128]{3,2,1,0:T(8,128)(2,1)S(1)} %bitcast.33, bf16[4,6,128,128]{3,2,1,0:T(8,128)(2,1)S(1)} %collective-permute-done.4.rest_1_, ...), custom_call_target="tpu_custom_call" | custom-call | flops 6000000000 | bytes 8000000 | tf_op jit(solution)/shard_map/backward/pallas_call | solution.py:451
  51.3 2.3 %collective-permute-done.14 = bf16[4,6,128,128]{3,2,1,0:T(8,128)(2,1)S(1)} collective-permute-done((bf16[4,6,128,128]{3,2,1,0:T(8,128)(2,1)S(1)}, bf16[4,6,128,128]{3,2,1,0:T(8,128)(2,1)S(1)}, u32[]{:S(2)}, u32[]{:S(2)}) %collective-permute-start.14) | collective-permute-done | bytes 786464 | tf_op jit(solution)/shard_map/ppermute | solution.py:333
  54.0 2.8 %collective-permute-start.15 = (bf16[6,128,128]{2,1,0:T(8,128)(2,1)S(1)}, bf16[6,128,128]{2,1,0:T(8,128)(2,1)S(1)}, u32[]{:S(2)}, u32[]{:S(2)}) collective-permute-start(bf16[6,128,128]{2,1,0:T(8,128)(2,1)S(1)} %get-tuple-element.58), channel_id=1, source_target_pairs={{0,8},{8,0},{16,24},{24,16},{1,9},{9,1},{17,25},{25,17},{2,10},{10... | collective-permute-start | bytes 589832 | tf_op jit(solution)/shard_map/ppermute | solution.py:333
  56.8 1.5 %collective-permute-start.17 = (bf16[6,128,128]{2,1,0:T(8,128)(2,1)S(1)}, bf16[6,128,128]{2,1,0:T(8,128)(2,1)S(1)}, u32[]{:S(2)}, u32[]{:S(2)}) collective-permute-start(bf16[6,128,128]{2,1,0:T(8,128)(2,1)S(1)} %get-tuple-element.60), channel_id=1, source_target_pairs={{0,24},{8,16},{16,8},{24,0},{1,25},{9,17},{17,9},{25,1},{2,26},{10... | collective-permute-start | bytes 589832 | tf_op jit(solution)/shard_map/ppermute | solution.py:333
  58.4 3.0 %collective-permute-start.20 = (bf16[2,2,32,128]{3,2,1,0:T(8,128)(2,1)S(1)}, bf16[2,2,32,128]{3,2,1,0:T(8,128)(2,1)S(1)}, u32[]{:S(2)}, u32[]{:S(2)}) collective-permute-start(bf16[2,2,32,128]{3,2,1,0:T(8,128)(2,1)S(1)} %get-tuple-element.82), channel_id=1, source_target_pairs={{0,2},{1,3},{2,0},{3,1},{4,6},{5,7},{6,4},{7,5},{8,10},{9,11},{10,... | collective-permute-start | bytes 98312 | tf_op jit(solution)/shard_map/ppermute | solution.py:333
  61.4 1.1 %collective-permute-done.19 = bf16[2,2,32,128]{3,2,1,0:T(8,128)(2,1)S(1)} collective-permute-done((bf16[2,2,32,128]{3,2,1,0:T(8,128)(2,1)S(1)}, bf16[2,2,32,128]{3,2,1,0:T(8,128)(2,1)S(1)}, u32[]{:S(2)}, u32[]{:S(2)}) %collective-permute-start.19) | collective-permute-done | bytes 32800 | tf_op jit(solution)/shard_map/ppermute | solution.py:333
  62.5 2.4 %collective-permute-start.21 = (bf16[2,2,32,128]{3,2,1,0:T(8,128)(2,1)S(1)}, bf16[2,2,32,128]{3,2,1,0:T(8,128)(2,1)S(1)}, u32[]{:S(2)}, u32[]{:S(2)}) collective-permute-start(bf16[2,2,32,128]{3,2,1,0:T(8,128)(2,1)S(1)} %get-tuple-element.79), channel_id=1, source_target_pairs={{0,3},{1,2},{2,1},{3,0},{4,7},{5,6},{6,5},{7,4},{8,11},{9,10},{10,... | collective-permute-start | bytes 98312 | tf_op jit(solution)/shard_map/ppermute | solution.py:333
  64.9 3.3 %collective-permute-done.21 = bf16[2,2,32,128]{3,2,1,0:T(8,128)(2,1)S(1)} collective-permute-done((bf16[2,2,32,128]{3,2,1,0:T(8,128)(2,1)S(1)}, bf16[2,2,32,128]{3,2,1,0:T(8,128)(2,1)S(1)}, u32[]{:S(2)}, u32[]{:S(2)}) %collective-permute-start.21) | collective-permute-done | bytes 32800 | tf_op jit(solution)/shard_map/ppermute | solution.py:333
  68.4 4.6 %collective-permute-done.22 = bf16[384,128]{1,0:T(8,128)(2,1)S(1)} collective-permute-done((bf16[384,128]{1,0:T(8,128)(2,1)S(1)}, bf16[384,128]{1,0:T(8,128)(2,1)S(1)}, u32[]{:S(2)}, u32[]{:S(2)}) %collective-permute-start.22) | collective-permute-done | bytes 98336 | tf_op jit(solution)/shard_map/ppermute | solution.py:333
  73.0 1.0 %collective-permute-start.23 = (bf16[384,128]{1,0:T(8,128)(2,1)S(1)}, bf16[384,128]{1,0:T(8,128)(2,1)S(1)}, u32[]{:S(2)}, u32[]{:S(2)}) collective-permute-start(bf16[384,128]{1,0:T(8,128)(2,1)S(1)} %fusion.5), channel_id=1, source_target_pairs={{0,2},{1,3},{2,0},{3,1},{4,6},{5,7},{6,4},{7,5},{8,10},{9,11},{10,... | collective-permute-start | bytes 294920 | tf_op jit(solution)/shard_map/ppermute | solution.py:333
  74.1 5.1 %collective-permute-done.23 = bf16[384,128]{1,0:T(8,128)(2,1)S(1)} collective-permute-done((bf16[384,128]{1,0:T(8,128)(2,1)S(1)}, bf16[384,128]{1,0:T(8,128)(2,1)S(1)}, u32[]{:S(2)}, u32[]{:S(2)}) %collective-permute-start.23) | collective-permute-done | bytes 98336 | tf_op jit(solution)/shard_map/ppermute | solution.py:333
  79.3 4.6 %collective-permute-done.24 = bf16[384,128]{1,0:T(8,128)(2,1)S(1)} collective-permute-done((bf16[384,128]{1,0:T(8,128)(2,1)S(1)}, bf16[384,128]{1,0:T(8,128)(2,1)S(1)}, u32[]{:S(2)}, u32[]{:S(2)}) %collective-permute-start.24) | collective-permute-done | bytes 98336 | tf_op jit(solution)/shard_map/ppermute | solution.py:333
  84.0 1.4 %collective-permute-done.25.other_ref = bf16[2,384,128]{2,1,0:T(8,128)(2,1)S(1)} collective-permute-done((bf16[2,384,128]{2,1,0:T(8,128)(2,1)S(1)}, bf16[2,384,128]{2,1,0:T(8,128)(2,1)S(1)}, u32[]{:S(2)}, u32[]{:S(2)}) %collective-permute-start.25) | collective-permute-done | bytes 196640 | tf_op jit(solution)/shard_map/ppermute | solution.py:333
  85.4 1.1 %closing.1 = (f32[1,9,128,128]{3,2,1,0:T(8,128)}, f32[1,3,128,128]{3,2,1,0:T(8,128)}) custom-call(bf16[2,384,128]{2,1,0:T(8,128)(2,1)S(1)} %pad_maximum_fusion.1.mine_ref, bf16[2,384,128]{2,1,0:T(8,128)(2,1)S(1)} %collective-permute-done.25.other_ref), custom_call_target="tpu_custom_call" | custom-call | tf_op jit(solution)/shard_map/closing/pallas_call | solution.py:504
  (60 shorter events, 5.9 us)
Async XLA Ops:
  0.6 21.6 %collective-permute-start.5 = (bf16[2,2,128,128]{3,2,1,0:T(8,128)(2,1)}, bf16[2,2,128,128]{3,2,1,0:T(8,128)(2,1)S(1)}, u32[]{:S(2)}, u32[]{:S(2)}) collective-permute-start(bf16[2,2,128,128]{3,2,1,0:T(8,128)(2,1)} %mine_ref.1), channel_id=1, source_target_pairs={{0,4},{4,0},{1,5},{5,1},{2,6},{6,2},{3,7},{7,3},{8,12},{12,8},{9,1... | collective-permute-start | bytes 393224 | tf_op jit(solution)/shard_map/ppermute | solution.py:333
  2.1 17.8 %collective-permute-start = (bf16[2,2,48,128]{3,2,1,0:T(8,128)(2,1)S(1)}, bf16[2,2,48,128]{3,2,1,0:T(8,128)(2,1)S(1)}, u32[]{:S(2)}, u32[]{:S(2)}) collective-permute-start(bf16[2,2,48,128]{3,2,1,0:T(8,128)(2,1)S(1)} %get-tuple-element.39), channel_id=1, source_target_pairs={{0,1},{1,0},{2,3},{3,2},{4,5},{5,4},{6,7},{7,6},{8,9},{9,8},{10,11... | collective-permute-start | bytes 147464 | tf_op jit(solution)/shard_map/ppermute | solution.py:333
  4.7 15.2 %collective-permute-start.1 = (bf16[2,2,48,128]{3,2,1,0:T(8,128)(2,1)S(1)}, bf16[2,2,48,128]{3,2,1,0:T(8,128)(2,1)S(1)}, u32[]{:S(2)}, u32[]{:S(2)}) collective-permute-start(bf16[2,2,48,128]{3,2,1,0:T(8,128)(2,1)S(1)} %get-tuple-element.40), channel_id=1, source_target_pairs={{0,2},{1,3},{2,0},{3,1},{4,6},{5,7},{6,4},{7,5},{8,10},{9,11},{10,... | collective-permute-start | bytes 147464 | tf_op jit(solution)/shard_map/ppermute | solution.py:333
  7.3 12.6 %collective-permute-start.2 = (bf16[2,2,48,128]{3,2,1,0:T(8,128)(2,1)S(1)}, bf16[2,2,48,128]{3,2,1,0:T(8,128)(2,1)S(1)}, u32[]{:S(2)}, u32[]{:S(2)}) collective-permute-start(bf16[2,2,48,128]{3,2,1,0:T(8,128)(2,1)S(1)} %get-tuple-element.41), channel_id=1, source_target_pairs={{0,3},{1,2},{2,1},{3,0},{4,7},{5,6},{6,5},{7,4},{8,11},{9,10},{10,... | collective-permute-start | bytes 147464 | tf_op jit(solution)/shard_map/ppermute | solution.py:333
  20.0 7.5 %collective-permute-start.3 = (bf16[4,2,2,48,128]{4,3,2,1,0:T(8,128)(2,1)S(1)}, bf16[4,2,2,48,128]{4,3,2,1,0:T(8,128)(2,1)S(1)}, u32[]{:S(2)}, u32[]{:S(2)}) collective-permute-start(bf16[4,2,2,48,128]{4,3,2,1,0:T(8,128)(2,1)S(1)} %pad_maximum_fusion.rest_2_), channel_id=1, source_target_pairs={{0,8},{1,9},{2,10},{3,11},{8,0},{9,1},{10,2},{11,3},{16,24},{17,25... | collective-permute-start | bytes 589832 | tf_op jit(solution)/shard_map/ppermute | solution.py:359
  21.6 8.9 %collective-permute-start.10 = (bf16[4,2,2,48,128]{4,3,2,1,0:T(8,128)(2,1)S(1)}, bf16[4,2,2,48,128]{4,3,2,1,0:T(8,128)(2,1)S(1)}, u32[]{:S(2)}, u32[]{:S(2)}) collective-permute-start(bf16[4,2,2,48,128]{4,3,2,1,0:T(8,128)(2,1)S(1)} %pad_maximum_fusion.rest_2_), channel_id=1, source_target_pairs={{8,16},{9,17},{10,18},{11,19},{16,8},{17,9},{18,10},{19,11},{12,20... | collective-permute-start | bytes 589832 | tf_op jit(solution)/shard_map/ppermute | solution.py:359
  22.3 7.3 %collective-permute-start.6 = (bf16[2,4,2,32,128]{4,3,2,1,0:T(8,128)(2,1)S(1)}, bf16[2,4,2,32,128]{4,3,2,1,0:T(8,128)(2,1)S(1)}, u32[]{:S(2)}, u32[]{:S(2)}) collective-permute-start(bf16[2,4,2,32,128]{4,3,2,1,0:T(8,128)(2,1)S(1)} %get-tuple-element.46), channel_id=1, source_target_pairs={{0,2},{1,3},{2,0},{3,1},{4,6},{5,7},{6,4},{7,5},{8,10},{9,11},{10,... | collective-permute-start | bytes 393224 | tf_op jit(solution)/shard_map/ppermute | solution.py:333
  27.5 11.3 %collective-permute-start.4 = (bf16[4,6,128,128]{3,2,1,0:T(8,128)(2,1)S(1)}, bf16[4,6,128,128]{3,2,1,0:T(8,128)(2,1)S(1)}, u32[]{:S(2)}, u32[]{:S(2)}) collective-permute-start(bf16[4,6,128,128]{3,2,1,0:T(8,128)(2,1)S(1)} %bitcast.31), channel_id=1, source_target_pairs={{0,4},{4,0},{1,5},{5,1},{2,6},{6,2},{3,7},{7,3},{8,12},{12,8},{9,1... | collective-permute-start | bytes 2359304 | tf_op jit(solution)/shard_map/ppermute | solution.py:333
  29.7 5.0 %collective-permute-start.7 = (bf16[2,4,2,32,128]{4,3,2,1,0:T(8,128)(2,1)S(1)}, bf16[2,4,2,32,128]{4,3,2,1,0:T(8,128)(2,1)S(1)}, u32[]{:S(2)}, u32[]{:S(2)}) collective-permute-start(bf16[2,4,2,32,128]{4,3,2,1,0:T(8,128)(2,1)S(1)} %pad_maximum_fusion.2), channel_id=1, source_target_pairs={{0,1},{1,0},{2,3},{3,2},{4,5},{5,4},{6,7},{7,6},{8,9},{9,8},{10,11... | collective-permute-start | bytes 393224 | tf_op jit(solution)/shard_map/ppermute | solution.py:333
  29.8 8.3 %collective-permute-start.11 = (bf16[4,2,2,48,128]{4,3,2,1,0:T(8,128)(2,1)S(1)}, bf16[4,2,2,48,128]{4,3,2,1,0:T(8,128)(2,1)S(1)}, u32[]{:S(2)}, u32[]{:S(2)}) collective-permute-start(bf16[4,2,2,48,128]{4,3,2,1,0:T(8,128)(2,1)S(1)} %pad_maximum_fusion.rest_2_), channel_id=1, source_target_pairs={{0,4},{4,0},{1,5},{5,1},{2,6},{6,2},{3,7},{7,3},{8,12},{12,8},{9,1... | collective-permute-start | bytes 589832 | tf_op jit(solution)/shard_map/ppermute | solution.py:333
  29.9 8.9 %collective-permute-start.12 = (bf16[4,2,2,48,128]{4,3,2,1,0:T(8,128)(2,1)S(1)}, bf16[4,2,2,48,128]{4,3,2,1,0:T(8,128)(2,1)S(1)}, u32[]{:S(2)}, u32[]{:S(2)}) collective-permute-start(bf16[4,2,2,48,128]{4,3,2,1,0:T(8,128)(2,1)S(1)} %collective-permute-done.3.rest_3_), channel_id=1, source_target_pairs={{0,4},{4,0},{1,5},{5,1},{2,6},{6,2},{3,7},{7,3},{8,12},{12,8},{9,1... | collective-permute-start | bytes 589832 | tf_op jit(solution)/shard_map/ppermute | solution.py:333
  30.4 8.4 %collective-permute-start.13 = (bf16[4,2,2,48,128]{4,3,2,1,0:T(8,128)(2,1)S(1)}, bf16[4,2,2,48,128]{4,3,2,1,0:T(8,128)(2,1)S(1)}, u32[]{:S(2)}, u32[]{:S(2)}) collective-permute-start(bf16[4,2,2,48,128]{4,3,2,1,0:T(8,128)(2,1)S(1)} %collective-permute-done.10.rest_4_), channel_id=1, source_target_pairs={{0,4},{4,0},{1,5},{5,1},{2,6},{6,2},{3,7},{7,3},{8,12},{12,8},{9,1... | collective-permute-start | bytes 589832 | tf_op jit(solution)/shard_map/ppermute | solution.py:333
  34.8 10.8 %collective-permute-start.8 = (bf16[2,4,2,32,128]{4,3,2,1,0:T(8,128)(2,1)S(1)}, bf16[2,4,2,32,128]{4,3,2,1,0:T(8,128)(2,1)S(1)}, u32[]{:S(2)}, u32[]{:S(2)}) collective-permute-start(bf16[2,4,2,32,128]{4,3,2,1,0:T(8,128)(2,1)S(1)} %get-tuple-element.78), channel_id=1, source_target_pairs={{0,8},{1,9},{2,10},{3,11},{8,0},{9,1},{10,2},{11,3},{16,24},{17,25... | collective-permute-start | bytes 393224 | tf_op jit(solution)/shard_map/ppermute | solution.py:359
  38.1 7.5 %collective-permute-start.9 = (bf16[2,4,2,32,128]{4,3,2,1,0:T(8,128)(2,1)S(1)}, bf16[2,4,2,32,128]{4,3,2,1,0:T(8,128)(2,1)S(1)}, u32[]{:S(2)}, u32[]{:S(2)}) collective-permute-start(bf16[2,4,2,32,128]{4,3,2,1,0:T(8,128)(2,1)S(1)} %get-tuple-element.77), channel_id=1, source_target_pairs={{8,16},{9,17},{10,18},{11,19},{16,8},{17,9},{18,10},{19,11},{12,20... | collective-permute-start | bytes 393224 | tf_op jit(solution)/shard_map/ppermute | solution.py:359
  53.8 4.4 %collective-permute-start.18 = (bf16[4,2,2,16,128]{4,3,2,1,0:T(8,128)(2,1)S(1)}, bf16[4,2,2,16,128]{4,3,2,1,0:T(8,128)(2,1)S(1)}, u32[]{:S(2)}, u32[]{:S(2)}) collective-permute-start(bf16[4,2,2,16,128]{4,3,2,1,0:T(8,128)(2,1)S(1)} %get-tuple-element.62), channel_id=1, source_target_pairs={{0,4},{4,0},{1,5},{5,1},{2,6},{6,2},{3,7},{7,3},{8,12},{12,8},{9,1... | collective-permute-start | bytes 196616 | tf_op jit(solution)/shard_map/ppermute | solution.py:333
  54.0 14.1 %collective-permute-start.15 = (bf16[6,128,128]{2,1,0:T(8,128)(2,1)S(1)}, bf16[6,128,128]{2,1,0:T(8,128)(2,1)S(1)}, u32[]{:S(2)}, u32[]{:S(2)}) collective-permute-start(bf16[6,128,128]{2,1,0:T(8,128)(2,1)S(1)} %get-tuple-element.58), channel_id=1, source_target_pairs={{0,8},{8,0},{16,24},{24,16},{1,9},{9,1},{17,25},{25,17},{2,10},{10... | collective-permute-start | bytes 589832 | tf_op jit(solution)/shard_map/ppermute | solution.py:333
  56.8 11.4 %collective-permute-start.16 = (bf16[6,128,128]{2,1,0:T(8,128)(2,1)S(1)}, bf16[6,128,128]{2,1,0:T(8,128)(2,1)S(1)}, u32[]{:S(2)}, u32[]{:S(2)}) collective-permute-start(bf16[6,128,128]{2,1,0:T(8,128)(2,1)S(1)} %get-tuple-element.59), channel_id=1, source_target_pairs={{0,16},{8,24},{16,0},{24,8},{1,17},{9,25},{17,1},{25,9},{2,18},{10... | collective-permute-start | bytes 589832 | tf_op jit(solution)/shard_map/ppermute | solution.py:333
  56.8 11.4 %collective-permute-start.17 = (bf16[6,128,128]{2,1,0:T(8,128)(2,1)S(1)}, bf16[6,128,128]{2,1,0:T(8,128)(2,1)S(1)}, u32[]{:S(2)}, u32[]{:S(2)}) collective-permute-start(bf16[6,128,128]{2,1,0:T(8,128)(2,1)S(1)} %get-tuple-element.60), channel_id=1, source_target_pairs={{0,24},{8,16},{16,8},{24,0},{1,25},{9,17},{17,9},{25,1},{2,26},{10... | collective-permute-start | bytes 589832 | tf_op jit(solution)/shard_map/ppermute | solution.py:333
  58.3 4.1 %collective-permute-start.19 = (bf16[2,2,32,128]{3,2,1,0:T(8,128)(2,1)S(1)}, bf16[2,2,32,128]{3,2,1,0:T(8,128)(2,1)S(1)}, u32[]{:S(2)}, u32[]{:S(2)}) collective-permute-start(bf16[2,2,32,128]{3,2,1,0:T(8,128)(2,1)S(1)} %get-tuple-element.81), channel_id=1, source_target_pairs={{0,1},{1,0},{2,3},{3,2},{4,5},{5,4},{6,7},{7,6},{8,9},{9,8},{10,11... | collective-permute-start | bytes 98312 | tf_op jit(solution)/shard_map/ppermute | solution.py:333
  58.4 6.5 %collective-permute-start.20 = (bf16[2,2,32,128]{3,2,1,0:T(8,128)(2,1)S(1)}, bf16[2,2,32,128]{3,2,1,0:T(8,128)(2,1)S(1)}, u32[]{:S(2)}, u32[]{:S(2)}) collective-permute-start(bf16[2,2,32,128]{3,2,1,0:T(8,128)(2,1)S(1)} %get-tuple-element.82), channel_id=1, source_target_pairs={{0,2},{1,3},{2,0},{3,1},{4,6},{5,7},{6,4},{7,5},{8,10},{9,11},{10,... | collective-permute-start | bytes 98312 | tf_op jit(solution)/shard_map/ppermute | solution.py:333
  62.5 5.7 %collective-permute-start.21 = (bf16[2,2,32,128]{3,2,1,0:T(8,128)(2,1)S(1)}, bf16[2,2,32,128]{3,2,1,0:T(8,128)(2,1)S(1)}, u32[]{:S(2)}, u32[]{:S(2)}) collective-permute-start(bf16[2,2,32,128]{3,2,1,0:T(8,128)(2,1)S(1)} %get-tuple-element.79), channel_id=1, source_target_pairs={{0,3},{1,2},{2,1},{3,0},{4,7},{5,6},{6,5},{7,4},{8,11},{9,10},{10,... | collective-permute-start | bytes 98312 | tf_op jit(solution)/shard_map/ppermute | solution.py:333
  68.3 4.7 %collective-permute-start.22 = (bf16[384,128]{1,0:T(8,128)(2,1)S(1)}, bf16[384,128]{1,0:T(8,128)(2,1)S(1)}, u32[]{:S(2)}, u32[]{:S(2)}) collective-permute-start(bf16[384,128]{1,0:T(8,128)(2,1)S(1)} %dynamic-slice_bitcast_fusion), channel_id=1, source_target_pairs={{0,1},{1,0},{2,3},{3,2},{4,5},{5,4},{6,7},{7,6},{8,9},{9,8},{10,11... | collective-permute-start | bytes 294920 | tf_op jit(solution)/shard_map/ppermute | solution.py:333
  73.0 6.1 %collective-permute-start.23 = (bf16[384,128]{1,0:T(8,128)(2,1)S(1)}, bf16[384,128]{1,0:T(8,128)(2,1)S(1)}, u32[]{:S(2)}, u32[]{:S(2)}) collective-permute-start(bf16[384,128]{1,0:T(8,128)(2,1)S(1)} %fusion.5), channel_id=1, source_target_pairs={{0,2},{1,3},{2,0},{3,1},{4,6},{5,7},{6,4},{7,5},{8,10},{9,11},{10,... | collective-permute-start | bytes 294920 | tf_op jit(solution)/shard_map/ppermute | solution.py:333
  79.2 4.7 %collective-permute-start.24 = (bf16[384,128]{1,0:T(8,128)(2,1)S(1)}, bf16[384,128]{1,0:T(8,128)(2,1)S(1)}, u32[]{:S(2)}, u32[]{:S(2)}) collective-permute-start(bf16[384,128]{1,0:T(8,128)(2,1)S(1)} %add_convert_fusion.5), channel_id=1, source_target_pairs={{0,1},{1,0},{2,3},{3,2},{4,5},{5,4},{6,7},{7,6},{8,9},{9,8},{10,11... | collective-permute-start | bytes 294920 | tf_op jit(solution)/shard_map/ppermute | solution.py:333
  (5 other events, 27.4 us)

commit v13 on v12

--- a/solution.py
+++ b/solution.py
@@ -112,22 +112,22 @@
         target[...] = wide_ref[:, :, pl.ds(pl.multiple_of(at, 16), span)].astype(BF16)
 
 
-def cotangent_kernel(halo, width, mine_ref, other_ref, *rest):
-    targets, wide_ref = rest[:-1], rest[-1]
-    count = targets[0].shape[0]
-    core, _, _, unit = placed(count * len(targets))
-    frames_in, rows, columns, chans = mine_ref.shape
-    edge = jnp.zeros((2 * frames_in, rows, halo, chans), F32)
-    wide_ref[:, :, :halo] = edge
-    wide_ref[:, :, halo + columns :] = edge
-    for whose, ref in ((core, mine_ref), (1 - core, other_ref)):
-        wide_ref[pl.ds(whose * frames_in, frames_in), :, halo : halo + columns] = ref[...].astype(F32)
+def cotangent_kernel(halo, width, *rest):
+    sources, targets, wide_ref = rest[:4], rest[4:-1], rest[-1]
+    core, _, _, unit = placed(len(targets))
+    frames_in, rows, columns, chans = sources[0].shape
+    edge = jnp.zeros((2, 2 * frames_in, rows, halo, chans), F32)
+    wide_ref[:, :, :, :halo] = edge
+    wide_ref[:, :, :, halo + columns :] = edge
+    for index, ref in enumerate(sources):
+        whose = core if index % 2 == 0 else 1 - core
+        wide_ref[index // 2, pl.ds(whose * frames_in, frames_in), :, halo : halo + columns] = ref[
+            ...
+        ].astype(F32)
     own = width - 2 * halo
-    for index, target in enumerate(targets):
-        for step in range(count):
-            at = (jnp.bitwise_xor(unit, index * count + step) * 2 + core) * own
-            at = pl.ds(pl.multiple_of(at, 16), width)
-            target[step] = wide_ref[:, :, at].astype(BF16)
+    for step, target in enumerate(targets):
+        at = (jnp.bitwise_xor(unit, step) * 2 + core) * own
+        target[...] = wide_ref[:, :, :, pl.ds(pl.multiple_of(at, 16), width)].astype(BF16)
 
 
 def closing_kernel(group, mine_ref, other_ref, spatial_ref, temporal_ref, flat_ref):
@@ -146,17 +146,25 @@
             temporal_ref[0, tap - count] = turned
 
 
+def place_kernels(core, section, w_ref, own_mine, own_other, mine_refs, other_refs):
+    w_ref[core, section] = own_mine[...]
+    w_ref[1 - core, section] = own_other[...]
+    for step, (mine_ref, other_ref) in enumerate(zip(mine_refs, other_refs)):
+        block = jnp.bitwise_xor(section, step + 1)
+        w_ref[core, block] = mine_ref[...]
+        w_ref[1 - core, block] = other_ref[...]
+
+
 def forward_kernel(geometry, *rest):
     blocks, cores, group, frames_in, rows_in, halo, tile, width, height, columns = geometry
     core, section, band, unit = placed(group)
     odd = band % 2
-    shared, rest = rest[:2], rest[2:]
+    shared, rest = rest[: 2 * blocks], rest[2 * blocks :]
     arrived, rest = rest[:6], rest[6:]
     xo_ref, ho_ref = rest[:2]
     d_refs = rest[2 : 2 + blocks]
     x_ref, h_ref, mask_ref, w_ref, start_ref, pair_ref = rest[2 + blocks :]
-    w_ref[core] = shared[0][...]
-    w_ref[1 - core] = shared[1][...]
+    place_kernels(core, section, w_ref, *shared[:2], shared[2 : 1 + blocks], shared[1 + blocks :])
     frames = cores * frames_in
     high = tile + 2 * halo
     chans = w_ref.shape[-1]
@@ -237,14 +245,13 @@
 def backward_kernel(geometry, factor, *rest):
     blocks, cores, group, frames_in, rows_in, halo, tile, width, height, columns = geometry
     core, section, band, unit = placed(group)
-    shared, rest = rest[:2], rest[2:]
-    arrived, rest = rest[:4], rest[4:]
+    shared, rest = rest[: 2 * blocks], rest[2 * blocks :]
+    arrived, rest = rest[:group], rest[group:]
     xo_ref, ho_ref = rest[:2]
     d_refs = rest[2 : 2 + blocks]
     keep_ref, give_ref, mine_out, other_out = rest[2 + blocks : 6 + blocks]
     g_ref, da_ref, dao_ref, go_ref, w_ref, grad_ref, out_ref, pair_ref = rest[6 + blocks :]
-    w_ref[core] = shared[0][...]
-    w_ref[1 - core] = shared[1][...]
+    place_kernels(core, section, w_ref, *shared[:2], shared[2 : 1 + blocks], shared[1 + blocks :])
     frames = cores * frames_in
     chans = w_ref.shape[-1]
     rim = blocks
@@ -252,14 +259,12 @@
     per_core = w_ref.shape[2]
     pixels = tile * (own_cols[1] - own_cols[0])
 
-    odd = band % 2
-    near = tile + rim - odd * (tile + rim)
     half = group // 2
-    for index, (base, ref) in enumerate(zip((rim, rim, near, tile + rim - near), arrived)):
-        for step in range(half):
-            at = jnp.bitwise_xor(unit, (half if index == 1 else 0) + step)
-            at = at if index < 2 else jnp.bitwise_and(at, half - 1)
-            g_ref[:, pl.ds(base + at * rows_in, rows_in)] = ref[step]
+    for step, ref in enumerate(arrived):
+        at = jnp.bitwise_xor(unit, step)
+        g_ref[:, pl.ds(rim + at * rows_in, rows_in)] = ref[0]
+        beyond = jnp.where(at < half, rim + tile + at * rows_in, (at - half) * rows_in)
+        g_ref[:, pl.ds(beyond, rows_in)] = ref[1]
 
     def put(block, tap, value):
         slot = jnp.where(core == tap // per_core, 0, 1)
@@ -360,6 +365,13 @@
 
     total_rows = blocks * tiles * rows_in
     half = group // 2
+    passed = []
+    for one in range(bands - 1):
+        for i in range(group):
+            low, high = one * group + i, (one + 1) * group + i
+            passed.append((high, low) if i < half else (low, high))
+    cot_halo = lax.ppermute(cotangent, ("section", "space"), passed)
+
     padded = columns + 2 * halo
     cuts = pl.pallas_call(
         functools.partial(window_kernel, halo, span),
@@ -370,17 +382,6 @@
         scratch_shapes=[pltpu.VMEM((frames_in, rows_in, padded, chans), F32)],
         compiler_params=params,
     )(video)
-    pair = jax.ShapeDtypeStruct((half, cores * frames_in, rows_in, width, chans), BF16)
-    low, high_pair = pl.pallas_call(
-        functools.partial(cotangent_kernel, halo, width),
-        name="cotangent",
-        in_specs=[vmem] * 2,
-        out_specs=[vmem] * 2,
-        out_shape=[pair] * 2,
-        scratch_shapes=[pltpu.VMEM((cores * frames_in, rows_in, padded, chans), F32)],
-        compiler_params=params,
-    )(cotangent, swapped(cotangent))
-
     def core_half(which, spatial, temporal):
         whole = jnp.concatenate([spatial[0], temporal[0]], 0)
         taps = whole.shape[0] // cores
@@ -392,25 +393,30 @@
     def gathered(pieces):
         return jnp.stack([pieces[0]] + [swapped(pieces[i], "space", i) for i in range(1, group)])
 
-    mine = lax.all_gather(half_kernels, "section")
+    along_x = swapped(half_kernels, "section", 1)
+    along_y = swapped(half_kernels, "section", 2)
     own_video = gathered(cuts)
     near, far = traded(own_video, 0), traded(own_video, 1)
-    near, mine = lax.optimization_barrier([near, mine])
-    shared = [mine, swapped(mine)]
+    _, along_x, along_y, cot_halo, spatial, temporal = lax.optimization_barrier(
+        [own_video, along_x, along_y, cot_halo, spatial_weights, temporal_weights]
+    )
+    mine = [along_x, along_y, swapped(along_x, "section", 2)]
+    rest_kernels = core_half(1 - core, spatial, temporal)
+    shared = [half_kernels, rest_kernels] + mine + [swapped(each) for each in mine]
+
+    cots = pl.pallas_call(
+        functools.partial(cotangent_kernel, halo, width),
+        name="cotangent",
+        in_specs=[vmem] * 4,
+        out_specs=[vmem] * group,
+        out_shape=[jax.ShapeDtypeStruct((2, cores * frames_in, rows_in, width, chans), BF16)] * group,
+        scratch_shapes=[pltpu.VMEM((2, cores * frames_in, rows_in, padded, chans), F32)],
+        compiler_params=params,
+    )(cotangent, swapped(cotangent), cot_halo, swapped(cot_halo))
+    cots = [cots[0]] + [swapped(cots[i], "space", i) for i in range(1, group)]
+    near, cots[1] = lax.optimization_barrier([near, cots[1]])
     videos = [own_video, near, far]
     videos += [swapped(each) for each in videos]
-
-    from_far = swapped(high_pair, "space", 2)
-    from_near = swapped(jnp.stack([low[1], from_far[1]]), "space", 1)
-    low = jnp.stack([low[0], from_near[0]])
-    high_pair = jnp.stack([from_far[0], from_near[1]])
-    upper = unit < half
-    cots = [
-        low,
-        high_pair,
-        traded(jnp.where(upper == (odd == 1), low, high_pair), 0),
-        traded(jnp.where(upper == (odd == 0), low, high_pair), 1),
-    ]
 
     geometry = (blocks, cores, group, frames_in, rows_in, halo, tile, width, total_rows, columns)
     frames = cores * frames_in
@@ -426,7 +432,7 @@
     features, hidden, *slopes = pl.pallas_call(
         functools.partial(forward_kernel, geometry),
         name="forward",
-        in_specs=[vmem] * 8,
+        in_specs=[vmem] * (2 * blocks + 6),
         out_specs=[vmem] * (2 + blocks),
         out_shape=[
             jax.ShapeDtypeStruct((blocks, frames, tile + 2, own_width, 3 * chans), BF16),
@@ -451,7 +457,7 @@
     keep, give, mine_grad, other_grad = pl.pallas_call(
         functools.partial(backward_kernel, geometry, factor),
         name="backward",
-        in_specs=[vmem] * (blocks + 8),
+        in_specs=[vmem] * (3 * blocks + group + 2),
         out_specs=[vmem] * 4,
         out_shape=[
             jax.ShapeDtypeStruct(per_section, BF16),
@@ -487,20 +493,21 @@
     parts, strips = received[:blocks], received[blocks:]
     part = sum(each.astype(F32) for each in parts).astype(BF16)
 
-    halves = part.reshape(2, -1, chans)
-    low = unit % 2
-
-    def picked(which):
-        return lax.dynamic_index_in_dim(halves, which, 0, keepdims=False)
-
-    part = (picked(low).astype(F32) + swapped(picked(1 - low), "space", 1).astype(F32)).astype(BF16)
-    part = part.astype(F32) + swapped(part, "space", 2).astype(F32)
+    units = part.reshape(group, -1, chans)
+
+    def chunk(step):
+        return lax.dynamic_index_in_dim(units, unit ^ step, 0, keepdims=False)
+
+    part = sum(
+        each.astype(F32)
+        for each in [chunk(0)] + [swapped(chunk(i), "space", i) for i in range(1, group)]
+    )
     if tiles != group:
         part = lax.psum(
             part, "space", axis_index_groups=[list(range(i, tiles, group)) for i in range(group)]
         )
     part = part.astype(BF16)
-    pair = jnp.stack([part, swapped(part, "space", 1)])
+    pair = jnp.stack([part] + [swapped(part, "space", i) for i in range(1, group)])
     spatial_out, temporal_out = pl.pallas_call(
         functools.partial(closing_kernel, group),
         name="closing",

time: 86.7 us -> 90.5 us (1.044)
  starting transfers between devices: 25.4 us -> 42.7 us
  blocking collectives: 11.6 us -> 0 us
  waiting for transfers between devices: 32.3 us -> 29 us
  other arithmetic: 1.53 us -> 2.46 us
    ppermute x22 -> x32, starting transfers between devices: 19.2 us -> 39.3 us  [swapped(): return lax.ppermute(value, axis, [(i, i ^ step) for i in range(count)])]
    all_gather x1 -> x0, blocking collectives: 11.6 us -> none  [on_device(): mine = lax.all_gather(half_kernels, 'section')]
    ppermute x4 -> x2, starting transfers between devices: 6.22 us -> 2.16 us  [traded(): return lax.ppermute(value, ('section', 'space'), pairs)]
    ppermute x4 -> x2, waiting for transfers between devices: 3.61 us -> 0.01 us  [traded(): return lax.ppermute(value, ('section', 'space'), pairs)]
    ppermute x0 -> x1, waiting for transfers between devices: none -> 1.37 us  [on_device(): cot_halo = lax.ppermute(cotangent, ('section', 'space'), passed)]
    ppermute x0 -> x1, starting transfers between devices: none -> 1.28 us  [on_device(): cot_halo = lax.ppermute(cotangent, ('section', 'space'), passed)]
    ppermute x22 -> x32, waiting for transfers between devices: 28.7 us -> 27.6 us  [swapped(): return lax.ppermute(value, axis, [(i, i ^ step) for i in range(count)])]
    concatenate x1 -> x2, other arithmetic: 0.99 us -> 2 us  [core_half(): whole = jnp.concatenate([spatial[0], temporal[0]], 0)]
  transfers between devices with their start and end apart: 26 -> 35, of which waited for: 10 -> 14; matrix products, arithmetic and copies ran while one was open for 1% -> 1% of each run, Pallas kernels for 8% -> 7%
where the time goes in v13:
time: 90.5 us; the launch traced here: 90.2 us
  starting transfers between devices  42.7 us (47%)
  waiting for transfers between devices  29 us (32%)
  Pallas kernels  13.4 us (15%)
  other arithmetic  2.46 us (3%)
  local copies, waits for them, and re-layouts  1.9 us (2%)
    ppermute x32, starting transfers between devices, swapped(): return lax.ppermute(value, axis, [(i, i ^ step) for i in range(count)])  39.3 us
    ppermute x32, waiting for transfers between devices, swapped(): return lax.ppermute(value, axis, [(i, i ^ step) for i in range(count)])  27.6 us
    pallas_call x1, Pallas kernels, on_device(): pl.pallas_call(functools.partial(forward_kernel, geometry), name='forward...  6.48 us
    pallas_call x1, Pallas kernels, on_device(): pl.pallas_call(functools.partial(backward_kernel, geometry, factor), name...  5.63 us
    ppermute x2, starting transfers between devices, traded(): return lax.ppermute(value, ('section', 'space'), pairs)  2.16 us
    concatenate x2, other arithmetic, core_half(): whole = jnp.concatenate([spatial[0], temporal[0]], 0)  2 us
  transfers between devices with their start and end apart: 35, of which 14 were waited for; matrix products, arithmetic and copies ran while one was open for 1% of the time, Pallas kernels for 7%

profile of v13, /device:TPU:0, one launch (start us, length us, event | category | flops | bytes accessed | tf_op | source)
XLA Modules:
  0.0 90.2 jit_solution(16601155642073973575)
XLA Ops:
  2.6 3.0 %collective-permute-start.3 = (bf16[6,128,128]{2,1,0:T(8,128)(2,1)S(1)}, bf16[6,128,128]{2,1,0:T(8,128)(2,1)S(1)}, u32[]{:S(2)}, u32[]{:S(2)}) collective-permute-start(bf16[6,128,128]{2,1,0:T(8,128)(2,1)S(1)} %fusion.5.rest_0_), channel_id=1, source_target_pairs={{0,8},{8,0},{16,24},{24,16},{1,9},{9,1},{17,25},{25,17},{2,10},{10... | collective-permute-start | bytes 589832 | tf_op jit(solution)/shard_map/ppermute | solution.py:338
  5.6 1.5 %collective-permute-start.4 = (bf16[6,128,128]{2,1,0:T(8,128)(2,1)S(1)}, bf16[6,128,128]{2,1,0:T(8,128)(2,1)S(1)}, u32[]{:S(2)}, u32[]{:S(2)}) collective-permute-start(bf16[6,128,128]{2,1,0:T(8,128)(2,1)S(1)} %fusion.5.rest_0_), channel_id=1, source_target_pairs={{0,16},{8,24},{16,0},{24,8},{1,17},{9,25},{17,1},{25,9},{2,18},{10... | collective-permute-start | bytes 589832 | tf_op jit(solution)/shard_map/ppermute | solution.py:338
  7.1 1.6 %collective-permute-start = (bf16[2,2,48,128]{3,2,1,0:T(8,128)(2,1)S(1)}, bf16[2,2,48,128]{3,2,1,0:T(8,128)(2,1)S(1)}, u32[]{:S(2)}, u32[]{:S(2)}) collective-permute-start(bf16[2,2,48,128]{3,2,1,0:T(8,128)(2,1)S(1)} %get-tuple-element.48), channel_id=1, source_target_pairs={{0,1},{1,0},{2,3},{3,2},{4,5},{5,4},{6,7},{7,6},{8,9},{9,8},{10,11... | collective-permute-start | bytes 147464 | tf_op jit(solution)/shard_map/ppermute | solution.py:338
  8.7 2.6 %collective-permute-start.1 = (bf16[2,2,48,128]{3,2,1,0:T(8,128)(2,1)S(1)}, bf16[2,2,48,128]{3,2,1,0:T(8,128)(2,1)S(1)}, u32[]{:S(2)}, u32[]{:S(2)}) collective-permute-start(bf16[2,2,48,128]{3,2,1,0:T(8,128)(2,1)S(1)} %get-tuple-element.49), channel_id=1, source_target_pairs={{0,2},{1,3},{2,0},{3,1},{4,6},{5,7},{6,4},{7,5},{8,10},{9,11},{10,... | collective-permute-start | bytes 147464 | tf_op jit(solution)/shard_map/ppermute | solution.py:338
  14.2 3.0 %collective-permute-done.2 = bf16[2,2,48,128]{3,2,1,0:T(8,128)(2,1)S(1)} collective-permute-done((bf16[2,2,48,128]{3,2,1,0:T(8,128)(2,1)S(1)}, bf16[2,2,48,128]{3,2,1,0:T(8,128)(2,1)S(1)}, u32[]{:S(2)}, u32[]{:S(2)}) %collective-permute-start.2) | collective-permute-done | bytes 49184 | tf_op jit(solution)/shard_map/ppermute | solution.py:338
  18.6 1.5 %collective-permute-start.12 = (bf16[4,2,2,48,128]{4,3,2,1,0:T(8,128)(2,1)S(1)}, bf16[4,2,2,48,128]{4,3,2,1,0:T(8,128)(2,1)S(1)}, u32[]{:S(2)}, u32[]{:S(2)}) collective-permute-start(bf16[4,2,2,48,128]{4,3,2,1,0:T(8,128)(2,1)S(1)} %pad_maximum_fusion.rest_8_), channel_id=1, source_target_pairs={{0,8},{1,9},{2,10},{3,11},{8,0},{9,1},{10,2},{11,3},{16,24},{17,25... | collective-permute-start | bytes 589832 | tf_op jit(solution)/shard_map/ppermute | solution.py:364
  20.8 3.4 %collective-permute-start.6 = (bf16[6,128,128]{2,1,0:T(8,128)(2,1)S(1)}, bf16[6,128,128]{2,1,0:T(8,128)(2,1)S(1)}, u32[]{:S(2)}, u32[]{:S(2)}) collective-permute-start(bf16[6,128,128]{2,1,0:T(8,128)(2,1)S(1)} %collective-permute-done.3.rest_2_), channel_id=1, source_target_pairs={{0,16},{8,24},{16,0},{24,8},{1,17},{9,25},{17,1},{25,9},{2,18},{10... | collective-permute-start | bytes 589832 | tf_op jit(solution)/shard_map/ppermute | solution.py:338
  27.0 5.5 %collective-permute-done.6.rest_4_ = bf16[6,128,128]{2,1,0:T(8,128)(2,1)S(1)} collective-permute-done((bf16[6,128,128]{2,1,0:T(8,128)(2,1)S(1)}, bf16[6,128,128]{2,1,0:T(8,128)(2,1)S(1)}, u32[]{:S(2)}, u32[]{:S(2)}) %collective-permute-start.6) | collective-permute-done | bytes 196640 | tf_op jit(solution)/shard_map/ppermute | solution.py:338
  35.3 2.5 %collective-permute-start.15 = (bf16[2,4,2,32,128]{4,3,2,1,0:T(8,128)(2,1)S(1)}, bf16[2,4,2,32,128]{4,3,2,1,0:T(8,128)(2,1)S(1)}, u32[]{:S(2)}, u32[]{:S(2)}) collective-permute-start(bf16[2,4,2,32,128]{4,3,2,1,0:T(8,128)(2,1)S(1)} %get-tuple-element.60), channel_id=1, source_target_pairs={{0,3},{1,2},{2,1},{3,0},{4,7},{5,6},{6,5},{7,4},{8,11},{9,10},{10,... | collective-permute-start | bytes 393224 | tf_op jit(solution)/shard_map/ppermute | solution.py:338
  37.8 6.5 %forward.1 = (bf16[4,4,10,16,384]{4,3,2,1,0:T(8,128)(2,1)S(1)}, bf16[4,4,8,16,128]{4,3,2,1,0:T(8,128)(2,1)S(1)}, f32[4,10,32,128]{3,2,1,0:T(8,128)S(1)}, f32[4,1...) custom-call(bf16[6,128,128]{2,1,0:T(8,128)(2,1)S(1)} %fusion.5.rest_0_, ...), custom_call_target="tpu_custom_call" | custom-call | flops 6000000000 | bytes 8000000 | tf_op jit(solution)/shard_map/forward/pallas_call | solution.py:432
  44.3 2.7 %collective-permute-done.14.rest_10_ = bf16[2,4,2,32,128]{4,3,2,1,0:T(8,128)(2,1)S(1)} collective-permute-done((bf16[2,4,2,32,128]{4,3,2,1,0:T(8,128)(2,1)S(1)}, bf16[2,4,2,32,128]{4,3,2,1,0:T(8,128)(2,1)S(1)}, u32[]{:S(2)}, u32[]{:S(2)}) %collective-permute-start.14) | collective-permute-done | bytes 131104 | tf_op jit(solution)/shard_map/ppermute | solution.py:338
  47.0 5.6 %backward.1 = (bf16[4,6,128,128]{3,2,1,0:T(8,128)(2,1)S(1)}, bf16[4,6,128,128]{3,2,1,0:T(8,128)(2,1)S(1)}, bf16[4,2,2,16,128]{4,3,2,1,0:T(8,128)(2,1)S(1)}, bf16[4,2,2,16,128]{4,3,2,1,0:T(8,128)(2,1)S(1)}) custom-call(bf16[6,128,128]{2,1,0:T(8,128)(2,1)S(1)} %fusion.5.rest_0_, bf16[6,128,128]{2,1,0:T(8,128)(2,1)S(1)} %fusion.4.rest_1_, ...), custom_call_target="tpu_custom_call" | custom-call | flops 6000000000 | bytes 8000000 | tf_op jit(solution)/shard_map/backward/pallas_call | solution.py:457
  52.7 2.3 %collective-permute-done.20 = bf16[4,6,128,128]{3,2,1,0:T(8,128)(2,1)S(1)} collective-permute-done((bf16[4,6,128,128]{3,2,1,0:T(8,128)(2,1)S(1)}, bf16[4,6,128,128]{3,2,1,0:T(8,128)(2,1)S(1)}, u32[]{:S(2)}, u32[]{:S(2)}) %collective-permute-start.20) | collective-permute-done | bytes 786464 | tf_op jit(solution)/shard_map/ppermute | solution.py:338
  55.4 1.6 %collective-permute-start.21 = (bf16[6,128,128]{2,1,0:T(8,128)(2,1)S(1)}, bf16[6,128,128]{2,1,0:T(8,128)(2,1)S(1)}, u32[]{:S(2)}, u32[]{:S(2)}) collective-permute-start(bf16[6,128,128]{2,1,0:T(8,128)(2,1)S(1)} %get-tuple-element.72), channel_id=1, source_target_pairs={{0,8},{8,0},{16,24},{24,16},{1,9},{9,1},{17,25},{25,17},{2,10},{10... | collective-permute-start | bytes 589832 | tf_op jit(solution)/shard_map/ppermute | solution.py:338
  59.4 3.0 %collective-permute-start.25 = (bf16[2,2,32,128]{3,2,1,0:T(8,128)(2,1)S(1)}, bf16[2,2,32,128]{3,2,1,0:T(8,128)(2,1)S(1)}, u32[]{:S(2)}, u32[]{:S(2)}) collective-permute-start(bf16[2,2,32,128]{3,2,1,0:T(8,128)(2,1)S(1)} %get-tuple-element.96), channel_id=1, source_target_pairs={{0,1},{1,0},{2,3},{3,2},{4,5},{5,4},{6,7},{7,6},{8,9},{9,8},{10,11... | collective-permute-start | bytes 98312 | tf_op jit(solution)/shard_map/ppermute | solution.py:338
  62.4 1.5 %collective-permute-start.26 = (bf16[2,2,32,128]{3,2,1,0:T(8,128)(2,1)S(1)}, bf16[2,2,32,128]{3,2,1,0:T(8,128)(2,1)S(1)}, u32[]{:S(2)}, u32[]{:S(2)}) collective-permute-start(bf16[2,2,32,128]{3,2,1,0:T(8,128)(2,1)S(1)} %get-tuple-element.97), channel_id=1, source_target_pairs={{0,2},{1,3},{2,0},{3,1},{4,6},{5,7},{6,4},{7,5},{8,10},{9,11},{10,... | collective-permute-start | bytes 98312 | tf_op jit(solution)/shard_map/ppermute | solution.py:338
  64.3 2.9 %collective-permute-start.27 = (bf16[2,2,32,128]{3,2,1,0:T(8,128)(2,1)S(1)}, bf16[2,2,32,128]{3,2,1,0:T(8,128)(2,1)S(1)}, u32[]{:S(2)}, u32[]{:S(2)}) collective-permute-start(bf16[2,2,32,128]{3,2,1,0:T(8,128)(2,1)S(1)} %get-tuple-element.94), channel_id=1, source_target_pairs={{0,3},{1,2},{2,1},{3,0},{4,7},{5,6},{6,5},{7,4},{8,11},{9,10},{10,... | collective-permute-start | bytes 98312 | tf_op jit(solution)/shard_map/ppermute | solution.py:338
  67.3 2.8 %collective-permute-done.27 = bf16[2,2,32,128]{3,2,1,0:T(8,128)(2,1)S(1)} collective-permute-done((bf16[2,2,32,128]{3,2,1,0:T(8,128)(2,1)S(1)}, bf16[2,2,32,128]{3,2,1,0:T(8,128)(2,1)S(1)}, u32[]{:S(2)}, u32[]{:S(2)}) %collective-permute-start.27) | collective-permute-done | bytes 32800 | tf_op jit(solution)/shard_map/ppermute | solution.py:338
  70.3 1.6 %collective-permute-start.28 = (bf16[192,128]{1,0:T(8,128)(2,1)S(1)}, bf16[192,128]{1,0:T(8,128)(2,1)S(1)}, u32[]{:S(2)}, u32[]{:S(2)}) collective-permute-start(bf16[192,128]{1,0:T(8,128)(2,1)S(1)} %get-tuple-element.91), channel_id=1, source_target_pairs={{0,1},{1,0},{2,3},{3,2},{4,5},{5,4},{6,7},{7,6},{8,9},{9,8},{10,11... | collective-permute-start | bytes 147464 | tf_op jit(solution)/shard_map/ppermute | solution.py:338
  71.9 1.8 %collective-permute-start.29 = (bf16[192,128]{1,0:T(8,128)(2,1)S(1)}, bf16[192,128]{1,0:T(8,128)(2,1)S(1)}, u32[]{:S(2)}, u32[]{:S(2)}) collective-permute-start(bf16[192,128]{1,0:T(8,128)(2,1)S(1)} %get-tuple-element.93), channel_id=1, source_target_pairs={{0,2},{1,3},{2,0},{3,1},{4,6},{5,7},{6,4},{7,5},{8,10},{9,11},{10,... | collective-permute-start | bytes 147464 | tf_op jit(solution)/shard_map/ppermute | solution.py:338
  75.1 3.3 %collective-permute-done.29 = bf16[192,128]{1,0:T(8,128)(2,1)S(1)} collective-permute-done((bf16[192,128]{1,0:T(8,128)(2,1)S(1)}, bf16[192,128]{1,0:T(8,128)(2,1)S(1)}, u32[]{:S(2)}, u32[]{:S(2)}) %collective-permute-start.29) | collective-permute-done | bytes 49184 | tf_op jit(solution)/shard_map/ppermute | solution.py:338
  79.8 1.9 %collective-permute-start.32 = (bf16[192,128]{1,0:T(8,128)(2,1)S(1)}, bf16[192,128]{1,0:T(8,128)(2,1)S(1)}, u32[]{:S(2)}, u32[]{:S(2)}) collective-permute-start(bf16[192,128]{1,0:T(8,128)(2,1)S(1)} %fusion.8), channel_id=1, source_target_pairs={{0,2},{1,3},{2,0},{3,1},{4,6},{5,7},{6,4},{7,5},{8,10},{9,11},{10,... | collective-permute-start | bytes 147464 | tf_op jit(solution)/shard_map/ppermute | solution.py:338
  81.7 2.4 %collective-permute-start.33 = (bf16[192,128]{1,0:T(8,128)(2,1)S(1)}, bf16[192,128]{1,0:T(8,128)(2,1)S(1)}, u32[]{:S(2)}, u32[]{:S(2)}) collective-permute-start(bf16[192,128]{1,0:T(8,128)(2,1)S(1)} %fusion.8), channel_id=1, source_target_pairs={{0,3},{1,2},{2,1},{3,0},{4,7},{5,6},{6,5},{7,4},{8,11},{9,10},{10,... | collective-permute-start | bytes 147464 | tf_op jit(solution)/shard_map/ppermute | solution.py:338
  84.9 2.7 %collective-permute-done.33 = bf16[192,128]{1,0:T(8,128)(2,1)S(1)} collective-permute-done((bf16[192,128]{1,0:T(8,128)(2,1)S(1)}, bf16[192,128]{1,0:T(8,128)(2,1)S(1)}, u32[]{:S(2)}, u32[]{:S(2)}) %collective-permute-start.33) | collective-permute-done | bytes 49184 | tf_op jit(solution)/shard_map/ppermute | solution.py:338
  (72 shorter events, 22.2 us)
Async XLA Ops:
  2.6 16.0 %collective-permute-start.3 = (bf16[6,128,128]{2,1,0:T(8,128)(2,1)S(1)}, bf16[6,128,128]{2,1,0:T(8,128)(2,1)S(1)}, u32[]{:S(2)}, u32[]{:S(2)}) collective-permute-start(bf16[6,128,128]{2,1,0:T(8,128)(2,1)S(1)} %fusion.5.rest_0_), channel_id=1, source_target_pairs={{0,8},{8,0},{16,24},{24,16},{1,9},{9,1},{17,25},{25,17},{2,10},{10... | collective-permute-start | bytes 589832 | tf_op jit(solution)/shard_map/ppermute | solution.py:338
  5.6 13.0 %collective-permute-start.4 = (bf16[6,128,128]{2,1,0:T(8,128)(2,1)S(1)}, bf16[6,128,128]{2,1,0:T(8,128)(2,1)S(1)}, u32[]{:S(2)}, u32[]{:S(2)}) collective-permute-start(bf16[6,128,128]{2,1,0:T(8,128)(2,1)S(1)} %fusion.5.rest_0_), channel_id=1, source_target_pairs={{0,16},{8,24},{16,0},{24,8},{1,17},{9,25},{17,1},{25,9},{2,18},{10... | collective-permute-start | bytes 589832 | tf_op jit(solution)/shard_map/ppermute | solution.py:338
  8.7 5.5 %collective-permute-start.1 = (bf16[2,2,48,128]{3,2,1,0:T(8,128)(2,1)S(1)}, bf16[2,2,48,128]{3,2,1,0:T(8,128)(2,1)S(1)}, u32[]{:S(2)}, u32[]{:S(2)}) collective-permute-start(bf16[2,2,48,128]{3,2,1,0:T(8,128)(2,1)S(1)} %get-tuple-element.49), channel_id=1, source_target_pairs={{0,2},{1,3},{2,0},{3,1},{4,6},{5,7},{6,4},{7,5},{8,10},{9,11},{10,... | collective-permute-start | bytes 147464 | tf_op jit(solution)/shard_map/ppermute | solution.py:338
  11.3 5.9 %collective-permute-start.2 = (bf16[2,2,48,128]{3,2,1,0:T(8,128)(2,1)S(1)}, bf16[2,2,48,128]{3,2,1,0:T(8,128)(2,1)S(1)}, u32[]{:S(2)}, u32[]{:S(2)}) collective-permute-start(bf16[2,2,48,128]{3,2,1,0:T(8,128)(2,1)S(1)} %get-tuple-element.50), channel_id=1, source_target_pairs={{0,3},{1,2},{2,1},{3,0},{4,7},{5,6},{6,5},{7,4},{8,11},{9,10},{10,... | collective-permute-start | bytes 147464 | tf_op jit(solution)/shard_map/ppermute | solution.py:338
  11.5 7.1 %collective-permute-start.5 = (bf16[2,2,128,128]{3,2,1,0:T(8,128)(2,1)}, bf16[2,2,128,128]{3,2,1,0:T(8,128)(2,1)S(1)}, u32[]{:S(2)}, u32[]{:S(2)}) collective-permute-start(bf16[2,2,128,128]{3,2,1,0:T(8,128)(2,1)} %rest_0_.1), channel_id=1, source_target_pairs={{8,0},{9,1},{2,10},{3,11},{16,8},{17,9},{10,18},{11,19},{24,16},{2... | collective-permute-start | bytes 393224 | tf_op jit(solution)/shard_map/ppermute | solution.py:373
  14.2 9.9 %collective-permute-start.10 = (bf16[2,2,128,128]{3,2,1,0:T(8,128)(2,1)}, bf16[2,2,128,128]{3,2,1,0:T(8,128)(2,1)S(1)}, u32[]{:S(2)}, u32[]{:S(2)}) collective-permute-start(bf16[2,2,128,128]{3,2,1,0:T(8,128)(2,1)} %rest_0_.1), channel_id=1, source_target_pairs={{0,4},{4,0},{1,5},{5,1},{2,6},{6,2},{3,7},{7,3},{8,12},{12,8},{9,1... | collective-permute-start | bytes 393224 | tf_op jit(solution)/shard_map/ppermute | solution.py:338
  18.6 5.5 %collective-permute-start.11 = (bf16[2,2,128,128]{3,2,1,0:T(8,128)(2,1)S(1)}, bf16[2,2,128,128]{3,2,1,0:T(8,128)(2,1)S(1)}, u32[]{:S(2)}, u32[]{:S(2)}) collective-permute-start(bf16[2,2,128,128]{3,2,1,0:T(8,128)(2,1)S(1)} %collective-permute-done.5.rest_2_), channel_id=1, source_target_pairs={{0,4},{4,0},{1,5},{5,1},{2,6},{6,2},{3,7},{7,3},{8,12},{12,8},{9,1... | collective-permute-start | bytes 393224 | tf_op jit(solution)/shard_map/ppermute | solution.py:338
  18.6 7.9 %collective-permute-start.12 = (bf16[4,2,2,48,128]{4,3,2,1,0:T(8,128)(2,1)S(1)}, bf16[4,2,2,48,128]{4,3,2,1,0:T(8,128)(2,1)S(1)}, u32[]{:S(2)}, u32[]{:S(2)}) collective-permute-start(bf16[4,2,2,48,128]{4,3,2,1,0:T(8,128)(2,1)S(1)} %pad_maximum_fusion.rest_8_), channel_id=1, source_target_pairs={{0,8},{1,9},{2,10},{3,11},{8,0},{9,1},{10,2},{11,3},{16,24},{17,25... | collective-permute-start | bytes 589832 | tf_op jit(solution)/shard_map/ppermute | solution.py:364
  20.1 6.7 %collective-permute-start.16 = (bf16[4,2,2,48,128]{4,3,2,1,0:T(8,128)(2,1)S(1)}, bf16[4,2,2,48,128]{4,3,2,1,0:T(8,128)(2,1)S(1)}, u32[]{:S(2)}, u32[]{:S(2)}) collective-permute-start(bf16[4,2,2,48,128]{4,3,2,1,0:T(8,128)(2,1)S(1)} %pad_maximum_fusion.rest_8_), channel_id=1, source_target_pairs={{8,16},{9,17},{10,18},{11,19},{16,8},{17,9},{18,10},{19,11},{12,20... | collective-permute-start | bytes 589832 | tf_op jit(solution)/shard_map/ppermute | solution.py:364
  20.8 11.8 %collective-permute-start.6 = (bf16[6,128,128]{2,1,0:T(8,128)(2,1)S(1)}, bf16[6,128,128]{2,1,0:T(8,128)(2,1)S(1)}, u32[]{:S(2)}, u32[]{:S(2)}) collective-permute-start(bf16[6,128,128]{2,1,0:T(8,128)(2,1)S(1)} %collective-permute-done.3.rest_2_), channel_id=1, source_target_pairs={{0,16},{8,24},{16,0},{24,8},{1,17},{9,25},{17,1},{25,9},{2,18},{10... | collective-permute-start | bytes 589832 | tf_op jit(solution)/shard_map/ppermute | solution.py:338
  24.1 8.9 %collective-permute-start.17 = (bf16[4,2,2,48,128]{4,3,2,1,0:T(8,128)(2,1)S(1)}, bf16[4,2,2,48,128]{4,3,2,1,0:T(8,128)(2,1)S(1)}, u32[]{:S(2)}, u32[]{:S(2)}) collective-permute-start(bf16[4,2,2,48,128]{4,3,2,1,0:T(8,128)(2,1)S(1)} %pad_maximum_fusion.rest_8_), channel_id=1, source_target_pairs={{0,4},{4,0},{1,5},{5,1},{2,6},{6,2},{3,7},{7,3},{8,12},{12,8},{9,1... | collective-permute-start | bytes 589832 | tf_op jit(solution)/shard_map/ppermute | solution.py:338
  25.2 7.4 %collective-permute-start.13 = (bf16[2,4,2,32,128]{4,3,2,1,0:T(8,128)(2,1)S(1)}, bf16[2,4,2,32,128]{4,3,2,1,0:T(8,128)(2,1)S(1)}, u32[]{:S(2)}, u32[]{:S(2)}) collective-permute-start(bf16[2,4,2,32,128]{4,3,2,1,0:T(8,128)(2,1)S(1)} %get-tuple-element.57), channel_id=1, source_target_pairs={{0,1},{1,0},{2,3},{3,2},{4,5},{5,4},{6,7},{7,6},{8,9},{9,8},{10,11... | collective-permute-start | bytes 393224 | tf_op jit(solution)/shard_map/ppermute | solution.py:338
  26.5 7.6 %collective-permute-start.7 = (bf16[6,128,128]{2,1,0:T(8,128)(2,1)S(1)}, bf16[6,128,128]{2,1,0:T(8,128)(2,1)S(1)}, u32[]{:S(2)}, u32[]{:S(2)}) collective-permute-start(bf16[6,128,128]{2,1,0:T(8,128)(2,1)S(1)} %collective-permute-done.3.rest_2_), channel_id=1, source_target_pairs={{0,4},{4,0},{1,5},{5,1},{2,6},{6,2},{3,7},{7,3},{8,12},{12,8},{9,1... | collective-permute-start | bytes 589832 | tf_op jit(solution)/shard_map/ppermute | solution.py:338
  26.7 8.6 %collective-permute-start.8 = (bf16[6,128,128]{2,1,0:T(8,128)(2,1)S(1)}, bf16[6,128,128]{2,1,0:T(8,128)(2,1)S(1)}, u32[]{:S(2)}, u32[]{:S(2)}) collective-permute-start(bf16[6,128,128]{2,1,0:T(8,128)(2,1)S(1)} %collective-permute-done.4.rest_3_), channel_id=1, source_target_pairs={{0,4},{4,0},{1,5},{5,1},{2,6},{6,2},{3,7},{7,3},{8,12},{12,8},{9,1... | collective-permute-start | bytes 589832 | tf_op jit(solution)/shard_map/ppermute | solution.py:338
  32.5 5.3 %collective-permute-start.19 = (bf16[4,2,2,48,128]{4,3,2,1,0:T(8,128)(2,1)S(1)}, bf16[4,2,2,48,128]{4,3,2,1,0:T(8,128)(2,1)S(1)}, u32[]{:S(2)}, u32[]{:S(2)}) collective-permute-start(bf16[4,2,2,48,128]{4,3,2,1,0:T(8,128)(2,1)S(1)} %collective-permute-done.16.rest_10_), channel_id=1, source_target_pairs={{0,4},{4,0},{1,5},{5,1},{2,6},{6,2},{3,7},{7,3},{8,12},{12,8},{9,1... | collective-permute-start | bytes 589832 | tf_op jit(solution)/shard_map/ppermute | solution.py:338
  34.1 12.9 %collective-permute-start.14 = (bf16[2,4,2,32,128]{4,3,2,1,0:T(8,128)(2,1)S(1)}, bf16[2,4,2,32,128]{4,3,2,1,0:T(8,128)(2,1)S(1)}, u32[]{:S(2)}, u32[]{:S(2)}) collective-permute-start(bf16[2,4,2,32,128]{4,3,2,1,0:T(8,128)(2,1)S(1)} %get-tuple-element.59), channel_id=1, source_target_pairs={{0,2},{1,3},{2,0},{3,1},{4,6},{5,7},{6,4},{7,5},{8,10},{9,11},{10,... | collective-permute-start | bytes 393224 | tf_op jit(solution)/shard_map/ppermute | solution.py:338
  35.3 11.7 %collective-permute-start.15 = (bf16[2,4,2,32,128]{4,3,2,1,0:T(8,128)(2,1)S(1)}, bf16[2,4,2,32,128]{4,3,2,1,0:T(8,128)(2,1)S(1)}, u32[]{:S(2)}, u32[]{:S(2)}) collective-permute-start(bf16[2,4,2,32,128]{4,3,2,1,0:T(8,128)(2,1)S(1)} %get-tuple-element.60), channel_id=1, source_target_pairs={{0,3},{1,2},{2,1},{3,0},{4,7},{5,6},{6,5},{7,4},{8,11},{9,10},{10,... | collective-permute-start | bytes 393224 | tf_op jit(solution)/shard_map/ppermute | solution.py:338
  55.4 14.7 %collective-permute-start.21 = (bf16[6,128,128]{2,1,0:T(8,128)(2,1)S(1)}, bf16[6,128,128]{2,1,0:T(8,128)(2,1)S(1)}, u32[]{:S(2)}, u32[]{:S(2)}) collective-permute-start(bf16[6,128,128]{2,1,0:T(8,128)(2,1)S(1)} %get-tuple-element.72), channel_id=1, source_target_pairs={{0,8},{8,0},{16,24},{24,16},{1,9},{9,1},{17,25},{25,17},{2,10},{10... | collective-permute-start | bytes 589832 | tf_op jit(solution)/shard_map/ppermute | solution.py:338
  57.1 13.1 %collective-permute-start.22 = (bf16[6,128,128]{2,1,0:T(8,128)(2,1)S(1)}, bf16[6,128,128]{2,1,0:T(8,128)(2,1)S(1)}, u32[]{:S(2)}, u32[]{:S(2)}) collective-permute-start(bf16[6,128,128]{2,1,0:T(8,128)(2,1)S(1)} %get-tuple-element.73), channel_id=1, source_target_pairs={{0,16},{8,24},{16,0},{24,8},{1,17},{9,25},{17,1},{25,9},{2,18},{10... | collective-permute-start | bytes 589832 | tf_op jit(solution)/shard_map/ppermute | solution.py:338
  57.9 12.2 %collective-permute-start.23 = (bf16[6,128,128]{2,1,0:T(8,128)(2,1)S(1)}, bf16[6,128,128]{2,1,0:T(8,128)(2,1)S(1)}, u32[]{:S(2)}, u32[]{:S(2)}) collective-permute-start(bf16[6,128,128]{2,1,0:T(8,128)(2,1)S(1)} %get-tuple-element.74), channel_id=1, source_target_pairs={{0,24},{8,16},{16,8},{24,0},{1,25},{9,17},{17,9},{25,1},{2,26},{10... | collective-permute-start | bytes 589832 | tf_op jit(solution)/shard_map/ppermute | solution.py:338
  64.3 5.8 %collective-permute-start.27 = (bf16[2,2,32,128]{3,2,1,0:T(8,128)(2,1)S(1)}, bf16[2,2,32,128]{3,2,1,0:T(8,128)(2,1)S(1)}, u32[]{:S(2)}, u32[]{:S(2)}) collective-permute-start(bf16[2,2,32,128]{3,2,1,0:T(8,128)(2,1)S(1)} %get-tuple-element.94), channel_id=1, source_target_pairs={{0,3},{1,2},{2,1},{3,0},{4,7},{5,6},{6,5},{7,4},{8,11},{9,10},{10,... | collective-permute-start | bytes 98312 | tf_op jit(solution)/shard_map/ppermute | solution.py:338
  71.9 6.5 %collective-permute-start.29 = (bf16[192,128]{1,0:T(8,128)(2,1)S(1)}, bf16[192,128]{1,0:T(8,128)(2,1)S(1)}, u32[]{:S(2)}, u32[]{:S(2)}) collective-permute-start(bf16[192,128]{1,0:T(8,128)(2,1)S(1)} %get-tuple-element.93), channel_id=1, source_target_pairs={{0,2},{1,3},{2,0},{3,1},{4,6},{5,7},{6,4},{7,5},{8,10},{9,11},{10,... | collective-permute-start | bytes 147464 | tf_op jit(solution)/shard_map/ppermute | solution.py:338
  73.7 5.9 %collective-permute-start.30 = (bf16[192,128]{1,0:T(8,128)(2,1)S(1)}, bf16[192,128]{1,0:T(8,128)(2,1)S(1)}, u32[]{:S(2)}, u32[]{:S(2)}) collective-permute-start(bf16[192,128]{1,0:T(8,128)(2,1)S(1)} %get-tuple-element.92), channel_id=1, source_target_pairs={{0,3},{1,2},{2,1},{3,0},{4,7},{5,6},{6,5},{7,4},{8,11},{9,10},{10,... | collective-permute-start | bytes 147464 | tf_op jit(solution)/shard_map/ppermute | solution.py:338
  81.7 5.9 %collective-permute-start.33 = (bf16[192,128]{1,0:T(8,128)(2,1)S(1)}, bf16[192,128]{1,0:T(8,128)(2,1)S(1)}, u32[]{:S(2)}, u32[]{:S(2)}) collective-permute-start(bf16[192,128]{1,0:T(8,128)(2,1)S(1)} %fusion.8), channel_id=1, source_target_pairs={{0,3},{1,2},{2,1},{3,0},{4,7},{5,6},{6,5},{7,4},{8,11},{9,10},{10,... | collective-permute-start | bytes 147464 | tf_op jit(solution)/shard_map/ppermute | solution.py:338
  (14 other events, 51.6 us)

commit v14 on v13

--- a/solution.py
+++ b/solution.py
@@ -112,22 +112,23 @@
         target[...] = wide_ref[:, :, pl.ds(pl.multiple_of(at, 16), span)].astype(BF16)
 
 
-def cotangent_kernel(halo, width, *rest):
+def cotangent_kernel(reach, width, *rest):
     sources, targets, wide_ref = rest[:4], rest[4:-1], rest[-1]
     core, _, _, unit = placed(len(targets))
     frames_in, rows, columns, chans = sources[0].shape
-    edge = jnp.zeros((2, 2 * frames_in, rows, halo, chans), F32)
-    wide_ref[:, :, :, :halo] = edge
-    wide_ref[:, :, :, halo + columns :] = edge
+    edge = jnp.zeros((2, 2 * frames_in, rows, reach, chans), F32)
+    wide_ref[:, :, :, :reach] = edge
+    wide_ref[:, :, :, reach + columns :] = edge
     for index, ref in enumerate(sources):
         whose = core if index % 2 == 0 else 1 - core
-        wide_ref[index // 2, pl.ds(whose * frames_in, frames_in), :, halo : halo + columns] = ref[
+        wide_ref[index // 2, pl.ds(whose * frames_in, frames_in), :, reach : reach + columns] = ref[
             ...
         ].astype(F32)
-    own = width - 2 * halo
+    own = width - 2 * reach
     for step, target in enumerate(targets):
         at = (jnp.bitwise_xor(unit, step) * 2 + core) * own
-        target[...] = wide_ref[:, :, :, pl.ds(pl.multiple_of(at, 16), width)].astype(BF16)
+        window = wide_ref[:, :, :, pl.ds(pl.multiple_of(at, 16), width)]
+        target[...] = window.reshape(target.shape).astype(BF16)
 
 
 def closing_kernel(group, mine_ref, other_ref, spatial_ref, temporal_ref, flat_ref):
@@ -260,11 +261,18 @@
     pixels = tile * (own_cols[1] - own_cols[0])
 
     half = group // 2
+    side = halo - rim
+    edge = jnp.zeros((frames, rows_in, side, chans), F32)
+
+    def widened(value):
+        value = value.astype(F32).reshape(frames, rows_in, width - 2 * side, chans)
+        return jnp.concatenate([edge, value, edge], 2).astype(BF16)
+
     for step, ref in enumerate(arrived):
         at = jnp.bitwise_xor(unit, step)
-        g_ref[:, pl.ds(rim + at * rows_in, rows_in)] = ref[0]
+        g_ref[:, pl.ds(rim + at * rows_in, rows_in)] = widened(ref[0])
         beyond = jnp.where(at < half, rim + tile + at * rows_in, (at - half) * rows_in)
-        g_ref[:, pl.ds(beyond, rows_in)] = ref[1]
+        g_ref[:, pl.ds(beyond, rows_in)] = widened(ref[1])
 
     def put(block, tap, value):
         slot = jnp.where(core == tap // per_core, 0, 1)
@@ -353,7 +361,6 @@
 
     bands = blocks * tiles // group
     core, section, band, unit = placed(group)
-    odd = band % 2
 
     def traded(value, shift):
         pairs = []
@@ -382,41 +389,46 @@
         scratch_shapes=[pltpu.VMEM((frames_in, rows_in, padded, chans), F32)],
         compiler_params=params,
     )(video)
-    def core_half(which, spatial, temporal):
+    *cuts, spatial, temporal = lax.optimization_barrier(
+        list(cuts) + [spatial_weights, temporal_weights]
+    )
+    def core_half(which):
         whole = jnp.concatenate([spatial[0], temporal[0]], 0)
         taps = whole.shape[0] // cores
         return lax.dynamic_slice_in_dim(whole, which * taps, taps, 0)
 
-    _, spatial, temporal = lax.optimization_barrier([cuts[0], spatial_weights, temporal_weights])
-    half_kernels = core_half(core, spatial, temporal)
+    half_kernels = core_half(core)
 
     def gathered(pieces):
         return jnp.stack([pieces[0]] + [swapped(pieces[i], "space", i) for i in range(1, group)])
 
     along_x = swapped(half_kernels, "section", 1)
     along_y = swapped(half_kernels, "section", 2)
-    own_video = gathered(cuts)
+    own_video, along_x, along_y, spatial, temporal = lax.optimization_barrier(
+        [gathered(cuts), along_x, along_y, spatial, temporal]
+    )
     near, far = traded(own_video, 0), traded(own_video, 1)
-    _, along_x, along_y, cot_halo, spatial, temporal = lax.optimization_barrier(
-        [own_video, along_x, along_y, cot_halo, spatial_weights, temporal_weights]
-    )
     mine = [along_x, along_y, swapped(along_x, "section", 2)]
-    rest_kernels = core_half(1 - core, spatial, temporal)
-    shared = [half_kernels, rest_kernels] + mine + [swapped(each) for each in mine]
-
-    cots = pl.pallas_call(
-        functools.partial(cotangent_kernel, halo, width),
+    shared = mine + [swapped(each) for each in mine]
+    rest_kernels = core_half(1 - core)
+
+    narrow = own_width + 2 * blocks
+    cuts = pl.pallas_call(
+        functools.partial(cotangent_kernel, blocks, narrow),
         name="cotangent",
         in_specs=[vmem] * 4,
         out_specs=[vmem] * group,
-        out_shape=[jax.ShapeDtypeStruct((2, cores * frames_in, rows_in, width, chans), BF16)] * group,
-        scratch_shapes=[pltpu.VMEM((2, cores * frames_in, rows_in, padded, chans), F32)],
+        out_shape=[jax.ShapeDtypeStruct((2, cores * frames_in, rows_in * narrow, chans), BF16)] * group,
+        scratch_shapes=[
+            pltpu.VMEM((2, cores * frames_in, rows_in, columns + 2 * blocks, chans), F32)
+        ],
         compiler_params=params,
     )(cotangent, swapped(cotangent), cot_halo, swapped(cot_halo))
-    cots = [cots[0]] + [swapped(cots[i], "space", i) for i in range(1, group)]
-    near, cots[1] = lax.optimization_barrier([near, cots[1]])
+    near, rest_kernels, *cuts = lax.optimization_barrier([near, rest_kernels] + list(cuts))
+    shared = [half_kernels, rest_kernels] + shared
     videos = [own_video, near, far]
     videos += [swapped(each) for each in videos]
+    cots = [cuts[0]] + [swapped(cuts[i], "space", i) for i in range(1, group)]
 
     geometry = (blocks, cores, group, frames_in, rows_in, halo, tile, width, total_rows, columns)
     frames = cores * frames_in
@@ -493,21 +505,20 @@
     parts, strips = received[:blocks], received[blocks:]
     part = sum(each.astype(F32) for each in parts).astype(BF16)
 
-    units = part.reshape(group, -1, chans)
-
-    def chunk(step):
-        return lax.dynamic_index_in_dim(units, unit ^ step, 0, keepdims=False)
-
-    part = sum(
-        each.astype(F32)
-        for each in [chunk(0)] + [swapped(chunk(i), "space", i) for i in range(1, group)]
-    )
+    halves = part.reshape(2, -1, chans)
+    low = unit % 2
+
+    def picked(which):
+        return lax.dynamic_index_in_dim(halves, which, 0, keepdims=False)
+
+    part = (picked(low).astype(F32) + swapped(picked(1 - low), "space", 1).astype(F32)).astype(BF16)
+    part = part.astype(F32) + swapped(part, "space", 2).astype(F32)
     if tiles != group:
         part = lax.psum(
             part, "space", axis_index_groups=[list(range(i, tiles, group)) for i in range(group)]
         )
     part = part.astype(BF16)
-    pair = jnp.stack([part] + [swapped(part, "space", i) for i in range(1, group)])
+    pair = jnp.stack([part, swapped(part, "space", 1)])
     spatial_out, temporal_out = pl.pallas_call(
         functools.partial(closing_kernel, group),
         name="closing",

time: 90.5 us -> 78.9 us (0.87)
  starting transfers between devices: 42.7 us -> 34.6 us
  waiting for transfers between devices: 29 us -> 25.4 us
    ppermute x32 -> x29, starting transfers between devices: 39.3 us -> 32.1 us  [swapped(): return lax.ppermute(value, axis, [(i, i ^ step) for i in range(count)])]
    ppermute x32 -> x29, waiting for transfers between devices: 27.6 us -> 22.8 us  [swapped(): return lax.ppermute(value, axis, [(i, i ^ step) for i in range(count)])]
    ppermute x2, waiting for transfers between devices: 0.01 us -> 1.89 us  [traded(): return lax.ppermute(value, ('section', 'space'), pairs)]
  transfers between devices with their start and end apart: 35 -> 32, of which waited for: 14 -> 15; matrix products, arithmetic and copies ran while one was open for 1% -> 1% of each run, Pallas kernels for 7% -> 8%
where the time goes in v14:
time: 78.9 us; the launch traced here: 78.6 us
  starting transfers between devices  34.6 us (44%)
  waiting for transfers between devices  25.4 us (32%)
  Pallas kernels  13.4 us (17%)
  other arithmetic  2.48 us (3%)
  local copies, waits for them, and re-layouts  1.9 us (2%)
  between operations  0.84 us (1%)
    ppermute x29, starting transfers between devices, swapped(): return lax.ppermute(value, axis, [(i, i ^ step) for i in range(count)])  32.1 us
    ppermute x29, waiting for transfers between devices, swapped(): return lax.ppermute(value, axis, [(i, i ^ step) for i in range(count)])  22.8 us
    pallas_call x1, Pallas kernels, on_device(): pl.pallas_call(functools.partial(forward_kernel, geometry), name='forward...  6.48 us
    pallas_call x1, Pallas kernels, on_device(): pl.pallas_call(functools.partial(backward_kernel, geometry, factor), name...  5.64 us
    concatenate x2, other arithmetic, core_half(): whole = jnp.concatenate([spatial[0], temporal[0]], 0)  2 us
    ppermute x2, waiting for transfers between devices, traded(): return lax.ppermute(value, ('section', 'space'), pairs)  1.89 us
    unnamed x6, local copies, waits for them, and re-layouts  1.81 us
  transfers between devices with their start and end apart: 32, of which 15 were waited for; matrix products, arithmetic and copies ran while one was open for 1% of the time, Pallas kernels for 8%

profile of v14, /device:TPU:0, one launch (start us, length us, event | category | flops | bytes accessed | tf_op | source)
XLA Modules:
  0.0 78.6 jit_solution(6148603336068853641)
XLA Ops:
  2.6 3.0 %collective-permute-start.3 = (bf16[6,128,128]{2,1,0:T(8,128)(2,1)S(1)}, bf16[6,128,128]{2,1,0:T(8,128)(2,1)S(1)}, u32[]{:S(2)}, u32[]{:S(2)}) collective-permute-start(bf16[6,128,128]{2,1,0:T(8,128)(2,1)S(1)} %fusion.5.rest_0_), channel_id=1, source_target_pairs={{0,8},{8,0},{16,24},{24,16},{1,9},{9,1},{17,25},{25,17},{2,10},{10... | collective-permute-start | bytes 589832 | tf_op jit(solution)/shard_map/ppermute | solution.py:346
  5.6 1.5 %collective-permute-start.4 = (bf16[6,128,128]{2,1,0:T(8,128)(2,1)S(1)}, bf16[6,128,128]{2,1,0:T(8,128)(2,1)S(1)}, u32[]{:S(2)}, u32[]{:S(2)}) collective-permute-start(bf16[6,128,128]{2,1,0:T(8,128)(2,1)S(1)} %fusion.5.rest_0_), channel_id=1, source_target_pairs={{0,16},{8,24},{16,0},{24,8},{1,17},{9,25},{17,1},{25,9},{2,18},{10... | collective-permute-start | bytes 589832 | tf_op jit(solution)/shard_map/ppermute | solution.py:346
  7.1 1.6 %collective-permute-start = (bf16[2,2,48,128]{3,2,1,0:T(8,128)(2,1)S(1)}, bf16[2,2,48,128]{3,2,1,0:T(8,128)(2,1)S(1)}, u32[]{:S(2)}, u32[]{:S(2)}) collective-permute-start(bf16[2,2,48,128]{3,2,1,0:T(8,128)(2,1)S(1)} %get-tuple-element.60), channel_id=1, source_target_pairs={{0,1},{1,0},{2,3},{3,2},{4,5},{5,4},{6,7},{7,6},{8,9},{9,8},{10,11... | collective-permute-start | bytes 147464 | tf_op jit(solution)/shard_map/ppermute | solution.py:346
  8.7 2.6 %collective-permute-start.1 = (bf16[2,2,48,128]{3,2,1,0:T(8,128)(2,1)S(1)}, bf16[2,2,48,128]{3,2,1,0:T(8,128)(2,1)S(1)}, u32[]{:S(2)}, u32[]{:S(2)}) collective-permute-start(bf16[2,2,48,128]{3,2,1,0:T(8,128)(2,1)S(1)} %get-tuple-element.61), channel_id=1, source_target_pairs={{0,2},{1,3},{2,0},{3,1},{4,6},{5,7},{6,4},{7,5},{8,10},{9,11},{10,... | collective-permute-start | bytes 147464 | tf_op jit(solution)/shard_map/ppermute | solution.py:346
  11.5 1.3 %collective-permute-start.7 = (bf16[2,2,128,128]{3,2,1,0:T(8,128)(2,1)}, bf16[2,2,128,128]{3,2,1,0:T(8,128)(2,1)S(1)}, u32[]{:S(2)}, u32[]{:S(2)}) collective-permute-start(bf16[2,2,128,128]{3,2,1,0:T(8,128)(2,1)} %rest_0_.1), channel_id=1, source_target_pairs={{8,0},{9,1},{2,10},{3,11},{16,8},{17,9},{10,18},{11,19},{24,16},{2... | collective-permute-start | bytes 393224 | tf_op jit(solution)/shard_map/ppermute | solution.py:380
  12.8 1.4 %collective-permute-done.1 = bf16[2,2,48,128]{3,2,1,0:T(8,128)(2,1)S(1)} collective-permute-done((bf16[2,2,48,128]{3,2,1,0:T(8,128)(2,1)S(1)}, bf16[2,2,48,128]{3,2,1,0:T(8,128)(2,1)S(1)}, u32[]{:S(2)}, u32[]{:S(2)}) %collective-permute-start.1) | collective-permute-done | bytes 49184 | tf_op jit(solution)/shard_map/ppermute | solution.py:346
  14.2 3.0 %collective-permute-done.2 = bf16[2,2,48,128]{3,2,1,0:T(8,128)(2,1)S(1)} collective-permute-done((bf16[2,2,48,128]{3,2,1,0:T(8,128)(2,1)S(1)}, bf16[2,2,48,128]{3,2,1,0:T(8,128)(2,1)S(1)}, u32[]{:S(2)}, u32[]{:S(2)}) %collective-permute-start.2) | collective-permute-done | bytes 49184 | tf_op jit(solution)/shard_map/ppermute | solution.py:346
  22.6 1.9 %collective-permute-done.5.rest_9_ = bf16[4,2,2,48,128]{4,3,2,1,0:T(8,128)(2,1)S(1)} collective-permute-done((bf16[4,2,2,48,128]{4,3,2,1,0:T(8,128)(2,1)S(1)}, bf16[4,2,2,48,128]{4,3,2,1,0:T(8,128)(2,1)S(1)}, u32[]{:S(2)}, u32[]{:S(2)}) %collective-permute-start.5) | collective-permute-done | bytes 196640 | tf_op jit(solution)/shard_map/ppermute | solution.py:371
  26.4 3.2 %collective-permute-start.14 = (bf16[2,4,48,128]{3,2,1,0:T(8,128)(2,1)S(1)}, bf16[2,4,48,128]{3,2,1,0:T(8,128)(2,1)S(1)}, u32[]{:S(2)}, u32[]{:S(2)}) collective-permute-start(bf16[2,4,48,128]{3,2,1,0:T(8,128)(2,1)S(1)} %get-tuple-element.75), channel_id=1, source_target_pairs={{0,2},{1,3},{2,0},{3,1},{4,6},{5,7},{6,4},{7,5},{8,10},{9,11},{10,... | collective-permute-start | bytes 294920 | tf_op jit(solution)/shard_map/ppermute | solution.py:346
  30.3 6.5 %forward.1 = (bf16[4,4,10,16,384]{4,3,2,1,0:T(8,128)(2,1)S(1)}, bf16[4,4,8,16,128]{4,3,2,1,0:T(8,128)(2,1)S(1)}, f32[4,10,32,128]{3,2,1,0:T(8,128)S(1)}, f32[4,1...) custom-call(bf16[6,128,128]{2,1,0:T(8,128)(2,1)S(1)} %fusion.5.rest_0_, ...), custom_call_target="tpu_custom_call" | custom-call | flops 6000000000 | bytes 8000000 | tf_op jit(solution)/shard_map/forward/pallas_call | solution.py:444
  37.4 5.6 %backward.1 = (bf16[4,6,128,128]{3,2,1,0:T(8,128)(2,1)S(1)}, bf16[4,6,128,128]{3,2,1,0:T(8,128)(2,1)S(1)}, bf16[4,2,2,16,128]{4,3,2,1,0:T(8,128)(2,1)S(1)}, bf16[4,2,2,16,128]{4,3,2,1,0:T(8,128)(2,1)S(1)}) custom-call(bf16[6,128,128]{2,1,0:T(8,128)(2,1)S(1)} %fusion.5.rest_0_, bf16[6,128,128]{2,1,0:T(8,128)(2,1)S(1)} %fusion.4.rest_1_, ...), custom_call_target="tpu_custom_call" | custom-call | flops 6000000000 | bytes 8000000 | tf_op jit(solution)/shard_map/backward/pallas_call | solution.py:469
  43.1 2.3 %collective-permute-done.20 = bf16[4,6,128,128]{3,2,1,0:T(8,128)(2,1)S(1)} collective-permute-done((bf16[4,6,128,128]{3,2,1,0:T(8,128)(2,1)S(1)}, bf16[4,6,128,128]{3,2,1,0:T(8,128)(2,1)S(1)}, u32[]{:S(2)}, u32[]{:S(2)}) %collective-permute-start.20) | collective-permute-done | bytes 786464 | tf_op jit(solution)/shard_map/ppermute | solution.py:346
  45.9 3.7 %collective-permute-start.21 = (bf16[6,128,128]{2,1,0:T(8,128)(2,1)S(1)}, bf16[6,128,128]{2,1,0:T(8,128)(2,1)S(1)}, u32[]{:S(2)}, u32[]{:S(2)}) collective-permute-start(bf16[6,128,128]{2,1,0:T(8,128)(2,1)S(1)} %get-tuple-element.88), channel_id=1, source_target_pairs={{0,8},{8,0},{16,24},{24,16},{1,9},{9,1},{17,25},{25,17},{2,10},{10... | collective-permute-start | bytes 589832 | tf_op jit(solution)/shard_map/ppermute | solution.py:346
  49.6 1.5 %collective-permute-start.23 = (bf16[6,128,128]{2,1,0:T(8,128)(2,1)S(1)}, bf16[6,128,128]{2,1,0:T(8,128)(2,1)S(1)}, u32[]{:S(2)}, u32[]{:S(2)}) collective-permute-start(bf16[6,128,128]{2,1,0:T(8,128)(2,1)S(1)} %get-tuple-element.90), channel_id=1, source_target_pairs={{0,24},{8,16},{16,8},{24,0},{1,25},{9,17},{17,9},{25,1},{2,26},{10... | collective-permute-start | bytes 589832 | tf_op jit(solution)/shard_map/ppermute | solution.py:346
  51.1 1.8 %collective-permute-start.25 = (bf16[2,2,32,128]{3,2,1,0:T(8,128)(2,1)S(1)}, bf16[2,2,32,128]{3,2,1,0:T(8,128)(2,1)S(1)}, u32[]{:S(2)}, u32[]{:S(2)}) collective-permute-start(bf16[2,2,32,128]{3,2,1,0:T(8,128)(2,1)S(1)} %get-tuple-element.109), channel_id=1, source_target_pairs={{0,1},{1,0},{2,3},{3,2},{4,5},{5,4},{6,7},{7,6},{8,9},{9,8},{10,11... | collective-permute-start | bytes 98312 | tf_op jit(solution)/shard_map/ppermute | solution.py:346
  55.1 2.4 %collective-permute-start.27 = (bf16[2,2,32,128]{3,2,1,0:T(8,128)(2,1)S(1)}, bf16[2,2,32,128]{3,2,1,0:T(8,128)(2,1)S(1)}, u32[]{:S(2)}, u32[]{:S(2)}) collective-permute-start(bf16[2,2,32,128]{3,2,1,0:T(8,128)(2,1)S(1)} %get-tuple-element.107), channel_id=1, source_target_pairs={{0,3},{1,2},{2,1},{3,0},{4,7},{5,6},{6,5},{7,4},{8,11},{9,10},{10,... | collective-permute-start | bytes 98312 | tf_op jit(solution)/shard_map/ppermute | solution.py:346
  57.9 2.9 %collective-permute-done.27 = bf16[2,2,32,128]{3,2,1,0:T(8,128)(2,1)S(1)} collective-permute-done((bf16[2,2,32,128]{3,2,1,0:T(8,128)(2,1)S(1)}, bf16[2,2,32,128]{3,2,1,0:T(8,128)(2,1)S(1)}, u32[]{:S(2)}, u32[]{:S(2)}) %collective-permute-start.27) | collective-permute-done | bytes 32800 | tf_op jit(solution)/shard_map/ppermute | solution.py:346
  60.9 1.7 %collective-permute-start.28 = (bf16[384,128]{1,0:T(8,128)(2,1)S(1)}, bf16[384,128]{1,0:T(8,128)(2,1)S(1)}, u32[]{:S(2)}, u32[]{:S(2)}) collective-permute-start(bf16[384,128]{1,0:T(8,128)(2,1)S(1)} %dynamic-slice_bitcast_fusion), channel_id=1, source_target_pairs={{0,1},{1,0},{2,3},{3,2},{4,5},{5,4},{6,7},{7,6},{8,9},{9,8},{10,11... | collective-permute-start | bytes 294920 | tf_op jit(solution)/shard_map/ppermute | solution.py:346
  62.6 3.0 %collective-permute-done.28 = bf16[384,128]{1,0:T(8,128)(2,1)S(1)} collective-permute-done((bf16[384,128]{1,0:T(8,128)(2,1)S(1)}, bf16[384,128]{1,0:T(8,128)(2,1)S(1)}, u32[]{:S(2)}, u32[]{:S(2)}) %collective-permute-start.28) | collective-permute-done | bytes 98336 | tf_op jit(solution)/shard_map/ppermute | solution.py:346
  65.7 2.3 %collective-permute-start.29 = (bf16[384,128]{1,0:T(8,128)(2,1)S(1)}, bf16[384,128]{1,0:T(8,128)(2,1)S(1)}, u32[]{:S(2)}, u32[]{:S(2)}) collective-permute-start(bf16[384,128]{1,0:T(8,128)(2,1)S(1)} %fusion.6), channel_id=1, source_target_pairs={{0,2},{1,3},{2,0},{3,1},{4,6},{5,7},{6,4},{7,5},{8,10},{9,11},{10,... | collective-permute-start | bytes 294920 | tf_op jit(solution)/shard_map/ppermute | solution.py:346
  68.0 3.3 %collective-permute-done.29 = bf16[384,128]{1,0:T(8,128)(2,1)S(1)} collective-permute-done((bf16[384,128]{1,0:T(8,128)(2,1)S(1)}, bf16[384,128]{1,0:T(8,128)(2,1)S(1)}, u32[]{:S(2)}, u32[]{:S(2)}) %collective-permute-start.29) | collective-permute-done | bytes 98336 | tf_op jit(solution)/shard_map/ppermute | solution.py:346
  71.3 1.6 %collective-permute-start.30 = (bf16[384,128]{1,0:T(8,128)(2,1)S(1)}, bf16[384,128]{1,0:T(8,128)(2,1)S(1)}, u32[]{:S(2)}, u32[]{:S(2)}) collective-permute-start(bf16[384,128]{1,0:T(8,128)(2,1)S(1)} %add_convert_fusion.5), channel_id=1, source_target_pairs={{0,1},{1,0},{2,3},{3,2},{4,5},{5,4},{6,7},{7,6},{8,9},{9,8},{10,11... | collective-permute-start | bytes 294920 | tf_op jit(solution)/shard_map/ppermute | solution.py:346
  73.0 3.0 %collective-permute-done.30 = bf16[384,128]{1,0:T(8,128)(2,1)S(1)} collective-permute-done((bf16[384,128]{1,0:T(8,128)(2,1)S(1)}, bf16[384,128]{1,0:T(8,128)(2,1)S(1)}, u32[]{:S(2)}, u32[]{:S(2)}) %collective-permute-start.30) | collective-permute-done | bytes 98336 | tf_op jit(solution)/shard_map/ppermute | solution.py:346
  76.2 1.4 %collective-permute-done.31.other_ref = bf16[2,384,128]{2,1,0:T(8,128)(2,1)S(1)} collective-permute-done((bf16[2,384,128]{2,1,0:T(8,128)(2,1)S(1)}, bf16[2,384,128]{2,1,0:T(8,128)(2,1)S(1)}, u32[]{:S(2)}, u32[]{:S(2)}) %collective-permute-start.31) | collective-permute-done | bytes 196640 | tf_op jit(solution)/shard_map/ppermute | solution.py:346
  (67 shorter events, 15.4 us)
Async XLA Ops:
  2.6 14.6 %collective-permute-start.3 = (bf16[6,128,128]{2,1,0:T(8,128)(2,1)S(1)}, bf16[6,128,128]{2,1,0:T(8,128)(2,1)S(1)}, u32[]{:S(2)}, u32[]{:S(2)}) collective-permute-start(bf16[6,128,128]{2,1,0:T(8,128)(2,1)S(1)} %fusion.5.rest_0_), channel_id=1, source_target_pairs={{0,8},{8,0},{16,24},{24,16},{1,9},{9,1},{17,25},{25,17},{2,10},{10... | collective-permute-start | bytes 589832 | tf_op jit(solution)/shard_map/ppermute | solution.py:346
  5.6 11.6 %collective-permute-start.4 = (bf16[6,128,128]{2,1,0:T(8,128)(2,1)S(1)}, bf16[6,128,128]{2,1,0:T(8,128)(2,1)S(1)}, u32[]{:S(2)}, u32[]{:S(2)}) collective-permute-start(bf16[6,128,128]{2,1,0:T(8,128)(2,1)S(1)} %fusion.5.rest_0_), channel_id=1, source_target_pairs={{0,16},{8,24},{16,0},{24,8},{1,17},{9,25},{17,1},{25,9},{2,18},{10... | collective-permute-start | bytes 589832 | tf_op jit(solution)/shard_map/ppermute | solution.py:346
  8.7 5.5 %collective-permute-start.1 = (bf16[2,2,48,128]{3,2,1,0:T(8,128)(2,1)S(1)}, bf16[2,2,48,128]{3,2,1,0:T(8,128)(2,1)S(1)}, u32[]{:S(2)}, u32[]{:S(2)}) collective-permute-start(bf16[2,2,48,128]{3,2,1,0:T(8,128)(2,1)S(1)} %get-tuple-element.61), channel_id=1, source_target_pairs={{0,2},{1,3},{2,0},{3,1},{4,6},{5,7},{6,4},{7,5},{8,10},{9,11},{10,... | collective-permute-start | bytes 147464 | tf_op jit(solution)/shard_map/ppermute | solution.py:346
  11.3 5.9 %collective-permute-start.2 = (bf16[2,2,48,128]{3,2,1,0:T(8,128)(2,1)S(1)}, bf16[2,2,48,128]{3,2,1,0:T(8,128)(2,1)S(1)}, u32[]{:S(2)}, u32[]{:S(2)}) collective-permute-start(bf16[2,2,48,128]{3,2,1,0:T(8,128)(2,1)S(1)} %get-tuple-element.62), channel_id=1, source_target_pairs={{0,3},{1,2},{2,1},{3,0},{4,7},{5,6},{6,5},{7,4},{8,11},{9,10},{10,... | collective-permute-start | bytes 147464 | tf_op jit(solution)/shard_map/ppermute | solution.py:346
  11.5 8.2 %collective-permute-start.7 = (bf16[2,2,128,128]{3,2,1,0:T(8,128)(2,1)}, bf16[2,2,128,128]{3,2,1,0:T(8,128)(2,1)S(1)}, u32[]{:S(2)}, u32[]{:S(2)}) collective-permute-start(bf16[2,2,128,128]{3,2,1,0:T(8,128)(2,1)} %rest_0_.1), channel_id=1, source_target_pairs={{8,0},{9,1},{2,10},{3,11},{16,8},{17,9},{10,18},{11,19},{24,16},{2... | collective-permute-start | bytes 393224 | tf_op jit(solution)/shard_map/ppermute | solution.py:380
  14.2 5.5 %collective-permute-start.6 = (bf16[2,2,128,128]{3,2,1,0:T(8,128)(2,1)}, bf16[2,2,128,128]{3,2,1,0:T(8,128)(2,1)S(1)}, u32[]{:S(2)}, u32[]{:S(2)}) collective-permute-start(bf16[2,2,128,128]{3,2,1,0:T(8,128)(2,1)} %rest_0_.1), channel_id=1, source_target_pairs={{0,4},{4,0},{1,5},{5,1},{2,6},{6,2},{3,7},{7,3},{8,12},{12,8},{9,1... | collective-permute-start | bytes 393224 | tf_op jit(solution)/shard_map/ppermute | solution.py:346
  17.2 7.2 %collective-permute-start.5 = (bf16[4,2,2,48,128]{4,3,2,1,0:T(8,128)(2,1)S(1)}, bf16[4,2,2,48,128]{4,3,2,1,0:T(8,128)(2,1)S(1)}, u32[]{:S(2)}, u32[]{:S(2)}) collective-permute-start(bf16[4,2,2,48,128]{4,3,2,1,0:T(8,128)(2,1)S(1)} %pad_maximum_fusion.rest_8_), channel_id=1, source_target_pairs={{0,8},{1,9},{2,10},{3,11},{8,0},{9,1},{10,2},{11,3},{16,24},{17,25... | collective-permute-start | bytes 589832 | tf_op jit(solution)/shard_map/ppermute | solution.py:371
  17.8 6.6 %collective-permute-start.9 = (bf16[6,128,128]{2,1,0:T(8,128)(2,1)S(1)}, bf16[6,128,128]{2,1,0:T(8,128)(2,1)S(1)}, u32[]{:S(2)}, u32[]{:S(2)}) collective-permute-start(bf16[6,128,128]{2,1,0:T(8,128)(2,1)S(1)} %collective-permute-done.3.rest_2_), channel_id=1, source_target_pairs={{0,16},{8,24},{16,0},{24,8},{1,17},{9,25},{17,1},{25,9},{2,18},{10... | collective-permute-start | bytes 589832 | tf_op jit(solution)/shard_map/ppermute | solution.py:346
  18.3 6.6 %collective-permute-start.16 = (bf16[4,2,2,48,128]{4,3,2,1,0:T(8,128)(2,1)S(1)}, bf16[4,2,2,48,128]{4,3,2,1,0:T(8,128)(2,1)S(1)}, u32[]{:S(2)}, u32[]{:S(2)}) collective-permute-start(bf16[4,2,2,48,128]{4,3,2,1,0:T(8,128)(2,1)S(1)} %pad_maximum_fusion.rest_8_), channel_id=1, source_target_pairs={{8,16},{9,17},{10,18},{11,19},{16,8},{17,9},{18,10},{19,11},{12,20... | collective-permute-start | bytes 589832 | tf_op jit(solution)/shard_map/ppermute | solution.py:371
  19.7 5.4 %collective-permute-start.10 = (bf16[6,128,128]{2,1,0:T(8,128)(2,1)S(1)}, bf16[6,128,128]{2,1,0:T(8,128)(2,1)S(1)}, u32[]{:S(2)}, u32[]{:S(2)}) collective-permute-start(bf16[6,128,128]{2,1,0:T(8,128)(2,1)S(1)} %collective-permute-done.3.rest_2_), channel_id=1, source_target_pairs={{0,4},{4,0},{1,5},{5,1},{2,6},{6,2},{3,7},{7,3},{8,12},{12,8},{9,1... | collective-permute-start | bytes 589832 | tf_op jit(solution)/shard_map/ppermute | solution.py:346
  21.3 5.1 %collective-permute-start.17 = (bf16[4,2,2,48,128]{4,3,2,1,0:T(8,128)(2,1)S(1)}, bf16[4,2,2,48,128]{4,3,2,1,0:T(8,128)(2,1)S(1)}, u32[]{:S(2)}, u32[]{:S(2)}) collective-permute-start(bf16[4,2,2,48,128]{4,3,2,1,0:T(8,128)(2,1)S(1)} %pad_maximum_fusion.rest_8_), channel_id=1, source_target_pairs={{0,4},{4,0},{1,5},{5,1},{2,6},{6,2},{3,7},{7,3},{8,12},{12,8},{9,1... | collective-permute-start | bytes 589832 | tf_op jit(solution)/shard_map/ppermute | solution.py:346
  24.4 5.1 %collective-permute-start.18 = (bf16[4,2,2,48,128]{4,3,2,1,0:T(8,128)(2,1)S(1)}, bf16[4,2,2,48,128]{4,3,2,1,0:T(8,128)(2,1)S(1)}, u32[]{:S(2)}, u32[]{:S(2)}) collective-permute-start(bf16[4,2,2,48,128]{4,3,2,1,0:T(8,128)(2,1)S(1)} %collective-permute-done.5.rest_9_), channel_id=1, source_target_pairs={{0,4},{4,0},{1,5},{5,1},{2,6},{6,2},{3,7},{7,3},{8,12},{12,8},{9,1... | collective-permute-start | bytes 589832 | tf_op jit(solution)/shard_map/ppermute | solution.py:346
  25.0 5.3 %collective-permute-start.12 = (bf16[6,128,128]{2,1,0:T(8,128)(2,1)S(1)}, bf16[6,128,128]{2,1,0:T(8,128)(2,1)S(1)}, u32[]{:S(2)}, u32[]{:S(2)}) collective-permute-start(bf16[6,128,128]{2,1,0:T(8,128)(2,1)S(1)} %collective-permute-done.9.rest_4_), channel_id=1, source_target_pairs={{0,4},{4,0},{1,5},{5,1},{2,6},{6,2},{3,7},{7,3},{8,12},{12,8},{9,1... | collective-permute-start | bytes 589832 | tf_op jit(solution)/shard_map/ppermute | solution.py:346
  25.0 5.3 %collective-permute-start.19 = (bf16[4,2,2,48,128]{4,3,2,1,0:T(8,128)(2,1)S(1)}, bf16[4,2,2,48,128]{4,3,2,1,0:T(8,128)(2,1)S(1)}, u32[]{:S(2)}, u32[]{:S(2)}) collective-permute-start(bf16[4,2,2,48,128]{4,3,2,1,0:T(8,128)(2,1)S(1)} %collective-permute-done.16.rest_10_), channel_id=1, source_target_pairs={{0,4},{4,0},{1,5},{5,1},{2,6},{6,2},{3,7},{7,3},{8,12},{12,8},{9,1... | collective-permute-start | bytes 589832 | tf_op jit(solution)/shard_map/ppermute | solution.py:346
  25.9 10.9 %collective-permute-start.13 = (bf16[2,4,48,128]{3,2,1,0:T(8,128)(2,1)S(1)}, bf16[2,4,48,128]{3,2,1,0:T(8,128)(2,1)S(1)}, u32[]{:S(2)}, u32[]{:S(2)}) collective-permute-start(bf16[2,4,48,128]{3,2,1,0:T(8,128)(2,1)S(1)} %get-tuple-element.74), channel_id=1, source_target_pairs={{0,1},{1,0},{2,3},{3,2},{4,5},{5,4},{6,7},{7,6},{8,9},{9,8},{10,11... | collective-permute-start | bytes 294920 | tf_op jit(solution)/shard_map/ppermute | solution.py:346
  26.4 11.0 %collective-permute-start.14 = (bf16[2,4,48,128]{3,2,1,0:T(8,128)(2,1)S(1)}, bf16[2,4,48,128]{3,2,1,0:T(8,128)(2,1)S(1)}, u32[]{:S(2)}, u32[]{:S(2)}) collective-permute-start(bf16[2,4,48,128]{3,2,1,0:T(8,128)(2,1)S(1)} %get-tuple-element.75), channel_id=1, source_target_pairs={{0,2},{1,3},{2,0},{3,1},{4,6},{5,7},{6,4},{7,5},{8,10},{9,11},{10,... | collective-permute-start | bytes 294920 | tf_op jit(solution)/shard_map/ppermute | solution.py:346
  29.5 7.9 %collective-permute-start.15 = (bf16[2,4,48,128]{3,2,1,0:T(8,128)(2,1)S(1)}, bf16[2,4,48,128]{3,2,1,0:T(8,128)(2,1)S(1)}, u32[]{:S(2)}, u32[]{:S(2)}) collective-permute-start(bf16[2,4,48,128]{3,2,1,0:T(8,128)(2,1)S(1)} %get-tuple-element.76), channel_id=1, source_target_pairs={{0,3},{1,2},{2,1},{3,0},{4,7},{5,6},{6,5},{7,4},{8,11},{9,10},{10,... | collective-permute-start | bytes 294920 | tf_op jit(solution)/shard_map/ppermute | solution.py:346
  45.7 5.4 %collective-permute-start.24 = (bf16[4,2,2,16,128]{4,3,2,1,0:T(8,128)(2,1)S(1)}, bf16[4,2,2,16,128]{4,3,2,1,0:T(8,128)(2,1)S(1)}, u32[]{:S(2)}, u32[]{:S(2)}) collective-permute-start(bf16[4,2,2,16,128]{4,3,2,1,0:T(8,128)(2,1)S(1)} %get-tuple-element.92), channel_id=1, source_target_pairs={{0,4},{4,0},{1,5},{5,1},{2,6},{6,2},{3,7},{7,3},{8,12},{12,8},{9,1... | collective-permute-start | bytes 196616 | tf_op jit(solution)/shard_map/ppermute | solution.py:346
  45.9 14.9 %collective-permute-start.21 = (bf16[6,128,128]{2,1,0:T(8,128)(2,1)S(1)}, bf16[6,128,128]{2,1,0:T(8,128)(2,1)S(1)}, u32[]{:S(2)}, u32[]{:S(2)}) collective-permute-start(bf16[6,128,128]{2,1,0:T(8,128)(2,1)S(1)} %get-tuple-element.88), channel_id=1, source_target_pairs={{0,8},{8,0},{16,24},{24,16},{1,9},{9,1},{17,25},{25,17},{2,10},{10... | collective-permute-start | bytes 589832 | tf_op jit(solution)/shard_map/ppermute | solution.py:346
  49.6 11.2 %collective-permute-start.22 = (bf16[6,128,128]{2,1,0:T(8,128)(2,1)S(1)}, bf16[6,128,128]{2,1,0:T(8,128)(2,1)S(1)}, u32[]{:S(2)}, u32[]{:S(2)}) collective-permute-start(bf16[6,128,128]{2,1,0:T(8,128)(2,1)S(1)} %get-tuple-element.89), channel_id=1, source_target_pairs={{0,16},{8,24},{16,0},{24,8},{1,17},{9,25},{17,1},{25,9},{2,18},{10... | collective-permute-start | bytes 589832 | tf_op jit(solution)/shard_map/ppermute | solution.py:346
  49.6 11.2 %collective-permute-start.23 = (bf16[6,128,128]{2,1,0:T(8,128)(2,1)S(1)}, bf16[6,128,128]{2,1,0:T(8,128)(2,1)S(1)}, u32[]{:S(2)}, u32[]{:S(2)}) collective-permute-start(bf16[6,128,128]{2,1,0:T(8,128)(2,1)S(1)} %get-tuple-element.90), channel_id=1, source_target_pairs={{0,24},{8,16},{16,8},{24,0},{1,25},{9,17},{17,9},{25,1},{2,26},{10... | collective-permute-start | bytes 589832 | tf_op jit(solution)/shard_map/ppermute | solution.py:346
  52.9 5.0 %collective-permute-start.26 = (bf16[2,2,32,128]{3,2,1,0:T(8,128)(2,1)S(1)}, bf16[2,2,32,128]{3,2,1,0:T(8,128)(2,1)S(1)}, u32[]{:S(2)}, u32[]{:S(2)}) collective-permute-start(bf16[2,2,32,128]{3,2,1,0:T(8,128)(2,1)S(1)} %get-tuple-element.110), channel_id=1, source_target_pairs={{0,2},{1,3},{2,0},{3,1},{4,6},{5,7},{6,4},{7,5},{8,10},{9,11},{10,... | collective-permute-start | bytes 98312 | tf_op jit(solution)/shard_map/ppermute | solution.py:346
  55.1 5.7 %collective-permute-start.27 = (bf16[2,2,32,128]{3,2,1,0:T(8,128)(2,1)S(1)}, bf16[2,2,32,128]{3,2,1,0:T(8,128)(2,1)S(1)}, u32[]{:S(2)}, u32[]{:S(2)}) collective-permute-start(bf16[2,2,32,128]{3,2,1,0:T(8,128)(2,1)S(1)} %get-tuple-element.107), channel_id=1, source_target_pairs={{0,3},{1,2},{2,1},{3,0},{4,7},{5,6},{6,5},{7,4},{8,11},{9,10},{10,... | collective-permute-start | bytes 98312 | tf_op jit(solution)/shard_map/ppermute | solution.py:346
  65.7 5.6 %collective-permute-start.29 = (bf16[384,128]{1,0:T(8,128)(2,1)S(1)}, bf16[384,128]{1,0:T(8,128)(2,1)S(1)}, u32[]{:S(2)}, u32[]{:S(2)}) collective-permute-start(bf16[384,128]{1,0:T(8,128)(2,1)S(1)} %fusion.6), channel_id=1, source_target_pairs={{0,2},{1,3},{2,0},{3,1},{4,6},{5,7},{6,4},{7,5},{8,10},{9,11},{10,... | collective-permute-start | bytes 294920 | tf_op jit(solution)/shard_map/ppermute | solution.py:346
  (11 other events, 28.9 us)

commit v15 on v14

--- a/solution.py
+++ b/solution.py
@@ -212,17 +212,19 @@
             taps = row_pairs(x_ref, frame, first - 1, count // 2)
             before = jnp.dot(taps, pair_ref[...], preferred_element_type=F32)
             before = woven(before, width)
-            sigma = 1.0 / (1.0 + jnp.exp(-before))
-            hidden = before * sigma * mask
-            slope = (sigma * (1.0 + before * (1.0 - sigma))) * mask
+            sigma = 0.5 + 0.5 * jnp.tanh(0.5 * before)
+            masked = sigma * mask
+            hidden = before * masked
             h_ref[frame, first:last] = hidden.astype(BF16).reshape(count, width, chans)
-            ho_ref[block, frame] = hidden.reshape(count, width, chans)[
+            hidden = hidden.reshape(count, width, chans)
+            ho_ref[block, frame] = hidden[
                 own_rows[0] - first : own_rows[1] - first, own_cols[0] : own_cols[1]
             ].astype(BF16)
             rim = block + 1
-            d_refs[block][frame] = slope.reshape(count, width, chans)[
-                own_rows[0] - rim - first : own_rows[1] + rim - first
-            ]
+            kept = slice(own_rows[0] - rim - first, own_rows[1] + rim - first)
+            sigma = sigma.reshape(count, width, chans)[kept]
+            masked = masked.reshape(count, width, chans)[kept]
+            d_refs[block][frame] = masked + hidden[kept] * (1.0 - sigma)
         if block + 1 == blocks:
             break
         for frame in range(0, frames, 2):
@@ -323,16 +325,21 @@
                 cut = new.astype(F32).reshape(inner, width, chans)[:, own_cols[0] : own_cols[1]]
                 out_ref[frame] = cut.astype(BF16)
         slopes = dao_ref[...].reshape(frames * pixels, chans)
-        for ky in range(3):
-            taps = xo_ref[block, :, ky : ky + tile].reshape(frames * pixels, 3 * chans)
-            sums = dot_first(slopes, taps)
-            for kx in range(3):
-                put(block, 3 * ky + kx, sums[:, kx * chans : (kx + 1) * chans])
+        taps = [
+            xo_ref[block, :, ky : ky + tile].reshape(frames * pixels, 3 * chans) for ky in range(3)
+        ]
+        sums = dot_first(slopes, jnp.concatenate(taps, 1))
+        for tap in range(9):
+            put(block, tap, sums[:, tap * chans : (tap + 1) * chans])
+        before = jnp.zeros((2 * pixels, chans), BF16)
+        earlier = ho_ref[block].reshape(frames * pixels, chans)
+        earlier = jnp.concatenate([before, earlier], 0)
+        timeline = [earlier[kt * pixels : (kt + frames) * pixels] for kt in range(3)]
+        sums = dot_first(
+            go_ref[...].reshape(frames * pixels, chans), jnp.concatenate(timeline, 1)
+        )
         for kt in range(3):
-            skip = 2 - kt
-            later = go_ref[skip:].reshape((frames - skip) * pixels, chans)
-            earlier = ho_ref[block, : frames - skip].reshape((frames - skip) * pixels, chans)
-            put(block, 9 + kt, dot_first(later, earlier))
+            put(block, 9 + kt, sums[:, kt * chans : (kt + 1) * chans])
     keep_ref[...] = grad_ref[0]
     give_ref[...] = grad_ref[1]
     for whose, target in ((core, mine_out), (1 - core, other_out)):

time: 78.9 us -> 78.6 us (level)
  no operation moved by 1% of the time
where the time goes in v15:
time: 78.6 us; the launch traced here: 78.4 us
  starting transfers between devices  34.6 us (44%)
  waiting for transfers between devices  25.8 us (33%)
  Pallas kernels  12.8 us (16%)
  other arithmetic  2.48 us (3%)
  local copies, waits for them, and re-layouts  1.9 us (2%)
  between operations  0.84 us (1%)
    ppermute x29, starting transfers between devices, swapped(): return lax.ppermute(value, axis, [(i, i ^ step) for i in range(count)])  32 us
    ppermute x29, waiting for transfers between devices, swapped(): return lax.ppermute(value, axis, [(i, i ^ step) for i in range(count)])  23.2 us
    pallas_call x1, Pallas kernels, on_device(): pl.pallas_call(functools.partial(forward_kernel, geometry), name='forward...  6.17 us
    pallas_call x1, Pallas kernels, on_device(): pl.pallas_call(functools.partial(backward_kernel, geometry, factor), name...  5.4 us
    concatenate x2, other arithmetic, core_half(): whole = jnp.concatenate([spatial[0], temporal[0]], 0)  2 us
    ppermute x2, waiting for transfers between devices, traded(): return lax.ppermute(value, ('section', 'space'), pairs)  1.89 us
    unnamed x6, local copies, waits for them, and re-layouts  1.81 us
  transfers between devices with their start and end apart: 32, of which 15 were waited for; matrix products, arithmetic and copies ran while one was open for 1% of the time, Pallas kernels for 8%

profile of v15, /device:TPU:0, one launch (start us, length us, event | category | flops | bytes accessed | tf_op | source)
XLA Modules:
  0.0 78.4 jit_solution(3637408837533465679)
XLA Ops:
  2.6 3.0 %collective-permute-start.3 = (bf16[6,128,128]{2,1,0:T(8,128)(2,1)S(1)}, bf16[6,128,128]{2,1,0:T(8,128)(2,1)S(1)}, u32[]{:S(2)}, u32[]{:S(2)}) collective-permute-start(bf16[6,128,128]{2,1,0:T(8,128)(2,1)S(1)} %fusion.5.rest_0_), channel_id=1, source_target_pairs={{0,8},{8,0},{16,24},{24,16},{1,9},{9,1},{17,25},{25,17},{2,10},{10... | collective-permute-start | bytes 589832 | tf_op jit(solution)/shard_map/ppermute | solution.py:353
  5.6 1.5 %collective-permute-start.4 = (bf16[6,128,128]{2,1,0:T(8,128)(2,1)S(1)}, bf16[6,128,128]{2,1,0:T(8,128)(2,1)S(1)}, u32[]{:S(2)}, u32[]{:S(2)}) collective-permute-start(bf16[6,128,128]{2,1,0:T(8,128)(2,1)S(1)} %fusion.5.rest_0_), channel_id=1, source_target_pairs={{0,16},{8,24},{16,0},{24,8},{1,17},{9,25},{17,1},{25,9},{2,18},{10... | collective-permute-start | bytes 589832 | tf_op jit(solution)/shard_map/ppermute | solution.py:353
  7.1 1.6 %collective-permute-start = (bf16[2,2,48,128]{3,2,1,0:T(8,128)(2,1)S(1)}, bf16[2,2,48,128]{3,2,1,0:T(8,128)(2,1)S(1)}, u32[]{:S(2)}, u32[]{:S(2)}) collective-permute-start(bf16[2,2,48,128]{3,2,1,0:T(8,128)(2,1)S(1)} %get-tuple-element.60), channel_id=1, source_target_pairs={{0,1},{1,0},{2,3},{3,2},{4,5},{5,4},{6,7},{7,6},{8,9},{9,8},{10,11... | collective-permute-start | bytes 147464 | tf_op jit(solution)/shard_map/ppermute | solution.py:353
  8.7 2.6 %collective-permute-start.1 = (bf16[2,2,48,128]{3,2,1,0:T(8,128)(2,1)S(1)}, bf16[2,2,48,128]{3,2,1,0:T(8,128)(2,1)S(1)}, u32[]{:S(2)}, u32[]{:S(2)}) collective-permute-start(bf16[2,2,48,128]{3,2,1,0:T(8,128)(2,1)S(1)} %get-tuple-element.61), channel_id=1, source_target_pairs={{0,2},{1,3},{2,0},{3,1},{4,6},{5,7},{6,4},{7,5},{8,10},{9,11},{10,... | collective-permute-start | bytes 147464 | tf_op jit(solution)/shard_map/ppermute | solution.py:353
  11.5 1.3 %collective-permute-start.7 = (bf16[2,2,128,128]{3,2,1,0:T(8,128)(2,1)}, bf16[2,2,128,128]{3,2,1,0:T(8,128)(2,1)S(1)}, u32[]{:S(2)}, u32[]{:S(2)}) collective-permute-start(bf16[2,2,128,128]{3,2,1,0:T(8,128)(2,1)} %rest_0_.1), channel_id=1, source_target_pairs={{8,0},{9,1},{2,10},{3,11},{16,8},{17,9},{10,18},{11,19},{24,16},{2... | collective-permute-start | bytes 393224 | tf_op jit(solution)/shard_map/ppermute | solution.py:387
  12.8 1.4 %collective-permute-done.1 = bf16[2,2,48,128]{3,2,1,0:T(8,128)(2,1)S(1)} collective-permute-done((bf16[2,2,48,128]{3,2,1,0:T(8,128)(2,1)S(1)}, bf16[2,2,48,128]{3,2,1,0:T(8,128)(2,1)S(1)}, u32[]{:S(2)}, u32[]{:S(2)}) %collective-permute-start.1) | collective-permute-done | bytes 49184 | tf_op jit(solution)/shard_map/ppermute | solution.py:353
  14.2 3.0 %collective-permute-done.2 = bf16[2,2,48,128]{3,2,1,0:T(8,128)(2,1)S(1)} collective-permute-done((bf16[2,2,48,128]{3,2,1,0:T(8,128)(2,1)S(1)}, bf16[2,2,48,128]{3,2,1,0:T(8,128)(2,1)S(1)}, u32[]{:S(2)}, u32[]{:S(2)}) %collective-permute-start.2) | collective-permute-done | bytes 49184 | tf_op jit(solution)/shard_map/ppermute | solution.py:353
  22.6 1.9 %collective-permute-done.5.rest_9_ = bf16[4,2,2,48,128]{4,3,2,1,0:T(8,128)(2,1)S(1)} collective-permute-done((bf16[4,2,2,48,128]{4,3,2,1,0:T(8,128)(2,1)S(1)}, bf16[4,2,2,48,128]{4,3,2,1,0:T(8,128)(2,1)S(1)}, u32[]{:S(2)}, u32[]{:S(2)}) %collective-permute-start.5) | collective-permute-done | bytes 196640 | tf_op jit(solution)/shard_map/ppermute | solution.py:378
  26.4 3.2 %collective-permute-start.14 = (bf16[2,4,48,128]{3,2,1,0:T(8,128)(2,1)S(1)}, bf16[2,4,48,128]{3,2,1,0:T(8,128)(2,1)S(1)}, u32[]{:S(2)}, u32[]{:S(2)}) collective-permute-start(bf16[2,4,48,128]{3,2,1,0:T(8,128)(2,1)S(1)} %get-tuple-element.75), channel_id=1, source_target_pairs={{0,2},{1,3},{2,0},{3,1},{4,6},{5,7},{6,4},{7,5},{8,10},{9,11},{10,... | collective-permute-start | bytes 294920 | tf_op jit(solution)/shard_map/ppermute | solution.py:353
  30.3 6.2 %forward.1 = (bf16[4,4,10,16,384]{4,3,2,1,0:T(8,128)(2,1)S(1)}, bf16[4,4,8,16,128]{4,3,2,1,0:T(8,128)(2,1)S(1)}, f32[4,10,32,128]{3,2,1,0:T(8,128)S(1)}, f32[4,1...) custom-call(bf16[6,128,128]{2,1,0:T(8,128)(2,1)S(1)} %fusion.5.rest_0_, ...), custom_call_target="tpu_custom_call" | custom-call | flops 6000000000 | bytes 8000000 | tf_op jit(solution)/shard_map/forward/pallas_call | solution.py:451
  37.4 5.4 %backward.1 = (bf16[4,6,128,128]{3,2,1,0:T(8,128)(2,1)S(1)}, bf16[4,6,128,128]{3,2,1,0:T(8,128)(2,1)S(1)}, bf16[4,2,2,16,128]{4,3,2,1,0:T(8,128)(2,1)S(1)}, bf16[4,2,2,16,128]{4,3,2,1,0:T(8,128)(2,1)S(1)}) custom-call(bf16[6,128,128]{2,1,0:T(8,128)(2,1)S(1)} %fusion.5.rest_0_, bf16[6,128,128]{2,1,0:T(8,128)(2,1)S(1)} %fusion.4.rest_1_, ...), custom_call_target="tpu_custom_call" | custom-call | flops 6000000000 | bytes 8000000 | tf_op jit(solution)/shard_map/backward/pallas_call | solution.py:476
  42.9 2.3 %collective-permute-done.20 = bf16[4,6,128,128]{3,2,1,0:T(8,128)(2,1)S(1)} collective-permute-done((bf16[4,6,128,128]{3,2,1,0:T(8,128)(2,1)S(1)}, bf16[4,6,128,128]{3,2,1,0:T(8,128)(2,1)S(1)}, u32[]{:S(2)}, u32[]{:S(2)}) %collective-permute-start.20) | collective-permute-done | bytes 786464 | tf_op jit(solution)/shard_map/ppermute | solution.py:353
  45.6 3.7 %collective-permute-start.21 = (bf16[6,128,128]{2,1,0:T(8,128)(2,1)S(1)}, bf16[6,128,128]{2,1,0:T(8,128)(2,1)S(1)}, u32[]{:S(2)}, u32[]{:S(2)}) collective-permute-start(bf16[6,128,128]{2,1,0:T(8,128)(2,1)S(1)} %get-tuple-element.88), channel_id=1, source_target_pairs={{0,8},{8,0},{16,24},{24,16},{1,9},{9,1},{17,25},{25,17},{2,10},{10... | collective-permute-start | bytes 589832 | tf_op jit(solution)/shard_map/ppermute | solution.py:353
  49.3 1.5 %collective-permute-start.23 = (bf16[6,128,128]{2,1,0:T(8,128)(2,1)S(1)}, bf16[6,128,128]{2,1,0:T(8,128)(2,1)S(1)}, u32[]{:S(2)}, u32[]{:S(2)}) collective-permute-start(bf16[6,128,128]{2,1,0:T(8,128)(2,1)S(1)} %get-tuple-element.90), channel_id=1, source_target_pairs={{0,24},{8,16},{16,8},{24,0},{1,25},{9,17},{17,9},{25,1},{2,26},{10... | collective-permute-start | bytes 589832 | tf_op jit(solution)/shard_map/ppermute | solution.py:353
  50.9 1.8 %collective-permute-start.25 = (bf16[2,2,32,128]{3,2,1,0:T(8,128)(2,1)S(1)}, bf16[2,2,32,128]{3,2,1,0:T(8,128)(2,1)S(1)}, u32[]{:S(2)}, u32[]{:S(2)}) collective-permute-start(bf16[2,2,32,128]{3,2,1,0:T(8,128)(2,1)S(1)} %get-tuple-element.109), channel_id=1, source_target_pairs={{0,1},{1,0},{2,3},{3,2},{4,5},{5,4},{6,7},{7,6},{8,9},{9,8},{10,11... | collective-permute-start | bytes 98312 | tf_op jit(solution)/shard_map/ppermute | solution.py:353
  54.8 2.4 %collective-permute-start.27 = (bf16[2,2,32,128]{3,2,1,0:T(8,128)(2,1)S(1)}, bf16[2,2,32,128]{3,2,1,0:T(8,128)(2,1)S(1)}, u32[]{:S(2)}, u32[]{:S(2)}) collective-permute-start(bf16[2,2,32,128]{3,2,1,0:T(8,128)(2,1)S(1)} %get-tuple-element.107), channel_id=1, source_target_pairs={{0,3},{1,2},{2,1},{3,0},{4,7},{5,6},{6,5},{7,4},{8,11},{9,10},{10,... | collective-permute-start | bytes 98312 | tf_op jit(solution)/shard_map/ppermute | solution.py:353
  57.7 2.9 %collective-permute-done.27 = bf16[2,2,32,128]{3,2,1,0:T(8,128)(2,1)S(1)} collective-permute-done((bf16[2,2,32,128]{3,2,1,0:T(8,128)(2,1)S(1)}, bf16[2,2,32,128]{3,2,1,0:T(8,128)(2,1)S(1)}, u32[]{:S(2)}, u32[]{:S(2)}) %collective-permute-start.27) | collective-permute-done | bytes 32800 | tf_op jit(solution)/shard_map/ppermute | solution.py:353
  60.7 1.7 %collective-permute-start.28 = (bf16[384,128]{1,0:T(8,128)(2,1)S(1)}, bf16[384,128]{1,0:T(8,128)(2,1)S(1)}, u32[]{:S(2)}, u32[]{:S(2)}) collective-permute-start(bf16[384,128]{1,0:T(8,128)(2,1)S(1)} %dynamic-slice_bitcast_fusion), channel_id=1, source_target_pairs={{0,1},{1,0},{2,3},{3,2},{4,5},{5,4},{6,7},{7,6},{8,9},{9,8},{10,11... | collective-permute-start | bytes 294920 | tf_op jit(solution)/shard_map/ppermute | solution.py:353
  62.4 3.0 %collective-permute-done.28 = bf16[384,128]{1,0:T(8,128)(2,1)S(1)} collective-permute-done((bf16[384,128]{1,0:T(8,128)(2,1)S(1)}, bf16[384,128]{1,0:T(8,128)(2,1)S(1)}, u32[]{:S(2)}, u32[]{:S(2)}) %collective-permute-start.28) | collective-permute-done | bytes 98336 | tf_op jit(solution)/shard_map/ppermute | solution.py:353
  65.4 2.3 %collective-permute-start.29 = (bf16[384,128]{1,0:T(8,128)(2,1)S(1)}, bf16[384,128]{1,0:T(8,128)(2,1)S(1)}, u32[]{:S(2)}, u32[]{:S(2)}) collective-permute-start(bf16[384,128]{1,0:T(8,128)(2,1)S(1)} %fusion.6), channel_id=1, source_target_pairs={{0,2},{1,3},{2,0},{3,1},{4,6},{5,7},{6,4},{7,5},{8,10},{9,11},{10,... | collective-permute-start | bytes 294920 | tf_op jit(solution)/shard_map/ppermute | solution.py:353
  67.7 3.3 %collective-permute-done.29 = bf16[384,128]{1,0:T(8,128)(2,1)S(1)} collective-permute-done((bf16[384,128]{1,0:T(8,128)(2,1)S(1)}, bf16[384,128]{1,0:T(8,128)(2,1)S(1)}, u32[]{:S(2)}, u32[]{:S(2)}) %collective-permute-start.29) | collective-permute-done | bytes 98336 | tf_op jit(solution)/shard_map/ppermute | solution.py:353
  71.1 1.6 %collective-permute-start.30 = (bf16[384,128]{1,0:T(8,128)(2,1)S(1)}, bf16[384,128]{1,0:T(8,128)(2,1)S(1)}, u32[]{:S(2)}, u32[]{:S(2)}) collective-permute-start(bf16[384,128]{1,0:T(8,128)(2,1)S(1)} %add_convert_fusion.5), channel_id=1, source_target_pairs={{0,1},{1,0},{2,3},{3,2},{4,5},{5,4},{6,7},{7,6},{8,9},{9,8},{10,11... | collective-permute-start | bytes 294920 | tf_op jit(solution)/shard_map/ppermute | solution.py:353
  72.7 3.0 %collective-permute-done.30 = bf16[384,128]{1,0:T(8,128)(2,1)S(1)} collective-permute-done((bf16[384,128]{1,0:T(8,128)(2,1)S(1)}, bf16[384,128]{1,0:T(8,128)(2,1)S(1)}, u32[]{:S(2)}, u32[]{:S(2)}) %collective-permute-start.30) | collective-permute-done | bytes 98336 | tf_op jit(solution)/shard_map/ppermute | solution.py:353
  75.9 1.4 %collective-permute-done.31.other_ref = bf16[2,384,128]{2,1,0:T(8,128)(2,1)S(1)} collective-permute-done((bf16[2,384,128]{2,1,0:T(8,128)(2,1)S(1)}, bf16[2,384,128]{2,1,0:T(8,128)(2,1)S(1)}, u32[]{:S(2)}, u32[]{:S(2)}) %collective-permute-start.31) | collective-permute-done | bytes 196640 | tf_op jit(solution)/shard_map/ppermute | solution.py:353
  (67 shorter events, 15.8 us)
Async XLA Ops:
  2.6 14.6 %collective-permute-start.3 = (bf16[6,128,128]{2,1,0:T(8,128)(2,1)S(1)}, bf16[6,128,128]{2,1,0:T(8,128)(2,1)S(1)}, u32[]{:S(2)}, u32[]{:S(2)}) collective-permute-start(bf16[6,128,128]{2,1,0:T(8,128)(2,1)S(1)} %fusion.5.rest_0_), channel_id=1, source_target_pairs={{0,8},{8,0},{16,24},{24,16},{1,9},{9,1},{17,25},{25,17},{2,10},{10... | collective-permute-start | bytes 589832 | tf_op jit(solution)/shard_map/ppermute | solution.py:353
  5.6 11.6 %collective-permute-start.4 = (bf16[6,128,128]{2,1,0:T(8,128)(2,1)S(1)}, bf16[6,128,128]{2,1,0:T(8,128)(2,1)S(1)}, u32[]{:S(2)}, u32[]{:S(2)}) collective-permute-start(bf16[6,128,128]{2,1,0:T(8,128)(2,1)S(1)} %fusion.5.rest_0_), channel_id=1, source_target_pairs={{0,16},{8,24},{16,0},{24,8},{1,17},{9,25},{17,1},{25,9},{2,18},{10... | collective-permute-start | bytes 589832 | tf_op jit(solution)/shard_map/ppermute | solution.py:353
  8.7 5.5 %collective-permute-start.1 = (bf16[2,2,48,128]{3,2,1,0:T(8,128)(2,1)S(1)}, bf16[2,2,48,128]{3,2,1,0:T(8,128)(2,1)S(1)}, u32[]{:S(2)}, u32[]{:S(2)}) collective-permute-start(bf16[2,2,48,128]{3,2,1,0:T(8,128)(2,1)S(1)} %get-tuple-element.61), channel_id=1, source_target_pairs={{0,2},{1,3},{2,0},{3,1},{4,6},{5,7},{6,4},{7,5},{8,10},{9,11},{10,... | collective-permute-start | bytes 147464 | tf_op jit(solution)/shard_map/ppermute | solution.py:353
  11.3 5.9 %collective-permute-start.2 = (bf16[2,2,48,128]{3,2,1,0:T(8,128)(2,1)S(1)}, bf16[2,2,48,128]{3,2,1,0:T(8,128)(2,1)S(1)}, u32[]{:S(2)}, u32[]{:S(2)}) collective-permute-start(bf16[2,2,48,128]{3,2,1,0:T(8,128)(2,1)S(1)} %get-tuple-element.62), channel_id=1, source_target_pairs={{0,3},{1,2},{2,1},{3,0},{4,7},{5,6},{6,5},{7,4},{8,11},{9,10},{10,... | collective-permute-start | bytes 147464 | tf_op jit(solution)/shard_map/ppermute | solution.py:353
  11.5 8.2 %collective-permute-start.7 = (bf16[2,2,128,128]{3,2,1,0:T(8,128)(2,1)}, bf16[2,2,128,128]{3,2,1,0:T(8,128)(2,1)S(1)}, u32[]{:S(2)}, u32[]{:S(2)}) collective-permute-start(bf16[2,2,128,128]{3,2,1,0:T(8,128)(2,1)} %rest_0_.1), channel_id=1, source_target_pairs={{8,0},{9,1},{2,10},{3,11},{16,8},{17,9},{10,18},{11,19},{24,16},{2... | collective-permute-start | bytes 393224 | tf_op jit(solution)/shard_map/ppermute | solution.py:387
  14.2 5.5 %collective-permute-start.6 = (bf16[2,2,128,128]{3,2,1,0:T(8,128)(2,1)}, bf16[2,2,128,128]{3,2,1,0:T(8,128)(2,1)S(1)}, u32[]{:S(2)}, u32[]{:S(2)}) collective-permute-start(bf16[2,2,128,128]{3,2,1,0:T(8,128)(2,1)} %rest_0_.1), channel_id=1, source_target_pairs={{0,4},{4,0},{1,5},{5,1},{2,6},{6,2},{3,7},{7,3},{8,12},{12,8},{9,1... | collective-permute-start | bytes 393224 | tf_op jit(solution)/shard_map/ppermute | solution.py:353
  17.2 7.2 %collective-permute-start.5 = (bf16[4,2,2,48,128]{4,3,2,1,0:T(8,128)(2,1)S(1)}, bf16[4,2,2,48,128]{4,3,2,1,0:T(8,128)(2,1)S(1)}, u32[]{:S(2)}, u32[]{:S(2)}) collective-permute-start(bf16[4,2,2,48,128]{4,3,2,1,0:T(8,128)(2,1)S(1)} %pad_maximum_fusion.rest_8_), channel_id=1, source_target_pairs={{0,8},{1,9},{2,10},{3,11},{8,0},{9,1},{10,2},{11,3},{16,24},{17,25... | collective-permute-start | bytes 589832 | tf_op jit(solution)/shard_map/ppermute | solution.py:378
  17.8 6.6 %collective-permute-start.9 = (bf16[6,128,128]{2,1,0:T(8,128)(2,1)S(1)}, bf16[6,128,128]{2,1,0:T(8,128)(2,1)S(1)}, u32[]{:S(2)}, u32[]{:S(2)}) collective-permute-start(bf16[6,128,128]{2,1,0:T(8,128)(2,1)S(1)} %collective-permute-done.3.rest_2_), channel_id=1, source_target_pairs={{0,16},{8,24},{16,0},{24,8},{1,17},{9,25},{17,1},{25,9},{2,18},{10... | collective-permute-start | bytes 589832 | tf_op jit(solution)/shard_map/ppermute | solution.py:353
  18.3 6.6 %collective-permute-start.16 = (bf16[4,2,2,48,128]{4,3,2,1,0:T(8,128)(2,1)S(1)}, bf16[4,2,2,48,128]{4,3,2,1,0:T(8,128)(2,1)S(1)}, u32[]{:S(2)}, u32[]{:S(2)}) collective-permute-start(bf16[4,2,2,48,128]{4,3,2,1,0:T(8,128)(2,1)S(1)} %pad_maximum_fusion.rest_8_), channel_id=1, source_target_pairs={{8,16},{9,17},{10,18},{11,19},{16,8},{17,9},{18,10},{19,11},{12,20... | collective-permute-start | bytes 589832 | tf_op jit(solution)/shard_map/ppermute | solution.py:378
  19.7 5.4 %collective-permute-start.10 = (bf16[6,128,128]{2,1,0:T(8,128)(2,1)S(1)}, bf16[6,128,128]{2,1,0:T(8,128)(2,1)S(1)}, u32[]{:S(2)}, u32[]{:S(2)}) collective-permute-start(bf16[6,128,128]{2,1,0:T(8,128)(2,1)S(1)} %collective-permute-done.3.rest_2_), channel_id=1, source_target_pairs={{0,4},{4,0},{1,5},{5,1},{2,6},{6,2},{3,7},{7,3},{8,12},{12,8},{9,1... | collective-permute-start | bytes 589832 | tf_op jit(solution)/shard_map/ppermute | solution.py:353
  21.3 5.1 %collective-permute-start.17 = (bf16[4,2,2,48,128]{4,3,2,1,0:T(8,128)(2,1)S(1)}, bf16[4,2,2,48,128]{4,3,2,1,0:T(8,128)(2,1)S(1)}, u32[]{:S(2)}, u32[]{:S(2)}) collective-permute-start(bf16[4,2,2,48,128]{4,3,2,1,0:T(8,128)(2,1)S(1)} %pad_maximum_fusion.rest_8_), channel_id=1, source_target_pairs={{0,4},{4,0},{1,5},{5,1},{2,6},{6,2},{3,7},{7,3},{8,12},{12,8},{9,1... | collective-permute-start | bytes 589832 | tf_op jit(solution)/shard_map/ppermute | solution.py:353
  24.4 5.1 %collective-permute-start.18 = (bf16[4,2,2,48,128]{4,3,2,1,0:T(8,128)(2,1)S(1)}, bf16[4,2,2,48,128]{4,3,2,1,0:T(8,128)(2,1)S(1)}, u32[]{:S(2)}, u32[]{:S(2)}) collective-permute-start(bf16[4,2,2,48,128]{4,3,2,1,0:T(8,128)(2,1)S(1)} %collective-permute-done.5.rest_9_), channel_id=1, source_target_pairs={{0,4},{4,0},{1,5},{5,1},{2,6},{6,2},{3,7},{7,3},{8,12},{12,8},{9,1... | collective-permute-start | bytes 589832 | tf_op jit(solution)/shard_map/ppermute | solution.py:353
  25.0 5.3 %collective-permute-start.12 = (bf16[6,128,128]{2,1,0:T(8,128)(2,1)S(1)}, bf16[6,128,128]{2,1,0:T(8,128)(2,1)S(1)}, u32[]{:S(2)}, u32[]{:S(2)}) collective-permute-start(bf16[6,128,128]{2,1,0:T(8,128)(2,1)S(1)} %collective-permute-done.9.rest_4_), channel_id=1, source_target_pairs={{0,4},{4,0},{1,5},{5,1},{2,6},{6,2},{3,7},{7,3},{8,12},{12,8},{9,1... | collective-permute-start | bytes 589832 | tf_op jit(solution)/shard_map/ppermute | solution.py:353
  25.0 5.3 %collective-permute-start.19 = (bf16[4,2,2,48,128]{4,3,2,1,0:T(8,128)(2,1)S(1)}, bf16[4,2,2,48,128]{4,3,2,1,0:T(8,128)(2,1)S(1)}, u32[]{:S(2)}, u32[]{:S(2)}) collective-permute-start(bf16[4,2,2,48,128]{4,3,2,1,0:T(8,128)(2,1)S(1)} %collective-permute-done.16.rest_10_), channel_id=1, source_target_pairs={{0,4},{4,0},{1,5},{5,1},{2,6},{6,2},{3,7},{7,3},{8,12},{12,8},{9,1... | collective-permute-start | bytes 589832 | tf_op jit(solution)/shard_map/ppermute | solution.py:353
  25.9 10.6 %collective-permute-start.13 = (bf16[2,4,48,128]{3,2,1,0:T(8,128)(2,1)S(1)}, bf16[2,4,48,128]{3,2,1,0:T(8,128)(2,1)S(1)}, u32[]{:S(2)}, u32[]{:S(2)}) collective-permute-start(bf16[2,4,48,128]{3,2,1,0:T(8,128)(2,1)S(1)} %get-tuple-element.74), channel_id=1, source_target_pairs={{0,1},{1,0},{2,3},{3,2},{4,5},{5,4},{6,7},{7,6},{8,9},{9,8},{10,11... | collective-permute-start | bytes 294920 | tf_op jit(solution)/shard_map/ppermute | solution.py:353
  26.4 11.0 %collective-permute-start.14 = (bf16[2,4,48,128]{3,2,1,0:T(8,128)(2,1)S(1)}, bf16[2,4,48,128]{3,2,1,0:T(8,128)(2,1)S(1)}, u32[]{:S(2)}, u32[]{:S(2)}) collective-permute-start(bf16[2,4,48,128]{3,2,1,0:T(8,128)(2,1)S(1)} %get-tuple-element.75), channel_id=1, source_target_pairs={{0,2},{1,3},{2,0},{3,1},{4,6},{5,7},{6,4},{7,5},{8,10},{9,11},{10,... | collective-permute-start | bytes 294920 | tf_op jit(solution)/shard_map/ppermute | solution.py:353
  29.5 7.9 %collective-permute-start.15 = (bf16[2,4,48,128]{3,2,1,0:T(8,128)(2,1)S(1)}, bf16[2,4,48,128]{3,2,1,0:T(8,128)(2,1)S(1)}, u32[]{:S(2)}, u32[]{:S(2)}) collective-permute-start(bf16[2,4,48,128]{3,2,1,0:T(8,128)(2,1)S(1)} %get-tuple-element.76), channel_id=1, source_target_pairs={{0,3},{1,2},{2,1},{3,0},{4,7},{5,6},{6,5},{7,4},{8,11},{9,10},{10,... | collective-permute-start | bytes 294920 | tf_op jit(solution)/shard_map/ppermute | solution.py:353
  45.4 5.4 %collective-permute-start.24 = (bf16[4,2,2,16,128]{4,3,2,1,0:T(8,128)(2,1)S(1)}, bf16[4,2,2,16,128]{4,3,2,1,0:T(8,128)(2,1)S(1)}, u32[]{:S(2)}, u32[]{:S(2)}) collective-permute-start(bf16[4,2,2,16,128]{4,3,2,1,0:T(8,128)(2,1)S(1)} %get-tuple-element.92), channel_id=1, source_target_pairs={{0,4},{4,0},{1,5},{5,1},{2,6},{6,2},{3,7},{7,3},{8,12},{12,8},{9,1... | collective-permute-start | bytes 196616 | tf_op jit(solution)/shard_map/ppermute | solution.py:353
  45.6 14.9 %collective-permute-start.21 = (bf16[6,128,128]{2,1,0:T(8,128)(2,1)S(1)}, bf16[6,128,128]{2,1,0:T(8,128)(2,1)S(1)}, u32[]{:S(2)}, u32[]{:S(2)}) collective-permute-start(bf16[6,128,128]{2,1,0:T(8,128)(2,1)S(1)} %get-tuple-element.88), channel_id=1, source_target_pairs={{0,8},{8,0},{16,24},{24,16},{1,9},{9,1},{17,25},{25,17},{2,10},{10... | collective-permute-start | bytes 589832 | tf_op jit(solution)/shard_map/ppermute | solution.py:353
  49.3 11.2 %collective-permute-start.22 = (bf16[6,128,128]{2,1,0:T(8,128)(2,1)S(1)}, bf16[6,128,128]{2,1,0:T(8,128)(2,1)S(1)}, u32[]{:S(2)}, u32[]{:S(2)}) collective-permute-start(bf16[6,128,128]{2,1,0:T(8,128)(2,1)S(1)} %get-tuple-element.89), channel_id=1, source_target_pairs={{0,16},{8,24},{16,0},{24,8},{1,17},{9,25},{17,1},{25,9},{2,18},{10... | collective-permute-start | bytes 589832 | tf_op jit(solution)/shard_map/ppermute | solution.py:353
  49.3 11.2 %collective-permute-start.23 = (bf16[6,128,128]{2,1,0:T(8,128)(2,1)S(1)}, bf16[6,128,128]{2,1,0:T(8,128)(2,1)S(1)}, u32[]{:S(2)}, u32[]{:S(2)}) collective-permute-start(bf16[6,128,128]{2,1,0:T(8,128)(2,1)S(1)} %get-tuple-element.90), channel_id=1, source_target_pairs={{0,24},{8,16},{16,8},{24,0},{1,25},{9,17},{17,9},{25,1},{2,26},{10... | collective-permute-start | bytes 589832 | tf_op jit(solution)/shard_map/ppermute | solution.py:353
  52.6 5.0 %collective-permute-start.26 = (bf16[2,2,32,128]{3,2,1,0:T(8,128)(2,1)S(1)}, bf16[2,2,32,128]{3,2,1,0:T(8,128)(2,1)S(1)}, u32[]{:S(2)}, u32[]{:S(2)}) collective-permute-start(bf16[2,2,32,128]{3,2,1,0:T(8,128)(2,1)S(1)} %get-tuple-element.110), channel_id=1, source_target_pairs={{0,2},{1,3},{2,0},{3,1},{4,6},{5,7},{6,4},{7,5},{8,10},{9,11},{10,... | collective-permute-start | bytes 98312 | tf_op jit(solution)/shard_map/ppermute | solution.py:353
  54.8 5.7 %collective-permute-start.27 = (bf16[2,2,32,128]{3,2,1,0:T(8,128)(2,1)S(1)}, bf16[2,2,32,128]{3,2,1,0:T(8,128)(2,1)S(1)}, u32[]{:S(2)}, u32[]{:S(2)}) collective-permute-start(bf16[2,2,32,128]{3,2,1,0:T(8,128)(2,1)S(1)} %get-tuple-element.107), channel_id=1, source_target_pairs={{0,3},{1,2},{2,1},{3,0},{4,7},{5,6},{6,5},{7,4},{8,11},{9,10},{10,... | collective-permute-start | bytes 98312 | tf_op jit(solution)/shard_map/ppermute | solution.py:353
  65.4 5.6 %collective-permute-start.29 = (bf16[384,128]{1,0:T(8,128)(2,1)S(1)}, bf16[384,128]{1,0:T(8,128)(2,1)S(1)}, u32[]{:S(2)}, u32[]{:S(2)}) collective-permute-start(bf16[384,128]{1,0:T(8,128)(2,1)S(1)} %fusion.6), channel_id=1, source_target_pairs={{0,2},{1,3},{2,0},{3,1},{4,6},{5,7},{6,4},{7,5},{8,10},{9,11},{10,... | collective-permute-start | bytes 294920 | tf_op jit(solution)/shard_map/ppermute | solution.py:353
  (11 other events, 28.9 us)

commit v16 on v15

--- a/solution.py
+++ b/solution.py
@@ -91,6 +91,10 @@
     chans = value.shape[1] // 2
     split = [value[:, i * chans : (i + 1) * chans].reshape(-1, 1, width, chans) for i in range(2)]
     return jnp.concatenate(split, 1).reshape(-1, chans)
+
+
+def ordered(count):
+    return [0] + list(range(count - 1, 0, -1))
 
 
 def placed(group):
@@ -195,10 +199,10 @@
     for index, ref in enumerate(arrived):
         base = (halo, near, tile + halo - near)[index % 3]
         whose = core if index < 3 else 1 - core
-        for step in range(group):
+        for piece, step in enumerate(ordered(group)):
             row = base + jnp.bitwise_xor(unit, step) * rows_in
             start_ref[pl.ds(whose * frames_in, frames_in), pl.ds(row, rows_in)] = ref[
-                step, :, :, columns_at, :
+                piece, :, :, columns_at, :
             ]
     for frame in range(frames):
         keep(0, frame, start_ref[frame].reshape(high * width, chans).astype(F32), 0)
@@ -270,7 +274,7 @@
         value = value.astype(F32).reshape(frames, rows_in, width - 2 * side, chans)
         return jnp.concatenate([edge, value, edge], 2).astype(BF16)
 
-    for step, ref in enumerate(arrived):
+    for step, ref in zip(ordered(group), arrived):
         at = jnp.bitwise_xor(unit, step)
         g_ref[:, pl.ds(rim + at * rows_in, rows_in)] = widened(ref[0])
         beyond = jnp.where(at < half, rim + tile + at * rows_in, (at - half) * rows_in)
@@ -353,6 +357,10 @@
     return lax.ppermute(value, axis, [(i, i ^ step) for i in range(count)])
 
 
+def exchanged(pieces, axis):
+    return [swapped(pieces[i], axis, i) if i else pieces[0] for i in ordered(len(pieces))]
+
+
 def on_device(video, cotangent, spatial_weights, temporal_weights):
     blocks, cores, tiles = (lax.axis_size(name) for name in ("section", "tm", "space"))
     frames_in, rows_in, columns, chans = video.shape
@@ -407,7 +415,7 @@
     half_kernels = core_half(core)
 
     def gathered(pieces):
-        return jnp.stack([pieces[0]] + [swapped(pieces[i], "space", i) for i in range(1, group)])
+        return jnp.stack(exchanged(pieces, "space"))
 
     along_x = swapped(half_kernels, "section", 1)
     along_y = swapped(half_kernels, "section", 2)
@@ -435,7 +443,7 @@
     shared = [half_kernels, rest_kernels] + shared
     videos = [own_video, near, far]
     videos += [swapped(each) for each in videos]
-    cots = [cuts[0]] + [swapped(cuts[i], "space", i) for i in range(1, group)]
+    cots = exchanged(cuts, "space")
 
     geometry = (blocks, cores, group, frames_in, rows_in, halo, tile, width, total_rows, columns)
     frames = cores * frames_in
@@ -501,13 +509,13 @@
     got = swapped(give)
     parts = [(keep[i].astype(F32) + got[i].astype(F32)).astype(BF16) for i in range(blocks)]
     other_grad, *parts = lax.optimization_barrier([other_grad] + parts)
-    parts = parts[:1] + [swapped(parts[i], "section", i) for i in range(1, blocks)]
+    parts = exchanged(parts, "section")
     other_grad = swapped(other_grad)
     first = core == 0
     wide = jnp.concatenate(
         [jnp.where(first, mine_grad, other_grad), jnp.where(first, other_grad, mine_grad)], 3
     )
-    strips = [wide[0]] + [swapped(wide[i], "space", i) for i in range(1, group)]
+    strips = exchanged([wide[i] for i in range(group)], "space")
     received = lax.optimization_barrier(parts + strips)
     parts, strips = received[:blocks], received[blocks:]
     part = sum(each.astype(F32) for each in parts).astype(BF16)
@@ -540,7 +548,7 @@
     )(pair, swapped(pair))
 
     grad_video = jnp.zeros(video.shape, BF16)
-    for step, strip in enumerate(strips):
+    for step, strip in zip(ordered(group), strips):
         grad_video = lax.dynamic_update_slice(
             grad_video, strip, (0, 0, (unit ^ step) * cores * own_width, 0)
         )

time: 78.6 us -> 80.3 us (1.022)
  waiting for transfers between devices: 25.8 us -> 30.9 us
  starting transfers between devices: 34.6 us -> 31.1 us
    ppermute x29, starting transfers between devices: 32 us -> 27.4 us  [swapped(): return lax.ppermute(value, axis, [(i, i ^ step) for i in range(count)])]
    ppermute x29, waiting for transfers between devices: 23.2 us -> 26.9 us  [swapped(): return lax.ppermute(value, axis, [(i, i ^ step) for i in range(count)])]
    ppermute x1, waiting for transfers between devices: 0.66 us -> 3.13 us  [on_device(): cot_halo = lax.ppermute(cotangent, ('section', 'space'), passed)]
    ppermute x2, starting transfers between devices: 1.26 us -> 2.43 us  [traded(): return lax.ppermute(value, ('section', 'space'), pairs)]
    ppermute x2, waiting for transfers between devices: 1.89 us -> 0.89 us  [traded(): return lax.ppermute(value, ('section', 'space'), pairs)]
where the time goes in v16:
time: 80.3 us; the launch traced here: 80 us
  starting transfers between devices  31.1 us (39%)
  waiting for transfers between devices  30.9 us (38%)
  Pallas kernels  12.8 us (16%)
  other arithmetic  2.48 us (3%)
  local copies, waits for them, and re-layouts  1.9 us (2%)
  between operations  0.84 us (1%)
    ppermute x29, starting transfers between devices, swapped(): return lax.ppermute(value, axis, [(i, i ^ step) for i in range(count)])  27.4 us
    ppermute x29, waiting for transfers between devices, swapped(): return lax.ppermute(value, axis, [(i, i ^ step) for i in range(count)])  26.9 us
    pallas_call x1, Pallas kernels, on_device(): pl.pallas_call(functools.partial(forward_kernel, geometry), name='forward...  6.17 us
    pallas_call x1, Pallas kernels, on_device(): pl.pallas_call(functools.partial(backward_kernel, geometry, factor), name...  5.4 us
    ppermute x1, waiting for transfers between devices, on_device(): cot_halo = lax.ppermute(cotangent, ('section', 'space'), passed)  3.13 us
    ppermute x2, starting transfers between devices, traded(): return lax.ppermute(value, ('section', 'space'), pairs)  2.43 us
    concatenate x2, other arithmetic, core_half(): whole = jnp.concatenate([spatial[0], temporal[0]], 0)  2 us
    unnamed x6, local copies, waits for them, and re-layouts  1.81 us
  transfers between devices with their start and end apart: 32, of which 15 were waited for; matrix products, arithmetic and copies ran while one was open for 1% of the time, Pallas kernels for 8%

profile of v16, /device:TPU:0, one launch (start us, length us, event | category | flops | bytes accessed | tf_op | source)
XLA Modules:
  0.0 80.0 jit_solution(15537963378685811293)
XLA Ops:
  2.6 3.0 %collective-permute-start.3 = (bf16[6,128,128]{2,1,0:T(8,128)(2,1)S(1)}, bf16[6,128,128]{2,1,0:T(8,128)(2,1)S(1)}, u32[]{:S(2)}, u32[]{:S(2)}) collective-permute-start(bf16[6,128,128]{2,1,0:T(8,128)(2,1)S(1)} %fusion.5.rest_0_), channel_id=1, source_target_pairs={{0,8},{8,0},{16,24},{24,16},{1,9},{9,1},{17,25},{25,17},{2,10},{10... | collective-permute-start | bytes 589832 | tf_op jit(solution)/shard_map/ppermute | solution.py:357
  5.6 1.5 %collective-permute-start.4 = (bf16[6,128,128]{2,1,0:T(8,128)(2,1)S(1)}, bf16[6,128,128]{2,1,0:T(8,128)(2,1)S(1)}, u32[]{:S(2)}, u32[]{:S(2)}) collective-permute-start(bf16[6,128,128]{2,1,0:T(8,128)(2,1)S(1)} %fusion.5.rest_0_), channel_id=1, source_target_pairs={{0,16},{8,24},{16,0},{24,8},{1,17},{9,25},{17,1},{25,9},{2,18},{10... | collective-permute-start | bytes 589832 | tf_op jit(solution)/shard_map/ppermute | solution.py:357
  7.1 3.6 %collective-permute-start = (bf16[2,2,48,128]{3,2,1,0:T(8,128)(2,1)S(1)}, bf16[2,2,48,128]{3,2,1,0:T(8,128)(2,1)S(1)}, u32[]{:S(2)}, u32[]{:S(2)}) collective-permute-start(bf16[2,2,48,128]{3,2,1,0:T(8,128)(2,1)S(1)} %get-tuple-element.60), channel_id=1, source_target_pairs={{0,3},{1,2},{2,1},{3,0},{4,7},{5,6},{6,5},{7,4},{8,11},{9,10},{10,... | collective-permute-start | bytes 147464 | tf_op jit(solution)/shard_map/ppermute | solution.py:357
  11.5 1.9 %collective-permute-done = bf16[2,2,48,128]{3,2,1,0:T(8,128)(2,1)S(1)} collective-permute-done((bf16[2,2,48,128]{3,2,1,0:T(8,128)(2,1)S(1)}, bf16[2,2,48,128]{3,2,1,0:T(8,128)(2,1)S(1)}, u32[]{:S(2)}, u32[]{:S(2)}) %collective-permute-start) | collective-permute-done | bytes 49184 | tf_op jit(solution)/shard_map/ppermute | solution.py:357
  13.4 1.3 %collective-permute-start.7 = (bf16[2,2,128,128]{3,2,1,0:T(8,128)(2,1)}, bf16[2,2,128,128]{3,2,1,0:T(8,128)(2,1)S(1)}, u32[]{:S(2)}, u32[]{:S(2)}) collective-permute-start(bf16[2,2,128,128]{3,2,1,0:T(8,128)(2,1)} %rest_0_.1), channel_id=1, source_target_pairs={{8,0},{9,1},{2,10},{3,11},{16,8},{17,9},{10,18},{11,19},{24,16},{2... | collective-permute-start | bytes 393224 | tf_op jit(solution)/shard_map/ppermute | solution.py:395
  15.8 1.8 %collective-permute-start.5 = (bf16[4,2,2,48,128]{4,3,2,1,0:T(8,128)(2,1)S(1)}, bf16[4,2,2,48,128]{4,3,2,1,0:T(8,128)(2,1)S(1)}, u32[]{:S(2)}, u32[]{:S(2)}) collective-permute-start(bf16[4,2,2,48,128]{4,3,2,1,0:T(8,128)(2,1)S(1)} %pad_maximum_fusion.rest_8_), channel_id=1, source_target_pairs={{0,8},{1,9},{2,10},{3,11},{8,0},{9,1},{10,2},{11,3},{16,24},{17,25... | collective-permute-start | bytes 589832 | tf_op jit(solution)/shard_map/ppermute | solution.py:386
  18.7 3.1 %collective-permute-done.7.rest_2_ = bf16[2,2,128,128]{3,2,1,0:T(8,128)(2,1)S(1)} collective-permute-done((bf16[2,2,128,128]{3,2,1,0:T(8,128)(2,1)}, bf16[2,2,128,128]{3,2,1,0:T(8,128)(2,1)S(1)}, u32[]{:S(2)}, u32[]{:S(2)}) %collective-permute-start.7) | collective-permute-done | bytes 131104 | tf_op jit(solution)/shard_map/ppermute | solution.py:395
  27.1 3.5 %collective-permute-start.13 = (bf16[2,4,48,128]{3,2,1,0:T(8,128)(2,1)S(1)}, bf16[2,4,48,128]{3,2,1,0:T(8,128)(2,1)S(1)}, u32[]{:S(2)}, u32[]{:S(2)}) collective-permute-start(bf16[2,4,48,128]{3,2,1,0:T(8,128)(2,1)S(1)} %get-tuple-element.74), channel_id=1, source_target_pairs={{0,3},{1,2},{2,1},{3,0},{4,7},{5,6},{6,5},{7,4},{8,11},{9,10},{10,... | collective-permute-start | bytes 294920 | tf_op jit(solution)/shard_map/ppermute | solution.py:357
  31.5 6.2 %forward.1 = (bf16[4,4,10,16,384]{4,3,2,1,0:T(8,128)(2,1)S(1)}, bf16[4,4,8,16,128]{4,3,2,1,0:T(8,128)(2,1)S(1)}, f32[4,10,32,128]{3,2,1,0:T(8,128)S(1)}, f32[4,1...) custom-call(bf16[6,128,128]{2,1,0:T(8,128)(2,1)S(1)} %fusion.5.rest_0_, ...), custom_call_target="tpu_custom_call" | custom-call | flops 6000000000 | bytes 8000000 | tf_op jit(solution)/shard_map/forward/pallas_call | solution.py:459
  38.1 5.4 %backward.1 = (bf16[4,6,128,128]{3,2,1,0:T(8,128)(2,1)S(1)}, bf16[4,6,128,128]{3,2,1,0:T(8,128)(2,1)S(1)}, bf16[4,2,2,16,128]{4,3,2,1,0:T(8,128)(2,1)S(1)}, bf16[4,2,2,16,128]{4,3,2,1,0:T(8,128)(2,1)S(1)}) custom-call(bf16[6,128,128]{2,1,0:T(8,128)(2,1)S(1)} %fusion.5.rest_0_, bf16[6,128,128]{2,1,0:T(8,128)(2,1)S(1)} %fusion.4.rest_1_, ...), custom_call_target="tpu_custom_call" | custom-call | flops 6000000000 | bytes 8000000 | tf_op jit(solution)/shard_map/backward/pallas_call | solution.py:484
  43.7 2.2 %collective-permute-done.20 = bf16[4,6,128,128]{3,2,1,0:T(8,128)(2,1)S(1)} collective-permute-done((bf16[4,6,128,128]{3,2,1,0:T(8,128)(2,1)S(1)}, bf16[4,6,128,128]{3,2,1,0:T(8,128)(2,1)S(1)}, u32[]{:S(2)}, u32[]{:S(2)}) %collective-permute-start.20) | collective-permute-done | bytes 786464 | tf_op jit(solution)/shard_map/ppermute | solution.py:357
  46.3 1.5 %collective-permute-start.21 = (bf16[6,128,128]{2,1,0:T(8,128)(2,1)S(1)}, bf16[6,128,128]{2,1,0:T(8,128)(2,1)S(1)}, u32[]{:S(2)}, u32[]{:S(2)}) collective-permute-start(bf16[6,128,128]{2,1,0:T(8,128)(2,1)S(1)} %get-tuple-element.88), channel_id=1, source_target_pairs={{0,24},{8,16},{16,8},{24,0},{1,25},{9,17},{17,9},{25,1},{2,26},{10... | collective-permute-start | bytes 589832 | tf_op jit(solution)/shard_map/ppermute | solution.py:357
  47.8 3.6 %collective-permute-start.22 = (bf16[6,128,128]{2,1,0:T(8,128)(2,1)S(1)}, bf16[6,128,128]{2,1,0:T(8,128)(2,1)S(1)}, u32[]{:S(2)}, u32[]{:S(2)}) collective-permute-start(bf16[6,128,128]{2,1,0:T(8,128)(2,1)S(1)} %get-tuple-element.89), channel_id=1, source_target_pairs={{0,16},{8,24},{16,0},{24,8},{1,17},{9,25},{17,1},{25,9},{2,18},{10... | collective-permute-start | bytes 589832 | tf_op jit(solution)/shard_map/ppermute | solution.py:357
  51.4 3.1 %collective-permute-start.25 = (bf16[2,2,32,128]{3,2,1,0:T(8,128)(2,1)S(1)}, bf16[2,2,32,128]{3,2,1,0:T(8,128)(2,1)S(1)}, u32[]{:S(2)}, u32[]{:S(2)}) collective-permute-start(bf16[2,2,32,128]{3,2,1,0:T(8,128)(2,1)S(1)} %get-tuple-element.109), channel_id=1, source_target_pairs={{0,3},{1,2},{2,1},{3,0},{4,7},{5,6},{6,5},{7,4},{8,11},{9,10},{10,... | collective-permute-start | bytes 98312 | tf_op jit(solution)/shard_map/ppermute | solution.py:357
  54.6 2.6 %collective-permute-done.25 = bf16[2,2,32,128]{3,2,1,0:T(8,128)(2,1)S(1)} collective-permute-done((bf16[2,2,32,128]{3,2,1,0:T(8,128)(2,1)S(1)}, bf16[2,2,32,128]{3,2,1,0:T(8,128)(2,1)S(1)}, u32[]{:S(2)}, u32[]{:S(2)}) %collective-permute-start.25) | collective-permute-done | bytes 32800 | tf_op jit(solution)/shard_map/ppermute | solution.py:357
  57.3 2.1 %collective-permute-done.26 = bf16[2,2,32,128]{3,2,1,0:T(8,128)(2,1)S(1)} collective-permute-done((bf16[2,2,32,128]{3,2,1,0:T(8,128)(2,1)S(1)}, bf16[2,2,32,128]{3,2,1,0:T(8,128)(2,1)S(1)}, u32[]{:S(2)}, u32[]{:S(2)}) %collective-permute-start.26) | collective-permute-done | bytes 32800 | tf_op jit(solution)/shard_map/ppermute | solution.py:357
  59.4 1.7 %collective-permute-done.27 = bf16[2,2,32,128]{3,2,1,0:T(8,128)(2,1)S(1)} collective-permute-done((bf16[2,2,32,128]{3,2,1,0:T(8,128)(2,1)S(1)}, bf16[2,2,32,128]{3,2,1,0:T(8,128)(2,1)S(1)}, u32[]{:S(2)}, u32[]{:S(2)}) %collective-permute-start.27) | collective-permute-done | bytes 32800 | tf_op jit(solution)/shard_map/ppermute | solution.py:357
  61.2 1.2 %collective-permute-start.28 = (bf16[384,128]{1,0:T(8,128)(2,1)S(1)}, bf16[384,128]{1,0:T(8,128)(2,1)S(1)}, u32[]{:S(2)}, u32[]{:S(2)}) collective-permute-start(bf16[384,128]{1,0:T(8,128)(2,1)S(1)} %dynamic-slice_bitcast_fusion), channel_id=1, source_target_pairs={{0,1},{1,0},{2,3},{3,2},{4,5},{5,4},{6,7},{7,6},{8,9},{9,8},{10,11... | collective-permute-start | bytes 294920 | tf_op jit(solution)/shard_map/ppermute | solution.py:357
  62.4 3.5 %collective-permute-done.28 = bf16[384,128]{1,0:T(8,128)(2,1)S(1)} collective-permute-done((bf16[384,128]{1,0:T(8,128)(2,1)S(1)}, bf16[384,128]{1,0:T(8,128)(2,1)S(1)}, u32[]{:S(2)}, u32[]{:S(2)}) %collective-permute-start.28) | collective-permute-done | bytes 98336 | tf_op jit(solution)/shard_map/ppermute | solution.py:357
  66.0 1.8 %collective-permute-start.29 = (bf16[384,128]{1,0:T(8,128)(2,1)S(1)}, bf16[384,128]{1,0:T(8,128)(2,1)S(1)}, u32[]{:S(2)}, u32[]{:S(2)}) collective-permute-start(bf16[384,128]{1,0:T(8,128)(2,1)S(1)} %fusion.6), channel_id=1, source_target_pairs={{0,2},{1,3},{2,0},{3,1},{4,6},{5,7},{6,4},{7,5},{8,10},{9,11},{10,... | collective-permute-start | bytes 294920 | tf_op jit(solution)/shard_map/ppermute | solution.py:357
  67.8 4.9 %collective-permute-done.29 = bf16[384,128]{1,0:T(8,128)(2,1)S(1)} collective-permute-done((bf16[384,128]{1,0:T(8,128)(2,1)S(1)}, bf16[384,128]{1,0:T(8,128)(2,1)S(1)}, u32[]{:S(2)}, u32[]{:S(2)}) %collective-permute-start.29) | collective-permute-done | bytes 98336 | tf_op jit(solution)/shard_map/ppermute | solution.py:357
  72.9 4.5 %collective-permute-done.30 = bf16[384,128]{1,0:T(8,128)(2,1)S(1)} collective-permute-done((bf16[384,128]{1,0:T(8,128)(2,1)S(1)}, bf16[384,128]{1,0:T(8,128)(2,1)S(1)}, u32[]{:S(2)}, u32[]{:S(2)}) %collective-permute-start.30) | collective-permute-done | bytes 98336 | tf_op jit(solution)/shard_map/ppermute | solution.py:357
  77.6 1.4 %collective-permute-done.31.other_ref = bf16[2,384,128]{2,1,0:T(8,128)(2,1)S(1)} collective-permute-done((bf16[2,384,128]{2,1,0:T(8,128)(2,1)S(1)}, bf16[2,384,128]{2,1,0:T(8,128)(2,1)S(1)}, u32[]{:S(2)}, u32[]{:S(2)}) %collective-permute-start.31) | collective-permute-done | bytes 196640 | tf_op jit(solution)/shard_map/ppermute | solution.py:357
  79.0 1.1 %closing.1 = (f32[1,9,128,128]{3,2,1,0:T(8,128)}, f32[1,3,128,128]{3,2,1,0:T(8,128)}) custom-call(bf16[2,384,128]{2,1,0:T(8,128)(2,1)S(1)} %pad_maximum_fusion.1.mine_ref, bf16[2,384,128]{2,1,0:T(8,128)(2,1)S(1)} %collective-permute-done.31.other_ref), custom_call_target="tpu_custom_call" | custom-call | tf_op jit(solution)/shard_map/closing/pallas_call | solution.py:537
  (67 shorter events, 12.7 us)
Async XLA Ops:
  2.6 13.2 %collective-permute-start.3 = (bf16[6,128,128]{2,1,0:T(8,128)(2,1)S(1)}, bf16[6,128,128]{2,1,0:T(8,128)(2,1)S(1)}, u32[]{:S(2)}, u32[]{:S(2)}) collective-permute-start(bf16[6,128,128]{2,1,0:T(8,128)(2,1)S(1)} %fusion.5.rest_0_), channel_id=1, source_target_pairs={{0,8},{8,0},{16,24},{24,16},{1,9},{9,1},{17,25},{25,17},{2,10},{10... | collective-permute-start | bytes 589832 | tf_op jit(solution)/shard_map/ppermute | solution.py:357
  5.6 10.2 %collective-permute-start.4 = (bf16[6,128,128]{2,1,0:T(8,128)(2,1)S(1)}, bf16[6,128,128]{2,1,0:T(8,128)(2,1)S(1)}, u32[]{:S(2)}, u32[]{:S(2)}) collective-permute-start(bf16[6,128,128]{2,1,0:T(8,128)(2,1)S(1)} %fusion.5.rest_0_), channel_id=1, source_target_pairs={{0,16},{8,24},{16,0},{24,8},{1,17},{9,25},{17,1},{25,9},{2,18},{10... | collective-permute-start | bytes 589832 | tf_op jit(solution)/shard_map/ppermute | solution.py:357
  7.1 6.3 %collective-permute-start = (bf16[2,2,48,128]{3,2,1,0:T(8,128)(2,1)S(1)}, bf16[2,2,48,128]{3,2,1,0:T(8,128)(2,1)S(1)}, u32[]{:S(2)}, u32[]{:S(2)}) collective-permute-start(bf16[2,2,48,128]{3,2,1,0:T(8,128)(2,1)S(1)} %get-tuple-element.60), channel_id=1, source_target_pairs={{0,3},{1,2},{2,1},{3,0},{4,7},{5,6},{6,5},{7,4},{8,11},{9,10},{10,... | collective-permute-start | bytes 147464 | tf_op jit(solution)/shard_map/ppermute | solution.py:357
  10.7 5.0 %collective-permute-start.1 = (bf16[2,2,48,128]{3,2,1,0:T(8,128)(2,1)S(1)}, bf16[2,2,48,128]{3,2,1,0:T(8,128)(2,1)S(1)}, u32[]{:S(2)}, u32[]{:S(2)}) collective-permute-start(bf16[2,2,48,128]{3,2,1,0:T(8,128)(2,1)S(1)} %get-tuple-element.61), channel_id=1, source_target_pairs={{0,2},{1,3},{2,0},{3,1},{4,6},{5,7},{6,4},{7,5},{8,10},{9,11},{10,... | collective-permute-start | bytes 147464 | tf_op jit(solution)/shard_map/ppermute | solution.py:357
  10.7 5.0 %collective-permute-start.2 = (bf16[2,2,48,128]{3,2,1,0:T(8,128)(2,1)S(1)}, bf16[2,2,48,128]{3,2,1,0:T(8,128)(2,1)S(1)}, u32[]{:S(2)}, u32[]{:S(2)}) collective-permute-start(bf16[2,2,48,128]{3,2,1,0:T(8,128)(2,1)S(1)} %get-tuple-element.62), channel_id=1, source_target_pairs={{0,1},{1,0},{2,3},{3,2},{4,5},{5,4},{6,7},{7,6},{8,9},{9,8},{10,11... | collective-permute-start | bytes 147464 | tf_op jit(solution)/shard_map/ppermute | solution.py:357
  13.4 8.5 %collective-permute-start.7 = (bf16[2,2,128,128]{3,2,1,0:T(8,128)(2,1)}, bf16[2,2,128,128]{3,2,1,0:T(8,128)(2,1)S(1)}, u32[]{:S(2)}, u32[]{:S(2)}) collective-permute-start(bf16[2,2,128,128]{3,2,1,0:T(8,128)(2,1)} %rest_0_.1), channel_id=1, source_target_pairs={{8,0},{9,1},{2,10},{3,11},{16,8},{17,9},{10,18},{11,19},{24,16},{2... | collective-permute-start | bytes 393224 | tf_op jit(solution)/shard_map/ppermute | solution.py:395
  15.7 6.1 %collective-permute-start.6 = (bf16[2,2,128,128]{3,2,1,0:T(8,128)(2,1)}, bf16[2,2,128,128]{3,2,1,0:T(8,128)(2,1)S(1)}, u32[]{:S(2)}, u32[]{:S(2)}) collective-permute-start(bf16[2,2,128,128]{3,2,1,0:T(8,128)(2,1)} %rest_0_.1), channel_id=1, source_target_pairs={{0,4},{4,0},{1,5},{5,1},{2,6},{6,2},{3,7},{7,3},{8,12},{12,8},{9,1... | collective-permute-start | bytes 393224 | tf_op jit(solution)/shard_map/ppermute | solution.py:357
  15.8 9.9 %collective-permute-start.5 = (bf16[4,2,2,48,128]{4,3,2,1,0:T(8,128)(2,1)S(1)}, bf16[4,2,2,48,128]{4,3,2,1,0:T(8,128)(2,1)S(1)}, u32[]{:S(2)}, u32[]{:S(2)}) collective-permute-start(bf16[4,2,2,48,128]{4,3,2,1,0:T(8,128)(2,1)S(1)} %pad_maximum_fusion.rest_8_), channel_id=1, source_target_pairs={{0,8},{1,9},{2,10},{3,11},{8,0},{9,1},{10,2},{11,3},{16,24},{17,25... | collective-permute-start | bytes 589832 | tf_op jit(solution)/shard_map/ppermute | solution.py:386
  17.5 8.1 %collective-permute-start.9 = (bf16[6,128,128]{2,1,0:T(8,128)(2,1)S(1)}, bf16[6,128,128]{2,1,0:T(8,128)(2,1)S(1)}, u32[]{:S(2)}, u32[]{:S(2)}) collective-permute-start(bf16[6,128,128]{2,1,0:T(8,128)(2,1)S(1)} %collective-permute-done.3.rest_2_), channel_id=1, source_target_pairs={{0,16},{8,24},{16,0},{24,8},{1,17},{9,25},{17,1},{25,9},{2,18},{10... | collective-permute-start | bytes 589832 | tf_op jit(solution)/shard_map/ppermute | solution.py:357
  18.0 8.1 %collective-permute-start.16 = (bf16[4,2,2,48,128]{4,3,2,1,0:T(8,128)(2,1)S(1)}, bf16[4,2,2,48,128]{4,3,2,1,0:T(8,128)(2,1)S(1)}, u32[]{:S(2)}, u32[]{:S(2)}) collective-permute-start(bf16[4,2,2,48,128]{4,3,2,1,0:T(8,128)(2,1)S(1)} %pad_maximum_fusion.rest_8_), channel_id=1, source_target_pairs={{8,16},{9,17},{10,18},{11,19},{16,8},{17,9},{18,10},{19,11},{12,20... | collective-permute-start | bytes 589832 | tf_op jit(solution)/shard_map/ppermute | solution.py:386
  23.5 7.1 %collective-permute-start.17 = (bf16[4,2,2,48,128]{4,3,2,1,0:T(8,128)(2,1)S(1)}, bf16[4,2,2,48,128]{4,3,2,1,0:T(8,128)(2,1)S(1)}, u32[]{:S(2)}, u32[]{:S(2)}) collective-permute-start(bf16[4,2,2,48,128]{4,3,2,1,0:T(8,128)(2,1)S(1)} %pad_maximum_fusion.rest_8_), channel_id=1, source_target_pairs={{0,4},{4,0},{1,5},{5,1},{2,6},{6,2},{3,7},{7,3},{8,12},{12,8},{9,1... | collective-permute-start | bytes 589832 | tf_op jit(solution)/shard_map/ppermute | solution.py:357
  25.6 4.9 %collective-permute-start.18 = (bf16[4,2,2,48,128]{4,3,2,1,0:T(8,128)(2,1)S(1)}, bf16[4,2,2,48,128]{4,3,2,1,0:T(8,128)(2,1)S(1)}, u32[]{:S(2)}, u32[]{:S(2)}) collective-permute-start(bf16[4,2,2,48,128]{4,3,2,1,0:T(8,128)(2,1)S(1)} %collective-permute-done.5.rest_9_), channel_id=1, source_target_pairs={{0,4},{4,0},{1,5},{5,1},{2,6},{6,2},{3,7},{7,3},{8,12},{12,8},{9,1... | collective-permute-start | bytes 589832 | tf_op jit(solution)/shard_map/ppermute | solution.py:357
  26.1 5.3 %collective-permute-start.12 = (bf16[6,128,128]{2,1,0:T(8,128)(2,1)S(1)}, bf16[6,128,128]{2,1,0:T(8,128)(2,1)S(1)}, u32[]{:S(2)}, u32[]{:S(2)}) collective-permute-start(bf16[6,128,128]{2,1,0:T(8,128)(2,1)S(1)} %collective-permute-done.9.rest_4_), channel_id=1, source_target_pairs={{0,4},{4,0},{1,5},{5,1},{2,6},{6,2},{3,7},{7,3},{8,12},{12,8},{9,1... | collective-permute-start | bytes 589832 | tf_op jit(solution)/shard_map/ppermute | solution.py:357
  26.2 5.3 %collective-permute-start.19 = (bf16[4,2,2,48,128]{4,3,2,1,0:T(8,128)(2,1)S(1)}, bf16[4,2,2,48,128]{4,3,2,1,0:T(8,128)(2,1)S(1)}, u32[]{:S(2)}, u32[]{:S(2)}) collective-permute-start(bf16[4,2,2,48,128]{4,3,2,1,0:T(8,128)(2,1)S(1)} %collective-permute-done.16.rest_10_), channel_id=1, source_target_pairs={{0,4},{4,0},{1,5},{5,1},{2,6},{6,2},{3,7},{7,3},{8,12},{12,8},{9,1... | collective-permute-start | bytes 589832 | tf_op jit(solution)/shard_map/ppermute | solution.py:357
  27.1 10.6 %collective-permute-start.13 = (bf16[2,4,48,128]{3,2,1,0:T(8,128)(2,1)S(1)}, bf16[2,4,48,128]{3,2,1,0:T(8,128)(2,1)S(1)}, u32[]{:S(2)}, u32[]{:S(2)}) collective-permute-start(bf16[2,4,48,128]{3,2,1,0:T(8,128)(2,1)S(1)} %get-tuple-element.74), channel_id=1, source_target_pairs={{0,3},{1,2},{2,1},{3,0},{4,7},{5,6},{6,5},{7,4},{8,11},{9,10},{10,... | collective-permute-start | bytes 294920 | tf_op jit(solution)/shard_map/ppermute | solution.py:357
  30.6 7.5 %collective-permute-start.14 = (bf16[2,4,48,128]{3,2,1,0:T(8,128)(2,1)S(1)}, bf16[2,4,48,128]{3,2,1,0:T(8,128)(2,1)S(1)}, u32[]{:S(2)}, u32[]{:S(2)}) collective-permute-start(bf16[2,4,48,128]{3,2,1,0:T(8,128)(2,1)S(1)} %get-tuple-element.75), channel_id=1, source_target_pairs={{0,2},{1,3},{2,0},{3,1},{4,6},{5,7},{6,4},{7,5},{8,10},{9,11},{10,... | collective-permute-start | bytes 294920 | tf_op jit(solution)/shard_map/ppermute | solution.py:357
  30.6 7.5 %collective-permute-start.15 = (bf16[2,4,48,128]{3,2,1,0:T(8,128)(2,1)S(1)}, bf16[2,4,48,128]{3,2,1,0:T(8,128)(2,1)S(1)}, u32[]{:S(2)}, u32[]{:S(2)}) collective-permute-start(bf16[2,4,48,128]{3,2,1,0:T(8,128)(2,1)S(1)} %get-tuple-element.76), channel_id=1, source_target_pairs={{0,1},{1,0},{2,3},{3,2},{4,5},{5,4},{6,7},{7,6},{8,9},{9,8},{10,11... | collective-permute-start | bytes 294920 | tf_op jit(solution)/shard_map/ppermute | solution.py:357
  46.1 5.2 %collective-permute-start.24 = (bf16[4,2,2,16,128]{4,3,2,1,0:T(8,128)(2,1)S(1)}, bf16[4,2,2,16,128]{4,3,2,1,0:T(8,128)(2,1)S(1)}, u32[]{:S(2)}, u32[]{:S(2)}) collective-permute-start(bf16[4,2,2,16,128]{4,3,2,1,0:T(8,128)(2,1)S(1)} %get-tuple-element.92), channel_id=1, source_target_pairs={{0,4},{4,0},{1,5},{5,1},{2,6},{6,2},{3,7},{7,3},{8,12},{12,8},{9,1... | collective-permute-start | bytes 196616 | tf_op jit(solution)/shard_map/ppermute | solution.py:357
  46.3 14.8 %collective-permute-start.21 = (bf16[6,128,128]{2,1,0:T(8,128)(2,1)S(1)}, bf16[6,128,128]{2,1,0:T(8,128)(2,1)S(1)}, u32[]{:S(2)}, u32[]{:S(2)}) collective-permute-start(bf16[6,128,128]{2,1,0:T(8,128)(2,1)S(1)} %get-tuple-element.88), channel_id=1, source_target_pairs={{0,24},{8,16},{16,8},{24,0},{1,25},{9,17},{17,9},{25,1},{2,26},{10... | collective-permute-start | bytes 589832 | tf_op jit(solution)/shard_map/ppermute | solution.py:357
  47.8 13.3 %collective-permute-start.22 = (bf16[6,128,128]{2,1,0:T(8,128)(2,1)S(1)}, bf16[6,128,128]{2,1,0:T(8,128)(2,1)S(1)}, u32[]{:S(2)}, u32[]{:S(2)}) collective-permute-start(bf16[6,128,128]{2,1,0:T(8,128)(2,1)S(1)} %get-tuple-element.89), channel_id=1, source_target_pairs={{0,16},{8,24},{16,0},{24,8},{1,17},{9,25},{17,1},{25,9},{2,18},{10... | collective-permute-start | bytes 589832 | tf_op jit(solution)/shard_map/ppermute | solution.py:357
  51.4 9.7 %collective-permute-start.23 = (bf16[6,128,128]{2,1,0:T(8,128)(2,1)S(1)}, bf16[6,128,128]{2,1,0:T(8,128)(2,1)S(1)}, u32[]{:S(2)}, u32[]{:S(2)}) collective-permute-start(bf16[6,128,128]{2,1,0:T(8,128)(2,1)S(1)} %get-tuple-element.90), channel_id=1, source_target_pairs={{0,8},{8,0},{16,24},{24,16},{1,9},{9,1},{17,25},{25,17},{2,10},{10... | collective-permute-start | bytes 589832 | tf_op jit(solution)/shard_map/ppermute | solution.py:357
  51.4 5.8 %collective-permute-start.25 = (bf16[2,2,32,128]{3,2,1,0:T(8,128)(2,1)S(1)}, bf16[2,2,32,128]{3,2,1,0:T(8,128)(2,1)S(1)}, u32[]{:S(2)}, u32[]{:S(2)}) collective-permute-start(bf16[2,2,32,128]{3,2,1,0:T(8,128)(2,1)S(1)} %get-tuple-element.109), channel_id=1, source_target_pairs={{0,3},{1,2},{2,1},{3,0},{4,7},{5,6},{6,5},{7,4},{8,11},{9,10},{10,... | collective-permute-start | bytes 98312 | tf_op jit(solution)/shard_map/ppermute | solution.py:357
  54.5 4.8 %collective-permute-start.26 = (bf16[2,2,32,128]{3,2,1,0:T(8,128)(2,1)S(1)}, bf16[2,2,32,128]{3,2,1,0:T(8,128)(2,1)S(1)}, u32[]{:S(2)}, u32[]{:S(2)}) collective-permute-start(bf16[2,2,32,128]{3,2,1,0:T(8,128)(2,1)S(1)} %get-tuple-element.110), channel_id=1, source_target_pairs={{0,2},{1,3},{2,0},{3,1},{4,6},{5,7},{6,4},{7,5},{8,10},{9,11},{10,... | collective-permute-start | bytes 98312 | tf_op jit(solution)/shard_map/ppermute | solution.py:357
  66.0 6.7 %collective-permute-start.29 = (bf16[384,128]{1,0:T(8,128)(2,1)S(1)}, bf16[384,128]{1,0:T(8,128)(2,1)S(1)}, u32[]{:S(2)}, u32[]{:S(2)}) collective-permute-start(bf16[384,128]{1,0:T(8,128)(2,1)S(1)} %fusion.6), channel_id=1, source_target_pairs={{0,2},{1,3},{2,0},{3,1},{4,6},{5,7},{6,4},{7,5},{8,10},{9,11},{10,... | collective-permute-start | bytes 294920 | tf_op jit(solution)/shard_map/ppermute | solution.py:357
  (11 other events, 28.9 us)

commit v17 on v15

--- a/solution.py
+++ b/solution.py
@@ -411,8 +411,8 @@
 
     along_x = swapped(half_kernels, "section", 1)
     along_y = swapped(half_kernels, "section", 2)
-    own_video, along_x, along_y, spatial, temporal = lax.optimization_barrier(
-        [gathered(cuts), along_x, along_y, spatial, temporal]
+    own_video, along_x, spatial, temporal = lax.optimization_barrier(
+        [gathered(cuts), along_x, spatial, temporal]
     )
     near, far = traded(own_video, 0), traded(own_video, 1)
     mine = [along_x, along_y, swapped(along_x, "section", 2)]

time: 78.6 us -> 80.2 us (1.020)
  starting transfers between devices: 34.6 us -> 36.1 us
    ppermute x29, starting transfers between devices: 32 us -> 33.5 us  [swapped(): return lax.ppermute(value, axis, [(i, i ^ step) for i in range(count)])]
  transfers between devices with their start and end apart: 32 -> 32, of which waited for: 15 -> 13; matrix products, arithmetic and copies ran while one was open for 1% -> 3% of each run, Pallas kernels for 8% -> 8%
where the time goes in v17:
time: 80.2 us; the launch traced here: 80 us
  starting transfers between devices  36.1 us (45%)
  waiting for transfers between devices  25.8 us (32%)
  Pallas kernels  12.8 us (16%)
  other arithmetic  2.48 us (3%)
  local copies, waits for them, and re-layouts  1.9 us (2%)
  between operations  0.88 us (1%)
    ppermute x29, starting transfers between devices, swapped(): return lax.ppermute(value, axis, [(i, i ^ step) for i in range(count)])  33.5 us
    ppermute x29, waiting for transfers between devices, swapped(): return lax.ppermute(value, axis, [(i, i ^ step) for i in range(count)])  23.5 us
    pallas_call x1, Pallas kernels, on_device(): pl.pallas_call(functools.partial(forward_kernel, geometry), name='forward...  6.17 us
    pallas_call x1, Pallas kernels, on_device(): pl.pallas_call(functools.partial(backward_kernel, geometry, factor), name...  5.39 us
    ppermute x2, waiting for transfers between devices, traded(): return lax.ppermute(value, ('section', 'space'), pairs)  2.31 us
    concatenate x2, other arithmetic, core_half(): whole = jnp.concatenate([spatial[0], temporal[0]], 0)  2.01 us
    unnamed x6, local copies, waits for them, and re-layouts  1.8 us
  transfers between devices with their start and end apart: 32, of which 13 were waited for; matrix products, arithmetic and copies ran while one was open for 3% of the time, Pallas kernels for 8%

profile of v17, /device:TPU:0, one launch (start us, length us, event | category | flops | bytes accessed | tf_op | source)
XLA Modules:
  0.0 80.0 jit_solution(14824565592244868598)
XLA Ops:
  3.9 3.6 %collective-permute-start.3 = (bf16[6,128,128]{2,1,0:T(8,128)(2,1)S(1)}, bf16[6,128,128]{2,1,0:T(8,128)(2,1)S(1)}, u32[]{:S(2)}, u32[]{:S(2)}) collective-permute-start(bf16[6,128,128]{2,1,0:T(8,128)(2,1)S(1)} %fusion.5.rest_0_), channel_id=1, source_target_pairs={{0,8},{8,0},{16,24},{24,16},{1,9},{9,1},{17,25},{25,17},{2,10},{10... | collective-permute-start | bytes 589832 | tf_op jit(solution)/shard_map/ppermute | solution.py:353
  7.5 2.1 %collective-permute-start = (bf16[2,2,48,128]{3,2,1,0:T(8,128)(2,1)S(1)}, bf16[2,2,48,128]{3,2,1,0:T(8,128)(2,1)S(1)}, u32[]{:S(2)}, u32[]{:S(2)}) collective-permute-start(bf16[2,2,48,128]{3,2,1,0:T(8,128)(2,1)S(1)} %get-tuple-element.59), channel_id=1, source_target_pairs={{0,1},{1,0},{2,3},{3,2},{4,5},{5,4},{6,7},{7,6},{8,9},{9,8},{10,11... | collective-permute-start | bytes 147464 | tf_op jit(solution)/shard_map/ppermute | solution.py:353
  9.6 3.5 %collective-permute-start.1 = (bf16[2,2,48,128]{3,2,1,0:T(8,128)(2,1)S(1)}, bf16[2,2,48,128]{3,2,1,0:T(8,128)(2,1)S(1)}, u32[]{:S(2)}, u32[]{:S(2)}) collective-permute-start(bf16[2,2,48,128]{3,2,1,0:T(8,128)(2,1)S(1)} %get-tuple-element.60), channel_id=1, source_target_pairs={{0,2},{1,3},{2,0},{3,1},{4,6},{5,7},{6,4},{7,5},{8,10},{9,11},{10,... | collective-permute-start | bytes 147464 | tf_op jit(solution)/shard_map/ppermute | solution.py:353
  13.7 2.3 %collective-permute-done.1 = bf16[2,2,48,128]{3,2,1,0:T(8,128)(2,1)S(1)} collective-permute-done((bf16[2,2,48,128]{3,2,1,0:T(8,128)(2,1)S(1)}, bf16[2,2,48,128]{3,2,1,0:T(8,128)(2,1)S(1)}, u32[]{:S(2)}, u32[]{:S(2)}) %collective-permute-start.1) | collective-permute-done | bytes 49184 | tf_op jit(solution)/shard_map/ppermute | solution.py:353
  16.5 2.5 %collective-permute-done.2 = bf16[2,2,48,128]{3,2,1,0:T(8,128)(2,1)S(1)} collective-permute-done((bf16[2,2,48,128]{3,2,1,0:T(8,128)(2,1)S(1)}, bf16[2,2,48,128]{3,2,1,0:T(8,128)(2,1)S(1)}, u32[]{:S(2)}, u32[]{:S(2)}) %collective-permute-start.2) | collective-permute-done | bytes 49184 | tf_op jit(solution)/shard_map/ppermute | solution.py:353
  19.7 1.5 %collective-permute-start.9 = (bf16[6,128,128]{2,1,0:T(8,128)(2,1)S(1)}, bf16[6,128,128]{2,1,0:T(8,128)(2,1)S(1)}, u32[]{:S(2)}, u32[]{:S(2)}) collective-permute-start(bf16[6,128,128]{2,1,0:T(8,128)(2,1)S(1)} %collective-permute-done.3.rest_2_), channel_id=1, source_target_pairs={{0,16},{8,24},{16,0},{24,8},{1,17},{9,25},{17,1},{25,9},{2,18},{10... | collective-permute-start | bytes 589832 | tf_op jit(solution)/shard_map/ppermute | solution.py:353
  24.6 2.3 %collective-permute-done.4.rest_9_ = bf16[4,2,2,48,128]{4,3,2,1,0:T(8,128)(2,1)S(1)} collective-permute-done((bf16[4,2,2,48,128]{4,3,2,1,0:T(8,128)(2,1)S(1)}, bf16[4,2,2,48,128]{4,3,2,1,0:T(8,128)(2,1)S(1)}, u32[]{:S(2)}, u32[]{:S(2)}) %collective-permute-start.4) | collective-permute-done | bytes 196640 | tf_op jit(solution)/shard_map/ppermute | solution.py:378
  26.9 1.4 %collective-permute-done.9.rest_4_ = bf16[6,128,128]{2,1,0:T(8,128)(2,1)S(1)} collective-permute-done((bf16[6,128,128]{2,1,0:T(8,128)(2,1)S(1)}, bf16[6,128,128]{2,1,0:T(8,128)(2,1)S(1)}, u32[]{:S(2)}, u32[]{:S(2)}) %collective-permute-start.9) | collective-permute-done | bytes 196640 | tf_op jit(solution)/shard_map/ppermute | solution.py:353
  29.3 2.5 %collective-permute-start.14 = (bf16[2,4,48,128]{3,2,1,0:T(8,128)(2,1)S(1)}, bf16[2,4,48,128]{3,2,1,0:T(8,128)(2,1)S(1)}, u32[]{:S(2)}, u32[]{:S(2)}) collective-permute-start(bf16[2,4,48,128]{3,2,1,0:T(8,128)(2,1)S(1)} %get-tuple-element.73), channel_id=1, source_target_pairs={{0,2},{1,3},{2,0},{3,1},{4,6},{5,7},{6,4},{7,5},{8,10},{9,11},{10,... | collective-permute-start | bytes 294920 | tf_op jit(solution)/shard_map/ppermute | solution.py:353
  31.8 1.5 %collective-permute-start.15 = (bf16[2,4,48,128]{3,2,1,0:T(8,128)(2,1)S(1)}, bf16[2,4,48,128]{3,2,1,0:T(8,128)(2,1)S(1)}, u32[]{:S(2)}, u32[]{:S(2)}) collective-permute-start(bf16[2,4,48,128]{3,2,1,0:T(8,128)(2,1)S(1)} %get-tuple-element.74), channel_id=1, source_target_pairs={{0,3},{1,2},{2,1},{3,0},{4,7},{5,6},{6,5},{7,4},{8,11},{9,10},{10,... | collective-permute-start | bytes 294920 | tf_op jit(solution)/shard_map/ppermute | solution.py:353
  33.3 6.2 %forward.1 = (bf16[4,4,10,16,384]{4,3,2,1,0:T(8,128)(2,1)S(1)}, bf16[4,4,8,16,128]{4,3,2,1,0:T(8,128)(2,1)S(1)}, f32[4,10,32,128]{3,2,1,0:T(8,128)S(1)}, f32[4,1...) custom-call(bf16[6,128,128]{2,1,0:T(8,128)(2,1)S(1)} %fusion.5.rest_0_, ...), custom_call_target="tpu_custom_call" | custom-call | flops 6000000000 | bytes 8000000 | tf_op jit(solution)/shard_map/forward/pallas_call | solution.py:451
  40.1 5.4 %backward.1 = (bf16[4,6,128,128]{3,2,1,0:T(8,128)(2,1)S(1)}, bf16[4,6,128,128]{3,2,1,0:T(8,128)(2,1)S(1)}, bf16[4,2,2,16,128]{4,3,2,1,0:T(8,128)(2,1)S(1)}, bf16[4,2,2,16,128]{4,3,2,1,0:T(8,128)(2,1)S(1)}) custom-call(bf16[6,128,128]{2,1,0:T(8,128)(2,1)S(1)} %fusion.5.rest_0_, bf16[6,128,128]{2,1,0:T(8,128)(2,1)S(1)} %fusion.4.rest_1_, ...), custom_call_target="tpu_custom_call" | custom-call | flops 6000000000 | bytes 8000000 | tf_op jit(solution)/shard_map/backward/pallas_call | solution.py:476
  45.6 2.3 %collective-permute-done.20 = bf16[4,6,128,128]{3,2,1,0:T(8,128)(2,1)S(1)} collective-permute-done((bf16[4,6,128,128]{3,2,1,0:T(8,128)(2,1)S(1)}, bf16[4,6,128,128]{3,2,1,0:T(8,128)(2,1)S(1)}, u32[]{:S(2)}, u32[]{:S(2)}) %collective-permute-start.20) | collective-permute-done | bytes 786464 | tf_op jit(solution)/shard_map/ppermute | solution.py:353
  48.3 2.2 %collective-permute-start.21 = (bf16[6,128,128]{2,1,0:T(8,128)(2,1)S(1)}, bf16[6,128,128]{2,1,0:T(8,128)(2,1)S(1)}, u32[]{:S(2)}, u32[]{:S(2)}) collective-permute-start(bf16[6,128,128]{2,1,0:T(8,128)(2,1)S(1)} %get-tuple-element.86), channel_id=1, source_target_pairs={{0,8},{8,0},{16,24},{24,16},{1,9},{9,1},{17,25},{25,17},{2,10},{10... | collective-permute-start | bytes 589832 | tf_op jit(solution)/shard_map/ppermute | solution.py:353
  50.8 1.5 %collective-permute-start.23 = (bf16[6,128,128]{2,1,0:T(8,128)(2,1)S(1)}, bf16[6,128,128]{2,1,0:T(8,128)(2,1)S(1)}, u32[]{:S(2)}, u32[]{:S(2)}) collective-permute-start(bf16[6,128,128]{2,1,0:T(8,128)(2,1)S(1)} %get-tuple-element.88), channel_id=1, source_target_pairs={{0,24},{8,16},{16,8},{24,0},{1,25},{9,17},{17,9},{25,1},{2,26},{10... | collective-permute-start | bytes 589832 | tf_op jit(solution)/shard_map/ppermute | solution.py:353
  52.3 2.0 %collective-permute-start.25 = (bf16[2,2,32,128]{3,2,1,0:T(8,128)(2,1)S(1)}, bf16[2,2,32,128]{3,2,1,0:T(8,128)(2,1)S(1)}, u32[]{:S(2)}, u32[]{:S(2)}) collective-permute-start(bf16[2,2,32,128]{3,2,1,0:T(8,128)(2,1)S(1)} %get-tuple-element.107), channel_id=1, source_target_pairs={{0,1},{1,0},{2,3},{3,2},{4,5},{5,4},{6,7},{7,6},{8,9},{9,8},{10,11... | collective-permute-start | bytes 98312 | tf_op jit(solution)/shard_map/ppermute | solution.py:353
  56.3 2.4 %collective-permute-start.27 = (bf16[2,2,32,128]{3,2,1,0:T(8,128)(2,1)S(1)}, bf16[2,2,32,128]{3,2,1,0:T(8,128)(2,1)S(1)}, u32[]{:S(2)}, u32[]{:S(2)}) collective-permute-start(bf16[2,2,32,128]{3,2,1,0:T(8,128)(2,1)S(1)} %get-tuple-element.105), channel_id=1, source_target_pairs={{0,3},{1,2},{2,1},{3,0},{4,7},{5,6},{6,5},{7,4},{8,11},{9,10},{10,... | collective-permute-start | bytes 98312 | tf_op jit(solution)/shard_map/ppermute | solution.py:353
  59.5 2.6 %collective-permute-done.27 = bf16[2,2,32,128]{3,2,1,0:T(8,128)(2,1)S(1)} collective-permute-done((bf16[2,2,32,128]{3,2,1,0:T(8,128)(2,1)S(1)}, bf16[2,2,32,128]{3,2,1,0:T(8,128)(2,1)S(1)}, u32[]{:S(2)}, u32[]{:S(2)}) %collective-permute-start.27) | collective-permute-done | bytes 32800 | tf_op jit(solution)/shard_map/ppermute | solution.py:353
  62.3 1.8 %collective-permute-start.28 = (bf16[384,128]{1,0:T(8,128)(2,1)S(1)}, bf16[384,128]{1,0:T(8,128)(2,1)S(1)}, u32[]{:S(2)}, u32[]{:S(2)}) collective-permute-start(bf16[384,128]{1,0:T(8,128)(2,1)S(1)} %dynamic-slice_bitcast_fusion), channel_id=1, source_target_pairs={{0,1},{1,0},{2,3},{3,2},{4,5},{5,4},{6,7},{7,6},{8,9},{9,8},{10,11... | collective-permute-start | bytes 294920 | tf_op jit(solution)/shard_map/ppermute | solution.py:353
  64.1 2.9 %collective-permute-done.28 = bf16[384,128]{1,0:T(8,128)(2,1)S(1)} collective-permute-done((bf16[384,128]{1,0:T(8,128)(2,1)S(1)}, bf16[384,128]{1,0:T(8,128)(2,1)S(1)}, u32[]{:S(2)}, u32[]{:S(2)}) %collective-permute-start.28) | collective-permute-done | bytes 98336 | tf_op jit(solution)/shard_map/ppermute | solution.py:353
  67.0 2.8 %collective-permute-start.29 = (bf16[384,128]{1,0:T(8,128)(2,1)S(1)}, bf16[384,128]{1,0:T(8,128)(2,1)S(1)}, u32[]{:S(2)}, u32[]{:S(2)}) collective-permute-start(bf16[384,128]{1,0:T(8,128)(2,1)S(1)} %fusion.6), channel_id=1, source_target_pairs={{0,2},{1,3},{2,0},{3,1},{4,6},{5,7},{6,4},{7,5},{8,10},{9,11},{10,... | collective-permute-start | bytes 294920 | tf_op jit(solution)/shard_map/ppermute | solution.py:353
  69.8 2.8 %collective-permute-done.29 = bf16[384,128]{1,0:T(8,128)(2,1)S(1)} collective-permute-done((bf16[384,128]{1,0:T(8,128)(2,1)S(1)}, bf16[384,128]{1,0:T(8,128)(2,1)S(1)}, u32[]{:S(2)}, u32[]{:S(2)}) %collective-permute-start.29) | collective-permute-done | bytes 98336 | tf_op jit(solution)/shard_map/ppermute | solution.py:353
  72.7 1.8 %collective-permute-start.30 = (bf16[384,128]{1,0:T(8,128)(2,1)S(1)}, bf16[384,128]{1,0:T(8,128)(2,1)S(1)}, u32[]{:S(2)}, u32[]{:S(2)}) collective-permute-start(bf16[384,128]{1,0:T(8,128)(2,1)S(1)} %add_convert_fusion.5), channel_id=1, source_target_pairs={{0,1},{1,0},{2,3},{3,2},{4,5},{5,4},{6,7},{7,6},{8,9},{9,8},{10,11... | collective-permute-start | bytes 294920 | tf_op jit(solution)/shard_map/ppermute | solution.py:353
  74.4 2.9 %collective-permute-done.30 = bf16[384,128]{1,0:T(8,128)(2,1)S(1)} collective-permute-done((bf16[384,128]{1,0:T(8,128)(2,1)S(1)}, bf16[384,128]{1,0:T(8,128)(2,1)S(1)}, u32[]{:S(2)}, u32[]{:S(2)}) %collective-permute-start.30) | collective-permute-done | bytes 98336 | tf_op jit(solution)/shard_map/ppermute | solution.py:353
  (67 shorter events, 16.3 us)
Async XLA Ops:
  0.6 12.6 %collective-permute-start.6 = (bf16[2,2,128,128]{3,2,1,0:T(8,128)(2,1)}, bf16[2,2,128,128]{3,2,1,0:T(8,128)(2,1)S(1)}, u32[]{:S(2)}, u32[]{:S(2)}) collective-permute-start(bf16[2,2,128,128]{3,2,1,0:T(8,128)(2,1)} %rest_0_.1), channel_id=1, source_target_pairs={{8,0},{9,1},{2,10},{3,11},{16,8},{17,9},{10,18},{11,19},{24,16},{2... | collective-permute-start | bytes 393224 | tf_op jit(solution)/shard_map/ppermute | solution.py:387
  3.9 15.2 %collective-permute-start.3 = (bf16[6,128,128]{2,1,0:T(8,128)(2,1)S(1)}, bf16[6,128,128]{2,1,0:T(8,128)(2,1)S(1)}, u32[]{:S(2)}, u32[]{:S(2)}) collective-permute-start(bf16[6,128,128]{2,1,0:T(8,128)(2,1)S(1)} %fusion.5.rest_0_), channel_id=1, source_target_pairs={{0,8},{8,0},{16,24},{24,16},{1,9},{9,1},{17,25},{25,17},{2,10},{10... | collective-permute-start | bytes 589832 | tf_op jit(solution)/shard_map/ppermute | solution.py:353
  7.5 5.7 %collective-permute-start = (bf16[2,2,48,128]{3,2,1,0:T(8,128)(2,1)S(1)}, bf16[2,2,48,128]{3,2,1,0:T(8,128)(2,1)S(1)}, u32[]{:S(2)}, u32[]{:S(2)}) collective-permute-start(bf16[2,2,48,128]{3,2,1,0:T(8,128)(2,1)S(1)} %get-tuple-element.59), channel_id=1, source_target_pairs={{0,1},{1,0},{2,3},{3,2},{4,5},{5,4},{6,7},{7,6},{8,9},{9,8},{10,11... | collective-permute-start | bytes 147464 | tf_op jit(solution)/shard_map/ppermute | solution.py:353
  9.6 6.3 %collective-permute-start.1 = (bf16[2,2,48,128]{3,2,1,0:T(8,128)(2,1)S(1)}, bf16[2,2,48,128]{3,2,1,0:T(8,128)(2,1)S(1)}, u32[]{:S(2)}, u32[]{:S(2)}) collective-permute-start(bf16[2,2,48,128]{3,2,1,0:T(8,128)(2,1)S(1)} %get-tuple-element.60), channel_id=1, source_target_pairs={{0,2},{1,3},{2,0},{3,1},{4,6},{5,7},{6,4},{7,5},{8,10},{9,11},{10,... | collective-permute-start | bytes 147464 | tf_op jit(solution)/shard_map/ppermute | solution.py:353
  13.2 5.9 %collective-permute-start.2 = (bf16[2,2,48,128]{3,2,1,0:T(8,128)(2,1)S(1)}, bf16[2,2,48,128]{3,2,1,0:T(8,128)(2,1)S(1)}, u32[]{:S(2)}, u32[]{:S(2)}) collective-permute-start(bf16[2,2,48,128]{3,2,1,0:T(8,128)(2,1)S(1)} %get-tuple-element.61), channel_id=1, source_target_pairs={{0,3},{1,2},{2,1},{3,0},{4,7},{5,6},{6,5},{7,4},{8,11},{9,10},{10,... | collective-permute-start | bytes 147464 | tf_op jit(solution)/shard_map/ppermute | solution.py:353
  13.2 8.0 %collective-permute-start.5 = (bf16[2,2,128,128]{3,2,1,0:T(8,128)(2,1)}, bf16[2,2,128,128]{3,2,1,0:T(8,128)(2,1)S(1)}, u32[]{:S(2)}, u32[]{:S(2)}) collective-permute-start(bf16[2,2,128,128]{3,2,1,0:T(8,128)(2,1)} %rest_0_.1), channel_id=1, source_target_pairs={{0,4},{4,0},{1,5},{5,1},{2,6},{6,2},{3,7},{7,3},{8,12},{12,8},{9,1... | collective-permute-start | bytes 393224 | tf_op jit(solution)/shard_map/ppermute | solution.py:353
  13.2 8.7 %collective-permute-start.7 = (bf16[2,2,128,128]{3,2,1,0:T(8,128)(2,1)S(1)}, bf16[2,2,128,128]{3,2,1,0:T(8,128)(2,1)S(1)}, u32[]{:S(2)}, u32[]{:S(2)}) collective-permute-start(bf16[2,2,128,128]{3,2,1,0:T(8,128)(2,1)S(1)} %collective-permute-done.6.rest_2_), channel_id=1, source_target_pairs={{0,4},{4,0},{1,5},{5,1},{2,6},{6,2},{3,7},{7,3},{8,12},{12,8},{9,1... | collective-permute-start | bytes 393224 | tf_op jit(solution)/shard_map/ppermute | solution.py:353
  16.0 8.1 %collective-permute-start.8 = (bf16[6,128,128]{2,1,0:T(8,128)(2,1)S(1)}, bf16[6,128,128]{2,1,0:T(8,128)(2,1)S(1)}, u32[]{:S(2)}, u32[]{:S(2)}) collective-permute-start(bf16[6,128,128]{2,1,0:T(8,128)(2,1)S(1)} %fusion.5.rest_0_), channel_id=1, source_target_pairs={{0,16},{8,24},{16,0},{24,8},{1,17},{9,25},{17,1},{25,9},{2,18},{10... | collective-permute-start | bytes 589832 | tf_op jit(solution)/shard_map/ppermute | solution.py:353
  19.1 7.8 %collective-permute-start.4 = (bf16[4,2,2,48,128]{4,3,2,1,0:T(8,128)(2,1)S(1)}, bf16[4,2,2,48,128]{4,3,2,1,0:T(8,128)(2,1)S(1)}, u32[]{:S(2)}, u32[]{:S(2)}) collective-permute-start(bf16[4,2,2,48,128]{4,3,2,1,0:T(8,128)(2,1)S(1)} %pad_maximum_fusion.rest_8_), channel_id=1, source_target_pairs={{0,8},{1,9},{2,10},{3,11},{8,0},{9,1},{10,2},{11,3},{16,24},{17,25... | collective-permute-start | bytes 589832 | tf_op jit(solution)/shard_map/ppermute | solution.py:378
  19.7 8.6 %collective-permute-start.9 = (bf16[6,128,128]{2,1,0:T(8,128)(2,1)S(1)}, bf16[6,128,128]{2,1,0:T(8,128)(2,1)S(1)}, u32[]{:S(2)}, u32[]{:S(2)}) collective-permute-start(bf16[6,128,128]{2,1,0:T(8,128)(2,1)S(1)} %collective-permute-done.3.rest_2_), channel_id=1, source_target_pairs={{0,16},{8,24},{16,0},{24,8},{1,17},{9,25},{17,1},{25,9},{2,18},{10... | collective-permute-start | bytes 589832 | tf_op jit(solution)/shard_map/ppermute | solution.py:353
  21.2 7.1 %collective-permute-start.16 = (bf16[4,2,2,48,128]{4,3,2,1,0:T(8,128)(2,1)S(1)}, bf16[4,2,2,48,128]{4,3,2,1,0:T(8,128)(2,1)S(1)}, u32[]{:S(2)}, u32[]{:S(2)}) collective-permute-start(bf16[4,2,2,48,128]{4,3,2,1,0:T(8,128)(2,1)S(1)} %pad_maximum_fusion.rest_8_), channel_id=1, source_target_pairs={{8,16},{9,17},{10,18},{11,19},{16,8},{17,9},{18,10},{19,11},{12,20... | collective-permute-start | bytes 589832 | tf_op jit(solution)/shard_map/ppermute | solution.py:378
  21.9 6.9 %collective-permute-start.10 = (bf16[6,128,128]{2,1,0:T(8,128)(2,1)S(1)}, bf16[6,128,128]{2,1,0:T(8,128)(2,1)S(1)}, u32[]{:S(2)}, u32[]{:S(2)}) collective-permute-start(bf16[6,128,128]{2,1,0:T(8,128)(2,1)S(1)} %collective-permute-done.3.rest_2_), channel_id=1, source_target_pairs={{0,4},{4,0},{1,5},{5,1},{2,6},{6,2},{3,7},{7,3},{8,12},{12,8},{9,1... | collective-permute-start | bytes 589832 | tf_op jit(solution)/shard_map/ppermute | solution.py:353
  24.0 4.9 %collective-permute-start.17 = (bf16[4,2,2,48,128]{4,3,2,1,0:T(8,128)(2,1)S(1)}, bf16[4,2,2,48,128]{4,3,2,1,0:T(8,128)(2,1)S(1)}, u32[]{:S(2)}, u32[]{:S(2)}) collective-permute-start(bf16[4,2,2,48,128]{4,3,2,1,0:T(8,128)(2,1)S(1)} %pad_maximum_fusion.rest_8_), channel_id=1, source_target_pairs={{0,4},{4,0},{1,5},{5,1},{2,6},{6,2},{3,7},{7,3},{8,12},{12,8},{9,1... | collective-permute-start | bytes 589832 | tf_op jit(solution)/shard_map/ppermute | solution.py:353
  28.3 5.0 %collective-permute-start.12 = (bf16[6,128,128]{2,1,0:T(8,128)(2,1)S(1)}, bf16[6,128,128]{2,1,0:T(8,128)(2,1)S(1)}, u32[]{:S(2)}, u32[]{:S(2)}) collective-permute-start(bf16[6,128,128]{2,1,0:T(8,128)(2,1)S(1)} %collective-permute-done.9.rest_4_), channel_id=1, source_target_pairs={{0,4},{4,0},{1,5},{5,1},{2,6},{6,2},{3,7},{7,3},{8,12},{12,8},{9,1... | collective-permute-start | bytes 589832 | tf_op jit(solution)/shard_map/ppermute | solution.py:353
  28.9 10.6 %collective-permute-start.13 = (bf16[2,4,48,128]{3,2,1,0:T(8,128)(2,1)S(1)}, bf16[2,4,48,128]{3,2,1,0:T(8,128)(2,1)S(1)}, u32[]{:S(2)}, u32[]{:S(2)}) collective-permute-start(bf16[2,4,48,128]{3,2,1,0:T(8,128)(2,1)S(1)} %get-tuple-element.72), channel_id=1, source_target_pairs={{0,1},{1,0},{2,3},{3,2},{4,5},{5,4},{6,7},{7,6},{8,9},{9,8},{10,11... | collective-permute-start | bytes 294920 | tf_op jit(solution)/shard_map/ppermute | solution.py:353
  29.3 10.8 %collective-permute-start.14 = (bf16[2,4,48,128]{3,2,1,0:T(8,128)(2,1)S(1)}, bf16[2,4,48,128]{3,2,1,0:T(8,128)(2,1)S(1)}, u32[]{:S(2)}, u32[]{:S(2)}) collective-permute-start(bf16[2,4,48,128]{3,2,1,0:T(8,128)(2,1)S(1)} %get-tuple-element.73), channel_id=1, source_target_pairs={{0,2},{1,3},{2,0},{3,1},{4,6},{5,7},{6,4},{7,5},{8,10},{9,11},{10,... | collective-permute-start | bytes 294920 | tf_op jit(solution)/shard_map/ppermute | solution.py:353
  31.8 8.3 %collective-permute-start.15 = (bf16[2,4,48,128]{3,2,1,0:T(8,128)(2,1)S(1)}, bf16[2,4,48,128]{3,2,1,0:T(8,128)(2,1)S(1)}, u32[]{:S(2)}, u32[]{:S(2)}) collective-permute-start(bf16[2,4,48,128]{3,2,1,0:T(8,128)(2,1)S(1)} %get-tuple-element.74), channel_id=1, source_target_pairs={{0,3},{1,2},{2,1},{3,0},{4,7},{5,6},{6,5},{7,4},{8,11},{9,10},{10,... | collective-permute-start | bytes 294920 | tf_op jit(solution)/shard_map/ppermute | solution.py:353
  48.3 13.8 %collective-permute-start.21 = (bf16[6,128,128]{2,1,0:T(8,128)(2,1)S(1)}, bf16[6,128,128]{2,1,0:T(8,128)(2,1)S(1)}, u32[]{:S(2)}, u32[]{:S(2)}) collective-permute-start(bf16[6,128,128]{2,1,0:T(8,128)(2,1)S(1)} %get-tuple-element.86), channel_id=1, source_target_pairs={{0,8},{8,0},{16,24},{24,16},{1,9},{9,1},{17,25},{25,17},{2,10},{10... | collective-permute-start | bytes 589832 | tf_op jit(solution)/shard_map/ppermute | solution.py:353
  50.6 11.6 %collective-permute-start.22 = (bf16[6,128,128]{2,1,0:T(8,128)(2,1)S(1)}, bf16[6,128,128]{2,1,0:T(8,128)(2,1)S(1)}, u32[]{:S(2)}, u32[]{:S(2)}) collective-permute-start(bf16[6,128,128]{2,1,0:T(8,128)(2,1)S(1)} %get-tuple-element.87), channel_id=1, source_target_pairs={{0,16},{8,24},{16,0},{24,8},{1,17},{9,25},{17,1},{25,9},{2,18},{10... | collective-permute-start | bytes 589832 | tf_op jit(solution)/shard_map/ppermute | solution.py:353
  50.8 11.3 %collective-permute-start.23 = (bf16[6,128,128]{2,1,0:T(8,128)(2,1)S(1)}, bf16[6,128,128]{2,1,0:T(8,128)(2,1)S(1)}, u32[]{:S(2)}, u32[]{:S(2)}) collective-permute-start(bf16[6,128,128]{2,1,0:T(8,128)(2,1)S(1)} %get-tuple-element.88), channel_id=1, source_target_pairs={{0,24},{8,16},{16,8},{24,0},{1,25},{9,17},{17,9},{25,1},{2,26},{10... | collective-permute-start | bytes 589832 | tf_op jit(solution)/shard_map/ppermute | solution.py:353
  54.4 5.1 %collective-permute-start.26 = (bf16[2,2,32,128]{3,2,1,0:T(8,128)(2,1)S(1)}, bf16[2,2,32,128]{3,2,1,0:T(8,128)(2,1)S(1)}, u32[]{:S(2)}, u32[]{:S(2)}) collective-permute-start(bf16[2,2,32,128]{3,2,1,0:T(8,128)(2,1)S(1)} %get-tuple-element.108), channel_id=1, source_target_pairs={{0,2},{1,3},{2,0},{3,1},{4,6},{5,7},{6,4},{7,5},{8,10},{9,11},{10,... | collective-permute-start | bytes 98312 | tf_op jit(solution)/shard_map/ppermute | solution.py:353
  56.3 5.8 %collective-permute-start.27 = (bf16[2,2,32,128]{3,2,1,0:T(8,128)(2,1)S(1)}, bf16[2,2,32,128]{3,2,1,0:T(8,128)(2,1)S(1)}, u32[]{:S(2)}, u32[]{:S(2)}) collective-permute-start(bf16[2,2,32,128]{3,2,1,0:T(8,128)(2,1)S(1)} %get-tuple-element.105), channel_id=1, source_target_pairs={{0,3},{1,2},{2,1},{3,0},{4,7},{5,6},{6,5},{7,4},{8,11},{9,10},{10,... | collective-permute-start | bytes 98312 | tf_op jit(solution)/shard_map/ppermute | solution.py:353
  62.3 4.7 %collective-permute-start.28 = (bf16[384,128]{1,0:T(8,128)(2,1)S(1)}, bf16[384,128]{1,0:T(8,128)(2,1)S(1)}, u32[]{:S(2)}, u32[]{:S(2)}) collective-permute-start(bf16[384,128]{1,0:T(8,128)(2,1)S(1)} %dynamic-slice_bitcast_fusion), channel_id=1, source_target_pairs={{0,1},{1,0},{2,3},{3,2},{4,5},{5,4},{6,7},{7,6},{8,9},{9,8},{10,11... | collective-permute-start | bytes 294920 | tf_op jit(solution)/shard_map/ppermute | solution.py:353
  67.0 5.6 %collective-permute-start.29 = (bf16[384,128]{1,0:T(8,128)(2,1)S(1)}, bf16[384,128]{1,0:T(8,128)(2,1)S(1)}, u32[]{:S(2)}, u32[]{:S(2)}) collective-permute-start(bf16[384,128]{1,0:T(8,128)(2,1)S(1)} %fusion.6), channel_id=1, source_target_pairs={{0,2},{1,3},{2,0},{3,1},{4,6},{5,7},{6,4},{7,5},{8,10},{9,11},{10,... | collective-permute-start | bytes 294920 | tf_op jit(solution)/shard_map/ppermute | solution.py:353
  (11 other events, 31.4 us)

commit v18 on v15

--- a/solution.py
+++ b/solution.py
@@ -37,6 +37,17 @@
 
 def turned(w_ref, block, tap):
     return kernel_of(w_ref, block, tap).astype(F32).T.astype(BF16)
+
+
+def arrangement_kernel(group, *rest):
+    shared, (rows_ref, four_ref, two_ref, w_ref) = rest[:-4], rest[-4:]
+    core, section, _, _ = placed(group)
+    blocks = rows_ref.shape[0]
+    place_kernels(core, section, w_ref, *shared[:2], shared[2 : 1 + blocks], shared[1 + blocks :])
+    for block in range(blocks):
+        pair_rows_back(w_ref, block, rows_ref.at[block])
+        four_ref[block] = pair_frames_back(w_ref, block, 4)
+        two_ref[block] = pair_frames_back(w_ref, block, 2)
 
 
 def pair_rows_back(w_ref, block, pair_ref):
@@ -248,18 +259,18 @@
 def backward_kernel(geometry, factor, *rest):
     blocks, cores, group, frames_in, rows_in, halo, tile, width, height, columns = geometry
     core, section, band, unit = placed(group)
-    shared, rest = rest[: 2 * blocks], rest[2 * blocks :]
+    rows_ref, four_ref, two_ref = rest[:3]
+    rest = rest[3:]
     arrived, rest = rest[:group], rest[group:]
     xo_ref, ho_ref = rest[:2]
     d_refs = rest[2 : 2 + blocks]
     keep_ref, give_ref, mine_out, other_out = rest[2 + blocks : 6 + blocks]
-    g_ref, da_ref, dao_ref, go_ref, w_ref, grad_ref, out_ref, pair_ref = rest[6 + blocks :]
-    place_kernels(core, section, w_ref, *shared[:2], shared[2 : 1 + blocks], shared[1 + blocks :])
+    g_ref, da_ref, dao_ref, go_ref, grad_ref, out_ref = rest[6 + blocks :]
     frames = cores * frames_in
-    chans = w_ref.shape[-1]
+    chans = g_ref.shape[-1]
     rim = blocks
     own_cols = (halo, width - halo)
-    per_core = w_ref.shape[2]
+    per_core = keep_ref.shape[1]
     pixels = tile * (own_cols[1] - own_cols[0])
 
     half = group // 2
@@ -289,7 +300,6 @@
             go_ref[frame] = g_ref[frame, rim : rim + tile].astype(F32)[
                 :, own_cols[0] : own_cols[1]
             ].astype(BF16)
-        pair_rows_back(w_ref, block, pair_ref)
         hiddens = []
         for frame in range(0, frames, 2):
             stop = min(frame + 4, frames)
@@ -300,7 +310,7 @@
                 ],
                 1,
             )
-            weights = pair_frames_back(w_ref, block, stop - frame)
+            weights = four_ref[block] if stop - frame == 4 else two_ref[block]
             both = jnp.dot(ahead, weights, preferred_element_type=F32)
             hiddens += [both[:, :chans], both[:, chans:]]
         for frame in range(frames):
@@ -316,7 +326,7 @@
         for frame in range(frames):
             inner = count - 2
             taps = row_pairs(da_ref, frame, first, inner // 2)
-            back = woven(jnp.dot(taps, pair_ref[...], preferred_element_type=F32), width)
+            back = woven(jnp.dot(taps, rows_ref[block], preferred_element_type=F32), width)
             old = g_ref[frame, first + 1 : last - 1].astype(F32).reshape(inner * width, chans)
             new = (old + back).astype(BF16)
             if block:
@@ -471,12 +481,26 @@
     )(*shared, *videos)
 
     back = jax.ShapeDtypeStruct((group, frames_in, rows_in, own_width, chans), BF16)
+    features, *after = lax.optimization_barrier([features] + shared)
+    arranged = [
+        jax.ShapeDtypeStruct((blocks, rows * chans, 2 * chans), BF16) for rows in (12, 4, 2)
+    ]
+    arranged = pl.pallas_call(
+        functools.partial(arrangement_kernel, group),
+        name="arrangement",
+        in_specs=[vmem] * len(after),
+        out_specs=[vmem] * 3,
+        out_shape=arranged,
+        scratch_shapes=[pltpu.VMEM(all_kernels, BF16)],
+        compiler_params=params,
+        cost_estimate=pl.CostEstimate(flops=10**9, bytes_accessed=10**6, transcendentals=0),
+    )(*after)
     pixel_count = frames * total_rows * columns
     factor = 1.0 / float(pixel_count) ** 0.5
     keep, give, mine_grad, other_grad = pl.pallas_call(
         functools.partial(backward_kernel, geometry, factor),
         name="backward",
-        in_specs=[vmem] * (3 * blocks + group + 2),
+        in_specs=[vmem] * (blocks + group + 5),
         out_specs=[vmem] * 4,
         out_shape=[
             jax.ShapeDtypeStruct(per_section, BF16),
@@ -490,13 +514,11 @@
             pltpu.VMEM((frames, tile, own_width, chans), BF16),
             pltpu.VMEM((frames, tile, own_width, chans), BF16),
             pltpu.VMEM(all_kernels, BF16),
-            pltpu.VMEM(all_kernels, BF16),
             pltpu.VMEM((frames, tile, own_width, chans), BF16),
-            pltpu.VMEM((12 * chans, 2 * chans), BF16),
         ],
         compiler_params=params,
         cost_estimate=cost,
-    )(*shared, *cots, features, hidden, *slopes)
+    )(*arranged, *cots, features, hidden, *slopes)
 
     got = swapped(give)
     parts = [(keep[i].astype(F32) + got[i].astype(F32)).astype(BF16) for i in range(blocks)]

time: 78.6 us -> 78.7 us (level)
  waiting for transfers between devices: 25.8 us -> 24.4 us
    ppermute x29, waiting for transfers between devices: 23.2 us -> 21.9 us  [swapped(): return lax.ppermute(value, axis, [(i, i ^ step) for i in range(count)])]
  transfers between devices with their start and end apart: 32 -> 32, of which waited for: 15 -> 15; matrix products, arithmetic and copies ran while one was open for 1% -> 1% of each run, Pallas kernels for 8% -> 9%
where the time goes in v18:
time: 78.7 us; the launch traced here: 78.2 us
  starting transfers between devices  35.2 us (45%)
  waiting for transfers between devices  24.4 us (31%)
  Pallas kernels  13.4 us (17%)
  other arithmetic  2.48 us (3%)
  local copies, waits for them, and re-layouts  1.9 us (2%)
  between operations  0.85 us (1%)
    ppermute x29, starting transfers between devices, swapped(): return lax.ppermute(value, axis, [(i, i ^ step) for i in range(count)])  32.7 us
    ppermute x29, waiting for transfers between devices, swapped(): return lax.ppermute(value, axis, [(i, i ^ step) for i in range(count)])  21.9 us
    pallas_call x1, Pallas kernels, on_device(): pl.pallas_call(functools.partial(forward_kernel, geometry), name='forward...  6.17 us
    pallas_call x1, Pallas kernels, on_device(): pl.pallas_call(functools.partial(backward_kernel, geometry, factor), name...  5.2 us
    concatenate x2, other arithmetic, core_half(): whole = jnp.concatenate([spatial[0], temporal[0]], 0)  2 us
    ppermute x2, waiting for transfers between devices, traded(): return lax.ppermute(value, ('section', 'space'), pairs)  1.89 us
    unnamed x6, local copies, waits for them, and re-layouts  1.81 us
  transfers between devices with their start and end apart: 32, of which 15 were waited for; matrix products, arithmetic and copies ran while one was open for 1% of the time, Pallas kernels for 9%

profile of v18, /device:TPU:0, one launch (start us, length us, event | category | flops | bytes accessed | tf_op | source)
XLA Modules:
  0.0 78.2 jit_solution(8807248948371762300)
XLA Ops:
  2.6 3.0 %collective-permute-start.3 = (bf16[6,128,128]{2,1,0:T(8,128)(2,1)S(1)}, bf16[6,128,128]{2,1,0:T(8,128)(2,1)S(1)}, u32[]{:S(2)}, u32[]{:S(2)}) collective-permute-start(bf16[6,128,128]{2,1,0:T(8,128)(2,1)S(1)} %fusion.5.rest_0_), channel_id=1, source_target_pairs={{0,8},{8,0},{16,24},{24,16},{1,9},{9,1},{17,25},{25,17},{2,10},{10... | collective-permute-start | bytes 589832 | tf_op jit(solution)/shard_map/ppermute | solution.py:363
  5.6 1.5 %collective-permute-start.4 = (bf16[6,128,128]{2,1,0:T(8,128)(2,1)S(1)}, bf16[6,128,128]{2,1,0:T(8,128)(2,1)S(1)}, u32[]{:S(2)}, u32[]{:S(2)}) collective-permute-start(bf16[6,128,128]{2,1,0:T(8,128)(2,1)S(1)} %fusion.5.rest_0_), channel_id=1, source_target_pairs={{0,16},{8,24},{16,0},{24,8},{1,17},{9,25},{17,1},{25,9},{2,18},{10... | collective-permute-start | bytes 589832 | tf_op jit(solution)/shard_map/ppermute | solution.py:363
  7.1 1.6 %collective-permute-start = (bf16[2,2,48,128]{3,2,1,0:T(8,128)(2,1)S(1)}, bf16[2,2,48,128]{3,2,1,0:T(8,128)(2,1)S(1)}, u32[]{:S(2)}, u32[]{:S(2)}) collective-permute-start(bf16[2,2,48,128]{3,2,1,0:T(8,128)(2,1)S(1)} %get-tuple-element.72), channel_id=1, source_target_pairs={{0,1},{1,0},{2,3},{3,2},{4,5},{5,4},{6,7},{7,6},{8,9},{9,8},{10,11... | collective-permute-start | bytes 147464 | tf_op jit(solution)/shard_map/ppermute | solution.py:363
  8.7 2.6 %collective-permute-start.1 = (bf16[2,2,48,128]{3,2,1,0:T(8,128)(2,1)S(1)}, bf16[2,2,48,128]{3,2,1,0:T(8,128)(2,1)S(1)}, u32[]{:S(2)}, u32[]{:S(2)}) collective-permute-start(bf16[2,2,48,128]{3,2,1,0:T(8,128)(2,1)S(1)} %get-tuple-element.73), channel_id=1, source_target_pairs={{0,2},{1,3},{2,0},{3,1},{4,6},{5,7},{6,4},{7,5},{8,10},{9,11},{10,... | collective-permute-start | bytes 147464 | tf_op jit(solution)/shard_map/ppermute | solution.py:363
  12.8 1.4 %collective-permute-done.1 = bf16[2,2,48,128]{3,2,1,0:T(8,128)(2,1)S(1)} collective-permute-done((bf16[2,2,48,128]{3,2,1,0:T(8,128)(2,1)S(1)}, bf16[2,2,48,128]{3,2,1,0:T(8,128)(2,1)S(1)}, u32[]{:S(2)}, u32[]{:S(2)}) %collective-permute-start.1) | collective-permute-done | bytes 49184 | tf_op jit(solution)/shard_map/ppermute | solution.py:363
  14.2 3.0 %collective-permute-done.2 = bf16[2,2,48,128]{3,2,1,0:T(8,128)(2,1)S(1)} collective-permute-done((bf16[2,2,48,128]{3,2,1,0:T(8,128)(2,1)S(1)}, bf16[2,2,48,128]{3,2,1,0:T(8,128)(2,1)S(1)}, u32[]{:S(2)}, u32[]{:S(2)}) %collective-permute-start.2) | collective-permute-done | bytes 49184 | tf_op jit(solution)/shard_map/ppermute | solution.py:363
  22.6 1.9 %collective-permute-done.5.rest_9_ = bf16[4,2,2,48,128]{4,3,2,1,0:T(8,128)(2,1)S(1)} collective-permute-done((bf16[4,2,2,48,128]{4,3,2,1,0:T(8,128)(2,1)S(1)}, bf16[4,2,2,48,128]{4,3,2,1,0:T(8,128)(2,1)S(1)}, u32[]{:S(2)}, u32[]{:S(2)}) %collective-permute-start.5) | collective-permute-done | bytes 196640 | tf_op jit(solution)/shard_map/ppermute | solution.py:388
  26.4 3.2 %collective-permute-start.18 = (bf16[2,4,48,128]{3,2,1,0:T(8,128)(2,1)S(1)}, bf16[2,4,48,128]{3,2,1,0:T(8,128)(2,1)S(1)}, u32[]{:S(2)}, u32[]{:S(2)}) collective-permute-start(bf16[2,4,48,128]{3,2,1,0:T(8,128)(2,1)S(1)} %get-tuple-element.100), channel_id=1, source_target_pairs={{0,2},{1,3},{2,0},{3,1},{4,6},{5,7},{6,4},{7,5},{8,10},{9,11},{10,... | collective-permute-start | bytes 294920 | tf_op jit(solution)/shard_map/ppermute | solution.py:363
  30.3 6.2 %forward.1 = (bf16[4,4,10,16,384]{4,3,2,1,0:T(8,128)(2,1)S(1)}, bf16[4,4,8,16,128]{4,3,2,1,0:T(8,128)(2,1)S(1)}, f32[4,10,32,128]{3,2,1,0:T(8,128)S(1)}, f32[4,1...) custom-call(bf16[6,128,128]{2,1,0:T(8,128)(2,1)S(1)} %fusion.5.rest_0_, ...), custom_call_target="tpu_custom_call" | custom-call | flops 6000000000 | bytes 8000000 | tf_op jit(solution)/shard_map/forward/pallas_call | solution.py:461
  37.4 5.2 %backward.1 = (bf16[4,6,128,128]{3,2,1,0:T(8,128)(2,1)S(1)}, bf16[4,6,128,128]{3,2,1,0:T(8,128)(2,1)S(1)}, bf16[4,2,2,16,128]{4,3,2,1,0:T(8,128)(2,1)S(1)}, bf16[4,2,2,16,128]{4,3,2,1,0:T(8,128)(2,1)S(1)}) custom-call(bf16[4,1536,256]{2,1,0:T(8,128)(2,1)S(1)} %get-tuple-element.95.rest_0_, bf16[4,512,256]{2,1,0:T(8,128)(2,1)S(1)} %get-tuple-element.96.rest_1_, ...), custom_call_target="tpu_custom_call" | custom-call | flops 6000000000 | bytes 8000000 | tf_op jit(solution)/shard_map/backward/pallas_call | solution.py:500
  42.7 2.3 %collective-permute-done.20 = bf16[4,6,128,128]{3,2,1,0:T(8,128)(2,1)S(1)} collective-permute-done((bf16[4,6,128,128]{3,2,1,0:T(8,128)(2,1)S(1)}, bf16[4,6,128,128]{3,2,1,0:T(8,128)(2,1)S(1)}, u32[]{:S(2)}, u32[]{:S(2)}) %collective-permute-start.20) | collective-permute-done | bytes 786464 | tf_op jit(solution)/shard_map/ppermute | solution.py:363
  45.4 3.8 %collective-permute-start.21 = (bf16[6,128,128]{2,1,0:T(8,128)(2,1)S(1)}, bf16[6,128,128]{2,1,0:T(8,128)(2,1)S(1)}, u32[]{:S(2)}, u32[]{:S(2)}) collective-permute-start(bf16[6,128,128]{2,1,0:T(8,128)(2,1)S(1)} %get-tuple-element.112), channel_id=1, source_target_pairs={{0,8},{8,0},{16,24},{24,16},{1,9},{9,1},{17,25},{25,17},{2,10},{10... | collective-permute-start | bytes 589832 | tf_op jit(solution)/shard_map/ppermute | solution.py:363
  49.2 1.5 %collective-permute-start.23 = (bf16[6,128,128]{2,1,0:T(8,128)(2,1)S(1)}, bf16[6,128,128]{2,1,0:T(8,128)(2,1)S(1)}, u32[]{:S(2)}, u32[]{:S(2)}) collective-permute-start(bf16[6,128,128]{2,1,0:T(8,128)(2,1)S(1)} %get-tuple-element.114), channel_id=1, source_target_pairs={{0,24},{8,16},{16,8},{24,0},{1,25},{9,17},{17,9},{25,1},{2,26},{10... | collective-permute-start | bytes 589832 | tf_op jit(solution)/shard_map/ppermute | solution.py:363
  50.7 1.7 %collective-permute-start.25 = (bf16[2,2,32,128]{3,2,1,0:T(8,128)(2,1)S(1)}, bf16[2,2,32,128]{3,2,1,0:T(8,128)(2,1)S(1)}, u32[]{:S(2)}, u32[]{:S(2)}) collective-permute-start(bf16[2,2,32,128]{3,2,1,0:T(8,128)(2,1)S(1)} %get-tuple-element.133), channel_id=1, source_target_pairs={{0,1},{1,0},{2,3},{3,2},{4,5},{5,4},{6,7},{7,6},{8,9},{9,8},{10,11... | collective-permute-start | bytes 98312 | tf_op jit(solution)/shard_map/ppermute | solution.py:363
  52.4 1.6 %collective-permute-start.26 = (bf16[2,2,32,128]{3,2,1,0:T(8,128)(2,1)S(1)}, bf16[2,2,32,128]{3,2,1,0:T(8,128)(2,1)S(1)}, u32[]{:S(2)}, u32[]{:S(2)}) collective-permute-start(bf16[2,2,32,128]{3,2,1,0:T(8,128)(2,1)S(1)} %get-tuple-element.134), channel_id=1, source_target_pairs={{0,2},{1,3},{2,0},{3,1},{4,6},{5,7},{6,4},{7,5},{8,10},{9,11},{10,... | collective-permute-start | bytes 98312 | tf_op jit(solution)/shard_map/ppermute | solution.py:363
  54.7 2.7 %collective-permute-start.27 = (bf16[2,2,32,128]{3,2,1,0:T(8,128)(2,1)S(1)}, bf16[2,2,32,128]{3,2,1,0:T(8,128)(2,1)S(1)}, u32[]{:S(2)}, u32[]{:S(2)}) collective-permute-start(bf16[2,2,32,128]{3,2,1,0:T(8,128)(2,1)S(1)} %get-tuple-element.131), channel_id=1, source_target_pairs={{0,3},{1,2},{2,1},{3,0},{4,7},{5,6},{6,5},{7,4},{8,11},{9,10},{10,... | collective-permute-start | bytes 98312 | tf_op jit(solution)/shard_map/ppermute | solution.py:363
  57.5 2.9 %collective-permute-done.27 = bf16[2,2,32,128]{3,2,1,0:T(8,128)(2,1)S(1)} collective-permute-done((bf16[2,2,32,128]{3,2,1,0:T(8,128)(2,1)S(1)}, bf16[2,2,32,128]{3,2,1,0:T(8,128)(2,1)S(1)}, u32[]{:S(2)}, u32[]{:S(2)}) %collective-permute-start.27) | collective-permute-done | bytes 32800 | tf_op jit(solution)/shard_map/ppermute | solution.py:363
  60.6 1.6 %collective-permute-start.28 = (bf16[384,128]{1,0:T(8,128)(2,1)S(1)}, bf16[384,128]{1,0:T(8,128)(2,1)S(1)}, u32[]{:S(2)}, u32[]{:S(2)}) collective-permute-start(bf16[384,128]{1,0:T(8,128)(2,1)S(1)} %dynamic-slice_bitcast_fusion), channel_id=1, source_target_pairs={{0,1},{1,0},{2,3},{3,2},{4,5},{5,4},{6,7},{7,6},{8,9},{9,8},{10,11... | collective-permute-start | bytes 294920 | tf_op jit(solution)/shard_map/ppermute | solution.py:363
  62.2 3.1 %collective-permute-done.28 = bf16[384,128]{1,0:T(8,128)(2,1)S(1)} collective-permute-done((bf16[384,128]{1,0:T(8,128)(2,1)S(1)}, bf16[384,128]{1,0:T(8,128)(2,1)S(1)}, u32[]{:S(2)}, u32[]{:S(2)}) %collective-permute-start.28) | collective-permute-done | bytes 98336 | tf_op jit(solution)/shard_map/ppermute | solution.py:363
  65.3 2.2 %collective-permute-start.29 = (bf16[384,128]{1,0:T(8,128)(2,1)S(1)}, bf16[384,128]{1,0:T(8,128)(2,1)S(1)}, u32[]{:S(2)}, u32[]{:S(2)}) collective-permute-start(bf16[384,128]{1,0:T(8,128)(2,1)S(1)} %fusion.6), channel_id=1, source_target_pairs={{0,2},{1,3},{2,0},{3,1},{4,6},{5,7},{6,4},{7,5},{8,10},{9,11},{10,... | collective-permute-start | bytes 294920 | tf_op jit(solution)/shard_map/ppermute | solution.py:363
  67.5 3.4 %collective-permute-done.29 = bf16[384,128]{1,0:T(8,128)(2,1)S(1)} collective-permute-done((bf16[384,128]{1,0:T(8,128)(2,1)S(1)}, bf16[384,128]{1,0:T(8,128)(2,1)S(1)}, u32[]{:S(2)}, u32[]{:S(2)}) %collective-permute-start.29) | collective-permute-done | bytes 98336 | tf_op jit(solution)/shard_map/ppermute | solution.py:363
  70.9 1.6 %collective-permute-start.30 = (bf16[384,128]{1,0:T(8,128)(2,1)S(1)}, bf16[384,128]{1,0:T(8,128)(2,1)S(1)}, u32[]{:S(2)}, u32[]{:S(2)}) collective-permute-start(bf16[384,128]{1,0:T(8,128)(2,1)S(1)} %add_convert_fusion.5), channel_id=1, source_target_pairs={{0,1},{1,0},{2,3},{3,2},{4,5},{5,4},{6,7},{7,6},{8,9},{9,8},{10,11... | collective-permute-start | bytes 294920 | tf_op jit(solution)/shard_map/ppermute | solution.py:363
  72.6 3.0 %collective-permute-done.30 = bf16[384,128]{1,0:T(8,128)(2,1)S(1)} collective-permute-done((bf16[384,128]{1,0:T(8,128)(2,1)S(1)}, bf16[384,128]{1,0:T(8,128)(2,1)S(1)}, u32[]{:S(2)}, u32[]{:S(2)}) %collective-permute-start.30) | collective-permute-done | bytes 98336 | tf_op jit(solution)/shard_map/ppermute | solution.py:363
  75.8 1.4 %collective-permute-done.31.other_ref = bf16[2,384,128]{2,1,0:T(8,128)(2,1)S(1)} collective-permute-done((bf16[2,384,128]{2,1,0:T(8,128)(2,1)S(1)}, bf16[2,384,128]{2,1,0:T(8,128)(2,1)S(1)}, u32[]{:S(2)}, u32[]{:S(2)}) %collective-permute-start.31) | collective-permute-done | bytes 196640 | tf_op jit(solution)/shard_map/ppermute | solution.py:363
  (68 shorter events, 15.1 us)
Async XLA Ops:
  2.6 14.6 %collective-permute-start.3 = (bf16[6,128,128]{2,1,0:T(8,128)(2,1)S(1)}, bf16[6,128,128]{2,1,0:T(8,128)(2,1)S(1)}, u32[]{:S(2)}, u32[]{:S(2)}) collective-permute-start(bf16[6,128,128]{2,1,0:T(8,128)(2,1)S(1)} %fusion.5.rest_0_), channel_id=1, source_target_pairs={{0,8},{8,0},{16,24},{24,16},{1,9},{9,1},{17,25},{25,17},{2,10},{10... | collective-permute-start | bytes 589832 | tf_op jit(solution)/shard_map/ppermute | solution.py:363
  5.6 11.6 %collective-permute-start.4 = (bf16[6,128,128]{2,1,0:T(8,128)(2,1)S(1)}, bf16[6,128,128]{2,1,0:T(8,128)(2,1)S(1)}, u32[]{:S(2)}, u32[]{:S(2)}) collective-permute-start(bf16[6,128,128]{2,1,0:T(8,128)(2,1)S(1)} %fusion.5.rest_0_), channel_id=1, source_target_pairs={{0,16},{8,24},{16,0},{24,8},{1,17},{9,25},{17,1},{25,9},{2,18},{10... | collective-permute-start | bytes 589832 | tf_op jit(solution)/shard_map/ppermute | solution.py:363
  8.7 5.5 %collective-permute-start.1 = (bf16[2,2,48,128]{3,2,1,0:T(8,128)(2,1)S(1)}, bf16[2,2,48,128]{3,2,1,0:T(8,128)(2,1)S(1)}, u32[]{:S(2)}, u32[]{:S(2)}) collective-permute-start(bf16[2,2,48,128]{3,2,1,0:T(8,128)(2,1)S(1)} %get-tuple-element.73), channel_id=1, source_target_pairs={{0,2},{1,3},{2,0},{3,1},{4,6},{5,7},{6,4},{7,5},{8,10},{9,11},{10,... | collective-permute-start | bytes 147464 | tf_op jit(solution)/shard_map/ppermute | solution.py:363
  11.3 5.9 %collective-permute-start.2 = (bf16[2,2,48,128]{3,2,1,0:T(8,128)(2,1)S(1)}, bf16[2,2,48,128]{3,2,1,0:T(8,128)(2,1)S(1)}, u32[]{:S(2)}, u32[]{:S(2)}) collective-permute-start(bf16[2,2,48,128]{3,2,1,0:T(8,128)(2,1)S(1)} %get-tuple-element.74), channel_id=1, source_target_pairs={{0,3},{1,2},{2,1},{3,0},{4,7},{5,6},{6,5},{7,4},{8,11},{9,10},{10,... | collective-permute-start | bytes 147464 | tf_op jit(solution)/shard_map/ppermute | solution.py:363
  11.5 8.2 %collective-permute-start.7 = (bf16[2,2,128,128]{3,2,1,0:T(8,128)(2,1)}, bf16[2,2,128,128]{3,2,1,0:T(8,128)(2,1)S(1)}, u32[]{:S(2)}, u32[]{:S(2)}) collective-permute-start(bf16[2,2,128,128]{3,2,1,0:T(8,128)(2,1)} %rest_0_.1), channel_id=1, source_target_pairs={{8,0},{9,1},{2,10},{3,11},{16,8},{17,9},{10,18},{11,19},{24,16},{2... | collective-permute-start | bytes 393224 | tf_op jit(solution)/shard_map/ppermute | solution.py:397
  14.2 5.5 %collective-permute-start.6 = (bf16[2,2,128,128]{3,2,1,0:T(8,128)(2,1)}, bf16[2,2,128,128]{3,2,1,0:T(8,128)(2,1)S(1)}, u32[]{:S(2)}, u32[]{:S(2)}) collective-permute-start(bf16[2,2,128,128]{3,2,1,0:T(8,128)(2,1)} %rest_0_.1), channel_id=1, source_target_pairs={{0,4},{4,0},{1,5},{5,1},{2,6},{6,2},{3,7},{7,3},{8,12},{12,8},{9,1... | collective-permute-start | bytes 393224 | tf_op jit(solution)/shard_map/ppermute | solution.py:363
  17.2 7.2 %collective-permute-start.5 = (bf16[4,2,2,48,128]{4,3,2,1,0:T(8,128)(2,1)S(1)}, bf16[4,2,2,48,128]{4,3,2,1,0:T(8,128)(2,1)S(1)}, u32[]{:S(2)}, u32[]{:S(2)}) collective-permute-start(bf16[4,2,2,48,128]{4,3,2,1,0:T(8,128)(2,1)S(1)} %pad_maximum_fusion.rest_8_), channel_id=1, source_target_pairs={{0,8},{1,9},{2,10},{3,11},{8,0},{9,1},{10,2},{11,3},{16,24},{17,25... | collective-permute-start | bytes 589832 | tf_op jit(solution)/shard_map/ppermute | solution.py:388
  17.8 6.6 %collective-permute-start.9 = (bf16[6,128,128]{2,1,0:T(8,128)(2,1)S(1)}, bf16[6,128,128]{2,1,0:T(8,128)(2,1)S(1)}, u32[]{:S(2)}, u32[]{:S(2)}) collective-permute-start(bf16[6,128,128]{2,1,0:T(8,128)(2,1)S(1)} %collective-permute-done.3.rest_2_), channel_id=1, source_target_pairs={{0,16},{8,24},{16,0},{24,8},{1,17},{9,25},{17,1},{25,9},{2,18},{10... | collective-permute-start | bytes 589832 | tf_op jit(solution)/shard_map/ppermute | solution.py:363
  18.3 6.6 %collective-permute-start.13 = (bf16[4,2,2,48,128]{4,3,2,1,0:T(8,128)(2,1)S(1)}, bf16[4,2,2,48,128]{4,3,2,1,0:T(8,128)(2,1)S(1)}, u32[]{:S(2)}, u32[]{:S(2)}) collective-permute-start(bf16[4,2,2,48,128]{4,3,2,1,0:T(8,128)(2,1)S(1)} %pad_maximum_fusion.rest_8_), channel_id=1, source_target_pairs={{8,16},{9,17},{10,18},{11,19},{16,8},{17,9},{18,10},{19,11},{12,20... | collective-permute-start | bytes 589832 | tf_op jit(solution)/shard_map/ppermute | solution.py:388
  19.7 5.4 %collective-permute-start.10 = (bf16[6,128,128]{2,1,0:T(8,128)(2,1)S(1)}, bf16[6,128,128]{2,1,0:T(8,128)(2,1)S(1)}, u32[]{:S(2)}, u32[]{:S(2)}) collective-permute-start(bf16[6,128,128]{2,1,0:T(8,128)(2,1)S(1)} %collective-permute-done.3.rest_2_), channel_id=1, source_target_pairs={{0,4},{4,0},{1,5},{5,1},{2,6},{6,2},{3,7},{7,3},{8,12},{12,8},{9,1... | collective-permute-start | bytes 589832 | tf_op jit(solution)/shard_map/ppermute | solution.py:363
  21.3 5.1 %collective-permute-start.14 = (bf16[4,2,2,48,128]{4,3,2,1,0:T(8,128)(2,1)S(1)}, bf16[4,2,2,48,128]{4,3,2,1,0:T(8,128)(2,1)S(1)}, u32[]{:S(2)}, u32[]{:S(2)}) collective-permute-start(bf16[4,2,2,48,128]{4,3,2,1,0:T(8,128)(2,1)S(1)} %pad_maximum_fusion.rest_8_), channel_id=1, source_target_pairs={{0,4},{4,0},{1,5},{5,1},{2,6},{6,2},{3,7},{7,3},{8,12},{12,8},{9,1... | collective-permute-start | bytes 589832 | tf_op jit(solution)/shard_map/ppermute | solution.py:363
  24.4 5.1 %collective-permute-start.15 = (bf16[4,2,2,48,128]{4,3,2,1,0:T(8,128)(2,1)S(1)}, bf16[4,2,2,48,128]{4,3,2,1,0:T(8,128)(2,1)S(1)}, u32[]{:S(2)}, u32[]{:S(2)}) collective-permute-start(bf16[4,2,2,48,128]{4,3,2,1,0:T(8,128)(2,1)S(1)} %collective-permute-done.5.rest_9_), channel_id=1, source_target_pairs={{0,4},{4,0},{1,5},{5,1},{2,6},{6,2},{3,7},{7,3},{8,12},{12,8},{9,1... | collective-permute-start | bytes 589832 | tf_op jit(solution)/shard_map/ppermute | solution.py:363
  25.0 5.3 %collective-permute-start.12 = (bf16[6,128,128]{2,1,0:T(8,128)(2,1)S(1)}, bf16[6,128,128]{2,1,0:T(8,128)(2,1)S(1)}, u32[]{:S(2)}, u32[]{:S(2)}) collective-permute-start(bf16[6,128,128]{2,1,0:T(8,128)(2,1)S(1)} %collective-permute-done.9.rest_4_), channel_id=1, source_target_pairs={{0,4},{4,0},{1,5},{5,1},{2,6},{6,2},{3,7},{7,3},{8,12},{12,8},{9,1... | collective-permute-start | bytes 589832 | tf_op jit(solution)/shard_map/ppermute | solution.py:363
  25.0 5.3 %collective-permute-start.16 = (bf16[4,2,2,48,128]{4,3,2,1,0:T(8,128)(2,1)S(1)}, bf16[4,2,2,48,128]{4,3,2,1,0:T(8,128)(2,1)S(1)}, u32[]{:S(2)}, u32[]{:S(2)}) collective-permute-start(bf16[4,2,2,48,128]{4,3,2,1,0:T(8,128)(2,1)S(1)} %collective-permute-done.13.rest_10_), channel_id=1, source_target_pairs={{0,4},{4,0},{1,5},{5,1},{2,6},{6,2},{3,7},{7,3},{8,12},{12,8},{9,1... | collective-permute-start | bytes 589832 | tf_op jit(solution)/shard_map/ppermute | solution.py:363
  25.9 11.4 %collective-permute-start.17 = (bf16[2,4,48,128]{3,2,1,0:T(8,128)(2,1)S(1)}, bf16[2,4,48,128]{3,2,1,0:T(8,128)(2,1)S(1)}, u32[]{:S(2)}, u32[]{:S(2)}) collective-permute-start(bf16[2,4,48,128]{3,2,1,0:T(8,128)(2,1)S(1)} %get-tuple-element.99), channel_id=1, source_target_pairs={{0,1},{1,0},{2,3},{3,2},{4,5},{5,4},{6,7},{7,6},{8,9},{9,8},{10,11... | collective-permute-start | bytes 294920 | tf_op jit(solution)/shard_map/ppermute | solution.py:363
  26.4 11.0 %collective-permute-start.18 = (bf16[2,4,48,128]{3,2,1,0:T(8,128)(2,1)S(1)}, bf16[2,4,48,128]{3,2,1,0:T(8,128)(2,1)S(1)}, u32[]{:S(2)}, u32[]{:S(2)}) collective-permute-start(bf16[2,4,48,128]{3,2,1,0:T(8,128)(2,1)S(1)} %get-tuple-element.100), channel_id=1, source_target_pairs={{0,2},{1,3},{2,0},{3,1},{4,6},{5,7},{6,4},{7,5},{8,10},{9,11},{10,... | collective-permute-start | bytes 294920 | tf_op jit(solution)/shard_map/ppermute | solution.py:363
  29.5 7.9 %collective-permute-start.19 = (bf16[2,4,48,128]{3,2,1,0:T(8,128)(2,1)S(1)}, bf16[2,4,48,128]{3,2,1,0:T(8,128)(2,1)S(1)}, u32[]{:S(2)}, u32[]{:S(2)}) collective-permute-start(bf16[2,4,48,128]{3,2,1,0:T(8,128)(2,1)S(1)} %get-tuple-element.101), channel_id=1, source_target_pairs={{0,3},{1,2},{2,1},{3,0},{4,7},{5,6},{6,5},{7,4},{8,11},{9,10},{10,... | collective-permute-start | bytes 294920 | tf_op jit(solution)/shard_map/ppermute | solution.py:363
  45.2 5.5 %collective-permute-start.24 = (bf16[4,2,2,16,128]{4,3,2,1,0:T(8,128)(2,1)S(1)}, bf16[4,2,2,16,128]{4,3,2,1,0:T(8,128)(2,1)S(1)}, u32[]{:S(2)}, u32[]{:S(2)}) collective-permute-start(bf16[4,2,2,16,128]{4,3,2,1,0:T(8,128)(2,1)S(1)} %get-tuple-element.116), channel_id=1, source_target_pairs={{0,4},{4,0},{1,5},{5,1},{2,6},{6,2},{3,7},{7,3},{8,12},{12,8},{9,1... | collective-permute-start | bytes 196616 | tf_op jit(solution)/shard_map/ppermute | solution.py:363
  45.4 15.0 %collective-permute-start.21 = (bf16[6,128,128]{2,1,0:T(8,128)(2,1)S(1)}, bf16[6,128,128]{2,1,0:T(8,128)(2,1)S(1)}, u32[]{:S(2)}, u32[]{:S(2)}) collective-permute-start(bf16[6,128,128]{2,1,0:T(8,128)(2,1)S(1)} %get-tuple-element.112), channel_id=1, source_target_pairs={{0,8},{8,0},{16,24},{24,16},{1,9},{9,1},{17,25},{25,17},{2,10},{10... | collective-permute-start | bytes 589832 | tf_op jit(solution)/shard_map/ppermute | solution.py:363
  49.2 11.2 %collective-permute-start.22 = (bf16[6,128,128]{2,1,0:T(8,128)(2,1)S(1)}, bf16[6,128,128]{2,1,0:T(8,128)(2,1)S(1)}, u32[]{:S(2)}, u32[]{:S(2)}) collective-permute-start(bf16[6,128,128]{2,1,0:T(8,128)(2,1)S(1)} %get-tuple-element.113), channel_id=1, source_target_pairs={{0,16},{8,24},{16,0},{24,8},{1,17},{9,25},{17,1},{25,9},{2,18},{10... | collective-permute-start | bytes 589832 | tf_op jit(solution)/shard_map/ppermute | solution.py:363
  49.2 11.2 %collective-permute-start.23 = (bf16[6,128,128]{2,1,0:T(8,128)(2,1)S(1)}, bf16[6,128,128]{2,1,0:T(8,128)(2,1)S(1)}, u32[]{:S(2)}, u32[]{:S(2)}) collective-permute-start(bf16[6,128,128]{2,1,0:T(8,128)(2,1)S(1)} %get-tuple-element.114), channel_id=1, source_target_pairs={{0,24},{8,16},{16,8},{24,0},{1,25},{9,17},{17,9},{25,1},{2,26},{10... | collective-permute-start | bytes 589832 | tf_op jit(solution)/shard_map/ppermute | solution.py:363
  52.4 5.1 %collective-permute-start.26 = (bf16[2,2,32,128]{3,2,1,0:T(8,128)(2,1)S(1)}, bf16[2,2,32,128]{3,2,1,0:T(8,128)(2,1)S(1)}, u32[]{:S(2)}, u32[]{:S(2)}) collective-permute-start(bf16[2,2,32,128]{3,2,1,0:T(8,128)(2,1)S(1)} %get-tuple-element.134), channel_id=1, source_target_pairs={{0,2},{1,3},{2,0},{3,1},{4,6},{5,7},{6,4},{7,5},{8,10},{9,11},{10,... | collective-permute-start | bytes 98312 | tf_op jit(solution)/shard_map/ppermute | solution.py:363
  54.7 5.7 %collective-permute-start.27 = (bf16[2,2,32,128]{3,2,1,0:T(8,128)(2,1)S(1)}, bf16[2,2,32,128]{3,2,1,0:T(8,128)(2,1)S(1)}, u32[]{:S(2)}, u32[]{:S(2)}) collective-permute-start(bf16[2,2,32,128]{3,2,1,0:T(8,128)(2,1)S(1)} %get-tuple-element.131), channel_id=1, source_target_pairs={{0,3},{1,2},{2,1},{3,0},{4,7},{5,6},{6,5},{7,4},{8,11},{9,10},{10,... | collective-permute-start | bytes 98312 | tf_op jit(solution)/shard_map/ppermute | solution.py:363
  65.3 5.6 %collective-permute-start.29 = (bf16[384,128]{1,0:T(8,128)(2,1)S(1)}, bf16[384,128]{1,0:T(8,128)(2,1)S(1)}, u32[]{:S(2)}, u32[]{:S(2)}) collective-permute-start(bf16[384,128]{1,0:T(8,128)(2,1)S(1)} %fusion.6), channel_id=1, source_target_pairs={{0,2},{1,3},{2,0},{3,1},{4,6},{5,7},{6,4},{7,5},{8,10},{9,11},{10,... | collective-permute-start | bytes 294920 | tf_op jit(solution)/shard_map/ppermute | solution.py:363
  (11 other events, 28.9 us)

commit v19 on v18

--- a/solution.py
+++ b/solution.py
@@ -394,7 +394,6 @@
         for i in range(group):
             low, high = one * group + i, (one + 1) * group + i
             passed.append((high, low) if i < half else (low, high))
-    cot_halo = lax.ppermute(cotangent, ("section", "space"), passed)
 
     padded = columns + 2 * halo
     cuts = pl.pallas_call(
@@ -417,12 +416,16 @@
     half_kernels = core_half(core)
 
     def gathered(pieces):
-        return jnp.stack([pieces[0]] + [swapped(pieces[i], "space", i) for i in range(1, group)])
+        return [pieces[0]] + [swapped(pieces[i], "space", i) for i in range(1, group)]
 
     along_x = swapped(half_kernels, "section", 1)
     along_y = swapped(half_kernels, "section", 2)
-    own_video, along_x, along_y, spatial, temporal = lax.optimization_barrier(
-        [gathered(cuts), along_x, along_y, spatial, temporal]
+    pieces = gathered(cuts)
+    pieces[1], cot_rows = lax.optimization_barrier([pieces[1], cotangent])
+    cot_halo = lax.ppermute(cot_rows, ("section", "space"), passed)
+    own_video = jnp.stack(pieces)
+    _, along_x, along_y, spatial, temporal = lax.optimization_barrier(
+        [own_video, along_x, along_y, spatial, temporal]
     )
     near, far = traded(own_video, 0), traded(own_video, 1)
     mine = [along_x, along_y, swapped(along_x, "section", 2)]

time: 78.7 us -> 82.7 us (1.051)
  waiting for transfers between devices: 24.4 us -> 27.3 us
  starting transfers between devices: 35.2 us -> 36.6 us
    ppermute x29, waiting for transfers between devices: 21.9 us -> 26.9 us  [swapped(): return lax.ppermute(value, axis, [(i, i ^ step) for i in range(count)])]
    ppermute x2, waiting for transfers between devices: 1.89 us -> 0.44 us  [traded(): return lax.ppermute(value, ('section', 'space'), pairs)]
    ppermute x29, starting transfers between devices: 32.7 us -> 33.6 us  [swapped(): return lax.ppermute(value, axis, [(i, i ^ step) for i in range(count)])]
  transfers between devices with their start and end apart: 32 -> 32, of which waited for: 15 -> 14; matrix products, arithmetic and copies ran while one was open for 1% -> 1% of each run, Pallas kernels for 9% -> 9%
where the time goes in v19:
time: 82.7 us; the launch traced here: 82.5 us
  starting transfers between devices  36.6 us (44%)
  waiting for transfers between devices  27.3 us (33%)
  Pallas kernels  13.4 us (16%)
  other arithmetic  2.48 us (3%)
  local copies, waits for them, and re-layouts  1.9 us (2%)
  between operations  0.86 us (1%)
    ppermute x29, starting transfers between devices, swapped(): return lax.ppermute(value, axis, [(i, i ^ step) for i in range(count)])  33.6 us
    ppermute x29, waiting for transfers between devices, swapped(): return lax.ppermute(value, axis, [(i, i ^ step) for i in range(count)])  26.9 us
    pallas_call x1, Pallas kernels, on_device(): pl.pallas_call(functools.partial(forward_kernel, geometry), name='forward...  6.18 us
    pallas_call x1, Pallas kernels, on_device(): pl.pallas_call(functools.partial(backward_kernel, geometry, factor), name...  5.19 us
    concatenate x2, other arithmetic, core_half(): whole = jnp.concatenate([spatial[0], temporal[0]], 0)  2 us
    unnamed x6, local copies, waits for them, and re-layouts  1.81 us
    ppermute x2, starting transfers between devices, traded(): return lax.ppermute(value, ('section', 'space'), pairs)  1.71 us
  transfers between devices with their start and end apart: 32, of which 14 were waited for; matrix products, arithmetic and copies ran while one was open for 1% of the time, Pallas kernels for 9%

profile of v19, /device:TPU:0, one launch (start us, length us, event | category | flops | bytes accessed | tf_op | source)
XLA Modules:
  0.0 82.5 jit_solution(12534477496354268072)
XLA Ops:
  2.6 3.0 %collective-permute-start.4 = (bf16[6,128,128]{2,1,0:T(8,128)(2,1)S(1)}, bf16[6,128,128]{2,1,0:T(8,128)(2,1)S(1)}, u32[]{:S(2)}, u32[]{:S(2)}) collective-permute-start(bf16[6,128,128]{2,1,0:T(8,128)(2,1)S(1)} %fusion.5.rest_0_), channel_id=1, source_target_pairs={{0,8},{8,0},{16,24},{24,16},{1,9},{9,1},{17,25},{25,17},{2,10},{10... | collective-permute-start | bytes 589832 | tf_op jit(solution)/shard_map/ppermute | solution.py:363
  5.6 1.5 %collective-permute-start.5 = (bf16[6,128,128]{2,1,0:T(8,128)(2,1)S(1)}, bf16[6,128,128]{2,1,0:T(8,128)(2,1)S(1)}, u32[]{:S(2)}, u32[]{:S(2)}) collective-permute-start(bf16[6,128,128]{2,1,0:T(8,128)(2,1)S(1)} %fusion.5.rest_0_), channel_id=1, source_target_pairs={{0,16},{8,24},{16,0},{24,8},{1,17},{9,25},{17,1},{25,9},{2,18},{10... | collective-permute-start | bytes 589832 | tf_op jit(solution)/shard_map/ppermute | solution.py:363
  7.1 1.6 %collective-permute-start = (bf16[2,2,48,128]{3,2,1,0:T(8,128)(2,1)S(1)}, bf16[2,2,48,128]{3,2,1,0:T(8,128)(2,1)S(1)}, u32[]{:S(2)}, u32[]{:S(2)}) collective-permute-start(bf16[2,2,48,128]{3,2,1,0:T(8,128)(2,1)S(1)} %get-tuple-element.73), channel_id=1, source_target_pairs={{0,1},{1,0},{2,3},{3,2},{4,5},{5,4},{6,7},{7,6},{8,9},{9,8},{10,11... | collective-permute-start | bytes 147464 | tf_op jit(solution)/shard_map/ppermute | solution.py:363
  8.7 2.6 %collective-permute-start.1 = (bf16[2,2,48,128]{3,2,1,0:T(8,128)(2,1)S(1)}, bf16[2,2,48,128]{3,2,1,0:T(8,128)(2,1)S(1)}, u32[]{:S(2)}, u32[]{:S(2)}) collective-permute-start(bf16[2,2,48,128]{3,2,1,0:T(8,128)(2,1)S(1)} %get-tuple-element.75), channel_id=1, source_target_pairs={{0,2},{1,3},{2,0},{3,1},{4,6},{5,7},{6,4},{7,5},{8,10},{9,11},{10,... | collective-permute-start | bytes 147464 | tf_op jit(solution)/shard_map/ppermute | solution.py:363
  11.5 2.7 %collective-permute-done.1 = bf16[2,2,48,128]{3,2,1,0:T(8,128)(2,1)S(1)} collective-permute-done((bf16[2,2,48,128]{3,2,1,0:T(8,128)(2,1)S(1)}, bf16[2,2,48,128]{3,2,1,0:T(8,128)(2,1)S(1)}, u32[]{:S(2)}, u32[]{:S(2)}) %collective-permute-start.1) | collective-permute-done | bytes 49184 | tf_op jit(solution)/shard_map/ppermute | solution.py:363
  14.2 1.3 %collective-permute-start.7 = (bf16[2,2,128,128]{3,2,1,0:T(8,128)(2,1)}, bf16[2,2,128,128]{3,2,1,0:T(8,128)(2,1)S(1)}, u32[]{:S(2)}, u32[]{:S(2)}) collective-permute-start(bf16[2,2,128,128]{3,2,1,0:T(8,128)(2,1)} %rest_0_.1), channel_id=1, source_target_pairs={{8,0},{9,1},{2,10},{3,11},{16,8},{17,9},{10,18},{11,19},{24,16},{2... | collective-permute-start | bytes 393224 | tf_op jit(solution)/shard_map/ppermute | solution.py:425
  15.5 1.7 %collective-permute-done.2 = bf16[2,2,48,128]{3,2,1,0:T(8,128)(2,1)S(1)} collective-permute-done((bf16[2,2,48,128]{3,2,1,0:T(8,128)(2,1)S(1)}, bf16[2,2,48,128]{3,2,1,0:T(8,128)(2,1)S(1)}, u32[]{:S(2)}, u32[]{:S(2)}) %collective-permute-start.2) | collective-permute-done | bytes 49184 | tf_op jit(solution)/shard_map/ppermute | solution.py:363
  19.0 3.8 %collective-permute-start.9 = (bf16[6,128,128]{2,1,0:T(8,128)(2,1)S(1)}, bf16[6,128,128]{2,1,0:T(8,128)(2,1)S(1)}, u32[]{:S(2)}, u32[]{:S(2)}) collective-permute-start(bf16[6,128,128]{2,1,0:T(8,128)(2,1)S(1)} %collective-permute-done.4.rest_2_), channel_id=1, source_target_pairs={{0,16},{8,24},{16,0},{24,8},{1,17},{9,25},{17,1},{25,9},{2,18},{10... | collective-permute-start | bytes 589832 | tf_op jit(solution)/shard_map/ppermute | solution.py:363
  26.5 3.4 %collective-permute-done.9.rest_4_ = bf16[6,128,128]{2,1,0:T(8,128)(2,1)S(1)} collective-permute-done((bf16[6,128,128]{2,1,0:T(8,128)(2,1)S(1)}, bf16[6,128,128]{2,1,0:T(8,128)(2,1)S(1)}, u32[]{:S(2)}, u32[]{:S(2)}) %collective-permute-start.9) | collective-permute-done | bytes 196640 | tf_op jit(solution)/shard_map/ppermute | solution.py:363
  30.6 3.1 %collective-permute-start.18 = (bf16[2,4,48,128]{3,2,1,0:T(8,128)(2,1)S(1)}, bf16[2,4,48,128]{3,2,1,0:T(8,128)(2,1)S(1)}, u32[]{:S(2)}, u32[]{:S(2)}) collective-permute-start(bf16[2,4,48,128]{3,2,1,0:T(8,128)(2,1)S(1)} %get-tuple-element.102), channel_id=1, source_target_pairs={{0,2},{1,3},{2,0},{3,1},{4,6},{5,7},{6,4},{7,5},{8,10},{9,11},{10,... | collective-permute-start | bytes 294920 | tf_op jit(solution)/shard_map/ppermute | solution.py:363
  34.3 6.2 %forward.1 = (bf16[4,4,10,16,384]{4,3,2,1,0:T(8,128)(2,1)S(1)}, bf16[4,4,8,16,128]{4,3,2,1,0:T(8,128)(2,1)S(1)}, f32[4,10,32,128]{3,2,1,0:T(8,128)S(1)}, f32[4,1...) custom-call(bf16[6,128,128]{2,1,0:T(8,128)(2,1)S(1)} %fusion.5.rest_0_, ...), custom_call_target="tpu_custom_call" | custom-call | flops 6000000000 | bytes 8000000 | tf_op jit(solution)/shard_map/forward/pallas_call | solution.py:464
  41.6 5.2 %backward.1 = (bf16[4,6,128,128]{3,2,1,0:T(8,128)(2,1)S(1)}, bf16[4,6,128,128]{3,2,1,0:T(8,128)(2,1)S(1)}, bf16[4,2,2,16,128]{4,3,2,1,0:T(8,128)(2,1)S(1)}, bf16[4,2,2,16,128]{4,3,2,1,0:T(8,128)(2,1)S(1)}) custom-call(bf16[4,1536,256]{2,1,0:T(8,128)(2,1)S(1)} %get-tuple-element.97.rest_0_, bf16[4,512,256]{2,1,0:T(8,128)(2,1)S(1)} %get-tuple-element.98.rest_1_, ...), custom_call_target="tpu_custom_call" | custom-call | flops 6000000000 | bytes 8000000 | tf_op jit(solution)/shard_map/backward/pallas_call | solution.py:503
  46.9 2.3 %collective-permute-done.20 = bf16[4,6,128,128]{3,2,1,0:T(8,128)(2,1)S(1)} collective-permute-done((bf16[4,6,128,128]{3,2,1,0:T(8,128)(2,1)S(1)}, bf16[4,6,128,128]{3,2,1,0:T(8,128)(2,1)S(1)}, u32[]{:S(2)}, u32[]{:S(2)}) %collective-permute-start.20) | collective-permute-done | bytes 786464 | tf_op jit(solution)/shard_map/ppermute | solution.py:363
  49.6 2.4 %collective-permute-start.21 = (bf16[6,128,128]{2,1,0:T(8,128)(2,1)S(1)}, bf16[6,128,128]{2,1,0:T(8,128)(2,1)S(1)}, u32[]{:S(2)}, u32[]{:S(2)}) collective-permute-start(bf16[6,128,128]{2,1,0:T(8,128)(2,1)S(1)} %get-tuple-element.114), channel_id=1, source_target_pairs={{0,8},{8,0},{16,24},{24,16},{1,9},{9,1},{17,25},{25,17},{2,10},{10... | collective-permute-start | bytes 589832 | tf_op jit(solution)/shard_map/ppermute | solution.py:363
  52.1 1.5 %collective-permute-start.23 = (bf16[6,128,128]{2,1,0:T(8,128)(2,1)S(1)}, bf16[6,128,128]{2,1,0:T(8,128)(2,1)S(1)}, u32[]{:S(2)}, u32[]{:S(2)}) collective-permute-start(bf16[6,128,128]{2,1,0:T(8,128)(2,1)S(1)} %get-tuple-element.116), channel_id=1, source_target_pairs={{0,24},{8,16},{16,8},{24,0},{1,25},{9,17},{17,9},{25,1},{2,26},{10... | collective-permute-start | bytes 589832 | tf_op jit(solution)/shard_map/ppermute | solution.py:363
  53.6 2.3 %collective-permute-start.25 = (bf16[2,2,32,128]{3,2,1,0:T(8,128)(2,1)S(1)}, bf16[2,2,32,128]{3,2,1,0:T(8,128)(2,1)S(1)}, u32[]{:S(2)}, u32[]{:S(2)}) collective-permute-start(bf16[2,2,32,128]{3,2,1,0:T(8,128)(2,1)S(1)} %get-tuple-element.135), channel_id=1, source_target_pairs={{0,1},{1,0},{2,3},{3,2},{4,5},{5,4},{6,7},{7,6},{8,9},{9,8},{10,11... | collective-permute-start | bytes 98312 | tf_op jit(solution)/shard_map/ppermute | solution.py:363
  57.8 2.7 %collective-permute-start.27 = (bf16[2,2,32,128]{3,2,1,0:T(8,128)(2,1)S(1)}, bf16[2,2,32,128]{3,2,1,0:T(8,128)(2,1)S(1)}, u32[]{:S(2)}, u32[]{:S(2)}) collective-permute-start(bf16[2,2,32,128]{3,2,1,0:T(8,128)(2,1)S(1)} %get-tuple-element.133), channel_id=1, source_target_pairs={{0,3},{1,2},{2,1},{3,0},{4,7},{5,6},{6,5},{7,4},{8,11},{9,10},{10,... | collective-permute-start | bytes 98312 | tf_op jit(solution)/shard_map/ppermute | solution.py:363
  61.1 2.5 %collective-permute-done.27 = bf16[2,2,32,128]{3,2,1,0:T(8,128)(2,1)S(1)} collective-permute-done((bf16[2,2,32,128]{3,2,1,0:T(8,128)(2,1)S(1)}, bf16[2,2,32,128]{3,2,1,0:T(8,128)(2,1)S(1)}, u32[]{:S(2)}, u32[]{:S(2)}) %collective-permute-start.27) | collective-permute-done | bytes 32800 | tf_op jit(solution)/shard_map/ppermute | solution.py:363
  63.8 1.6 %collective-permute-start.28 = (bf16[384,128]{1,0:T(8,128)(2,1)S(1)}, bf16[384,128]{1,0:T(8,128)(2,1)S(1)}, u32[]{:S(2)}, u32[]{:S(2)}) collective-permute-start(bf16[384,128]{1,0:T(8,128)(2,1)S(1)} %dynamic-slice_bitcast_fusion), channel_id=1, source_target_pairs={{0,1},{1,0},{2,3},{3,2},{4,5},{5,4},{6,7},{7,6},{8,9},{9,8},{10,11... | collective-permute-start | bytes 294920 | tf_op jit(solution)/shard_map/ppermute | solution.py:363
  65.4 3.1 %collective-permute-done.28 = bf16[384,128]{1,0:T(8,128)(2,1)S(1)} collective-permute-done((bf16[384,128]{1,0:T(8,128)(2,1)S(1)}, bf16[384,128]{1,0:T(8,128)(2,1)S(1)}, u32[]{:S(2)}, u32[]{:S(2)}) %collective-permute-start.28) | collective-permute-done | bytes 98336 | tf_op jit(solution)/shard_map/ppermute | solution.py:363
  68.5 2.6 %collective-permute-start.29 = (bf16[384,128]{1,0:T(8,128)(2,1)S(1)}, bf16[384,128]{1,0:T(8,128)(2,1)S(1)}, u32[]{:S(2)}, u32[]{:S(2)}) collective-permute-start(bf16[384,128]{1,0:T(8,128)(2,1)S(1)} %fusion.6), channel_id=1, source_target_pairs={{0,2},{1,3},{2,0},{3,1},{4,6},{5,7},{6,4},{7,5},{8,10},{9,11},{10,... | collective-permute-start | bytes 294920 | tf_op jit(solution)/shard_map/ppermute | solution.py:363
  71.1 4.0 %collective-permute-done.29 = bf16[384,128]{1,0:T(8,128)(2,1)S(1)} collective-permute-done((bf16[384,128]{1,0:T(8,128)(2,1)S(1)}, bf16[384,128]{1,0:T(8,128)(2,1)S(1)}, u32[]{:S(2)}, u32[]{:S(2)}) %collective-permute-start.29) | collective-permute-done | bytes 98336 | tf_op jit(solution)/shard_map/ppermute | solution.py:363
  75.8 4.0 %collective-permute-done.30 = bf16[384,128]{1,0:T(8,128)(2,1)S(1)} collective-permute-done((bf16[384,128]{1,0:T(8,128)(2,1)S(1)}, bf16[384,128]{1,0:T(8,128)(2,1)S(1)}, u32[]{:S(2)}, u32[]{:S(2)}) %collective-permute-start.30) | collective-permute-done | bytes 98336 | tf_op jit(solution)/shard_map/ppermute | solution.py:363
  80.0 1.4 %collective-permute-done.31.other_ref = bf16[2,384,128]{2,1,0:T(8,128)(2,1)S(1)} collective-permute-done((bf16[2,384,128]{2,1,0:T(8,128)(2,1)S(1)}, bf16[2,384,128]{2,1,0:T(8,128)(2,1)S(1)}, u32[]{:S(2)}, u32[]{:S(2)}) %collective-permute-start.31) | collective-permute-done | bytes 196640 | tf_op jit(solution)/shard_map/ppermute | solution.py:363
  (68 shorter events, 15.1 us)
Async XLA Ops:
  2.6 15.7 %collective-permute-start.4 = (bf16[6,128,128]{2,1,0:T(8,128)(2,1)S(1)}, bf16[6,128,128]{2,1,0:T(8,128)(2,1)S(1)}, u32[]{:S(2)}, u32[]{:S(2)}) collective-permute-start(bf16[6,128,128]{2,1,0:T(8,128)(2,1)S(1)} %fusion.5.rest_0_), channel_id=1, source_target_pairs={{0,8},{8,0},{16,24},{24,16},{1,9},{9,1},{17,25},{25,17},{2,10},{10... | collective-permute-start | bytes 589832 | tf_op jit(solution)/shard_map/ppermute | solution.py:363
  5.6 13.3 %collective-permute-start.5 = (bf16[6,128,128]{2,1,0:T(8,128)(2,1)S(1)}, bf16[6,128,128]{2,1,0:T(8,128)(2,1)S(1)}, u32[]{:S(2)}, u32[]{:S(2)}) collective-permute-start(bf16[6,128,128]{2,1,0:T(8,128)(2,1)S(1)} %fusion.5.rest_0_), channel_id=1, source_target_pairs={{0,16},{8,24},{16,0},{24,8},{1,17},{9,25},{17,1},{25,9},{2,18},{10... | collective-permute-start | bytes 589832 | tf_op jit(solution)/shard_map/ppermute | solution.py:363
  8.7 5.5 %collective-permute-start.1 = (bf16[2,2,48,128]{3,2,1,0:T(8,128)(2,1)S(1)}, bf16[2,2,48,128]{3,2,1,0:T(8,128)(2,1)S(1)}, u32[]{:S(2)}, u32[]{:S(2)}) collective-permute-start(bf16[2,2,48,128]{3,2,1,0:T(8,128)(2,1)S(1)} %get-tuple-element.75), channel_id=1, source_target_pairs={{0,2},{1,3},{2,0},{3,1},{4,6},{5,7},{6,4},{7,5},{8,10},{9,11},{10,... | collective-permute-start | bytes 147464 | tf_op jit(solution)/shard_map/ppermute | solution.py:363
  11.3 5.9 %collective-permute-start.2 = (bf16[2,2,48,128]{3,2,1,0:T(8,128)(2,1)S(1)}, bf16[2,2,48,128]{3,2,1,0:T(8,128)(2,1)S(1)}, u32[]{:S(2)}, u32[]{:S(2)}) collective-permute-start(bf16[2,2,48,128]{3,2,1,0:T(8,128)(2,1)S(1)} %get-tuple-element.76), channel_id=1, source_target_pairs={{0,3},{1,2},{2,1},{3,0},{4,7},{5,6},{6,5},{7,4},{8,11},{9,10},{10,... | collective-permute-start | bytes 147464 | tf_op jit(solution)/shard_map/ppermute | solution.py:363
  11.5 7.5 %collective-permute-start.6 = (bf16[2,2,128,128]{3,2,1,0:T(8,128)(2,1)}, bf16[2,2,128,128]{3,2,1,0:T(8,128)(2,1)S(1)}, u32[]{:S(2)}, u32[]{:S(2)}) collective-permute-start(bf16[2,2,128,128]{3,2,1,0:T(8,128)(2,1)} %rest_0_.1), channel_id=1, source_target_pairs={{0,4},{4,0},{1,5},{5,1},{2,6},{6,2},{3,7},{7,3},{8,12},{12,8},{9,1... | collective-permute-start | bytes 393224 | tf_op jit(solution)/shard_map/ppermute | solution.py:363
  14.2 8.6 %collective-permute-start.7 = (bf16[2,2,128,128]{3,2,1,0:T(8,128)(2,1)}, bf16[2,2,128,128]{3,2,1,0:T(8,128)(2,1)S(1)}, u32[]{:S(2)}, u32[]{:S(2)}) collective-permute-start(bf16[2,2,128,128]{3,2,1,0:T(8,128)(2,1)} %rest_0_.1), channel_id=1, source_target_pairs={{8,0},{9,1},{2,10},{3,11},{16,8},{17,9},{10,18},{11,19},{24,16},{2... | collective-permute-start | bytes 393224 | tf_op jit(solution)/shard_map/ppermute | solution.py:425
  17.2 8.7 %collective-permute-start.3 = (bf16[4,2,2,48,128]{4,3,2,1,0:T(8,128)(2,1)S(1)}, bf16[4,2,2,48,128]{4,3,2,1,0:T(8,128)(2,1)S(1)}, u32[]{:S(2)}, u32[]{:S(2)}) collective-permute-start(bf16[4,2,2,48,128]{4,3,2,1,0:T(8,128)(2,1)S(1)} %pad_maximum_fusion.rest_8_), channel_id=1, source_target_pairs={{0,8},{1,9},{2,10},{3,11},{8,0},{9,1},{10,2},{11,3},{16,24},{17,25... | collective-permute-start | bytes 589832 | tf_op jit(solution)/shard_map/ppermute | solution.py:388
  18.3 7.6 %collective-permute-start.13 = (bf16[4,2,2,48,128]{4,3,2,1,0:T(8,128)(2,1)S(1)}, bf16[4,2,2,48,128]{4,3,2,1,0:T(8,128)(2,1)S(1)}, u32[]{:S(2)}, u32[]{:S(2)}) collective-permute-start(bf16[4,2,2,48,128]{4,3,2,1,0:T(8,128)(2,1)S(1)} %pad_maximum_fusion.rest_8_), channel_id=1, source_target_pairs={{8,16},{9,17},{10,18},{11,19},{16,8},{17,9},{18,10},{19,11},{12,20... | collective-permute-start | bytes 589832 | tf_op jit(solution)/shard_map/ppermute | solution.py:388
  18.9 7.5 %collective-permute-start.14 = (bf16[4,2,2,48,128]{4,3,2,1,0:T(8,128)(2,1)S(1)}, bf16[4,2,2,48,128]{4,3,2,1,0:T(8,128)(2,1)S(1)}, u32[]{:S(2)}, u32[]{:S(2)}) collective-permute-start(bf16[4,2,2,48,128]{4,3,2,1,0:T(8,128)(2,1)S(1)} %pad_maximum_fusion.rest_8_), channel_id=1, source_target_pairs={{0,4},{4,0},{1,5},{5,1},{2,6},{6,2},{3,7},{7,3},{8,12},{12,8},{9,1... | collective-permute-start | bytes 589832 | tf_op jit(solution)/shard_map/ppermute | solution.py:363
  19.0 10.9 %collective-permute-start.9 = (bf16[6,128,128]{2,1,0:T(8,128)(2,1)S(1)}, bf16[6,128,128]{2,1,0:T(8,128)(2,1)S(1)}, u32[]{:S(2)}, u32[]{:S(2)}) collective-permute-start(bf16[6,128,128]{2,1,0:T(8,128)(2,1)S(1)} %collective-permute-done.4.rest_2_), channel_id=1, source_target_pairs={{0,16},{8,24},{16,0},{24,8},{1,17},{9,25},{17,1},{25,9},{2,18},{10... | collective-permute-start | bytes 589832 | tf_op jit(solution)/shard_map/ppermute | solution.py:363
  24.2 5.7 %collective-permute-start.10 = (bf16[6,128,128]{2,1,0:T(8,128)(2,1)S(1)}, bf16[6,128,128]{2,1,0:T(8,128)(2,1)S(1)}, u32[]{:S(2)}, u32[]{:S(2)}) collective-permute-start(bf16[6,128,128]{2,1,0:T(8,128)(2,1)S(1)} %collective-permute-done.4.rest_2_), channel_id=1, source_target_pairs={{0,4},{4,0},{1,5},{5,1},{2,6},{6,2},{3,7},{7,3},{8,12},{12,8},{9,1... | collective-permute-start | bytes 589832 | tf_op jit(solution)/shard_map/ppermute | solution.py:363
  25.9 4.8 %collective-permute-start.11 = (bf16[6,128,128]{2,1,0:T(8,128)(2,1)S(1)}, bf16[6,128,128]{2,1,0:T(8,128)(2,1)S(1)}, u32[]{:S(2)}, u32[]{:S(2)}) collective-permute-start(bf16[6,128,128]{2,1,0:T(8,128)(2,1)S(1)} %collective-permute-done.5.rest_3_), channel_id=1, source_target_pairs={{0,4},{4,0},{1,5},{5,1},{2,6},{6,2},{3,7},{7,3},{8,12},{12,8},{9,1... | collective-permute-start | bytes 589832 | tf_op jit(solution)/shard_map/ppermute | solution.py:363
  25.9 7.9 %collective-permute-start.16 = (bf16[4,2,2,48,128]{4,3,2,1,0:T(8,128)(2,1)S(1)}, bf16[4,2,2,48,128]{4,3,2,1,0:T(8,128)(2,1)S(1)}, u32[]{:S(2)}, u32[]{:S(2)}) collective-permute-start(bf16[4,2,2,48,128]{4,3,2,1,0:T(8,128)(2,1)S(1)} %collective-permute-done.13.rest_10_), channel_id=1, source_target_pairs={{0,4},{4,0},{1,5},{5,1},{2,6},{6,2},{3,7},{7,3},{8,12},{12,8},{9,1... | collective-permute-start | bytes 589832 | tf_op jit(solution)/shard_map/ppermute | solution.py:363
  26.4 7.9 %collective-permute-start.15 = (bf16[4,2,2,48,128]{4,3,2,1,0:T(8,128)(2,1)S(1)}, bf16[4,2,2,48,128]{4,3,2,1,0:T(8,128)(2,1)S(1)}, u32[]{:S(2)}, u32[]{:S(2)}) collective-permute-start(bf16[4,2,2,48,128]{4,3,2,1,0:T(8,128)(2,1)S(1)} %collective-permute-done.3.rest_9_), channel_id=1, source_target_pairs={{0,4},{4,0},{1,5},{5,1},{2,6},{6,2},{3,7},{7,3},{8,12},{12,8},{9,1... | collective-permute-start | bytes 589832 | tf_op jit(solution)/shard_map/ppermute | solution.py:363
  29.9 11.4 %collective-permute-start.17 = (bf16[2,4,48,128]{3,2,1,0:T(8,128)(2,1)S(1)}, bf16[2,4,48,128]{3,2,1,0:T(8,128)(2,1)S(1)}, u32[]{:S(2)}, u32[]{:S(2)}) collective-permute-start(bf16[2,4,48,128]{3,2,1,0:T(8,128)(2,1)S(1)} %get-tuple-element.101), channel_id=1, source_target_pairs={{0,1},{1,0},{2,3},{3,2},{4,5},{5,4},{6,7},{7,6},{8,9},{9,8},{10,11... | collective-permute-start | bytes 294920 | tf_op jit(solution)/shard_map/ppermute | solution.py:363
  30.6 10.9 %collective-permute-start.18 = (bf16[2,4,48,128]{3,2,1,0:T(8,128)(2,1)S(1)}, bf16[2,4,48,128]{3,2,1,0:T(8,128)(2,1)S(1)}, u32[]{:S(2)}, u32[]{:S(2)}) collective-permute-start(bf16[2,4,48,128]{3,2,1,0:T(8,128)(2,1)S(1)} %get-tuple-element.102), channel_id=1, source_target_pairs={{0,2},{1,3},{2,0},{3,1},{4,6},{5,7},{6,4},{7,5},{8,10},{9,11},{10,... | collective-permute-start | bytes 294920 | tf_op jit(solution)/shard_map/ppermute | solution.py:363
  33.8 7.8 %collective-permute-start.19 = (bf16[2,4,48,128]{3,2,1,0:T(8,128)(2,1)S(1)}, bf16[2,4,48,128]{3,2,1,0:T(8,128)(2,1)S(1)}, u32[]{:S(2)}, u32[]{:S(2)}) collective-permute-start(bf16[2,4,48,128]{3,2,1,0:T(8,128)(2,1)S(1)} %get-tuple-element.103), channel_id=1, source_target_pairs={{0,3},{1,2},{2,1},{3,0},{4,7},{5,6},{6,5},{7,4},{8,11},{9,10},{10,... | collective-permute-start | bytes 294920 | tf_op jit(solution)/shard_map/ppermute | solution.py:363
  49.6 14.1 %collective-permute-start.21 = (bf16[6,128,128]{2,1,0:T(8,128)(2,1)S(1)}, bf16[6,128,128]{2,1,0:T(8,128)(2,1)S(1)}, u32[]{:S(2)}, u32[]{:S(2)}) collective-permute-start(bf16[6,128,128]{2,1,0:T(8,128)(2,1)S(1)} %get-tuple-element.114), channel_id=1, source_target_pairs={{0,8},{8,0},{16,24},{24,16},{1,9},{9,1},{17,25},{25,17},{2,10},{10... | collective-permute-start | bytes 589832 | tf_op jit(solution)/shard_map/ppermute | solution.py:363
  52.0 11.7 %collective-permute-start.22 = (bf16[6,128,128]{2,1,0:T(8,128)(2,1)S(1)}, bf16[6,128,128]{2,1,0:T(8,128)(2,1)S(1)}, u32[]{:S(2)}, u32[]{:S(2)}) collective-permute-start(bf16[6,128,128]{2,1,0:T(8,128)(2,1)S(1)} %get-tuple-element.115), channel_id=1, source_target_pairs={{0,16},{8,24},{16,0},{24,8},{1,17},{9,25},{17,1},{25,9},{2,18},{10... | collective-permute-start | bytes 589832 | tf_op jit(solution)/shard_map/ppermute | solution.py:363
  52.1 11.6 %collective-permute-start.23 = (bf16[6,128,128]{2,1,0:T(8,128)(2,1)S(1)}, bf16[6,128,128]{2,1,0:T(8,128)(2,1)S(1)}, u32[]{:S(2)}, u32[]{:S(2)}) collective-permute-start(bf16[6,128,128]{2,1,0:T(8,128)(2,1)S(1)} %get-tuple-element.116), channel_id=1, source_target_pairs={{0,24},{8,16},{16,8},{24,0},{1,25},{9,17},{17,9},{25,1},{2,26},{10... | collective-permute-start | bytes 589832 | tf_op jit(solution)/shard_map/ppermute | solution.py:363
  55.9 5.2 %collective-permute-start.26 = (bf16[2,2,32,128]{3,2,1,0:T(8,128)(2,1)S(1)}, bf16[2,2,32,128]{3,2,1,0:T(8,128)(2,1)S(1)}, u32[]{:S(2)}, u32[]{:S(2)}) collective-permute-start(bf16[2,2,32,128]{3,2,1,0:T(8,128)(2,1)S(1)} %get-tuple-element.136), channel_id=1, source_target_pairs={{0,2},{1,3},{2,0},{3,1},{4,6},{5,7},{6,4},{7,5},{8,10},{9,11},{10,... | collective-permute-start | bytes 98312 | tf_op jit(solution)/shard_map/ppermute | solution.py:363
  57.8 5.8 %collective-permute-start.27 = (bf16[2,2,32,128]{3,2,1,0:T(8,128)(2,1)S(1)}, bf16[2,2,32,128]{3,2,1,0:T(8,128)(2,1)S(1)}, u32[]{:S(2)}, u32[]{:S(2)}) collective-permute-start(bf16[2,2,32,128]{3,2,1,0:T(8,128)(2,1)S(1)} %get-tuple-element.133), channel_id=1, source_target_pairs={{0,3},{1,2},{2,1},{3,0},{4,7},{5,6},{6,5},{7,4},{8,11},{9,10},{10,... | collective-permute-start | bytes 98312 | tf_op jit(solution)/shard_map/ppermute | solution.py:363
  63.8 4.7 %collective-permute-start.28 = (bf16[384,128]{1,0:T(8,128)(2,1)S(1)}, bf16[384,128]{1,0:T(8,128)(2,1)S(1)}, u32[]{:S(2)}, u32[]{:S(2)}) collective-permute-start(bf16[384,128]{1,0:T(8,128)(2,1)S(1)} %dynamic-slice_bitcast_fusion), channel_id=1, source_target_pairs={{0,1},{1,0},{2,3},{3,2},{4,5},{5,4},{6,7},{7,6},{8,9},{9,8},{10,11... | collective-permute-start | bytes 294920 | tf_op jit(solution)/shard_map/ppermute | solution.py:363
  68.5 6.6 %collective-permute-start.29 = (bf16[384,128]{1,0:T(8,128)(2,1)S(1)}, bf16[384,128]{1,0:T(8,128)(2,1)S(1)}, u32[]{:S(2)}, u32[]{:S(2)}) collective-permute-start(bf16[384,128]{1,0:T(8,128)(2,1)S(1)} %fusion.6), channel_id=1, source_target_pairs={{0,2},{1,3},{2,0},{3,1},{4,6},{5,7},{6,4},{7,5},{8,10},{9,11},{10,... | collective-permute-start | bytes 294920 | tf_op jit(solution)/shard_map/ppermute | solution.py:363
  (11 other events, 31.4 us)

commit v20 on v15

--- a/solution.py
+++ b/solution.py
@@ -91,6 +91,10 @@
     chans = value.shape[1] // 2
     split = [value[:, i * chans : (i + 1) * chans].reshape(-1, 1, width, chans) for i in range(2)]
     return jnp.concatenate(split, 1).reshape(-1, chans)
+
+
+def ordered(count):
+    return [0] + list(range(count - 1, 0, -1))
 
 
 def placed(group):
@@ -270,7 +274,7 @@
         value = value.astype(F32).reshape(frames, rows_in, width - 2 * side, chans)
         return jnp.concatenate([edge, value, edge], 2).astype(BF16)
 
-    for step, ref in enumerate(arrived):
+    for step, ref in zip(ordered(group), arrived):
         at = jnp.bitwise_xor(unit, step)
         g_ref[:, pl.ds(rim + at * rows_in, rows_in)] = widened(ref[0])
         beyond = jnp.where(at < half, rim + tile + at * rows_in, (at - half) * rows_in)
@@ -435,7 +439,7 @@
     shared = [half_kernels, rest_kernels] + shared
     videos = [own_video, near, far]
     videos += [swapped(each) for each in videos]
-    cots = [cuts[0]] + [swapped(cuts[i], "space", i) for i in range(1, group)]
+    cots = [swapped(cuts[i], "space", i) if i else cuts[0] for i in ordered(group)]
 
     geometry = (blocks, cores, group, frames_in, rows_in, halo, tile, width, total_rows, columns)
     frames = cores * frames_in

time: 78.6 us -> 79.3 us (level)
  waiting for transfers between devices: 25.8 us -> 31.4 us
  starting transfers between devices: 34.6 us -> 29.5 us
    ppermute x29, waiting for transfers between devices: 23.2 us -> 28.9 us  [swapped(): return lax.ppermute(value, axis, [(i, i ^ step) for i in range(count)])]
    ppermute x29, starting transfers between devices: 32 us -> 27 us  [swapped(): return lax.ppermute(value, axis, [(i, i ^ step) for i in range(count)])]
  transfers between devices with their start and end apart: 32 -> 32, of which waited for: 15 -> 14; matrix products, arithmetic and copies ran while one was open for 1% -> 1% of each run, Pallas kernels for 8% -> 8%
where the time goes in v20:
time: 79.3 us; the launch traced here: 79.1 us
  waiting for transfers between devices  31.4 us (40%)
  starting transfers between devices  29.5 us (37%)
  Pallas kernels  12.8 us (16%)
  other arithmetic  2.48 us (3%)
  local copies, waits for them, and re-layouts  1.91 us (2%)
  between operations  0.9 us (1%)
    ppermute x29, waiting for transfers between devices, swapped(): return lax.ppermute(value, axis, [(i, i ^ step) for i in range(count)])  28.9 us
    ppermute x29, starting transfers between devices, swapped(): return lax.ppermute(value, axis, [(i, i ^ step) for i in range(count)])  27 us
    pallas_call x1, Pallas kernels, on_device(): pl.pallas_call(functools.partial(forward_kernel, geometry), name='forward...  6.17 us
    pallas_call x1, Pallas kernels, on_device(): pl.pallas_call(functools.partial(backward_kernel, geometry, factor), name...  5.4 us
    concatenate x2, other arithmetic, core_half(): whole = jnp.concatenate([spatial[0], temporal[0]], 0)  2 us
    ppermute x2, waiting for transfers between devices, traded(): return lax.ppermute(value, ('section', 'space'), pairs)  1.89 us
    unnamed x6, local copies, waits for them, and re-layouts  1.81 us
  transfers between devices with their start and end apart: 32, of which 14 were waited for; matrix products, arithmetic and copies ran while one was open for 1% of the time, Pallas kernels for 8%

profile of v20, /device:TPU:0, one launch (start us, length us, event | category | flops | bytes accessed | tf_op | source)
XLA Modules:
  0.0 79.1 jit_solution(14099724297256195361)
XLA Ops:
  2.6 3.0 %collective-permute-start.3 = (bf16[6,128,128]{2,1,0:T(8,128)(2,1)S(1)}, bf16[6,128,128]{2,1,0:T(8,128)(2,1)S(1)}, u32[]{:S(2)}, u32[]{:S(2)}) collective-permute-start(bf16[6,128,128]{2,1,0:T(8,128)(2,1)S(1)} %fusion.5.rest_0_), channel_id=1, source_target_pairs={{0,8},{8,0},{16,24},{24,16},{1,9},{9,1},{17,25},{25,17},{2,10},{10... | collective-permute-start | bytes 589832 | tf_op jit(solution)/shard_map/ppermute | solution.py:357
  5.6 1.5 %collective-permute-start.4 = (bf16[6,128,128]{2,1,0:T(8,128)(2,1)S(1)}, bf16[6,128,128]{2,1,0:T(8,128)(2,1)S(1)}, u32[]{:S(2)}, u32[]{:S(2)}) collective-permute-start(bf16[6,128,128]{2,1,0:T(8,128)(2,1)S(1)} %fusion.5.rest_0_), channel_id=1, source_target_pairs={{0,16},{8,24},{16,0},{24,8},{1,17},{9,25},{17,1},{25,9},{2,18},{10... | collective-permute-start | bytes 589832 | tf_op jit(solution)/shard_map/ppermute | solution.py:357
  7.1 1.6 %collective-permute-start = (bf16[2,2,48,128]{3,2,1,0:T(8,128)(2,1)S(1)}, bf16[2,2,48,128]{3,2,1,0:T(8,128)(2,1)S(1)}, u32[]{:S(2)}, u32[]{:S(2)}) collective-permute-start(bf16[2,2,48,128]{3,2,1,0:T(8,128)(2,1)S(1)} %get-tuple-element.60), channel_id=1, source_target_pairs={{0,1},{1,0},{2,3},{3,2},{4,5},{5,4},{6,7},{7,6},{8,9},{9,8},{10,11... | collective-permute-start | bytes 147464 | tf_op jit(solution)/shard_map/ppermute | solution.py:357
  8.7 2.6 %collective-permute-start.1 = (bf16[2,2,48,128]{3,2,1,0:T(8,128)(2,1)S(1)}, bf16[2,2,48,128]{3,2,1,0:T(8,128)(2,1)S(1)}, u32[]{:S(2)}, u32[]{:S(2)}) collective-permute-start(bf16[2,2,48,128]{3,2,1,0:T(8,128)(2,1)S(1)} %get-tuple-element.61), channel_id=1, source_target_pairs={{0,2},{1,3},{2,0},{3,1},{4,6},{5,7},{6,4},{7,5},{8,10},{9,11},{10,... | collective-permute-start | bytes 147464 | tf_op jit(solution)/shard_map/ppermute | solution.py:357
  11.5 1.3 %collective-permute-start.7 = (bf16[2,2,128,128]{3,2,1,0:T(8,128)(2,1)}, bf16[2,2,128,128]{3,2,1,0:T(8,128)(2,1)S(1)}, u32[]{:S(2)}, u32[]{:S(2)}) collective-permute-start(bf16[2,2,128,128]{3,2,1,0:T(8,128)(2,1)} %rest_0_.1), channel_id=1, source_target_pairs={{8,0},{9,1},{2,10},{3,11},{16,8},{17,9},{10,18},{11,19},{24,16},{2... | collective-permute-start | bytes 393224 | tf_op jit(solution)/shard_map/ppermute | solution.py:391
  12.8 1.4 %collective-permute-done.1 = bf16[2,2,48,128]{3,2,1,0:T(8,128)(2,1)S(1)} collective-permute-done((bf16[2,2,48,128]{3,2,1,0:T(8,128)(2,1)S(1)}, bf16[2,2,48,128]{3,2,1,0:T(8,128)(2,1)S(1)}, u32[]{:S(2)}, u32[]{:S(2)}) %collective-permute-start.1) | collective-permute-done | bytes 49184 | tf_op jit(solution)/shard_map/ppermute | solution.py:357
  14.2 3.0 %collective-permute-done.2 = bf16[2,2,48,128]{3,2,1,0:T(8,128)(2,1)S(1)} collective-permute-done((bf16[2,2,48,128]{3,2,1,0:T(8,128)(2,1)S(1)}, bf16[2,2,48,128]{3,2,1,0:T(8,128)(2,1)S(1)}, u32[]{:S(2)}, u32[]{:S(2)}) %collective-permute-start.2) | collective-permute-done | bytes 49184 | tf_op jit(solution)/shard_map/ppermute | solution.py:357
  22.6 1.9 %collective-permute-done.5.rest_9_ = bf16[4,2,2,48,128]{4,3,2,1,0:T(8,128)(2,1)S(1)} collective-permute-done((bf16[4,2,2,48,128]{4,3,2,1,0:T(8,128)(2,1)S(1)}, bf16[4,2,2,48,128]{4,3,2,1,0:T(8,128)(2,1)S(1)}, u32[]{:S(2)}, u32[]{:S(2)}) %collective-permute-start.5) | collective-permute-done | bytes 196640 | tf_op jit(solution)/shard_map/ppermute | solution.py:382
  25.9 3.1 %collective-permute-start.13 = (bf16[2,4,48,128]{3,2,1,0:T(8,128)(2,1)S(1)}, bf16[2,4,48,128]{3,2,1,0:T(8,128)(2,1)S(1)}, u32[]{:S(2)}, u32[]{:S(2)}) collective-permute-start(bf16[2,4,48,128]{3,2,1,0:T(8,128)(2,1)S(1)} %get-tuple-element.74), channel_id=1, source_target_pairs={{0,3},{1,2},{2,1},{3,0},{4,7},{5,6},{6,5},{7,4},{8,11},{9,10},{10,... | collective-permute-start | bytes 294920 | tf_op jit(solution)/shard_map/ppermute | solution.py:357
  29.0 1.3 %collective-permute-start.15 = (bf16[2,4,48,128]{3,2,1,0:T(8,128)(2,1)S(1)}, bf16[2,4,48,128]{3,2,1,0:T(8,128)(2,1)S(1)}, u32[]{:S(2)}, u32[]{:S(2)}) collective-permute-start(bf16[2,4,48,128]{3,2,1,0:T(8,128)(2,1)S(1)} %get-tuple-element.76), channel_id=1, source_target_pairs={{0,1},{1,0},{2,3},{3,2},{4,5},{5,4},{6,7},{7,6},{8,9},{9,8},{10,11... | collective-permute-start | bytes 294920 | tf_op jit(solution)/shard_map/ppermute | solution.py:357
  30.3 6.2 %forward.1 = (bf16[4,4,10,16,384]{4,3,2,1,0:T(8,128)(2,1)S(1)}, bf16[4,4,8,16,128]{4,3,2,1,0:T(8,128)(2,1)S(1)}, f32[4,10,32,128]{3,2,1,0:T(8,128)S(1)}, f32[4,1...) custom-call(bf16[6,128,128]{2,1,0:T(8,128)(2,1)S(1)} %fusion.5.rest_0_, ...), custom_call_target="tpu_custom_call" | custom-call | flops 6000000000 | bytes 8000000 | tf_op jit(solution)/shard_map/forward/pallas_call | solution.py:455
  37.1 5.4 %backward.1 = (bf16[4,6,128,128]{3,2,1,0:T(8,128)(2,1)S(1)}, bf16[4,6,128,128]{3,2,1,0:T(8,128)(2,1)S(1)}, bf16[4,2,2,16,128]{4,3,2,1,0:T(8,128)(2,1)S(1)}, bf16[4,2,2,16,128]{4,3,2,1,0:T(8,128)(2,1)S(1)}) custom-call(bf16[6,128,128]{2,1,0:T(8,128)(2,1)S(1)} %fusion.5.rest_0_, bf16[6,128,128]{2,1,0:T(8,128)(2,1)S(1)} %fusion.4.rest_1_, ...), custom_call_target="tpu_custom_call" | custom-call | flops 6000000000 | bytes 8000000 | tf_op jit(solution)/shard_map/backward/pallas_call | solution.py:480
  42.6 2.3 %collective-permute-done.20 = bf16[4,6,128,128]{3,2,1,0:T(8,128)(2,1)S(1)} collective-permute-done((bf16[4,6,128,128]{3,2,1,0:T(8,128)(2,1)S(1)}, bf16[4,6,128,128]{3,2,1,0:T(8,128)(2,1)S(1)}, u32[]{:S(2)}, u32[]{:S(2)}) %collective-permute-start.20) | collective-permute-done | bytes 786464 | tf_op jit(solution)/shard_map/ppermute | solution.py:357
  45.3 3.9 %collective-permute-start.21 = (bf16[6,128,128]{2,1,0:T(8,128)(2,1)S(1)}, bf16[6,128,128]{2,1,0:T(8,128)(2,1)S(1)}, u32[]{:S(2)}, u32[]{:S(2)}) collective-permute-start(bf16[6,128,128]{2,1,0:T(8,128)(2,1)S(1)} %get-tuple-element.88), channel_id=1, source_target_pairs={{0,8},{8,0},{16,24},{24,16},{1,9},{9,1},{17,25},{25,17},{2,10},{10... | collective-permute-start | bytes 589832 | tf_op jit(solution)/shard_map/ppermute | solution.py:357
  49.2 1.5 %collective-permute-start.23 = (bf16[6,128,128]{2,1,0:T(8,128)(2,1)S(1)}, bf16[6,128,128]{2,1,0:T(8,128)(2,1)S(1)}, u32[]{:S(2)}, u32[]{:S(2)}) collective-permute-start(bf16[6,128,128]{2,1,0:T(8,128)(2,1)S(1)} %get-tuple-element.90), channel_id=1, source_target_pairs={{0,24},{8,16},{16,8},{24,0},{1,25},{9,17},{17,9},{25,1},{2,26},{10... | collective-permute-start | bytes 589832 | tf_op jit(solution)/shard_map/ppermute | solution.py:357
  51.3 2.2 %collective-permute-start.26 = (bf16[2,2,32,128]{3,2,1,0:T(8,128)(2,1)S(1)}, bf16[2,2,32,128]{3,2,1,0:T(8,128)(2,1)S(1)}, u32[]{:S(2)}, u32[]{:S(2)}) collective-permute-start(bf16[2,2,32,128]{3,2,1,0:T(8,128)(2,1)S(1)} %get-tuple-element.110), channel_id=1, source_target_pairs={{0,2},{1,3},{2,0},{3,1},{4,6},{5,7},{6,4},{7,5},{8,10},{9,11},{10,... | collective-permute-start | bytes 98312 | tf_op jit(solution)/shard_map/ppermute | solution.py:357
  53.5 1.5 %collective-permute-done.25 = bf16[2,2,32,128]{3,2,1,0:T(8,128)(2,1)S(1)} collective-permute-done((bf16[2,2,32,128]{3,2,1,0:T(8,128)(2,1)S(1)}, bf16[2,2,32,128]{3,2,1,0:T(8,128)(2,1)S(1)}, u32[]{:S(2)}, u32[]{:S(2)}) %collective-permute-start.25) | collective-permute-done | bytes 32800 | tf_op jit(solution)/shard_map/ppermute | solution.py:357
  55.0 2.1 %collective-permute-start.27 = (bf16[2,2,32,128]{3,2,1,0:T(8,128)(2,1)S(1)}, bf16[2,2,32,128]{3,2,1,0:T(8,128)(2,1)S(1)}, u32[]{:S(2)}, u32[]{:S(2)}) collective-permute-start(bf16[2,2,32,128]{3,2,1,0:T(8,128)(2,1)S(1)} %get-tuple-element.107), channel_id=1, source_target_pairs={{0,3},{1,2},{2,1},{3,0},{4,7},{5,6},{6,5},{7,4},{8,11},{9,10},{10,... | collective-permute-start | bytes 98312 | tf_op jit(solution)/shard_map/ppermute | solution.py:357
  57.1 3.7 %collective-permute-done.27 = bf16[2,2,32,128]{3,2,1,0:T(8,128)(2,1)S(1)} collective-permute-done((bf16[2,2,32,128]{3,2,1,0:T(8,128)(2,1)S(1)}, bf16[2,2,32,128]{3,2,1,0:T(8,128)(2,1)S(1)}, u32[]{:S(2)}, u32[]{:S(2)}) %collective-permute-start.27) | collective-permute-done | bytes 32800 | tf_op jit(solution)/shard_map/ppermute | solution.py:357
  61.0 4.6 %collective-permute-done.28 = bf16[384,128]{1,0:T(8,128)(2,1)S(1)} collective-permute-done((bf16[384,128]{1,0:T(8,128)(2,1)S(1)}, bf16[384,128]{1,0:T(8,128)(2,1)S(1)}, u32[]{:S(2)}, u32[]{:S(2)}) %collective-permute-start.28) | collective-permute-done | bytes 98336 | tf_op jit(solution)/shard_map/ppermute | solution.py:357
  66.3 5.4 %collective-permute-done.29 = bf16[384,128]{1,0:T(8,128)(2,1)S(1)} collective-permute-done((bf16[384,128]{1,0:T(8,128)(2,1)S(1)}, bf16[384,128]{1,0:T(8,128)(2,1)S(1)}, u32[]{:S(2)}, u32[]{:S(2)}) %collective-permute-start.29) | collective-permute-done | bytes 98336 | tf_op jit(solution)/shard_map/ppermute | solution.py:357
  71.9 4.6 %collective-permute-done.30 = bf16[384,128]{1,0:T(8,128)(2,1)S(1)} collective-permute-done((bf16[384,128]{1,0:T(8,128)(2,1)S(1)}, bf16[384,128]{1,0:T(8,128)(2,1)S(1)}, u32[]{:S(2)}, u32[]{:S(2)}) %collective-permute-start.30) | collective-permute-done | bytes 98336 | tf_op jit(solution)/shard_map/ppermute | solution.py:357
  76.6 1.4 %collective-permute-done.31.other_ref = bf16[2,384,128]{2,1,0:T(8,128)(2,1)S(1)} collective-permute-done((bf16[2,384,128]{2,1,0:T(8,128)(2,1)S(1)}, bf16[2,384,128]{2,1,0:T(8,128)(2,1)S(1)}, u32[]{:S(2)}, u32[]{:S(2)}) %collective-permute-start.31) | collective-permute-done | bytes 196640 | tf_op jit(solution)/shard_map/ppermute | solution.py:357
  78.0 1.1 %closing.1 = (f32[1,9,128,128]{3,2,1,0:T(8,128)}, f32[1,3,128,128]{3,2,1,0:T(8,128)}) custom-call(bf16[2,384,128]{2,1,0:T(8,128)(2,1)S(1)} %pad_maximum_fusion.1.mine_ref, bf16[2,384,128]{2,1,0:T(8,128)(2,1)S(1)} %collective-permute-done.31.other_ref), custom_call_target="tpu_custom_call" | custom-call | tf_op jit(solution)/shard_map/closing/pallas_call | solution.py:533
  (67 shorter events, 11.9 us)
Async XLA Ops:
  2.6 14.6 %collective-permute-start.3 = (bf16[6,128,128]{2,1,0:T(8,128)(2,1)S(1)}, bf16[6,128,128]{2,1,0:T(8,128)(2,1)S(1)}, u32[]{:S(2)}, u32[]{:S(2)}) collective-permute-start(bf16[6,128,128]{2,1,0:T(8,128)(2,1)S(1)} %fusion.5.rest_0_), channel_id=1, source_target_pairs={{0,8},{8,0},{16,24},{24,16},{1,9},{9,1},{17,25},{25,17},{2,10},{10... | collective-permute-start | bytes 589832 | tf_op jit(solution)/shard_map/ppermute | solution.py:357
  5.6 11.6 %collective-permute-start.4 = (bf16[6,128,128]{2,1,0:T(8,128)(2,1)S(1)}, bf16[6,128,128]{2,1,0:T(8,128)(2,1)S(1)}, u32[]{:S(2)}, u32[]{:S(2)}) collective-permute-start(bf16[6,128,128]{2,1,0:T(8,128)(2,1)S(1)} %fusion.5.rest_0_), channel_id=1, source_target_pairs={{0,16},{8,24},{16,0},{24,8},{1,17},{9,25},{17,1},{25,9},{2,18},{10... | collective-permute-start | bytes 589832 | tf_op jit(solution)/shard_map/ppermute | solution.py:357
  8.7 5.5 %collective-permute-start.1 = (bf16[2,2,48,128]{3,2,1,0:T(8,128)(2,1)S(1)}, bf16[2,2,48,128]{3,2,1,0:T(8,128)(2,1)S(1)}, u32[]{:S(2)}, u32[]{:S(2)}) collective-permute-start(bf16[2,2,48,128]{3,2,1,0:T(8,128)(2,1)S(1)} %get-tuple-element.61), channel_id=1, source_target_pairs={{0,2},{1,3},{2,0},{3,1},{4,6},{5,7},{6,4},{7,5},{8,10},{9,11},{10,... | collective-permute-start | bytes 147464 | tf_op jit(solution)/shard_map/ppermute | solution.py:357
  11.3 5.9 %collective-permute-start.2 = (bf16[2,2,48,128]{3,2,1,0:T(8,128)(2,1)S(1)}, bf16[2,2,48,128]{3,2,1,0:T(8,128)(2,1)S(1)}, u32[]{:S(2)}, u32[]{:S(2)}) collective-permute-start(bf16[2,2,48,128]{3,2,1,0:T(8,128)(2,1)S(1)} %get-tuple-element.62), channel_id=1, source_target_pairs={{0,3},{1,2},{2,1},{3,0},{4,7},{5,6},{6,5},{7,4},{8,11},{9,10},{10,... | collective-permute-start | bytes 147464 | tf_op jit(solution)/shard_map/ppermute | solution.py:357
  11.5 8.2 %collective-permute-start.7 = (bf16[2,2,128,128]{3,2,1,0:T(8,128)(2,1)}, bf16[2,2,128,128]{3,2,1,0:T(8,128)(2,1)S(1)}, u32[]{:S(2)}, u32[]{:S(2)}) collective-permute-start(bf16[2,2,128,128]{3,2,1,0:T(8,128)(2,1)} %rest_0_.1), channel_id=1, source_target_pairs={{8,0},{9,1},{2,10},{3,11},{16,8},{17,9},{10,18},{11,19},{24,16},{2... | collective-permute-start | bytes 393224 | tf_op jit(solution)/shard_map/ppermute | solution.py:391
  14.2 5.5 %collective-permute-start.6 = (bf16[2,2,128,128]{3,2,1,0:T(8,128)(2,1)}, bf16[2,2,128,128]{3,2,1,0:T(8,128)(2,1)S(1)}, u32[]{:S(2)}, u32[]{:S(2)}) collective-permute-start(bf16[2,2,128,128]{3,2,1,0:T(8,128)(2,1)} %rest_0_.1), channel_id=1, source_target_pairs={{0,4},{4,0},{1,5},{5,1},{2,6},{6,2},{3,7},{7,3},{8,12},{12,8},{9,1... | collective-permute-start | bytes 393224 | tf_op jit(solution)/shard_map/ppermute | solution.py:357
  17.2 7.2 %collective-permute-start.5 = (bf16[4,2,2,48,128]{4,3,2,1,0:T(8,128)(2,1)S(1)}, bf16[4,2,2,48,128]{4,3,2,1,0:T(8,128)(2,1)S(1)}, u32[]{:S(2)}, u32[]{:S(2)}) collective-permute-start(bf16[4,2,2,48,128]{4,3,2,1,0:T(8,128)(2,1)S(1)} %pad_maximum_fusion.rest_8_), channel_id=1, source_target_pairs={{0,8},{1,9},{2,10},{3,11},{8,0},{9,1},{10,2},{11,3},{16,24},{17,25... | collective-permute-start | bytes 589832 | tf_op jit(solution)/shard_map/ppermute | solution.py:382
  17.8 6.6 %collective-permute-start.9 = (bf16[6,128,128]{2,1,0:T(8,128)(2,1)S(1)}, bf16[6,128,128]{2,1,0:T(8,128)(2,1)S(1)}, u32[]{:S(2)}, u32[]{:S(2)}) collective-permute-start(bf16[6,128,128]{2,1,0:T(8,128)(2,1)S(1)} %collective-permute-done.3.rest_2_), channel_id=1, source_target_pairs={{0,16},{8,24},{16,0},{24,8},{1,17},{9,25},{17,1},{25,9},{2,18},{10... | collective-permute-start | bytes 589832 | tf_op jit(solution)/shard_map/ppermute | solution.py:357
  18.3 6.6 %collective-permute-start.16 = (bf16[4,2,2,48,128]{4,3,2,1,0:T(8,128)(2,1)S(1)}, bf16[4,2,2,48,128]{4,3,2,1,0:T(8,128)(2,1)S(1)}, u32[]{:S(2)}, u32[]{:S(2)}) collective-permute-start(bf16[4,2,2,48,128]{4,3,2,1,0:T(8,128)(2,1)S(1)} %pad_maximum_fusion.rest_8_), channel_id=1, source_target_pairs={{8,16},{9,17},{10,18},{11,19},{16,8},{17,9},{18,10},{19,11},{12,20... | collective-permute-start | bytes 589832 | tf_op jit(solution)/shard_map/ppermute | solution.py:382
  19.7 5.4 %collective-permute-start.10 = (bf16[6,128,128]{2,1,0:T(8,128)(2,1)S(1)}, bf16[6,128,128]{2,1,0:T(8,128)(2,1)S(1)}, u32[]{:S(2)}, u32[]{:S(2)}) collective-permute-start(bf16[6,128,128]{2,1,0:T(8,128)(2,1)S(1)} %collective-permute-done.3.rest_2_), channel_id=1, source_target_pairs={{0,4},{4,0},{1,5},{5,1},{2,6},{6,2},{3,7},{7,3},{8,12},{12,8},{9,1... | collective-permute-start | bytes 589832 | tf_op jit(solution)/shard_map/ppermute | solution.py:357
  21.3 7.7 %collective-permute-start.17 = (bf16[4,2,2,48,128]{4,3,2,1,0:T(8,128)(2,1)S(1)}, bf16[4,2,2,48,128]{4,3,2,1,0:T(8,128)(2,1)S(1)}, u32[]{:S(2)}, u32[]{:S(2)}) collective-permute-start(bf16[4,2,2,48,128]{4,3,2,1,0:T(8,128)(2,1)S(1)} %pad_maximum_fusion.rest_8_), channel_id=1, source_target_pairs={{0,4},{4,0},{1,5},{5,1},{2,6},{6,2},{3,7},{7,3},{8,12},{12,8},{9,1... | collective-permute-start | bytes 589832 | tf_op jit(solution)/shard_map/ppermute | solution.py:357
  25.0 5.3 %collective-permute-start.12 = (bf16[6,128,128]{2,1,0:T(8,128)(2,1)S(1)}, bf16[6,128,128]{2,1,0:T(8,128)(2,1)S(1)}, u32[]{:S(2)}, u32[]{:S(2)}) collective-permute-start(bf16[6,128,128]{2,1,0:T(8,128)(2,1)S(1)} %collective-permute-done.9.rest_4_), channel_id=1, source_target_pairs={{0,4},{4,0},{1,5},{5,1},{2,6},{6,2},{3,7},{7,3},{8,12},{12,8},{9,1... | collective-permute-start | bytes 589832 | tf_op jit(solution)/shard_map/ppermute | solution.py:357
  25.0 5.3 %collective-permute-start.19 = (bf16[4,2,2,48,128]{4,3,2,1,0:T(8,128)(2,1)S(1)}, bf16[4,2,2,48,128]{4,3,2,1,0:T(8,128)(2,1)S(1)}, u32[]{:S(2)}, u32[]{:S(2)}) collective-permute-start(bf16[4,2,2,48,128]{4,3,2,1,0:T(8,128)(2,1)S(1)} %collective-permute-done.16.rest_10_), channel_id=1, source_target_pairs={{0,4},{4,0},{1,5},{5,1},{2,6},{6,2},{3,7},{7,3},{8,12},{12,8},{9,1... | collective-permute-start | bytes 589832 | tf_op jit(solution)/shard_map/ppermute | solution.py:357
  25.9 10.6 %collective-permute-start.13 = (bf16[2,4,48,128]{3,2,1,0:T(8,128)(2,1)S(1)}, bf16[2,4,48,128]{3,2,1,0:T(8,128)(2,1)S(1)}, u32[]{:S(2)}, u32[]{:S(2)}) collective-permute-start(bf16[2,4,48,128]{3,2,1,0:T(8,128)(2,1)S(1)} %get-tuple-element.74), channel_id=1, source_target_pairs={{0,3},{1,2},{2,1},{3,0},{4,7},{5,6},{6,5},{7,4},{8,11},{9,10},{10,... | collective-permute-start | bytes 294920 | tf_op jit(solution)/shard_map/ppermute | solution.py:357
  29.0 8.1 %collective-permute-start.14 = (bf16[2,4,48,128]{3,2,1,0:T(8,128)(2,1)S(1)}, bf16[2,4,48,128]{3,2,1,0:T(8,128)(2,1)S(1)}, u32[]{:S(2)}, u32[]{:S(2)}) collective-permute-start(bf16[2,4,48,128]{3,2,1,0:T(8,128)(2,1)S(1)} %get-tuple-element.75), channel_id=1, source_target_pairs={{0,2},{1,3},{2,0},{3,1},{4,6},{5,7},{6,4},{7,5},{8,10},{9,11},{10,... | collective-permute-start | bytes 294920 | tf_op jit(solution)/shard_map/ppermute | solution.py:357
  29.0 8.1 %collective-permute-start.15 = (bf16[2,4,48,128]{3,2,1,0:T(8,128)(2,1)S(1)}, bf16[2,4,48,128]{3,2,1,0:T(8,128)(2,1)S(1)}, u32[]{:S(2)}, u32[]{:S(2)}) collective-permute-start(bf16[2,4,48,128]{3,2,1,0:T(8,128)(2,1)S(1)} %get-tuple-element.76), channel_id=1, source_target_pairs={{0,1},{1,0},{2,3},{3,2},{4,5},{5,4},{6,7},{7,6},{8,9},{9,8},{10,11... | collective-permute-start | bytes 294920 | tf_op jit(solution)/shard_map/ppermute | solution.py:357
  45.1 5.6 %collective-permute-start.24 = (bf16[4,2,2,16,128]{4,3,2,1,0:T(8,128)(2,1)S(1)}, bf16[4,2,2,16,128]{4,3,2,1,0:T(8,128)(2,1)S(1)}, u32[]{:S(2)}, u32[]{:S(2)}) collective-permute-start(bf16[4,2,2,16,128]{4,3,2,1,0:T(8,128)(2,1)S(1)} %get-tuple-element.92), channel_id=1, source_target_pairs={{0,4},{4,0},{1,5},{5,1},{2,6},{6,2},{3,7},{7,3},{8,12},{12,8},{9,1... | collective-permute-start | bytes 196616 | tf_op jit(solution)/shard_map/ppermute | solution.py:357
  45.3 15.4 %collective-permute-start.21 = (bf16[6,128,128]{2,1,0:T(8,128)(2,1)S(1)}, bf16[6,128,128]{2,1,0:T(8,128)(2,1)S(1)}, u32[]{:S(2)}, u32[]{:S(2)}) collective-permute-start(bf16[6,128,128]{2,1,0:T(8,128)(2,1)S(1)} %get-tuple-element.88), channel_id=1, source_target_pairs={{0,8},{8,0},{16,24},{24,16},{1,9},{9,1},{17,25},{25,17},{2,10},{10... | collective-permute-start | bytes 589832 | tf_op jit(solution)/shard_map/ppermute | solution.py:357
  49.2 11.6 %collective-permute-start.22 = (bf16[6,128,128]{2,1,0:T(8,128)(2,1)S(1)}, bf16[6,128,128]{2,1,0:T(8,128)(2,1)S(1)}, u32[]{:S(2)}, u32[]{:S(2)}) collective-permute-start(bf16[6,128,128]{2,1,0:T(8,128)(2,1)S(1)} %get-tuple-element.89), channel_id=1, source_target_pairs={{0,16},{8,24},{16,0},{24,8},{1,17},{9,25},{17,1},{25,9},{2,18},{10... | collective-permute-start | bytes 589832 | tf_op jit(solution)/shard_map/ppermute | solution.py:357
  49.2 11.6 %collective-permute-start.23 = (bf16[6,128,128]{2,1,0:T(8,128)(2,1)S(1)}, bf16[6,128,128]{2,1,0:T(8,128)(2,1)S(1)}, u32[]{:S(2)}, u32[]{:S(2)}) collective-permute-start(bf16[6,128,128]{2,1,0:T(8,128)(2,1)S(1)} %get-tuple-element.90), channel_id=1, source_target_pairs={{0,24},{8,16},{16,8},{24,0},{1,25},{9,17},{17,9},{25,1},{2,26},{10... | collective-permute-start | bytes 589832 | tf_op jit(solution)/shard_map/ppermute | solution.py:357
  51.3 5.7 %collective-permute-start.26 = (bf16[2,2,32,128]{3,2,1,0:T(8,128)(2,1)S(1)}, bf16[2,2,32,128]{3,2,1,0:T(8,128)(2,1)S(1)}, u32[]{:S(2)}, u32[]{:S(2)}) collective-permute-start(bf16[2,2,32,128]{3,2,1,0:T(8,128)(2,1)S(1)} %get-tuple-element.110), channel_id=1, source_target_pairs={{0,2},{1,3},{2,0},{3,1},{4,6},{5,7},{6,4},{7,5},{8,10},{9,11},{10,... | collective-permute-start | bytes 98312 | tf_op jit(solution)/shard_map/ppermute | solution.py:357
  55.0 5.7 %collective-permute-start.27 = (bf16[2,2,32,128]{3,2,1,0:T(8,128)(2,1)S(1)}, bf16[2,2,32,128]{3,2,1,0:T(8,128)(2,1)S(1)}, u32[]{:S(2)}, u32[]{:S(2)}) collective-permute-start(bf16[2,2,32,128]{3,2,1,0:T(8,128)(2,1)S(1)} %get-tuple-element.107), channel_id=1, source_target_pairs={{0,3},{1,2},{2,1},{3,0},{4,7},{5,6},{6,5},{7,4},{8,11},{9,10},{10,... | collective-permute-start | bytes 98312 | tf_op jit(solution)/shard_map/ppermute | solution.py:357
  60.9 4.7 %collective-permute-start.28 = (bf16[384,128]{1,0:T(8,128)(2,1)S(1)}, bf16[384,128]{1,0:T(8,128)(2,1)S(1)}, u32[]{:S(2)}, u32[]{:S(2)}) collective-permute-start(bf16[384,128]{1,0:T(8,128)(2,1)S(1)} %dynamic-slice_bitcast_fusion), channel_id=1, source_target_pairs={{0,1},{1,0},{2,3},{3,2},{4,5},{5,4},{6,7},{7,6},{8,9},{9,8},{10,11... | collective-permute-start | bytes 294920 | tf_op jit(solution)/shard_map/ppermute | solution.py:357
  65.6 6.1 %collective-permute-start.29 = (bf16[384,128]{1,0:T(8,128)(2,1)S(1)}, bf16[384,128]{1,0:T(8,128)(2,1)S(1)}, u32[]{:S(2)}, u32[]{:S(2)}) collective-permute-start(bf16[384,128]{1,0:T(8,128)(2,1)S(1)} %fusion.6), channel_id=1, source_target_pairs={{0,2},{1,3},{2,0},{3,1},{4,6},{5,7},{6,4},{7,5},{8,10},{9,11},{10,... | collective-permute-start | bytes 294920 | tf_op jit(solution)/shard_map/ppermute | solution.py:357
  (11 other events, 29.1 us)
